TPU v7x, 32 devices: a whole 2x2x4 slice. The times are simulated.
32 devices in a mesh: dp: 16 (over z, y, x), tensor: 2 (over core).
Axes of the slice: x: 2, y: 2, z: 4, core: 2. Of those that a mesh axis runs over, the one named last changes fastest.
Arguments:
- tokens: bfloat16 [8192, 1024], P('dp', 'tensor'), may hold values from -6 to 6
- cotangent: bfloat16 [8192, 1024], P('dp', 'tensor'), may hold values from -6 to 6
- w_in: bfloat16 [4096, 1024], P(('dp', 'tensor')), may hold values from -0.1875 to 0.1875
- b_in: bfloat16 [4096], P(('dp', 'tensor')), may hold values from -4 to 4
- w_out: bfloat16 [4096, 1024], P(('dp', 'tensor')), may hold values from -0.09375 to 0.09375
Outputs:
- mixed: bfloat16 [8192, 1024], P('dp', 'tensor')
- grad_in: float32 [4096, 1024], P(('dp', 'tensor'))
All inputs are finite; a program needn't handle non-finite values.
Results may differ from a plain program's by a relative error of at most 0.017.
Values may be sent and summed in bfloat16 or wider, within the bound.
No kernel may reach another device: no remote copies, remote signals or barrier semaphores. Data moves between devices by JAX's collectives and lax.ppermute only.
A program may use at most 64 MiB of HBM per device.

v0:
```python
import math

import jax
import jax.numpy as jnp
from jax import lax
from jax.sharding import PartitionSpec as P


def gelu_parts(value):
    coeff = 0.7978845608
    inner = coeff * (value + 0.044715 * value * value * value)
    tangent = jnp.tanh(inner)
    result = 0.5 * value * (1.0 + tangent)
    slope = 0.5 * (1.0 + tangent) + 0.5 * value * (1.0 - tangent * tangent) * coeff * (
        1.0 + 3.0 * 0.044715 * value * value
    )
    return (result, slope)


def on_device(tokens, cotangent, w_in, b_in, w_out):
    contract_last = (((1,), (1,)), ((), ()))
    contract_first = (((0,), (0,)), ((), ()))
    total_rows = tokens.shape[0] * lax.axis_size("dp")
    scale = 1.0 / math.sqrt(total_rows)
    tok_full, cot_full = (
        lax.all_gather(tokens, "tensor", axis=1, tiled=True),
        lax.all_gather(cotangent, "tensor", axis=1, tiled=True),
    )
    in_rows, bias_rows = (
        lax.all_gather(w_in, "dp", axis=0, tiled=True),
        lax.all_gather(b_in, "dp", axis=0, tiled=True),
    )
    proj_rows = lax.all_gather(w_out, "dp", axis=0, tiled=True)
    pre = lax.dot_general(
        tok_full, in_rows, contract_last, preferred_element_type=jnp.float32
    ) + bias_rows.astype(jnp.float32)
    act_value, slope = gelu_parts(pre)
    act = act_value.astype(jnp.bfloat16)
    term = jnp.dot(act, proj_rows, preferred_element_type=jnp.float32)
    mixed = lax.psum_scatter(term.astype(jnp.bfloat16), "tensor", scatter_dimension=1, tiled=True)
    dact = lax.dot_general(cot_full, proj_rows, contract_last, preferred_element_type=jnp.float32)
    dpre = (dact * slope).astype(jnp.bfloat16)
    grad_sum = lax.psum_scatter(
        lax.dot_general(dpre, tok_full, contract_first, preferred_element_type=jnp.float32),
        "dp",
        scatter_dimension=0,
        tiled=True,
    )
    grad_in = grad_sum * scale
    return (mixed, grad_in)


def solution(mesh):
    in_specs = (
        P("dp", "tensor"),
        P("dp", "tensor"),
        P(("dp", "tensor"), None),
        P(("dp", "tensor")),
        P(("dp", "tensor"), None),
    )
    out_specs = (P("dp", "tensor"), P(("dp", "tensor"), None))
    return jax.shard_map(
        on_device, mesh=mesh, in_specs=in_specs, out_specs=out_specs, check_vma=False
    )
```

profile of v0, /device:TPU:0, one launch (start us, length us, event | category | flops | bytes accessed | tf_op | source)
XLA Modules:
  0.0 398.5 jit_solution(281047781318342530)
XLA Ops:
  7.2 0.0 all-gather.6.cloned.1.call-start
  7.2 0.7 all-gather.6.cloned.1.call-update
  7.9 0.0 all-gather.8.cloned.1.call-start
  7.9 0.7 all-gather.8.cloned.1.call-update
  8.6 0.0 all-gather.12.cloned.1.call-start
  8.7 0.7 all-gather.12.cloned.1.call-update
  9.4 0.0 all-gather.10.cloned.1.call-start
  9.4 0.5 all-gather.10.cloned.1.call-update
  10.0 0.0 reduce-scatter.5.cloned.1.call-start
  10.0 42.5 %all-gather = bf16[16,1,128]{2,1,0:T(2,128)(2,1)S(1)} all-gather(bf16[1,1,128]{2,1,0:T(2,128)(2,1)} %bitcast.10), channel_id=1, replica_groups=mesh['dp'=16,'tensor'=2] {'dp'}, dimensions={0}, use_global_device_ids=true | all-gather | bytes 4352 | tf_op jit(solution)/shard_map/all_gather | solution.py:31
  52.5 0.0 all-gather.6.cloned.1.call-done
  52.5 0.0 copy-start
  52.5 48.9 %all-gather.8.cloned.1.call-done = bf16[2048,1024]{1,0:T(8,128)(2,1)} async-done(((bf16[128,1024]{1,0:T(8,128)(2,1)}), bf16[2048,1024]{1,0:T(8,128)(2,1)}) %all-gather.8.cloned.1.call-update) | async-done | bytes 4194320 | tf_op jit(solution)/shard_map/all_gather | solution.py:30
  101.4 6.8 %fusion.19 = f32[512,2048]{1,0:T(8,128)} fusion(bf16[512,1024]{1,0:T(8,128)(2,1)} %all-gather.6.cloned.1.call-done, bf16[2048,1024]{1,0:T(8,128)(2,1)} %all-gather.8.cloned.1.call-done), kind=kOutput, calls=%fused_computation.23 | convolution fusion | flops 2147483648 | bytes 9437184 | tf_op jit(solution)/shard_map/dot_general | solution.py:34
  108.2 2.4 all-gather.12.cloned.1.call-done
  110.6 79.9 %all-gather.10.cloned.1.call-done = bf16[2048,1024]{1,0:T(8,128)(2,1)} async-done(((bf16[128,1024]{1,0:T(8,128)(2,1)}), bf16[2048,1024]{1,0:T(8,128)(2,1)}) %all-gather.10.cloned.1.call-update) | async-done | bytes 4194320 | tf_op jit(solution)/shard_map/all_gather | solution.py:33
  190.5 0.0 copy-done
  190.5 10.9 %fusion.9 = f32[2048,1024]{1,0:T(8,128)} fusion(bf16[512,1024]{1,0:T(8,128)(2,1)S(1)} %copy-done, f32[512,2048]{1,0:T(8,128)} %fusion.19, bf16[512,1024]{1,0:T(8,128)(2,1)} %all-gather.12.cloned.1.call-done, bf16[2048,1024]{1,0:T(8,128)(2,1)} %all-gather.10.cloned.1.call-done, f32[2048]{0:T(1024)S(1)} %bitcast.8), kind=kOutput, calls=%fused_computation.12 | convolution fusion | flops 4315938816 | bytes 18882560 | tf_op jit(solution)/shard_map/dot_general | solution.py:44
  201.4 0.0 reduce-scatter.5.cloned.1.call-update
  201.4 0.0 reduce-scatter.3.cloned.1.call-start
  201.5 7.2 %fusion.8 = bf16[512,1024]{1,0:T(8,128)(2,1)} fusion(bf16[2048,1024]{1,0:T(8,128)(2,1)} %all-gather.10.cloned.1.call-done, f32[512,2048]{1,0:T(8,128)} %fusion.19, f32[2048]{0:T(1024)S(1)} %bitcast.9), kind=kOutput, calls=%fused_computation.11 | convolution fusion | flops 2158493696 | bytes 9445376 | tf_op jit(solution)/shard_map/dot_general | solution.py:39
  208.7 0.0 reduce-scatter.3.cloned.1.call-update
  208.7 169.3 %reduce-scatter.5.cloned.1.call-done = f32[128,1024]{1,0:T(8,128)} async-done(((f32[2048,1024]{1,0:T(8,128)}), f32[128,1024]{1,0:T(8,128)}) %reduce-scatter.5.cloned.1.call-update) | async-done | bytes 524304 | tf_op jit(solution)/shard_map/reduce_scatter | solution.py:43
  378.0 1.9 broadcast_multiply_fusion
  379.9 11.8 %reduce-scatter.3.cloned.1.call-done = bf16[512,512]{1,0:T(8,128)(2,1)} async-done(((bf16[512,1024]{1,0:T(8,128)(2,1)}), bf16[512,512]{1,0:T(8,128)(2,1)}) %reduce-scatter.3.cloned.1.call-update) | async-done | bytes 524304 | tf_op jit(solution)/shard_map/reduce_scatter | solution.py:40
  (1 shorter events, 0.0 us)
Async XLA Ops:
  7.2 45.3 %all-gather.6.cloned.1.call-start = ((), (), s32[]{:S(2)}) async-start(), calls=%async_computation.2 | async-start | bytes 1572864 | tf_op jit(solution)/shard_map/all_gather | solution.py:26
  7.9 93.5 %all-gather.8.cloned.1.call-start = ((), (), s32[]{:S(2)}) async-start(), calls=%async_computation.3 | async-start | bytes 4456448 | tf_op jit(solution)/shard_map/all_gather | solution.py:30
  8.6 102.0 %all-gather.12.cloned.1.call-start = ((), (), s32[]{:S(2)}) async-start(), calls=%async_computation.6 | async-start | bytes 1572864 | tf_op jit(solution)/shard_map/all_gather | solution.py:27
  9.4 181.1 %all-gather.10.cloned.1.call-start = ((), (), s32[]{:S(2)}) async-start(), calls=%async_computation.4 | async-start | bytes 4456448 | tf_op jit(solution)/shard_map/all_gather | solution.py:33
  10.0 368.0 %reduce-scatter.5.cloned.1.call-start = ((), (), s32[]{:S(2)}) async-start(), calls=%async_computation.7 | async-start | bytes 8912896 | tf_op jit(solution)/shard_map/reduce_scatter | solution.py:43
  52.5 138.0 %copy-start = (bf16[512,1024]{1,0:T(8,128)(2,1)S(1)}, bf16[512,1024]{1,0:T(8,128)(2,1)}, u32[]{:S(2)}) copy-start(bf16[512,1024]{1,0:T(8,128)(2,1)} %all-gather.6.cloned.1.call-done) | copy-start | bytes 3145732
  201.4 190.2 %reduce-scatter.3.cloned.1.call-start = ((), (), s32[]{:S(2)}) async-start(), calls=%async_computation.5 | async-start | bytes 1572864 | tf_op jit(solution)/shard_map/reduce_scatter | solution.py:40
Sparse Core Ops, SparseCore 0:
  9.5 11.7 all-gather.5
  24.1 77.2 all-gather.7
  102.9 7.6 all-gather.11
  113.2 77.2 all-gather.9
  201.5 176.4 reduce-scatter.4
  380.7 10.9 reduce-scatter.2
where the time goes:
time: 399 us; the launch traced here: 398 us
  waiting for transfers between devices  315 us (79%)
  blocking collectives  42.5 us (11%)
  matrix products  24.9 us (6%)
  between operations  14.1 us (4%)
    reduce_scatter x1, waiting for transfers between devices, on_device(): lax.psum_scatter(lax.dot_general(dpre, tok_full, contract_first, preferre...  169 us
    all_gather x1, waiting for transfers between devices, on_device(): proj_rows = lax.all_gather(w_out, 'dp', axis=0, tiled=True)  79.9 us
    all_gather x1, waiting for transfers between devices, on_device(): lax.all_gather(w_in, 'dp', axis=0, tiled=True)  48.9 us
    all_gather x1, blocking collectives, on_device(): lax.all_gather(b_in, 'dp', axis=0, tiled=True)  42.5 us
    reduce_scatter x1, waiting for transfers between devices, on_device(): lax.psum_scatter(term.astype(jnp.bfloat16), 'tensor', scatter_dimension=1...  11.8 us
    dot_general x1, matrix products, on_device(): lax.dot_general(dpre, tok_full, contract_first, preferred_element_type=jn...  10.9 us
  transfers between devices with their start and end apart: 6, of which 5 were waited for; matrix products, arithmetic and copies ran while one was open for 4% of the time, Pallas kernels for 0%

commit v1 on v0

v1 whole, which is shorter than its diff:
```python
import math

import jax
import jax.numpy as jnp
from jax import lax
from jax.sharding import Mesh, PartitionSpec as P


def gelu_parts(value):
    coeff = 0.7978845608
    inner = coeff * (value + 0.044715 * value * value * value)
    tangent = jnp.tanh(inner)
    result = 0.5 * value * (1.0 + tangent)
    slope = 0.5 * (1.0 + tangent) + 0.5 * value * (1.0 - tangent * tangent) * coeff * (
        1.0 + 3.0 * 0.044715 * value * value
    )
    return (result, slope)


NEAR = 4
CONTRACT_LAST = (((1,), (1,)), ((), ()))
CONTRACT_FIRST = (((0,), (0,)), ((), ()))


def on_device(tokens, cotangent, w_in, b_in, w_out):
    far = lax.axis_size("far")
    near = lax.axis_size("near")
    tensor = lax.axis_size("tensor")
    rows, feats = tokens.shape
    owned, width = w_in.shape
    scale = 1.0 / math.sqrt(rows * far * near)
    bias_rows = jnp.pad(b_in.reshape(1, owned), ((0, 15), (0, width - owned)))
    weights = lax.all_gather(jnp.concatenate([w_in, w_out, bias_rows], 0), "far", axis=0)
    in_rows = weights[:, :owned].reshape(far * owned, width)
    proj_rows = weights[:, owned : 2 * owned].reshape(far * owned, width)
    bias = weights[:, 2 * owned, :owned].reshape(far * owned).astype(jnp.float32)
    tok = lax.all_gather(tokens, ("near", "tensor"), axis=0).reshape(near, tensor, rows, feats)
    cot = lax.all_gather(cotangent, ("near", "tensor"), axis=0).reshape(near, tensor, rows, feats)
    tok_full = tok.transpose(0, 2, 1, 3).reshape(near * rows, width)
    cot_full = cot.transpose(0, 2, 1, 3).reshape(near * rows, width)
    pre = lax.dot_general(
        tok_full, in_rows, CONTRACT_LAST, preferred_element_type=jnp.float32
    ) + bias
    act_value, slope = gelu_parts(pre)
    act = act_value.astype(jnp.bfloat16)
    term = jnp.dot(act, proj_rows, preferred_element_type=jnp.float32).astype(jnp.bfloat16)
    term = term.reshape(near, rows, tensor, feats).transpose(0, 2, 1, 3)
    mixed = lax.psum_scatter(
        term.reshape(near * tensor, rows, feats), ("near", "tensor"), scatter_dimension=0
    )
    dact = lax.dot_general(cot_full, proj_rows, CONTRACT_LAST, preferred_element_type=jnp.float32)
    dpre = (dact * slope).astype(jnp.bfloat16)
    grad = lax.dot_general(dpre, tok_full, CONTRACT_FIRST, preferred_element_type=jnp.float32)
    grad_sum = lax.psum_scatter(grad.astype(jnp.bfloat16), "far", scatter_dimension=0, tiled=True)
    return (mixed, grad_sum.astype(jnp.float32) * scale)


def solution(mesh):
    dp, tensor = mesh.shape["dp"], mesh.shape["tensor"]
    fine = Mesh(mesh.devices.reshape(dp // NEAR, NEAR, tensor), ("far", "near", "tensor"))
    rows = ("far", "near")
    owners = ("far", "near", "tensor")
    in_specs = (P(rows, "tensor"), P(rows, "tensor"), P(owners, None), P(owners), P(owners, None))
    out_specs = (P(rows, "tensor"), P(owners, None))
    return jax.shard_map(
        on_device, mesh=fine, in_specs=in_specs, out_specs=out_specs, check_vma=False
    )
```

time: 399 us -> 251 us (0.63)
  waiting for transfers between devices: 315 us -> 175 us
  blocking collectives: 42.5 us -> 0 us
  local copies, waits for them, and re-layouts: 0.01 us -> 33.8 us
    reduce_scatter x2, waiting for transfers between devices: 181 us -> 59.5 us  [the longest x1 52.3 us: on_device(): lax.psum_scatter(term.reshape(near * tensor, rows, feats), ('near', 'tens...]
    all_gather x1 -> x0, blocking collectives: 42.5 us -> none  [on_device(): lax.all_gather(b_in, 'dp', axis=0, tiled=True)]
    reshape x0 -> x3, local copies, waits for them, and re-layouts: none -> 20.9 us  [the longest x1 7.86 us: on_device(): term = term.reshape(near, rows, tensor, feats).transpose(0, 2, 1, 3)]
    all_gather x4 -> x3, waiting for transfers between devices: 131 us -> 114 us  [the longest x1 50 us: on_device(): lax.all_gather(jnp.concatenate([w_in, w_out, bias_rows], 0), 'far', axis=0)]
    unnamed x2 -> x4, local copies, waits for them, and re-layouts: 0.01 us -> 6.33 us
    transpose x0 -> x1, local copies, waits for them, and re-layouts: none -> 4.92 us  [on_device(): term = term.reshape(near, rows, tensor, feats).transpose(0, 2, 1, 3)]
  transfers between devices with their start and end apart: 6 -> 5, of which waited for: 5 -> 5; matrix products, arithmetic and copies ran while one was open for 4% -> 14% of each run, Pallas kernels for 0% -> 0%
where the time goes in v1:
time: 251 us; the launch traced here: 250 us
  waiting for transfers between devices  175 us (70%)
  local copies, waits for them, and re-layouts  33.8 us (13%)
  matrix products  23 us (9%)
  between operations  13.8 us (5%)
  other arithmetic  4.39 us (2%)
    reduce_scatter x1, waiting for transfers between devices, on_device(): lax.psum_scatter(term.reshape(near * tensor, rows, feats), ('near', 'tens...  52.3 us
    all_gather x1, waiting for transfers between devices, on_device(): lax.all_gather(jnp.concatenate([w_in, w_out, bias_rows], 0), 'far', axis=0)  50 us
    all_gather x1, waiting for transfers between devices, on_device(): lax.all_gather(tokens, ('near', 'tensor'), axis=0)  35 us
    all_gather x1, waiting for transfers between devices, on_device(): lax.all_gather(cotangent, ('near', 'tensor'), axis=0)  29 us
    dot_general x1, matrix products, on_device(): lax.dot_general(dpre, tok_full, CONTRACT_FIRST, preferred_element_type=jn...  11.2 us
    reshape x1, local copies, waits for them, and re-layouts, on_device(): term = term.reshape(near, rows, tensor, feats).transpose(0, 2, 1, 3)  7.86 us
    dot_general x1, matrix products, on_device(): jnp.dot(act, proj_rows, preferred_element_type=jnp.float32)  7.35 us
    reduce_scatter x1, waiting for transfers between devices, on_device(): lax.psum_scatter(grad.astype(jnp.bfloat16), 'far', scatter_dimension=0, t...  7.12 us
  transfers between devices with their start and end apart: 5, of which 5 were waited for; matrix products, arithmetic and copies ran while one was open for 14% of the time, Pallas kernels for 0%

profile of v1, /device:TPU:0, one launch (start us, length us, event | category | flops | bytes accessed | tf_op | source)
XLA Modules:
  0.0 250.1 jit_solution(1310537609534475220)
XLA Ops:
  7.2 0.0 all-gather.7.cloned.1.call-start
  7.2 1.9 fusion.13
  9.1 0.0 all-gather.7.cloned.1.call-update
  9.1 0.0 all-gather.9.cloned.1.call-start
  9.2 0.7 all-gather.9.cloned.1.call-update
  9.9 0.0 all-gather.11.cloned.1.call-start
  9.9 0.7 all-gather.11.cloned.1.call-update
  10.6 0.0 reduce-scatter.5.cloned.1.call-start
  10.7 50.0 %all-gather.7.cloned.1.call-done = bf16[1088,1024]{1,0:T(8,128)(2,1)} async-done(((bf16[272,1024]{1,0:T(8,128)(2,1)}), bf16[1088,1024]{1,0:T(8,128)(2,1)}) %all-gather.7.cloned.1.call-update) | async-done | bytes 2228240 | tf_op jit(solution)/shard_map/all_gather | solution.py:33
  60.6 0.7 slice_convert_fusion
  61.3 1.7 fusion.23
  63.0 35.0 %all-gather.9.cloned.1.call-done = bf16[4096,512]{1,0:T(8,128)(2,1)} async-done(((bf16[512,512]{1,0:T(8,128)(2,1)}), bf16[4096,512]{1,0:T(8,128)(2,1)}) %all-gather.9.cloned.1.call-update) | async-done | bytes 4194320 | tf_op jit(solution)/shard_map/all_gather | solution.py:37
  98.1 6.5 %copy.8 = bf16[4,2,512,512]{3,1,2,0:T(2,128)(2,1)S(1)} copy(bf16[4,2,512,512]{3,2,1,0:T(8,128)(2,1)} %bitcast.47) | data formatting | bytes 8388608 | tf_op jit(solution)/shard_map/reshape | solution.py:37
  104.6 3.2 %copy.11 = bf16[256,8,2,512]{3,1,2,0:T(8,128)(2,1)} copy(bf16[256,8,2,512]{3,2,1,0:T(2,128)(2,1)S(1)} %bitcast.44) | data formatting | bytes 8388608
  107.8 29.0 %all-gather.11.cloned.1.call-done = bf16[4096,512]{1,0:T(8,128)(2,1)} async-done(((bf16[512,512]{1,0:T(8,128)(2,1)}), bf16[4096,512]{1,0:T(8,128)(2,1)}) %all-gather.11.cloned.1.call-update) | async-done | bytes 4194320 | tf_op jit(solution)/shard_map/all_gather | solution.py:38
  136.7 6.5 %copy.10 = bf16[4,2,512,512]{3,1,2,0:T(2,128)(2,1)S(1)} copy(bf16[4,2,512,512]{3,2,1,0:T(8,128)(2,1)} %bitcast.48) | data formatting | bytes 8388608 | tf_op jit(solution)/shard_map/reshape | solution.py:38
  143.2 0.0 copy-start
  143.2 3.2 %copy.12 = bf16[256,8,2,512]{3,1,2,0:T(8,128)(2,1)} copy(bf16[256,8,2,512]{3,2,1,0:T(2,128)(2,1)S(1)} %bitcast.45) | data formatting | bytes 8388608
  146.4 0.0 copy-done
  146.4 4.5 %fusion.24 = f32[512,2048]{1,0:T(8,128)} fusion(bf16[512,1024]{1,0:T(8,128)(2,1)S(1)} %bitcast.56, bf16[2048,1024]{1,0:T(8,128)(2,1)S(1)} %bitcast.50), kind=kOutput, calls=%fused_computation.33 | convolution fusion | flops 2147483648 | bytes 9437184 | tf_op jit(solution)/shard_map/dot_general | solution.py:41
  150.9 11.2 %convolution_convert_fusion.1 = bf16[512,1024]{1,0:T(8,128)(2,1)} fusion(bf16[2048,1024]{1,0:T(8,128)(2,1)} %bitcast.49, f32[512,2048]{1,0:T(8,128)} %fusion.24, bf16[512,1024]{1,0:T(8,128)(2,1)S(1)} %bitcast.54, bf16[2048,1024]{1,0:T(8,128)(2,1)} %bitcast.51, f32[512]{0:T(512)S(1)} %bitcast.57), kind=kOutput, calls=%fused_computation.17 | convolution fusion | flops 4316463104 | bytes 14682112 | tf_op jit(solution)/shard_map/dot_general | solution.py:53
  162.1 0.0 reduce-scatter.5.cloned.1.call-update
  162.1 0.0 reduce-scatter.3.cloned.1.call-start
  162.2 7.4 %convolution_convert_fusion = bf16[2048,1024]{1,0:T(8,128)(2,1)} fusion(bf16[512,1024]{1,0:T(8,128)(2,1)S(1)} %bitcast.55, f32[512,2048]{1,0:T(8,128)} %fusion.24, f32[512]{0:T(512)S(1)} %bitcast.58), kind=kOutput, calls=%fused_computation.11 | convolution fusion | flops 2160066560 | bytes 9439232 | tf_op jit(solution)/shard_map/dot_general | solution.py:46
  169.5 7.9 %reshape.43 = bf16[4,512,2,512]{3,2,1,0:T(2,128)(2,1)} reshape(bf16[2048,1024]{1,0:T(8,128)(2,1)} %convolution_convert_fusion) | data formatting | bytes 8388608 | tf_op jit(solution)/shard_map/reshape | solution.py:47
  177.4 4.9 %copy.9 = bf16[4,2,512,512]{3,2,1,0:T(8,128)(2,1)} copy(bf16[4,2,512,512]{3,1,2,0:T(2,128)(2,1)} %bitcast.46) | data formatting | bytes 8388608 | tf_op jit(solution)/shard_map/transpose | solution.py:47
  182.3 0.0 reduce-scatter.3.cloned.1.call-update
  182.3 7.1 %reduce-scatter.5.cloned.1.call-done = bf16[128,1024]{1,0:T(8,128)(2,1)} async-done(((bf16[512,1024]{1,0:T(8,128)(2,1)}), bf16[128,1024]{1,0:T(8,128)(2,1)}) %reduce-scatter.5.cloned.1.call-update) | async-done | bytes 262160 | tf_op jit(solution)/shard_map/reduce_scatter | solution.py:54
  189.5 1.8 convert_multiply_fusion
  191.3 52.3 %reduce-scatter.3.cloned.1.call-done = bf16[1,512,512]{2,1,0:T(8,128)(2,1)} async-done(((bf16[8,512,512]{2,1,0:T(8,128)(2,1)}), bf16[1,512,512]{2,1,0:T(8,128)(2,1)}) %reduce-scatter.3.cloned.1.call-update) | async-done | bytes 524304 | tf_op jit(solution)/shard_map/reduce_scatter | solution.py:48
Async XLA Ops:
  7.2 53.5 %all-gather.7.cloned.1.call-start = ((), (), s32[]{:S(2)}) async-start(), calls=%async_computation.4 | async-start | bytes 2785280 | tf_op jit(solution)/shard_map/all_gather | solution.py:33
  9.1 89.0 %all-gather.9.cloned.1.call-start = ((), (), s32[]{:S(2)}) async-start(), calls=%async_computation.5 | async-start | bytes 4718592 | tf_op jit(solution)/shard_map/all_gather | solution.py:37
  9.9 126.8 %all-gather.11.cloned.1.call-start = ((), (), s32[]{:S(2)}) async-start(), calls=%async_computation.6 | async-start | bytes 4718592 | tf_op jit(solution)/shard_map/all_gather | solution.py:38
  10.6 178.8 %reduce-scatter.5.cloned.1.call-start = ((), (), s32[]{:S(2)}) async-start(), calls=%async_computation.3 | async-start | bytes 1310720 | tf_op jit(solution)/shard_map/reduce_scatter | solution.py:54
  143.2 3.2 %copy-start = (bf16[256,8,2,512]{3,1,2,0:T(8,128)(2,1)S(1)}, bf16[256,8,2,512]{3,1,2,0:T(8,128)(2,1)}, u32[]{:S(2)}) copy-start(bf16[256,8,2,512]{3,1,2,0:T(8,128)(2,1)} %copy.11) | copy-start | bytes 12582916
  162.1 81.5 %reduce-scatter.3.cloned.1.call-start = ((), (), s32[]{:S(2)}) async-start(), calls=%async_computation.2 | async-start | bytes 4718592 | tf_op jit(solution)/shard_map/reduce_scatter | solution.py:48
Sparse Core Ops, SparseCore 0:
  9.6 51.0 all-gather.6
  62.5 35.5 all-gather.8
  100.0 36.7 all-gather.10
  162.2 27.1 reduce-scatter.4
  193.6 49.9 reduce-scatter.2

commit v2 on v1

--- a/solution.py
+++ b/solution.py
@@ -1,9 +1,18 @@
+import functools
 import math
 
 import jax
 import jax.numpy as jnp
 from jax import lax
+from jax.experimental import pallas as pl
+from jax.experimental.pallas import tpu as pltpu
 from jax.sharding import Mesh, PartitionSpec as P
+
+NEAR = 4
+AXES = ("far", "y", "x", "core")
+CONTRACT_LAST = (((1,), (1,)), ((), ()))
+CONTRACT_FIRST = (((0,), (0,)), ((), ()))
+VMEM_LIMIT = 56 * 1024 * 1024
 
 
 def gelu_parts(value):
@@ -17,15 +26,8 @@
     return (result, slope)
 
 
-NEAR = 4
-CONTRACT_LAST = (((1,), (1,)), ((), ()))
-CONTRACT_FIRST = (((0,), (0,)), ((), ()))
-
-
-def on_device(tokens, cotangent, w_in, b_in, w_out):
-    far = lax.axis_size("far")
-    near = lax.axis_size("near")
-    tensor = lax.axis_size("tensor")
+def on_device_any(tokens, cotangent, w_in, b_in, w_out):
+    far, near, tensor = lax.axis_size("far"), lax.axis_size("near"), lax.axis_size("tensor")
     rows, feats = tokens.shape
     owned, width = w_in.shape
     scale = 1.0 / math.sqrt(rows * far * near)
@@ -55,13 +57,262 @@
     return (mixed, grad_sum.astype(jnp.float32) * scale)
 
 
+def backward_kernel(far, owned, part, feats, *refs):
+    blocks = NEAR
+    tok_refs = refs[: 2 * blocks]
+    w_refs = refs[2 * blocks : 2 * blocks + 2 * far]
+    act_ref, mine_ref, other_ref = refs[2 * blocks + 2 * far : 2 * blocks + 2 * far + 3]
+    tok, cot, w_in, w_out, bias, dpre, tok_sem, cot_sem, in_sem, out_sem, bias_sem = refs[
+        2 * blocks + 2 * far + 3 :
+    ]
+    core = lax.axis_index("core")
+    tok_copies, cot_copies, in_copies, out_copies, bias_copies = [], [], [], [], []
+    for at, ref in enumerate(w_refs):
+        in_copies.append(
+            pltpu.make_async_copy(
+                ref.at[pl.ds(0, owned)], w_in.at[pl.ds(at * owned, owned)], in_sem.at[at]
+            )
+        )
+        bias_copies.append(
+            pltpu.make_async_copy(
+                ref.at[pl.ds(2 * owned, 16), pl.ds(0, owned)],
+                bias.at[:, pl.ds(at * owned, owned)],
+                bias_sem.at[at],
+            )
+        )
+        out_copies.append(
+            pltpu.make_async_copy(
+                ref.at[pl.ds(owned, owned)], w_out.at[pl.ds(at * owned, owned)], out_sem.at[at]
+            )
+        )
+    for at, ref in enumerate(tok_refs):
+        block, shift = at // 2, at % 2
+        source = lax.rem(core + shift, 2)
+        columns = pl.ds(pl.multiple_of(source * feats, feats), feats)
+        spot = pl.ds(block * part, part)
+        tok_copies.append(
+            pltpu.make_async_copy(ref.at[0], tok.at[spot, columns], tok_sem.at[at])
+        )
+        cot_copies.append(
+            pltpu.make_async_copy(ref.at[1], cot.at[spot, columns], cot_sem.at[at])
+        )
+    for copy in in_copies + bias_copies + tok_copies + out_copies + cot_copies:
+        copy.start()
+    for copy in in_copies + bias_copies + tok_copies + out_copies + cot_copies:
+        copy.wait()
+
+    @pl.loop(0, blocks)
+    def _(block):
+        spot = pl.ds(pl.multiple_of(block * part, part), part)
+        pre = lax.dot_general(
+            tok[spot, :], w_in[...], CONTRACT_LAST, preferred_element_type=jnp.float32
+        ) + bias[0:1, :].astype(jnp.float32)
+        value, slope = gelu_parts(pre)
+        act_ref[spot, :] = value.astype(jnp.bfloat16)
+        dact = lax.dot_general(
+            cot[spot, :], w_out[...], CONTRACT_LAST, preferred_element_type=jnp.float32
+        )
+        dpre[spot, :] = (dact * slope).astype(jnp.bfloat16)
+
+    @pl.loop(0, far)
+    def _(at):
+        units = pl.ds(pl.multiple_of(at * 2 * owned, 2 * owned), 2 * owned)
+        grad = lax.dot_general(
+            dpre[:, units], tok[...], CONTRACT_FIRST, preferred_element_type=jnp.float32
+        ).astype(jnp.bfloat16)
+        mine_ref[at] = grad[:owned]
+        other_ref[at] = grad[owned:]
+
+
+def project_kernel(far, owned, part, feats, *refs):
+    act_ref = refs[0]
+    w_refs = refs[1 : 1 + 2 * far]
+    out_refs = refs[1 + 2 * far : 1 + 2 * far + 2 * NEAR]
+    w_out, out_sem = refs[1 + 2 * far + 2 * NEAR :]
+    core = lax.axis_index("core")
+    copies = []
+    for at, ref in enumerate(w_refs):
+        copies.append(
+            pltpu.make_async_copy(
+                ref.at[pl.ds(owned, owned)], w_out.at[pl.ds(at * owned, owned)], out_sem.at[at]
+            )
+        )
+    for copy in copies:
+        copy.start()
+    for copy in copies:
+        copy.wait()
+    for shift in range(2):
+        half = lax.rem(core + shift, 2)
+        columns = pl.ds(pl.multiple_of(half * feats, feats), feats)
+        for block in range(NEAR):
+            out_refs[2 * block + shift][...] = jnp.dot(
+                act_ref[pl.ds(block * part, part), :],
+                w_out[:, columns],
+                preferred_element_type=jnp.float32,
+            ).astype(jnp.bfloat16)
+
+
+def pair_kernel(far, mine_ref, other_ref, *out_refs):
+    for at in range(far):
+        out_refs[at][...] = (
+            mine_ref[at].astype(jnp.float32) + other_ref[at].astype(jnp.float32)
+        ).astype(jnp.bfloat16)
+
+
+def sum_kernel(part, *refs):
+    out_ref = refs[-1]
+    core = lax.axis_index("core")
+    for shift in range(2):
+        total = refs[shift][...].astype(jnp.float32)
+        for block in range(1, NEAR):
+            total = total + refs[2 * block + shift][...].astype(jnp.float32)
+        spot = pl.ds(pl.multiple_of(lax.rem(core + shift, 2) * part, part), part)
+        out_ref[spot, :] = total.astype(jnp.bfloat16)
+
+
+def vmem(count):
+    return [pl.BlockSpec(memory_space=pltpu.VMEM)] * count
+
+
+def anywhere(count):
+    return [pl.BlockSpec(memory_space=pl.ANY)] * count
+
+
+def bf16(*shape):
+    return jax.ShapeDtypeStruct(shape, jnp.bfloat16)
+
+
+def on_device_pairs(sizes, tokens, cotangent, w_in, b_in, w_out):
+    far = sizes[0]
+    rows, feats = tokens.shape
+    owned, width = w_in.shape
+    part = rows // 2
+    units = far * 2 * owned
+    count = NEAR * part
+    scale = 1.0 / math.sqrt(rows * far * NEAR)
+    core = lax.axis_index("core")
+    params = pltpu.CompilerParams(vmem_limit_bytes=VMEM_LIMIT)
+
+    def move(value, d_far=0, d_y=0, d_x=0, d_core=0):
+        pairs = []
+        for f in range(far):
+            for y in range(2):
+                for x in range(2):
+                    for c in range(2):
+                        there = ((f + d_far) % far, (y + d_y) % 2, (x + d_x) % 2, (c + d_core) % 2)
+                        here = ((f * 2 + y) * 2 + x) * 2 + c
+                        pairs.append((here, ((there[0] * 2 + there[1]) * 2 + there[2]) * 2 + there[3]))
+        return lax.ppermute(value, AXES, pairs)
+
+    pieces = []
+    for shift in range(2):
+        start = lax.rem(core + shift, 2) * part
+        pieces.append(
+            jnp.stack(
+                [
+                    lax.dynamic_slice_in_dim(tokens, start, part, 0),
+                    lax.dynamic_slice_in_dim(cotangent, start, part, 0),
+                ]
+            )
+        )
+    bias_rows = jnp.pad(b_in.reshape(1, owned), ((0, 15), (0, width - owned)))
+    own_w = jnp.concatenate([w_in, w_out, bias_rows], 0)
+
+    x_same = move(pieces[0], d_x=1)
+    y_cross = move(pieces[1], d_y=1, d_core=1)
+    lines = [own_w] + [move(own_w, d_far=k) for k in range(1, far)]
+    x_cross = move(pieces[1], d_x=1, d_core=1)
+    y_same = move(pieces[0], d_y=1)
+    own_cross = move(pieces[1], d_core=1)
+    d_same = move(x_same, d_y=1)
+    d_cross = move(y_cross, d_x=1)
+    toks = [pieces[0], own_cross, x_same, x_cross, y_same, y_cross, d_same, d_cross]
+    weights = []
+    for line in lines:
+        weights += [line, move(line, d_core=1)]
+
+    dma = pltpu.SemaphoreType.DMA
+    act, mine, other = pl.pallas_call(
+        functools.partial(backward_kernel, far, owned, part, feats),
+        out_shape=(bf16(count, units), bf16(far, owned, width), bf16(far, owned, width)),
+        in_specs=anywhere(len(toks) + len(weights)),
+        out_specs=vmem(3),
+        scratch_shapes=[
+            pltpu.VMEM((count, width), jnp.bfloat16),
+            pltpu.VMEM((count, width), jnp.bfloat16),
+            pltpu.VMEM((units, width), jnp.bfloat16),
+            pltpu.VMEM((units, width), jnp.bfloat16),
+            pltpu.VMEM((16, units), jnp.bfloat16),
+            pltpu.VMEM((count, units), jnp.bfloat16),
+            dma((len(toks),)),
+            dma((len(toks),)),
+            dma((len(weights),)),
+            dma((len(weights),)),
+            dma((len(weights),)),
+        ],
+        compiler_params=params,
+        cost_estimate=pl.CostEstimate(
+            flops=6 * count * units * width, bytes_accessed=14 * count * width, transcendentals=0
+        ),
+        name="backward",
+    )(*toks, *weights)
+    other = move(other, d_core=1)
+
+    terms = pl.pallas_call(
+        functools.partial(project_kernel, far, owned, part, feats),
+        out_shape=[bf16(part, feats)] * (2 * NEAR),
+        in_specs=vmem(1) + anywhere(len(weights)),
+        out_specs=vmem(2 * NEAR),
+        scratch_shapes=[pltpu.VMEM((units, width), jnp.bfloat16), dma((len(weights),))],
+        compiler_params=params,
+        cost_estimate=pl.CostEstimate(
+            flops=2 * count * units * width, bytes_accessed=6 * count * width, transcendentals=0
+        ),
+        name="project",
+    )(act, *weights)
+    sent = []
+    for block, (d_x, d_y) in enumerate(((0, 0), (1, 0), (0, 1), (1, 1))):
+        for shift in range(2):
+            term = terms[2 * block + shift]
+            if block or shift:
+                term = move(term, d_x=d_x, d_y=d_y, d_core=shift)
+            sent.append(term)
+
+    sums = pl.pallas_call(
+        functools.partial(pair_kernel, far),
+        out_shape=[bf16(owned, width)] * far,
+        in_specs=vmem(2),
+        out_specs=vmem(far),
+        compiler_params=params,
+        name="pair_sum",
+    )(mine, other)
+    total = sums[0].astype(jnp.float32)
+    for k in range(1, far):
+        total = total + move(sums[k], d_far=-k).astype(jnp.float32)
+    mixed = pl.pallas_call(
+        functools.partial(sum_kernel, part),
+        out_shape=bf16(rows, feats),
+        in_specs=vmem(2 * NEAR),
+        out_specs=pl.BlockSpec(memory_space=pltpu.VMEM),
+        compiler_params=params,
+        name="mixed_sum",
+    )(*sent)
+    return (mixed, total * scale)
+
+
 def solution(mesh):
     dp, tensor = mesh.shape["dp"], mesh.shape["tensor"]
-    fine = Mesh(mesh.devices.reshape(dp // NEAR, NEAR, tensor), ("far", "near", "tensor"))
-    rows = ("far", "near")
-    owners = ("far", "near", "tensor")
-    in_specs = (P(rows, "tensor"), P(rows, "tensor"), P(owners, None), P(owners), P(owners, None))
-    out_specs = (P(rows, "tensor"), P(owners, None))
+    far = dp // NEAR
+    if tensor == 2 and far <= 4:
+        fine = Mesh(mesh.devices.reshape(far, 2, 2, tensor), AXES)
+        rows, owners, halves = ("far", "y", "x"), AXES, "core"
+        body = functools.partial(on_device_pairs, (far,))
+    else:
+        fine = Mesh(mesh.devices.reshape(far, NEAR, tensor), ("far", "near", "tensor"))
+        rows, owners, halves = ("far", "near"), ("far", "near", "tensor"), "tensor"
+        body = on_device_any
+    in_specs = (P(rows, halves), P(rows, halves), P(owners, None), P(owners), P(owners, None))
+    out_specs = (P(rows, halves), P(owners, None))
     return jax.shard_map(
-        on_device, mesh=fine, in_specs=in_specs, out_specs=out_specs, check_vma=False
+        body, mesh=fine, in_specs=in_specs, out_specs=out_specs, check_vma=False
     )

time: 251 us -> 139 us (0.55)
  waiting for transfers between devices: 175 us -> 77.9 us
  local copies, waits for them, and re-layouts: 33.8 us -> 4.5 us
  starting transfers between devices: 0.2 us -> 29.3 us
  Pallas kernels: 0 us -> 25.2 us
  matrix products: 23 us -> 0 us
  between operations: 13.8 us -> 0.95 us
  other arithmetic: 4.39 us -> 1.1 us
    all_gather x3 -> x0, waiting for transfers between devices: 114 us -> none  [the longest x1 50 us: on_device(): lax.all_gather(jnp.concatenate([w_in, w_out, bias_rows], 0), 'far', axis=0)]
    ppermute x0 -> x25, waiting for transfers between devices: none -> 77.9 us  [move(): return lax.ppermute(value, AXES, pairs)]
    reduce_scatter x2 -> x0, waiting for transfers between devices: 59.5 us -> none  [the longest x1 52.3 us: on_device(): lax.psum_scatter(term.reshape(near * tensor, rows, feats), ('near', 'tens...]
    ppermute x0 -> x25, starting transfers between devices: none -> 29.3 us  [move(): return lax.ppermute(value, AXES, pairs)]
    pallas_call x0 -> x4, Pallas kernels: none -> 25.2 us  [the longest x1 13.8 us: on_device_pairs(): pl.pallas_call(functools.partial(backward_kernel, far, owned, part, feats...]
    dot_general x3 -> x0, matrix products: 23 us -> none  [the longest x1 11.2 us: on_device(): lax.dot_general(dpre, tok_full, CONTRACT_FIRST, preferred_element_type=jn...]
    reshape x3 -> x0, local copies, waits for them, and re-layouts: 20.9 us -> none  [the longest x1 7.86 us: on_device(): term = term.reshape(near, rows, tensor, feats).transpose(0, 2, 1, 3)]
    transpose x1 -> x0, local copies, waits for them, and re-layouts: 4.92 us -> none  [on_device(): term = term.reshape(near, rows, tensor, feats).transpose(0, 2, 1, 3)]
  transfers between devices with their start and end apart: 5 -> 25, of which waited for: 5 -> 10; matrix products, arithmetic and copies ran while one was open for 14% -> 0% of each run, Pallas kernels for 0% -> 8%
where the time goes in v2:
time: 139 us
  waiting for transfers between devices  77.9 us (56%)
  starting transfers between devices  29.3 us (21%)
  Pallas kernels  25.2 us (18%)
  local copies, waits for them, and re-layouts  4.5 us (3%)
    ppermute x25, waiting for transfers between devices, move(): return lax.ppermute(value, AXES, pairs)  77.9 us
    ppermute x25, starting transfers between devices, move(): return lax.ppermute(value, AXES, pairs)  29.3 us
    pallas_call x1, Pallas kernels, on_device_pairs(): pl.pallas_call(functools.partial(backward_kernel, far, owned, part, feats...  13.8 us
    pallas_call x1, Pallas kernels, on_device_pairs(): pl.pallas_call(functools.partial(project_kernel, far, owned, part, feats)...  6.27 us
    unnamed x60, local copies, waits for them, and re-layouts  3.23 us
  transfers between devices with their start and end apart: 25, of which 10 were waited for; matrix products, arithmetic and copies ran while one was open for 0% of the time, Pallas kernels for 8%

profile of v2, /device:TPU:0, one launch (start us, length us, event | category | flops | bytes accessed | tf_op | source)
XLA Modules:
  0.0 138.9 jit_solution(13821546328361056433)
XLA Ops:
  0.6 1.3 dynamic-slice_bitcast_fusion
  2.0 3.0 %collective-permute-start.3 = (bf16[2,256,512]{2,1,0:T(8,128)(2,1)S(1)}, bf16[2,256,512]{2,1,0:T(8,128)(2,1)S(1)}, u32[]{:S(2)}, u32[]{:S(2)}) collective-permute-start(bf16[2,256,512]{2,1,0:T(8,128)(2,1)S(1)} %pad_maximum_fusion.refs_0_), channel_id=1, source_target_pairs={{0,4},{1,5},{2,6},{3,7},{4,0},{5,1},{6,2},{7,3},{8,12},{9,13},{10,... | collective-permute-start | bytes 1572872 | tf_op jit(solution)/shard_map/ppermute | solution.py:205
  5.0 1.5 %collective-permute-start.1 = (bf16[2,256,512]{2,1,0:T(8,128)(2,1)S(1)}, bf16[2,256,512]{2,1,0:T(8,128)(2,1)S(1)}, u32[]{:S(2)}, u32[]{:S(2)}) collective-permute-start(bf16[2,256,512]{2,1,0:T(8,128)(2,1)S(1)} %pad_maximum_fusion.refs_0_), channel_id=1, source_target_pairs={{0,2},{1,3},{2,0},{3,1},{4,6},{5,7},{6,4},{7,5},{8,10},{9,11},{10,... | collective-permute-start | bytes 1572872 | tf_op jit(solution)/shard_map/ppermute | solution.py:205
  7.1 4.1 %collective-permute-start.12 = (bf16[272,1024]{1,0:T(8,128)(2,1)S(1)}, bf16[272,1024]{1,0:T(8,128)(2,1)S(1)}, u32[]{:S(2)}, u32[]{:S(2)}) collective-permute-start(bf16[272,1024]{1,0:T(8,128)(2,1)S(1)} %fusion.1.refs_8_.refs_1_), channel_id=1, source_target_pairs={{0,24},{1,25},{2,26},{3,27},{4,28},{5,29},{6,30},{7,31},{8,0},{9,1... | collective-permute-start | bytes 1671176 | tf_op jit(solution)/shard_map/ppermute | solution.py:205
  11.1 6.7 %collective-permute-done.3.refs_4_ = bf16[2,256,512]{2,1,0:T(8,128)(2,1)S(1)} collective-permute-done((bf16[2,256,512]{2,1,0:T(8,128)(2,1)S(1)}, bf16[2,256,512]{2,1,0:T(8,128)(2,1)S(1)}, u32[]{:S(2)}, u32[]{:S(2)}) %collective-permute-start.3) | collective-permute-done | bytes 524320 | tf_op jit(solution)/shard_map/ppermute | solution.py:205
  17.8 3.1 %collective-permute-start.10 = (bf16[272,1024]{1,0:T(8,128)(2,1)S(1)}, bf16[272,1024]{1,0:T(8,128)(2,1)S(1)}, u32[]{:S(2)}, u32[]{:S(2)}) collective-permute-start(bf16[272,1024]{1,0:T(8,128)(2,1)S(1)} %fusion.1.refs_8_.refs_1_), channel_id=1, source_target_pairs={{0,16},{1,17},{2,18},{3,19},{4,20},{5,21},{6,22},{7,23},{8,24},{9,... | collective-permute-start | bytes 1671176 | tf_op jit(solution)/shard_map/ppermute | solution.py:205
  20.9 1.6 %collective-permute-start.8 = (bf16[272,1024]{1,0:T(8,128)(2,1)S(1)}, bf16[272,1024]{1,0:T(8,128)(2,1)S(1)}, u32[]{:S(2)}, u32[]{:S(2)}) collective-permute-start(bf16[272,1024]{1,0:T(8,128)(2,1)S(1)} %fusion.1.refs_8_.refs_1_), channel_id=1, source_target_pairs={{0,8},{1,9},{2,10},{3,11},{4,12},{5,13},{6,14},{7,15},{8,16},{9,17... | collective-permute-start | bytes 1671176 | tf_op jit(solution)/shard_map/ppermute | solution.py:205
  22.5 5.0 %collective-permute-done.4.refs_5_ = bf16[2,256,512]{2,1,0:T(8,128)(2,1)S(1)} collective-permute-done((bf16[2,256,512]{2,1,0:T(8,128)(2,1)S(1)}, bf16[2,256,512]{2,1,0:T(8,128)(2,1)S(1)}, u32[]{:S(2)}, u32[]{:S(2)}) %collective-permute-start.4) | collective-permute-done | bytes 524320 | tf_op jit(solution)/shard_map/ppermute | solution.py:205
  27.5 0.9 collective-permute-start.7
  28.7 1.1 collective-permute-start
  29.9 29.0 %collective-permute-done.10.refs_12_.refs_5_ = bf16[272,1024]{1,0:T(8,128)(2,1)S(1)} collective-permute-done((bf16[272,1024]{1,0:T(8,128)(2,1)S(1)}, bf16[272,1024]{1,0:T(8,128)(2,1)S(1)}, u32[]{:S(2)}, u32[]{:S(2)}) %collective-permute-start.10) | collective-permute-done | bytes 557088 | tf_op jit(solution)/shard_map/ppermute | solution.py:205
  59.4 1.4 %collective-permute-start.5 = (bf16[2,256,512]{2,1,0:T(8,128)(2,1)S(1)}, bf16[2,256,512]{2,1,0:T(8,128)(2,1)S(1)}, u32[]{:S(2)}, u32[]{:S(2)}) collective-permute-start(bf16[2,256,512]{2,1,0:T(8,128)(2,1)S(1)} %collective-permute-done.1.refs_2_), channel_id=1, source_target_pairs={{0,4},{1,5},{2,6},{3,7},{4,0},{5,1},{6,2},{7,3},{8,12},{9,13},{10,... | collective-permute-start | bytes 1572872 | tf_op jit(solution)/shard_map/ppermute | solution.py:205
  60.8 0.9 collective-permute-start.6
  61.7 11.6 %collective-permute-done.5.refs_6_ = bf16[2,256,512]{2,1,0:T(8,128)(2,1)S(1)} collective-permute-done((bf16[2,256,512]{2,1,0:T(8,128)(2,1)S(1)}, bf16[2,256,512]{2,1,0:T(8,128)(2,1)S(1)}, u32[]{:S(2)}, u32[]{:S(2)}) %collective-permute-start.5) | collective-permute-done | bytes 524320 | tf_op jit(solution)/shard_map/ppermute | solution.py:205
  73.3 1.2 collective-permute-done.6.refs_7_
  74.5 0.8 copy-done.27
  76.1 0.8 copy-done.20
  77.0 13.8 %backward.1 = (bf16[1024,1024]{1,0:T(8,128)(2,1)}, bf16[4,128,1024]{2,1,0:T(8,128)(2,1)}, bf16[4,128,1024]{2,1,0:T(8,128)(2,1)}) custom-call(bf16[2,256,512]{2,1,0:T(8,128)(2,1)} %copy-done.2, bf16[2,256,512]{2,1,0:T(8,128)(2,1)} %copy-done.25, bf16[2,256,512]{2,1,0:T(8,128)(2,1)} %copy-done.22, bf16[2,256,512]{2,1,0:T(8,128)(2,1)} %copy-done.24, ...), custom_call_target="tpu_custom_call" | custom-call | flops 6442450944 | bytes 14680064 | tf_op jit(solution)/shard_map/backward/pallas_call | solution.py:235
  90.8 6.3 %project.1 = (bf16[256,512]{1,0:T(8,128)(2,1)}, bf16[256,512]{1,0:T(8,128)(2,1)}, bf16[256,512]{1,0:T(8,128)(2,1)}, bf16[256,512]{1,0:T(8,128)(2,1)}, bf16[256,5...) custom-call(bf16[1024,1024]{1,0:T(8,128)(2,1)} %get-tuple-element.17.refs_0_, ...), custom_call_target="tpu_custom_call" | custom-call | flops 2147483648 | bytes 6291456 | tf_op jit(solution)/shard_map/project/pallas_call | solution.py:261
  97.7 0.9 collective-permute-start.15
  99.1 0.7 collective-permute-start.17
  99.8 1.4 %collective-permute-start.18 = (bf16[256,512]{1,0:T(8,128)(2,1)}, bf16[256,512]{1,0:T(8,128)(2,1)S(1)}, u32[]{:S(2)}, u32[]{:S(2)}) collective-permute-start(bf16[256,512]{1,0:T(8,128)(2,1)} %get-tuple-element.23), channel_id=1, source_target_pairs={{0,5},{1,4},{2,7},{3,6},{4,1},{5,0},{6,3},{7,2},{8,13},{9,12},{10,... | collective-permute-start | bytes 786440 | tf_op jit(solution)/shard_map/ppermute | solution.py:205
  101.2 2.6 %pair_sum.1 = (bf16[128,1024]{1,0:T(8,128)(2,1)}, bf16[128,1024]{1,0:T(8,128)(2,1)}, bf16[128,1024]{1,0:T(8,128)(2,1)}, bf16[128,1024]{1,0:T(8,128)(2,1)}) custom-call(bf16[4,128,1024]{2,1,0:T(8,128)(2,1)} %get-tuple-element.26.mine_ref, bf16[4,128,1024]{2,1,0:T(8,128)(2,1)} %copy-done), custom_call_target="tpu_custom_call" | custom-call | tf_op jit(solution)/shard_map/pair_sum/pallas_call | solution.py:281
  103.8 1.6 %collective-permute-start.19 = (bf16[256,512]{1,0:T(8,128)(2,1)S(1)}, bf16[256,512]{1,0:T(8,128)(2,1)S(1)}, u32[]{:S(2)}, u32[]{:S(2)}) collective-permute-start(bf16[256,512]{1,0:T(8,128)(2,1)S(1)} %copy-done.29), channel_id=1, source_target_pairs={{0,6},{1,7},{2,4},{3,5},{4,2},{5,3},{6,0},{7,1},{8,14},{9,15},{10,... | collective-permute-start | bytes 786440 | tf_op jit(solution)/shard_map/ppermute | solution.py:205
  105.3 1.7 %collective-permute-done.15.refs_2_ = bf16[256,512]{1,0:T(8,128)(2,1)S(1)} collective-permute-done((bf16[256,512]{1,0:T(8,128)(2,1)}, bf16[256,512]{1,0:T(8,128)(2,1)S(1)}, u32[]{:S(2)}, u32[]{:S(2)}) %collective-permute-start.15) | collective-permute-done | bytes 262176 | tf_op jit(solution)/shard_map/ppermute | solution.py:205
  107.0 4.2 %collective-permute-done.16.refs_3_ = bf16[256,512]{1,0:T(8,128)(2,1)S(1)} collective-permute-done((bf16[256,512]{1,0:T(8,128)(2,1)}, bf16[256,512]{1,0:T(8,128)(2,1)S(1)}, u32[]{:S(2)}, u32[]{:S(2)}) %collective-permute-start.16) | collective-permute-done | bytes 262176 | tf_op jit(solution)/shard_map/ppermute | solution.py:205
  111.2 3.5 %collective-permute-start.23 = (bf16[128,1024]{1,0:T(8,128)(2,1)}, bf16[128,1024]{1,0:T(8,128)(2,1)S(1)}, u32[]{:S(2)}, u32[]{:S(2)}) collective-permute-start(bf16[128,1024]{1,0:T(8,128)(2,1)} %get-tuple-element.30), channel_id=1, source_target_pairs={{0,16},{1,17},{2,18},{3,19},{4,20},{5,21},{6,22},{7,23},{8,24},{9,... | collective-permute-start | bytes 786440 | tf_op jit(solution)/shard_map/ppermute | solution.py:205
  114.7 10.1 %collective-permute-done.18.refs_5_ = bf16[256,512]{1,0:T(8,128)(2,1)S(1)} collective-permute-done((bf16[256,512]{1,0:T(8,128)(2,1)}, bf16[256,512]{1,0:T(8,128)(2,1)S(1)}, u32[]{:S(2)}, u32[]{:S(2)}) %collective-permute-start.18) | collective-permute-done | bytes 262176 | tf_op jit(solution)/shard_map/ppermute | solution.py:205
  124.8 1.5 %collective-permute-start.24 = (bf16[128,1024]{1,0:T(8,128)(2,1)}, bf16[128,1024]{1,0:T(8,128)(2,1)S(1)}, u32[]{:S(2)}, u32[]{:S(2)}) collective-permute-start(bf16[128,1024]{1,0:T(8,128)(2,1)} %get-tuple-element.31), channel_id=1, source_target_pairs={{0,8},{1,9},{2,10},{3,11},{4,12},{5,13},{6,14},{7,15},{8,16},{9,17... | collective-permute-start | bytes 786440 | tf_op jit(solution)/shard_map/ppermute | solution.py:205
  127.2 2.6 %mixed_sum.1 = bf16[512,512]{1,0:T(8,128)(2,1)} custom-call(bf16[256,512]{1,0:T(8,128)(2,1)} %get-tuple-element.18.refs_0_, bf16[256,512]{1,0:T(8,128)(2,1)} %copy-done.3, bf16[256,512]{1,0:T(8,128)(2,1)} %copy-done.4, bf16[256,512]{1,0:T(8,128)(2,1)} %copy-done.5, bf16[256,512]{1,0:T(8,128)(2,1)} %copy-done.6, bf16[256,512]{1,0:T(8,128)(2,1)} %copy-done.7, ...), custom_call_target="tpu_custom_call" | custom-call | tf_op jit(solution)/shard_map/mixed_sum/pallas_call | solution.py:292
  129.8 8.2 %collective-permute-done.23 = bf16[128,1024]{1,0:T(8,128)(2,1)S(1)} collective-permute-done((bf16[128,1024]{1,0:T(8,128)(2,1)}, bf16[128,1024]{1,0:T(8,128)(2,1)S(1)}, u32[]{:S(2)}, u32[]{:S(2)}) %collective-permute-start.23) | collective-permute-done | bytes 262176 | tf_op jit(solution)/shard_map/ppermute | solution.py:205
  137.9 1.0 add_multiply_fusion
  (87 shorter events, 4.2 us)
Async XLA Ops:
  2.0 73.3 %copy-start.2 = (bf16[2,256,512]{2,1,0:T(8,128)(2,1)}, bf16[2,256,512]{2,1,0:T(8,128)(2,1)S(1)}, u32[]{:S(2)}) copy-start(bf16[2,256,512]{2,1,0:T(8,128)(2,1)S(1)} %pad_maximum_fusion.refs_0_) | copy-start | bytes 1572868
  2.0 15.8 %collective-permute-start.3 = (bf16[2,256,512]{2,1,0:T(8,128)(2,1)S(1)}, bf16[2,256,512]{2,1,0:T(8,128)(2,1)S(1)}, u32[]{:S(2)}, u32[]{:S(2)}) collective-permute-start(bf16[2,256,512]{2,1,0:T(8,128)(2,1)S(1)} %pad_maximum_fusion.refs_0_), channel_id=1, source_target_pairs={{0,4},{1,5},{2,6},{3,7},{4,0},{5,1},{6,2},{7,3},{8,12},{9,13},{10,... | collective-permute-start | bytes 1572872 | tf_op jit(solution)/shard_map/ppermute | solution.py:205
  5.0 15.9 %collective-permute-start.1 = (bf16[2,256,512]{2,1,0:T(8,128)(2,1)S(1)}, bf16[2,256,512]{2,1,0:T(8,128)(2,1)S(1)}, u32[]{:S(2)}, u32[]{:S(2)}) collective-permute-start(bf16[2,256,512]{2,1,0:T(8,128)(2,1)S(1)} %pad_maximum_fusion.refs_0_), channel_id=1, source_target_pairs={{0,2},{1,3},{2,0},{3,1},{4,6},{5,7},{6,4},{7,5},{8,10},{9,11},{10,... | collective-permute-start | bytes 1572872 | tf_op jit(solution)/shard_map/ppermute | solution.py:205
  6.6 20.9 %collective-permute-start.4 = (bf16[2,256,512]{2,1,0:T(8,128)(2,1)S(1)}, bf16[2,256,512]{2,1,0:T(8,128)(2,1)S(1)}, u32[]{:S(2)}, u32[]{:S(2)}) collective-permute-start(bf16[2,256,512]{2,1,0:T(8,128)(2,1)S(1)} %pad_maximum_fusion.1), channel_id=1, source_target_pairs={{0,5},{1,4},{2,7},{3,6},{4,1},{5,0},{6,3},{7,2},{8,13},{9,12},{10,... | collective-permute-start | bytes 1572872 | tf_op jit(solution)/shard_map/ppermute | solution.py:205
  6.7 22.0 %collective-permute-start.2 = (bf16[2,256,512]{2,1,0:T(8,128)(2,1)S(1)}, bf16[2,256,512]{2,1,0:T(8,128)(2,1)S(1)}, u32[]{:S(2)}, u32[]{:S(2)}) collective-permute-start(bf16[2,256,512]{2,1,0:T(8,128)(2,1)S(1)} %pad_maximum_fusion.1), channel_id=1, source_target_pairs={{0,3},{1,2},{2,1},{3,0},{4,7},{5,6},{6,5},{7,4},{8,11},{9,10},{10,... | collective-permute-start | bytes 1572872 | tf_op jit(solution)/shard_map/ppermute | solution.py:205
  7.0 68.2 %copy-start.1 = (bf16[272,1024]{1,0:T(8,128)(2,1)}, bf16[272,1024]{1,0:T(8,128)(2,1)S(1)}, u32[]{:S(2)}) copy-start(bf16[272,1024]{1,0:T(8,128)(2,1)S(1)} %fusion.1.refs_8_.refs_1_) | copy-start | bytes 1671172
  7.1 22.7 %collective-permute-start.12 = (bf16[272,1024]{1,0:T(8,128)(2,1)S(1)}, bf16[272,1024]{1,0:T(8,128)(2,1)S(1)}, u32[]{:S(2)}, u32[]{:S(2)}) collective-permute-start(bf16[272,1024]{1,0:T(8,128)(2,1)S(1)} %fusion.1.refs_8_.refs_1_), channel_id=1, source_target_pairs={{0,24},{1,25},{2,26},{3,27},{4,28},{5,29},{6,30},{7,31},{8,0},{9,1... | collective-permute-start | bytes 1671176 | tf_op jit(solution)/shard_map/ppermute | solution.py:205
  17.8 57.5 %copy-start.21 = (bf16[2,256,512]{2,1,0:T(8,128)(2,1)}, bf16[2,256,512]{2,1,0:T(8,128)(2,1)S(1)}, u32[]{:S(2)}) copy-start(bf16[2,256,512]{2,1,0:T(8,128)(2,1)S(1)} %collective-permute-done.3.refs_4_) | copy-start | bytes 1572868
  17.8 41.1 %collective-permute-start.10 = (bf16[272,1024]{1,0:T(8,128)(2,1)S(1)}, bf16[272,1024]{1,0:T(8,128)(2,1)S(1)}, u32[]{:S(2)}, u32[]{:S(2)}) collective-permute-start(bf16[272,1024]{1,0:T(8,128)(2,1)S(1)} %fusion.1.refs_8_.refs_1_), channel_id=1, source_target_pairs={{0,16},{1,17},{2,18},{3,19},{4,20},{5,21},{6,22},{7,23},{8,24},{9,... | collective-permute-start | bytes 1671176 | tf_op jit(solution)/shard_map/ppermute | solution.py:205
  20.9 54.4 %copy-start.22 = (bf16[2,256,512]{2,1,0:T(8,128)(2,1)}, bf16[2,256,512]{2,1,0:T(8,128)(2,1)S(1)}, u32[]{:S(2)}) copy-start(bf16[2,256,512]{2,1,0:T(8,128)(2,1)S(1)} %collective-permute-done.1.refs_2_) | copy-start | bytes 1572868
  20.9 37.9 %collective-permute-start.8 = (bf16[272,1024]{1,0:T(8,128)(2,1)S(1)}, bf16[272,1024]{1,0:T(8,128)(2,1)S(1)}, u32[]{:S(2)}, u32[]{:S(2)}) collective-permute-start(bf16[272,1024]{1,0:T(8,128)(2,1)S(1)} %fusion.1.refs_8_.refs_1_), channel_id=1, source_target_pairs={{0,8},{1,9},{2,10},{3,11},{4,12},{5,13},{6,14},{7,15},{8,16},{9,17... | collective-permute-start | bytes 1671176 | tf_op jit(solution)/shard_map/ppermute | solution.py:205
  27.5 47.8 %copy-start.23 = (bf16[2,256,512]{2,1,0:T(8,128)(2,1)}, bf16[2,256,512]{2,1,0:T(8,128)(2,1)S(1)}, u32[]{:S(2)}) copy-start(bf16[2,256,512]{2,1,0:T(8,128)(2,1)S(1)} %collective-permute-done.4.refs_5_) | copy-start | bytes 1572868
  27.5 33.3 %collective-permute-start.7 = (bf16[272,1024]{1,0:T(8,128)(2,1)S(1)}, bf16[272,1024]{1,0:T(8,128)(2,1)S(1)}, u32[]{:S(2)}, u32[]{:S(2)}) collective-permute-start(bf16[272,1024]{1,0:T(8,128)(2,1)S(1)} %fusion.1.refs_8_.refs_1_), channel_id=1, source_target_pairs={{0,1},{1,0},{2,3},{3,2},{4,5},{5,4},{6,7},{7,6},{8,9},{9,8},{10,11... | collective-permute-start | bytes 1671176 | tf_op jit(solution)/shard_map/ppermute | solution.py:205
  28.7 46.6 %copy-start.24 = (bf16[2,256,512]{2,1,0:T(8,128)(2,1)}, bf16[2,256,512]{2,1,0:T(8,128)(2,1)S(1)}, u32[]{:S(2)}) copy-start(bf16[2,256,512]{2,1,0:T(8,128)(2,1)S(1)} %collective-permute-done.2.refs_3_) | copy-start | bytes 1572868
  28.7 30.7 %collective-permute-start = (bf16[2,256,512]{2,1,0:T(8,128)(2,1)S(1)}, bf16[2,256,512]{2,1,0:T(8,128)(2,1)S(1)}, u32[]{:S(2)}, u32[]{:S(2)}) collective-permute-start(bf16[2,256,512]{2,1,0:T(8,128)(2,1)S(1)} %pad_maximum_fusion.1), channel_id=1, source_target_pairs={{0,1},{1,0},{2,3},{3,2},{4,5},{5,4},{6,7},{7,6},{8,9},{9,8},{10,11... | collective-permute-start | bytes 1572872 | tf_op jit(solution)/shard_map/ppermute | solution.py:205
  29.8 45.5 %copy-start.14 = (bf16[272,1024]{1,0:T(8,128)(2,1)}, bf16[272,1024]{1,0:T(8,128)(2,1)S(1)}, u32[]{:S(2)}) copy-start(bf16[272,1024]{1,0:T(8,128)(2,1)S(1)} %collective-permute-done.12.refs_14_.refs_7_) | copy-start | bytes 1671172
  29.8 44.7 %collective-permute-start.13 = (bf16[272,1024]{1,0:T(8,128)(2,1)S(1)}, bf16[272,1024]{1,0:T(8,128)(2,1)S(1)}, u32[]{:S(2)}, u32[]{:S(2)}) collective-permute-start(bf16[272,1024]{1,0:T(8,128)(2,1)S(1)} %collective-permute-done.12.refs_14_.refs_7_), channel_id=1, source_target_pairs={{0,1},{1,0},{2,3},{3,2},{4,5},{5,4},{6,7},{7,6},{8,9},{9,8},{10,11... | collective-permute-start | bytes 1671176 | tf_op jit(solution)/shard_map/ppermute | solution.py:205
  58.9 15.6 %collective-permute-start.11 = (bf16[272,1024]{1,0:T(8,128)(2,1)S(1)}, bf16[272,1024]{1,0:T(8,128)(2,1)S(1)}, u32[]{:S(2)}, u32[]{:S(2)}) collective-permute-start(bf16[272,1024]{1,0:T(8,128)(2,1)S(1)} %collective-permute-done.10.refs_12_.refs_5_), channel_id=1, source_target_pairs={{0,1},{1,0},{2,3},{3,2},{4,5},{5,4},{6,7},{7,6},{8,9},{9,8},{10,11... | collective-permute-start | bytes 1671176 | tf_op jit(solution)/shard_map/ppermute | solution.py:205
  58.9 16.4 %collective-permute-start.9 = (bf16[272,1024]{1,0:T(8,128)(2,1)S(1)}, bf16[272,1024]{1,0:T(8,128)(2,1)S(1)}, u32[]{:S(2)}, u32[]{:S(2)}) collective-permute-start(bf16[272,1024]{1,0:T(8,128)(2,1)S(1)} %collective-permute-done.8.refs_10_.refs_3_), channel_id=1, source_target_pairs={{0,1},{1,0},{2,3},{3,2},{4,5},{5,4},{6,7},{7,6},{8,9},{9,8},{10,11... | collective-permute-start | bytes 1671176 | tf_op jit(solution)/shard_map/ppermute | solution.py:205
  59.4 13.9 %collective-permute-start.5 = (bf16[2,256,512]{2,1,0:T(8,128)(2,1)S(1)}, bf16[2,256,512]{2,1,0:T(8,128)(2,1)S(1)}, u32[]{:S(2)}, u32[]{:S(2)}) collective-permute-start(bf16[2,256,512]{2,1,0:T(8,128)(2,1)S(1)} %collective-permute-done.1.refs_2_), channel_id=1, source_target_pairs={{0,4},{1,5},{2,6},{3,7},{4,0},{5,1},{6,2},{7,3},{8,12},{9,13},{10,... | collective-permute-start | bytes 1572872 | tf_op jit(solution)/shard_map/ppermute | solution.py:205
  60.8 13.6 %collective-permute-start.6 = (bf16[2,256,512]{2,1,0:T(8,128)(2,1)S(1)}, bf16[2,256,512]{2,1,0:T(8,128)(2,1)S(1)}, u32[]{:S(2)}, u32[]{:S(2)}) collective-permute-start(bf16[2,256,512]{2,1,0:T(8,128)(2,1)S(1)} %collective-permute-done.4.refs_5_), channel_id=1, source_target_pairs={{0,2},{1,3},{2,0},{3,1},{4,6},{5,7},{6,4},{7,5},{8,10},{9,11},{10,... | collective-permute-start | bytes 1572872 | tf_op jit(solution)/shard_map/ppermute | solution.py:205
  90.7 9.0 %collective-permute-start.21 = (bf16[4,128,1024]{2,1,0:T(8,128)(2,1)}, bf16[4,128,1024]{2,1,0:T(8,128)(2,1)S(1)}, u32[]{:S(2)}, u32[]{:S(2)}) collective-permute-start(bf16[4,128,1024]{2,1,0:T(8,128)(2,1)} %get-tuple-element.27), channel_id=1, source_target_pairs={{0,1},{1,0},{2,3},{3,2},{4,5},{5,4},{6,7},{7,6},{8,9},{9,8},{10,11... | collective-permute-start | bytes 3145736 | tf_op jit(solution)/shard_map/ppermute | solution.py:205
  97.1 6.6 %collective-permute-start.14 = (bf16[256,512]{1,0:T(8,128)(2,1)}, bf16[256,512]{1,0:T(8,128)(2,1)S(1)}, u32[]{:S(2)}, u32[]{:S(2)}) collective-permute-start(bf16[256,512]{1,0:T(8,128)(2,1)} %get-tuple-element.19), channel_id=1, source_target_pairs={{0,1},{1,0},{2,3},{3,2},{4,5},{5,4},{6,7},{7,6},{8,9},{9,8},{10,11... | collective-permute-start | bytes 786440 | tf_op jit(solution)/shard_map/ppermute | solution.py:205
  97.7 9.4 %collective-permute-start.15 = (bf16[256,512]{1,0:T(8,128)(2,1)}, bf16[256,512]{1,0:T(8,128)(2,1)S(1)}, u32[]{:S(2)}, u32[]{:S(2)}) collective-permute-start(bf16[256,512]{1,0:T(8,128)(2,1)} %get-tuple-element.20), channel_id=1, source_target_pairs={{0,2},{1,3},{2,0},{3,1},{4,6},{5,7},{6,4},{7,5},{8,10},{9,11},{10,... | collective-permute-start | bytes 786440 | tf_op jit(solution)/shard_map/ppermute | solution.py:205
  98.6 12.6 %collective-permute-start.16 = (bf16[256,512]{1,0:T(8,128)(2,1)}, bf16[256,512]{1,0:T(8,128)(2,1)S(1)}, u32[]{:S(2)}, u32[]{:S(2)}) collective-permute-start(bf16[256,512]{1,0:T(8,128)(2,1)} %get-tuple-element.21), channel_id=1, source_target_pairs={{0,3},{1,2},{2,1},{3,0},{4,7},{5,6},{6,5},{7,4},{8,11},{9,10},{10,... | collective-permute-start | bytes 786440 | tf_op jit(solution)/shard_map/ppermute | solution.py:205
  99.1 12.1 %collective-permute-start.17 = (bf16[256,512]{1,0:T(8,128)(2,1)}, bf16[256,512]{1,0:T(8,128)(2,1)S(1)}, u32[]{:S(2)}, u32[]{:S(2)}) collective-permute-start(bf16[256,512]{1,0:T(8,128)(2,1)} %get-tuple-element.22), channel_id=1, source_target_pairs={{0,4},{1,5},{2,6},{3,7},{4,0},{5,1},{6,2},{7,3},{8,12},{9,13},{10,... | collective-permute-start | bytes 786440 | tf_op jit(solution)/shard_map/ppermute | solution.py:205
  99.8 25.1 %collective-permute-start.18 = (bf16[256,512]{1,0:T(8,128)(2,1)}, bf16[256,512]{1,0:T(8,128)(2,1)S(1)}, u32[]{:S(2)}, u32[]{:S(2)}) collective-permute-start(bf16[256,512]{1,0:T(8,128)(2,1)} %get-tuple-element.23), channel_id=1, source_target_pairs={{0,5},{1,4},{2,7},{3,6},{4,1},{5,0},{6,3},{7,2},{8,13},{9,12},{10,... | collective-permute-start | bytes 786440 | tf_op jit(solution)/shard_map/ppermute | solution.py:205
  103.8 22.6 %collective-permute-start.19 = (bf16[256,512]{1,0:T(8,128)(2,1)S(1)}, bf16[256,512]{1,0:T(8,128)(2,1)S(1)}, u32[]{:S(2)}, u32[]{:S(2)}) collective-permute-start(bf16[256,512]{1,0:T(8,128)(2,1)S(1)} %copy-done.29), channel_id=1, source_target_pairs={{0,6},{1,7},{2,4},{3,5},{4,2},{5,3},{6,0},{7,1},{8,14},{9,15},{10,... | collective-permute-start | bytes 786440 | tf_op jit(solution)/shard_map/ppermute | solution.py:205
  107.0 19.3 %collective-permute-start.20 = (bf16[256,512]{1,0:T(8,128)(2,1)S(1)}, bf16[256,512]{1,0:T(8,128)(2,1)S(1)}, u32[]{:S(2)}, u32[]{:S(2)}) collective-permute-start(bf16[256,512]{1,0:T(8,128)(2,1)S(1)} %copy-done.28), channel_id=1, source_target_pairs={{0,7},{1,6},{2,5},{3,4},{4,3},{5,2},{6,1},{7,0},{8,15},{9,14},{10,... | collective-permute-start | bytes 786440 | tf_op jit(solution)/shard_map/ppermute | solution.py:205
  111.2 18.6 %collective-permute-start.22 = (bf16[128,1024]{1,0:T(8,128)(2,1)}, bf16[128,1024]{1,0:T(8,128)(2,1)S(1)}, u32[]{:S(2)}, u32[]{:S(2)}) collective-permute-start(bf16[128,1024]{1,0:T(8,128)(2,1)} %get-tuple-element.29), channel_id=1, source_target_pairs={{0,24},{1,25},{2,26},{3,27},{4,28},{5,29},{6,30},{7,31},{8,0},{9,1... | collective-permute-start | bytes 786440 | tf_op jit(solution)/shard_map/ppermute | solution.py:205
  111.2 26.7 %collective-permute-start.23 = (bf16[128,1024]{1,0:T(8,128)(2,1)}, bf16[128,1024]{1,0:T(8,128)(2,1)S(1)}, u32[]{:S(2)}, u32[]{:S(2)}) collective-permute-start(bf16[128,1024]{1,0:T(8,128)(2,1)} %get-tuple-element.30), channel_id=1, source_target_pairs={{0,16},{1,17},{2,18},{3,19},{4,20},{5,21},{6,22},{7,23},{8,24},{9,... | collective-permute-start | bytes 786440 | tf_op jit(solution)/shard_map/ppermute | solution.py:205
  124.8 13.1 %collective-permute-start.24 = (bf16[128,1024]{1,0:T(8,128)(2,1)}, bf16[128,1024]{1,0:T(8,128)(2,1)S(1)}, u32[]{:S(2)}, u32[]{:S(2)}) collective-permute-start(bf16[128,1024]{1,0:T(8,128)(2,1)} %get-tuple-element.31), channel_id=1, source_target_pairs={{0,8},{1,9},{2,10},{3,11},{4,12},{5,13},{6,14},{7,15},{8,16},{9,17... | collective-permute-start | bytes 786440 | tf_op jit(solution)/shard_map/ppermute | solution.py:205
  (23 other events, 188.6 us)

commit v3 on v1

--- a/solution.py
+++ b/solution.py
@@ -1,9 +1,18 @@
+import functools
 import math
 
 import jax
 import jax.numpy as jnp
 from jax import lax
+from jax.experimental import pallas as pl
+from jax.experimental.pallas import tpu as pltpu
 from jax.sharding import Mesh, PartitionSpec as P
+
+NEAR = 4
+AXES = ("far", "y", "x", "core")
+CONTRACT_LAST = (((1,), (1,)), ((), ()))
+CONTRACT_FIRST = (((0,), (0,)), ((), ()))
+VMEM_LIMIT = 28 * 1024 * 1024
 
 
 def gelu_parts(value):
@@ -17,15 +26,8 @@
     return (result, slope)
 
 
-NEAR = 4
-CONTRACT_LAST = (((1,), (1,)), ((), ()))
-CONTRACT_FIRST = (((0,), (0,)), ((), ()))
-
-
-def on_device(tokens, cotangent, w_in, b_in, w_out):
-    far = lax.axis_size("far")
-    near = lax.axis_size("near")
-    tensor = lax.axis_size("tensor")
+def on_device_any(tokens, cotangent, w_in, b_in, w_out):
+    far, near, tensor = lax.axis_size("far"), lax.axis_size("near"), lax.axis_size("tensor")
     rows, feats = tokens.shape
     owned, width = w_in.shape
     scale = 1.0 / math.sqrt(rows * far * near)
@@ -55,13 +57,266 @@
     return (mixed, grad_sum.astype(jnp.float32) * scale)
 
 
+def weight_copies(ref, at, owned, w_in, w_out, bias, sem):
+    spot = pl.ds(at * owned, owned)
+    return [
+        pltpu.make_async_copy(ref.at[pl.ds(0, owned)], w_in.at[spot], sem.at[at, 0]),
+        pltpu.make_async_copy(ref.at[pl.ds(owned, owned)], w_out.at[spot], sem.at[at, 1]),
+        pltpu.make_async_copy(
+            ref.at[pl.ds(2 * owned, 16), pl.ds(0, owned)], bias.at[:, spot], sem.at[at, 2]
+        ),
+    ]
+
+
+def forward_kernel(owned, rows, feats, *refs):
+    piece_refs, w_refs = refs[:10], refs[10:14]
+    mine_ref, other_ref, dpre_ref = refs[14:17]
+    tok, cot, w_in, w_out, bias, tok_sem, cot_sem, w_sem = refs[17:]
+    core = lax.axis_index("core")
+    w_copies = []
+    for at, ref in enumerate(w_refs):
+        w_copies += weight_copies(ref, at, owned, w_in, w_out, bias, w_sem)
+    for copy in w_copies:
+        copy.start()
+    copies = token_copies(core, rows, feats, piece_refs, tok, tok_sem, 0)
+    cot_copies = token_copies(core, rows, feats, piece_refs, cot, cot_sem, 1)
+    for block in range(NEAR):
+        for copy in copies[block] + cot_copies[block]:
+            copy.start()
+    for copy in w_copies:
+        copy.wait()
+    own_half = pl.ds(pl.multiple_of(core * feats, feats), feats)
+    other_half = pl.ds(pl.multiple_of((1 - core) * feats, feats), feats)
+    step = rows // 2
+    for block in range(NEAR):
+        for copy in copies[block] + cot_copies[block]:
+            copy.wait()
+
+        @pl.loop(0, 2)
+        def _(sub):
+            start = pl.multiple_of(block * rows + sub * step, step)
+            spot = pl.ds(start, step)
+            pre = lax.dot_general(
+                tok[spot, :], w_in[...], CONTRACT_LAST, preferred_element_type=jnp.float32
+            ) + bias[0:1, :].astype(jnp.float32)
+            value, slope = gelu_parts(pre)
+            act = value.astype(jnp.bfloat16)
+            dact = lax.dot_general(
+                cot[spot, :], w_out[...], CONTRACT_LAST, preferred_element_type=jnp.float32
+            )
+            dpre_ref[spot, :] = (dact * slope).astype(jnp.bfloat16)
+            mine_ref[spot, :] = jnp.dot(
+                act, w_out[:, own_half], preferred_element_type=jnp.float32
+            ).astype(jnp.bfloat16)
+            other_ref[spot, :] = jnp.dot(
+                act, w_out[:, other_half], preferred_element_type=jnp.float32
+            ).astype(jnp.bfloat16)
+
+
+def token_copies(core, rows, feats, piece_refs, whole, sems, which):
+    blocks = []
+    for block in range(NEAR):
+        copies = []
+        for shift in range(2):
+            if block < NEAR - 1:
+                source = piece_refs[2 * block + shift].at[which]
+            else:
+                source = piece_refs[6 + 2 * which + shift]
+            columns = pl.ds(pl.multiple_of(lax.rem(core + shift, 2) * feats, feats), feats)
+            copies.append(
+                pltpu.make_async_copy(
+                    source,
+                    whole.at[pl.ds(block * rows, rows), columns],
+                    sems.at[2 * block + shift],
+                )
+            )
+        blocks.append(copies)
+    return blocks
+
+
+def gradient_kernel(owned, rows, feats, *refs):
+    dpre_ref, piece_refs, out_refs = refs[0], refs[1:11], refs[11:15]
+    tok, tok_sem = refs[15:]
+    core = lax.axis_index("core")
+    copies = token_copies(core, rows, feats, piece_refs, tok, tok_sem, 0)
+    for block in range(NEAR):
+        for copy in copies[block]:
+            copy.start()
+    for block in range(NEAR):
+        for copy in copies[block]:
+            copy.wait()
+    for at in range(0, 4, 2):
+        grad = lax.dot_general(
+            dpre_ref[:, at * owned : (at + 2) * owned],
+            tok[...],
+            CONTRACT_FIRST,
+            preferred_element_type=jnp.float32,
+        ).astype(jnp.bfloat16)
+        out_refs[at][...] = grad[:owned]
+        out_refs[at + 1][...] = grad[owned:]
+
+
+def pair_kernel(rows, mine_ref, other_ref, *out_refs):
+    for block in range(NEAR):
+        spot = pl.ds(block * rows, rows)
+        out_refs[block][...] = (
+            mine_ref[spot, :].astype(jnp.float32) + other_ref[spot, :].astype(jnp.float32)
+        ).astype(jnp.bfloat16)
+
+
+def vmem(count):
+    return [pl.BlockSpec(memory_space=pltpu.VMEM)] * count
+
+
+def anywhere(count):
+    return [pl.BlockSpec(memory_space=pl.ANY)] * count
+
+
+def bf16(*shape):
+    return jax.ShapeDtypeStruct(shape, jnp.bfloat16)
+
+
+def permute(value, there):
+    pairs = []
+    for f in range(4):
+        for y in range(2):
+            for x in range(2):
+                for c in range(2):
+                    to = there(f, y, x, c)
+                    here = ((f * 2 + y) * 2 + x) * 2 + c
+                    pairs.append((here, ((to[0] * 2 + to[1]) * 2 + to[2]) * 2 + to[3]))
+    return lax.ppermute(value, AXES, pairs)
+
+
+def to_x(value):
+    return permute(value, lambda f, y, x, c: (f, y, 1 - x, c))
+
+
+def to_y(value):
+    return permute(value, lambda f, y, x, c: (f, 1 - y, x, c))
+
+
+def to_diagonal(value):
+    return permute(value, lambda f, y, x, c: (f, 1 - y, 1 - x, c))
+
+
+def to_core(value):
+    return permute(value, lambda f, y, x, c: (f, y, x, 1 - c))
+
+
+def to_far(value, flip):
+    return permute(value, lambda f, y, x, c: (f ^ flip, y, x, c))
+
+
+def on_device_lines(tokens, cotangent, w_in, b_in, w_out):
+    rows, feats = tokens.shape
+    owned, width = w_in.shape
+    units = 4 * owned
+    count = NEAR * rows
+    scale = 1.0 / math.sqrt(4 * count)
+    params = pltpu.CompilerParams(vmem_limit_bytes=VMEM_LIMIT)
+    dma = pltpu.SemaphoreType.DMA
+
+    own = jnp.stack([tokens, cotangent])
+    bias_rows = jnp.pad(b_in.reshape(1, owned), ((0, 15), (0, width - owned)))
+    own_w = jnp.concatenate([w_in, w_out, bias_rows], 0)
+
+    from_x = to_x(own)
+    from_y = to_y(own)
+    w_two = to_far(own_w, 2)
+    w_one = to_far(own_w, 1)
+    own_other = to_core(own)
+    from_x, from_y, w_two, w_one, own_other = lax.optimization_barrier(
+        (from_x, from_y, w_two, w_one, own_other)
+    )
+    diag_tok = to_y(from_x[0])
+    diag_cot = to_x(from_y[1])
+    w_three = to_far(w_two, 1)
+    x_other = to_core(from_x)
+    y_other = to_core(from_y)
+    pieces = [own, own_other, from_x, x_other, from_y, y_other]
+    pieces += [diag_tok, to_core(diag_tok), diag_cot, to_core(diag_cot)]
+    weights = [own_w, w_one, w_two, w_three]
+
+    mine, other, dpre = pl.pallas_call(
+        functools.partial(forward_kernel, owned, rows, feats),
+        out_shape=(bf16(count, feats), bf16(count, feats), bf16(count, units)),
+        in_specs=anywhere(len(pieces) + len(weights)),
+        out_specs=vmem(3),
+        scratch_shapes=[
+            pltpu.VMEM((count, width), jnp.bfloat16),
+            pltpu.VMEM((count, width), jnp.bfloat16),
+            pltpu.VMEM((units, width), jnp.bfloat16),
+            pltpu.VMEM((units, width), jnp.bfloat16),
+            pltpu.VMEM((16, units), jnp.bfloat16),
+            dma((2 * NEAR,)),
+            dma((2 * NEAR,)),
+            dma((4, 3)),
+        ],
+        compiler_params=params,
+        cost_estimate=pl.CostEstimate(
+            flops=6 * count * units * width, bytes_accessed=8 * count * width, transcendentals=0
+        ),
+        name="forward",
+    )(*pieces, *weights)
+    received = to_core(other)
+
+    grads = pl.pallas_call(
+        functools.partial(gradient_kernel, owned, rows, feats),
+        out_shape=[bf16(owned, width)] * 4,
+        in_specs=vmem(1) + anywhere(len(pieces)),
+        out_specs=vmem(4),
+        scratch_shapes=[pltpu.VMEM((count, width), jnp.bfloat16), dma((2 * NEAR,))],
+        compiler_params=params,
+        cost_estimate=pl.CostEstimate(
+            flops=2 * count * units * width, bytes_accessed=4 * count * width, transcendentals=0
+        ),
+        name="gradient",
+    )(dpre, *pieces)
+    grad_one = to_far(grads[1], 1)
+    grad_two = to_far(grads[2], 2)
+    grad_three = to_far(grads[3], 3)
+
+    sums = pl.pallas_call(
+        functools.partial(pair_kernel, rows),
+        out_shape=[bf16(rows, feats)] * NEAR,
+        in_specs=vmem(2),
+        out_specs=vmem(NEAR),
+        compiler_params=params,
+        name="pair_sum",
+    )(mine, received)
+    mixed_x = to_x(sums[1])
+    mixed_y = to_y(sums[2])
+    last, grad_one = lax.optimization_barrier((sums[3], grad_one))
+    mixed_diag = to_diagonal(last)
+    mixed = (
+        sums[0].astype(jnp.float32)
+        + mixed_x.astype(jnp.float32)
+        + mixed_y.astype(jnp.float32)
+        + mixed_diag.astype(jnp.float32)
+    ).astype(jnp.bfloat16)
+    total = (
+        grads[0].astype(jnp.float32)
+        + grad_one.astype(jnp.float32)
+        + grad_two.astype(jnp.float32)
+        + grad_three.astype(jnp.float32)
+    )
+    return (mixed, total * scale)
+
+
 def solution(mesh):
     dp, tensor = mesh.shape["dp"], mesh.shape["tensor"]
-    fine = Mesh(mesh.devices.reshape(dp // NEAR, NEAR, tensor), ("far", "near", "tensor"))
-    rows = ("far", "near")
-    owners = ("far", "near", "tensor")
-    in_specs = (P(rows, "tensor"), P(rows, "tensor"), P(owners, None), P(owners), P(owners, None))
-    out_specs = (P(rows, "tensor"), P(owners, None))
+    far = dp // NEAR
+    if tensor == 2 and far == 4:
+        fine = Mesh(mesh.devices.reshape(far, 2, 2, tensor), AXES)
+        rows, owners, halves = ("far", "y", "x"), AXES, "core"
+        body = on_device_lines
+    else:
+        fine = Mesh(mesh.devices.reshape(far, NEAR, tensor), ("far", "near", "tensor"))
+        rows, owners, halves = ("far", "near"), ("far", "near", "tensor"), "tensor"
+        body = on_device_any
+    in_specs = (P(rows, halves), P(rows, halves), P(owners, None), P(owners), P(owners, None))
+    out_specs = (P(rows, halves), P(owners, None))
     return jax.shard_map(
-        on_device, mesh=fine, in_specs=in_specs, out_specs=out_specs, check_vma=False
-    )
+        body, mesh=fine, in_specs=in_specs, out_specs=out_specs, check_vma=False
+    )

time: 251 us -> 107 us (0.43)
  waiting for transfers between devices: 175 us -> 68.6 us
  local copies, waits for them, and re-layouts: 33.8 us -> 0.08 us
  matrix products: 23 us -> 0 us
  starting transfers between devices: 0.2 us -> 19.1 us
  Pallas kernels: 0 us -> 14.6 us
  between operations: 13.8 us -> 0.74 us
    all_gather x3 -> x0, waiting for transfers between devices: 114 us -> none  [the longest x1 50 us: on_device(): lax.all_gather(jnp.concatenate([w_in, w_out, bias_rows], 0), 'far', axis=0)]
    ppermute x0 -> x19, waiting for transfers between devices: none -> 68.6 us  [permute(): return lax.ppermute(value, AXES, pairs)]
    reduce_scatter x2 -> x0, waiting for transfers between devices: 59.5 us -> none  [the longest x1 52.3 us: on_device(): lax.psum_scatter(term.reshape(near * tensor, rows, feats), ('near', 'tens...]
    dot_general x3 -> x0, matrix products: 23 us -> none  [the longest x1 11.2 us: on_device(): lax.dot_general(dpre, tok_full, CONTRACT_FIRST, preferred_element_type=jn...]
    reshape x3 -> x0, local copies, waits for them, and re-layouts: 20.9 us -> none  [the longest x1 7.86 us: on_device(): term = term.reshape(near, rows, tensor, feats).transpose(0, 2, 1, 3)]
    ppermute x0 -> x19, starting transfers between devices: none -> 19.1 us  [permute(): return lax.ppermute(value, AXES, pairs)]
    pallas_call x0 -> x3, Pallas kernels: none -> 14.6 us  [the longest x1 11 us: on_device_lines(): pl.pallas_call(functools.partial(forward_kernel, owned, rows, feats), out...]
    unnamed x4 -> x6, local copies, waits for them, and re-layouts: 6.33 us -> 0.01 us
  transfers between devices with their start and end apart: 5 -> 19, of which waited for: 5 -> 9; matrix products, arithmetic and copies ran while one was open for 14% -> 1% of each run, Pallas kernels for 0% -> 3%
where the time goes in v3:
time: 107 us
  waiting for transfers between devices  68.6 us (64%)
  starting transfers between devices  19.1 us (18%)
  Pallas kernels  14.6 us (14%)
  other arithmetic  3.41 us (3%)
    ppermute x19, waiting for transfers between devices, permute(): return lax.ppermute(value, AXES, pairs)  68.6 us
    ppermute x19, starting transfers between devices, permute(): return lax.ppermute(value, AXES, pairs)  19.1 us
    pallas_call x1, Pallas kernels, on_device_lines(): pl.pallas_call(functools.partial(forward_kernel, owned, rows, feats), out...  11 us
    pallas_call x1, Pallas kernels, on_device_lines(): pl.pallas_call(functools.partial(gradient_kernel, owned, rows, feats), ou...  3.08 us
  transfers between devices with their start and end apart: 19, of which 9 were waited for; matrix products, arithmetic and copies ran while one was open for 1% of the time, Pallas kernels for 3%

profile of v3, /device:TPU:0, one launch (start us, length us, event | category | flops | bytes accessed | tf_op | source)
XLA Modules:
  0.0 106.6 jit_solution(3104963002265219576)
XLA Ops:
  0.7 1.4 %pad_maximum_fusion.refs_0_.refs_1_ = bf16[2,512,512]{2,1,0:T(8,128)(2,1)S(1)} fusion(bf16[1,512,512]{2,1,0:T(8,128)(2,1)} %bitcast.7, bf16[1,512,512]{2,1,0:T(8,128)(2,1)} %bitcast.8), kind=kLoop, calls=%fused_computation.2 | loop fusion | flops 524288 | bytes 2097152 | tf_op jit(solution)/shard_map/stack | solution.py:220
  2.0 0.5 collective-permute-start.4
  2.5 2.6 %collective-permute-start.1 = (bf16[2,512,512]{2,1,0:T(8,128)(2,1)S(1)}, bf16[2,512,512]{2,1,0:T(8,128)(2,1)S(1)}, u32[]{:S(2)}, u32[]{:S(2)}) collective-permute-start(bf16[2,512,512]{2,1,0:T(8,128)(2,1)S(1)} %pad_maximum_fusion.refs_0_.refs_1_), channel_id=1, source_target_pairs={{0,4},{1,5},{2,6},{3,7},{4,0},{5,1},{6,2},{7,3},{8,12},{9,13},{10,... | collective-permute-start | bytes 3145736 | tf_op jit(solution)/shard_map/ppermute | solution.py:188
  5.1 1.5 %collective-permute-start = (bf16[2,512,512]{2,1,0:T(8,128)(2,1)S(1)}, bf16[2,512,512]{2,1,0:T(8,128)(2,1)S(1)}, u32[]{:S(2)}, u32[]{:S(2)}) collective-permute-start(bf16[2,512,512]{2,1,0:T(8,128)(2,1)S(1)} %pad_maximum_fusion.refs_0_.refs_1_), channel_id=1, source_target_pairs={{0,2},{1,3},{2,0},{3,1},{4,6},{5,7},{6,4},{7,5},{8,10},{9,11},{10,... | collective-permute-start | bytes 3145736 | tf_op jit(solution)/shard_map/ppermute | solution.py:188
  6.7 1.6 %collective-permute-start.3 = (bf16[272,1024]{1,0:T(8,128)(2,1)S(1)}, bf16[272,1024]{1,0:T(8,128)(2,1)S(1)}, u32[]{:S(2)}, u32[]{:S(2)}) collective-permute-start(bf16[272,1024]{1,0:T(8,128)(2,1)S(1)} %fusion.1.refs_10_), channel_id=1, source_target_pairs={{0,8},{1,9},{2,10},{3,11},{4,12},{5,13},{6,14},{7,15},{8,0},{9,1},... | collective-permute-start | bytes 1671176 | tf_op jit(solution)/shard_map/ppermute | solution.py:188
  8.3 2.6 %collective-permute-start.2 = (bf16[272,1024]{1,0:T(8,128)(2,1)S(1)}, bf16[272,1024]{1,0:T(8,128)(2,1)S(1)}, u32[]{:S(2)}, u32[]{:S(2)}) collective-permute-start(bf16[272,1024]{1,0:T(8,128)(2,1)S(1)} %fusion.1.refs_10_), channel_id=1, source_target_pairs={{0,16},{1,17},{2,18},{3,19},{4,20},{5,21},{6,22},{7,23},{8,24},{9,... | collective-permute-start | bytes 1671176 | tf_op jit(solution)/shard_map/ppermute | solution.py:188
  10.9 22.1 %collective-permute-done.3.refs_11_ = bf16[272,1024]{1,0:T(8,128)(2,1)S(1)} collective-permute-done((bf16[272,1024]{1,0:T(8,128)(2,1)S(1)}, bf16[272,1024]{1,0:T(8,128)(2,1)S(1)}, u32[]{:S(2)}, u32[]{:S(2)}) %collective-permute-start.3) | collective-permute-done | bytes 557088 | tf_op jit(solution)/shard_map/ppermute | solution.py:188
  33.0 2.4 %collective-permute-done.2.refs_12_ = bf16[272,1024]{1,0:T(8,128)(2,1)S(1)} collective-permute-done((bf16[272,1024]{1,0:T(8,128)(2,1)S(1)}, bf16[272,1024]{1,0:T(8,128)(2,1)S(1)}, u32[]{:S(2)}, u32[]{:S(2)}) %collective-permute-start.2) | collective-permute-done | bytes 557088 | tf_op jit(solution)/shard_map/ppermute | solution.py:188
  35.4 0.6 collective-permute-start.9
  36.0 0.6 collective-permute-start.7
  36.6 0.5 collective-permute-start.6
  37.1 0.4 collective-permute-start.11
  37.6 8.4 %collective-permute-done.9.refs_8_.refs_9_ = bf16[512,512]{1,0:T(8,128)(2,1)S(1)} collective-permute-done((bf16[512,512]{1,0:T(8,128)(2,1)S(1)}, bf16[512,512]{1,0:T(8,128)(2,1)S(1)}, u32[]{:S(2)}, u32[]{:S(2)}) %collective-permute-start.9) | collective-permute-done | bytes 524320 | tf_op jit(solution)/shard_map/ppermute | solution.py:188
  46.0 0.4 collective-permute-done.7.refs_6_.refs_7_
  46.3 0.2 collective-permute-start.8
  46.5 5.2 %collective-permute-done.11.refs_13_ = bf16[272,1024]{1,0:T(8,128)(2,1)S(1)} collective-permute-done((bf16[272,1024]{1,0:T(8,128)(2,1)S(1)}, bf16[272,1024]{1,0:T(8,128)(2,1)S(1)}, u32[]{:S(2)}, u32[]{:S(2)}) %collective-permute-start.11) | collective-permute-done | bytes 557088 | tf_op jit(solution)/shard_map/ppermute | solution.py:188
  51.7 11.0 %forward.1 = (bf16[2048,512]{1,0:T(8,128)(2,1)S(1)}, bf16[2048,512]{1,0:T(8,128)(2,1)S(1)}, bf16[2048,512]{1,0:T(8,128)(2,1)S(1)}) custom-call(bf16[2,512,512]{2,1,0:T(8,128)(2,1)S(1)} %pad_maximum_fusion.refs_0_.refs_1_, bf16[2,512,512]{2,1,0:T(8,128)(2,1)S(1)} %collective-permute-done.4.refs_1_.refs_2_, ...), custom_call_target="tpu_custom_call" | custom-call | flops 6442450944 | bytes 16777216 | tf_op jit(solution)/shard_map/forward/pallas_call | solution.py:241
  62.7 0.1 collective-permute-start.12
  62.8 3.1 %gradient.1 = (bf16[128,1024]{1,0:T(8,128)(2,1)S(1)}, bf16[128,1024]{1,0:T(8,128)(2,1)S(1)}, bf16[128,1024]{1,0:T(8,128)(2,1)S(1)}, bf16[128,1024]{1,0:T(8,128)(2,1)S(1)}) custom-call(bf16[2048,512]{1,0:T(8,128)(2,1)S(1)} %get-tuple-element.31.refs_0_, bf16[2,512,512]{2,1,0:T(8,128)(2,1)S(1)} %pad_maximum_fusion.refs_0_.refs_1_, ...), custom_call_target="tpu_custom_call" | custom-call | flops 2147483648 | bytes 8388608 | tf_op jit(solution)/shard_map/gradient/pallas_call | solution.py:264
  65.9 0.5 collective-permute-start.15
  66.4 2.6 %collective-permute-start.17 = (bf16[128,1024]{1,0:T(8,128)(2,1)S(1)}, bf16[128,1024]{1,0:T(8,128)(2,1)S(1)}, u32[]{:S(2)}, u32[]{:S(2)}) collective-permute-start(bf16[128,1024]{1,0:T(8,128)(2,1)S(1)} %get-tuple-element.36), channel_id=1, source_target_pairs={{0,16},{1,17},{2,18},{3,19},{4,20},{5,21},{6,22},{7,23},{8,24},{9,... | collective-permute-start | bytes 786440 | tf_op jit(solution)/shard_map/ppermute | solution.py:188
  69.0 1.4 %collective-permute-start.18 = (bf16[128,1024]{1,0:T(8,128)(2,1)S(1)}, bf16[128,1024]{1,0:T(8,128)(2,1)S(1)}, u32[]{:S(2)}, u32[]{:S(2)}) collective-permute-start(bf16[128,1024]{1,0:T(8,128)(2,1)S(1)} %get-tuple-element.37), channel_id=1, source_target_pairs={{0,24},{1,25},{2,26},{3,27},{4,28},{5,29},{6,30},{7,31},{8,16},{9,... | collective-permute-start | bytes 786440 | tf_op jit(solution)/shard_map/ppermute | solution.py:188
  70.3 0.5 pair_sum.1
  70.8 8.9 %collective-permute-done.15 = bf16[128,1024]{1,0:T(8,128)(2,1)S(1)} collective-permute-done((bf16[128,1024]{1,0:T(8,128)(2,1)S(1)}, bf16[128,1024]{1,0:T(8,128)(2,1)S(1)}, u32[]{:S(2)}, u32[]{:S(2)}) %collective-permute-start.15) | collective-permute-done | bytes 262176 | tf_op jit(solution)/shard_map/ppermute | solution.py:188
  79.8 2.4 %collective-permute-start.16 = (bf16[512,512]{1,0:T(8,128)(2,1)S(1)}, bf16[512,512]{1,0:T(8,128)(2,1)S(1)}, u32[]{:S(2)}, u32[]{:S(2)}) collective-permute-start(bf16[512,512]{1,0:T(8,128)(2,1)S(1)} %get-tuple-element.33), channel_id=1, source_target_pairs={{0,6},{1,7},{2,4},{3,5},{4,2},{5,3},{6,0},{7,1},{8,14},{9,15},{10,... | collective-permute-start | bytes 1572872 | tf_op jit(solution)/shard_map/ppermute | solution.py:188
  82.2 0.5 collective-permute-start.13
  82.7 0.5 collective-permute-start.14
  83.2 4.5 %collective-permute-done.17 = bf16[128,1024]{1,0:T(8,128)(2,1)S(1)} collective-permute-done((bf16[128,1024]{1,0:T(8,128)(2,1)S(1)}, bf16[128,1024]{1,0:T(8,128)(2,1)S(1)}, u32[]{:S(2)}, u32[]{:S(2)}) %collective-permute-start.17) | collective-permute-done | bytes 262176 | tf_op jit(solution)/shard_map/ppermute | solution.py:188
  87.7 1.0 add_multiply_fusion
  88.7 6.9 %collective-permute-done.16 = bf16[512,512]{1,0:T(8,128)(2,1)S(1)} collective-permute-done((bf16[512,512]{1,0:T(8,128)(2,1)S(1)}, bf16[512,512]{1,0:T(8,128)(2,1)S(1)}, u32[]{:S(2)}, u32[]{:S(2)}) %collective-permute-start.16) | collective-permute-done | bytes 524320 | tf_op jit(solution)/shard_map/ppermute | solution.py:188
  95.5 10.0 %collective-permute-done.13 = bf16[512,512]{1,0:T(8,128)(2,1)S(1)} collective-permute-done((bf16[512,512]{1,0:T(8,128)(2,1)S(1)}, bf16[512,512]{1,0:T(8,128)(2,1)S(1)}, u32[]{:S(2)}, u32[]{:S(2)}) %collective-permute-start.13) | collective-permute-done | bytes 524320 | tf_op jit(solution)/shard_map/ppermute | solution.py:188
  105.5 1.1 add_convert_fusion
  (21 shorter events, 0.2 us)
Async XLA Ops:
  0.6 6.0 %copy-start = (bf16[128,1024]{1,0:T(8,128)(2,1)S(1)}, bf16[128,1024]{1,0:T(8,128)(2,1)}, u32[]{:S(2)}) copy-start(bf16[128,1024]{1,0:T(8,128)(2,1)} %param.9) | copy-start | bytes 786436
  0.6 6.0 %copy-start.2 = (bf16[128]{0:T(256)(128)(2,1)S(1)}, bf16[128]{0:T(256)(128)(2,1)}, u32[]{:S(2)}) copy-start(bf16[128]{0:T(256)(128)(2,1)} %param.8) | copy-start | bytes 772
  0.7 6.0 %copy-start.1 = (bf16[128,1024]{1,0:T(8,128)(2,1)S(1)}, bf16[128,1024]{1,0:T(8,128)(2,1)}, u32[]{:S(2)}) copy-start(bf16[128,1024]{1,0:T(8,128)(2,1)} %param.7) | copy-start | bytes 786436
  2.0 33.3 %collective-permute-start.4 = (bf16[2,512,512]{2,1,0:T(8,128)(2,1)S(1)}, bf16[2,512,512]{2,1,0:T(8,128)(2,1)S(1)}, u32[]{:S(2)}, u32[]{:S(2)}) collective-permute-start(bf16[2,512,512]{2,1,0:T(8,128)(2,1)S(1)} %pad_maximum_fusion.refs_0_.refs_1_), channel_id=1, source_target_pairs={{0,1},{1,0},{2,3},{3,2},{4,5},{5,4},{6,7},{7,6},{8,9},{9,8},{10,11... | collective-permute-start | bytes 3145736 | tf_op jit(solution)/shard_map/ppermute | solution.py:188
  2.5 32.8 %collective-permute-start.1 = (bf16[2,512,512]{2,1,0:T(8,128)(2,1)S(1)}, bf16[2,512,512]{2,1,0:T(8,128)(2,1)S(1)}, u32[]{:S(2)}, u32[]{:S(2)}) collective-permute-start(bf16[2,512,512]{2,1,0:T(8,128)(2,1)S(1)} %pad_maximum_fusion.refs_0_.refs_1_), channel_id=1, source_target_pairs={{0,4},{1,5},{2,6},{3,7},{4,0},{5,1},{6,2},{7,3},{8,12},{9,13},{10,... | collective-permute-start | bytes 3145736 | tf_op jit(solution)/shard_map/ppermute | solution.py:188
  5.1 30.2 %collective-permute-start = (bf16[2,512,512]{2,1,0:T(8,128)(2,1)S(1)}, bf16[2,512,512]{2,1,0:T(8,128)(2,1)S(1)}, u32[]{:S(2)}, u32[]{:S(2)}) collective-permute-start(bf16[2,512,512]{2,1,0:T(8,128)(2,1)S(1)} %pad_maximum_fusion.refs_0_.refs_1_), channel_id=1, source_target_pairs={{0,2},{1,3},{2,0},{3,1},{4,6},{5,7},{6,4},{7,5},{8,10},{9,11},{10,... | collective-permute-start | bytes 3145736 | tf_op jit(solution)/shard_map/ppermute | solution.py:188
  6.7 26.3 %collective-permute-start.3 = (bf16[272,1024]{1,0:T(8,128)(2,1)S(1)}, bf16[272,1024]{1,0:T(8,128)(2,1)S(1)}, u32[]{:S(2)}, u32[]{:S(2)}) collective-permute-start(bf16[272,1024]{1,0:T(8,128)(2,1)S(1)} %fusion.1.refs_10_), channel_id=1, source_target_pairs={{0,8},{1,9},{2,10},{3,11},{4,12},{5,13},{6,14},{7,15},{8,0},{9,1},... | collective-permute-start | bytes 1671176 | tf_op jit(solution)/shard_map/ppermute | solution.py:188
  8.3 27.0 %collective-permute-start.2 = (bf16[272,1024]{1,0:T(8,128)(2,1)S(1)}, bf16[272,1024]{1,0:T(8,128)(2,1)S(1)}, u32[]{:S(2)}, u32[]{:S(2)}) collective-permute-start(bf16[272,1024]{1,0:T(8,128)(2,1)S(1)} %fusion.1.refs_10_), channel_id=1, source_target_pairs={{0,16},{1,17},{2,18},{3,19},{4,20},{5,21},{6,22},{7,23},{8,24},{9,... | collective-permute-start | bytes 1671176 | tf_op jit(solution)/shard_map/ppermute | solution.py:188
  35.4 10.6 %collective-permute-start.9 = (bf16[512,512]{1,0:T(8,128)(2,1)S(1)}, bf16[512,512]{1,0:T(8,128)(2,1)S(1)}, u32[]{:S(2)}, u32[]{:S(2)}) collective-permute-start(bf16[512,512]{1,0:T(8,128)(2,1)S(1)} %slice_bitcast_fusion), channel_id=1, source_target_pairs={{0,2},{1,3},{2,0},{3,1},{4,6},{5,7},{6,4},{7,5},{8,10},{9,11},{10,... | collective-permute-start | bytes 1572872 | tf_op jit(solution)/shard_map/ppermute | solution.py:188
  36.0 10.3 %collective-permute-start.7 = (bf16[512,512]{1,0:T(8,128)(2,1)S(1)}, bf16[512,512]{1,0:T(8,128)(2,1)S(1)}, u32[]{:S(2)}, u32[]{:S(2)}) collective-permute-start(bf16[512,512]{1,0:T(8,128)(2,1)S(1)} %slice_bitcast_fusion.1), channel_id=1, source_target_pairs={{0,4},{1,5},{2,6},{3,7},{4,0},{5,1},{6,2},{7,3},{8,12},{9,13},{10,... | collective-permute-start | bytes 1572872 | tf_op jit(solution)/shard_map/ppermute | solution.py:188
  36.6 15.1 %collective-permute-start.5 = (bf16[2,512,512]{2,1,0:T(8,128)(2,1)S(1)}, bf16[2,512,512]{2,1,0:T(8,128)(2,1)S(1)}, u32[]{:S(2)}, u32[]{:S(2)}) collective-permute-start(bf16[2,512,512]{2,1,0:T(8,128)(2,1)S(1)} %collective-permute-done.refs_2_.refs_3_), channel_id=1, source_target_pairs={{0,1},{1,0},{2,3},{3,2},{4,5},{5,4},{6,7},{7,6},{8,9},{9,8},{10,11... | collective-permute-start | bytes 3145736 | tf_op jit(solution)/shard_map/ppermute | solution.py:188
  36.6 15.1 %collective-permute-start.6 = (bf16[2,512,512]{2,1,0:T(8,128)(2,1)S(1)}, bf16[2,512,512]{2,1,0:T(8,128)(2,1)S(1)}, u32[]{:S(2)}, u32[]{:S(2)}) collective-permute-start(bf16[2,512,512]{2,1,0:T(8,128)(2,1)S(1)} %collective-permute-done.1.refs_4_.refs_5_), channel_id=1, source_target_pairs={{0,1},{1,0},{2,3},{3,2},{4,5},{5,4},{6,7},{7,6},{8,9},{9,8},{10,11... | collective-permute-start | bytes 3145736 | tf_op jit(solution)/shard_map/ppermute | solution.py:188
  37.1 14.5 %collective-permute-start.11 = (bf16[272,1024]{1,0:T(8,128)(2,1)S(1)}, bf16[272,1024]{1,0:T(8,128)(2,1)S(1)}, u32[]{:S(2)}, u32[]{:S(2)}) collective-permute-start(bf16[272,1024]{1,0:T(8,128)(2,1)S(1)} %collective-permute-done.2.refs_12_), channel_id=1, source_target_pairs={{0,8},{1,9},{2,10},{3,11},{4,12},{5,13},{6,14},{7,15},{8,0},{9,1},... | collective-permute-start | bytes 1671176 | tf_op jit(solution)/shard_map/ppermute | solution.py:188
  46.0 5.7 %collective-permute-start.10 = (bf16[512,512]{1,0:T(8,128)(2,1)S(1)}, bf16[512,512]{1,0:T(8,128)(2,1)S(1)}, u32[]{:S(2)}, u32[]{:S(2)}) collective-permute-start(bf16[512,512]{1,0:T(8,128)(2,1)S(1)} %collective-permute-done.9.refs_8_.refs_9_), channel_id=1, source_target_pairs={{0,1},{1,0},{2,3},{3,2},{4,5},{5,4},{6,7},{7,6},{8,9},{9,8},{10,11... | collective-permute-start | bytes 1572872 | tf_op jit(solution)/shard_map/ppermute | solution.py:188
  46.3 5.3 %collective-permute-start.8 = (bf16[512,512]{1,0:T(8,128)(2,1)S(1)}, bf16[512,512]{1,0:T(8,128)(2,1)S(1)}, u32[]{:S(2)}, u32[]{:S(2)}) collective-permute-start(bf16[512,512]{1,0:T(8,128)(2,1)S(1)} %collective-permute-done.7.refs_6_.refs_7_), channel_id=1, source_target_pairs={{0,1},{1,0},{2,3},{3,2},{4,5},{5,4},{6,7},{7,6},{8,9},{9,8},{10,11... | collective-permute-start | bytes 1572872 | tf_op jit(solution)/shard_map/ppermute | solution.py:188
  62.7 7.6 %collective-permute-start.12 = (bf16[2048,512]{1,0:T(8,128)(2,1)S(1)}, bf16[2048,512]{1,0:T(8,128)(2,1)S(1)}, u32[]{:S(2)}, u32[]{:S(2)}) collective-permute-start(bf16[2048,512]{1,0:T(8,128)(2,1)S(1)} %get-tuple-element.26), channel_id=1, source_target_pairs={{0,1},{1,0},{2,3},{3,2},{4,5},{5,4},{6,7},{7,6},{8,9},{9,8},{10,11... | collective-permute-start | bytes 6291464 | tf_op jit(solution)/shard_map/ppermute | solution.py:188
  65.9 13.9 %collective-permute-start.15 = (bf16[128,1024]{1,0:T(8,128)(2,1)S(1)}, bf16[128,1024]{1,0:T(8,128)(2,1)S(1)}, u32[]{:S(2)}, u32[]{:S(2)}) collective-permute-start(bf16[128,1024]{1,0:T(8,128)(2,1)S(1)} %get-tuple-element.32), channel_id=1, source_target_pairs={{0,8},{1,9},{2,10},{3,11},{4,12},{5,13},{6,14},{7,15},{8,0},{9,1},... | collective-permute-start | bytes 786440 | tf_op jit(solution)/shard_map/ppermute | solution.py:188
  66.4 21.3 %collective-permute-start.17 = (bf16[128,1024]{1,0:T(8,128)(2,1)S(1)}, bf16[128,1024]{1,0:T(8,128)(2,1)S(1)}, u32[]{:S(2)}, u32[]{:S(2)}) collective-permute-start(bf16[128,1024]{1,0:T(8,128)(2,1)S(1)} %get-tuple-element.36), channel_id=1, source_target_pairs={{0,16},{1,17},{2,18},{3,19},{4,20},{5,21},{6,22},{7,23},{8,24},{9,... | collective-permute-start | bytes 786440 | tf_op jit(solution)/shard_map/ppermute | solution.py:188
  69.0 18.7 %collective-permute-start.18 = (bf16[128,1024]{1,0:T(8,128)(2,1)S(1)}, bf16[128,1024]{1,0:T(8,128)(2,1)S(1)}, u32[]{:S(2)}, u32[]{:S(2)}) collective-permute-start(bf16[128,1024]{1,0:T(8,128)(2,1)S(1)} %get-tuple-element.37), channel_id=1, source_target_pairs={{0,24},{1,25},{2,26},{3,27},{4,28},{5,29},{6,30},{7,31},{8,16},{9,... | collective-permute-start | bytes 786440 | tf_op jit(solution)/shard_map/ppermute | solution.py:188
  79.8 15.8 %collective-permute-start.16 = (bf16[512,512]{1,0:T(8,128)(2,1)S(1)}, bf16[512,512]{1,0:T(8,128)(2,1)S(1)}, u32[]{:S(2)}, u32[]{:S(2)}) collective-permute-start(bf16[512,512]{1,0:T(8,128)(2,1)S(1)} %get-tuple-element.33), channel_id=1, source_target_pairs={{0,6},{1,7},{2,4},{3,5},{4,2},{5,3},{6,0},{7,1},{8,14},{9,15},{10,... | collective-permute-start | bytes 1572872 | tf_op jit(solution)/shard_map/ppermute | solution.py:188
  82.2 23.3 %collective-permute-start.13 = (bf16[512,512]{1,0:T(8,128)(2,1)S(1)}, bf16[512,512]{1,0:T(8,128)(2,1)S(1)}, u32[]{:S(2)}, u32[]{:S(2)}) collective-permute-start(bf16[512,512]{1,0:T(8,128)(2,1)S(1)} %get-tuple-element.28), channel_id=1, source_target_pairs={{0,2},{1,3},{2,0},{3,1},{4,6},{5,7},{6,4},{7,5},{8,10},{9,11},{10,... | collective-permute-start | bytes 1572872 | tf_op jit(solution)/shard_map/ppermute | solution.py:188
  82.7 22.8 %collective-permute-start.14 = (bf16[512,512]{1,0:T(8,128)(2,1)S(1)}, bf16[512,512]{1,0:T(8,128)(2,1)S(1)}, u32[]{:S(2)}, u32[]{:S(2)}) collective-permute-start(bf16[512,512]{1,0:T(8,128)(2,1)S(1)} %get-tuple-element.29), channel_id=1, source_target_pairs={{0,4},{1,5},{2,6},{3,7},{4,0},{5,1},{6,2},{7,3},{8,12},{9,13},{10,... | collective-permute-start | bytes 1572872 | tf_op jit(solution)/shard_map/ppermute | solution.py:188

commit v4 on v3

--- a/solution.py
+++ b/solution.py
@@ -135,8 +135,8 @@
 
 
 def gradient_kernel(owned, rows, feats, *refs):
-    dpre_ref, piece_refs, out_refs = refs[0], refs[1:11], refs[11:15]
-    tok, tok_sem = refs[15:]
+    dpre_ref, piece_refs = refs[0], refs[1:11]
+    keep_ref, send_ref, tok, tok_sem = refs[11:]
     core = lax.axis_index("core")
     copies = token_copies(core, rows, feats, piece_refs, tok, tok_sem, 0)
     for block in range(NEAR):
@@ -152,8 +152,8 @@
             CONTRACT_FIRST,
             preferred_element_type=jnp.float32,
         ).astype(jnp.bfloat16)
-        out_refs[at][...] = grad[:owned]
-        out_refs[at + 1][...] = grad[owned:]
+        keep_ref[at // 2] = grad[:owned]
+        send_ref[at // 2] = grad[owned:]
 
 
 def pair_kernel(rows, mine_ref, other_ref, *out_refs):
@@ -220,10 +220,9 @@
     own = jnp.stack([tokens, cotangent])
     bias_rows = jnp.pad(b_in.reshape(1, owned), ((0, 15), (0, width - owned)))
     own_w = jnp.concatenate([w_in, w_out, bias_rows], 0)
-
+    w_two = to_far(own_w, 2)
     from_x = to_x(own)
     from_y = to_y(own)
-    w_two = to_far(own_w, 2)
     w_one = to_far(own_w, 1)
     own_other = to_core(own)
     from_x, from_y, w_two, w_one, own_other = lax.optimization_barrier(
@@ -261,11 +260,11 @@
     )(*pieces, *weights)
     received = to_core(other)
 
-    grads = pl.pallas_call(
+    keep, send = pl.pallas_call(
         functools.partial(gradient_kernel, owned, rows, feats),
-        out_shape=[bf16(owned, width)] * 4,
+        out_shape=[bf16(2, owned, width)] * 2,
         in_specs=vmem(1) + anywhere(len(pieces)),
-        out_specs=vmem(4),
+        out_specs=vmem(2),
         scratch_shapes=[pltpu.VMEM((count, width), jnp.bfloat16), dma((2 * NEAR,))],
         compiler_params=params,
         cost_estimate=pl.CostEstimate(
@@ -273,9 +272,7 @@
         ),
         name="gradient",
     )(dpre, *pieces)
-    grad_one = to_far(grads[1], 1)
-    grad_two = to_far(grads[2], 2)
-    grad_three = to_far(grads[3], 3)
+    sent = to_far(send, 1)
 
     sums = pl.pallas_call(
         functools.partial(pair_kernel, rows),
@@ -287,21 +284,17 @@
     )(mine, received)
     mixed_x = to_x(sums[1])
     mixed_y = to_y(sums[2])
-    last, grad_one = lax.optimization_barrier((sums[3], grad_one))
-    mixed_diag = to_diagonal(last)
+    mixed_diag = to_diagonal(sums[3])
+    keep, _ = lax.optimization_barrier((keep, sums[0]))
+    pair = keep.astype(jnp.float32) + sent.astype(jnp.float32)
+    grad_two = to_far(pair[1].astype(jnp.bfloat16), 2)
     mixed = (
         sums[0].astype(jnp.float32)
         + mixed_x.astype(jnp.float32)
         + mixed_y.astype(jnp.float32)
         + mixed_diag.astype(jnp.float32)
     ).astype(jnp.bfloat16)
-    total = (
-        grads[0].astype(jnp.float32)
-        + grad_one.astype(jnp.float32)
-        + grad_two.astype(jnp.float32)
-        + grad_three.astype(jnp.float32)
-    )
-    return (mixed, total * scale)
+    return (mixed, (pair[0] + grad_two.astype(jnp.float32)) * scale)
 
 
 def solution(mesh):

time: 107 us -> 97 us (0.907)
  waiting for transfers between devices: 68.6 us -> 61.2 us
  starting transfers between devices: 19.1 us -> 16.6 us
    ppermute x19 -> x18, waiting for transfers between devices: 68.6 us -> 61.2 us  [permute(): return lax.ppermute(value, AXES, pairs)]
    ppermute x19 -> x18, starting transfers between devices: 19.1 us -> 16.6 us  [permute(): return lax.ppermute(value, AXES, pairs)]
  transfers between devices with their start and end apart: 19 -> 18, of which waited for: 9 -> 8; matrix products, arithmetic and copies ran while one was open for 1% -> 1% of each run, Pallas kernels for 3% -> 4%
where the time goes in v4:
time: 97 us; the launch traced here: 96.8 us
  waiting for transfers between devices  61.2 us (63%)
  starting transfers between devices  16.6 us (17%)
  Pallas kernels  14.6 us (15%)
  other arithmetic  3.48 us (4%)
    ppermute x18, waiting for transfers between devices, permute(): return lax.ppermute(value, AXES, pairs)  61.2 us
    ppermute x18, starting transfers between devices, permute(): return lax.ppermute(value, AXES, pairs)  16.6 us
    pallas_call x1, Pallas kernels, on_device_lines(): pl.pallas_call(functools.partial(forward_kernel, owned, rows, feats), out...  11 us
    pallas_call x1, Pallas kernels, on_device_lines(): pl.pallas_call(functools.partial(gradient_kernel, owned, rows, feats), ou...  3.08 us
  transfers between devices with their start and end apart: 18, of which 8 were waited for; matrix products, arithmetic and copies ran while one was open for 1% of the time, Pallas kernels for 4%

profile of v4, /device:TPU:0, one launch (start us, length us, event | category | flops | bytes accessed | tf_op | source)
XLA Modules:
  0.0 96.8 jit_solution(10888772237282090660)
XLA Ops:
  0.7 1.4 %pad_maximum_fusion.refs_0_.refs_1_ = bf16[2,512,512]{2,1,0:T(8,128)(2,1)S(1)} fusion(bf16[1,512,512]{2,1,0:T(8,128)(2,1)} %bitcast.15, bf16[1,512,512]{2,1,0:T(8,128)(2,1)} %bitcast.16), kind=kLoop, calls=%fused_computation.2 | loop fusion | flops 524288 | bytes 2097152 | tf_op jit(solution)/shard_map/stack | solution.py:220
  2.0 0.5 collective-permute-start.4
  2.5 2.6 %collective-permute-start.1 = (bf16[2,512,512]{2,1,0:T(8,128)(2,1)S(1)}, bf16[2,512,512]{2,1,0:T(8,128)(2,1)S(1)}, u32[]{:S(2)}, u32[]{:S(2)}) collective-permute-start(bf16[2,512,512]{2,1,0:T(8,128)(2,1)S(1)} %pad_maximum_fusion.refs_0_.refs_1_), channel_id=1, source_target_pairs={{0,4},{1,5},{2,6},{3,7},{4,0},{5,1},{6,2},{7,3},{8,12},{9,13},{10,... | collective-permute-start | bytes 3145736 | tf_op jit(solution)/shard_map/ppermute | solution.py:188
  5.1 1.5 %collective-permute-start = (bf16[2,512,512]{2,1,0:T(8,128)(2,1)S(1)}, bf16[2,512,512]{2,1,0:T(8,128)(2,1)S(1)}, u32[]{:S(2)}, u32[]{:S(2)}) collective-permute-start(bf16[2,512,512]{2,1,0:T(8,128)(2,1)S(1)} %pad_maximum_fusion.refs_0_.refs_1_), channel_id=1, source_target_pairs={{0,2},{1,3},{2,0},{3,1},{4,6},{5,7},{6,4},{7,5},{8,10},{9,11},{10,... | collective-permute-start | bytes 3145736 | tf_op jit(solution)/shard_map/ppermute | solution.py:188
  6.7 1.6 %collective-permute-start.3 = (bf16[272,1024]{1,0:T(8,128)(2,1)S(1)}, bf16[272,1024]{1,0:T(8,128)(2,1)S(1)}, u32[]{:S(2)}, u32[]{:S(2)}) collective-permute-start(bf16[272,1024]{1,0:T(8,128)(2,1)S(1)} %fusion.1.refs_10_), channel_id=1, source_target_pairs={{0,8},{1,9},{2,10},{3,11},{4,12},{5,13},{6,14},{7,15},{8,0},{9,1},... | collective-permute-start | bytes 1671176 | tf_op jit(solution)/shard_map/ppermute | solution.py:188
  8.3 2.6 %collective-permute-start.2 = (bf16[272,1024]{1,0:T(8,128)(2,1)S(1)}, bf16[272,1024]{1,0:T(8,128)(2,1)S(1)}, u32[]{:S(2)}, u32[]{:S(2)}) collective-permute-start(bf16[272,1024]{1,0:T(8,128)(2,1)S(1)} %fusion.1.refs_10_), channel_id=1, source_target_pairs={{0,16},{1,17},{2,18},{3,19},{4,20},{5,21},{6,22},{7,23},{8,24},{9,... | collective-permute-start | bytes 1671176 | tf_op jit(solution)/shard_map/ppermute | solution.py:188
  10.9 22.1 %collective-permute-done.3.refs_11_ = bf16[272,1024]{1,0:T(8,128)(2,1)S(1)} collective-permute-done((bf16[272,1024]{1,0:T(8,128)(2,1)S(1)}, bf16[272,1024]{1,0:T(8,128)(2,1)S(1)}, u32[]{:S(2)}, u32[]{:S(2)}) %collective-permute-start.3) | collective-permute-done | bytes 557088 | tf_op jit(solution)/shard_map/ppermute | solution.py:188
  33.0 2.4 %collective-permute-done.2.refs_12_ = bf16[272,1024]{1,0:T(8,128)(2,1)S(1)} collective-permute-done((bf16[272,1024]{1,0:T(8,128)(2,1)S(1)}, bf16[272,1024]{1,0:T(8,128)(2,1)S(1)}, u32[]{:S(2)}, u32[]{:S(2)}) %collective-permute-start.2) | collective-permute-done | bytes 557088 | tf_op jit(solution)/shard_map/ppermute | solution.py:188
  35.4 0.6 collective-permute-start.9
  36.0 0.6 collective-permute-start.7
  36.6 0.5 collective-permute-start.6
  37.1 0.4 collective-permute-start.11
  37.6 8.4 %collective-permute-done.9.refs_8_.refs_9_ = bf16[512,512]{1,0:T(8,128)(2,1)S(1)} collective-permute-done((bf16[512,512]{1,0:T(8,128)(2,1)S(1)}, bf16[512,512]{1,0:T(8,128)(2,1)S(1)}, u32[]{:S(2)}, u32[]{:S(2)}) %collective-permute-start.9) | collective-permute-done | bytes 524320 | tf_op jit(solution)/shard_map/ppermute | solution.py:188
  46.0 0.4 collective-permute-done.7.refs_6_.refs_7_
  46.3 0.2 collective-permute-start.8
  46.5 5.2 %collective-permute-done.11.refs_13_ = bf16[272,1024]{1,0:T(8,128)(2,1)S(1)} collective-permute-done((bf16[272,1024]{1,0:T(8,128)(2,1)S(1)}, bf16[272,1024]{1,0:T(8,128)(2,1)S(1)}, u32[]{:S(2)}, u32[]{:S(2)}) %collective-permute-start.11) | collective-permute-done | bytes 557088 | tf_op jit(solution)/shard_map/ppermute | solution.py:188
  51.7 0.0 collective-permute-done.5.refs_3_.refs_4_
  51.7 11.0 %forward.1 = (bf16[2048,512]{1,0:T(8,128)(2,1)S(1)}, bf16[2048,512]{1,0:T(8,128)(2,1)S(1)}, bf16[2048,512]{1,0:T(8,128)(2,1)S(1)}) custom-call(bf16[2,512,512]{2,1,0:T(8,128)(2,1)S(1)} %pad_maximum_fusion.refs_0_.refs_1_, bf16[2,512,512]{2,1,0:T(8,128)(2,1)S(1)} %collective-permute-done.4.refs_1_.refs_2_, ...), custom_call_target="tpu_custom_call" | custom-call | flops 6442450944 | bytes 16777216 | tf_op jit(solution)/shard_map/forward/pallas_call | solution.py:240
  62.7 0.1 collective-permute-start.12
  62.8 3.1 %gradient.1 = (bf16[2,128,1024]{2,1,0:T(8,128)(2,1)S(1)}, bf16[2,128,1024]{2,1,0:T(8,128)(2,1)S(1)}) custom-call(bf16[2048,512]{1,0:T(8,128)(2,1)S(1)} %get-tuple-element.28.refs_0_, bf16[2,512,512]{2,1,0:T(8,128)(2,1)S(1)} %pad_maximum_fusion.refs_0_.refs_1_, bf16[2,512,512]{2,1,0:T(8,128)(2,1)S(1)} %collective-permute-done.4.refs_1_.refs_2_, ...), custom_call_target="tpu_custom_call" | custom-call | flops 2147483648 | bytes 8388608 | tf_op jit(solution)/shard_map/gradient/pallas_call | solution.py:263
  65.9 0.5 collective-permute-start.16
  66.4 0.5 collective-permute-done.12.other_ref
  66.9 0.5 pair_sum.1
  67.4 1.6 %collective-permute-start.13 = (bf16[512,512]{1,0:T(8,128)(2,1)S(1)}, bf16[512,512]{1,0:T(8,128)(2,1)S(1)}, u32[]{:S(2)}, u32[]{:S(2)}) collective-permute-start(bf16[512,512]{1,0:T(8,128)(2,1)S(1)} %get-tuple-element.25), channel_id=1, source_target_pairs={{0,2},{1,3},{2,0},{3,1},{4,6},{5,7},{6,4},{7,5},{8,10},{9,11},{10,... | collective-permute-start | bytes 1572872 | tf_op jit(solution)/shard_map/ppermute | solution.py:188
  69.0 1.5 %collective-permute-start.14 = (bf16[512,512]{1,0:T(8,128)(2,1)S(1)}, bf16[512,512]{1,0:T(8,128)(2,1)S(1)}, u32[]{:S(2)}, u32[]{:S(2)}) collective-permute-start(bf16[512,512]{1,0:T(8,128)(2,1)S(1)} %get-tuple-element.26), channel_id=1, source_target_pairs={{0,4},{1,5},{2,6},{3,7},{4,0},{5,1},{6,2},{7,3},{8,12},{9,13},{10,... | collective-permute-start | bytes 1572872 | tf_op jit(solution)/shard_map/ppermute | solution.py:188
  70.5 0.5 collective-permute-start.15
  71.0 9.3 %collective-permute-done.16 = bf16[2,128,1024]{2,1,0:T(8,128)(2,1)S(1)} collective-permute-done((bf16[2,128,1024]{2,1,0:T(8,128)(2,1)S(1)}, bf16[2,128,1024]{2,1,0:T(8,128)(2,1)S(1)}, u32[]{:S(2)}, u32[]{:S(2)}) %collective-permute-start.16) | collective-permute-done | bytes 524320 | tf_op jit(solution)/shard_map/ppermute | solution.py:188
  80.3 0.2 convert_add_fusion
  80.5 1.4 %collective-permute-start.17 = (bf16[128,1024]{1,0:T(8,128)(2,1)S(1)}, bf16[128,1024]{1,0:T(8,128)(2,1)S(1)}, u32[]{:S(2)}, u32[]{:S(2)}) collective-permute-start(bf16[128,1024]{1,0:T(8,128)(2,1)S(1)} %fusion.4), channel_id=1, source_target_pairs={{0,16},{1,17},{2,18},{3,19},{4,20},{5,21},{6,22},{7,23},{8,24},{9,... | collective-permute-start | bytes 786440 | tf_op jit(solution)/shard_map/ppermute | solution.py:188
  81.8 13.0 %collective-permute-done.17 = bf16[128,1024]{1,0:T(8,128)(2,1)S(1)} collective-permute-done((bf16[128,1024]{1,0:T(8,128)(2,1)S(1)}, bf16[128,1024]{1,0:T(8,128)(2,1)S(1)}, u32[]{:S(2)}, u32[]{:S(2)}) %collective-permute-start.17) | collective-permute-done | bytes 262176 | tf_op jit(solution)/shard_map/ppermute | solution.py:188
  94.9 0.9 fusion.3
  95.7 1.1 %add_convert_fusion = bf16[512,512]{1,0:T(8,128)(2,1)} fusion(bf16[512,512]{1,0:T(8,128)(2,1)S(1)} %collective-permute-done.15, bf16[512,512]{1,0:T(8,128)(2,1)S(1)} %collective-permute-done.14, bf16[512,512]{1,0:T(8,128)(2,1)S(1)} %collective-permute-done.13, bf16[512,512]{1,0:T(8,128)(2,1)S(1)} %get-tuple-element.24), kind=kLoop, calls=%fused_computation.4 | loop fusion | flops 2097152 | bytes 2621440 | tf_op jit(solution)/shard_map/convert_element_type | solution.py:296
  (21 shorter events, 0.2 us)
Async XLA Ops:
  0.6 6.0 %copy-start = (bf16[128,1024]{1,0:T(8,128)(2,1)S(1)}, bf16[128,1024]{1,0:T(8,128)(2,1)}, u32[]{:S(2)}) copy-start(bf16[128,1024]{1,0:T(8,128)(2,1)} %param.9) | copy-start | bytes 786436
  0.6 6.0 %copy-start.2 = (bf16[128]{0:T(256)(128)(2,1)S(1)}, bf16[128]{0:T(256)(128)(2,1)}, u32[]{:S(2)}) copy-start(bf16[128]{0:T(256)(128)(2,1)} %param.8) | copy-start | bytes 772
  0.7 6.0 %copy-start.1 = (bf16[128,1024]{1,0:T(8,128)(2,1)S(1)}, bf16[128,1024]{1,0:T(8,128)(2,1)}, u32[]{:S(2)}) copy-start(bf16[128,1024]{1,0:T(8,128)(2,1)} %param.7) | copy-start | bytes 786436
  2.0 33.3 %collective-permute-start.4 = (bf16[2,512,512]{2,1,0:T(8,128)(2,1)S(1)}, bf16[2,512,512]{2,1,0:T(8,128)(2,1)S(1)}, u32[]{:S(2)}, u32[]{:S(2)}) collective-permute-start(bf16[2,512,512]{2,1,0:T(8,128)(2,1)S(1)} %pad_maximum_fusion.refs_0_.refs_1_), channel_id=1, source_target_pairs={{0,1},{1,0},{2,3},{3,2},{4,5},{5,4},{6,7},{7,6},{8,9},{9,8},{10,11... | collective-permute-start | bytes 3145736 | tf_op jit(solution)/shard_map/ppermute | solution.py:188
  2.5 32.8 %collective-permute-start.1 = (bf16[2,512,512]{2,1,0:T(8,128)(2,1)S(1)}, bf16[2,512,512]{2,1,0:T(8,128)(2,1)S(1)}, u32[]{:S(2)}, u32[]{:S(2)}) collective-permute-start(bf16[2,512,512]{2,1,0:T(8,128)(2,1)S(1)} %pad_maximum_fusion.refs_0_.refs_1_), channel_id=1, source_target_pairs={{0,4},{1,5},{2,6},{3,7},{4,0},{5,1},{6,2},{7,3},{8,12},{9,13},{10,... | collective-permute-start | bytes 3145736 | tf_op jit(solution)/shard_map/ppermute | solution.py:188
  5.1 30.2 %collective-permute-start = (bf16[2,512,512]{2,1,0:T(8,128)(2,1)S(1)}, bf16[2,512,512]{2,1,0:T(8,128)(2,1)S(1)}, u32[]{:S(2)}, u32[]{:S(2)}) collective-permute-start(bf16[2,512,512]{2,1,0:T(8,128)(2,1)S(1)} %pad_maximum_fusion.refs_0_.refs_1_), channel_id=1, source_target_pairs={{0,2},{1,3},{2,0},{3,1},{4,6},{5,7},{6,4},{7,5},{8,10},{9,11},{10,... | collective-permute-start | bytes 3145736 | tf_op jit(solution)/shard_map/ppermute | solution.py:188
  6.7 26.3 %collective-permute-start.3 = (bf16[272,1024]{1,0:T(8,128)(2,1)S(1)}, bf16[272,1024]{1,0:T(8,128)(2,1)S(1)}, u32[]{:S(2)}, u32[]{:S(2)}) collective-permute-start(bf16[272,1024]{1,0:T(8,128)(2,1)S(1)} %fusion.1.refs_10_), channel_id=1, source_target_pairs={{0,8},{1,9},{2,10},{3,11},{4,12},{5,13},{6,14},{7,15},{8,0},{9,1},... | collective-permute-start | bytes 1671176 | tf_op jit(solution)/shard_map/ppermute | solution.py:188
  8.3 27.0 %collective-permute-start.2 = (bf16[272,1024]{1,0:T(8,128)(2,1)S(1)}, bf16[272,1024]{1,0:T(8,128)(2,1)S(1)}, u32[]{:S(2)}, u32[]{:S(2)}) collective-permute-start(bf16[272,1024]{1,0:T(8,128)(2,1)S(1)} %fusion.1.refs_10_), channel_id=1, source_target_pairs={{0,16},{1,17},{2,18},{3,19},{4,20},{5,21},{6,22},{7,23},{8,24},{9,... | collective-permute-start | bytes 1671176 | tf_op jit(solution)/shard_map/ppermute | solution.py:188
  35.4 10.6 %collective-permute-start.9 = (bf16[512,512]{1,0:T(8,128)(2,1)S(1)}, bf16[512,512]{1,0:T(8,128)(2,1)S(1)}, u32[]{:S(2)}, u32[]{:S(2)}) collective-permute-start(bf16[512,512]{1,0:T(8,128)(2,1)S(1)} %slice_bitcast_fusion.1), channel_id=1, source_target_pairs={{0,2},{1,3},{2,0},{3,1},{4,6},{5,7},{6,4},{7,5},{8,10},{9,11},{10,... | collective-permute-start | bytes 1572872 | tf_op jit(solution)/shard_map/ppermute | solution.py:188
  36.0 10.3 %collective-permute-start.7 = (bf16[512,512]{1,0:T(8,128)(2,1)S(1)}, bf16[512,512]{1,0:T(8,128)(2,1)S(1)}, u32[]{:S(2)}, u32[]{:S(2)}) collective-permute-start(bf16[512,512]{1,0:T(8,128)(2,1)S(1)} %slice_bitcast_fusion.2), channel_id=1, source_target_pairs={{0,4},{1,5},{2,6},{3,7},{4,0},{5,1},{6,2},{7,3},{8,12},{9,13},{10,... | collective-permute-start | bytes 1572872 | tf_op jit(solution)/shard_map/ppermute | solution.py:188
  36.6 15.1 %collective-permute-start.5 = (bf16[2,512,512]{2,1,0:T(8,128)(2,1)S(1)}, bf16[2,512,512]{2,1,0:T(8,128)(2,1)S(1)}, u32[]{:S(2)}, u32[]{:S(2)}) collective-permute-start(bf16[2,512,512]{2,1,0:T(8,128)(2,1)S(1)} %collective-permute-done.refs_2_.refs_3_), channel_id=1, source_target_pairs={{0,1},{1,0},{2,3},{3,2},{4,5},{5,4},{6,7},{7,6},{8,9},{9,8},{10,11... | collective-permute-start | bytes 3145736 | tf_op jit(solution)/shard_map/ppermute | solution.py:188
  36.6 15.1 %collective-permute-start.6 = (bf16[2,512,512]{2,1,0:T(8,128)(2,1)S(1)}, bf16[2,512,512]{2,1,0:T(8,128)(2,1)S(1)}, u32[]{:S(2)}, u32[]{:S(2)}) collective-permute-start(bf16[2,512,512]{2,1,0:T(8,128)(2,1)S(1)} %collective-permute-done.1.refs_4_.refs_5_), channel_id=1, source_target_pairs={{0,1},{1,0},{2,3},{3,2},{4,5},{5,4},{6,7},{7,6},{8,9},{9,8},{10,11... | collective-permute-start | bytes 3145736 | tf_op jit(solution)/shard_map/ppermute | solution.py:188
  37.1 14.5 %collective-permute-start.11 = (bf16[272,1024]{1,0:T(8,128)(2,1)S(1)}, bf16[272,1024]{1,0:T(8,128)(2,1)S(1)}, u32[]{:S(2)}, u32[]{:S(2)}) collective-permute-start(bf16[272,1024]{1,0:T(8,128)(2,1)S(1)} %collective-permute-done.2.refs_12_), channel_id=1, source_target_pairs={{0,8},{1,9},{2,10},{3,11},{4,12},{5,13},{6,14},{7,15},{8,0},{9,1},... | collective-permute-start | bytes 1671176 | tf_op jit(solution)/shard_map/ppermute | solution.py:188
  46.0 5.7 %collective-permute-start.10 = (bf16[512,512]{1,0:T(8,128)(2,1)S(1)}, bf16[512,512]{1,0:T(8,128)(2,1)S(1)}, u32[]{:S(2)}, u32[]{:S(2)}) collective-permute-start(bf16[512,512]{1,0:T(8,128)(2,1)S(1)} %collective-permute-done.9.refs_8_.refs_9_), channel_id=1, source_target_pairs={{0,1},{1,0},{2,3},{3,2},{4,5},{5,4},{6,7},{7,6},{8,9},{9,8},{10,11... | collective-permute-start | bytes 1572872 | tf_op jit(solution)/shard_map/ppermute | solution.py:188
  46.3 5.3 %collective-permute-start.8 = (bf16[512,512]{1,0:T(8,128)(2,1)S(1)}, bf16[512,512]{1,0:T(8,128)(2,1)S(1)}, u32[]{:S(2)}, u32[]{:S(2)}) collective-permute-start(bf16[512,512]{1,0:T(8,128)(2,1)S(1)} %collective-permute-done.7.refs_6_.refs_7_), channel_id=1, source_target_pairs={{0,1},{1,0},{2,3},{3,2},{4,5},{5,4},{6,7},{7,6},{8,9},{9,8},{10,11... | collective-permute-start | bytes 1572872 | tf_op jit(solution)/shard_map/ppermute | solution.py:188
  62.7 4.2 %collective-permute-start.12 = (bf16[2048,512]{1,0:T(8,128)(2,1)S(1)}, bf16[2048,512]{1,0:T(8,128)(2,1)S(1)}, u32[]{:S(2)}, u32[]{:S(2)}) collective-permute-start(bf16[2048,512]{1,0:T(8,128)(2,1)S(1)} %get-tuple-element.23), channel_id=1, source_target_pairs={{0,1},{1,0},{2,3},{3,2},{4,5},{5,4},{6,7},{7,6},{8,9},{9,8},{10,11... | collective-permute-start | bytes 6291464 | tf_op jit(solution)/shard_map/ppermute | solution.py:188
  65.9 14.4 %collective-permute-start.16 = (bf16[2,128,1024]{2,1,0:T(8,128)(2,1)S(1)}, bf16[2,128,1024]{2,1,0:T(8,128)(2,1)S(1)}, u32[]{:S(2)}, u32[]{:S(2)}) collective-permute-start(bf16[2,128,1024]{2,1,0:T(8,128)(2,1)S(1)} %get-tuple-element.31), channel_id=1, source_target_pairs={{0,8},{1,9},{2,10},{3,11},{4,12},{5,13},{6,14},{7,15},{8,0},{9,1},... | collective-permute-start | bytes 1572872 | tf_op jit(solution)/shard_map/ppermute | solution.py:188
  67.4 28.3 %collective-permute-start.13 = (bf16[512,512]{1,0:T(8,128)(2,1)S(1)}, bf16[512,512]{1,0:T(8,128)(2,1)S(1)}, u32[]{:S(2)}, u32[]{:S(2)}) collective-permute-start(bf16[512,512]{1,0:T(8,128)(2,1)S(1)} %get-tuple-element.25), channel_id=1, source_target_pairs={{0,2},{1,3},{2,0},{3,1},{4,6},{5,7},{6,4},{7,5},{8,10},{9,11},{10,... | collective-permute-start | bytes 1572872 | tf_op jit(solution)/shard_map/ppermute | solution.py:188
  69.0 26.8 %collective-permute-start.14 = (bf16[512,512]{1,0:T(8,128)(2,1)S(1)}, bf16[512,512]{1,0:T(8,128)(2,1)S(1)}, u32[]{:S(2)}, u32[]{:S(2)}) collective-permute-start(bf16[512,512]{1,0:T(8,128)(2,1)S(1)} %get-tuple-element.26), channel_id=1, source_target_pairs={{0,4},{1,5},{2,6},{3,7},{4,0},{5,1},{6,2},{7,3},{8,12},{9,13},{10,... | collective-permute-start | bytes 1572872 | tf_op jit(solution)/shard_map/ppermute | solution.py:188
  70.5 25.3 %collective-permute-start.15 = (bf16[512,512]{1,0:T(8,128)(2,1)S(1)}, bf16[512,512]{1,0:T(8,128)(2,1)S(1)}, u32[]{:S(2)}, u32[]{:S(2)}) collective-permute-start(bf16[512,512]{1,0:T(8,128)(2,1)S(1)} %get-tuple-element.27), channel_id=1, source_target_pairs={{0,6},{1,7},{2,4},{3,5},{4,2},{5,3},{6,0},{7,1},{8,14},{9,15},{10,... | collective-permute-start | bytes 1572872 | tf_op jit(solution)/shard_map/ppermute | solution.py:188
  80.5 14.4 %collective-permute-start.17 = (bf16[128,1024]{1,0:T(8,128)(2,1)S(1)}, bf16[128,1024]{1,0:T(8,128)(2,1)S(1)}, u32[]{:S(2)}, u32[]{:S(2)}) collective-permute-start(bf16[128,1024]{1,0:T(8,128)(2,1)S(1)} %fusion.4), channel_id=1, source_target_pairs={{0,16},{1,17},{2,18},{3,19},{4,20},{5,21},{6,22},{7,23},{8,24},{9,... | collective-permute-start | bytes 786440 | tf_op jit(solution)/shard_map/ppermute | solution.py:188

commit v5 on v1

--- a/solution.py
+++ b/solution.py
@@ -1,9 +1,18 @@
+import functools
 import math
 
 import jax
 import jax.numpy as jnp
 from jax import lax
+from jax.experimental import pallas as pl
+from jax.experimental.pallas import tpu as pltpu
 from jax.sharding import Mesh, PartitionSpec as P
+
+NEAR = 4
+AXES = ("far", "y", "x", "core")
+CONTRACT_LAST = (((1,), (1,)), ((), ()))
+CONTRACT_FIRST = (((0,), (0,)), ((), ()))
+VMEM_LIMIT = 28 * 1024 * 1024
 
 
 def gelu_parts(value):
@@ -17,15 +26,8 @@
     return (result, slope)
 
 
-NEAR = 4
-CONTRACT_LAST = (((1,), (1,)), ((), ()))
-CONTRACT_FIRST = (((0,), (0,)), ((), ()))
-
-
-def on_device(tokens, cotangent, w_in, b_in, w_out):
-    far = lax.axis_size("far")
-    near = lax.axis_size("near")
-    tensor = lax.axis_size("tensor")
+def on_device_any(tokens, cotangent, w_in, b_in, w_out):
+    far, near, tensor = lax.axis_size("far"), lax.axis_size("near"), lax.axis_size("tensor")
     rows, feats = tokens.shape
     owned, width = w_in.shape
     scale = 1.0 / math.sqrt(rows * far * near)
@@ -55,13 +57,371 @@
     return (mixed, grad_sum.astype(jnp.float32) * scale)
 
 
+def half_columns(core, shift, feats):
+    return pl.ds(pl.multiple_of(lax.rem(core + shift, 2) * feats, feats), feats)
+
+
+def side_by_side(core, pair, whole, start, sem):
+    rows, feats = pair[0].shape
+    return [
+        pltpu.make_async_copy(
+            pair[shift],
+            whole.at[pl.ds(start, rows), half_columns(core, shift, feats)],
+            sem.at[shift],
+        )
+        for shift in range(2)
+    ]
+
+
+def weight_copies(refs, owned, w_in, w_out, bias, sem):
+    ins, outs = [], []
+    for at, ref in enumerate(refs):
+        spot = pl.ds(at * owned, owned)
+        ins.append(pltpu.make_async_copy(ref.at[pl.ds(0, owned)], w_in.at[spot], sem.at[0, at]))
+        ins.append(
+            pltpu.make_async_copy(
+                ref.at[pl.ds(2 * owned, 16), pl.ds(0, owned)], bias.at[:, spot], sem.at[1, at]
+            )
+        )
+        outs.append(
+            pltpu.make_async_copy(ref.at[pl.ds(owned, owned)], w_out.at[spot], sem.at[2, at])
+        )
+    return ins, outs
+
+
+def run(copies, what):
+    for copy in copies:
+        getattr(copy, what)()
+
+
+def activate(tok, w_in, bias):
+    pre = lax.dot_general(
+        tok, w_in, CONTRACT_LAST, preferred_element_type=jnp.float32
+    ) + bias.astype(jnp.float32)
+    return gelu_parts(pre)
+
+
+def dot_last(left, right):
+    return lax.dot_general(left, right, CONTRACT_LAST, preferred_element_type=jnp.float32)
+
+
+def early_kernel(owned, *refs):
+    blocks = NEAR - 1
+    pair_refs, w_refs = refs[: 2 * blocks], refs[2 * blocks : 2 * blocks + 3]
+    act_ref, dpre_ref, tok, cot = refs[2 * blocks + 3 : 2 * blocks + 7]
+    w_in, w_out, bias, tok_sem, cot_sem, w_sem = refs[2 * blocks + 7 :]
+    core = lax.axis_index("core")
+    rows = pair_refs[0].shape[1]
+    ins, outs = weight_copies(w_refs, owned, w_in, w_out, bias, w_sem)
+    loads = []
+    for block in range(blocks):
+        first, second = pair_refs[2 * block], pair_refs[2 * block + 1]
+        loads.append(
+            side_by_side(core, (first.at[0], second.at[0]), tok, block * rows, tok_sem.at[block])
+            + side_by_side(core, (first.at[1], second.at[1]), cot, block * rows, cot_sem.at[block])
+        )
+    run(ins + outs, "start")
+    for load in loads:
+        run(load, "start")
+    run(ins + outs, "wait")
+    step = rows // 2
+    for block, load in enumerate(loads):
+        run(load, "wait")
+
+        @pl.loop(0, 2)
+        def _(sub):
+            spot = pl.ds(pl.multiple_of(block * rows + sub * step, step), step)
+            value, slope = activate(tok[spot, :], w_in[...], bias[0:1, :])
+            act_ref[spot, :] = value.astype(jnp.bfloat16)
+            dact = dot_last(cot[spot, :], w_out[...])
+            dpre_ref[spot, :] = (dact * slope).astype(jnp.bfloat16)
+
+
+def output_kernel(owned, *refs):
+    early_act, tok, diag_refs, w_refs = refs[0], refs[1], refs[2:4], refs[4:8]
+    mine_ref, other_ref, slope_ref, slope_diag_ref, tok_diag, w_out = refs[8:14]
+    act, w_in, bias, act_sem, tok_sem, w_sem = refs[14:]
+    core = lax.axis_index("core")
+    rows, feats = diag_refs[0].shape
+    early_rows, early_units = early_act.shape
+    ins, outs = weight_copies(w_refs, owned, w_in, w_out, bias, w_sem)
+    load = side_by_side(core, diag_refs, tok_diag, 0, tok_sem)
+    moved = pltpu.make_async_copy(
+        early_act, act.at[pl.ds(0, early_rows), pl.ds(0, early_units)], act_sem
+    )
+    run(ins + load + [moved] + outs, "start")
+    run(ins, "wait")
+    rest = slice(early_units, early_units + owned)
+    step = rows // 2
+
+    @pl.loop(0, early_rows // rows)
+    def _(block):
+        spot = pl.ds(pl.multiple_of(block * rows, rows), rows)
+        value, slope = activate(tok[spot, :], w_in[rest, :], bias[0:1, rest])
+        act[spot, rest] = value.astype(jnp.bfloat16)
+        slope_ref[spot, :] = slope
+
+    run(load, "wait")
+
+    @pl.loop(0, 2)
+    def _(sub):
+        spot = pl.ds(pl.multiple_of(sub * step, step), step)
+        value, slope = activate(tok_diag[spot, :], w_in[...], bias[0:1, :])
+        act[pl.ds(pl.multiple_of(early_rows + sub * step, step), step), :] = value.astype(
+            jnp.bfloat16
+        )
+        slope_diag_ref[spot, :] = slope
+
+    run([moved] + outs, "wait")
+
+    @pl.loop(0, NEAR)
+    def _(block):
+        spot = pl.ds(pl.multiple_of(block * rows, rows), rows)
+        for shift, ref in enumerate((mine_ref, other_ref)):
+            ref[spot, :] = jnp.dot(
+                act[spot, :],
+                w_out[:, half_columns(core, shift, feats)],
+                preferred_element_type=jnp.float32,
+            ).astype(jnp.bfloat16)
+
+
+def gradient_kernel(owned, *refs):
+    early_dpre, tok, tok_diag, cot, slope, slope_diag, w_out, diag_refs = refs[:7] + (refs[7:9],)
+    own_ref, one_ref, two_ref, three_ref, cot_diag, dpre, dpre_sem, cot_sem = refs[9:]
+    core = lax.axis_index("core")
+    rows = diag_refs[0].shape[0]
+    early_rows, early_units = early_dpre.shape
+    load = side_by_side(core, diag_refs, cot_diag, 0, cot_sem)
+    moved = pltpu.make_async_copy(
+        early_dpre, dpre.at[pl.ds(0, early_rows), pl.ds(0, early_units)], dpre_sem
+    )
+    run(load + [moved], "start")
+    rest = slice(early_units, early_units + owned)
+    step = rows // 2
+
+    @pl.loop(0, early_rows // rows)
+    def _(block):
+        spot = pl.ds(pl.multiple_of(block * rows, rows), rows)
+        dact = dot_last(cot[spot, :], w_out[rest, :])
+        dpre[spot, rest] = (dact * slope[spot, :]).astype(jnp.bfloat16)
+
+    run(load, "wait")
+
+    @pl.loop(0, 2)
+    def _(sub):
+        spot = pl.ds(pl.multiple_of(sub * step, step), step)
+        dact = dot_last(cot_diag[spot, :], w_out[...])
+        dpre[pl.ds(pl.multiple_of(early_rows + sub * step, step), step), :] = (
+            dact * slope_diag[spot, :]
+        ).astype(jnp.bfloat16)
+
+    run([moved], "wait")
+    for at, (first_ref, second_ref) in ((0, (own_ref, one_ref)), (2, (two_ref, three_ref))):
+        units = slice(at * owned, (at + 2) * owned)
+        grad = lax.dot_general(
+            dpre[:early_rows, units], tok[...], CONTRACT_FIRST, preferred_element_type=jnp.float32
+        ) + lax.dot_general(
+            dpre[early_rows:, units],
+            tok_diag[...],
+            CONTRACT_FIRST,
+            preferred_element_type=jnp.float32,
+        )
+        first_ref[...] = grad[:owned].astype(jnp.bfloat16)
+        second_ref[...] = grad[owned:].astype(jnp.bfloat16)
+
+
+def pair_kernel(rows, mine_ref, other_ref, *out_refs):
+    for block in range(NEAR):
+        spot = pl.ds(block * rows, rows)
+        out_refs[block][...] = (
+            mine_ref[spot, :].astype(jnp.float32) + other_ref[spot, :].astype(jnp.float32)
+        ).astype(jnp.bfloat16)
+
+
+def vmem(count):
+    return [pl.BlockSpec(memory_space=pltpu.VMEM)] * count
+
+
+def anywhere(count):
+    return [pl.BlockSpec(memory_space=pl.ANY)] * count
+
+
+def bf16(*shape):
+    return jax.ShapeDtypeStruct(shape, jnp.bfloat16)
+
+
+def permute(value, there):
+    pairs = []
+    for f in range(4):
+        for y in range(2):
+            for x in range(2):
+                for c in range(2):
+                    to = there(f, y, x, c)
+                    here = ((f * 2 + y) * 2 + x) * 2 + c
+                    pairs.append((here, ((to[0] * 2 + to[1]) * 2 + to[2]) * 2 + to[3]))
+    return lax.ppermute(value, AXES, pairs)
+
+
+def to_x(value):
+    return permute(value, lambda f, y, x, c: (f, y, 1 - x, c))
+
+
+def to_y(value):
+    return permute(value, lambda f, y, x, c: (f, 1 - y, x, c))
+
+
+def to_diagonal(value):
+    return permute(value, lambda f, y, x, c: (f, 1 - y, 1 - x, c))
+
+
+def to_core(value):
+    return permute(value, lambda f, y, x, c: (f, y, x, 1 - c))
+
+
+def to_far(value, flip):
+    return permute(value, lambda f, y, x, c: (f ^ flip, y, x, c))
+
+
+def on_device_lines(tokens, cotangent, w_in, b_in, w_out):
+    rows, feats = tokens.shape
+    owned, width = w_in.shape
+    units = 4 * owned
+    count = NEAR * rows
+    scale = 1.0 / math.sqrt(4 * count)
+    params = pltpu.CompilerParams(vmem_limit_bytes=VMEM_LIMIT)
+    dma = pltpu.SemaphoreType.DMA
+    barrier = lax.optimization_barrier
+    early_rows, early_units = (NEAR - 1) * rows, 3 * owned
+
+    def f32(*shape):
+        return jax.ShapeDtypeStruct(shape, jnp.float32)
+
+    def cost(flops, traffic):
+        return pl.CostEstimate(flops=flops, bytes_accessed=traffic, transcendentals=0)
+
+    bias_rows = jnp.pad(b_in.reshape(1, owned), ((0, 15), (0, width - owned)))
+    own_w = jnp.concatenate([w_in, w_out, bias_rows], 0)
+    own_w, tokens, cotangent = barrier((own_w, tokens, cotangent))
+    own = jnp.stack([tokens, cotangent])
+    w_two, w_one = to_far(own_w, 2), to_far(own_w, 1)
+    from_x, from_y = to_x(own), to_y(own)
+    own_other = to_core(own)
+    from_x, from_y, w_two, w_one, own_other = barrier((from_x, from_y, w_two, w_one, own_other))
+    tok_diag, cot_diag = to_y(from_x[0]), to_x(from_y[1])
+    w_three = to_far(w_two, 1)
+    x_other, y_other = to_core(from_x), to_core(from_y)
+    early_w = [own_w, w_one, w_two]
+    early_act, early_dpre, tok, cot = pl.pallas_call(
+        functools.partial(early_kernel, owned),
+        out_shape=(
+            bf16(early_rows, early_units),
+            bf16(early_rows, early_units),
+            bf16(early_rows, width),
+            bf16(early_rows, width),
+        ),
+        in_specs=anywhere(2 * (NEAR - 1) + 3),
+        out_specs=vmem(4),
+        scratch_shapes=[
+            pltpu.VMEM((early_units, width), jnp.bfloat16),
+            pltpu.VMEM((early_units, width), jnp.bfloat16),
+            pltpu.VMEM((16, early_units), jnp.bfloat16),
+            dma((NEAR - 1, 2)),
+            dma((NEAR - 1, 2)),
+            dma((3, 3)),
+        ],
+        compiler_params=params,
+        cost_estimate=cost(4 * early_rows * early_units * width, 8 * early_rows * width),
+        name="early",
+    )(own, own_other, from_x, x_other, from_y, y_other, *early_w)
+    tok_diag, cot_diag, early_act = barrier((tok_diag, cot_diag, early_act))
+    tok_diag_other, cot_diag_other = barrier((to_core(tok_diag), to_core(cot_diag)))
+
+    mine, other, slope, slope_diag, tok_last, w_out_all = pl.pallas_call(
+        functools.partial(output_kernel, owned),
+        out_shape=(
+            bf16(count, feats),
+            bf16(count, feats),
+            f32(early_rows, owned),
+            f32(rows, units),
+            bf16(rows, width),
+            bf16(units, width),
+        ),
+        in_specs=vmem(2) + anywhere(6),
+        out_specs=vmem(6),
+        scratch_shapes=[
+            pltpu.VMEM((count, units), jnp.bfloat16),
+            pltpu.VMEM((units, width), jnp.bfloat16),
+            pltpu.VMEM((16, units), jnp.bfloat16),
+            dma,
+            dma((2,)),
+            dma((3, 4)),
+        ],
+        compiler_params=params,
+        cost_estimate=cost(4 * count * units * width, 4 * count * width),
+        name="output",
+    )(early_act, tok, tok_diag, tok_diag_other, *early_w, w_three)
+    received = to_core(other)
+
+    grad_own, grad_one, grad_two, grad_three = pl.pallas_call(
+        functools.partial(gradient_kernel, owned),
+        out_shape=[bf16(owned, width)] * 4,
+        in_specs=vmem(7) + anywhere(2),
+        out_specs=vmem(4),
+        scratch_shapes=[
+            pltpu.VMEM((rows, width), jnp.bfloat16),
+            pltpu.VMEM((count, units), jnp.bfloat16),
+            dma,
+            dma((2,)),
+        ],
+        compiler_params=params,
+        cost_estimate=cost(4 * count * units * width, 4 * count * width),
+        name="gradient",
+    )(
+        early_dpre, tok, tok_last, cot, slope, slope_diag, w_out_all, cot_diag, cot_diag_other
+    )
+    relayed = to_far(grad_three, 1)
+    from_one = to_far(grad_one, 1)
+
+    sums = pl.pallas_call(
+        functools.partial(pair_kernel, rows),
+        out_shape=[bf16(rows, feats)] * NEAR,
+        in_specs=vmem(2),
+        out_specs=vmem(NEAR),
+        compiler_params=params,
+        name="pair_sum",
+    )(mine, received)
+    mixed_x, mixed_y, mixed_diag = to_x(sums[1]), to_y(sums[2]), to_diagonal(sums[3])
+    grad_two, _ = barrier((grad_two, sums[0]))
+    from_two = to_far(
+        (grad_two.astype(jnp.float32) + relayed.astype(jnp.float32)).astype(jnp.bfloat16), 2
+    )
+    total = (
+        grad_own.astype(jnp.float32)
+        + from_one.astype(jnp.float32)
+        + from_two.astype(jnp.float32)
+    )
+    mixed = (
+        sums[0].astype(jnp.float32)
+        + mixed_x.astype(jnp.float32)
+        + mixed_y.astype(jnp.float32)
+        + mixed_diag.astype(jnp.float32)
+    ).astype(jnp.bfloat16)
+    return (mixed, total * scale)
+
+
 def solution(mesh):
     dp, tensor = mesh.shape["dp"], mesh.shape["tensor"]
-    fine = Mesh(mesh.devices.reshape(dp // NEAR, NEAR, tensor), ("far", "near", "tensor"))
-    rows = ("far", "near")
-    owners = ("far", "near", "tensor")
-    in_specs = (P(rows, "tensor"), P(rows, "tensor"), P(owners, None), P(owners), P(owners, None))
-    out_specs = (P(rows, "tensor"), P(owners, None))
+    far = dp // NEAR
+    if tensor == 2 and far == 4:
+        fine = Mesh(mesh.devices.reshape(far, 2, 2, tensor), AXES)
+        rows, owners, halves = ("far", "y", "x"), AXES, "core"
+        body = on_device_lines
+    else:
+        fine = Mesh(mesh.devices.reshape(far, NEAR, tensor), ("far", "near", "tensor"))
+        rows, owners, halves = ("far", "near"), ("far", "near", "tensor"), "tensor"
+        body = on_device_any
+    in_specs = (P(rows, halves), P(rows, halves), P(owners, None), P(owners), P(owners, None))
+    out_specs = (P(rows, halves), P(owners, None))
     return jax.shard_map(
-        on_device, mesh=fine, in_specs=in_specs, out_specs=out_specs, check_vma=False
-    )
+        body, mesh=fine, in_specs=in_specs, out_specs=out_specs, check_vma=False
+    )

time: 251 us -> 94.4 us (0.38)
  waiting for transfers between devices: 175 us -> 54.1 us
  local copies, waits for them, and re-layouts: 33.8 us -> 0.25 us
  matrix products: 23 us -> 0 us
  starting transfers between devices: 0.2 us -> 18.4 us
  Pallas kernels: 0 us -> 17.5 us
  between operations: 13.8 us -> 0.73 us
    all_gather x3 -> x0, waiting for transfers between devices: 114 us -> none  [the longest x1 50 us: on_device(): lax.all_gather(jnp.concatenate([w_in, w_out, bias_rows], 0), 'far', axis=0)]
    reduce_scatter x2 -> x0, waiting for transfers between devices: 59.5 us -> none  [the longest x1 52.3 us: on_device(): lax.psum_scatter(term.reshape(near * tensor, rows, feats), ('near', 'tens...]
    ppermute x0 -> x19, waiting for transfers between devices: none -> 54.1 us  [permute(): return lax.ppermute(value, AXES, pairs)]
    dot_general x3 -> x0, matrix products: 23 us -> none  [the longest x1 11.2 us: on_device(): lax.dot_general(dpre, tok_full, CONTRACT_FIRST, preferred_element_type=jn...]
    reshape x3 -> x0, local copies, waits for them, and re-layouts: 20.9 us -> none  [the longest x1 7.86 us: on_device(): term = term.reshape(near, rows, tensor, feats).transpose(0, 2, 1, 3)]
    ppermute x0 -> x19, starting transfers between devices: none -> 18.4 us  [permute(): return lax.ppermute(value, AXES, pairs)]
    pallas_call x0 -> x4, Pallas kernels: none -> 17.5 us  [the longest x1 6.46 us: on_device_lines(): pl.pallas_call(functools.partial(output_kernel, owned), out_shape=(bf16(c...]
    unnamed x4, local copies, waits for them, and re-layouts: 6.33 us -> 0.18 us
  transfers between devices with their start and end apart: 5 -> 19, of which waited for: 5 -> 12; matrix products, arithmetic and copies ran while one was open for 14% -> 1% of each run, Pallas kernels for 0% -> 12%
where the time goes in v5:
time: 94.4 us; the launch traced here: 94.3 us
  waiting for transfers between devices  54.1 us (57%)
  starting transfers between devices  18.4 us (19%)
  Pallas kernels  17.5 us (19%)
  other arithmetic  3.3 us (3%)
    ppermute x19, waiting for transfers between devices, permute(): return lax.ppermute(value, AXES, pairs)  54.1 us
    ppermute x19, starting transfers between devices, permute(): return lax.ppermute(value, AXES, pairs)  18.4 us
    pallas_call x1, Pallas kernels, on_device_lines(): pl.pallas_call(functools.partial(output_kernel, owned), out_shape=(bf16(c...  6.46 us
    pallas_call x1, Pallas kernels, on_device_lines(): pl.pallas_call(functools.partial(early_kernel, owned), out_shape=(bf16(ea...  5.62 us
    pallas_call x1, Pallas kernels, on_device_lines(): pl.pallas_call(functools.partial(gradient_kernel, owned), out_shape=[bf16...  4.92 us
  transfers between devices with their start and end apart: 19, of which 12 were waited for; matrix products, arithmetic and copies ran while one was open for 1% of the time, Pallas kernels for 12%

profile of v5, /device:TPU:0, one launch (start us, length us, event | category | flops | bytes accessed | tf_op | source)
XLA Modules:
  0.0 94.3 jit_solution(2863682412401918805)
XLA Ops:
  0.7 1.2 %fusion.1.refs_6_.refs_4_ = bf16[272,1024]{1,0:T(8,128)(2,1)S(1)} fusion(bf16[1,128]{1,0:T(2,128)(2,1)} %bitcast.9, bf16[128,1024]{1,0:T(8,128)(2,1)} %param.9, bf16[128,1024]{1,0:T(8,128)(2,1)} %param.7), kind=kLoop, calls=%fused_computation.4 | loop fusion | flops 2228224 | bytes 1081600 | tf_op jit(solution)/shard_map/concatenate | solution.py:303
  2.1 0.5 collective-permute-start.4
  2.6 2.6 %collective-permute-start.1 = (bf16[2,512,512]{2,1,0:T(8,128)(2,1)S(1)}, bf16[2,512,512]{2,1,0:T(8,128)(2,1)S(1)}, u32[]{:S(2)}, u32[]{:S(2)}) collective-permute-start(bf16[2,512,512]{2,1,0:T(8,128)(2,1)S(1)} %pad_maximum_fusion.refs_0_), channel_id=1, source_target_pairs={{0,4},{1,5},{2,6},{3,7},{4,0},{5,1},{6,2},{7,3},{8,12},{9,13},{10,... | collective-permute-start | bytes 3145736 | tf_op jit(solution)/shard_map/ppermute | solution.py:262
  5.2 1.5 %collective-permute-start = (bf16[2,512,512]{2,1,0:T(8,128)(2,1)S(1)}, bf16[2,512,512]{2,1,0:T(8,128)(2,1)S(1)}, u32[]{:S(2)}, u32[]{:S(2)}) collective-permute-start(bf16[2,512,512]{2,1,0:T(8,128)(2,1)S(1)} %pad_maximum_fusion.refs_0_), channel_id=1, source_target_pairs={{0,2},{1,3},{2,0},{3,1},{4,6},{5,7},{6,4},{7,5},{8,10},{9,11},{10,... | collective-permute-start | bytes 3145736 | tf_op jit(solution)/shard_map/ppermute | solution.py:262
  6.7 1.6 %collective-permute-start.3 = (bf16[272,1024]{1,0:T(8,128)(2,1)S(1)}, bf16[272,1024]{1,0:T(8,128)(2,1)S(1)}, u32[]{:S(2)}, u32[]{:S(2)}) collective-permute-start(bf16[272,1024]{1,0:T(8,128)(2,1)S(1)} %fusion.1.refs_6_.refs_4_), channel_id=1, source_target_pairs={{0,8},{1,9},{2,10},{3,11},{4,12},{5,13},{6,14},{7,15},{8,0},{9,1},... | collective-permute-start | bytes 1671176 | tf_op jit(solution)/shard_map/ppermute | solution.py:262
  8.3 2.6 %collective-permute-start.2 = (bf16[272,1024]{1,0:T(8,128)(2,1)S(1)}, bf16[272,1024]{1,0:T(8,128)(2,1)S(1)}, u32[]{:S(2)}, u32[]{:S(2)}) collective-permute-start(bf16[272,1024]{1,0:T(8,128)(2,1)S(1)} %fusion.1.refs_6_.refs_4_), channel_id=1, source_target_pairs={{0,16},{1,17},{2,18},{3,19},{4,20},{5,21},{6,22},{7,23},{8,24},{9,... | collective-permute-start | bytes 1671176 | tf_op jit(solution)/shard_map/ppermute | solution.py:262
  10.9 22.1 %collective-permute-done.3.refs_7_.refs_5_ = bf16[272,1024]{1,0:T(8,128)(2,1)S(1)} collective-permute-done((bf16[272,1024]{1,0:T(8,128)(2,1)S(1)}, bf16[272,1024]{1,0:T(8,128)(2,1)S(1)}, u32[]{:S(2)}, u32[]{:S(2)}) %collective-permute-start.3) | collective-permute-done | bytes 557088 | tf_op jit(solution)/shard_map/ppermute | solution.py:262
  32.9 2.4 %collective-permute-done.2.refs_8_.refs_6_ = bf16[272,1024]{1,0:T(8,128)(2,1)S(1)} collective-permute-done((bf16[272,1024]{1,0:T(8,128)(2,1)S(1)}, bf16[272,1024]{1,0:T(8,128)(2,1)S(1)}, u32[]{:S(2)}, u32[]{:S(2)}) %collective-permute-start.2) | collective-permute-done | bytes 557088 | tf_op jit(solution)/shard_map/ppermute | solution.py:262
  35.4 0.5 collective-permute-start.8
  36.0 0.6 collective-permute-start.6
  36.6 0.5 collective-permute-start.5
  37.5 0.5 collective-permute-done.7.refs_3_
  38.0 1.5 %collective-permute-done.8.refs_5_ = bf16[2,512,512]{2,1,0:T(8,128)(2,1)S(1)} collective-permute-done((bf16[2,512,512]{2,1,0:T(8,128)(2,1)S(1)}, bf16[2,512,512]{2,1,0:T(8,128)(2,1)S(1)}, u32[]{:S(2)}, u32[]{:S(2)}) %collective-permute-start.8) | collective-permute-done | bytes 1048608 | tf_op jit(solution)/shard_map/ppermute | solution.py:262
  39.5 5.6 %early.1 = (bf16[1536,384]{1,0:T(8,128)(2,1)S(1)}, bf16[1536,384]{1,0:T(8,128)(2,1)S(1)}, bf16[1536,1024]{1,0:T(8,128)(2,1)S(1)}, bf16[1536,1024]{1,0:T(8,128)(2,1)S(1)}) custom-call(bf16[2,512,512]{2,1,0:T(8,128)(2,1)S(1)} %pad_maximum_fusion.refs_0_, bf16[2,512,512]{2,1,0:T(8,128)(2,1)S(1)} %collective-permute-done.4.refs_1_, ...), custom_call_target="tpu_custom_call" | custom-call | flops 2415919104 | bytes 12582912 | tf_op jit(solution)/shard_map/early/pallas_call | solution.py:314
  45.2 4.8 %collective-permute-done.6.refs_7_ = bf16[512,512]{1,0:T(8,128)(2,1)S(1)} collective-permute-done((bf16[512,512]{1,0:T(8,128)(2,1)S(1)}, bf16[512,512]{1,0:T(8,128)(2,1)S(1)}, u32[]{:S(2)}, u32[]{:S(2)}) %collective-permute-start.6) | collective-permute-done | bytes 524320 | tf_op jit(solution)/shard_map/ppermute | solution.py:262
  50.2 0.5 collective-permute-start.10
  50.7 1.4 %collective-permute-done.9.refs_3_ = bf16[512,512]{1,0:T(8,128)(2,1)S(1)} collective-permute-done((bf16[512,512]{1,0:T(8,128)(2,1)S(1)}, bf16[512,512]{1,0:T(8,128)(2,1)S(1)}, u32[]{:S(2)}, u32[]{:S(2)}) %collective-permute-start.9) | collective-permute-done | bytes 524320 | tf_op jit(solution)/shard_map/ppermute | solution.py:262
  52.1 0.7 collective-permute-done.10.refs_8_
  52.9 6.5 %output.1 = (bf16[2048,512]{1,0:T(8,128)(2,1)S(1)}, bf16[2048,512]{1,0:T(8,128)(2,1)S(1)}, f32[1536,128]{1,0:T(8,128)S(1)}, f32[512,512]{1,0:T(8,128)S(1)}, bf16...) custom-call(bf16[1536,384]{1,0:T(8,128)(2,1)S(1)} %get-tuple-element.43.refs_0_, ...), custom_call_target="tpu_custom_call" | custom-call | flops 4294967296 | bytes 8388608 | tf_op jit(solution)/shard_map/output/pallas_call | solution.py:339
  59.5 4.9 %gradient.1 = (bf16[128,1024]{1,0:T(8,128)(2,1)S(1)}, bf16[128,1024]{1,0:T(8,128)(2,1)S(1)}, bf16[128,1024]{1,0:T(8,128)(2,1)S(1)}, bf16[128,1024]{1,0:T(8,128)(2,1)S(1)}) custom-call(bf16[1536,384]{1,0:T(8,128)(2,1)S(1)} %get-tuple-element.54.refs_0_, bf16[1536,1024]{1,0:T(8,128)(2,1)S(1)} %get-tuple-element.44.refs_1_, ...), custom_call_target="tpu_custom_call" | custom-call | flops 4294967296 | bytes 8388608 | tf_op jit(solution)/shard_map/gradient/pallas_call | solution.py:365
  64.5 0.5 collective-permute-start.17
  65.0 1.6 %collective-permute-start.16 = (bf16[128,1024]{1,0:T(8,128)(2,1)S(1)}, bf16[128,1024]{1,0:T(8,128)(2,1)S(1)}, u32[]{:S(2)}, u32[]{:S(2)}) collective-permute-start(bf16[128,1024]{1,0:T(8,128)(2,1)S(1)} %get-tuple-element.62), channel_id=1, source_target_pairs={{0,8},{1,9},{2,10},{3,11},{4,12},{5,13},{6,14},{7,15},{8,0},{9,1},... | collective-permute-start | bytes 786440 | tf_op jit(solution)/shard_map/ppermute | solution.py:262
  67.1 1.6 %collective-permute-start.13 = (bf16[512,512]{1,0:T(8,128)(2,1)S(1)}, bf16[512,512]{1,0:T(8,128)(2,1)S(1)}, u32[]{:S(2)}, u32[]{:S(2)}) collective-permute-start(bf16[512,512]{1,0:T(8,128)(2,1)S(1)} %get-tuple-element.51), channel_id=1, source_target_pairs={{0,2},{1,3},{2,0},{3,1},{4,6},{5,7},{6,4},{7,5},{8,10},{9,11},{10,... | collective-permute-start | bytes 1572872 | tf_op jit(solution)/shard_map/ppermute | solution.py:262
  68.6 0.5 collective-permute-start.14
  69.1 1.5 %collective-permute-start.15 = (bf16[512,512]{1,0:T(8,128)(2,1)S(1)}, bf16[512,512]{1,0:T(8,128)(2,1)S(1)}, u32[]{:S(2)}, u32[]{:S(2)}) collective-permute-start(bf16[512,512]{1,0:T(8,128)(2,1)S(1)} %get-tuple-element.53), channel_id=1, source_target_pairs={{0,6},{1,7},{2,4},{3,5},{4,2},{5,3},{6,0},{7,1},{8,14},{9,15},{10,... | collective-permute-start | bytes 1572872 | tf_op jit(solution)/shard_map/ppermute | solution.py:262
  70.6 3.1 %collective-permute-done.17 = bf16[128,1024]{1,0:T(8,128)(2,1)S(1)} collective-permute-done((bf16[128,1024]{1,0:T(8,128)(2,1)S(1)}, bf16[128,1024]{1,0:T(8,128)(2,1)S(1)}, u32[]{:S(2)}, u32[]{:S(2)}) %collective-permute-start.17) | collective-permute-done | bytes 262176 | tf_op jit(solution)/shard_map/ppermute | solution.py:262
  73.8 1.1 %collective-permute-start.18 = (bf16[128,1024]{1,0:T(8,128)(2,1)S(1)}, bf16[128,1024]{1,0:T(8,128)(2,1)S(1)}, u32[]{:S(2)}, u32[]{:S(2)}) collective-permute-start(bf16[128,1024]{1,0:T(8,128)(2,1)S(1)} %add_convert_fusion.1), channel_id=1, source_target_pairs={{0,16},{1,17},{2,18},{3,19},{4,20},{5,21},{6,22},{7,23},{8,24},{9,... | collective-permute-start | bytes 786440 | tf_op jit(solution)/shard_map/ppermute | solution.py:262
  74.9 7.1 %collective-permute-done.16 = bf16[128,1024]{1,0:T(8,128)(2,1)S(1)} collective-permute-done((bf16[128,1024]{1,0:T(8,128)(2,1)S(1)}, bf16[128,1024]{1,0:T(8,128)(2,1)S(1)}, u32[]{:S(2)}, u32[]{:S(2)}) %collective-permute-start.16) | collective-permute-done | bytes 262176 | tf_op jit(solution)/shard_map/ppermute | solution.py:262
  82.0 5.6 %collective-permute-done.18 = bf16[128,1024]{1,0:T(8,128)(2,1)S(1)} collective-permute-done((bf16[128,1024]{1,0:T(8,128)(2,1)S(1)}, bf16[128,1024]{1,0:T(8,128)(2,1)S(1)}, u32[]{:S(2)}, u32[]{:S(2)}) %collective-permute-start.18) | collective-permute-done | bytes 262176 | tf_op jit(solution)/shard_map/ppermute | solution.py:262
  87.6 0.9 add_multiply_fusion
  88.5 4.7 %collective-permute-done.14 = bf16[512,512]{1,0:T(8,128)(2,1)S(1)} collective-permute-done((bf16[512,512]{1,0:T(8,128)(2,1)S(1)}, bf16[512,512]{1,0:T(8,128)(2,1)S(1)}, u32[]{:S(2)}, u32[]{:S(2)}) %collective-permute-start.14) | collective-permute-done | bytes 524320 | tf_op jit(solution)/shard_map/ppermute | solution.py:262
  93.2 1.1 %add_convert_fusion = bf16[512,512]{1,0:T(8,128)(2,1)} fusion(bf16[512,512]{1,0:T(8,128)(2,1)S(1)} %collective-permute-done.15, bf16[512,512]{1,0:T(8,128)(2,1)S(1)} %collective-permute-done.14, bf16[512,512]{1,0:T(8,128)(2,1)S(1)} %collective-permute-done.13, bf16[512,512]{1,0:T(8,128)(2,1)S(1)} %get-tuple-element.50), kind=kLoop, calls=%fused_computation.3 | loop fusion | flops 2097152 | bytes 2621440 | tf_op jit(solution)/shard_map/convert_element_type | solution.py:408
  (21 shorter events, 1.9 us)
Async XLA Ops:
  0.6 1.2 %copy-start = (bf16[512,512]{1,0:T(8,128)(2,1)S(1)}, bf16[512,512]{1,0:T(8,128)(2,1)}, u32[]{:S(2)}) copy-start(bf16[512,512]{1,0:T(8,128)(2,1)} %param.6) | copy-start | bytes 1572868
  0.6 1.4 %copy-start.1 = (bf16[512,512]{1,0:T(8,128)(2,1)S(1)}, bf16[512,512]{1,0:T(8,128)(2,1)}, u32[]{:S(2)}) copy-start(bf16[512,512]{1,0:T(8,128)(2,1)} %param.5) | copy-start | bytes 1572868
  2.1 33.2 %collective-permute-start.4 = (bf16[2,512,512]{2,1,0:T(8,128)(2,1)S(1)}, bf16[2,512,512]{2,1,0:T(8,128)(2,1)S(1)}, u32[]{:S(2)}, u32[]{:S(2)}) collective-permute-start(bf16[2,512,512]{2,1,0:T(8,128)(2,1)S(1)} %pad_maximum_fusion.refs_0_), channel_id=1, source_target_pairs={{0,1},{1,0},{2,3},{3,2},{4,5},{5,4},{6,7},{7,6},{8,9},{9,8},{10,11... | collective-permute-start | bytes 3145736 | tf_op jit(solution)/shard_map/ppermute | solution.py:262
  2.6 32.7 %collective-permute-start.1 = (bf16[2,512,512]{2,1,0:T(8,128)(2,1)S(1)}, bf16[2,512,512]{2,1,0:T(8,128)(2,1)S(1)}, u32[]{:S(2)}, u32[]{:S(2)}) collective-permute-start(bf16[2,512,512]{2,1,0:T(8,128)(2,1)S(1)} %pad_maximum_fusion.refs_0_), channel_id=1, source_target_pairs={{0,4},{1,5},{2,6},{3,7},{4,0},{5,1},{6,2},{7,3},{8,12},{9,13},{10,... | collective-permute-start | bytes 3145736 | tf_op jit(solution)/shard_map/ppermute | solution.py:262
  5.2 30.1 %collective-permute-start = (bf16[2,512,512]{2,1,0:T(8,128)(2,1)S(1)}, bf16[2,512,512]{2,1,0:T(8,128)(2,1)S(1)}, u32[]{:S(2)}, u32[]{:S(2)}) collective-permute-start(bf16[2,512,512]{2,1,0:T(8,128)(2,1)S(1)} %pad_maximum_fusion.refs_0_), channel_id=1, source_target_pairs={{0,2},{1,3},{2,0},{3,1},{4,6},{5,7},{6,4},{7,5},{8,10},{9,11},{10,... | collective-permute-start | bytes 3145736 | tf_op jit(solution)/shard_map/ppermute | solution.py:262
  6.7 26.2 %collective-permute-start.3 = (bf16[272,1024]{1,0:T(8,128)(2,1)S(1)}, bf16[272,1024]{1,0:T(8,128)(2,1)S(1)}, u32[]{:S(2)}, u32[]{:S(2)}) collective-permute-start(bf16[272,1024]{1,0:T(8,128)(2,1)S(1)} %fusion.1.refs_6_.refs_4_), channel_id=1, source_target_pairs={{0,8},{1,9},{2,10},{3,11},{4,12},{5,13},{6,14},{7,15},{8,0},{9,1},... | collective-permute-start | bytes 1671176 | tf_op jit(solution)/shard_map/ppermute | solution.py:262
  8.3 27.0 %collective-permute-start.2 = (bf16[272,1024]{1,0:T(8,128)(2,1)S(1)}, bf16[272,1024]{1,0:T(8,128)(2,1)S(1)}, u32[]{:S(2)}, u32[]{:S(2)}) collective-permute-start(bf16[272,1024]{1,0:T(8,128)(2,1)S(1)} %fusion.1.refs_6_.refs_4_), channel_id=1, source_target_pairs={{0,16},{1,17},{2,18},{3,19},{4,20},{5,21},{6,22},{7,23},{8,24},{9,... | collective-permute-start | bytes 1671176 | tf_op jit(solution)/shard_map/ppermute | solution.py:262
  35.3 2.7 %collective-permute-start.7 = (bf16[2,512,512]{2,1,0:T(8,128)(2,1)S(1)}, bf16[2,512,512]{2,1,0:T(8,128)(2,1)S(1)}, u32[]{:S(2)}, u32[]{:S(2)}) collective-permute-start(bf16[2,512,512]{2,1,0:T(8,128)(2,1)S(1)} %collective-permute-done.refs_2_), channel_id=1, source_target_pairs={{0,1},{1,0},{2,3},{3,2},{4,5},{5,4},{6,7},{7,6},{8,9},{9,8},{10,11... | collective-permute-start | bytes 3145736 | tf_op jit(solution)/shard_map/ppermute | solution.py:262
  35.4 4.1 %collective-permute-start.8 = (bf16[2,512,512]{2,1,0:T(8,128)(2,1)S(1)}, bf16[2,512,512]{2,1,0:T(8,128)(2,1)S(1)}, u32[]{:S(2)}, u32[]{:S(2)}) collective-permute-start(bf16[2,512,512]{2,1,0:T(8,128)(2,1)S(1)} %collective-permute-done.1.refs_4_), channel_id=1, source_target_pairs={{0,1},{1,0},{2,3},{3,2},{4,5},{5,4},{6,7},{7,6},{8,9},{9,8},{10,11... | collective-permute-start | bytes 3145736 | tf_op jit(solution)/shard_map/ppermute | solution.py:262
  36.0 14.0 %collective-permute-start.6 = (bf16[512,512]{1,0:T(8,128)(2,1)S(1)}, bf16[512,512]{1,0:T(8,128)(2,1)S(1)}, u32[]{:S(2)}, u32[]{:S(2)}) collective-permute-start(bf16[512,512]{1,0:T(8,128)(2,1)S(1)} %slice_bitcast_fusion), channel_id=1, source_target_pairs={{0,2},{1,3},{2,0},{3,1},{4,6},{5,7},{6,4},{7,5},{8,10},{9,11},{10,... | collective-permute-start | bytes 1572872 | tf_op jit(solution)/shard_map/ppermute | solution.py:262
  36.6 13.6 %collective-permute-start.5 = (bf16[512,512]{1,0:T(8,128)(2,1)S(1)}, bf16[512,512]{1,0:T(8,128)(2,1)S(1)}, u32[]{:S(2)}, u32[]{:S(2)}) collective-permute-start(bf16[512,512]{1,0:T(8,128)(2,1)S(1)} %slice_bitcast_fusion.1), channel_id=1, source_target_pairs={{0,4},{1,5},{2,6},{3,7},{4,0},{5,1},{6,2},{7,3},{8,12},{9,13},{10,... | collective-permute-start | bytes 1572872 | tf_op jit(solution)/shard_map/ppermute | solution.py:262
  37.1 15.8 %collective-permute-start.11 = (bf16[272,1024]{1,0:T(8,128)(2,1)S(1)}, bf16[272,1024]{1,0:T(8,128)(2,1)S(1)}, u32[]{:S(2)}, u32[]{:S(2)}) collective-permute-start(bf16[272,1024]{1,0:T(8,128)(2,1)S(1)} %collective-permute-done.2.refs_8_.refs_6_), channel_id=1, source_target_pairs={{0,8},{1,9},{2,10},{3,11},{4,12},{5,13},{6,14},{7,15},{8,0},{9,1},... | collective-permute-start | bytes 1671176 | tf_op jit(solution)/shard_map/ppermute | solution.py:262
  50.2 1.9 %collective-permute-start.9 = (bf16[512,512]{1,0:T(8,128)(2,1)S(1)}, bf16[512,512]{1,0:T(8,128)(2,1)S(1)}, u32[]{:S(2)}, u32[]{:S(2)}) collective-permute-start(bf16[512,512]{1,0:T(8,128)(2,1)S(1)} %collective-permute-done.5.refs_2_), channel_id=1, source_target_pairs={{0,1},{1,0},{2,3},{3,2},{4,5},{5,4},{6,7},{7,6},{8,9},{9,8},{10,11... | collective-permute-start | bytes 1572872 | tf_op jit(solution)/shard_map/ppermute | solution.py:262
  50.2 2.7 %collective-permute-start.10 = (bf16[512,512]{1,0:T(8,128)(2,1)S(1)}, bf16[512,512]{1,0:T(8,128)(2,1)S(1)}, u32[]{:S(2)}, u32[]{:S(2)}) collective-permute-start(bf16[512,512]{1,0:T(8,128)(2,1)S(1)} %collective-permute-done.6.refs_7_), channel_id=1, source_target_pairs={{0,1},{1,0},{2,3},{3,2},{4,5},{5,4},{6,7},{7,6},{8,9},{9,8},{10,11... | collective-permute-start | bytes 1572872 | tf_op jit(solution)/shard_map/ppermute | solution.py:262
  59.3 7.2 %collective-permute-start.12 = (bf16[2048,512]{1,0:T(8,128)(2,1)S(1)}, bf16[2048,512]{1,0:T(8,128)(2,1)S(1)}, u32[]{:S(2)}, u32[]{:S(2)}) collective-permute-start(bf16[2048,512]{1,0:T(8,128)(2,1)S(1)} %get-tuple-element.49), channel_id=1, source_target_pairs={{0,1},{1,0},{2,3},{3,2},{4,5},{5,4},{6,7},{7,6},{8,9},{9,8},{10,11... | collective-permute-start | bytes 6291464 | tf_op jit(solution)/shard_map/ppermute | solution.py:262
  64.5 9.2 %collective-permute-start.17 = (bf16[128,1024]{1,0:T(8,128)(2,1)S(1)}, bf16[128,1024]{1,0:T(8,128)(2,1)S(1)}, u32[]{:S(2)}, u32[]{:S(2)}) collective-permute-start(bf16[128,1024]{1,0:T(8,128)(2,1)S(1)} %get-tuple-element.65), channel_id=1, source_target_pairs={{0,8},{1,9},{2,10},{3,11},{4,12},{5,13},{6,14},{7,15},{8,0},{9,1},... | collective-permute-start | bytes 786440 | tf_op jit(solution)/shard_map/ppermute | solution.py:262
  65.0 17.0 %collective-permute-start.16 = (bf16[128,1024]{1,0:T(8,128)(2,1)S(1)}, bf16[128,1024]{1,0:T(8,128)(2,1)S(1)}, u32[]{:S(2)}, u32[]{:S(2)}) collective-permute-start(bf16[128,1024]{1,0:T(8,128)(2,1)S(1)} %get-tuple-element.62), channel_id=1, source_target_pairs={{0,8},{1,9},{2,10},{3,11},{4,12},{5,13},{6,14},{7,15},{8,0},{9,1},... | collective-permute-start | bytes 786440 | tf_op jit(solution)/shard_map/ppermute | solution.py:262
  67.1 21.4 %collective-permute-start.13 = (bf16[512,512]{1,0:T(8,128)(2,1)S(1)}, bf16[512,512]{1,0:T(8,128)(2,1)S(1)}, u32[]{:S(2)}, u32[]{:S(2)}) collective-permute-start(bf16[512,512]{1,0:T(8,128)(2,1)S(1)} %get-tuple-element.51), channel_id=1, source_target_pairs={{0,2},{1,3},{2,0},{3,1},{4,6},{5,7},{6,4},{7,5},{8,10},{9,11},{10,... | collective-permute-start | bytes 1572872 | tf_op jit(solution)/shard_map/ppermute | solution.py:262
  68.6 24.6 %collective-permute-start.14 = (bf16[512,512]{1,0:T(8,128)(2,1)S(1)}, bf16[512,512]{1,0:T(8,128)(2,1)S(1)}, u32[]{:S(2)}, u32[]{:S(2)}) collective-permute-start(bf16[512,512]{1,0:T(8,128)(2,1)S(1)} %get-tuple-element.52), channel_id=1, source_target_pairs={{0,4},{1,5},{2,6},{3,7},{4,0},{5,1},{6,2},{7,3},{8,12},{9,13},{10,... | collective-permute-start | bytes 1572872 | tf_op jit(solution)/shard_map/ppermute | solution.py:262
  69.1 24.1 %collective-permute-start.15 = (bf16[512,512]{1,0:T(8,128)(2,1)S(1)}, bf16[512,512]{1,0:T(8,128)(2,1)S(1)}, u32[]{:S(2)}, u32[]{:S(2)}) collective-permute-start(bf16[512,512]{1,0:T(8,128)(2,1)S(1)} %get-tuple-element.53), channel_id=1, source_target_pairs={{0,6},{1,7},{2,4},{3,5},{4,2},{5,3},{6,0},{7,1},{8,14},{9,15},{10,... | collective-permute-start | bytes 1572872 | tf_op jit(solution)/shard_map/ppermute | solution.py:262
  73.8 13.8 %collective-permute-start.18 = (bf16[128,1024]{1,0:T(8,128)(2,1)S(1)}, bf16[128,1024]{1,0:T(8,128)(2,1)S(1)}, u32[]{:S(2)}, u32[]{:S(2)}) collective-permute-start(bf16[128,1024]{1,0:T(8,128)(2,1)S(1)} %add_convert_fusion.1), channel_id=1, source_target_pairs={{0,16},{1,17},{2,18},{3,19},{4,20},{5,21},{6,22},{7,23},{8,24},{9,... | collective-permute-start | bytes 786440 | tf_op jit(solution)/shard_map/ppermute | solution.py:262

commit v6 on v5

--- a/solution.py
+++ b/solution.py
@@ -108,10 +108,11 @@
 def early_kernel(owned, *refs):
     blocks = NEAR - 1
     pair_refs, w_refs = refs[: 2 * blocks], refs[2 * blocks : 2 * blocks + 3]
-    act_ref, dpre_ref, tok, cot = refs[2 * blocks + 3 : 2 * blocks + 7]
-    w_in, w_out, bias, tok_sem, cot_sem, w_sem = refs[2 * blocks + 7 :]
+    act_ref, dpre_ref, mixed_ref, grad_ref, tok, cot = refs[2 * blocks + 3 : 2 * blocks + 9]
+    w_in, w_out, bias, dpre, tok_sem, cot_sem, w_sem = refs[2 * blocks + 9 :]
     core = lax.axis_index("core")
     rows = pair_refs[0].shape[1]
+    two = 2 * owned
     ins, outs = weight_copies(w_refs, owned, w_in, w_out, bias, w_sem)
     loads = []
     for block in range(blocks):
@@ -132,108 +133,106 @@
         def _(sub):
             spot = pl.ds(pl.multiple_of(block * rows + sub * step, step), step)
             value, slope = activate(tok[spot, :], w_in[...], bias[0:1, :])
-            act_ref[spot, :] = value.astype(jnp.bfloat16)
+            act = value.astype(jnp.bfloat16)
+            act_ref[spot, :] = act[:, two:]
             dact = dot_last(cot[spot, :], w_out[...])
-            dpre_ref[spot, :] = (dact * slope).astype(jnp.bfloat16)
+            terms = (dact * slope).astype(jnp.bfloat16)
+            dpre[spot, :] = terms[:, :two]
+            dpre_ref[spot, :] = terms[:, two:]
+            mixed_ref[spot, :] = jnp.dot(
+                act[:, :two], w_out[:two, :], preferred_element_type=jnp.float32
+            )
+
+    grad_ref[...] = dot_first(dpre[...], tok[...])
+
+
+def dot_first(left, right):
+    return lax.dot_general(left, right, CONTRACT_FIRST, preferred_element_type=jnp.float32)
 
 
 def output_kernel(owned, *refs):
-    early_act, tok, diag_refs, w_refs = refs[0], refs[1], refs[2:4], refs[4:8]
-    mine_ref, other_ref, slope_ref, slope_diag_ref, tok_diag, w_out = refs[8:14]
-    act, w_in, bias, act_sem, tok_sem, w_sem = refs[14:]
+    early_act, tok, early_mixed, w_refs = refs[0], refs[1], refs[2], refs[3:7]
+    mine_ref, other_ref, slope_ref, w_in, w_out, bias = refs[7:13]
+    act, act_sem, w_sem = refs[13:]
+    core = lax.axis_index("core")
+    early_rows, feats = mine_ref.shape
+    two = 2 * owned
+    ins, outs = weight_copies(w_refs, owned, w_in, w_out, bias, w_sem)
+    moved = pltpu.make_async_copy(early_act, act.at[:, pl.ds(0, owned)], act_sem)
+    run(ins + outs + [moved], "start")
+    run(ins + outs + [moved], "wait")
+    rest = slice(3 * owned, 4 * owned)
+    step = early_rows // 3
+
+    @pl.loop(0, 3)
+    def _(block):
+        spot = pl.ds(pl.multiple_of(block * step, step), step)
+        value, slope = activate(tok[spot, :], w_in[rest, :], bias[0:1, rest])
+        act[spot, owned:] = value.astype(jnp.bfloat16)
+        slope_ref[spot, :] = slope
+        for shift, ref in enumerate((mine_ref, other_ref)):
+            half = half_columns(core, shift, feats)
+            ref[spot, :] = (
+                early_mixed[spot, half]
+                + jnp.dot(act[spot, :], w_out[two:, half], preferred_element_type=jnp.float32)
+            ).astype(jnp.bfloat16)
+
+
+def diagonal_kernel(*refs):
+    w_in, w_out, bias, diag_refs = refs[0], refs[1], refs[2], refs[3:5]
+    mine_ref, other_ref, slope_ref, tok_diag, tok_sem = refs[5:]
     core = lax.axis_index("core")
     rows, feats = diag_refs[0].shape
-    early_rows, early_units = early_act.shape
-    ins, outs = weight_copies(w_refs, owned, w_in, w_out, bias, w_sem)
     load = side_by_side(core, diag_refs, tok_diag, 0, tok_sem)
-    moved = pltpu.make_async_copy(
-        early_act, act.at[pl.ds(0, early_rows), pl.ds(0, early_units)], act_sem
-    )
-    run(ins + load + [moved] + outs, "start")
-    run(ins, "wait")
-    rest = slice(early_units, early_units + owned)
+    run(load, "start")
+    run(load, "wait")
     step = rows // 2
-
-    @pl.loop(0, early_rows // rows)
-    def _(block):
-        spot = pl.ds(pl.multiple_of(block * rows, rows), rows)
-        value, slope = activate(tok[spot, :], w_in[rest, :], bias[0:1, rest])
-        act[spot, rest] = value.astype(jnp.bfloat16)
-        slope_ref[spot, :] = slope
-
-    run(load, "wait")
 
     @pl.loop(0, 2)
     def _(sub):
         spot = pl.ds(pl.multiple_of(sub * step, step), step)
         value, slope = activate(tok_diag[spot, :], w_in[...], bias[0:1, :])
-        act[pl.ds(pl.multiple_of(early_rows + sub * step, step), step), :] = value.astype(
-            jnp.bfloat16
-        )
-        slope_diag_ref[spot, :] = slope
-
-    run([moved] + outs, "wait")
-
-    @pl.loop(0, NEAR)
-    def _(block):
-        spot = pl.ds(pl.multiple_of(block * rows, rows), rows)
+        act = value.astype(jnp.bfloat16)
+        slope_ref[spot, :] = slope
         for shift, ref in enumerate((mine_ref, other_ref)):
             ref[spot, :] = jnp.dot(
-                act[spot, :],
-                w_out[:, half_columns(core, shift, feats)],
-                preferred_element_type=jnp.float32,
+                act, w_out[:, half_columns(core, shift, feats)], preferred_element_type=jnp.float32
             ).astype(jnp.bfloat16)
 
 
 def gradient_kernel(owned, *refs):
-    early_dpre, tok, tok_diag, cot, slope, slope_diag, w_out, diag_refs = refs[:7] + (refs[7:9],)
-    own_ref, one_ref, two_ref, three_ref, cot_diag, dpre, dpre_sem, cot_sem = refs[9:]
+    early_dpre, early_grad, tok, tok_diag, cot, slope, slope_diag, w_out = refs[:8]
+    diag_refs = refs[8:10]
+    own_ref, one_ref, two_ref, three_ref, cot_diag, dpre, dpre_diag, dpre_sem, cot_sem = refs[10:]
     core = lax.axis_index("core")
     rows = diag_refs[0].shape[0]
-    early_rows, early_units = early_dpre.shape
+    early_rows = early_dpre.shape[0]
+    two = 2 * owned
     load = side_by_side(core, diag_refs, cot_diag, 0, cot_sem)
-    moved = pltpu.make_async_copy(
-        early_dpre, dpre.at[pl.ds(0, early_rows), pl.ds(0, early_units)], dpre_sem
-    )
+    moved = pltpu.make_async_copy(early_dpre, dpre.at[:, pl.ds(0, owned)], dpre_sem)
     run(load + [moved], "start")
-    rest = slice(early_units, early_units + owned)
-    step = rows // 2
+    rest = slice(3 * owned, 4 * owned)
 
     @pl.loop(0, early_rows // rows)
     def _(block):
         spot = pl.ds(pl.multiple_of(block * rows, rows), rows)
         dact = dot_last(cot[spot, :], w_out[rest, :])
-        dpre[spot, rest] = (dact * slope[spot, :]).astype(jnp.bfloat16)
-
-    run(load, "wait")
-
-    @pl.loop(0, 2)
-    def _(sub):
-        spot = pl.ds(pl.multiple_of(sub * step, step), step)
-        dact = dot_last(cot_diag[spot, :], w_out[...])
-        dpre[pl.ds(pl.multiple_of(early_rows + sub * step, step), step), :] = (
-            dact * slope_diag[spot, :]
-        ).astype(jnp.bfloat16)
-
-    run([moved], "wait")
-    for at, (first_ref, second_ref) in ((0, (own_ref, one_ref)), (2, (two_ref, three_ref))):
-        units = slice(at * owned, (at + 2) * owned)
-        grad = lax.dot_general(
-            dpre[:early_rows, units], tok[...], CONTRACT_FIRST, preferred_element_type=jnp.float32
-        ) + lax.dot_general(
-            dpre[early_rows:, units],
-            tok_diag[...],
-            CONTRACT_FIRST,
-            preferred_element_type=jnp.float32,
-        )
-        first_ref[...] = grad[:owned].astype(jnp.bfloat16)
-        second_ref[...] = grad[owned:].astype(jnp.bfloat16)
+        dpre[spot, owned:] = (dact * slope[spot, :]).astype(jnp.bfloat16)
+
+    run(load + [moved], "wait")
+    dpre_diag[...] = (dot_last(cot_diag[...], w_out[...]) * slope_diag[...]).astype(jnp.bfloat16)
+    grad = dot_first(dpre[...], tok[...]) + dot_first(dpre_diag[:, two:], tok_diag[...])
+    two_ref[...] = grad[:owned].astype(jnp.bfloat16)
+    three_ref[...] = grad[owned:].astype(jnp.bfloat16)
+    grad = early_grad[...] + dot_first(dpre_diag[:, :two], tok_diag[...])
+    own_ref[...] = grad[:owned].astype(jnp.bfloat16)
+    one_ref[...] = grad[owned:].astype(jnp.bfloat16)
 
 
 def pair_kernel(rows, mine_ref, other_ref, *out_refs):
-    for block in range(NEAR):
+    for block, ref in enumerate(out_refs):
         spot = pl.ds(block * rows, rows)
-        out_refs[block][...] = (
+        ref[...] = (
             mine_ref[spot, :].astype(jnp.float32) + other_ref[spot, :].astype(jnp.float32)
         ).astype(jnp.bfloat16)
 
@@ -291,7 +290,7 @@
     params = pltpu.CompilerParams(vmem_limit_bytes=VMEM_LIMIT)
     dma = pltpu.SemaphoreType.DMA
     barrier = lax.optimization_barrier
-    early_rows, early_units = (NEAR - 1) * rows, 3 * owned
+    early_rows = (NEAR - 1) * rows
 
     def f32(*shape):
         return jax.ShapeDtypeStruct(shape, jnp.float32)
@@ -306,92 +305,116 @@
     w_two, w_one = to_far(own_w, 2), to_far(own_w, 1)
     from_x, from_y = to_x(own), to_y(own)
     own_other = to_core(own)
-    from_x, from_y, w_two, w_one, own_other = barrier((from_x, from_y, w_two, w_one, own_other))
     tok_diag, cot_diag = to_y(from_x[0]), to_x(from_y[1])
+    from_x, from_y, own_other, w_one, w_two = barrier((from_x, from_y, own_other, w_one, w_two))
+    x_other, y_other = to_core(from_x), to_core(from_y)
     w_three = to_far(w_two, 1)
-    x_other, y_other = to_core(from_x), to_core(from_y)
     early_w = [own_w, w_one, w_two]
-    early_act, early_dpre, tok, cot = pl.pallas_call(
+    early_act, early_dpre, early_mixed, early_grad, tok, cot = pl.pallas_call(
         functools.partial(early_kernel, owned),
         out_shape=(
-            bf16(early_rows, early_units),
-            bf16(early_rows, early_units),
+            bf16(early_rows, owned),
+            bf16(early_rows, owned),
+            f32(early_rows, width),
+            f32(2 * owned, width),
             bf16(early_rows, width),
             bf16(early_rows, width),
         ),
         in_specs=anywhere(2 * (NEAR - 1) + 3),
-        out_specs=vmem(4),
+        out_specs=vmem(6),
         scratch_shapes=[
-            pltpu.VMEM((early_units, width), jnp.bfloat16),
-            pltpu.VMEM((early_units, width), jnp.bfloat16),
-            pltpu.VMEM((16, early_units), jnp.bfloat16),
+            pltpu.VMEM((3 * owned, width), jnp.bfloat16),
+            pltpu.VMEM((3 * owned, width), jnp.bfloat16),
+            pltpu.VMEM((16, 3 * owned), jnp.bfloat16),
+            pltpu.VMEM((early_rows, 2 * owned), jnp.bfloat16),
             dma((NEAR - 1, 2)),
             dma((NEAR - 1, 2)),
             dma((3, 3)),
         ],
         compiler_params=params,
-        cost_estimate=cost(4 * early_rows * early_units * width, 8 * early_rows * width),
+        cost_estimate=cost(early_rows * units, early_rows),
         name="early",
     )(own, own_other, from_x, x_other, from_y, y_other, *early_w)
     tok_diag, cot_diag, early_act = barrier((tok_diag, cot_diag, early_act))
-    tok_diag_other, cot_diag_other = barrier((to_core(tok_diag), to_core(cot_diag)))
-
-    mine, other, slope, slope_diag, tok_last, w_out_all = pl.pallas_call(
+    tok_diag_other, cot_diag_other = to_core(tok_diag), to_core(cot_diag)
+
+    mine, other, slope, w_in_all, w_out_all, bias = pl.pallas_call(
         functools.partial(output_kernel, owned),
         out_shape=(
-            bf16(count, feats),
-            bf16(count, feats),
+            bf16(early_rows, feats),
+            bf16(early_rows, feats),
             f32(early_rows, owned),
-            f32(rows, units),
-            bf16(rows, width),
             bf16(units, width),
+            bf16(units, width),
+            bf16(16, units),
         ),
-        in_specs=vmem(2) + anywhere(6),
+        in_specs=vmem(3) + anywhere(4),
         out_specs=vmem(6),
-        scratch_shapes=[
-            pltpu.VMEM((count, units), jnp.bfloat16),
-            pltpu.VMEM((units, width), jnp.bfloat16),
-            pltpu.VMEM((16, units), jnp.bfloat16),
-            dma,
-            dma((2,)),
-            dma((3, 4)),
-        ],
-        compiler_params=params,
-        cost_estimate=cost(4 * count * units * width, 4 * count * width),
+        scratch_shapes=[pltpu.VMEM((early_rows, 2 * owned), jnp.bfloat16), dma, dma((3, 4))],
+        compiler_params=params,
+        cost_estimate=cost(8 * early_rows * units * width, 4 * count * width),
         name="output",
-    )(early_act, tok, tok_diag, tok_diag_other, *early_w, w_three)
+    )(early_act, tok, early_mixed, *early_w, w_three)
     received = to_core(other)
+
+    tok_diag_other, cot_diag_other, w_in_all = barrier((tok_diag_other, cot_diag_other, w_in_all))
+    mine_diag, other_diag, slope_diag, tok_last = pl.pallas_call(
+        diagonal_kernel,
+        out_shape=(bf16(rows, feats), bf16(rows, feats), f32(rows, units), bf16(rows, width)),
+        in_specs=vmem(3) + anywhere(2),
+        out_specs=vmem(4),
+        scratch_shapes=[dma((2,))],
+        compiler_params=params,
+        cost_estimate=cost(48 * rows * units * width, 4 * rows * width),
+        name="diagonal",
+    )(w_in_all, w_out_all, bias, tok_diag, tok_diag_other)
+    received_diag = to_core(other_diag)
+
+    mine, slope_diag = barrier((mine, slope_diag))
+    sums = pl.pallas_call(
+        functools.partial(pair_kernel, rows),
+        out_shape=[bf16(rows, feats)] * (NEAR - 1),
+        in_specs=vmem(2),
+        out_specs=vmem(NEAR - 1),
+        compiler_params=params,
+        name="pair_sum",
+    )(mine, received)
+    mixed_x, mixed_y = to_x(sums[1]), to_y(sums[2])
+    early_grad, mixed_own = barrier((early_grad, sums[0]))
 
     grad_own, grad_one, grad_two, grad_three = pl.pallas_call(
         functools.partial(gradient_kernel, owned),
         out_shape=[bf16(owned, width)] * 4,
-        in_specs=vmem(7) + anywhere(2),
+        in_specs=vmem(8) + anywhere(2),
         out_specs=vmem(4),
         scratch_shapes=[
             pltpu.VMEM((rows, width), jnp.bfloat16),
-            pltpu.VMEM((count, units), jnp.bfloat16),
+            pltpu.VMEM((early_rows, 2 * owned), jnp.bfloat16),
+            pltpu.VMEM((rows, units), jnp.bfloat16),
             dma,
             dma((2,)),
         ],
         compiler_params=params,
-        cost_estimate=cost(4 * count * units * width, 4 * count * width),
+        cost_estimate=cost(early_rows * units, early_rows),
         name="gradient",
     )(
-        early_dpre, tok, tok_last, cot, slope, slope_diag, w_out_all, cot_diag, cot_diag_other
+        early_dpre, early_grad, tok, tok_last, cot, slope, slope_diag, w_out_all,
+        cot_diag, cot_diag_other,
     )
     relayed = to_far(grad_three, 1)
     from_one = to_far(grad_one, 1)
 
-    sums = pl.pallas_call(
+    mine_diag, grad_own = barrier((mine_diag, grad_own))
+    (sum_diag,) = pl.pallas_call(
         functools.partial(pair_kernel, rows),
-        out_shape=[bf16(rows, feats)] * NEAR,
+        out_shape=[bf16(rows, feats)],
         in_specs=vmem(2),
-        out_specs=vmem(NEAR),
-        compiler_params=params,
-        name="pair_sum",
-    )(mine, received)
-    mixed_x, mixed_y, mixed_diag = to_x(sums[1]), to_y(sums[2]), to_diagonal(sums[3])
-    grad_two, _ = barrier((grad_two, sums[0]))
+        out_specs=vmem(1),
+        compiler_params=params,
+        name="pair_sum_diagonal",
+    )(mine_diag, received_diag)
+    mixed_diag = to_diagonal(sum_diag)
+    grad_two, mixed_x, mixed_y, _ = barrier((grad_two, mixed_x, mixed_y, sum_diag))
     from_two = to_far(
         (grad_two.astype(jnp.float32) + relayed.astype(jnp.float32)).astype(jnp.bfloat16), 2
     )
@@ -401,7 +424,7 @@
         + from_two.astype(jnp.float32)
     )
     mixed = (
-        sums[0].astype(jnp.float32)
+        mixed_own.astype(jnp.float32)
         + mixed_x.astype(jnp.float32)
         + mixed_y.astype(jnp.float32)
         + mixed_diag.astype(jnp.float32)

time: 94.4 us -> 98.6 us (1.044)
  the two profiles are of different devices: /device:TPU:0 before, /device:TPU:6 now
where the time goes in v6:
time: 98.6 us; the launch traced here: 98.5 us
  waiting for transfers between devices  56.8 us (58%)
  starting transfers between devices  18.9 us (19%)
  Pallas kernels  18.5 us (19%)
  other arithmetic  3.3 us (3%)
    ppermute x20, waiting for transfers between devices, permute(): return lax.ppermute(value, AXES, pairs)  56.8 us
    ppermute x20, starting transfers between devices, permute(): return lax.ppermute(value, AXES, pairs)  18.9 us
    pallas_call x1, Pallas kernels, on_device_lines(): pl.pallas_call(functools.partial(early_kernel, owned), out_shape=(bf16(ea...  7.57 us
    pallas_call x1, Pallas kernels, on_device_lines(): pl.pallas_call(functools.partial(output_kernel, owned), out_shape=(bf16(e...  4.35 us
    pallas_call x1, Pallas kernels, on_device_lines(): pl.pallas_call(functools.partial(gradient_kernel, owned), out_shape=[bf16...  3.78 us
    pallas_call x1, Pallas kernels, on_device_lines(): pl.pallas_call(diagonal_kernel, out_shape=(bf16(rows, feats), bf16(rows,...  2.28 us
  transfers between devices with their start and end apart: 20, of which 8 were waited for; matrix products, arithmetic and copies ran while one was open for 1% of the time, Pallas kernels for 19%

profile of v6, /device:TPU:6, one launch (start us, length us, event | category | flops | bytes accessed | tf_op | source)
XLA Modules:
  0.0 98.5 jit_solution(15948791873135318846)
XLA Ops:
  0.7 1.2 %fusion.1.refs_6_.refs_3_ = bf16[272,1024]{1,0:T(8,128)(2,1)S(1)} fusion(bf16[1,128]{1,0:T(2,128)(2,1)} %bitcast.9, bf16[128,1024]{1,0:T(8,128)(2,1)} %param.9, bf16[128,1024]{1,0:T(8,128)(2,1)} %param.7), kind=kLoop, calls=%fused_computation.4 | loop fusion | flops 2228224 | bytes 1081600 | tf_op jit(solution)/shard_map/concatenate | solution.py:302
  1.8 0.2 copy-done
  2.1 0.6 collective-permute-start
  2.8 2.0 %collective-permute-start.3 = (bf16[272,1024]{1,0:T(8,128)(2,1)S(1)}, bf16[272,1024]{1,0:T(8,128)(2,1)S(1)}, u32[]{:S(2)}, u32[]{:S(2)}) collective-permute-start(bf16[272,1024]{1,0:T(8,128)(2,1)S(1)} %fusion.1.refs_6_.refs_3_), channel_id=1, source_target_pairs={{0,8},{1,9},{2,10},{3,11},{4,12},{5,13},{6,14},{7,15},{8,0},{9,1},... | collective-permute-start | bytes 1671176 | tf_op jit(solution)/shard_map/ppermute | solution.py:261
  4.8 2.6 %collective-permute-start.4 = (bf16[272,1024]{1,0:T(8,128)(2,1)S(1)}, bf16[272,1024]{1,0:T(8,128)(2,1)S(1)}, u32[]{:S(2)}, u32[]{:S(2)}) collective-permute-start(bf16[272,1024]{1,0:T(8,128)(2,1)S(1)} %fusion.1.refs_6_.refs_3_), channel_id=1, source_target_pairs={{0,16},{1,17},{2,18},{3,19},{4,20},{5,21},{6,22},{7,23},{8,24},{9,... | collective-permute-start | bytes 1671176 | tf_op jit(solution)/shard_map/ppermute | solution.py:261
  7.4 22.5 %collective-permute-done.3.refs_7_.refs_4_ = bf16[272,1024]{1,0:T(8,128)(2,1)S(1)} collective-permute-done((bf16[272,1024]{1,0:T(8,128)(2,1)S(1)}, bf16[272,1024]{1,0:T(8,128)(2,1)S(1)}, u32[]{:S(2)}, u32[]{:S(2)}) %collective-permute-start.3) | collective-permute-done | bytes 557088 | tf_op jit(solution)/shard_map/ppermute | solution.py:261
  29.9 2.5 %collective-permute-done.4.refs_8_.refs_5_ = bf16[272,1024]{1,0:T(8,128)(2,1)S(1)} collective-permute-done((bf16[272,1024]{1,0:T(8,128)(2,1)S(1)}, bf16[272,1024]{1,0:T(8,128)(2,1)S(1)}, u32[]{:S(2)}, u32[]{:S(2)}) %collective-permute-start.4) | collective-permute-done | bytes 557088 | tf_op jit(solution)/shard_map/ppermute | solution.py:261
  32.5 0.5 collective-permute-start.6
  33.1 1.6 %collective-permute-start.7 = (bf16[512,512]{1,0:T(8,128)(2,1)S(1)}, bf16[512,512]{1,0:T(8,128)(2,1)S(1)}, u32[]{:S(2)}, u32[]{:S(2)}) collective-permute-start(bf16[512,512]{1,0:T(8,128)(2,1)S(1)} %slice_bitcast_fusion.1), channel_id=1, source_target_pairs={{0,4},{1,5},{2,6},{3,7},{4,0},{5,1},{6,2},{7,3},{8,12},{9,13},{10,... | collective-permute-start | bytes 1572872 | tf_op jit(solution)/shard_map/ppermute | solution.py:261
  34.6 0.4 collective-permute-start.9
  35.1 1.6 %collective-permute-start.8 = (bf16[512,512]{1,0:T(8,128)(2,1)S(1)}, bf16[512,512]{1,0:T(8,128)(2,1)S(1)}, u32[]{:S(2)}, u32[]{:S(2)}) collective-permute-start(bf16[512,512]{1,0:T(8,128)(2,1)S(1)} %slice_bitcast_fusion), channel_id=1, source_target_pairs={{0,2},{1,3},{2,0},{3,1},{4,6},{5,7},{6,4},{7,5},{8,10},{9,11},{10,... | collective-permute-start | bytes 1572872 | tf_op jit(solution)/shard_map/ppermute | solution.py:261
  36.7 7.6 %early.1 = (bf16[1536,128]{1,0:T(8,128)(2,1)S(1)}, bf16[1536,128]{1,0:T(8,128)(2,1)S(1)}, f32[1536,1024]{1,0:T(8,128)S(1)}, f32[256,1024]{1,0:T(8,128)S(1)}, bf1...) custom-call(bf16[2,512,512]{2,1,0:T(8,128)(2,1)S(1)} %pad_maximum_fusion.refs_0_, ...), custom_call_target="tpu_custom_call" | custom-call | flops 786432 | bytes 1536 | tf_op jit(solution)/shard_map/early/pallas_call | solution.py:313
  44.3 2.8 %collective-permute-done.7.refs_3_ = bf16[512,512]{1,0:T(8,128)(2,1)S(1)} collective-permute-done((bf16[512,512]{1,0:T(8,128)(2,1)S(1)}, bf16[512,512]{1,0:T(8,128)(2,1)S(1)}, u32[]{:S(2)}, u32[]{:S(2)}) %collective-permute-start.7) | collective-permute-done | bytes 524320 | tf_op jit(solution)/shard_map/ppermute | solution.py:261
  47.0 1.5 %collective-permute-done.8.refs_8_ = bf16[512,512]{1,0:T(8,128)(2,1)S(1)} collective-permute-done((bf16[512,512]{1,0:T(8,128)(2,1)S(1)}, bf16[512,512]{1,0:T(8,128)(2,1)S(1)}, u32[]{:S(2)}, u32[]{:S(2)}) %collective-permute-start.8) | collective-permute-done | bytes 524320 | tf_op jit(solution)/shard_map/ppermute | solution.py:261
  48.6 0.5 collective-permute-start.11
  49.1 4.4 %output.1 = (bf16[1536,512]{1,0:T(8,128)(2,1)S(1)}, bf16[1536,512]{1,0:T(8,128)(2,1)S(1)}, f32[1536,128]{1,0:T(8,128)S(1)}, bf16[512,1024]{1,0:T(8,128)(2,1)S(1)...) custom-call(bf16[1536,128]{1,0:T(8,128)(2,1)S(1)} %get-tuple-element.58.refs_0_, ...), custom_call_target="tpu_custom_call" | custom-call | flops 6442450944 | bytes 8388608 | tf_op jit(solution)/shard_map/output/pallas_call | solution.py:341
  53.5 2.3 %diagonal.1 = (bf16[512,512]{1,0:T(8,128)(2,1)S(1)}, bf16[512,512]{1,0:T(8,128)(2,1)S(1)}, f32[512,512]{1,0:T(8,128)S(1)}, bf16[512,1024]{1,0:T(8,128)(2,1)S(1)}) custom-call(bf16[512,1024]{1,0:T(8,128)(2,1)S(1)} %get-tuple-element.65.refs_0_, bf16[512,1024]{1,0:T(8,128)(2,1)S(1)} %get-tuple-element.66.refs_1_.refs_7_, ...), custom_call_target="tpu_custom_call" | custom-call | flops 12884901888 | bytes 2097152 | tf_op jit(solution)/shard_map/diagonal/pallas_call | solution.py:361
  55.8 0.5 collective-permute-start.15
  56.4 0.5 collective-permute-done.12.other_ref
  56.9 0.4 pair_sum.1
  57.3 1.6 %collective-permute-start.13 = (bf16[512,512]{1,0:T(8,128)(2,1)S(1)}, bf16[512,512]{1,0:T(8,128)(2,1)S(1)}, u32[]{:S(2)}, u32[]{:S(2)}) collective-permute-start(bf16[512,512]{1,0:T(8,128)(2,1)S(1)} %get-tuple-element.82), channel_id=1, source_target_pairs={{0,2},{1,3},{2,0},{3,1},{4,6},{5,7},{6,4},{7,5},{8,10},{9,11},{10,... | collective-permute-start | bytes 1572872 | tf_op jit(solution)/shard_map/ppermute | solution.py:261
  58.8 0.5 collective-permute-start.14
  59.3 3.8 %gradient.1 = (bf16[128,1024]{1,0:T(8,128)(2,1)S(1)}, bf16[128,1024]{1,0:T(8,128)(2,1)S(1)}, bf16[128,1024]{1,0:T(8,128)(2,1)S(1)}, bf16[128,1024]{1,0:T(8,128)(2,1)S(1)}) custom-call(bf16[1536,128]{1,0:T(8,128)(2,1)S(1)} %get-tuple-element.74.refs_0_, f32[256,1024]{1,0:T(8,128)S(1)} %get-tuple-element.75.refs_1_, ...), custom_call_target="tpu_custom_call" | custom-call | flops 786432 | bytes 1536 | tf_op jit(solution)/shard_map/gradient/pallas_call | solution.py:385
  63.3 1.6 %collective-permute-start.16 = (bf16[512,512]{1,0:T(8,128)(2,1)S(1)}, bf16[512,512]{1,0:T(8,128)(2,1)S(1)}, u32[]{:S(2)}, u32[]{:S(2)}) collective-permute-start(bf16[512,512]{1,0:T(8,128)(2,1)S(1)} %pair_sum_diagonal.1), channel_id=1, source_target_pairs={{0,6},{1,7},{2,4},{3,5},{4,2},{5,3},{6,0},{7,1},{8,14},{9,15},{10,... | collective-permute-start | bytes 1572872 | tf_op jit(solution)/shard_map/ppermute | solution.py:261
  64.8 1.6 %collective-permute-start.18 = (bf16[128,1024]{1,0:T(8,128)(2,1)S(1)}, bf16[128,1024]{1,0:T(8,128)(2,1)S(1)}, u32[]{:S(2)}, u32[]{:S(2)}) collective-permute-start(bf16[128,1024]{1,0:T(8,128)(2,1)S(1)} %get-tuple-element.93), channel_id=1, source_target_pairs={{0,8},{1,9},{2,10},{3,11},{4,12},{5,13},{6,14},{7,15},{8,0},{9,1},... | collective-permute-start | bytes 786440 | tf_op jit(solution)/shard_map/ppermute | solution.py:261
  66.4 0.4 collective-permute-start.17
  66.8 5.3 %collective-permute-done.13 = bf16[512,512]{1,0:T(8,128)(2,1)S(1)} collective-permute-done((bf16[512,512]{1,0:T(8,128)(2,1)S(1)}, bf16[512,512]{1,0:T(8,128)(2,1)S(1)}, u32[]{:S(2)}, u32[]{:S(2)}) %collective-permute-start.13) | collective-permute-done | bytes 524320 | tf_op jit(solution)/shard_map/ppermute | solution.py:261
  72.1 11.6 %collective-permute-done.14 = bf16[512,512]{1,0:T(8,128)(2,1)S(1)} collective-permute-done((bf16[512,512]{1,0:T(8,128)(2,1)S(1)}, bf16[512,512]{1,0:T(8,128)(2,1)S(1)}, u32[]{:S(2)}, u32[]{:S(2)}) %collective-permute-start.14) | collective-permute-done | bytes 524320 | tf_op jit(solution)/shard_map/ppermute | solution.py:261
  83.8 2.7 %collective-permute-start.19 = (bf16[128,1024]{1,0:T(8,128)(2,1)S(1)}, bf16[128,1024]{1,0:T(8,128)(2,1)S(1)}, u32[]{:S(2)}, u32[]{:S(2)}) collective-permute-start(bf16[128,1024]{1,0:T(8,128)(2,1)S(1)} %add_convert_fusion.1), channel_id=1, source_target_pairs={{0,16},{1,17},{2,18},{3,19},{4,20},{5,21},{6,22},{7,23},{8,24},{9,... | collective-permute-start | bytes 786440 | tf_op jit(solution)/shard_map/ppermute | solution.py:261
  86.5 1.1 %add_convert_fusion = bf16[512,512]{1,0:T(8,128)(2,1)} fusion(bf16[512,512]{1,0:T(8,128)(2,1)S(1)} %collective-permute-done.16, bf16[512,512]{1,0:T(8,128)(2,1)S(1)} %collective-permute-done.14, bf16[512,512]{1,0:T(8,128)(2,1)S(1)} %collective-permute-done.13, bf16[512,512]{1,0:T(8,128)(2,1)S(1)} %get-tuple-element.73), kind=kLoop, calls=%fused_computation.3 | loop fusion | flops 2097152 | bytes 2621440 | tf_op jit(solution)/shard_map/convert_element_type | solution.py:431
  87.5 10.1 %collective-permute-done.19 = bf16[128,1024]{1,0:T(8,128)(2,1)S(1)} collective-permute-done((bf16[128,1024]{1,0:T(8,128)(2,1)S(1)}, bf16[128,1024]{1,0:T(8,128)(2,1)S(1)}, u32[]{:S(2)}, u32[]{:S(2)}) %collective-permute-start.19) | collective-permute-done | bytes 262176 | tf_op jit(solution)/shard_map/ppermute | solution.py:261
  97.6 0.9 add_multiply_fusion
  (25 shorter events, 0.6 us)
Async XLA Ops:
  0.6 1.2 %copy-start.1 = (bf16[512,512]{1,0:T(8,128)(2,1)S(1)}, bf16[512,512]{1,0:T(8,128)(2,1)}, u32[]{:S(2)}) copy-start(bf16[512,512]{1,0:T(8,128)(2,1)} %param.5) | copy-start | bytes 1572868
  0.6 1.4 %copy-start = (bf16[512,512]{1,0:T(8,128)(2,1)S(1)}, bf16[512,512]{1,0:T(8,128)(2,1)}, u32[]{:S(2)}) copy-start(bf16[512,512]{1,0:T(8,128)(2,1)} %param.6) | copy-start | bytes 1572868
  2.1 30.3 %collective-permute-start = (bf16[2,512,512]{2,1,0:T(8,128)(2,1)S(1)}, bf16[2,512,512]{2,1,0:T(8,128)(2,1)S(1)}, u32[]{:S(2)}, u32[]{:S(2)}) collective-permute-start(bf16[2,512,512]{2,1,0:T(8,128)(2,1)S(1)} %pad_maximum_fusion.refs_0_), channel_id=1, source_target_pairs={{0,2},{1,3},{2,0},{3,1},{4,6},{5,7},{6,4},{7,5},{8,10},{9,11},{10,... | collective-permute-start | bytes 3145736 | tf_op jit(solution)/shard_map/ppermute | solution.py:261
  2.7 29.7 %collective-permute-start.1 = (bf16[2,512,512]{2,1,0:T(8,128)(2,1)S(1)}, bf16[2,512,512]{2,1,0:T(8,128)(2,1)S(1)}, u32[]{:S(2)}, u32[]{:S(2)}) collective-permute-start(bf16[2,512,512]{2,1,0:T(8,128)(2,1)S(1)} %pad_maximum_fusion.refs_0_), channel_id=1, source_target_pairs={{0,4},{1,5},{2,6},{3,7},{4,0},{5,1},{6,2},{7,3},{8,12},{9,13},{10,... | collective-permute-start | bytes 3145736 | tf_op jit(solution)/shard_map/ppermute | solution.py:261
  2.8 29.7 %collective-permute-start.2 = (bf16[2,512,512]{2,1,0:T(8,128)(2,1)S(1)}, bf16[2,512,512]{2,1,0:T(8,128)(2,1)S(1)}, u32[]{:S(2)}, u32[]{:S(2)}) collective-permute-start(bf16[2,512,512]{2,1,0:T(8,128)(2,1)S(1)} %pad_maximum_fusion.refs_0_), channel_id=1, source_target_pairs={{0,1},{1,0},{2,3},{3,2},{4,5},{5,4},{6,7},{7,6},{8,9},{9,8},{10,11... | collective-permute-start | bytes 3145736 | tf_op jit(solution)/shard_map/ppermute | solution.py:261
  2.8 27.1 %collective-permute-start.3 = (bf16[272,1024]{1,0:T(8,128)(2,1)S(1)}, bf16[272,1024]{1,0:T(8,128)(2,1)S(1)}, u32[]{:S(2)}, u32[]{:S(2)}) collective-permute-start(bf16[272,1024]{1,0:T(8,128)(2,1)S(1)} %fusion.1.refs_6_.refs_3_), channel_id=1, source_target_pairs={{0,8},{1,9},{2,10},{3,11},{4,12},{5,13},{6,14},{7,15},{8,0},{9,1},... | collective-permute-start | bytes 1671176 | tf_op jit(solution)/shard_map/ppermute | solution.py:261
  4.8 27.6 %collective-permute-start.4 = (bf16[272,1024]{1,0:T(8,128)(2,1)S(1)}, bf16[272,1024]{1,0:T(8,128)(2,1)S(1)}, u32[]{:S(2)}, u32[]{:S(2)}) collective-permute-start(bf16[272,1024]{1,0:T(8,128)(2,1)S(1)} %fusion.1.refs_6_.refs_3_), channel_id=1, source_target_pairs={{0,16},{1,17},{2,18},{3,19},{4,20},{5,21},{6,22},{7,23},{8,24},{9,... | collective-permute-start | bytes 1671176 | tf_op jit(solution)/shard_map/ppermute | solution.py:261
  32.4 4.2 %collective-permute-start.5 = (bf16[2,512,512]{2,1,0:T(8,128)(2,1)S(1)}, bf16[2,512,512]{2,1,0:T(8,128)(2,1)S(1)}, u32[]{:S(2)}, u32[]{:S(2)}) collective-permute-start(bf16[2,512,512]{2,1,0:T(8,128)(2,1)S(1)} %collective-permute-done.refs_2_), channel_id=1, source_target_pairs={{0,1},{1,0},{2,3},{3,2},{4,5},{5,4},{6,7},{7,6},{8,9},{9,8},{10,11... | collective-permute-start | bytes 3145736 | tf_op jit(solution)/shard_map/ppermute | solution.py:261
  32.5 4.2 %collective-permute-start.6 = (bf16[2,512,512]{2,1,0:T(8,128)(2,1)S(1)}, bf16[2,512,512]{2,1,0:T(8,128)(2,1)S(1)}, u32[]{:S(2)}, u32[]{:S(2)}) collective-permute-start(bf16[2,512,512]{2,1,0:T(8,128)(2,1)S(1)} %collective-permute-done.1.refs_4_), channel_id=1, source_target_pairs={{0,1},{1,0},{2,3},{3,2},{4,5},{5,4},{6,7},{7,6},{8,9},{9,8},{10,11... | collective-permute-start | bytes 3145736 | tf_op jit(solution)/shard_map/ppermute | solution.py:261
  33.1 14.0 %collective-permute-start.7 = (bf16[512,512]{1,0:T(8,128)(2,1)S(1)}, bf16[512,512]{1,0:T(8,128)(2,1)S(1)}, u32[]{:S(2)}, u32[]{:S(2)}) collective-permute-start(bf16[512,512]{1,0:T(8,128)(2,1)S(1)} %slice_bitcast_fusion.1), channel_id=1, source_target_pairs={{0,4},{1,5},{2,6},{3,7},{4,0},{5,1},{6,2},{7,3},{8,12},{9,13},{10,... | collective-permute-start | bytes 1572872 | tf_op jit(solution)/shard_map/ppermute | solution.py:261
  34.6 14.4 %collective-permute-start.9 = (bf16[272,1024]{1,0:T(8,128)(2,1)S(1)}, bf16[272,1024]{1,0:T(8,128)(2,1)S(1)}, u32[]{:S(2)}, u32[]{:S(2)}) collective-permute-start(bf16[272,1024]{1,0:T(8,128)(2,1)S(1)} %collective-permute-done.4.refs_8_.refs_5_), channel_id=1, source_target_pairs={{0,8},{1,9},{2,10},{3,11},{4,12},{5,13},{6,14},{7,15},{8,0},{9,1},... | collective-permute-start | bytes 1671176 | tf_op jit(solution)/shard_map/ppermute | solution.py:261
  35.1 13.4 %collective-permute-start.8 = (bf16[512,512]{1,0:T(8,128)(2,1)S(1)}, bf16[512,512]{1,0:T(8,128)(2,1)S(1)}, u32[]{:S(2)}, u32[]{:S(2)}) collective-permute-start(bf16[512,512]{1,0:T(8,128)(2,1)S(1)} %slice_bitcast_fusion), channel_id=1, source_target_pairs={{0,2},{1,3},{2,0},{3,1},{4,6},{5,7},{6,4},{7,5},{8,10},{9,11},{10,... | collective-permute-start | bytes 1572872 | tf_op jit(solution)/shard_map/ppermute | solution.py:261
  48.5 5.0 %collective-permute-start.10 = (bf16[512,512]{1,0:T(8,128)(2,1)S(1)}, bf16[512,512]{1,0:T(8,128)(2,1)S(1)}, u32[]{:S(2)}, u32[]{:S(2)}) collective-permute-start(bf16[512,512]{1,0:T(8,128)(2,1)S(1)} %collective-permute-done.7.refs_3_), channel_id=1, source_target_pairs={{0,1},{1,0},{2,3},{3,2},{4,5},{5,4},{6,7},{7,6},{8,9},{9,8},{10,11... | collective-permute-start | bytes 1572872 | tf_op jit(solution)/shard_map/ppermute | solution.py:261
  48.6 5.0 %collective-permute-start.11 = (bf16[512,512]{1,0:T(8,128)(2,1)S(1)}, bf16[512,512]{1,0:T(8,128)(2,1)S(1)}, u32[]{:S(2)}, u32[]{:S(2)}) collective-permute-start(bf16[512,512]{1,0:T(8,128)(2,1)S(1)} %collective-permute-done.8.refs_8_), channel_id=1, source_target_pairs={{0,1},{1,0},{2,3},{3,2},{4,5},{5,4},{6,7},{7,6},{8,9},{9,8},{10,11... | collective-permute-start | bytes 1572872 | tf_op jit(solution)/shard_map/ppermute | solution.py:261
  53.4 3.5 %collective-permute-start.12 = (bf16[1536,512]{1,0:T(8,128)(2,1)S(1)}, bf16[1536,512]{1,0:T(8,128)(2,1)S(1)}, u32[]{:S(2)}, u32[]{:S(2)}) collective-permute-start(bf16[1536,512]{1,0:T(8,128)(2,1)S(1)} %get-tuple-element.71), channel_id=1, source_target_pairs={{0,1},{1,0},{2,3},{3,2},{4,5},{5,4},{6,7},{7,6},{8,9},{9,8},{10,11... | collective-permute-start | bytes 4718600 | tf_op jit(solution)/shard_map/ppermute | solution.py:261
  55.8 7.3 %collective-permute-start.15 = (bf16[512,512]{1,0:T(8,128)(2,1)S(1)}, bf16[512,512]{1,0:T(8,128)(2,1)S(1)}, u32[]{:S(2)}, u32[]{:S(2)}) collective-permute-start(bf16[512,512]{1,0:T(8,128)(2,1)S(1)} %get-tuple-element.87), channel_id=1, source_target_pairs={{0,1},{1,0},{2,3},{3,2},{4,5},{5,4},{6,7},{7,6},{8,9},{9,8},{10,11... | collective-permute-start | bytes 1572872 | tf_op jit(solution)/shard_map/ppermute | solution.py:261
  57.3 14.8 %collective-permute-start.13 = (bf16[512,512]{1,0:T(8,128)(2,1)S(1)}, bf16[512,512]{1,0:T(8,128)(2,1)S(1)}, u32[]{:S(2)}, u32[]{:S(2)}) collective-permute-start(bf16[512,512]{1,0:T(8,128)(2,1)S(1)} %get-tuple-element.82), channel_id=1, source_target_pairs={{0,2},{1,3},{2,0},{3,1},{4,6},{5,7},{6,4},{7,5},{8,10},{9,11},{10,... | collective-permute-start | bytes 1572872 | tf_op jit(solution)/shard_map/ppermute | solution.py:261
  58.8 24.9 %collective-permute-start.14 = (bf16[512,512]{1,0:T(8,128)(2,1)S(1)}, bf16[512,512]{1,0:T(8,128)(2,1)S(1)}, u32[]{:S(2)}, u32[]{:S(2)}) collective-permute-start(bf16[512,512]{1,0:T(8,128)(2,1)S(1)} %get-tuple-element.83), channel_id=1, source_target_pairs={{0,4},{1,5},{2,6},{3,7},{4,0},{5,1},{6,2},{7,3},{8,12},{9,13},{10,... | collective-permute-start | bytes 1572872 | tf_op jit(solution)/shard_map/ppermute | solution.py:261
  63.3 23.2 %collective-permute-start.16 = (bf16[512,512]{1,0:T(8,128)(2,1)S(1)}, bf16[512,512]{1,0:T(8,128)(2,1)S(1)}, u32[]{:S(2)}, u32[]{:S(2)}) collective-permute-start(bf16[512,512]{1,0:T(8,128)(2,1)S(1)} %pair_sum_diagonal.1), channel_id=1, source_target_pairs={{0,6},{1,7},{2,4},{3,5},{4,2},{5,3},{6,0},{7,1},{8,14},{9,15},{10,... | collective-permute-start | bytes 1572872 | tf_op jit(solution)/shard_map/ppermute | solution.py:261
  64.8 18.9 %collective-permute-start.18 = (bf16[128,1024]{1,0:T(8,128)(2,1)S(1)}, bf16[128,1024]{1,0:T(8,128)(2,1)S(1)}, u32[]{:S(2)}, u32[]{:S(2)}) collective-permute-start(bf16[128,1024]{1,0:T(8,128)(2,1)S(1)} %get-tuple-element.93), channel_id=1, source_target_pairs={{0,8},{1,9},{2,10},{3,11},{4,12},{5,13},{6,14},{7,15},{8,0},{9,1},... | collective-permute-start | bytes 786440 | tf_op jit(solution)/shard_map/ppermute | solution.py:261
  66.4 21.1 %collective-permute-start.17 = (bf16[128,1024]{1,0:T(8,128)(2,1)S(1)}, bf16[128,1024]{1,0:T(8,128)(2,1)S(1)}, u32[]{:S(2)}, u32[]{:S(2)}) collective-permute-start(bf16[128,1024]{1,0:T(8,128)(2,1)S(1)} %get-tuple-element.91), channel_id=1, source_target_pairs={{0,8},{1,9},{2,10},{3,11},{4,12},{5,13},{6,14},{7,15},{8,0},{9,1},... | collective-permute-start | bytes 786440 | tf_op jit(solution)/shard_map/ppermute | solution.py:261
  83.8 13.8 %collective-permute-start.19 = (bf16[128,1024]{1,0:T(8,128)(2,1)S(1)}, bf16[128,1024]{1,0:T(8,128)(2,1)S(1)}, u32[]{:S(2)}, u32[]{:S(2)}) collective-permute-start(bf16[128,1024]{1,0:T(8,128)(2,1)S(1)} %add_convert_fusion.1), channel_id=1, source_target_pairs={{0,16},{1,17},{2,18},{3,19},{4,20},{5,21},{6,22},{7,23},{8,24},{9,... | collective-permute-start | bytes 786440 | tf_op jit(solution)/shard_map/ppermute | solution.py:261

commit v7 on v6

--- a/solution.py
+++ b/solution.py
@@ -13,6 +13,8 @@
 CONTRACT_LAST = (((1,), (1,)), ((), ()))
 CONTRACT_FIRST = (((0,), (0,)), ((), ()))
 VMEM_LIMIT = 28 * 1024 * 1024
+OWN_COST = 10**10
+PLANE_COST = 10**10
 
 
 def gelu_parts(value):
@@ -105,77 +107,109 @@
     return lax.dot_general(left, right, CONTRACT_LAST, preferred_element_type=jnp.float32)
 
 
+def dot_first(left, right):
+    return lax.dot_general(left, right, CONTRACT_FIRST, preferred_element_type=jnp.float32)
+
+
+def early_block(start, step, tok, cot, w_in, w_out, bias, two, act_ref, dpre_ref, mixed_ref, dpre):
+    @pl.loop(0, 2)
+    def _(sub):
+        spot = pl.ds(pl.multiple_of(start + sub * step, step), step)
+        value, slope = activate(tok[spot, :], w_in[...], bias[0:1, :])
+        act = value.astype(jnp.bfloat16)
+        act_ref[spot, :] = act[:, two:]
+        dact = dot_last(cot[spot, :], w_out[...])
+        terms = (dact * slope).astype(jnp.bfloat16)
+        dpre[spot, :] = terms[:, :two]
+        dpre_ref[spot, :] = terms[:, two:]
+        mixed_ref[spot, :] = jnp.dot(
+            act[:, :two], w_out[:two, :], preferred_element_type=jnp.float32
+        )
+
+
+def own_kernel(owned, *refs):
+    own_ref, other_ref, w_refs = refs[0], refs[1], refs[2:5]
+    act_ref, dpre_ref, mixed_ref, grad_ref, tok, cot, w_in, w_out, bias = refs[5:14]
+    dpre, tok_sem, cot_sem, w_sem = refs[14:]
+    core = lax.axis_index("core")
+    rows = own_ref.shape[1]
+    ins, outs = weight_copies(w_refs, owned, w_in, w_out, bias, w_sem)
+    load = side_by_side(core, (own_ref.at[0], other_ref.at[0]), tok, 0, tok_sem)
+    load += side_by_side(core, (own_ref.at[1], other_ref.at[1]), cot, 0, cot_sem)
+    run(ins + outs + load, "start")
+    run(ins + outs + load, "wait")
+    early_block(
+        0, rows // 2, tok, cot, w_in, w_out, bias, 2 * owned, act_ref, dpre_ref, mixed_ref, dpre
+    )
+    grad_ref[...] = dot_first(dpre[...], tok[...])
+
+
 def early_kernel(owned, *refs):
-    blocks = NEAR - 1
-    pair_refs, w_refs = refs[: 2 * blocks], refs[2 * blocks : 2 * blocks + 3]
-    act_ref, dpre_ref, mixed_ref, grad_ref, tok, cot = refs[2 * blocks + 3 : 2 * blocks + 9]
-    w_in, w_out, bias, dpre, tok_sem, cot_sem, w_sem = refs[2 * blocks + 9 :]
+    pair_refs, w_in, w_out, bias, grad_own_ref = refs[:4], refs[4], refs[5], refs[6], refs[7]
+    act_ref, dpre_ref, mixed_ref, grad_ref, tok, cot = refs[8:14]
+    dpre, tok_sem, cot_sem = refs[14:]
     core = lax.axis_index("core")
     rows = pair_refs[0].shape[1]
-    two = 2 * owned
-    ins, outs = weight_copies(w_refs, owned, w_in, w_out, bias, w_sem)
     loads = []
-    for block in range(blocks):
+    for block in range(2):
         first, second = pair_refs[2 * block], pair_refs[2 * block + 1]
         loads.append(
             side_by_side(core, (first.at[0], second.at[0]), tok, block * rows, tok_sem.at[block])
             + side_by_side(core, (first.at[1], second.at[1]), cot, block * rows, cot_sem.at[block])
         )
-    run(ins + outs, "start")
     for load in loads:
         run(load, "start")
-    run(ins + outs, "wait")
-    step = rows // 2
     for block, load in enumerate(loads):
         run(load, "wait")
+        early_block(
+            block * rows, rows // 2, tok, cot, w_in, w_out, bias, 2 * owned,
+            act_ref, dpre_ref, mixed_ref, dpre,
+        )
+    grad_ref[...] = grad_own_ref[...] + dot_first(dpre[...], tok[...])
+
+
+def output_kernel(owned, *refs):
+    groups = (refs[0:3], refs[3:6])
+    w_in, w_out, bias, w_three = refs[6:10]
+    mine_ref, other_ref, slope_ref, w_in_all, w_out_all, bias_all = refs[10:16]
+    w_last, sem = refs[16:]
+    core = lax.axis_index("core")
+    feats = mine_ref.shape[1]
+    two, three = 2 * owned, 3 * owned
+    first, last = pl.ds(0, three), pl.ds(three, owned)
+    copies = [
+        pltpu.make_async_copy(w_in, w_in_all.at[first], sem.at[0]),
+        pltpu.make_async_copy(w_three.at[pl.ds(0, owned)], w_in_all.at[last], sem.at[1]),
+        pltpu.make_async_copy(w_out, w_out_all.at[first], sem.at[2]),
+        pltpu.make_async_copy(w_three.at[pl.ds(owned, owned)], w_out_all.at[last], sem.at[3]),
+    ]
+    run(copies, "start")
+    bias_last = w_three[two : two + 16, :owned]
+    bias_all[:, :three] = bias[...]
+    bias_all[:, three:] = bias_last
+    w_last[:owned, :] = w_out[two:, :]
+    w_last[owned:, :] = w_three[owned:two, :]
+    start = 0
+    for act_two, tok, early_mixed in groups:
+        rows = tok.shape[0]
+        step = rows // 2
 
         @pl.loop(0, 2)
         def _(sub):
-            spot = pl.ds(pl.multiple_of(block * rows + sub * step, step), step)
-            value, slope = activate(tok[spot, :], w_in[...], bias[0:1, :])
-            act = value.astype(jnp.bfloat16)
-            act_ref[spot, :] = act[:, two:]
-            dact = dot_last(cot[spot, :], w_out[...])
-            terms = (dact * slope).astype(jnp.bfloat16)
-            dpre[spot, :] = terms[:, :two]
-            dpre_ref[spot, :] = terms[:, two:]
-            mixed_ref[spot, :] = jnp.dot(
-                act[:, :two], w_out[:two, :], preferred_element_type=jnp.float32
-            )
-
-    grad_ref[...] = dot_first(dpre[...], tok[...])
-
-
-def dot_first(left, right):
-    return lax.dot_general(left, right, CONTRACT_FIRST, preferred_element_type=jnp.float32)
-
-
-def output_kernel(owned, *refs):
-    early_act, tok, early_mixed, w_refs = refs[0], refs[1], refs[2], refs[3:7]
-    mine_ref, other_ref, slope_ref, w_in, w_out, bias = refs[7:13]
-    act, act_sem, w_sem = refs[13:]
-    core = lax.axis_index("core")
-    early_rows, feats = mine_ref.shape
-    two = 2 * owned
-    ins, outs = weight_copies(w_refs, owned, w_in, w_out, bias, w_sem)
-    moved = pltpu.make_async_copy(early_act, act.at[:, pl.ds(0, owned)], act_sem)
-    run(ins + outs + [moved], "start")
-    run(ins + outs + [moved], "wait")
-    rest = slice(3 * owned, 4 * owned)
-    step = early_rows // 3
-
-    @pl.loop(0, 3)
-    def _(block):
-        spot = pl.ds(pl.multiple_of(block * step, step), step)
-        value, slope = activate(tok[spot, :], w_in[rest, :], bias[0:1, rest])
-        act[spot, owned:] = value.astype(jnp.bfloat16)
-        slope_ref[spot, :] = slope
-        for shift, ref in enumerate((mine_ref, other_ref)):
-            half = half_columns(core, shift, feats)
-            ref[spot, :] = (
-                early_mixed[spot, half]
-                + jnp.dot(act[spot, :], w_out[two:, half], preferred_element_type=jnp.float32)
-            ).astype(jnp.bfloat16)
+            here = pl.ds(pl.multiple_of(sub * step, step), step)
+            spot = pl.ds(pl.multiple_of(start + sub * step, step), step)
+            value, slope = activate(tok[here, :], w_three[:owned, :], bias_last[0:1, :])
+            slope_ref[spot, :] = slope
+            act = jnp.concatenate([act_two[here, :], value.astype(jnp.bfloat16)], axis=1)
+            for shift, ref in enumerate((mine_ref, other_ref)):
+                half = half_columns(core, shift, feats)
+                ref[spot, :] = (
+                    early_mixed[here, half]
+                    + jnp.dot(act, w_last[:, half], preferred_element_type=jnp.float32)
+                ).astype(jnp.bfloat16)
+
+        start += rows
+    run(copies, "wait")
 
 
 def diagonal_kernel(*refs):
@@ -201,27 +235,25 @@
 
 
 def gradient_kernel(owned, *refs):
-    early_dpre, early_grad, tok, tok_diag, cot, slope, slope_diag, w_out = refs[:8]
-    diag_refs = refs[8:10]
-    own_ref, one_ref, two_ref, three_ref, cot_diag, dpre, dpre_diag, dpre_sem, cot_sem = refs[10:]
+    groups = (refs[0:3], refs[3:6])
+    early_grad, tok_diag, slope, slope_diag, w_out = refs[6:11]
+    diag_refs = refs[11:13]
+    own_ref, one_ref, two_ref, three_ref, cot_diag, dpre_diag, cot_sem = refs[13:]
     core = lax.axis_index("core")
-    rows = diag_refs[0].shape[0]
-    early_rows = early_dpre.shape[0]
     two = 2 * owned
     load = side_by_side(core, diag_refs, cot_diag, 0, cot_sem)
-    moved = pltpu.make_async_copy(early_dpre, dpre.at[:, pl.ds(0, owned)], dpre_sem)
-    run(load + [moved], "start")
-    rest = slice(3 * owned, 4 * owned)
-
-    @pl.loop(0, early_rows // rows)
-    def _(block):
-        spot = pl.ds(pl.multiple_of(block * rows, rows), rows)
-        dact = dot_last(cot[spot, :], w_out[rest, :])
-        dpre[spot, owned:] = (dact * slope[spot, :]).astype(jnp.bfloat16)
-
-    run(load + [moved], "wait")
+    run(load, "start")
+    start, grad = 0, None
+    for dpre_two, tok, cot in groups:
+        rows = tok.shape[0]
+        dact = dot_last(cot[...], w_out[3 * owned :, :])
+        last = (dact * slope[pl.ds(start, rows), :]).astype(jnp.bfloat16)
+        terms = dot_first(jnp.concatenate([dpre_two[...], last], axis=1), tok[...])
+        grad = terms if grad is None else grad + terms
+        start += rows
+    run(load, "wait")
     dpre_diag[...] = (dot_last(cot_diag[...], w_out[...]) * slope_diag[...]).astype(jnp.bfloat16)
-    grad = dot_first(dpre[...], tok[...]) + dot_first(dpre_diag[:, two:], tok_diag[...])
+    grad = grad + dot_first(dpre_diag[:, two:], tok_diag[...])
     two_ref[...] = grad[:owned].astype(jnp.bfloat16)
     three_ref[...] = grad[owned:].astype(jnp.bfloat16)
     grad = early_grad[...] + dot_first(dpre_diag[:, :two], tok_diag[...])
@@ -235,6 +267,14 @@
         ref[...] = (
             mine_ref[spot, :].astype(jnp.float32) + other_ref[spot, :].astype(jnp.float32)
         ).astype(jnp.bfloat16)
+
+
+def plane_kernel(own_ref, x_ref, y_ref, out_ref):
+    out_ref[...] = (
+        own_ref[...].astype(jnp.float32)
+        + x_ref[...].astype(jnp.float32)
+        + y_ref[...].astype(jnp.float32)
+    )
 
 
 def vmem(count):
@@ -305,37 +345,54 @@
     w_two, w_one = to_far(own_w, 2), to_far(own_w, 1)
     from_x, from_y = to_x(own), to_y(own)
     own_other = to_core(own)
+    w_three = to_far(w_two, 1)
+
+    def early_shapes(here):
+        return (
+            bf16(here, owned),
+            bf16(here, owned),
+            f32(here, width),
+            f32(2 * owned, width),
+            bf16(here, width),
+            bf16(here, width),
+        )
+
+    act_own, dpre_own, mixed_terms_own, grad_terms, tok_own, cot_own, w_in_three, w_out_three, bias = (
+        pl.pallas_call(
+            functools.partial(own_kernel, owned),
+            out_shape=early_shapes(rows)
+            + (bf16(3 * owned, width), bf16(3 * owned, width), bf16(16, 3 * owned)),
+            in_specs=anywhere(5),
+            out_specs=vmem(9),
+            scratch_shapes=[
+                pltpu.VMEM((rows, 2 * owned), jnp.bfloat16),
+                dma((2,)),
+                dma((2,)),
+                dma((3, 3)),
+            ],
+            compiler_params=params,
+            cost_estimate=cost(OWN_COST, rows),
+            name="own",
+        )(own, own_other, own_w, w_one, w_two)
+    )
+    from_x, from_y, grad_terms = barrier((from_x, from_y, grad_terms))
     tok_diag, cot_diag = to_y(from_x[0]), to_x(from_y[1])
-    from_x, from_y, own_other, w_one, w_two = barrier((from_x, from_y, own_other, w_one, w_two))
     x_other, y_other = to_core(from_x), to_core(from_y)
-    w_three = to_far(w_two, 1)
-    early_w = [own_w, w_one, w_two]
-    early_act, early_dpre, early_mixed, early_grad, tok, cot = pl.pallas_call(
+    act_near, dpre_near, mixed_terms_near, grad_terms, tok_near, cot_near = pl.pallas_call(
         functools.partial(early_kernel, owned),
-        out_shape=(
-            bf16(early_rows, owned),
-            bf16(early_rows, owned),
-            f32(early_rows, width),
-            f32(2 * owned, width),
-            bf16(early_rows, width),
-            bf16(early_rows, width),
-        ),
-        in_specs=anywhere(2 * (NEAR - 1) + 3),
+        out_shape=early_shapes(2 * rows),
+        in_specs=anywhere(4) + vmem(4),
         out_specs=vmem(6),
         scratch_shapes=[
-            pltpu.VMEM((3 * owned, width), jnp.bfloat16),
-            pltpu.VMEM((3 * owned, width), jnp.bfloat16),
-            pltpu.VMEM((16, 3 * owned), jnp.bfloat16),
-            pltpu.VMEM((early_rows, 2 * owned), jnp.bfloat16),
-            dma((NEAR - 1, 2)),
-            dma((NEAR - 1, 2)),
-            dma((3, 3)),
+            pltpu.VMEM((2 * rows, 2 * owned), jnp.bfloat16),
+            dma((2, 2)),
+            dma((2, 2)),
         ],
         compiler_params=params,
         cost_estimate=cost(early_rows * units, early_rows),
         name="early",
-    )(own, own_other, from_x, x_other, from_y, y_other, *early_w)
-    tok_diag, cot_diag, early_act = barrier((tok_diag, cot_diag, early_act))
+    )(from_x, x_other, from_y, y_other, w_in_three, w_out_three, bias, grad_terms)
+    tok_diag, cot_diag, act_near = barrier((tok_diag, cot_diag, act_near))
     tok_diag_other, cot_diag_other = to_core(tok_diag), to_core(cot_diag)
 
     mine, other, slope, w_in_all, w_out_all, bias = pl.pallas_call(
@@ -348,13 +405,16 @@
             bf16(units, width),
             bf16(16, units),
         ),
-        in_specs=vmem(3) + anywhere(4),
+        in_specs=vmem(10),
         out_specs=vmem(6),
-        scratch_shapes=[pltpu.VMEM((early_rows, 2 * owned), jnp.bfloat16), dma, dma((3, 4))],
+        scratch_shapes=[pltpu.VMEM((2 * owned, width), jnp.bfloat16), dma((4,))],
         compiler_params=params,
         cost_estimate=cost(8 * early_rows * units * width, 4 * count * width),
         name="output",
-    )(early_act, tok, early_mixed, *early_w, w_three)
+    )(
+        act_own, tok_own, mixed_terms_own, act_near, tok_near, mixed_terms_near,
+        w_in_three, w_out_three, bias, w_three,
+    )
     received = to_core(other)
 
     tok_diag_other, cot_diag_other, w_in_all = barrier((tok_diag_other, cot_diag_other, w_in_all))
@@ -380,26 +440,24 @@
         name="pair_sum",
     )(mine, received)
     mixed_x, mixed_y = to_x(sums[1]), to_y(sums[2])
-    early_grad, mixed_own = barrier((early_grad, sums[0]))
+    grad_terms, mixed_own = barrier((grad_terms, sums[0]))
 
     grad_own, grad_one, grad_two, grad_three = pl.pallas_call(
         functools.partial(gradient_kernel, owned),
         out_shape=[bf16(owned, width)] * 4,
-        in_specs=vmem(8) + anywhere(2),
+        in_specs=vmem(11) + anywhere(2),
         out_specs=vmem(4),
         scratch_shapes=[
             pltpu.VMEM((rows, width), jnp.bfloat16),
-            pltpu.VMEM((early_rows, 2 * owned), jnp.bfloat16),
             pltpu.VMEM((rows, units), jnp.bfloat16),
-            dma,
             dma((2,)),
         ],
         compiler_params=params,
         cost_estimate=cost(early_rows * units, early_rows),
         name="gradient",
     )(
-        early_dpre, early_grad, tok, tok_last, cot, slope, slope_diag, w_out_all,
-        cot_diag, cot_diag_other,
+        dpre_own, tok_own, cot_own, dpre_near, tok_near, cot_near,
+        grad_terms, tok_last, slope, slope_diag, w_out_all, cot_diag, cot_diag_other,
     )
     relayed = to_far(grad_three, 1)
     from_one = to_far(grad_one, 1)
@@ -414,7 +472,7 @@
         name="pair_sum_diagonal",
     )(mine_diag, received_diag)
     mixed_diag = to_diagonal(sum_diag)
-    grad_two, mixed_x, mixed_y, _ = barrier((grad_two, mixed_x, mixed_y, sum_diag))
+    grad_two, _ = barrier((grad_two, sum_diag))
     from_two = to_far(
         (grad_two.astype(jnp.float32) + relayed.astype(jnp.float32)).astype(jnp.bfloat16), 2
     )
@@ -423,12 +481,16 @@
         + from_one.astype(jnp.float32)
         + from_two.astype(jnp.float32)
     )
-    mixed = (
-        mixed_own.astype(jnp.float32)
-        + mixed_x.astype(jnp.float32)
-        + mixed_y.astype(jnp.float32)
-        + mixed_diag.astype(jnp.float32)
-    ).astype(jnp.bfloat16)
+    mixed = pl.pallas_call(
+        plane_kernel,
+        out_shape=f32(rows, feats),
+        in_specs=vmem(3),
+        out_specs=pl.BlockSpec(memory_space=pltpu.VMEM),
+        compiler_params=params,
+        cost_estimate=cost(PLANE_COST, rows),
+        name="plane_sum",
+    )(mixed_own, mixed_x, mixed_y)
+    mixed = (mixed + mixed_diag.astype(jnp.float32)).astype(jnp.bfloat16)
     return (mixed, total * scale)
 
 

time: 98.6 us -> 90.8 us (0.921)
  the two profiles are of different devices: /device:TPU:6 before, /device:TPU:0 now
where the time goes in v7:
time: 90.8 us; the launch traced here: 90.7 us
  waiting for transfers between devices  43.1 us (47%)
  starting transfers between devices  23.2 us (26%)
  Pallas kernels  19.3 us (21%)
  other arithmetic  4.31 us (5%)
    ppermute x20, waiting for transfers between devices, permute(): return lax.ppermute(value, AXES, pairs)  43.1 us
    ppermute x20, starting transfers between devices, permute(): return lax.ppermute(value, AXES, pairs)  23.2 us
    pallas_call x1, Pallas kernels, on_device_lines(): pl.pallas_call(functools.partial(early_kernel, owned), out_shape=early_sh...  5.15 us
    pallas_call x1, Pallas kernels, on_device_lines(): pl.pallas_call(functools.partial(output_kernel, owned), out_shape=(bf16(e...  4.32 us
    pallas_call x1, Pallas kernels, on_device_lines(): pl.pallas_call(functools.partial(gradient_kernel, owned), out_shape=[bf16...  4.14 us
    pallas_call x1, Pallas kernels, on_device_lines(): pl.pallas_call(functools.partial(own_kernel, owned), out_shape=early_shap...  2.8 us
    pallas_call x1, Pallas kernels, on_device_lines(): pl.pallas_call(diagonal_kernel, out_shape=(bf16(rows, feats), bf16(rows,...  2.27 us
  transfers between devices with their start and end apart: 20, of which 9 were waited for; matrix products, arithmetic and copies ran while one was open for 1% of the time, Pallas kernels for 21%

profile of v7, /device:TPU:0, one launch (start us, length us, event | category | flops | bytes accessed | tf_op | source)
XLA Modules:
  0.0 90.7 jit_solution(13698642160996242588)
XLA Ops:
  0.6 1.1 %fusion.1.refs_2_ = bf16[272,1024]{1,0:T(8,128)(2,1)S(1)} fusion(bf16[1,128]{1,0:T(2,128)(2,1)} %bitcast.9, bf16[128,1024]{1,0:T(8,128)(2,1)} %param.9, bf16[128,1024]{1,0:T(8,128)(2,1)} %param.7), kind=kLoop, calls=%fused_computation.4 | loop fusion | flops 2228224 | bytes 1081600 | tf_op jit(solution)/shard_map/concatenate | solution.py:342
  1.7 1.3 %pad_maximum_fusion.refs_0_ = bf16[2,512,512]{2,1,0:T(8,128)(2,1)S(1)} fusion(bf16[1,512,512]{2,1,0:T(8,128)(2,1)} %bitcast.7, bf16[1,512,512]{2,1,0:T(8,128)(2,1)} %bitcast.8), kind=kLoop, calls=%fused_computation.2 | loop fusion | flops 524288 | bytes 2097152 | tf_op jit(solution)/shard_map/stack | solution.py:344
  3.0 0.5 collective-permute-start.2
  3.5 3.7 %collective-permute-start.4 = (bf16[272,1024]{1,0:T(8,128)(2,1)S(1)}, bf16[272,1024]{1,0:T(8,128)(2,1)S(1)}, u32[]{:S(2)}, u32[]{:S(2)}) collective-permute-start(bf16[272,1024]{1,0:T(8,128)(2,1)S(1)} %fusion.1.refs_2_), channel_id=1, source_target_pairs={{0,16},{1,17},{2,18},{3,19},{4,20},{5,21},{6,22},{7,23},{8,24},{9,... | collective-permute-start | bytes 1671176 | tf_op jit(solution)/shard_map/ppermute | solution.py:301
  7.2 1.6 %collective-permute-start.3 = (bf16[272,1024]{1,0:T(8,128)(2,1)S(1)}, bf16[272,1024]{1,0:T(8,128)(2,1)S(1)}, u32[]{:S(2)}, u32[]{:S(2)}) collective-permute-start(bf16[272,1024]{1,0:T(8,128)(2,1)S(1)} %fusion.1.refs_2_), channel_id=1, source_target_pairs={{0,8},{1,9},{2,10},{3,11},{4,12},{5,13},{6,14},{7,15},{8,0},{9,1},... | collective-permute-start | bytes 1671176 | tf_op jit(solution)/shard_map/ppermute | solution.py:301
  8.8 1.5 %collective-permute-start.1 = (bf16[2,512,512]{2,1,0:T(8,128)(2,1)S(1)}, bf16[2,512,512]{2,1,0:T(8,128)(2,1)S(1)}, u32[]{:S(2)}, u32[]{:S(2)}) collective-permute-start(bf16[2,512,512]{2,1,0:T(8,128)(2,1)S(1)} %pad_maximum_fusion.refs_0_), channel_id=1, source_target_pairs={{0,4},{1,5},{2,6},{3,7},{4,0},{5,1},{6,2},{7,3},{8,12},{9,13},{10,... | collective-permute-start | bytes 3145736 | tf_op jit(solution)/shard_map/ppermute | solution.py:301
  10.3 1.5 %collective-permute-start = (bf16[2,512,512]{2,1,0:T(8,128)(2,1)S(1)}, bf16[2,512,512]{2,1,0:T(8,128)(2,1)S(1)}, u32[]{:S(2)}, u32[]{:S(2)}) collective-permute-start(bf16[2,512,512]{2,1,0:T(8,128)(2,1)S(1)} %pad_maximum_fusion.refs_0_), channel_id=1, source_target_pairs={{0,2},{1,3},{2,0},{3,1},{4,6},{5,7},{6,4},{7,5},{8,10},{9,11},{10,... | collective-permute-start | bytes 3145736 | tf_op jit(solution)/shard_map/ppermute | solution.py:301
  11.8 20.7 %collective-permute-done.4.refs_4_ = bf16[272,1024]{1,0:T(8,128)(2,1)S(1)} collective-permute-done((bf16[272,1024]{1,0:T(8,128)(2,1)S(1)}, bf16[272,1024]{1,0:T(8,128)(2,1)S(1)}, u32[]{:S(2)}, u32[]{:S(2)}) %collective-permute-start.4) | collective-permute-done | bytes 557088 | tf_op jit(solution)/shard_map/ppermute | solution.py:301
  32.7 2.8 %own.1 = (bf16[512,128]{1,0:T(8,128)(2,1)S(1)}, bf16[512,128]{1,0:T(8,128)(2,1)S(1)}, f32[512,1024]{1,0:T(8,128)S(1)}, f32[256,1024]{1,0:T(8,128)S(1)}, bf16[512...) custom-call(bf16[2,512,512]{2,1,0:T(8,128)(2,1)S(1)} %pad_maximum_fu, ...), custom_call_target="tpu_custom_call" | custom-call | flops 10000000000 | bytes 512 | tf_op jit(solution)/shard_map/own/pallas_call | solution.py:361
  36.1 1.5 %collective-permute-start.9 = (bf16[272,1024]{1,0:T(8,128)(2,1)S(1)}, bf16[272,1024]{1,0:T(8,128)(2,1)S(1)}, u32[]{:S(2)}, u32[]{:S(2)}) collective-permute-start(bf16[272,1024]{1,0:T(8,128)(2,1)S(1)} %collective-permute-done.4.refs_4_), channel_id=1, source_target_pairs={{0,8},{1,9},{2,10},{3,11},{4,12},{5,13},{6,14},{7,15},{8,0},{9,1},... | collective-permute-start | bytes 1671176 | tf_op jit(solution)/shard_map/ppermute | solution.py:301
  37.6 1.6 %collective-permute-start.8 = (bf16[512,512]{1,0:T(8,128)(2,1)S(1)}, bf16[512,512]{1,0:T(8,128)(2,1)S(1)}, u32[]{:S(2)}, u32[]{:S(2)}) collective-permute-start(bf16[512,512]{1,0:T(8,128)(2,1)S(1)} %slice_bitcast_fusion), channel_id=1, source_target_pairs={{0,2},{1,3},{2,0},{3,1},{4,6},{5,7},{6,4},{7,5},{8,10},{9,11},{10,... | collective-permute-start | bytes 1572872 | tf_op jit(solution)/shard_map/ppermute | solution.py:301
  39.2 1.5 %collective-permute-start.7 = (bf16[512,512]{1,0:T(8,128)(2,1)S(1)}, bf16[512,512]{1,0:T(8,128)(2,1)S(1)}, u32[]{:S(2)}, u32[]{:S(2)}) collective-permute-start(bf16[512,512]{1,0:T(8,128)(2,1)S(1)} %slice_bitcast_fusion.1), channel_id=1, source_target_pairs={{0,4},{1,5},{2,6},{3,7},{4,0},{5,1},{6,2},{7,3},{8,12},{9,13},{10,... | collective-permute-start | bytes 1572872 | tf_op jit(solution)/shard_map/ppermute | solution.py:301
  40.7 5.2 %early.1 = (bf16[1024,128]{1,0:T(8,128)(2,1)S(1)}, bf16[1024,128]{1,0:T(8,128)(2,1)S(1)}, f32[1024,1024]{1,0:T(8,128)S(1)}, f32[256,1024]{1,0:T(8,128)S(1)}, bf1...) custom-call(bf16[2,512,512]{2,1,0:T(8,128)(2,1)S(1)} %collective-permute-done.refs_0_, ...), custom_call_target="tpu_custom_call" | custom-call | flops 786432 | bytes 1536 | tf_op jit(solution)/shard_map/early/pallas_call | solution.py:381
  45.9 5.4 %collective-permute-done.8.refs_11_ = bf16[512,512]{1,0:T(8,128)(2,1)S(1)} collective-permute-done((bf16[512,512]{1,0:T(8,128)(2,1)S(1)}, bf16[512,512]{1,0:T(8,128)(2,1)S(1)}, u32[]{:S(2)}, u32[]{:S(2)}) %collective-permute-start.8) | collective-permute-done | bytes 524320 | tf_op jit(solution)/shard_map/ppermute | solution.py:301
  51.3 1.2 %collective-permute-done.7.refs_3_ = bf16[512,512]{1,0:T(8,128)(2,1)S(1)} collective-permute-done((bf16[512,512]{1,0:T(8,128)(2,1)S(1)}, bf16[512,512]{1,0:T(8,128)(2,1)S(1)}, u32[]{:S(2)}, u32[]{:S(2)}) %collective-permute-start.7) | collective-permute-done | bytes 524320 | tf_op jit(solution)/shard_map/ppermute | solution.py:301
  53.1 4.3 %output.1 = (bf16[1536,512]{1,0:T(8,128)(2,1)S(1)}, bf16[1536,512]{1,0:T(8,128)(2,1)S(1)}, f32[1536,128]{1,0:T(8,128)S(1)}, bf16[512,1024]{1,0:T(8,128)(2,1)S(1)...) custom-call(bf16[512,128]{1,0:T(8,128)(2,1)S(1)} %get-tuple-element.64.refs_0_, ...), custom_call_target="tpu_custom_call" | custom-call | flops 6442450944 | bytes 8388608 | tf_op jit(solution)/shard_map/output/pallas_call | solution.py:398
  57.5 2.3 %diagonal.1 = (bf16[512,512]{1,0:T(8,128)(2,1)S(1)}, bf16[512,512]{1,0:T(8,128)(2,1)S(1)}, f32[512,512]{1,0:T(8,128)S(1)}, bf16[512,1024]{1,0:T(8,128)(2,1)S(1)}) custom-call(bf16[512,1024]{1,0:T(8,128)(2,1)S(1)} %get-tuple-element.75.refs_0_, bf16[512,1024]{1,0:T(8,128)(2,1)S(1)} %get-tuple-element.76.refs_1_.refs_10_, ...), custom_call_target="tpu_custom_call" | custom-call | flops 12884901888 | bytes 2097152 | tf_op jit(solution)/shard_map/diagonal/pallas_call | solution.py:421
  59.8 0.6 collective-permute-start.15
  60.3 0.6 collective-permute-done.12.other_ref
  61.2 0.6 collective-permute-start.13
  61.8 1.5 %collective-permute-start.14 = (bf16[512,512]{1,0:T(8,128)(2,1)S(1)}, bf16[512,512]{1,0:T(8,128)(2,1)S(1)}, u32[]{:S(2)}, u32[]{:S(2)}) collective-permute-start(bf16[512,512]{1,0:T(8,128)(2,1)S(1)} %get-tuple-element.85), channel_id=1, source_target_pairs={{0,4},{1,5},{2,6},{3,7},{4,0},{5,1},{6,2},{7,3},{8,12},{9,13},{10,... | collective-permute-start | bytes 1572872 | tf_op jit(solution)/shard_map/ppermute | solution.py:301
  63.4 4.1 %gradient.1 = (bf16[128,1024]{1,0:T(8,128)(2,1)S(1)}, bf16[128,1024]{1,0:T(8,128)(2,1)S(1)}, bf16[128,1024]{1,0:T(8,128)(2,1)S(1)}, bf16[128,1024]{1,0:T(8,128)(2,1)S(1)}) custom-call(bf16[512,128]{1,0:T(8,128)(2,1)S(1)} %get-tuple-element.87.refs_0_, bf16[512,1024]{1,0:T(8,128)(2,1)S(1)} %get-tuple-element.65.refs_1_, ...), custom_call_target="tpu_custom_call" | custom-call | flops 786432 | bytes 1536 | tf_op jit(solution)/shard_map/gradient/pallas_call | solution.py:445
  67.5 0.6 collective-permute-start.18
  68.3 1.5 %collective-permute-start.16 = (bf16[512,512]{1,0:T(8,128)(2,1)S(1)}, bf16[512,512]{1,0:T(8,128)(2,1)S(1)}, u32[]{:S(2)}, u32[]{:S(2)}) collective-permute-start(bf16[512,512]{1,0:T(8,128)(2,1)S(1)} %pair_sum_diagonal.1), channel_id=1, source_target_pairs={{0,6},{1,7},{2,4},{3,5},{4,2},{5,3},{6,0},{7,1},{8,14},{9,15},{10,... | collective-permute-start | bytes 1572872 | tf_op jit(solution)/shard_map/ppermute | solution.py:301
  69.8 1.4 %collective-permute-start.17 = (bf16[128,1024]{1,0:T(8,128)(2,1)S(1)}, bf16[128,1024]{1,0:T(8,128)(2,1)S(1)}, u32[]{:S(2)}, u32[]{:S(2)}) collective-permute-start(bf16[128,1024]{1,0:T(8,128)(2,1)S(1)} %get-tuple-element.100), channel_id=1, source_target_pairs={{0,8},{1,9},{2,10},{3,11},{4,12},{5,13},{6,14},{7,15},{8,0},{9,1},... | collective-permute-start | bytes 786440 | tf_op jit(solution)/shard_map/ppermute | solution.py:301
  71.2 5.6 %collective-permute-done.18 = bf16[128,1024]{1,0:T(8,128)(2,1)S(1)} collective-permute-done((bf16[128,1024]{1,0:T(8,128)(2,1)S(1)}, bf16[128,1024]{1,0:T(8,128)(2,1)S(1)}, u32[]{:S(2)}, u32[]{:S(2)}) %collective-permute-start.18) | collective-permute-done | bytes 262176 | tf_op jit(solution)/shard_map/ppermute | solution.py:301
  76.9 2.4 %collective-permute-start.19 = (bf16[128,1024]{1,0:T(8,128)(2,1)S(1)}, bf16[128,1024]{1,0:T(8,128)(2,1)S(1)}, u32[]{:S(2)}, u32[]{:S(2)}) collective-permute-start(bf16[128,1024]{1,0:T(8,128)(2,1)S(1)} %add_convert_fusion.1), channel_id=1, source_target_pairs={{0,16},{1,17},{2,18},{3,19},{4,20},{5,21},{6,22},{7,23},{8,24},{9,... | collective-permute-start | bytes 786440 | tf_op jit(solution)/shard_map/ppermute | solution.py:301
  79.3 6.6 %collective-permute-done.14.y_ref = bf16[512,512]{1,0:T(8,128)(2,1)S(1)} collective-permute-done((bf16[512,512]{1,0:T(8,128)(2,1)S(1)}, bf16[512,512]{1,0:T(8,128)(2,1)S(1)}, u32[]{:S(2)}, u32[]{:S(2)}) %collective-permute-start.14) | collective-permute-done | bytes 524320 | tf_op jit(solution)/shard_map/ppermute | solution.py:301
  86.0 1.5 %collective-permute-done.16 = bf16[512,512]{1,0:T(8,128)(2,1)S(1)} collective-permute-done((bf16[512,512]{1,0:T(8,128)(2,1)S(1)}, bf16[512,512]{1,0:T(8,128)(2,1)S(1)}, u32[]{:S(2)}, u32[]{:S(2)}) %collective-permute-start.16) | collective-permute-done | bytes 524320 | tf_op jit(solution)/shard_map/ppermute | solution.py:301
  87.5 1.0 %add_convert_fusion = bf16[512,512]{1,0:T(8,128)(2,1)} fusion(f32[512,512]{1,0:T(8,128)S(1)} %plane_sum.1, bf16[512,512]{1,0:T(8,128)(2,1)S(1)} %collective-permute-done.16), kind=kLoop, calls=%fused_computation.3 | loop fusion | flops 786432 | bytes 2097152 | tf_op jit(solution)/shard_map/convert_element_type | solution.py:493
  88.4 1.4 %collective-permute-done.19 = bf16[128,1024]{1,0:T(8,128)(2,1)S(1)} collective-permute-done((bf16[128,1024]{1,0:T(8,128)(2,1)S(1)}, bf16[128,1024]{1,0:T(8,128)(2,1)S(1)}, u32[]{:S(2)}, u32[]{:S(2)}) %collective-permute-start.19) | collective-permute-done | bytes 262176 | tf_op jit(solution)/shard_map/ppermute | solution.py:301
  89.8 0.9 %add_multiply_fusion = f32[128,1024]{1,0:T(8,128)} fusion(bf16[128,1024]{1,0:T(8,128)(2,1)S(1)} %collective-permute-done.19, bf16[128,1024]{1,0:T(8,128)(2,1)S(1)} %collective-permute-done.17, bf16[128,1024]{1,0:T(8,128)(2,1)S(1)} %get-tuple-element.99), kind=kLoop, calls=%fused_computation.5 | loop fusion | flops 786432 | bytes 1310720 | tf_op jit(solution)/shard_map/mul | solution.py:494
  (23 shorter events, 2.2 us)
Async XLA Ops:
  3.0 29.6 %collective-permute-start.2 = (bf16[2,512,512]{2,1,0:T(8,128)(2,1)S(1)}, bf16[2,512,512]{2,1,0:T(8,128)(2,1)S(1)}, u32[]{:S(2)}, u32[]{:S(2)}) collective-permute-start(bf16[2,512,512]{2,1,0:T(8,128)(2,1)S(1)} %pad_maximum_fusion.refs_0_), channel_id=1, source_target_pairs={{0,1},{1,0},{2,3},{3,2},{4,5},{5,4},{6,7},{7,6},{8,9},{9,8},{10,11... | collective-permute-start | bytes 3145736 | tf_op jit(solution)/shard_map/ppermute | solution.py:301
  3.5 28.9 %collective-permute-start.4 = (bf16[272,1024]{1,0:T(8,128)(2,1)S(1)}, bf16[272,1024]{1,0:T(8,128)(2,1)S(1)}, u32[]{:S(2)}, u32[]{:S(2)}) collective-permute-start(bf16[272,1024]{1,0:T(8,128)(2,1)S(1)} %fusion.1.refs_2_), channel_id=1, source_target_pairs={{0,16},{1,17},{2,18},{3,19},{4,20},{5,21},{6,22},{7,23},{8,24},{9,... | collective-permute-start | bytes 1671176 | tf_op jit(solution)/shard_map/ppermute | solution.py:301
  7.2 25.5 %collective-permute-start.3 = (bf16[272,1024]{1,0:T(8,128)(2,1)S(1)}, bf16[272,1024]{1,0:T(8,128)(2,1)S(1)}, u32[]{:S(2)}, u32[]{:S(2)}) collective-permute-start(bf16[272,1024]{1,0:T(8,128)(2,1)S(1)} %fusion.1.refs_2_), channel_id=1, source_target_pairs={{0,8},{1,9},{2,10},{3,11},{4,12},{5,13},{6,14},{7,15},{8,0},{9,1},... | collective-permute-start | bytes 1671176 | tf_op jit(solution)/shard_map/ppermute | solution.py:301
  8.8 26.7 %collective-permute-start.1 = (bf16[2,512,512]{2,1,0:T(8,128)(2,1)S(1)}, bf16[2,512,512]{2,1,0:T(8,128)(2,1)S(1)}, u32[]{:S(2)}, u32[]{:S(2)}) collective-permute-start(bf16[2,512,512]{2,1,0:T(8,128)(2,1)S(1)} %pad_maximum_fusion.refs_0_), channel_id=1, source_target_pairs={{0,4},{1,5},{2,6},{3,7},{4,0},{5,1},{6,2},{7,3},{8,12},{9,13},{10,... | collective-permute-start | bytes 3145736 | tf_op jit(solution)/shard_map/ppermute | solution.py:301
  10.3 25.2 %collective-permute-start = (bf16[2,512,512]{2,1,0:T(8,128)(2,1)S(1)}, bf16[2,512,512]{2,1,0:T(8,128)(2,1)S(1)}, u32[]{:S(2)}, u32[]{:S(2)}) collective-permute-start(bf16[2,512,512]{2,1,0:T(8,128)(2,1)S(1)} %pad_maximum_fusion.refs_0_), channel_id=1, source_target_pairs={{0,2},{1,3},{2,0},{3,1},{4,6},{5,7},{6,4},{7,5},{8,10},{9,11},{10,... | collective-permute-start | bytes 3145736 | tf_op jit(solution)/shard_map/ppermute | solution.py:301
  35.5 5.2 %collective-permute-start.5 = (bf16[2,512,512]{2,1,0:T(8,128)(2,1)S(1)}, bf16[2,512,512]{2,1,0:T(8,128)(2,1)S(1)}, u32[]{:S(2)}, u32[]{:S(2)}) collective-permute-start(bf16[2,512,512]{2,1,0:T(8,128)(2,1)S(1)} %collective-permute-done.refs_0_), channel_id=1, source_target_pairs={{0,1},{1,0},{2,3},{3,2},{4,5},{5,4},{6,7},{7,6},{8,9},{9,8},{10,11... | collective-permute-start | bytes 3145736 | tf_op jit(solution)/shard_map/ppermute | solution.py:301
  35.6 5.2 %collective-permute-start.6 = (bf16[2,512,512]{2,1,0:T(8,128)(2,1)S(1)}, bf16[2,512,512]{2,1,0:T(8,128)(2,1)S(1)}, u32[]{:S(2)}, u32[]{:S(2)}) collective-permute-start(bf16[2,512,512]{2,1,0:T(8,128)(2,1)S(1)} %collective-permute-done.1.refs_2_), channel_id=1, source_target_pairs={{0,1},{1,0},{2,3},{3,2},{4,5},{5,4},{6,7},{7,6},{8,9},{9,8},{10,11... | collective-permute-start | bytes 3145736 | tf_op jit(solution)/shard_map/ppermute | solution.py:301
  36.1 17.0 %collective-permute-start.9 = (bf16[272,1024]{1,0:T(8,128)(2,1)S(1)}, bf16[272,1024]{1,0:T(8,128)(2,1)S(1)}, u32[]{:S(2)}, u32[]{:S(2)}) collective-permute-start(bf16[272,1024]{1,0:T(8,128)(2,1)S(1)} %collective-permute-done.4.refs_4_), channel_id=1, source_target_pairs={{0,8},{1,9},{2,10},{3,11},{4,12},{5,13},{6,14},{7,15},{8,0},{9,1},... | collective-permute-start | bytes 1671176 | tf_op jit(solution)/shard_map/ppermute | solution.py:301
  37.6 13.7 %collective-permute-start.8 = (bf16[512,512]{1,0:T(8,128)(2,1)S(1)}, bf16[512,512]{1,0:T(8,128)(2,1)S(1)}, u32[]{:S(2)}, u32[]{:S(2)}) collective-permute-start(bf16[512,512]{1,0:T(8,128)(2,1)S(1)} %slice_bitcast_fusion), channel_id=1, source_target_pairs={{0,2},{1,3},{2,0},{3,1},{4,6},{5,7},{6,4},{7,5},{8,10},{9,11},{10,... | collective-permute-start | bytes 1572872 | tf_op jit(solution)/shard_map/ppermute | solution.py:301
  39.2 13.3 %collective-permute-start.7 = (bf16[512,512]{1,0:T(8,128)(2,1)S(1)}, bf16[512,512]{1,0:T(8,128)(2,1)S(1)}, u32[]{:S(2)}, u32[]{:S(2)}) collective-permute-start(bf16[512,512]{1,0:T(8,128)(2,1)S(1)} %slice_bitcast_fusion.1), channel_id=1, source_target_pairs={{0,4},{1,5},{2,6},{3,7},{4,0},{5,1},{6,2},{7,3},{8,12},{9,13},{10,... | collective-permute-start | bytes 1572872 | tf_op jit(solution)/shard_map/ppermute | solution.py:301
  52.6 4.9 %collective-permute-start.10 = (bf16[512,512]{1,0:T(8,128)(2,1)S(1)}, bf16[512,512]{1,0:T(8,128)(2,1)S(1)}, u32[]{:S(2)}, u32[]{:S(2)}) collective-permute-start(bf16[512,512]{1,0:T(8,128)(2,1)S(1)} %collective-permute-done.7.refs_3_), channel_id=1, source_target_pairs={{0,1},{1,0},{2,3},{3,2},{4,5},{5,4},{6,7},{7,6},{8,9},{9,8},{10,11... | collective-permute-start | bytes 1572872 | tf_op jit(solution)/shard_map/ppermute | solution.py:301
  52.6 4.9 %collective-permute-start.11 = (bf16[512,512]{1,0:T(8,128)(2,1)S(1)}, bf16[512,512]{1,0:T(8,128)(2,1)S(1)}, u32[]{:S(2)}, u32[]{:S(2)}) collective-permute-start(bf16[512,512]{1,0:T(8,128)(2,1)S(1)} %collective-permute-done.8.refs_11_), channel_id=1, source_target_pairs={{0,1},{1,0},{2,3},{3,2},{4,5},{5,4},{6,7},{7,6},{8,9},{9,8},{10,11... | collective-permute-start | bytes 1572872 | tf_op jit(solution)/shard_map/ppermute | solution.py:301
  57.4 3.5 %collective-permute-start.12 = (bf16[1536,512]{1,0:T(8,128)(2,1)S(1)}, bf16[1536,512]{1,0:T(8,128)(2,1)S(1)}, u32[]{:S(2)}, u32[]{:S(2)}) collective-permute-start(bf16[1536,512]{1,0:T(8,128)(2,1)S(1)} %get-tuple-element.81), channel_id=1, source_target_pairs={{0,1},{1,0},{2,3},{3,2},{4,5},{5,4},{6,7},{7,6},{8,9},{9,8},{10,11... | collective-permute-start | bytes 4718600 | tf_op jit(solution)/shard_map/ppermute | solution.py:301
  59.8 8.4 %collective-permute-start.15 = (bf16[512,512]{1,0:T(8,128)(2,1)S(1)}, bf16[512,512]{1,0:T(8,128)(2,1)S(1)}, u32[]{:S(2)}, u32[]{:S(2)}) collective-permute-start(bf16[512,512]{1,0:T(8,128)(2,1)S(1)} %get-tuple-element.98), channel_id=1, source_target_pairs={{0,1},{1,0},{2,3},{3,2},{4,5},{5,4},{6,7},{7,6},{8,9},{9,8},{10,11... | collective-permute-start | bytes 1572872 | tf_op jit(solution)/shard_map/ppermute | solution.py:301
  61.2 18.0 %collective-permute-start.13 = (bf16[512,512]{1,0:T(8,128)(2,1)S(1)}, bf16[512,512]{1,0:T(8,128)(2,1)S(1)}, u32[]{:S(2)}, u32[]{:S(2)}) collective-permute-start(bf16[512,512]{1,0:T(8,128)(2,1)S(1)} %get-tuple-element.84), channel_id=1, source_target_pairs={{0,2},{1,3},{2,0},{3,1},{4,6},{5,7},{6,4},{7,5},{8,10},{9,11},{10,... | collective-permute-start | bytes 1572872 | tf_op jit(solution)/shard_map/ppermute | solution.py:301
  61.8 24.0 %collective-permute-start.14 = (bf16[512,512]{1,0:T(8,128)(2,1)S(1)}, bf16[512,512]{1,0:T(8,128)(2,1)S(1)}, u32[]{:S(2)}, u32[]{:S(2)}) collective-permute-start(bf16[512,512]{1,0:T(8,128)(2,1)S(1)} %get-tuple-element.85), channel_id=1, source_target_pairs={{0,4},{1,5},{2,6},{3,7},{4,0},{5,1},{6,2},{7,3},{8,12},{9,13},{10,... | collective-permute-start | bytes 1572872 | tf_op jit(solution)/shard_map/ppermute | solution.py:301
  67.5 9.3 %collective-permute-start.18 = (bf16[128,1024]{1,0:T(8,128)(2,1)S(1)}, bf16[128,1024]{1,0:T(8,128)(2,1)S(1)}, u32[]{:S(2)}, u32[]{:S(2)}) collective-permute-start(bf16[128,1024]{1,0:T(8,128)(2,1)S(1)} %get-tuple-element.103), channel_id=1, source_target_pairs={{0,8},{1,9},{2,10},{3,11},{4,12},{5,13},{6,14},{7,15},{8,0},{9,1},... | collective-permute-start | bytes 786440 | tf_op jit(solution)/shard_map/ppermute | solution.py:301
  68.3 19.2 %collective-permute-start.16 = (bf16[512,512]{1,0:T(8,128)(2,1)S(1)}, bf16[512,512]{1,0:T(8,128)(2,1)S(1)}, u32[]{:S(2)}, u32[]{:S(2)}) collective-permute-start(bf16[512,512]{1,0:T(8,128)(2,1)S(1)} %pair_sum_diagonal.1), channel_id=1, source_target_pairs={{0,6},{1,7},{2,4},{3,5},{4,2},{5,3},{6,0},{7,1},{8,14},{9,15},{10,... | collective-permute-start | bytes 1572872 | tf_op jit(solution)/shard_map/ppermute | solution.py:301
  69.8 18.6 %collective-permute-start.17 = (bf16[128,1024]{1,0:T(8,128)(2,1)S(1)}, bf16[128,1024]{1,0:T(8,128)(2,1)S(1)}, u32[]{:S(2)}, u32[]{:S(2)}) collective-permute-start(bf16[128,1024]{1,0:T(8,128)(2,1)S(1)} %get-tuple-element.100), channel_id=1, source_target_pairs={{0,8},{1,9},{2,10},{3,11},{4,12},{5,13},{6,14},{7,15},{8,0},{9,1},... | collective-permute-start | bytes 786440 | tf_op jit(solution)/shard_map/ppermute | solution.py:301
  76.9 12.9 %collective-permute-start.19 = (bf16[128,1024]{1,0:T(8,128)(2,1)S(1)}, bf16[128,1024]{1,0:T(8,128)(2,1)S(1)}, u32[]{:S(2)}, u32[]{:S(2)}) collective-permute-start(bf16[128,1024]{1,0:T(8,128)(2,1)S(1)} %add_convert_fusion.1), channel_id=1, source_target_pairs={{0,16},{1,17},{2,18},{3,19},{4,20},{5,21},{6,22},{7,23},{8,24},{9,... | collective-permute-start | bytes 786440 | tf_op jit(solution)/shard_map/ppermute | solution.py:301

commit v8 on v7

--- a/solution.py
+++ b/solution.py
@@ -13,8 +13,8 @@
 CONTRACT_LAST = (((1,), (1,)), ((), ()))
 CONTRACT_FIRST = (((0,), (0,)), ((), ()))
 VMEM_LIMIT = 28 * 1024 * 1024
-OWN_COST = 10**10
 PLANE_COST = 10**10
+EXTRA = 48
 
 
 def gelu_parts(value):
@@ -127,52 +127,37 @@
         )
 
 
-def own_kernel(owned, *refs):
-    own_ref, other_ref, w_refs = refs[0], refs[1], refs[2:5]
-    act_ref, dpre_ref, mixed_ref, grad_ref, tok, cot, w_in, w_out, bias = refs[5:14]
-    dpre, tok_sem, cot_sem, w_sem = refs[14:]
-    core = lax.axis_index("core")
-    rows = own_ref.shape[1]
-    ins, outs = weight_copies(w_refs, owned, w_in, w_out, bias, w_sem)
-    load = side_by_side(core, (own_ref.at[0], other_ref.at[0]), tok, 0, tok_sem)
-    load += side_by_side(core, (own_ref.at[1], other_ref.at[1]), cot, 0, cot_sem)
-    run(ins + outs + load, "start")
-    run(ins + outs + load, "wait")
-    early_block(
-        0, rows // 2, tok, cot, w_in, w_out, bias, 2 * owned, act_ref, dpre_ref, mixed_ref, dpre
-    )
-    grad_ref[...] = dot_first(dpre[...], tok[...])
-
-
 def early_kernel(owned, *refs):
-    pair_refs, w_in, w_out, bias, grad_own_ref = refs[:4], refs[4], refs[5], refs[6], refs[7]
-    act_ref, dpre_ref, mixed_ref, grad_ref, tok, cot = refs[8:14]
-    dpre, tok_sem, cot_sem = refs[14:]
+    pair_refs, w_refs = refs[:6], refs[6:9]
+    act_ref, dpre_ref, mixed_ref, grad_ref, tok, cot, w_in, w_out, bias = refs[9:18]
+    dpre, tok_sem, cot_sem, w_sem = refs[18:]
     core = lax.axis_index("core")
     rows = pair_refs[0].shape[1]
+    ins, outs = weight_copies(w_refs, owned, w_in, w_out, bias, w_sem)
     loads = []
-    for block in range(2):
+    for block in range(NEAR - 1):
         first, second = pair_refs[2 * block], pair_refs[2 * block + 1]
         loads.append(
             side_by_side(core, (first.at[0], second.at[0]), tok, block * rows, tok_sem.at[block])
             + side_by_side(core, (first.at[1], second.at[1]), cot, block * rows, cot_sem.at[block])
         )
+    run(ins + outs, "start")
     for load in loads:
         run(load, "start")
+    run(ins + outs, "wait")
     for block, load in enumerate(loads):
         run(load, "wait")
         early_block(
             block * rows, rows // 2, tok, cot, w_in, w_out, bias, 2 * owned,
             act_ref, dpre_ref, mixed_ref, dpre,
         )
-    grad_ref[...] = grad_own_ref[...] + dot_first(dpre[...], tok[...])
+    grad_ref[...] = dot_first(dpre[...], tok[...])
 
 
 def output_kernel(owned, *refs):
-    groups = (refs[0:3], refs[3:6])
-    w_in, w_out, bias, w_three = refs[6:10]
-    mine_ref, other_ref, slope_ref, w_in_all, w_out_all, bias_all = refs[10:16]
-    w_last, sem = refs[16:]
+    act_two, tok, early_mixed, w_in, w_out, bias, w_three = refs[:7]
+    mine_ref, other_ref, slope_ref, w_in_all, w_out_all, bias_all = refs[7:13]
+    w_last, sem = refs[13:]
     core = lax.axis_index("core")
     feats = mine_ref.shape[1]
     two, three = 2 * owned, 3 * owned
@@ -189,34 +174,30 @@
     bias_all[:, three:] = bias_last
     w_last[:owned, :] = w_out[two:, :]
     w_last[owned:, :] = w_three[owned:two, :]
-    start = 0
-    for act_two, tok, early_mixed in groups:
-        rows = tok.shape[0]
-        step = rows // 2
-
-        @pl.loop(0, 2)
-        def _(sub):
-            here = pl.ds(pl.multiple_of(sub * step, step), step)
-            spot = pl.ds(pl.multiple_of(start + sub * step, step), step)
-            value, slope = activate(tok[here, :], w_three[:owned, :], bias_last[0:1, :])
-            slope_ref[spot, :] = slope
-            act = jnp.concatenate([act_two[here, :], value.astype(jnp.bfloat16)], axis=1)
-            for shift, ref in enumerate((mine_ref, other_ref)):
-                half = half_columns(core, shift, feats)
-                ref[spot, :] = (
-                    early_mixed[here, half]
-                    + jnp.dot(act, w_last[:, half], preferred_element_type=jnp.float32)
-                ).astype(jnp.bfloat16)
-
-        start += rows
+    step = tok.shape[0] // 6
+
+    @pl.loop(0, 6)
+    def _(sub):
+        spot = pl.ds(pl.multiple_of(sub * step, step), step)
+        value, slope = activate(tok[spot, :], w_three[:owned, :], bias_last[0:1, :])
+        slope_ref[spot, :] = slope
+        act = jnp.concatenate([act_two[spot, :], value.astype(jnp.bfloat16)], axis=1)
+        for shift, ref in enumerate((mine_ref, other_ref)):
+            half = half_columns(core, shift, feats)
+            ref[spot, :] = (
+                early_mixed[spot, half]
+                + jnp.dot(act, w_last[:, half], preferred_element_type=jnp.float32)
+            ).astype(jnp.bfloat16)
+
     run(copies, "wait")
 
 
 def diagonal_kernel(*refs):
-    w_in, w_out, bias, diag_refs = refs[0], refs[1], refs[2], refs[3:5]
+    w_in, w_out, bias = refs[:3]
     mine_ref, other_ref, slope_ref, tok_diag, tok_sem = refs[5:]
     core = lax.axis_index("core")
-    rows, feats = diag_refs[0].shape
+    rows, feats = mine_ref.shape
+    diag_refs = [ref.at[pl.ds(0, rows)] for ref in refs[3:5]]
     load = side_by_side(core, diag_refs, tok_diag, 0, tok_sem)
     run(load, "start")
     run(load, "wait")
@@ -235,22 +216,16 @@
 
 
 def gradient_kernel(owned, *refs):
-    groups = (refs[0:3], refs[3:6])
-    early_grad, tok_diag, slope, slope_diag, w_out = refs[6:11]
-    diag_refs = refs[11:13]
-    own_ref, one_ref, two_ref, three_ref, cot_diag, dpre_diag, cot_sem = refs[13:]
+    dpre_two, tok, cot, early_grad, tok_diag, slope, slope_diag, w_out = refs[:8]
+    own_ref, one_ref, two_ref, three_ref, cot_diag, dpre_diag, cot_sem = refs[10:]
+    diag_refs = [ref.at[pl.ds(EXTRA, cot_diag.shape[0])] for ref in refs[8:10]]
     core = lax.axis_index("core")
     two = 2 * owned
     load = side_by_side(core, diag_refs, cot_diag, 0, cot_sem)
     run(load, "start")
-    start, grad = 0, None
-    for dpre_two, tok, cot in groups:
-        rows = tok.shape[0]
-        dact = dot_last(cot[...], w_out[3 * owned :, :])
-        last = (dact * slope[pl.ds(start, rows), :]).astype(jnp.bfloat16)
-        terms = dot_first(jnp.concatenate([dpre_two[...], last], axis=1), tok[...])
-        grad = terms if grad is None else grad + terms
-        start += rows
+    dact = dot_last(cot[...], w_out[3 * owned :, :])
+    last = (dact * slope[...]).astype(jnp.bfloat16)
+    grad = dot_first(jnp.concatenate([dpre_two[...], last], axis=1), tok[...])
     run(load, "wait")
     dpre_diag[...] = (dot_last(cot_diag[...], w_out[...]) * slope_diag[...]).astype(jnp.bfloat16)
     grad = grad + dot_first(dpre_diag[:, two:], tok_diag[...])
@@ -345,54 +320,39 @@
     w_two, w_one = to_far(own_w, 2), to_far(own_w, 1)
     from_x, from_y = to_x(own), to_y(own)
     own_other = to_core(own)
+    from_x, from_y, own_other, w_one = barrier((from_x, from_y, own_other, w_one))
+    tok_diag = to_y(from_x.reshape(2 * rows, feats)[: rows + EXTRA])
+    cot_diag = to_x(from_y.reshape(2 * rows, feats)[rows - EXTRA :])
+    x_other, y_other = to_core(from_x), to_core(from_y)
     w_three = to_far(w_two, 1)
-
-    def early_shapes(here):
-        return (
-            bf16(here, owned),
-            bf16(here, owned),
-            f32(here, width),
-            f32(2 * owned, width),
-            bf16(here, width),
-            bf16(here, width),
-        )
-
-    act_own, dpre_own, mixed_terms_own, grad_terms, tok_own, cot_own, w_in_three, w_out_three, bias = (
+    act_two, dpre_two, mixed_terms, grad_terms, tok, cot, w_in_three, w_out_three, bias = (
         pl.pallas_call(
-            functools.partial(own_kernel, owned),
-            out_shape=early_shapes(rows)
-            + (bf16(3 * owned, width), bf16(3 * owned, width), bf16(16, 3 * owned)),
-            in_specs=anywhere(5),
+            functools.partial(early_kernel, owned),
+            out_shape=(
+                bf16(early_rows, owned),
+                bf16(early_rows, owned),
+                f32(early_rows, width),
+                f32(2 * owned, width),
+                bf16(early_rows, width),
+                bf16(early_rows, width),
+                bf16(3 * owned, width),
+                bf16(3 * owned, width),
+                bf16(16, 3 * owned),
+            ),
+            in_specs=anywhere(9),
             out_specs=vmem(9),
             scratch_shapes=[
-                pltpu.VMEM((rows, 2 * owned), jnp.bfloat16),
-                dma((2,)),
-                dma((2,)),
+                pltpu.VMEM((early_rows, 2 * owned), jnp.bfloat16),
+                dma((NEAR - 1, 2)),
+                dma((NEAR - 1, 2)),
                 dma((3, 3)),
             ],
             compiler_params=params,
-            cost_estimate=cost(OWN_COST, rows),
-            name="own",
-        )(own, own_other, own_w, w_one, w_two)
-    )
-    from_x, from_y, grad_terms = barrier((from_x, from_y, grad_terms))
-    tok_diag, cot_diag = to_y(from_x[0]), to_x(from_y[1])
-    x_other, y_other = to_core(from_x), to_core(from_y)
-    act_near, dpre_near, mixed_terms_near, grad_terms, tok_near, cot_near = pl.pallas_call(
-        functools.partial(early_kernel, owned),
-        out_shape=early_shapes(2 * rows),
-        in_specs=anywhere(4) + vmem(4),
-        out_specs=vmem(6),
-        scratch_shapes=[
-            pltpu.VMEM((2 * rows, 2 * owned), jnp.bfloat16),
-            dma((2, 2)),
-            dma((2, 2)),
-        ],
-        compiler_params=params,
-        cost_estimate=cost(early_rows * units, early_rows),
-        name="early",
-    )(from_x, x_other, from_y, y_other, w_in_three, w_out_three, bias, grad_terms)
-    tok_diag, cot_diag, act_near = barrier((tok_diag, cot_diag, act_near))
+            cost_estimate=cost(early_rows * units, early_rows),
+            name="early",
+        )(own, own_other, from_x, x_other, from_y, y_other, own_w, w_one, w_two)
+    )
+    tok_diag, cot_diag, act_two = barrier((tok_diag, cot_diag, act_two))
     tok_diag_other, cot_diag_other = to_core(tok_diag), to_core(cot_diag)
 
     mine, other, slope, w_in_all, w_out_all, bias = pl.pallas_call(
@@ -405,16 +365,13 @@
             bf16(units, width),
             bf16(16, units),
         ),
-        in_specs=vmem(10),
+        in_specs=vmem(7),
         out_specs=vmem(6),
         scratch_shapes=[pltpu.VMEM((2 * owned, width), jnp.bfloat16), dma((4,))],
         compiler_params=params,
         cost_estimate=cost(8 * early_rows * units * width, 4 * count * width),
         name="output",
-    )(
-        act_own, tok_own, mixed_terms_own, act_near, tok_near, mixed_terms_near,
-        w_in_three, w_out_three, bias, w_three,
-    )
+    )(act_two, tok, mixed_terms, w_in_three, w_out_three, bias, w_three)
     received = to_core(other)
 
     tok_diag_other, cot_diag_other, w_in_all = barrier((tok_diag_other, cot_diag_other, w_in_all))
@@ -445,7 +402,7 @@
     grad_own, grad_one, grad_two, grad_three = pl.pallas_call(
         functools.partial(gradient_kernel, owned),
         out_shape=[bf16(owned, width)] * 4,
-        in_specs=vmem(11) + anywhere(2),
+        in_specs=vmem(8) + anywhere(2),
         out_specs=vmem(4),
         scratch_shapes=[
             pltpu.VMEM((rows, width), jnp.bfloat16),
@@ -456,8 +413,8 @@
         cost_estimate=cost(early_rows * units, early_rows),
         name="gradient",
     )(
-        dpre_own, tok_own, cot_own, dpre_near, tok_near, cot_near,
-        grad_terms, tok_last, slope, slope_diag, w_out_all, cot_diag, cot_diag_other,
+        dpre_two, tok, cot, grad_terms, tok_last, slope, slope_diag, w_out_all,
+        cot_diag, cot_diag_other,
     )
     relayed = to_far(grad_three, 1)
     from_one = to_far(grad_one, 1)

time: 90.8 us -> 89.1 us (0.981)
  starting transfers between devices: 23.2 us -> 18.9 us
  waiting for transfers between devices: 43.1 us -> 45.2 us
  Pallas kernels: 19.3 us -> 20.6 us
  other arithmetic: 4.31 us -> 3.2 us
    ppermute x20, starting transfers between devices: 23.2 us -> 18.9 us  [permute(): return lax.ppermute(value, AXES, pairs)]
    ppermute x20, waiting for transfers between devices: 43.1 us -> 45.2 us  [permute(): return lax.ppermute(value, AXES, pairs)]
    another operation x1, other arithmetic: 1.3 us -> 0.1 us  [on_device_lines(): own = jnp.stack([tokens, cotangent])]
    pallas_call x1, Pallas kernels: 4.14 us -> 5.12 us  [on_device_lines(): pl.pallas_call(functools.partial(gradient_kernel, owned), out_shape=[bf16...]
    pallas_call x2 -> x1, Pallas kernels: 7.95 us -> 7.7 us  [on_device_lines(): pl.pallas_call(functools.partial(early_kernel, owned), out_shape=(bf16(ea...]
  transfers between devices with their start and end apart: 20 -> 20, of which waited for: 9 -> 10; matrix products, arithmetic and copies ran while one was open for 1% -> 1% of each run, Pallas kernels for 21% -> 23%
where the time goes in v8:
time: 89.1 us; the launch traced here: 89 us
  waiting for transfers between devices  45.2 us (51%)
  Pallas kernels  20.6 us (23%)
  starting transfers between devices  18.9 us (21%)
  other arithmetic  3.2 us (4%)
    ppermute x20, waiting for transfers between devices, permute(): return lax.ppermute(value, AXES, pairs)  45.2 us
    ppermute x20, starting transfers between devices, permute(): return lax.ppermute(value, AXES, pairs)  18.9 us
    pallas_call x1, Pallas kernels, on_device_lines(): pl.pallas_call(functools.partial(early_kernel, owned), out_shape=(bf16(ea...  7.7 us
    pallas_call x1, Pallas kernels, on_device_lines(): pl.pallas_call(functools.partial(gradient_kernel, owned), out_shape=[bf16...  5.12 us
    pallas_call x1, Pallas kernels, on_device_lines(): pl.pallas_call(functools.partial(output_kernel, owned), out_shape=(bf16(e...  4.87 us
    pallas_call x1, Pallas kernels, on_device_lines(): pl.pallas_call(diagonal_kernel, out_shape=(bf16(rows, feats), bf16(rows,...  2.28 us
  transfers between devices with their start and end apart: 20, of which 10 were waited for; matrix products, arithmetic and copies ran while one was open for 1% of the time, Pallas kernels for 23%

profile of v8, /device:TPU:0, one launch (start us, length us, event | category | flops | bytes accessed | tf_op | source)
XLA Modules:
  0.0 89.0 jit_solution(2029495903823374330)
XLA Ops:
  0.7 1.2 %fusion.1.refs_6_ = bf16[272,1024]{1,0:T(8,128)(2,1)S(1)} fusion(bf16[1,128]{1,0:T(2,128)(2,1)} %bitcast.9, bf16[128,1024]{1,0:T(8,128)(2,1)} %param.9, bf16[128,1024]{1,0:T(8,128)(2,1)} %param.7), kind=kLoop, calls=%fused_computation.4 | loop fusion | flops 2228224 | bytes 1081600 | tf_op jit(solution)/shard_map/concatenate | solution.py:317
  2.1 3.0 %collective-permute-start = (bf16[2,512,512]{2,1,0:T(8,128)(2,1)S(1)}, bf16[2,512,512]{2,1,0:T(8,128)(2,1)S(1)}, u32[]{:S(2)}, u32[]{:S(2)}) collective-permute-start(bf16[2,512,512]{2,1,0:T(8,128)(2,1)S(1)} %pad_maximum_fusion.refs_0_), channel_id=1, source_target_pairs={{0,2},{1,3},{2,0},{3,1},{4,6},{5,7},{6,4},{7,5},{8,10},{9,11},{10,... | collective-permute-start | bytes 3145736 | tf_op jit(solution)/shard_map/ppermute | solution.py:276
  5.1 1.5 %collective-permute-start.1 = (bf16[2,512,512]{2,1,0:T(8,128)(2,1)S(1)}, bf16[2,512,512]{2,1,0:T(8,128)(2,1)S(1)}, u32[]{:S(2)}, u32[]{:S(2)}) collective-permute-start(bf16[2,512,512]{2,1,0:T(8,128)(2,1)S(1)} %pad_maximum_fusion.refs_0_), channel_id=1, source_target_pairs={{0,4},{1,5},{2,6},{3,7},{4,0},{5,1},{6,2},{7,3},{8,12},{9,13},{10,... | collective-permute-start | bytes 3145736 | tf_op jit(solution)/shard_map/ppermute | solution.py:276
  6.6 1.6 %collective-permute-start.3 = (bf16[272,1024]{1,0:T(8,128)(2,1)S(1)}, bf16[272,1024]{1,0:T(8,128)(2,1)S(1)}, u32[]{:S(2)}, u32[]{:S(2)}) collective-permute-start(bf16[272,1024]{1,0:T(8,128)(2,1)S(1)} %fusion.1.refs_6_), channel_id=1, source_target_pairs={{0,8},{1,9},{2,10},{3,11},{4,12},{5,13},{6,14},{7,15},{8,0},{9,1},... | collective-permute-start | bytes 1671176 | tf_op jit(solution)/shard_map/ppermute | solution.py:276
  8.2 2.6 %collective-permute-start.6 = (bf16[272,1024]{1,0:T(8,128)(2,1)S(1)}, bf16[272,1024]{1,0:T(8,128)(2,1)S(1)}, u32[]{:S(2)}, u32[]{:S(2)}) collective-permute-start(bf16[272,1024]{1,0:T(8,128)(2,1)S(1)} %fusion.1.refs_6_), channel_id=1, source_target_pairs={{0,16},{1,17},{2,18},{3,19},{4,20},{5,21},{6,22},{7,23},{8,24},{9,... | collective-permute-start | bytes 1671176 | tf_op jit(solution)/shard_map/ppermute | solution.py:276
  10.8 22.7 %collective-permute-done.3.refs_7_ = bf16[272,1024]{1,0:T(8,128)(2,1)S(1)} collective-permute-done((bf16[272,1024]{1,0:T(8,128)(2,1)S(1)}, bf16[272,1024]{1,0:T(8,128)(2,1)S(1)}, u32[]{:S(2)}, u32[]{:S(2)}) %collective-permute-start.3) | collective-permute-done | bytes 557088 | tf_op jit(solution)/shard_map/ppermute | solution.py:276
  33.6 0.5 collective-permute-start.5
  34.1 0.6 collective-permute-start.7
  34.7 0.4 collective-permute-start.8
  35.2 0.7 collective-permute-done.6.refs_8_
  35.9 0.4 collective-permute-start.9
  36.3 1.4 %collective-permute-done.5.refs_5_ = bf16[2,512,512]{2,1,0:T(8,128)(2,1)S(1)} collective-permute-done((bf16[2,512,512]{2,1,0:T(8,128)(2,1)S(1)}, bf16[2,512,512]{2,1,0:T(8,128)(2,1)S(1)}, u32[]{:S(2)}, u32[]{:S(2)}) %collective-permute-start.5) | collective-permute-done | bytes 1048608 | tf_op jit(solution)/shard_map/ppermute | solution.py:276
  37.7 7.7 %early.1 = (bf16[1536,128]{1,0:T(8,128)(2,1)S(1)}, bf16[1536,128]{1,0:T(8,128)(2,1)S(1)}, f32[1536,1024]{1,0:T(8,128)S(1)}, f32[256,1024]{1,0:T(8,128)S(1)}, bf1...) custom-call(bf16[2,512,512]{2,1,0:T(8,128)(2,1)S(1)} %pad_maximum_fu, ...), custom_call_target="tpu_custom_call" | custom-call | flops 786432 | bytes 1536 | tf_op jit(solution)/shard_map/early/pallas_call | solution.py:329
  45.4 3.7 %collective-permute-done.7.refs_3_ = bf16[560,512]{1,0:T(8,128)(2,1)S(1)} collective-permute-done((bf16[560,512]{1,0:T(8,128)(2,1)S(1)}, bf16[560,512]{1,0:T(8,128)(2,1)S(1)}, u32[]{:S(2)}, u32[]{:S(2)}) %collective-permute-start.7) | collective-permute-done | bytes 573472 | tf_op jit(solution)/shard_map/ppermute | solution.py:276
  49.5 0.5 collective-permute-start.11
  50.0 4.9 %output.1 = (bf16[1536,512]{1,0:T(8,128)(2,1)S(1)}, bf16[1536,512]{1,0:T(8,128)(2,1)S(1)}, f32[1536,128]{1,0:T(8,128)S(1)}, bf16[512,1024]{1,0:T(8,128)(2,1)S(1)...) custom-call(bf16[1536,128]{1,0:T(8,128)(2,1)S(1)} %get-tuple-element.57.refs_0_, ...), custom_call_target="tpu_custom_call" | custom-call | flops 6442450944 | bytes 8388608 | tf_op jit(solution)/shard_map/output/pallas_call | solution.py:358
  55.0 2.3 %diagonal.1 = (bf16[512,512]{1,0:T(8,128)(2,1)S(1)}, bf16[512,512]{1,0:T(8,128)(2,1)S(1)}, f32[512,512]{1,0:T(8,128)S(1)}, bf16[512,1024]{1,0:T(8,128)(2,1)S(1)}) custom-call(bf16[512,1024]{1,0:T(8,128)(2,1)S(1)} %get-tuple-element.67.refs_0_, bf16[512,1024]{1,0:T(8,128)(2,1)S(1)} %get-tuple-element.68.refs_1_.refs_7_, ...), custom_call_target="tpu_custom_call" | custom-call | flops 12884901888 | bytes 2097152 | tf_op jit(solution)/shard_map/diagonal/pallas_call | solution.py:378
  57.3 0.5 collective-permute-start.15
  57.8 0.5 collective-permute-done.12.other_ref
  58.3 0.4 pair_sum.1
  58.7 1.0 %collective-permute-start.13 = (bf16[512,512]{1,0:T(8,128)(2,1)S(1)}, bf16[512,512]{1,0:T(8,128)(2,1)S(1)}, u32[]{:S(2)}, u32[]{:S(2)}) collective-permute-start(bf16[512,512]{1,0:T(8,128)(2,1)S(1)} %get-tuple-element.76), channel_id=1, source_target_pairs={{0,2},{1,3},{2,0},{3,1},{4,6},{5,7},{6,4},{7,5},{8,10},{9,11},{10,... | collective-permute-start | bytes 1572872 | tf_op jit(solution)/shard_map/ppermute | solution.py:276
  59.7 1.5 %collective-permute-start.14 = (bf16[512,512]{1,0:T(8,128)(2,1)S(1)}, bf16[512,512]{1,0:T(8,128)(2,1)S(1)}, u32[]{:S(2)}, u32[]{:S(2)}) collective-permute-start(bf16[512,512]{1,0:T(8,128)(2,1)S(1)} %get-tuple-element.77), channel_id=1, source_target_pairs={{0,4},{1,5},{2,6},{3,7},{4,0},{5,1},{6,2},{7,3},{8,12},{9,13},{10,... | collective-permute-start | bytes 1572872 | tf_op jit(solution)/shard_map/ppermute | solution.py:276
  61.2 5.1 %gradient.1 = (bf16[128,1024]{1,0:T(8,128)(2,1)S(1)}, bf16[128,1024]{1,0:T(8,128)(2,1)S(1)}, bf16[128,1024]{1,0:T(8,128)(2,1)S(1)}, bf16[128,1024]{1,0:T(8,128)(2,1)S(1)}) custom-call(bf16[1536,128]{1,0:T(8,128)(2,1)S(1)} %get-tuple-element.79.refs_0_, bf16[1536,1024]{1,0:T(8,128)(2,1)S(1)} %get-tuple-element.58.refs_1_, ...), custom_call_target="tpu_custom_call" | custom-call | flops 786432 | bytes 1536 | tf_op jit(solution)/shard_map/gradient/pallas_call | solution.py:402
  66.8 1.4 %collective-permute-start.16 = (bf16[512,512]{1,0:T(8,128)(2,1)S(1)}, bf16[512,512]{1,0:T(8,128)(2,1)S(1)}, u32[]{:S(2)}, u32[]{:S(2)}) collective-permute-start(bf16[512,512]{1,0:T(8,128)(2,1)S(1)} %pair_sum_diagonal.1), channel_id=1, source_target_pairs={{0,6},{1,7},{2,4},{3,5},{4,2},{5,3},{6,0},{7,1},{8,14},{9,15},{10,... | collective-permute-start | bytes 1572872 | tf_op jit(solution)/shard_map/ppermute | solution.py:276
  68.2 1.5 %collective-permute-start.17 = (bf16[128,1024]{1,0:T(8,128)(2,1)S(1)}, bf16[128,1024]{1,0:T(8,128)(2,1)S(1)}, u32[]{:S(2)}, u32[]{:S(2)}) collective-permute-start(bf16[128,1024]{1,0:T(8,128)(2,1)S(1)} %get-tuple-element.90), channel_id=1, source_target_pairs={{0,8},{1,9},{2,10},{3,11},{4,12},{5,13},{6,14},{7,15},{8,0},{9,1},... | collective-permute-start | bytes 786440 | tf_op jit(solution)/shard_map/ppermute | solution.py:276
  69.7 5.9 %collective-permute-done.18 = bf16[128,1024]{1,0:T(8,128)(2,1)S(1)} collective-permute-done((bf16[128,1024]{1,0:T(8,128)(2,1)S(1)}, bf16[128,1024]{1,0:T(8,128)(2,1)S(1)}, u32[]{:S(2)}, u32[]{:S(2)}) %collective-permute-start.18) | collective-permute-done | bytes 262176 | tf_op jit(solution)/shard_map/ppermute | solution.py:276
  75.7 1.4 %collective-permute-start.19 = (bf16[128,1024]{1,0:T(8,128)(2,1)S(1)}, bf16[128,1024]{1,0:T(8,128)(2,1)S(1)}, u32[]{:S(2)}, u32[]{:S(2)}) collective-permute-start(bf16[128,1024]{1,0:T(8,128)(2,1)S(1)} %add_convert_fusion.1), channel_id=1, source_target_pairs={{0,16},{1,17},{2,18},{3,19},{4,20},{5,21},{6,22},{7,23},{8,24},{9,... | collective-permute-start | bytes 786440 | tf_op jit(solution)/shard_map/ppermute | solution.py:276
  77.0 6.6 %collective-permute-done.14.y_ref = bf16[512,512]{1,0:T(8,128)(2,1)S(1)} collective-permute-done((bf16[512,512]{1,0:T(8,128)(2,1)S(1)}, bf16[512,512]{1,0:T(8,128)(2,1)S(1)}, u32[]{:S(2)}, u32[]{:S(2)}) %collective-permute-start.14) | collective-permute-done | bytes 524320 | tf_op jit(solution)/shard_map/ppermute | solution.py:276
  83.8 1.1 %collective-permute-done.16 = bf16[512,512]{1,0:T(8,128)(2,1)S(1)} collective-permute-done((bf16[512,512]{1,0:T(8,128)(2,1)S(1)}, bf16[512,512]{1,0:T(8,128)(2,1)S(1)}, u32[]{:S(2)}, u32[]{:S(2)}) %collective-permute-start.16) | collective-permute-done | bytes 524320 | tf_op jit(solution)/shard_map/ppermute | solution.py:276
  84.9 1.0 %add_convert_fusion = bf16[512,512]{1,0:T(8,128)(2,1)} fusion(f32[512,512]{1,0:T(8,128)S(1)} %plane_sum.1, bf16[512,512]{1,0:T(8,128)(2,1)S(1)} %collective-permute-done.16), kind=kLoop, calls=%fused_computation.3 | loop fusion | flops 786432 | bytes 2097152 | tf_op jit(solution)/shard_map/convert_element_type | solution.py:450
  85.9 2.2 %collective-permute-done.19 = bf16[128,1024]{1,0:T(8,128)(2,1)S(1)} collective-permute-done((bf16[128,1024]{1,0:T(8,128)(2,1)S(1)}, bf16[128,1024]{1,0:T(8,128)(2,1)S(1)}, u32[]{:S(2)}, u32[]{:S(2)}) %collective-permute-start.19) | collective-permute-done | bytes 262176 | tf_op jit(solution)/shard_map/ppermute | solution.py:276
  88.1 0.9 %add_multiply_fusion = f32[128,1024]{1,0:T(8,128)} fusion(bf16[128,1024]{1,0:T(8,128)(2,1)S(1)} %collective-permute-done.19, bf16[128,1024]{1,0:T(8,128)(2,1)S(1)} %collective-permute-done.17, bf16[128,1024]{1,0:T(8,128)(2,1)S(1)} %get-tuple-element.89), kind=kLoop, calls=%fused_computation.5 | loop fusion | flops 786432 | bytes 1310720 | tf_op jit(solution)/shard_map/mul | solution.py:451
  (26 shorter events, 1.6 us)
Async XLA Ops:
  0.6 1.2 %copy-start.1 = (bf16[512,512]{1,0:T(8,128)(2,1)S(1)}, bf16[512,512]{1,0:T(8,128)(2,1)}, u32[]{:S(2)}) copy-start(bf16[512,512]{1,0:T(8,128)(2,1)} %param.5) | copy-start | bytes 1572868
  0.6 1.4 %copy-start = (bf16[512,512]{1,0:T(8,128)(2,1)S(1)}, bf16[512,512]{1,0:T(8,128)(2,1)}, u32[]{:S(2)}) copy-start(bf16[512,512]{1,0:T(8,128)(2,1)} %param.6) | copy-start | bytes 1572868
  2.1 31.4 %collective-permute-start = (bf16[2,512,512]{2,1,0:T(8,128)(2,1)S(1)}, bf16[2,512,512]{2,1,0:T(8,128)(2,1)S(1)}, u32[]{:S(2)}, u32[]{:S(2)}) collective-permute-start(bf16[2,512,512]{2,1,0:T(8,128)(2,1)S(1)} %pad_maximum_fusion.refs_0_), channel_id=1, source_target_pairs={{0,2},{1,3},{2,0},{3,1},{4,6},{5,7},{6,4},{7,5},{8,10},{9,11},{10,... | collective-permute-start | bytes 3145736 | tf_op jit(solution)/shard_map/ppermute | solution.py:276
  5.1 28.4 %collective-permute-start.1 = (bf16[2,512,512]{2,1,0:T(8,128)(2,1)S(1)}, bf16[2,512,512]{2,1,0:T(8,128)(2,1)S(1)}, u32[]{:S(2)}, u32[]{:S(2)}) collective-permute-start(bf16[2,512,512]{2,1,0:T(8,128)(2,1)S(1)} %pad_maximum_fusion.refs_0_), channel_id=1, source_target_pairs={{0,4},{1,5},{2,6},{3,7},{4,0},{5,1},{6,2},{7,3},{8,12},{9,13},{10,... | collective-permute-start | bytes 3145736 | tf_op jit(solution)/shard_map/ppermute | solution.py:276
  6.6 26.9 %collective-permute-start.2 = (bf16[2,512,512]{2,1,0:T(8,128)(2,1)S(1)}, bf16[2,512,512]{2,1,0:T(8,128)(2,1)S(1)}, u32[]{:S(2)}, u32[]{:S(2)}) collective-permute-start(bf16[2,512,512]{2,1,0:T(8,128)(2,1)S(1)} %pad_maximum_fusion.refs_0_), channel_id=1, source_target_pairs={{0,1},{1,0},{2,3},{3,2},{4,5},{5,4},{6,7},{7,6},{8,9},{9,8},{10,11... | collective-permute-start | bytes 3145736 | tf_op jit(solution)/shard_map/ppermute | solution.py:276
  6.6 26.9 %collective-permute-start.3 = (bf16[272,1024]{1,0:T(8,128)(2,1)S(1)}, bf16[272,1024]{1,0:T(8,128)(2,1)S(1)}, u32[]{:S(2)}, u32[]{:S(2)}) collective-permute-start(bf16[272,1024]{1,0:T(8,128)(2,1)S(1)} %fusion.1.refs_6_), channel_id=1, source_target_pairs={{0,8},{1,9},{2,10},{3,11},{4,12},{5,13},{6,14},{7,15},{8,0},{9,1},... | collective-permute-start | bytes 1671176 | tf_op jit(solution)/shard_map/ppermute | solution.py:276
  8.2 27.6 %collective-permute-start.6 = (bf16[272,1024]{1,0:T(8,128)(2,1)S(1)}, bf16[272,1024]{1,0:T(8,128)(2,1)S(1)}, u32[]{:S(2)}, u32[]{:S(2)}) collective-permute-start(bf16[272,1024]{1,0:T(8,128)(2,1)S(1)} %fusion.1.refs_6_), channel_id=1, source_target_pairs={{0,16},{1,17},{2,18},{3,19},{4,20},{5,21},{6,22},{7,23},{8,24},{9,... | collective-permute-start | bytes 1671176 | tf_op jit(solution)/shard_map/ppermute | solution.py:276
  33.5 2.8 %collective-permute-start.4 = (bf16[2,512,512]{2,1,0:T(8,128)(2,1)S(1)}, bf16[2,512,512]{2,1,0:T(8,128)(2,1)S(1)}, u32[]{:S(2)}, u32[]{:S(2)}) collective-permute-start(bf16[2,512,512]{2,1,0:T(8,128)(2,1)S(1)} %collective-permute-done.refs_2_), channel_id=1, source_target_pairs={{0,1},{1,0},{2,3},{3,2},{4,5},{5,4},{6,7},{7,6},{8,9},{9,8},{10,11... | collective-permute-start | bytes 3145736 | tf_op jit(solution)/shard_map/ppermute | solution.py:276
  33.6 4.1 %collective-permute-start.5 = (bf16[2,512,512]{2,1,0:T(8,128)(2,1)S(1)}, bf16[2,512,512]{2,1,0:T(8,128)(2,1)S(1)}, u32[]{:S(2)}, u32[]{:S(2)}) collective-permute-start(bf16[2,512,512]{2,1,0:T(8,128)(2,1)S(1)} %collective-permute-done.1.refs_4_), channel_id=1, source_target_pairs={{0,1},{1,0},{2,3},{3,2},{4,5},{5,4},{6,7},{7,6},{8,9},{9,8},{10,11... | collective-permute-start | bytes 3145736 | tf_op jit(solution)/shard_map/ppermute | solution.py:276
  34.1 15.0 %collective-permute-start.7 = (bf16[560,512]{1,0:T(8,128)(2,1)S(1)}, bf16[560,512]{1,0:T(8,128)(2,1)S(1)}, u32[]{:S(2)}, u32[]{:S(2)}) collective-permute-start(bf16[560,512]{1,0:T(8,128)(2,1)S(1)} %slice.8), channel_id=1, source_target_pairs={{0,4},{1,5},{2,6},{3,7},{4,0},{5,1},{6,2},{7,3},{8,12},{9,13},{10,... | collective-permute-start | bytes 1720328 | tf_op jit(solution)/shard_map/ppermute | solution.py:276
  34.7 14.7 %collective-permute-start.8 = (bf16[560,512]{1,0:T(8,128)(2,1)S(1)}, bf16[560,512]{1,0:T(8,128)(2,1)S(1)}, u32[]{:S(2)}, u32[]{:S(2)}) collective-permute-start(bf16[560,512]{1,0:T(8,128)(2,1)S(1)} %slice.9), channel_id=1, source_target_pairs={{0,2},{1,3},{2,0},{3,1},{4,6},{5,7},{6,4},{7,5},{8,10},{9,11},{10,... | collective-permute-start | bytes 1720328 | tf_op jit(solution)/shard_map/ppermute | solution.py:276
  35.9 14.1 %collective-permute-start.9 = (bf16[272,1024]{1,0:T(8,128)(2,1)S(1)}, bf16[272,1024]{1,0:T(8,128)(2,1)S(1)}, u32[]{:S(2)}, u32[]{:S(2)}) collective-permute-start(bf16[272,1024]{1,0:T(8,128)(2,1)S(1)} %collective-permute-done.6.refs_8_), channel_id=1, source_target_pairs={{0,8},{1,9},{2,10},{3,11},{4,12},{5,13},{6,14},{7,15},{8,0},{9,1},... | collective-permute-start | bytes 1671176 | tf_op jit(solution)/shard_map/ppermute | solution.py:276
  49.5 5.5 %collective-permute-start.10 = (bf16[560,512]{1,0:T(8,128)(2,1)S(1)}, bf16[560,512]{1,0:T(8,128)(2,1)S(1)}, u32[]{:S(2)}, u32[]{:S(2)}) collective-permute-start(bf16[560,512]{1,0:T(8,128)(2,1)S(1)} %collective-permute-done.7.refs_3_), channel_id=1, source_target_pairs={{0,1},{1,0},{2,3},{3,2},{4,5},{5,4},{6,7},{7,6},{8,9},{9,8},{10,11... | collective-permute-start | bytes 1720328 | tf_op jit(solution)/shard_map/ppermute | solution.py:276
  49.5 5.5 %collective-permute-start.11 = (bf16[560,512]{1,0:T(8,128)(2,1)S(1)}, bf16[560,512]{1,0:T(8,128)(2,1)S(1)}, u32[]{:S(2)}, u32[]{:S(2)}) collective-permute-start(bf16[560,512]{1,0:T(8,128)(2,1)S(1)} %collective-permute-done.8.refs_8_), channel_id=1, source_target_pairs={{0,1},{1,0},{2,3},{3,2},{4,5},{5,4},{6,7},{7,6},{8,9},{9,8},{10,11... | collective-permute-start | bytes 1720328 | tf_op jit(solution)/shard_map/ppermute | solution.py:276
  54.9 3.5 %collective-permute-start.12 = (bf16[1536,512]{1,0:T(8,128)(2,1)S(1)}, bf16[1536,512]{1,0:T(8,128)(2,1)S(1)}, u32[]{:S(2)}, u32[]{:S(2)}) collective-permute-start(bf16[1536,512]{1,0:T(8,128)(2,1)S(1)} %get-tuple-element.73), channel_id=1, source_target_pairs={{0,1},{1,0},{2,3},{3,2},{4,5},{5,4},{6,7},{7,6},{8,9},{9,8},{10,11... | collective-permute-start | bytes 4718600 | tf_op jit(solution)/shard_map/ppermute | solution.py:276
  57.3 9.4 %collective-permute-start.15 = (bf16[512,512]{1,0:T(8,128)(2,1)S(1)}, bf16[512,512]{1,0:T(8,128)(2,1)S(1)}, u32[]{:S(2)}, u32[]{:S(2)}) collective-permute-start(bf16[512,512]{1,0:T(8,128)(2,1)S(1)} %get-tuple-element.88), channel_id=1, source_target_pairs={{0,1},{1,0},{2,3},{3,2},{4,5},{5,4},{6,7},{7,6},{8,9},{9,8},{10,11... | collective-permute-start | bytes 1572872 | tf_op jit(solution)/shard_map/ppermute | solution.py:276
  58.7 18.3 %collective-permute-start.13 = (bf16[512,512]{1,0:T(8,128)(2,1)S(1)}, bf16[512,512]{1,0:T(8,128)(2,1)S(1)}, u32[]{:S(2)}, u32[]{:S(2)}) collective-permute-start(bf16[512,512]{1,0:T(8,128)(2,1)S(1)} %get-tuple-element.76), channel_id=1, source_target_pairs={{0,2},{1,3},{2,0},{3,1},{4,6},{5,7},{6,4},{7,5},{8,10},{9,11},{10,... | collective-permute-start | bytes 1572872 | tf_op jit(solution)/shard_map/ppermute | solution.py:276
  59.7 24.0 %collective-permute-start.14 = (bf16[512,512]{1,0:T(8,128)(2,1)S(1)}, bf16[512,512]{1,0:T(8,128)(2,1)S(1)}, u32[]{:S(2)}, u32[]{:S(2)}) collective-permute-start(bf16[512,512]{1,0:T(8,128)(2,1)S(1)} %get-tuple-element.77), channel_id=1, source_target_pairs={{0,4},{1,5},{2,6},{3,7},{4,0},{5,1},{6,2},{7,3},{8,12},{9,13},{10,... | collective-permute-start | bytes 1572872 | tf_op jit(solution)/shard_map/ppermute | solution.py:276
  66.3 9.3 %collective-permute-start.18 = (bf16[128,1024]{1,0:T(8,128)(2,1)S(1)}, bf16[128,1024]{1,0:T(8,128)(2,1)S(1)}, u32[]{:S(2)}, u32[]{:S(2)}) collective-permute-start(bf16[128,1024]{1,0:T(8,128)(2,1)S(1)} %get-tuple-element.93), channel_id=1, source_target_pairs={{0,8},{1,9},{2,10},{3,11},{4,12},{5,13},{6,14},{7,15},{8,0},{9,1},... | collective-permute-start | bytes 786440 | tf_op jit(solution)/shard_map/ppermute | solution.py:276
  66.8 18.1 %collective-permute-start.16 = (bf16[512,512]{1,0:T(8,128)(2,1)S(1)}, bf16[512,512]{1,0:T(8,128)(2,1)S(1)}, u32[]{:S(2)}, u32[]{:S(2)}) collective-permute-start(bf16[512,512]{1,0:T(8,128)(2,1)S(1)} %pair_sum_diagonal.1), channel_id=1, source_target_pairs={{0,6},{1,7},{2,4},{3,5},{4,2},{5,3},{6,0},{7,1},{8,14},{9,15},{10,... | collective-permute-start | bytes 1572872 | tf_op jit(solution)/shard_map/ppermute | solution.py:276
  68.2 17.7 %collective-permute-start.17 = (bf16[128,1024]{1,0:T(8,128)(2,1)S(1)}, bf16[128,1024]{1,0:T(8,128)(2,1)S(1)}, u32[]{:S(2)}, u32[]{:S(2)}) collective-permute-start(bf16[128,1024]{1,0:T(8,128)(2,1)S(1)} %get-tuple-element.90), channel_id=1, source_target_pairs={{0,8},{1,9},{2,10},{3,11},{4,12},{5,13},{6,14},{7,15},{8,0},{9,1},... | collective-permute-start | bytes 786440 | tf_op jit(solution)/shard_map/ppermute | solution.py:276
  75.7 12.4 %collective-permute-start.19 = (bf16[128,1024]{1,0:T(8,128)(2,1)S(1)}, bf16[128,1024]{1,0:T(8,128)(2,1)S(1)}, u32[]{:S(2)}, u32[]{:S(2)}) collective-permute-start(bf16[128,1024]{1,0:T(8,128)(2,1)S(1)} %add_convert_fusion.1), channel_id=1, source_target_pairs={{0,16},{1,17},{2,18},{3,19},{4,20},{5,21},{6,22},{7,23},{8,24},{9,... | collective-permute-start | bytes 786440 | tf_op jit(solution)/shard_map/ppermute | solution.py:276

commit v9 on v8

--- a/solution.py
+++ b/solution.py
@@ -14,7 +14,10 @@
 CONTRACT_FIRST = (((0,), (0,)), ((), ()))
 VMEM_LIMIT = 28 * 1024 * 1024
 PLANE_COST = 10**10
+GRADIENT_COST = 10**10
+DIAGONAL_COST = 10**6
 EXTRA = 48
+MORE = 16
 
 
 def gelu_parts(value):
@@ -174,11 +177,11 @@
     bias_all[:, three:] = bias_last
     w_last[:owned, :] = w_out[two:, :]
     w_last[owned:, :] = w_three[owned:two, :]
-    step = tok.shape[0] // 6
-
-    @pl.loop(0, 6)
-    def _(sub):
-        spot = pl.ds(pl.multiple_of(sub * step, step), step)
+    step = tok.shape[0] // 3
+
+    @pl.loop(0, 3)
+    def _(block):
+        spot = pl.ds(pl.multiple_of(block * step, step), step)
         value, slope = activate(tok[spot, :], w_three[:owned, :], bias_last[0:1, :])
         slope_ref[spot, :] = slope
         act = jnp.concatenate([act_two[spot, :], value.astype(jnp.bfloat16)], axis=1)
@@ -192,13 +195,29 @@
     run(copies, "wait")
 
 
-def diagonal_kernel(*refs):
-    w_in, w_out, bias = refs[:3]
-    mine_ref, other_ref, slope_ref, tok_diag, tok_sem = refs[5:]
+def gradient_kernel(dpre_two, tok, cot, slope, w_three, grad_ref, dpre):
+    owned = slope.shape[1]
+    step = tok.shape[0] // 3
+
+    @pl.loop(0, 3)
+    def _(block):
+        spot = pl.ds(pl.multiple_of(block * step, step), step)
+        dact = dot_last(cot[spot, :], w_three[owned : 2 * owned, :])
+        last = (dact * slope[spot, :]).astype(jnp.bfloat16)
+        dpre[spot, :] = jnp.concatenate([dpre_two[spot, :], last], axis=1)
+
+    grad_ref[...] = dot_first(dpre[...], tok[...])
+
+
+def diagonal_kernel(owned, *refs):
+    w_in, w_out, bias, grad_first, grad_last = refs[:5]
+    mine_ref, other_ref, own_ref, one_ref, two_ref, three_ref = refs[9:15]
+    tok, cot, dpre, tok_sem, cot_sem = refs[15:]
     core = lax.axis_index("core")
     rows, feats = mine_ref.shape
-    diag_refs = [ref.at[pl.ds(0, rows)] for ref in refs[3:5]]
-    load = side_by_side(core, diag_refs, tok_diag, 0, tok_sem)
+    two = 2 * owned
+    load = side_by_side(core, [ref.at[pl.ds(0, rows)] for ref in refs[5:7]], tok, 0, tok_sem)
+    load += side_by_side(core, [ref.at[pl.ds(EXTRA, rows)] for ref in refs[7:9]], cot, 0, cot_sem)
     run(load, "start")
     run(load, "wait")
     step = rows // 2
@@ -206,32 +225,19 @@
     @pl.loop(0, 2)
     def _(sub):
         spot = pl.ds(pl.multiple_of(sub * step, step), step)
-        value, slope = activate(tok_diag[spot, :], w_in[...], bias[0:1, :])
+        value, slope = activate(tok[spot, :], w_in[...], bias[0:1, :])
         act = value.astype(jnp.bfloat16)
-        slope_ref[spot, :] = slope
+        dact = dot_last(cot[spot, :], w_out[...])
+        dpre[spot, :] = (dact * slope).astype(jnp.bfloat16)
         for shift, ref in enumerate((mine_ref, other_ref)):
             ref[spot, :] = jnp.dot(
                 act, w_out[:, half_columns(core, shift, feats)], preferred_element_type=jnp.float32
             ).astype(jnp.bfloat16)
 
-
-def gradient_kernel(owned, *refs):
-    dpre_two, tok, cot, early_grad, tok_diag, slope, slope_diag, w_out = refs[:8]
-    own_ref, one_ref, two_ref, three_ref, cot_diag, dpre_diag, cot_sem = refs[10:]
-    diag_refs = [ref.at[pl.ds(EXTRA, cot_diag.shape[0])] for ref in refs[8:10]]
-    core = lax.axis_index("core")
-    two = 2 * owned
-    load = side_by_side(core, diag_refs, cot_diag, 0, cot_sem)
-    run(load, "start")
-    dact = dot_last(cot[...], w_out[3 * owned :, :])
-    last = (dact * slope[...]).astype(jnp.bfloat16)
-    grad = dot_first(jnp.concatenate([dpre_two[...], last], axis=1), tok[...])
-    run(load, "wait")
-    dpre_diag[...] = (dot_last(cot_diag[...], w_out[...]) * slope_diag[...]).astype(jnp.bfloat16)
-    grad = grad + dot_first(dpre_diag[:, two:], tok_diag[...])
+    grad = grad_last[...] + dot_first(dpre[:, two:], tok[...])
     two_ref[...] = grad[:owned].astype(jnp.bfloat16)
     three_ref[...] = grad[owned:].astype(jnp.bfloat16)
-    grad = early_grad[...] + dot_first(dpre_diag[:, :two], tok_diag[...])
+    grad = grad_first[...] + dot_first(dpre[:, :two], tok[...])
     own_ref[...] = grad[:owned].astype(jnp.bfloat16)
     one_ref[...] = grad[owned:].astype(jnp.bfloat16)
 
@@ -239,16 +245,19 @@
 def pair_kernel(rows, mine_ref, other_ref, *out_refs):
     for block, ref in enumerate(out_refs):
         spot = pl.ds(block * rows, rows)
-        ref[...] = (
+        ref[:rows, :] = (
             mine_ref[spot, :].astype(jnp.float32) + other_ref[spot, :].astype(jnp.float32)
         ).astype(jnp.bfloat16)
+        if ref.shape[0] > rows:
+            ref[rows:, :] = jnp.zeros_like(ref[rows:, :])
 
 
 def plane_kernel(own_ref, x_ref, y_ref, out_ref):
+    rows = own_ref.shape[0]
     out_ref[...] = (
         own_ref[...].astype(jnp.float32)
-        + x_ref[...].astype(jnp.float32)
-        + y_ref[...].astype(jnp.float32)
+        + x_ref[:rows, :].astype(jnp.float32)
+        + y_ref[:rows, :].astype(jnp.float32)
     )
 
 
@@ -320,7 +329,7 @@
     w_two, w_one = to_far(own_w, 2), to_far(own_w, 1)
     from_x, from_y = to_x(own), to_y(own)
     own_other = to_core(own)
-    from_x, from_y, own_other, w_one = barrier((from_x, from_y, own_other, w_one))
+    from_x, from_y, own_other = barrier((from_x, from_y, own_other))
     tok_diag = to_y(from_x.reshape(2 * rows, feats)[: rows + EXTRA])
     cot_diag = to_x(from_y.reshape(2 * rows, feats)[rows - EXTRA :])
     x_other, y_other = to_core(from_x), to_core(from_y)
@@ -352,8 +361,6 @@
             name="early",
         )(own, own_other, from_x, x_other, from_y, y_other, own_w, w_one, w_two)
     )
-    tok_diag, cot_diag, act_two = barrier((tok_diag, cot_diag, act_two))
-    tok_diag_other, cot_diag_other = to_core(tok_diag), to_core(cot_diag)
 
     mine, other, slope, w_in_all, w_out_all, bias = pl.pallas_call(
         functools.partial(output_kernel, owned),
@@ -369,70 +376,81 @@
         out_specs=vmem(6),
         scratch_shapes=[pltpu.VMEM((2 * owned, width), jnp.bfloat16), dma((4,))],
         compiler_params=params,
-        cost_estimate=cost(8 * early_rows * units * width, 4 * count * width),
+        cost_estimate=cost(early_rows * units, early_rows),
         name="output",
     )(act_two, tok, mixed_terms, w_in_three, w_out_three, bias, w_three)
+    tok_diag, cot_diag, other = barrier((tok_diag, cot_diag, other))
     received = to_core(other)
-
-    tok_diag_other, cot_diag_other, w_in_all = barrier((tok_diag_other, cot_diag_other, w_in_all))
-    mine_diag, other_diag, slope_diag, tok_last = pl.pallas_call(
-        diagonal_kernel,
-        out_shape=(bf16(rows, feats), bf16(rows, feats), f32(rows, units), bf16(rows, width)),
-        in_specs=vmem(3) + anywhere(2),
-        out_specs=vmem(4),
-        scratch_shapes=[dma((2,))],
-        compiler_params=params,
-        cost_estimate=cost(48 * rows * units * width, 4 * rows * width),
-        name="diagonal",
-    )(w_in_all, w_out_all, bias, tok_diag, tok_diag_other)
-    received_diag = to_core(other_diag)
-
-    mine, slope_diag = barrier((mine, slope_diag))
+    tok_diag_other, cot_diag_other = to_core(tok_diag), to_core(cot_diag)
+    slope, tok_diag = barrier((slope, tok_diag))
+    grad_last = pl.pallas_call(
+        gradient_kernel,
+        out_shape=f32(2 * owned, width),
+        in_specs=vmem(5),
+        out_specs=pl.BlockSpec(memory_space=pltpu.VMEM),
+        scratch_shapes=[pltpu.VMEM((early_rows, 2 * owned), jnp.bfloat16)],
+        compiler_params=params,
+        cost_estimate=cost(GRADIENT_COST, early_rows),
+        name="gradient",
+    )(dpre_two, tok, cot, slope, w_three)
+
+    mine, grad_last = barrier((mine, grad_last))
     sums = pl.pallas_call(
         functools.partial(pair_kernel, rows),
-        out_shape=[bf16(rows, feats)] * (NEAR - 1),
+        out_shape=[bf16(rows, feats)] + [bf16(rows + MORE, feats)] * 2,
         in_specs=vmem(2),
         out_specs=vmem(NEAR - 1),
         compiler_params=params,
+        cost_estimate=cost(rows, rows),
         name="pair_sum",
     )(mine, received)
     mixed_x, mixed_y = to_x(sums[1]), to_y(sums[2])
     grad_terms, mixed_own = barrier((grad_terms, sums[0]))
 
-    grad_own, grad_one, grad_two, grad_three = pl.pallas_call(
-        functools.partial(gradient_kernel, owned),
-        out_shape=[bf16(owned, width)] * 4,
-        in_specs=vmem(8) + anywhere(2),
-        out_specs=vmem(4),
+    mine_diag, other_diag, grad_own, grad_one, grad_two, grad_three = pl.pallas_call(
+        functools.partial(diagonal_kernel, owned),
+        out_shape=[bf16(rows, feats)] * 2 + [bf16(owned, width)] * 4,
+        in_specs=vmem(5) + anywhere(4),
+        out_specs=vmem(6),
         scratch_shapes=[
+            pltpu.VMEM((rows, width), jnp.bfloat16),
             pltpu.VMEM((rows, width), jnp.bfloat16),
             pltpu.VMEM((rows, units), jnp.bfloat16),
             dma((2,)),
+            dma((2,)),
         ],
         compiler_params=params,
-        cost_estimate=cost(early_rows * units, early_rows),
-        name="gradient",
+        cost_estimate=cost(DIAGONAL_COST, rows),
+        name="diagonal",
     )(
-        dpre_two, tok, cot, grad_terms, tok_last, slope, slope_diag, w_out_all,
-        cot_diag, cot_diag_other,
-    )
+        w_in_all, w_out_all, bias, grad_terms, grad_last,
+        tok_diag, tok_diag_other, cot_diag, cot_diag_other,
+    )
+    received_diag = to_core(other_diag)
     relayed = to_far(grad_three, 1)
     from_one = to_far(grad_one, 1)
 
-    mine_diag, grad_own = barrier((mine_diag, grad_own))
     (sum_diag,) = pl.pallas_call(
         functools.partial(pair_kernel, rows),
         out_shape=[bf16(rows, feats)],
         in_specs=vmem(2),
         out_specs=vmem(1),
         compiler_params=params,
+        cost_estimate=cost(rows, rows),
         name="pair_sum_diagonal",
     )(mine_diag, received_diag)
     mixed_diag = to_diagonal(sum_diag)
     grad_two, _ = barrier((grad_two, sum_diag))
-    from_two = to_far(
-        (grad_two.astype(jnp.float32) + relayed.astype(jnp.float32)).astype(jnp.bfloat16), 2
-    )
+    (line_sum,) = pl.pallas_call(
+        functools.partial(pair_kernel, owned),
+        out_shape=[bf16(owned, width)],
+        in_specs=vmem(2),
+        out_specs=vmem(1),
+        compiler_params=params,
+        cost_estimate=cost(rows, rows),
+        name="line_sum",
+    )(grad_two, relayed)
+    from_two = to_far(line_sum, 2)
     total = (
         grad_own.astype(jnp.float32)
         + from_one.astype(jnp.float32)

time: 89.1 us -> 88 us (0.988)
  starting transfers between devices: 18.9 us -> 21.5 us
  Pallas kernels: 20.6 us -> 18.1 us
  waiting for transfers between devices: 45.2 us -> 44.1 us
    ppermute x20, starting transfers between devices: 18.9 us -> 21.5 us  [permute(): return lax.ppermute(value, AXES, pairs)]
    pallas_call x2 -> x3, Pallas kernels: 7.41 us -> 5.87 us  [the longest x1 3.49 us: on_device_lines(): pl.pallas_call(functools.partial(diagonal_kernel, owned), out_shape=[bf16...]
    ppermute x20, waiting for transfers between devices: 45.2 us -> 44.1 us  [permute(): return lax.ppermute(value, AXES, pairs)]
  transfers between devices with their start and end apart: 20 -> 20, of which waited for: 10 -> 8; matrix products, arithmetic and copies ran while one was open for 1% -> 1% of each run, Pallas kernels for 23% -> 21%
where the time goes in v9:
time: 88 us; the launch traced here: 87.8 us
  waiting for transfers between devices  44.1 us (50%)
  starting transfers between devices  21.5 us (24%)
  Pallas kernels  18.1 us (21%)
  other arithmetic  3.13 us (4%)
    ppermute x20, waiting for transfers between devices, permute(): return lax.ppermute(value, AXES, pairs)  44.1 us
    ppermute x20, starting transfers between devices, permute(): return lax.ppermute(value, AXES, pairs)  21.5 us
    pallas_call x1, Pallas kernels, on_device_lines(): pl.pallas_call(functools.partial(early_kernel, owned), out_shape=(bf16(ea...  7.48 us
    pallas_call x1, Pallas kernels, on_device_lines(): pl.pallas_call(functools.partial(output_kernel, owned), out_shape=(bf16(e...  4.05 us
    pallas_call x1, Pallas kernels, on_device_lines(): pl.pallas_call(functools.partial(diagonal_kernel, owned), out_shape=[bf16...  3.49 us
    pallas_call x1, Pallas kernels, on_device_lines(): pl.pallas_call(gradient_kernel, out_shape=f32(2 * owned, width), in_specs...  2.31 us
  transfers between devices with their start and end apart: 20, of which 8 were waited for; matrix products, arithmetic and copies ran while one was open for 1% of the time, Pallas kernels for 21%

profile of v9, /device:TPU:0, one launch (start us, length us, event | category | flops | bytes accessed | tf_op | source)
XLA Modules:
  0.0 87.8 jit_solution(2299657718356129642)
XLA Ops:
  0.7 1.2 %fusion.1.refs_6_ = bf16[272,1024]{1,0:T(8,128)(2,1)S(1)} fusion(bf16[1,128]{1,0:T(2,128)(2,1)} %bitcast.9, bf16[128,1024]{1,0:T(8,128)(2,1)} %param.9, bf16[128,1024]{1,0:T(8,128)(2,1)} %param.7), kind=kLoop, calls=%fused_computation.4 | loop fusion | flops 2228224 | bytes 1081600 | tf_op jit(solution)/shard_map/concatenate | solution.py:326
  2.1 3.0 %collective-permute-start = (bf16[2,512,512]{2,1,0:T(8,128)(2,1)S(1)}, bf16[2,512,512]{2,1,0:T(8,128)(2,1)S(1)}, u32[]{:S(2)}, u32[]{:S(2)}) collective-permute-start(bf16[2,512,512]{2,1,0:T(8,128)(2,1)S(1)} %pad_maximum_fusion.refs_0_), channel_id=1, source_target_pairs={{0,2},{1,3},{2,0},{3,1},{4,6},{5,7},{6,4},{7,5},{8,10},{9,11},{10,... | collective-permute-start | bytes 3145736 | tf_op jit(solution)/shard_map/ppermute | solution.py:285
  5.1 1.5 %collective-permute-start.1 = (bf16[2,512,512]{2,1,0:T(8,128)(2,1)S(1)}, bf16[2,512,512]{2,1,0:T(8,128)(2,1)S(1)}, u32[]{:S(2)}, u32[]{:S(2)}) collective-permute-start(bf16[2,512,512]{2,1,0:T(8,128)(2,1)S(1)} %pad_maximum_fusion.refs_0_), channel_id=1, source_target_pairs={{0,4},{1,5},{2,6},{3,7},{4,0},{5,1},{6,2},{7,3},{8,12},{9,13},{10,... | collective-permute-start | bytes 3145736 | tf_op jit(solution)/shard_map/ppermute | solution.py:285
  6.6 2.6 %collective-permute-start.6 = (bf16[272,1024]{1,0:T(8,128)(2,1)S(1)}, bf16[272,1024]{1,0:T(8,128)(2,1)S(1)}, u32[]{:S(2)}, u32[]{:S(2)}) collective-permute-start(bf16[272,1024]{1,0:T(8,128)(2,1)S(1)} %fusion.1.refs_6_), channel_id=1, source_target_pairs={{0,16},{1,17},{2,18},{3,19},{4,20},{5,21},{6,22},{7,23},{8,24},{9,... | collective-permute-start | bytes 1671176 | tf_op jit(solution)/shard_map/ppermute | solution.py:285
  9.2 1.6 %collective-permute-start.5 = (bf16[272,1024]{1,0:T(8,128)(2,1)S(1)}, bf16[272,1024]{1,0:T(8,128)(2,1)S(1)}, u32[]{:S(2)}, u32[]{:S(2)}) collective-permute-start(bf16[272,1024]{1,0:T(8,128)(2,1)S(1)} %fusion.1.refs_6_), channel_id=1, source_target_pairs={{0,8},{1,9},{2,10},{3,11},{4,12},{5,13},{6,14},{7,15},{8,0},{9,1},... | collective-permute-start | bytes 1671176 | tf_op jit(solution)/shard_map/ppermute | solution.py:285
  10.8 17.5 %collective-permute-done.refs_2_ = bf16[2,512,512]{2,1,0:T(8,128)(2,1)S(1)} collective-permute-done((bf16[2,512,512]{2,1,0:T(8,128)(2,1)S(1)}, bf16[2,512,512]{2,1,0:T(8,128)(2,1)S(1)}, u32[]{:S(2)}, u32[]{:S(2)}) %collective-permute-start) | collective-permute-done | bytes 1048608 | tf_op jit(solution)/shard_map/ppermute | solution.py:285
  28.3 1.5 %collective-permute-done.1.refs_4_ = bf16[2,512,512]{2,1,0:T(8,128)(2,1)S(1)} collective-permute-done((bf16[2,512,512]{2,1,0:T(8,128)(2,1)S(1)}, bf16[2,512,512]{2,1,0:T(8,128)(2,1)S(1)}, u32[]{:S(2)}, u32[]{:S(2)}) %collective-permute-start.1) | collective-permute-done | bytes 1048608 | tf_op jit(solution)/shard_map/ppermute | solution.py:285
  29.7 0.5 collective-permute-start.4
  30.3 1.6 %collective-permute-start.8 = (bf16[560,512]{1,0:T(8,128)(2,1)S(1)}, bf16[560,512]{1,0:T(8,128)(2,1)S(1)}, u32[]{:S(2)}, u32[]{:S(2)}) collective-permute-start(bf16[560,512]{1,0:T(8,128)(2,1)S(1)} %slice.8), channel_id=1, source_target_pairs={{0,4},{1,5},{2,6},{3,7},{4,0},{5,1},{6,2},{7,3},{8,12},{9,13},{10,... | collective-permute-start | bytes 1720328 | tf_op jit(solution)/shard_map/ppermute | solution.py:285
  31.9 2.7 %collective-permute-done.6.refs_8_ = bf16[272,1024]{1,0:T(8,128)(2,1)S(1)} collective-permute-done((bf16[272,1024]{1,0:T(8,128)(2,1)S(1)}, bf16[272,1024]{1,0:T(8,128)(2,1)S(1)}, u32[]{:S(2)}, u32[]{:S(2)}) %collective-permute-start.6) | collective-permute-done | bytes 557088 | tf_op jit(solution)/shard_map/ppermute | solution.py:285
  34.6 0.5 collective-permute-start.9
  35.2 1.1 %collective-permute-start.7 = (bf16[272,1024]{1,0:T(8,128)(2,1)S(1)}, bf16[272,1024]{1,0:T(8,128)(2,1)S(1)}, u32[]{:S(2)}, u32[]{:S(2)}) collective-permute-start(bf16[272,1024]{1,0:T(8,128)(2,1)S(1)} %collective-permute-done.6.refs_8_), channel_id=1, source_target_pairs={{0,8},{1,9},{2,10},{3,11},{4,12},{5,13},{6,14},{7,15},{8,0},{9,1},... | collective-permute-start | bytes 1671176 | tf_op jit(solution)/shard_map/ppermute | solution.py:285
  36.2 7.5 %early.1 = (bf16[1536,128]{1,0:T(8,128)(2,1)S(1)}, bf16[1536,128]{1,0:T(8,128)(2,1)S(1)}, f32[1536,1024]{1,0:T(8,128)S(1)}, f32[256,1024]{1,0:T(8,128)S(1)}, bf1...) custom-call(bf16[2,512,512]{2,1,0:T(8,128)(2,1)S(1)} %pad_maximum_fu, ...), custom_call_target="tpu_custom_call" | custom-call | flops 786432 | bytes 1536 | tf_op jit(solution)/shard_map/early/pallas_call | solution.py:338
  43.7 5.3 %collective-permute-done.7.refs_6_.w_three = bf16[272,1024]{1,0:T(8,128)(2,1)S(1)} collective-permute-done((bf16[272,1024]{1,0:T(8,128)(2,1)S(1)}, bf16[272,1024]{1,0:T(8,128)(2,1)S(1)}, u32[]{:S(2)}, u32[]{:S(2)}) %collective-permute-start.7) | collective-permute-done | bytes 557088 | tf_op jit(solution)/shard_map/ppermute | solution.py:285
  49.1 4.1 %output.1 = (bf16[1536,512]{1,0:T(8,128)(2,1)S(1)}, bf16[1536,512]{1,0:T(8,128)(2,1)S(1)}, f32[1536,128]{1,0:T(8,128)S(1)}, bf16[512,1024]{1,0:T(8,128)(2,1)S(1)...) custom-call(bf16[1536,128]{1,0:T(8,128)(2,1)S(1)} %get-tuple-element.49.refs_0_, ...), custom_call_target="tpu_custom_call" | custom-call | flops 786432 | bytes 1536 | tf_op jit(solution)/shard_map/output/pallas_call | solution.py:365
  53.2 0.5 collective-permute-start.13
  53.8 2.3 %gradient.1.refs_4_ = f32[256,1024]{1,0:T(8,128)S(1)} custom-call(bf16[1536,128]{1,0:T(8,128)(2,1)S(1)} %get-tuple-element.56.dpre_two, bf16[1536,1024]{1,0:T(8,128)(2,1)S(1)} %get-tuple-element.50.refs_1_.tok, bf16[1536,1024]{1,0:T(8,128)(2,1)S(1)} %get-tuple-element.57.cot, f32[1536,128]{1,0:T(8,128)S(1)} %get-tuple-element.61.slope, ...), custom_call_target="tpu_custom_call" | custom-call | flops 10000000000 | bytes 1536 | tf_op jit(solution)/shard_map/gradient/pallas_call | solution.py:386
  56.1 0.5 collective-permute-done.10.other_ref
  56.6 0.4 pair_sum.1
  57.0 1.6 %collective-permute-start.11 = (bf16[528,512]{1,0:T(8,128)(2,1)S(1)}, bf16[528,512]{1,0:T(8,128)(2,1)S(1)}, u32[]{:S(2)}, u32[]{:S(2)}) collective-permute-start(bf16[528,512]{1,0:T(8,128)(2,1)S(1)} %get-tuple-element.66), channel_id=1, source_target_pairs={{0,2},{1,3},{2,0},{3,1},{4,6},{5,7},{6,4},{7,5},{8,10},{9,11},{10,... | collective-permute-start | bytes 1622024 | tf_op jit(solution)/shard_map/ppermute | solution.py:285
  58.6 0.5 collective-permute-start.12
  59.1 3.5 %diagonal.1 = (bf16[512,512]{1,0:T(8,128)(2,1)S(1)}, bf16[512,512]{1,0:T(8,128)(2,1)S(1)}, bf16[128,1024]{1,0:T(8,128)(2,1)S(1)}, bf16[128,1024]{1,0:T(8,128)(2,...) custom-call(bf16[512,1024]{1,0:T(8,128)(2,1)S(1)} %get-tuple-element.68.refs_0_, ...), custom_call_target="tpu_custom_call" | custom-call | flops 1000000 | bytes 512 | tf_op jit(solution)/shard_map/diagonal/pallas_call | solution.py:410
  62.7 1.0 %collective-permute-start.18 = (bf16[128,1024]{1,0:T(8,128)(2,1)S(1)}, bf16[128,1024]{1,0:T(8,128)(2,1)S(1)}, u32[]{:S(2)}, u32[]{:S(2)}) collective-permute-start(bf16[128,1024]{1,0:T(8,128)(2,1)S(1)} %get-tuple-element.81), channel_id=1, source_target_pairs={{0,8},{1,9},{2,10},{3,11},{4,12},{5,13},{6,14},{7,15},{8,0},{9,1},... | collective-permute-start | bytes 786440 | tf_op jit(solution)/shard_map/ppermute | solution.py:285
  63.7 1.1 %collective-permute-start.17 = (bf16[128,1024]{1,0:T(8,128)(2,1)S(1)}, bf16[128,1024]{1,0:T(8,128)(2,1)S(1)}, u32[]{:S(2)}, u32[]{:S(2)}) collective-permute-start(bf16[128,1024]{1,0:T(8,128)(2,1)S(1)} %get-tuple-element.78), channel_id=1, source_target_pairs={{0,8},{1,9},{2,10},{3,11},{4,12},{5,13},{6,14},{7,15},{8,0},{9,1},... | collective-permute-start | bytes 786440 | tf_op jit(solution)/shard_map/ppermute | solution.py:285
  64.9 1.5 %collective-permute-start.16 = (bf16[512,512]{1,0:T(8,128)(2,1)S(1)}, bf16[512,512]{1,0:T(8,128)(2,1)S(1)}, u32[]{:S(2)}, u32[]{:S(2)}) collective-permute-start(bf16[512,512]{1,0:T(8,128)(2,1)S(1)} %pair_sum_diagonal.1), channel_id=1, source_target_pairs={{0,6},{1,7},{2,4},{3,5},{4,2},{5,3},{6,0},{7,1},{8,14},{9,15},{10,... | collective-permute-start | bytes 1572872 | tf_op jit(solution)/shard_map/ppermute | solution.py:285
  66.5 5.4 %collective-permute-done.18.other_ref = bf16[128,1024]{1,0:T(8,128)(2,1)S(1)} collective-permute-done((bf16[128,1024]{1,0:T(8,128)(2,1)S(1)}, bf16[128,1024]{1,0:T(8,128)(2,1)S(1)}, u32[]{:S(2)}, u32[]{:S(2)}) %collective-permute-start.18) | collective-permute-done | bytes 262176 | tf_op jit(solution)/shard_map/ppermute | solution.py:285
  71.9 2.7 %collective-permute-start.19 = (bf16[128,1024]{1,0:T(8,128)(2,1)S(1)}, bf16[128,1024]{1,0:T(8,128)(2,1)S(1)}, u32[]{:S(2)}, u32[]{:S(2)}) collective-permute-start(bf16[128,1024]{1,0:T(8,128)(2,1)S(1)} %line_sum.1), channel_id=1, source_target_pairs={{0,16},{1,17},{2,18},{3,19},{4,20},{5,21},{6,22},{7,23},{8,24},{9,... | collective-permute-start | bytes 786440 | tf_op jit(solution)/shard_map/ppermute | solution.py:285
  74.6 9.3 %collective-permute-done.12.y_ref = bf16[528,512]{1,0:T(8,128)(2,1)S(1)} collective-permute-done((bf16[528,512]{1,0:T(8,128)(2,1)S(1)}, bf16[528,512]{1,0:T(8,128)(2,1)S(1)}, u32[]{:S(2)}, u32[]{:S(2)}) %collective-permute-start.12) | collective-permute-done | bytes 540704 | tf_op jit(solution)/shard_map/ppermute | solution.py:285
  83.9 0.2 plane_sum.1
  84.1 1.9 %collective-permute-done.19 = bf16[128,1024]{1,0:T(8,128)(2,1)S(1)} collective-permute-done((bf16[128,1024]{1,0:T(8,128)(2,1)S(1)}, bf16[128,1024]{1,0:T(8,128)(2,1)S(1)}, u32[]{:S(2)}, u32[]{:S(2)}) %collective-permute-start.19) | collective-permute-done | bytes 262176 | tf_op jit(solution)/shard_map/ppermute | solution.py:285
  86.0 0.9 %add_multiply_fusion = f32[128,1024]{1,0:T(8,128)} fusion(bf16[128,1024]{1,0:T(8,128)(2,1)S(1)} %collective-permute-done.19, bf16[128,1024]{1,0:T(8,128)(2,1)S(1)} %collective-permute-done.17, bf16[128,1024]{1,0:T(8,128)(2,1)S(1)} %get-tuple-element.77), kind=kLoop, calls=%fused_computation.5 | loop fusion | flops 786432 | bytes 1310720 | tf_op jit(solution)/shard_map/mul | solution.py:469
  86.9 1.0 %add_convert_fusion = bf16[512,512]{1,0:T(8,128)(2,1)} fusion(f32[512,512]{1,0:T(8,128)S(1)} %plane_sum.1, bf16[512,512]{1,0:T(8,128)(2,1)S(1)} %collective-permute-done.16), kind=kLoop, calls=%fused_computation.3 | loop fusion | flops 786432 | bytes 2097152 | tf_op jit(solution)/shard_map/convert_element_type | solution.py:468
  (26 shorter events, 0.8 us)
Async XLA Ops:
  0.6 1.2 %copy-start.1 = (bf16[512,512]{1,0:T(8,128)(2,1)S(1)}, bf16[512,512]{1,0:T(8,128)(2,1)}, u32[]{:S(2)}) copy-start(bf16[512,512]{1,0:T(8,128)(2,1)} %param.5) | copy-start | bytes 1572868
  0.6 1.4 %copy-start = (bf16[512,512]{1,0:T(8,128)(2,1)S(1)}, bf16[512,512]{1,0:T(8,128)(2,1)}, u32[]{:S(2)}) copy-start(bf16[512,512]{1,0:T(8,128)(2,1)} %param.6) | copy-start | bytes 1572868
  2.1 26.2 %collective-permute-start = (bf16[2,512,512]{2,1,0:T(8,128)(2,1)S(1)}, bf16[2,512,512]{2,1,0:T(8,128)(2,1)S(1)}, u32[]{:S(2)}, u32[]{:S(2)}) collective-permute-start(bf16[2,512,512]{2,1,0:T(8,128)(2,1)S(1)} %pad_maximum_fusion.refs_0_), channel_id=1, source_target_pairs={{0,2},{1,3},{2,0},{3,1},{4,6},{5,7},{6,4},{7,5},{8,10},{9,11},{10,... | collective-permute-start | bytes 3145736 | tf_op jit(solution)/shard_map/ppermute | solution.py:285
  5.1 24.6 %collective-permute-start.1 = (bf16[2,512,512]{2,1,0:T(8,128)(2,1)S(1)}, bf16[2,512,512]{2,1,0:T(8,128)(2,1)S(1)}, u32[]{:S(2)}, u32[]{:S(2)}) collective-permute-start(bf16[2,512,512]{2,1,0:T(8,128)(2,1)S(1)} %pad_maximum_fusion.refs_0_), channel_id=1, source_target_pairs={{0,4},{1,5},{2,6},{3,7},{4,0},{5,1},{6,2},{7,3},{8,12},{9,13},{10,... | collective-permute-start | bytes 3145736 | tf_op jit(solution)/shard_map/ppermute | solution.py:285
  6.6 23.1 %collective-permute-start.2 = (bf16[2,512,512]{2,1,0:T(8,128)(2,1)S(1)}, bf16[2,512,512]{2,1,0:T(8,128)(2,1)S(1)}, u32[]{:S(2)}, u32[]{:S(2)}) collective-permute-start(bf16[2,512,512]{2,1,0:T(8,128)(2,1)S(1)} %pad_maximum_fusion.refs_0_), channel_id=1, source_target_pairs={{0,1},{1,0},{2,3},{3,2},{4,5},{5,4},{6,7},{7,6},{8,9},{9,8},{10,11... | collective-permute-start | bytes 3145736 | tf_op jit(solution)/shard_map/ppermute | solution.py:285
  6.6 28.0 %collective-permute-start.6 = (bf16[272,1024]{1,0:T(8,128)(2,1)S(1)}, bf16[272,1024]{1,0:T(8,128)(2,1)S(1)}, u32[]{:S(2)}, u32[]{:S(2)}) collective-permute-start(bf16[272,1024]{1,0:T(8,128)(2,1)S(1)} %fusion.1.refs_6_), channel_id=1, source_target_pairs={{0,16},{1,17},{2,18},{3,19},{4,20},{5,21},{6,22},{7,23},{8,24},{9,... | collective-permute-start | bytes 1671176 | tf_op jit(solution)/shard_map/ppermute | solution.py:285
  9.2 25.9 %collective-permute-start.5 = (bf16[272,1024]{1,0:T(8,128)(2,1)S(1)}, bf16[272,1024]{1,0:T(8,128)(2,1)S(1)}, u32[]{:S(2)}, u32[]{:S(2)}) collective-permute-start(bf16[272,1024]{1,0:T(8,128)(2,1)S(1)} %fusion.1.refs_6_), channel_id=1, source_target_pairs={{0,8},{1,9},{2,10},{3,11},{4,12},{5,13},{6,14},{7,15},{8,0},{9,1},... | collective-permute-start | bytes 1671176 | tf_op jit(solution)/shard_map/ppermute | solution.py:285
  29.7 6.5 %collective-permute-start.3 = (bf16[2,512,512]{2,1,0:T(8,128)(2,1)S(1)}, bf16[2,512,512]{2,1,0:T(8,128)(2,1)S(1)}, u32[]{:S(2)}, u32[]{:S(2)}) collective-permute-start(bf16[2,512,512]{2,1,0:T(8,128)(2,1)S(1)} %collective-permute-done.refs_2_), channel_id=1, source_target_pairs={{0,1},{1,0},{2,3},{3,2},{4,5},{5,4},{6,7},{7,6},{8,9},{9,8},{10,11... | collective-permute-start | bytes 3145736 | tf_op jit(solution)/shard_map/ppermute | solution.py:285
  29.7 6.5 %collective-permute-start.4 = (bf16[2,512,512]{2,1,0:T(8,128)(2,1)S(1)}, bf16[2,512,512]{2,1,0:T(8,128)(2,1)S(1)}, u32[]{:S(2)}, u32[]{:S(2)}) collective-permute-start(bf16[2,512,512]{2,1,0:T(8,128)(2,1)S(1)} %collective-permute-done.1.refs_4_), channel_id=1, source_target_pairs={{0,1},{1,0},{2,3},{3,2},{4,5},{5,4},{6,7},{7,6},{8,9},{9,8},{10,11... | collective-permute-start | bytes 3145736 | tf_op jit(solution)/shard_map/ppermute | solution.py:285
  30.3 22.8 %collective-permute-start.8 = (bf16[560,512]{1,0:T(8,128)(2,1)S(1)}, bf16[560,512]{1,0:T(8,128)(2,1)S(1)}, u32[]{:S(2)}, u32[]{:S(2)}) collective-permute-start(bf16[560,512]{1,0:T(8,128)(2,1)S(1)} %slice.8), channel_id=1, source_target_pairs={{0,4},{1,5},{2,6},{3,7},{4,0},{5,1},{6,2},{7,3},{8,12},{9,13},{10,... | collective-permute-start | bytes 1720328 | tf_op jit(solution)/shard_map/ppermute | solution.py:285
  34.6 18.5 %collective-permute-start.9 = (bf16[560,512]{1,0:T(8,128)(2,1)S(1)}, bf16[560,512]{1,0:T(8,128)(2,1)S(1)}, u32[]{:S(2)}, u32[]{:S(2)}) collective-permute-start(bf16[560,512]{1,0:T(8,128)(2,1)S(1)} %slice.9), channel_id=1, source_target_pairs={{0,2},{1,3},{2,0},{3,1},{4,6},{5,7},{6,4},{7,5},{8,10},{9,11},{10,... | collective-permute-start | bytes 1720328 | tf_op jit(solution)/shard_map/ppermute | solution.py:285
  35.2 13.9 %collective-permute-start.7 = (bf16[272,1024]{1,0:T(8,128)(2,1)S(1)}, bf16[272,1024]{1,0:T(8,128)(2,1)S(1)}, u32[]{:S(2)}, u32[]{:S(2)}) collective-permute-start(bf16[272,1024]{1,0:T(8,128)(2,1)S(1)} %collective-permute-done.6.refs_8_), channel_id=1, source_target_pairs={{0,8},{1,9},{2,10},{3,11},{4,12},{5,13},{6,14},{7,15},{8,0},{9,1},... | collective-permute-start | bytes 1671176 | tf_op jit(solution)/shard_map/ppermute | solution.py:285
  53.1 3.5 %collective-permute-start.10 = (bf16[1536,512]{1,0:T(8,128)(2,1)S(1)}, bf16[1536,512]{1,0:T(8,128)(2,1)S(1)}, u32[]{:S(2)}, u32[]{:S(2)}) collective-permute-start(bf16[1536,512]{1,0:T(8,128)(2,1)S(1)} %get-tuple-element.63), channel_id=1, source_target_pairs={{0,1},{1,0},{2,3},{3,2},{4,5},{5,4},{6,7},{7,6},{8,9},{9,8},{10,11... | collective-permute-start | bytes 4718600 | tf_op jit(solution)/shard_map/ppermute | solution.py:285
  53.2 5.9 %collective-permute-start.13 = (bf16[560,512]{1,0:T(8,128)(2,1)S(1)}, bf16[560,512]{1,0:T(8,128)(2,1)S(1)}, u32[]{:S(2)}, u32[]{:S(2)}) collective-permute-start(bf16[560,512]{1,0:T(8,128)(2,1)S(1)} %collective-permute-done.8.refs_5_), channel_id=1, source_target_pairs={{0,1},{1,0},{2,3},{3,2},{4,5},{5,4},{6,7},{7,6},{8,9},{9,8},{10,11... | collective-permute-start | bytes 1720328 | tf_op jit(solution)/shard_map/ppermute | solution.py:285
  53.7 5.4 %collective-permute-start.14 = (bf16[560,512]{1,0:T(8,128)(2,1)S(1)}, bf16[560,512]{1,0:T(8,128)(2,1)S(1)}, u32[]{:S(2)}, u32[]{:S(2)}) collective-permute-start(bf16[560,512]{1,0:T(8,128)(2,1)S(1)} %collective-permute-done.9.refs_7_), channel_id=1, source_target_pairs={{0,1},{1,0},{2,3},{3,2},{4,5},{5,4},{6,7},{7,6},{8,9},{9,8},{10,11... | collective-permute-start | bytes 1720328 | tf_op jit(solution)/shard_map/ppermute | solution.py:285
  57.0 17.6 %collective-permute-start.11 = (bf16[528,512]{1,0:T(8,128)(2,1)S(1)}, bf16[528,512]{1,0:T(8,128)(2,1)S(1)}, u32[]{:S(2)}, u32[]{:S(2)}) collective-permute-start(bf16[528,512]{1,0:T(8,128)(2,1)S(1)} %get-tuple-element.66), channel_id=1, source_target_pairs={{0,2},{1,3},{2,0},{3,1},{4,6},{5,7},{6,4},{7,5},{8,10},{9,11},{10,... | collective-permute-start | bytes 1622024 | tf_op jit(solution)/shard_map/ppermute | solution.py:285
  58.6 25.3 %collective-permute-start.12 = (bf16[528,512]{1,0:T(8,128)(2,1)S(1)}, bf16[528,512]{1,0:T(8,128)(2,1)S(1)}, u32[]{:S(2)}, u32[]{:S(2)}) collective-permute-start(bf16[528,512]{1,0:T(8,128)(2,1)S(1)} %get-tuple-element.67), channel_id=1, source_target_pairs={{0,4},{1,5},{2,6},{3,7},{4,0},{5,1},{6,2},{7,3},{8,12},{9,13},{10,... | collective-permute-start | bytes 1622024 | tf_op jit(solution)/shard_map/ppermute | solution.py:285
  62.6 2.2 %collective-permute-start.15 = (bf16[512,512]{1,0:T(8,128)(2,1)S(1)}, bf16[512,512]{1,0:T(8,128)(2,1)S(1)}, u32[]{:S(2)}, u32[]{:S(2)}) collective-permute-start(bf16[512,512]{1,0:T(8,128)(2,1)S(1)} %get-tuple-element.76), channel_id=1, source_target_pairs={{0,1},{1,0},{2,3},{3,2},{4,5},{5,4},{6,7},{7,6},{8,9},{9,8},{10,11... | collective-permute-start | bytes 1572872 | tf_op jit(solution)/shard_map/ppermute | solution.py:285
  62.7 9.2 %collective-permute-start.18 = (bf16[128,1024]{1,0:T(8,128)(2,1)S(1)}, bf16[128,1024]{1,0:T(8,128)(2,1)S(1)}, u32[]{:S(2)}, u32[]{:S(2)}) collective-permute-start(bf16[128,1024]{1,0:T(8,128)(2,1)S(1)} %get-tuple-element.81), channel_id=1, source_target_pairs={{0,8},{1,9},{2,10},{3,11},{4,12},{5,13},{6,14},{7,15},{8,0},{9,1},... | collective-permute-start | bytes 786440 | tf_op jit(solution)/shard_map/ppermute | solution.py:285
  63.7 20.3 %collective-permute-start.17 = (bf16[128,1024]{1,0:T(8,128)(2,1)S(1)}, bf16[128,1024]{1,0:T(8,128)(2,1)S(1)}, u32[]{:S(2)}, u32[]{:S(2)}) collective-permute-start(bf16[128,1024]{1,0:T(8,128)(2,1)S(1)} %get-tuple-element.78), channel_id=1, source_target_pairs={{0,8},{1,9},{2,10},{3,11},{4,12},{5,13},{6,14},{7,15},{8,0},{9,1},... | collective-permute-start | bytes 786440 | tf_op jit(solution)/shard_map/ppermute | solution.py:285
  64.9 22.0 %collective-permute-start.16 = (bf16[512,512]{1,0:T(8,128)(2,1)S(1)}, bf16[512,512]{1,0:T(8,128)(2,1)S(1)}, u32[]{:S(2)}, u32[]{:S(2)}) collective-permute-start(bf16[512,512]{1,0:T(8,128)(2,1)S(1)} %pair_sum_diagonal.1), channel_id=1, source_target_pairs={{0,6},{1,7},{2,4},{3,5},{4,2},{5,3},{6,0},{7,1},{8,14},{9,15},{10,... | collective-permute-start | bytes 1572872 | tf_op jit(solution)/shard_map/ppermute | solution.py:285
  71.9 14.0 %collective-permute-start.19 = (bf16[128,1024]{1,0:T(8,128)(2,1)S(1)}, bf16[128,1024]{1,0:T(8,128)(2,1)S(1)}, u32[]{:S(2)}, u32[]{:S(2)}) collective-permute-start(bf16[128,1024]{1,0:T(8,128)(2,1)S(1)} %line_sum.1), channel_id=1, source_target_pairs={{0,16},{1,17},{2,18},{3,19},{4,20},{5,21},{6,22},{7,23},{8,24},{9,... | collective-permute-start | bytes 786440 | tf_op jit(solution)/shard_map/ppermute | solution.py:285

commit v10 on v8

--- a/solution.py
+++ b/solution.py
@@ -14,7 +14,11 @@
 CONTRACT_FIRST = (((0,), (0,)), ((), ()))
 VMEM_LIMIT = 28 * 1024 * 1024
 PLANE_COST = 10**10
+GRADIENT_COST = 10**11
+DIAGONAL_COST = 10**6
+OUTPUT_COST = 10**6
 EXTRA = 48
+HAND_ON_COST = 2 * 10**10
 
 
 def gelu_parts(value):
@@ -154,84 +158,88 @@
     grad_ref[...] = dot_first(dpre[...], tok[...])
 
 
+def diagonal_kernel(owned, *refs):
+    w_in, w_out, bias = refs[:3]
+    act_ref, slope_ref, mixed_ref, tok, tok_sem = refs[5:]
+    core = lax.axis_index("core")
+    rows = tok.shape[0]
+    two = 2 * owned
+    load = side_by_side(core, (refs[3].at[pl.ds(0, rows)], refs[4]), tok, 0, tok_sem)
+    run(load, "start")
+    run(load, "wait")
+    step = rows // 2
+
+    @pl.loop(0, 2)
+    def _(sub):
+        spot = pl.ds(pl.multiple_of(sub * step, step), step)
+        value, slope = activate(tok[spot, :], w_in[...], bias[0:1, :])
+        slope_ref[spot, :] = slope
+        act = value.astype(jnp.bfloat16)
+        act_ref[spot, :] = act[:, two:]
+        mixed_ref[spot, :] = jnp.dot(
+            act[:, :two], w_out[:two, :], preferred_element_type=jnp.float32
+        )
+
+
 def output_kernel(owned, *refs):
-    act_two, tok, early_mixed, w_in, w_out, bias, w_three = refs[:7]
-    mine_ref, other_ref, slope_ref, w_in_all, w_out_all, bias_all = refs[7:13]
-    w_last, sem = refs[13:]
+    act_two, tok, early_mixed, act_diag, tok_diag, mixed_diag, w_out, w_three = refs[:8]
+    mine_ref, other_ref, slope_ref, w_last = refs[8:]
     core = lax.axis_index("core")
     feats = mine_ref.shape[1]
-    two, three = 2 * owned, 3 * owned
-    first, last = pl.ds(0, three), pl.ds(three, owned)
-    copies = [
-        pltpu.make_async_copy(w_in, w_in_all.at[first], sem.at[0]),
-        pltpu.make_async_copy(w_three.at[pl.ds(0, owned)], w_in_all.at[last], sem.at[1]),
-        pltpu.make_async_copy(w_out, w_out_all.at[first], sem.at[2]),
-        pltpu.make_async_copy(w_three.at[pl.ds(owned, owned)], w_out_all.at[last], sem.at[3]),
-    ]
-    run(copies, "start")
-    bias_last = w_three[two : two + 16, :owned]
-    bias_all[:, :three] = bias[...]
-    bias_all[:, three:] = bias_last
+    two = 2 * owned
     w_last[:owned, :] = w_out[two:, :]
     w_last[owned:, :] = w_three[owned:two, :]
-    step = tok.shape[0] // 6
-
-    @pl.loop(0, 6)
-    def _(sub):
-        spot = pl.ds(pl.multiple_of(sub * step, step), step)
-        value, slope = activate(tok[spot, :], w_three[:owned, :], bias_last[0:1, :])
+    step = tok_diag.shape[0]
+
+    def rows_of(here, spot, act_part, tok_part, mixed_part):
+        value, slope = activate(
+            tok_part[here, :], w_three[:owned, :], w_three[two : two + 16, :owned][0:1, :]
+        )
         slope_ref[spot, :] = slope
-        act = jnp.concatenate([act_two[spot, :], value.astype(jnp.bfloat16)], axis=1)
+        act = jnp.concatenate([act_part[here, :], value.astype(jnp.bfloat16)], axis=1)
         for shift, ref in enumerate((mine_ref, other_ref)):
             half = half_columns(core, shift, feats)
             ref[spot, :] = (
-                early_mixed[spot, half]
+                mixed_part[here, half]
                 + jnp.dot(act, w_last[:, half], preferred_element_type=jnp.float32)
             ).astype(jnp.bfloat16)
 
-    run(copies, "wait")
-
-
-def diagonal_kernel(*refs):
-    w_in, w_out, bias = refs[:3]
-    mine_ref, other_ref, slope_ref, tok_diag, tok_sem = refs[5:]
+    @pl.loop(0, NEAR - 1)
+    def _(block):
+        spot = pl.ds(pl.multiple_of(block * step, step), step)
+        rows_of(spot, spot, act_two, tok, early_mixed)
+
+    rows_of(
+        slice(None), pl.ds((NEAR - 1) * step, step), act_diag, tok_diag, mixed_diag
+    )
+
+
+def gradient_kernel(owned, *refs):
+    dpre_two, tok, cot, slope, w_three, w_out, grad_first, tok_diag, slope_diag = refs[:9]
+    own_ref, one_ref, two_ref, three_ref, cot_diag, dpre, dpre_diag, cot_sem = refs[11:]
     core = lax.axis_index("core")
-    rows, feats = mine_ref.shape
-    diag_refs = [ref.at[pl.ds(0, rows)] for ref in refs[3:5]]
-    load = side_by_side(core, diag_refs, tok_diag, 0, tok_sem)
+    step = tok_diag.shape[0]
+    two, three = 2 * owned, 3 * owned
+    pair = (refs[9].at[pl.ds(EXTRA, step)], refs[10])
+    load = side_by_side(core, pair, cot_diag, 0, cot_sem)
     run(load, "start")
+
+    @pl.loop(0, NEAR - 1)
+    def _(block):
+        spot = pl.ds(pl.multiple_of(block * step, step), step)
+        dact = dot_last(cot[spot, :], w_three[owned:two, :])
+        last = (dact * slope[spot, :]).astype(jnp.bfloat16)
+        dpre[spot, :] = jnp.concatenate([dpre_two[spot, :], last], axis=1)
+
     run(load, "wait")
-    step = rows // 2
-
-    @pl.loop(0, 2)
-    def _(sub):
-        spot = pl.ds(pl.multiple_of(sub * step, step), step)
-        value, slope = activate(tok_diag[spot, :], w_in[...], bias[0:1, :])
-        act = value.astype(jnp.bfloat16)
-        slope_ref[spot, :] = slope
-        for shift, ref in enumerate((mine_ref, other_ref)):
-            ref[spot, :] = jnp.dot(
-                act, w_out[:, half_columns(core, shift, feats)], preferred_element_type=jnp.float32
-            ).astype(jnp.bfloat16)
-
-
-def gradient_kernel(owned, *refs):
-    dpre_two, tok, cot, early_grad, tok_diag, slope, slope_diag, w_out = refs[:8]
-    own_ref, one_ref, two_ref, three_ref, cot_diag, dpre_diag, cot_sem = refs[10:]
-    diag_refs = [ref.at[pl.ds(EXTRA, cot_diag.shape[0])] for ref in refs[8:10]]
-    core = lax.axis_index("core")
-    two = 2 * owned
-    load = side_by_side(core, diag_refs, cot_diag, 0, cot_sem)
-    run(load, "start")
-    dact = dot_last(cot[...], w_out[3 * owned :, :])
-    last = (dact * slope[...]).astype(jnp.bfloat16)
-    grad = dot_first(jnp.concatenate([dpre_two[...], last], axis=1), tok[...])
-    run(load, "wait")
-    dpre_diag[...] = (dot_last(cot_diag[...], w_out[...]) * slope_diag[...]).astype(jnp.bfloat16)
-    grad = grad + dot_first(dpre_diag[:, two:], tok_diag[...])
+    dact = dot_last(cot_diag[...], w_out[...])
+    dpre_diag[:, :three] = (dact * slope_diag[...]).astype(jnp.bfloat16)
+    dact = dot_last(cot_diag[...], w_three[owned:two, :])
+    dpre_diag[:, three:] = (dact * slope[(NEAR - 1) * step :, :]).astype(jnp.bfloat16)
+    grad = dot_first(dpre[...], tok[...]) + dot_first(dpre_diag[:, two:], tok_diag[...])
     two_ref[...] = grad[:owned].astype(jnp.bfloat16)
     three_ref[...] = grad[owned:].astype(jnp.bfloat16)
-    grad = early_grad[...] + dot_first(dpre_diag[:, :two], tok_diag[...])
+    grad = grad_first[...] + dot_first(dpre_diag[:, :two], tok_diag[...])
     own_ref[...] = grad[:owned].astype(jnp.bfloat16)
     one_ref[...] = grad[owned:].astype(jnp.bfloat16)
 
@@ -244,12 +252,17 @@
         ).astype(jnp.bfloat16)
 
 
-def plane_kernel(own_ref, x_ref, y_ref, out_ref):
+def hand_on_kernel(in_ref, out_ref):
+    out_ref[...] = in_ref[...]
+
+
+def plane_kernel(own_ref, x_ref, y_ref, diag_ref, out_ref):
     out_ref[...] = (
         own_ref[...].astype(jnp.float32)
         + x_ref[...].astype(jnp.float32)
         + y_ref[...].astype(jnp.float32)
-    )
+        + diag_ref[...].astype(jnp.float32)
+    ).astype(jnp.bfloat16)
 
 
 def vmem(count):
@@ -320,11 +333,20 @@
     w_two, w_one = to_far(own_w, 2), to_far(own_w, 1)
     from_x, from_y = to_x(own), to_y(own)
     own_other = to_core(own)
-    from_x, from_y, own_other, w_one = barrier((from_x, from_y, own_other, w_one))
+    from_x, from_y, own_other = barrier((from_x, from_y, own_other))
     tok_diag = to_y(from_x.reshape(2 * rows, feats)[: rows + EXTRA])
     cot_diag = to_x(from_y.reshape(2 * rows, feats)[rows - EXTRA :])
     x_other, y_other = to_core(from_x), to_core(from_y)
-    w_three = to_far(w_two, 1)
+    w_again = pl.pallas_call(
+        hand_on_kernel,
+        out_shape=bf16(*w_two.shape),
+        in_specs=vmem(1),
+        out_specs=pl.BlockSpec(memory_space=pltpu.VMEM),
+        compiler_params=params,
+        cost_estimate=cost(HAND_ON_COST, rows),
+        name="hand_on",
+    )(w_two)
+    w_three = to_far(w_again, 1)
     act_two, dpre_two, mixed_terms, grad_terms, tok, cot, w_in_three, w_out_three, bias = (
         pl.pallas_call(
             functools.partial(early_kernel, owned),
@@ -352,87 +374,81 @@
             name="early",
         )(own, own_other, from_x, x_other, from_y, y_other, own_w, w_one, w_two)
     )
-    tok_diag, cot_diag, act_two = barrier((tok_diag, cot_diag, act_two))
-    tok_diag_other, cot_diag_other = to_core(tok_diag), to_core(cot_diag)
-
-    mine, other, slope, w_in_all, w_out_all, bias = pl.pallas_call(
-        functools.partial(output_kernel, owned),
+
+    tok_diag, act_two = barrier((tok_diag, act_two))
+    tok_diag_other = to_core(tok_diag[:rows])
+    act_diag, slope_diag, mixed_terms_diag, tok_last = pl.pallas_call(
+        functools.partial(diagonal_kernel, owned),
         out_shape=(
-            bf16(early_rows, feats),
-            bf16(early_rows, feats),
-            f32(early_rows, owned),
-            bf16(units, width),
-            bf16(units, width),
-            bf16(16, units),
+            bf16(rows, owned),
+            f32(rows, 3 * owned),
+            f32(rows, width),
+            bf16(rows, width),
         ),
-        in_specs=vmem(7),
-        out_specs=vmem(6),
-        scratch_shapes=[pltpu.VMEM((2 * owned, width), jnp.bfloat16), dma((4,))],
-        compiler_params=params,
-        cost_estimate=cost(8 * early_rows * units * width, 4 * count * width),
-        name="output",
-    )(act_two, tok, mixed_terms, w_in_three, w_out_three, bias, w_three)
-    received = to_core(other)
-
-    tok_diag_other, cot_diag_other, w_in_all = barrier((tok_diag_other, cot_diag_other, w_in_all))
-    mine_diag, other_diag, slope_diag, tok_last = pl.pallas_call(
-        diagonal_kernel,
-        out_shape=(bf16(rows, feats), bf16(rows, feats), f32(rows, units), bf16(rows, width)),
         in_specs=vmem(3) + anywhere(2),
         out_specs=vmem(4),
         scratch_shapes=[dma((2,))],
         compiler_params=params,
-        cost_estimate=cost(48 * rows * units * width, 4 * rows * width),
+        cost_estimate=cost(DIAGONAL_COST, rows),
         name="diagonal",
-    )(w_in_all, w_out_all, bias, tok_diag, tok_diag_other)
-    received_diag = to_core(other_diag)
-
-    mine, slope_diag = barrier((mine, slope_diag))
-    sums = pl.pallas_call(
-        functools.partial(pair_kernel, rows),
-        out_shape=[bf16(rows, feats)] * (NEAR - 1),
-        in_specs=vmem(2),
-        out_specs=vmem(NEAR - 1),
-        compiler_params=params,
-        name="pair_sum",
-    )(mine, received)
-    mixed_x, mixed_y = to_x(sums[1]), to_y(sums[2])
-    grad_terms, mixed_own = barrier((grad_terms, sums[0]))
+    )(w_in_three, w_out_three, bias, tok_diag, tok_diag_other)
+    cot_diag_other = to_core(cot_diag[EXTRA:])
+
+    mine, other, slope = pl.pallas_call(
+        functools.partial(output_kernel, owned),
+        out_shape=(bf16(count, feats), bf16(count, feats), f32(count, owned)),
+        in_specs=vmem(8),
+        out_specs=vmem(3),
+        scratch_shapes=[pltpu.VMEM((2 * owned, width), jnp.bfloat16)],
+        compiler_params=params,
+        cost_estimate=cost(OUTPUT_COST, early_rows),
+        name="output",
+    )(act_two, tok, mixed_terms, act_diag, tok_last, mixed_terms_diag, w_out_three, w_three)
+    received = to_core(other)
 
     grad_own, grad_one, grad_two, grad_three = pl.pallas_call(
         functools.partial(gradient_kernel, owned),
         out_shape=[bf16(owned, width)] * 4,
-        in_specs=vmem(8) + anywhere(2),
+        in_specs=vmem(9) + anywhere(2),
         out_specs=vmem(4),
         scratch_shapes=[
             pltpu.VMEM((rows, width), jnp.bfloat16),
+            pltpu.VMEM((early_rows, 2 * owned), jnp.bfloat16),
             pltpu.VMEM((rows, units), jnp.bfloat16),
             dma((2,)),
         ],
         compiler_params=params,
-        cost_estimate=cost(early_rows * units, early_rows),
+        cost_estimate=cost(GRADIENT_COST, early_rows),
         name="gradient",
     )(
-        dpre_two, tok, cot, grad_terms, tok_last, slope, slope_diag, w_out_all,
+        dpre_two, tok, cot, slope, w_three, w_out_three, grad_terms, tok_last, slope_diag,
         cot_diag, cot_diag_other,
     )
     relayed = to_far(grad_three, 1)
-    from_one = to_far(grad_one, 1)
-
-    mine_diag, grad_own = barrier((mine_diag, grad_own))
-    (sum_diag,) = pl.pallas_call(
+    mine, grad_own = barrier((mine, grad_own))
+    sums = pl.pallas_call(
         functools.partial(pair_kernel, rows),
-        out_shape=[bf16(rows, feats)],
+        out_shape=[bf16(rows, feats)] * NEAR,
+        in_specs=vmem(2),
+        out_specs=vmem(NEAR),
+        compiler_params=params,
+        cost_estimate=cost(rows, rows),
+        name="pair_sum",
+    )(mine, received)
+    mixed_own = sums[0]
+    mixed_x, mixed_y, mixed_diag = to_x(sums[1]), to_y(sums[2]), to_diagonal(sums[3])
+    grad_one, grad_two, _ = barrier((grad_one, grad_two, sums[0]))
+    (line_sum,) = pl.pallas_call(
+        functools.partial(pair_kernel, owned),
+        out_shape=[bf16(owned, width)],
         in_specs=vmem(2),
         out_specs=vmem(1),
         compiler_params=params,
-        name="pair_sum_diagonal",
-    )(mine_diag, received_diag)
-    mixed_diag = to_diagonal(sum_diag)
-    grad_two, _ = barrier((grad_two, sum_diag))
-    from_two = to_far(
-        (grad_two.astype(jnp.float32) + relayed.astype(jnp.float32)).astype(jnp.bfloat16), 2
-    )
+        cost_estimate=cost(rows, rows),
+        name="line_sum",
+    )(grad_two, relayed)
+    from_two = to_far(line_sum, 2)
+    from_one = to_far(grad_one, 1)
     total = (
         grad_own.astype(jnp.float32)
         + from_one.astype(jnp.float32)
@@ -440,14 +456,13 @@
     )
     mixed = pl.pallas_call(
         plane_kernel,
-        out_shape=f32(rows, feats),
-        in_specs=vmem(3),
+        out_shape=bf16(rows, feats),
+        in_specs=vmem(4),
         out_specs=pl.BlockSpec(memory_space=pltpu.VMEM),
         compiler_params=params,
         cost_estimate=cost(PLANE_COST, rows),
         name="plane_sum",
-    )(mixed_own, mixed_x, mixed_y)
-    mixed = (mixed + mixed_diag.astype(jnp.float32)).astype(jnp.bfloat16)
+    )(mixed_own, mixed_x, mixed_y, mixed_diag)
     return (mixed, total * scale)
 
 

time: 89.1 us -> 91.3 us (1.025)
  starting transfers between devices: 18.9 us -> 22.1 us
  waiting for transfers between devices: 45.2 us -> 43.2 us
  Pallas kernels: 20.6 us -> 21.7 us
    ppermute x20 -> x19, starting transfers between devices: 18.9 us -> 22.1 us  [permute(): return lax.ppermute(value, AXES, pairs)]
    ppermute x20 -> x19, waiting for transfers between devices: 45.2 us -> 43.2 us  [permute(): return lax.ppermute(value, AXES, pairs)]
    another operation x1, other arithmetic: 0.1 us -> 1.3 us  [on_device_lines(): own = jnp.stack([tokens, cotangent])]
    convert_element_type x2 -> x0, other arithmetic: 1.02 us -> none  [the longest x1 0.95 us: on_device_lines(): mixed = (mixed + mixed_diag.astype(jnp.float32)).astype(jnp.bfloat16)]
    pallas_call x3 -> x5, Pallas kernels: 7.32 us -> 8.16 us  [the longest x1 5.13 us: on_device_lines(): pl.pallas_call(functools.partial(output_kernel, owned), out_shape=(bf16(c...]
  transfers between devices with their start and end apart: 20 -> 19, of which waited for: 10 -> 9; matrix products, arithmetic and copies ran while one was open for 1% -> 1% of each run, Pallas kernels for 23% -> 23%
where the time goes in v10:
time: 91.3 us; the launch traced here: 91.1 us
  waiting for transfers between devices  43.2 us (47%)
  starting transfers between devices  22.1 us (24%)
  Pallas kernels  21.7 us (24%)
  other arithmetic  3.29 us (4%)
    ppermute x19, waiting for transfers between devices, permute(): return lax.ppermute(value, AXES, pairs)  43.2 us
    ppermute x19, starting transfers between devices, permute(): return lax.ppermute(value, AXES, pairs)  22.1 us
    pallas_call x1, Pallas kernels, on_device_lines(): pl.pallas_call(functools.partial(early_kernel, owned), out_shape=(bf16(ea...  7.46 us
    pallas_call x1, Pallas kernels, on_device_lines(): pl.pallas_call(functools.partial(gradient_kernel, owned), out_shape=[bf16...  5.6 us
    pallas_call x1, Pallas kernels, on_device_lines(): pl.pallas_call(functools.partial(output_kernel, owned), out_shape=(bf16(c...  5.13 us
    pallas_call x1, Pallas kernels, on_device_lines(): pl.pallas_call(functools.partial(diagonal_kernel, owned), out_shape=(bf16...  1.88 us
  transfers between devices with their start and end apart: 19, of which 9 were waited for; matrix products, arithmetic and copies ran while one was open for 1% of the time, Pallas kernels for 23%

profile of v10, /device:TPU:0, one launch (start us, length us, event | category | flops | bytes accessed | tf_op | source)
XLA Modules:
  0.0 91.1 jit_solution(12993200509562333825)
XLA Ops:
  0.6 1.1 %fusion.1.refs_6_ = bf16[272,1024]{1,0:T(8,128)(2,1)S(1)} fusion(bf16[1,128]{1,0:T(2,128)(2,1)} %bitcast.9, bf16[128,1024]{1,0:T(8,128)(2,1)} %param.9, bf16[128,1024]{1,0:T(8,128)(2,1)} %param.7), kind=kLoop, calls=%fused_computation.3 | loop fusion | flops 2228224 | bytes 1081600 | tf_op jit(solution)/shard_map/concatenate | solution.py:330
  1.7 1.3 %pad_maximum_fusion.refs_0_ = bf16[2,512,512]{2,1,0:T(8,128)(2,1)S(1)} fusion(bf16[1,512,512]{2,1,0:T(8,128)(2,1)} %bitcast.7, bf16[1,512,512]{2,1,0:T(8,128)(2,1)} %bitcast.8), kind=kLoop, calls=%fused_computation.2 | loop fusion | flops 524288 | bytes 2097152 | tf_op jit(solution)/shard_map/stack | solution.py:332
  3.0 3.0 %collective-permute-start = (bf16[2,512,512]{2,1,0:T(8,128)(2,1)S(1)}, bf16[2,512,512]{2,1,0:T(8,128)(2,1)S(1)}, u32[]{:S(2)}, u32[]{:S(2)}) collective-permute-start(bf16[2,512,512]{2,1,0:T(8,128)(2,1)S(1)} %pad_maximum_fusion.refs_0_), channel_id=1, source_target_pairs={{0,2},{1,3},{2,0},{3,1},{4,6},{5,7},{6,4},{7,5},{8,10},{9,11},{10,... | collective-permute-start | bytes 3145736 | tf_op jit(solution)/shard_map/ppermute | solution.py:289
  6.0 1.5 %collective-permute-start.1 = (bf16[2,512,512]{2,1,0:T(8,128)(2,1)S(1)}, bf16[2,512,512]{2,1,0:T(8,128)(2,1)S(1)}, u32[]{:S(2)}, u32[]{:S(2)}) collective-permute-start(bf16[2,512,512]{2,1,0:T(8,128)(2,1)S(1)} %pad_maximum_fusion.refs_0_), channel_id=1, source_target_pairs={{0,4},{1,5},{2,6},{3,7},{4,0},{5,1},{6,2},{7,3},{8,12},{9,13},{10,... | collective-permute-start | bytes 3145736 | tf_op jit(solution)/shard_map/ppermute | solution.py:289
  7.5 2.6 %collective-permute-start.7 = (bf16[272,1024]{1,0:T(8,128)(2,1)S(1)}, bf16[272,1024]{1,0:T(8,128)(2,1)S(1)}, u32[]{:S(2)}, u32[]{:S(2)}) collective-permute-start(bf16[272,1024]{1,0:T(8,128)(2,1)S(1)} %fusion.1.refs_6_), channel_id=1, source_target_pairs={{0,16},{1,17},{2,18},{3,19},{4,20},{5,21},{6,22},{7,23},{8,24},{9,... | collective-permute-start | bytes 1671176 | tf_op jit(solution)/shard_map/ppermute | solution.py:289
  10.1 1.6 %collective-permute-start.6 = (bf16[272,1024]{1,0:T(8,128)(2,1)S(1)}, bf16[272,1024]{1,0:T(8,128)(2,1)S(1)}, u32[]{:S(2)}, u32[]{:S(2)}) collective-permute-start(bf16[272,1024]{1,0:T(8,128)(2,1)S(1)} %fusion.1.refs_6_), channel_id=1, source_target_pairs={{0,8},{1,9},{2,10},{3,11},{4,12},{5,13},{6,14},{7,15},{8,0},{9,1},... | collective-permute-start | bytes 1671176 | tf_op jit(solution)/shard_map/ppermute | solution.py:289
  11.7 17.5 %collective-permute-done.refs_2_ = bf16[2,512,512]{2,1,0:T(8,128)(2,1)S(1)} collective-permute-done((bf16[2,512,512]{2,1,0:T(8,128)(2,1)S(1)}, bf16[2,512,512]{2,1,0:T(8,128)(2,1)S(1)}, u32[]{:S(2)}, u32[]{:S(2)}) %collective-permute-start) | collective-permute-done | bytes 1048608 | tf_op jit(solution)/shard_map/ppermute | solution.py:289
  29.2 1.5 %collective-permute-done.1.refs_4_ = bf16[2,512,512]{2,1,0:T(8,128)(2,1)S(1)} collective-permute-done((bf16[2,512,512]{2,1,0:T(8,128)(2,1)S(1)}, bf16[2,512,512]{2,1,0:T(8,128)(2,1)S(1)}, u32[]{:S(2)}, u32[]{:S(2)}) %collective-permute-start.1) | collective-permute-done | bytes 1048608 | tf_op jit(solution)/shard_map/ppermute | solution.py:289
  30.7 0.5 collective-permute-start.5
  31.2 1.6 %collective-permute-start.3 = (bf16[560,512]{1,0:T(8,128)(2,1)S(1)}, bf16[560,512]{1,0:T(8,128)(2,1)S(1)}, u32[]{:S(2)}, u32[]{:S(2)}) collective-permute-start(bf16[560,512]{1,0:T(8,128)(2,1)S(1)} %slice.16), channel_id=1, source_target_pairs={{0,4},{1,5},{2,6},{3,7},{4,0},{5,1},{6,2},{7,3},{8,12},{9,13},{10,... | collective-permute-start | bytes 1720328 | tf_op jit(solution)/shard_map/ppermute | solution.py:289
  32.8 2.7 %collective-permute-done.7.refs_8_.in_ref = bf16[272,1024]{1,0:T(8,128)(2,1)S(1)} collective-permute-done((bf16[272,1024]{1,0:T(8,128)(2,1)S(1)}, bf16[272,1024]{1,0:T(8,128)(2,1)S(1)}, u32[]{:S(2)}, u32[]{:S(2)}) %collective-permute-start.7) | collective-permute-done | bytes 557088 | tf_op jit(solution)/shard_map/ppermute | solution.py:289
  35.5 0.5 collective-permute-start.10
  36.1 1.0 %collective-permute-start.9 = (bf16[272,1024]{1,0:T(8,128)(2,1)S(1)}, bf16[272,1024]{1,0:T(8,128)(2,1)S(1)}, u32[]{:S(2)}, u32[]{:S(2)}) collective-permute-start(bf16[272,1024]{1,0:T(8,128)(2,1)S(1)} %hand_on.1), channel_id=1, source_target_pairs={{0,8},{1,9},{2,10},{3,11},{4,12},{5,13},{6,14},{7,15},{8,0},{9,1},... | collective-permute-start | bytes 1671176 | tf_op jit(solution)/shard_map/ppermute | solution.py:289
  37.2 7.5 %early.1 = (bf16[1536,128]{1,0:T(8,128)(2,1)S(1)}, bf16[1536,128]{1,0:T(8,128)(2,1)S(1)}, f32[1536,1024]{1,0:T(8,128)S(1)}, f32[256,1024]{1,0:T(8,128)S(1)}, bf1...) custom-call(bf16[2,512,512]{2,1,0:T(8,128)(2,1)S(1)} %pad_maximum_fu, ...), custom_call_target="tpu_custom_call" | custom-call | flops 786432 | bytes 1536 | tf_op jit(solution)/shard_map/early/pallas_call | solution.py:351
  44.6 1.5 %collective-permute-done.3.refs_3_ = bf16[560,512]{1,0:T(8,128)(2,1)S(1)} collective-permute-done((bf16[560,512]{1,0:T(8,128)(2,1)S(1)}, bf16[560,512]{1,0:T(8,128)(2,1)S(1)}, u32[]{:S(2)}, u32[]{:S(2)}) %collective-permute-start.3) | collective-permute-done | bytes 573472 | tf_op jit(solution)/shard_map/ppermute | solution.py:289
  46.3 3.8 %collective-permute-done.10.refs_9_ = bf16[560,512]{1,0:T(8,128)(2,1)S(1)} collective-permute-done((bf16[560,512]{1,0:T(8,128)(2,1)S(1)}, bf16[560,512]{1,0:T(8,128)(2,1)S(1)}, u32[]{:S(2)}, u32[]{:S(2)}) %collective-permute-start.10) | collective-permute-done | bytes 573472 | tf_op jit(solution)/shard_map/ppermute | solution.py:289
  50.2 1.9 %diagonal.1 = (bf16[512,128]{1,0:T(8,128)(2,1)S(1)}, f32[512,384]{1,0:T(8,128)S(1)}, f32[512,1024]{1,0:T(8,128)S(1)}, bf16[512,1024]{1,0:T(8,128)(2,1)S(1)}) custom-call(bf16[384,1024]{1,0:T(8,128)(2,1)S(1)} %get-tuple-element.48.refs_0_, bf16[384,1024]{1,0:T(8,128)(2,1)S(1)} %get-tuple-element.49.refs_1_.refs_6_.refs_5_, ...), custom_call_target="tpu_custom_call" | custom-call | flops 1000000 | bytes 512 | tf_op jit(solution)/shard_map/diagonal/pallas_call | solution.py:380
  52.1 5.1 %output.1 = (bf16[2048,512]{1,0:T(8,128)(2,1)S(1)}, bf16[2048,512]{1,0:T(8,128)(2,1)S(1)}, f32[2048,128]{1,0:T(8,128)S(1)}) custom-call(bf16[1536,128]{1,0:T(8,128)(2,1)S(1)} %get-tuple-element.45.refs_0_, bf16[1536,1024]{1,0:T(8,128)(2,1)S(1)} %get-tuple-element.46.refs_1_, f32[1536,1024]{1,0:T(8,128)S(1)} %get-tuple-element.47.refs_2_, ...), custom_call_target="tpu_custom_call" | custom-call | flops 1000000 | bytes 1536 | tf_op jit(solution)/shard_map/output/pallas_call | solution.py:397
  57.2 0.6 collective-permute-start.12
  57.8 5.6 %gradient.1 = (bf16[128,1024]{1,0:T(8,128)(2,1)S(1)}, bf16[128,1024]{1,0:T(8,128)(2,1)S(1)}, bf16[128,1024]{1,0:T(8,128)(2,1)S(1)}, bf16[128,1024]{1,0:T(8,128)(2,1)S(1)}) custom-call(bf16[1536,128]{1,0:T(8,128)(2,1)S(1)} %get-tuple-element.56.refs_0_, bf16[1536,1024]{1,0:T(8,128)(2,1)S(1)} %get-tuple-element.46.refs_1_, ...), custom_call_target="tpu_custom_call" | custom-call | flops 99999997952 | bytes 1536 | tf_op jit(solution)/shard_map/gradient/pallas_call | solution.py:409
  63.4 1.0 %collective-permute-start.17 = (bf16[128,1024]{1,0:T(8,128)(2,1)S(1)}, bf16[128,1024]{1,0:T(8,128)(2,1)S(1)}, u32[]{:S(2)}, u32[]{:S(2)}) collective-permute-start(bf16[128,1024]{1,0:T(8,128)(2,1)S(1)} %get-tuple-element.73), channel_id=1, source_target_pairs={{0,8},{1,9},{2,10},{3,11},{4,12},{5,13},{6,14},{7,15},{8,0},{9,1},... | collective-permute-start | bytes 786440 | tf_op jit(solution)/shard_map/ppermute | solution.py:289
  64.5 0.5 pair_sum.1
  64.9 0.6 collective-permute-start.13
  65.5 0.5 collective-permute-start.14
  66.1 2.4 %collective-permute-start.15 = (bf16[512,512]{1,0:T(8,128)(2,1)S(1)}, bf16[512,512]{1,0:T(8,128)(2,1)S(1)}, u32[]{:S(2)}, u32[]{:S(2)}) collective-permute-start(bf16[512,512]{1,0:T(8,128)(2,1)S(1)} %get-tuple-element.67), channel_id=1, source_target_pairs={{0,6},{1,7},{2,4},{3,5},{4,2},{5,3},{6,0},{7,1},{8,14},{9,15},{10,... | collective-permute-start | bytes 1572872 | tf_op jit(solution)/shard_map/ppermute | solution.py:289
  68.5 3.2 %collective-permute-done.17.other_ref = bf16[128,1024]{1,0:T(8,128)(2,1)S(1)} collective-permute-done((bf16[128,1024]{1,0:T(8,128)(2,1)S(1)}, bf16[128,1024]{1,0:T(8,128)(2,1)S(1)}, u32[]{:S(2)}, u32[]{:S(2)}) %collective-permute-start.17) | collective-permute-done | bytes 262176 | tf_op jit(solution)/shard_map/ppermute | solution.py:289
  71.8 2.7 %collective-permute-start.18 = (bf16[128,1024]{1,0:T(8,128)(2,1)S(1)}, bf16[128,1024]{1,0:T(8,128)(2,1)S(1)}, u32[]{:S(2)}, u32[]{:S(2)}) collective-permute-start(bf16[128,1024]{1,0:T(8,128)(2,1)S(1)} %line_sum.1), channel_id=1, source_target_pairs={{0,16},{1,17},{2,18},{3,19},{4,20},{5,21},{6,22},{7,23},{8,24},{9,... | collective-permute-start | bytes 786440 | tf_op jit(solution)/shard_map/ppermute | solution.py:289
  74.5 1.7 %collective-permute-start.16 = (bf16[128,1024]{1,0:T(8,128)(2,1)S(1)}, bf16[128,1024]{1,0:T(8,128)(2,1)S(1)}, u32[]{:S(2)}, u32[]{:S(2)}) collective-permute-start(bf16[128,1024]{1,0:T(8,128)(2,1)S(1)} %get-tuple-element.71), channel_id=1, source_target_pairs={{0,8},{1,9},{2,10},{3,11},{4,12},{5,13},{6,14},{7,15},{8,0},{9,1},... | collective-permute-start | bytes 786440 | tf_op jit(solution)/shard_map/ppermute | solution.py:289
  76.2 10.0 %collective-permute-done.18 = bf16[128,1024]{1,0:T(8,128)(2,1)S(1)} collective-permute-done((bf16[128,1024]{1,0:T(8,128)(2,1)S(1)}, bf16[128,1024]{1,0:T(8,128)(2,1)S(1)}, u32[]{:S(2)}, u32[]{:S(2)}) %collective-permute-start.18) | collective-permute-done | bytes 262176 | tf_op jit(solution)/shard_map/ppermute | solution.py:289
  86.6 0.9 add_multiply_fusion
  87.5 2.6 %collective-permute-done.14.y_ref = bf16[512,512]{1,0:T(8,128)(2,1)S(1)} collective-permute-done((bf16[512,512]{1,0:T(8,128)(2,1)S(1)}, bf16[512,512]{1,0:T(8,128)(2,1)S(1)}, u32[]{:S(2)}, u32[]{:S(2)}) %collective-permute-start.14) | collective-permute-done | bytes 524320 | tf_op jit(solution)/shard_map/ppermute | solution.py:289
  90.1 1.1 %plane_sum.1 = bf16[512,512]{1,0:T(8,128)(2,1)} custom-call(bf16[512,512]{1,0:T(8,128)(2,1)S(1)} %get-tuple-element.64.own_ref, bf16[512,512]{1,0:T(8,128)(2,1)S(1)} %collective-permute-done.13.x_ref, bf16[512,512]{1,0:T(8,128)(2,1)S(1)} %collective-permute-done.14.y_ref, bf16[512,512]{1,0:T(8,128)(2,1)S(1)} %collective-permute-done.15.diag_ref), custom_call_target="tpu_custom_call" | custom-call | flops 10000000000 | bytes 512 | tf_op jit(solution)/shard_map/plane_sum/pallas_call | solution.py:457
  (21 shorter events, 0.8 us)
Async XLA Ops:
  3.0 26.2 %collective-permute-start = (bf16[2,512,512]{2,1,0:T(8,128)(2,1)S(1)}, bf16[2,512,512]{2,1,0:T(8,128)(2,1)S(1)}, u32[]{:S(2)}, u32[]{:S(2)}) collective-permute-start(bf16[2,512,512]{2,1,0:T(8,128)(2,1)S(1)} %pad_maximum_fusion.refs_0_), channel_id=1, source_target_pairs={{0,2},{1,3},{2,0},{3,1},{4,6},{5,7},{6,4},{7,5},{8,10},{9,11},{10,... | collective-permute-start | bytes 3145736 | tf_op jit(solution)/shard_map/ppermute | solution.py:289
  6.0 24.6 %collective-permute-start.1 = (bf16[2,512,512]{2,1,0:T(8,128)(2,1)S(1)}, bf16[2,512,512]{2,1,0:T(8,128)(2,1)S(1)}, u32[]{:S(2)}, u32[]{:S(2)}) collective-permute-start(bf16[2,512,512]{2,1,0:T(8,128)(2,1)S(1)} %pad_maximum_fusion.refs_0_), channel_id=1, source_target_pairs={{0,4},{1,5},{2,6},{3,7},{4,0},{5,1},{6,2},{7,3},{8,12},{9,13},{10,... | collective-permute-start | bytes 3145736 | tf_op jit(solution)/shard_map/ppermute | solution.py:289
  7.5 23.1 %collective-permute-start.2 = (bf16[2,512,512]{2,1,0:T(8,128)(2,1)S(1)}, bf16[2,512,512]{2,1,0:T(8,128)(2,1)S(1)}, u32[]{:S(2)}, u32[]{:S(2)}) collective-permute-start(bf16[2,512,512]{2,1,0:T(8,128)(2,1)S(1)} %pad_maximum_fusion.refs_0_), channel_id=1, source_target_pairs={{0,1},{1,0},{2,3},{3,2},{4,5},{5,4},{6,7},{7,6},{8,9},{9,8},{10,11... | collective-permute-start | bytes 3145736 | tf_op jit(solution)/shard_map/ppermute | solution.py:289
  7.5 28.0 %collective-permute-start.7 = (bf16[272,1024]{1,0:T(8,128)(2,1)S(1)}, bf16[272,1024]{1,0:T(8,128)(2,1)S(1)}, u32[]{:S(2)}, u32[]{:S(2)}) collective-permute-start(bf16[272,1024]{1,0:T(8,128)(2,1)S(1)} %fusion.1.refs_6_), channel_id=1, source_target_pairs={{0,16},{1,17},{2,18},{3,19},{4,20},{5,21},{6,22},{7,23},{8,24},{9,... | collective-permute-start | bytes 1671176 | tf_op jit(solution)/shard_map/ppermute | solution.py:289
  10.1 26.0 %collective-permute-start.6 = (bf16[272,1024]{1,0:T(8,128)(2,1)S(1)}, bf16[272,1024]{1,0:T(8,128)(2,1)S(1)}, u32[]{:S(2)}, u32[]{:S(2)}) collective-permute-start(bf16[272,1024]{1,0:T(8,128)(2,1)S(1)} %fusion.1.refs_6_), channel_id=1, source_target_pairs={{0,8},{1,9},{2,10},{3,11},{4,12},{5,13},{6,14},{7,15},{8,0},{9,1},... | collective-permute-start | bytes 1671176 | tf_op jit(solution)/shard_map/ppermute | solution.py:289
  30.6 6.5 %collective-permute-start.4 = (bf16[2,512,512]{2,1,0:T(8,128)(2,1)S(1)}, bf16[2,512,512]{2,1,0:T(8,128)(2,1)S(1)}, u32[]{:S(2)}, u32[]{:S(2)}) collective-permute-start(bf16[2,512,512]{2,1,0:T(8,128)(2,1)S(1)} %collective-permute-done.refs_2_), channel_id=1, source_target_pairs={{0,1},{1,0},{2,3},{3,2},{4,5},{5,4},{6,7},{7,6},{8,9},{9,8},{10,11... | collective-permute-start | bytes 3145736 | tf_op jit(solution)/shard_map/ppermute | solution.py:289
  30.7 6.5 %collective-permute-start.5 = (bf16[2,512,512]{2,1,0:T(8,128)(2,1)S(1)}, bf16[2,512,512]{2,1,0:T(8,128)(2,1)S(1)}, u32[]{:S(2)}, u32[]{:S(2)}) collective-permute-start(bf16[2,512,512]{2,1,0:T(8,128)(2,1)S(1)} %collective-permute-done.1.refs_4_), channel_id=1, source_target_pairs={{0,1},{1,0},{2,3},{3,2},{4,5},{5,4},{6,7},{7,6},{8,9},{9,8},{10,11... | collective-permute-start | bytes 3145736 | tf_op jit(solution)/shard_map/ppermute | solution.py:289
  31.2 15.0 %collective-permute-start.3 = (bf16[560,512]{1,0:T(8,128)(2,1)S(1)}, bf16[560,512]{1,0:T(8,128)(2,1)S(1)}, u32[]{:S(2)}, u32[]{:S(2)}) collective-permute-start(bf16[560,512]{1,0:T(8,128)(2,1)S(1)} %slice.16), channel_id=1, source_target_pairs={{0,4},{1,5},{2,6},{3,7},{4,0},{5,1},{6,2},{7,3},{8,12},{9,13},{10,... | collective-permute-start | bytes 1720328 | tf_op jit(solution)/shard_map/ppermute | solution.py:289
  35.5 14.5 %collective-permute-start.10 = (bf16[560,512]{1,0:T(8,128)(2,1)S(1)}, bf16[560,512]{1,0:T(8,128)(2,1)S(1)}, u32[]{:S(2)}, u32[]{:S(2)}) collective-permute-start(bf16[560,512]{1,0:T(8,128)(2,1)S(1)} %slice.17), channel_id=1, source_target_pairs={{0,2},{1,3},{2,0},{3,1},{4,6},{5,7},{6,4},{7,5},{8,10},{9,11},{10,... | collective-permute-start | bytes 1720328 | tf_op jit(solution)/shard_map/ppermute | solution.py:289
  36.1 16.0 %collective-permute-start.9 = (bf16[272,1024]{1,0:T(8,128)(2,1)S(1)}, bf16[272,1024]{1,0:T(8,128)(2,1)S(1)}, u32[]{:S(2)}, u32[]{:S(2)}) collective-permute-start(bf16[272,1024]{1,0:T(8,128)(2,1)S(1)} %hand_on.1), channel_id=1, source_target_pairs={{0,8},{1,9},{2,10},{3,11},{4,12},{5,13},{6,14},{7,15},{8,0},{9,1},... | collective-permute-start | bytes 1671176 | tf_op jit(solution)/shard_map/ppermute | solution.py:289
  46.2 4.0 %collective-permute-start.8 = (bf16[512,512]{1,0:T(8,128)(2,1)S(1)}, bf16[512,512]{1,0:T(8,128)(2,1)S(1)}, u32[]{:S(2)}, u32[]{:S(2)}) collective-permute-start(bf16[512,512]{1,0:T(8,128)(2,1)S(1)} %slice.13), channel_id=1, source_target_pairs={{0,1},{1,0},{2,3},{3,2},{4,5},{5,4},{6,7},{7,6},{8,9},{9,8},{10,11... | collective-permute-start | bytes 1572872 | tf_op jit(solution)/shard_map/ppermute | solution.py:289
  50.1 7.7 %collective-permute-start.11 = (bf16[512,512]{1,0:T(8,128)(2,1)S(1)}, bf16[512,512]{1,0:T(8,128)(2,1)S(1)}, u32[]{:S(2)}, u32[]{:S(2)}) collective-permute-start(bf16[512,512]{1,0:T(8,128)(2,1)S(1)} %slice.18), channel_id=1, source_target_pairs={{0,1},{1,0},{2,3},{3,2},{4,5},{5,4},{6,7},{7,6},{8,9},{9,8},{10,11... | collective-permute-start | bytes 1572872 | tf_op jit(solution)/shard_map/ppermute | solution.py:289
  57.2 7.2 %collective-permute-start.12 = (bf16[2048,512]{1,0:T(8,128)(2,1)S(1)}, bf16[2048,512]{1,0:T(8,128)(2,1)S(1)}, u32[]{:S(2)}, u32[]{:S(2)}) collective-permute-start(bf16[2048,512]{1,0:T(8,128)(2,1)S(1)} %get-tuple-element.63), channel_id=1, source_target_pairs={{0,1},{1,0},{2,3},{3,2},{4,5},{5,4},{6,7},{7,6},{8,9},{9,8},{10,11... | collective-permute-start | bytes 6291464 | tf_op jit(solution)/shard_map/ppermute | solution.py:289
  63.4 8.3 %collective-permute-start.17 = (bf16[128,1024]{1,0:T(8,128)(2,1)S(1)}, bf16[128,1024]{1,0:T(8,128)(2,1)S(1)}, u32[]{:S(2)}, u32[]{:S(2)}) collective-permute-start(bf16[128,1024]{1,0:T(8,128)(2,1)S(1)} %get-tuple-element.73), channel_id=1, source_target_pairs={{0,8},{1,9},{2,10},{3,11},{4,12},{5,13},{6,14},{7,15},{8,0},{9,1},... | collective-permute-start | bytes 786440 | tf_op jit(solution)/shard_map/ppermute | solution.py:289
  64.9 22.5 %collective-permute-start.13 = (bf16[512,512]{1,0:T(8,128)(2,1)S(1)}, bf16[512,512]{1,0:T(8,128)(2,1)S(1)}, u32[]{:S(2)}, u32[]{:S(2)}) collective-permute-start(bf16[512,512]{1,0:T(8,128)(2,1)S(1)} %get-tuple-element.65), channel_id=1, source_target_pairs={{0,2},{1,3},{2,0},{3,1},{4,6},{5,7},{6,4},{7,5},{8,10},{9,11},{10,... | collective-permute-start | bytes 1572872 | tf_op jit(solution)/shard_map/ppermute | solution.py:289
  65.5 24.5 %collective-permute-start.14 = (bf16[512,512]{1,0:T(8,128)(2,1)S(1)}, bf16[512,512]{1,0:T(8,128)(2,1)S(1)}, u32[]{:S(2)}, u32[]{:S(2)}) collective-permute-start(bf16[512,512]{1,0:T(8,128)(2,1)S(1)} %get-tuple-element.66), channel_id=1, source_target_pairs={{0,4},{1,5},{2,6},{3,7},{4,0},{5,1},{6,2},{7,3},{8,12},{9,13},{10,... | collective-permute-start | bytes 1572872 | tf_op jit(solution)/shard_map/ppermute | solution.py:289
  66.1 24.0 %collective-permute-start.15 = (bf16[512,512]{1,0:T(8,128)(2,1)S(1)}, bf16[512,512]{1,0:T(8,128)(2,1)S(1)}, u32[]{:S(2)}, u32[]{:S(2)}) collective-permute-start(bf16[512,512]{1,0:T(8,128)(2,1)S(1)} %get-tuple-element.67), channel_id=1, source_target_pairs={{0,6},{1,7},{2,4},{3,5},{4,2},{5,3},{6,0},{7,1},{8,14},{9,15},{10,... | collective-permute-start | bytes 1572872 | tf_op jit(solution)/shard_map/ppermute | solution.py:289
  71.8 14.4 %collective-permute-start.18 = (bf16[128,1024]{1,0:T(8,128)(2,1)S(1)}, bf16[128,1024]{1,0:T(8,128)(2,1)S(1)}, u32[]{:S(2)}, u32[]{:S(2)}) collective-permute-start(bf16[128,1024]{1,0:T(8,128)(2,1)S(1)} %line_sum.1), channel_id=1, source_target_pairs={{0,16},{1,17},{2,18},{3,19},{4,20},{5,21},{6,22},{7,23},{8,24},{9,... | collective-permute-start | bytes 786440 | tf_op jit(solution)/shard_map/ppermute | solution.py:289
  74.5 12.1 %collective-permute-start.16 = (bf16[128,1024]{1,0:T(8,128)(2,1)S(1)}, bf16[128,1024]{1,0:T(8,128)(2,1)S(1)}, u32[]{:S(2)}, u32[]{:S(2)}) collective-permute-start(bf16[128,1024]{1,0:T(8,128)(2,1)S(1)} %get-tuple-element.71), channel_id=1, source_target_pairs={{0,8},{1,9},{2,10},{3,11},{4,12},{5,13},{6,14},{7,15},{8,0},{9,1},... | collective-permute-start | bytes 786440 | tf_op jit(solution)/shard_map/ppermute | solution.py:289

commit v11 on v9

--- a/solution.py
+++ b/solution.py
@@ -17,6 +17,7 @@
 GRADIENT_COST = 10**10
 DIAGONAL_COST = 10**6
 EXTRA = 48
+BIAS_ROWS = 8
 MORE = 16
 
 
@@ -78,20 +79,19 @@
     ]
 
 
-def weight_copies(refs, owned, w_in, w_out, bias, sem):
-    ins, outs = [], []
+def weight_copies(refs, owned, w_in, w_out, sem):
+    copies = []
     for at, ref in enumerate(refs):
         spot = pl.ds(at * owned, owned)
-        ins.append(pltpu.make_async_copy(ref.at[pl.ds(0, owned)], w_in.at[spot], sem.at[0, at]))
-        ins.append(
-            pltpu.make_async_copy(
-                ref.at[pl.ds(2 * owned, 16), pl.ds(0, owned)], bias.at[:, spot], sem.at[1, at]
-            )
+        copies.append(pltpu.make_async_copy(ref.at[pl.ds(0, owned)], w_in.at[spot], sem.at[0, at]))
+        copies.append(
+            pltpu.make_async_copy(ref.at[pl.ds(owned, owned)], w_out.at[spot], sem.at[1, at])
         )
-        outs.append(
-            pltpu.make_async_copy(ref.at[pl.ds(owned, owned)], w_out.at[spot], sem.at[2, at])
-        )
-    return ins, outs
+    return copies
+
+
+def bias_of(ref, owned):
+    return ref[2 * owned : 2 * owned + BIAS_ROWS, :owned].astype(jnp.float32)
 
 
 def run(copies, what):
@@ -102,7 +102,7 @@
 def activate(tok, w_in, bias):
     pre = lax.dot_general(
         tok, w_in, CONTRACT_LAST, preferred_element_type=jnp.float32
-    ) + bias.astype(jnp.float32)
+    ) + bias
     return gelu_parts(pre)
 
 
@@ -136,7 +136,7 @@
     dpre, tok_sem, cot_sem, w_sem = refs[18:]
     core = lax.axis_index("core")
     rows = pair_refs[0].shape[1]
-    ins, outs = weight_copies(w_refs, owned, w_in, w_out, bias, w_sem)
+    w_copies = weight_copies(w_refs, owned, w_in, w_out, w_sem)
     loads = []
     for block in range(NEAR - 1):
         first, second = pair_refs[2 * block], pair_refs[2 * block + 1]
@@ -144,10 +144,12 @@
             side_by_side(core, (first.at[0], second.at[0]), tok, block * rows, tok_sem.at[block])
             + side_by_side(core, (first.at[1], second.at[1]), cot, block * rows, cot_sem.at[block])
         )
-    run(ins + outs, "start")
+    run(w_copies, "start")
     for load in loads:
         run(load, "start")
-    run(ins + outs, "wait")
+    for at, ref in enumerate(w_refs):
+        bias[:, at * owned : (at + 1) * owned] = bias_of(ref, owned)
+    run(w_copies, "wait")
     for block, load in enumerate(loads):
         run(load, "wait")
         early_block(
@@ -172,7 +174,7 @@
         pltpu.make_async_copy(w_three.at[pl.ds(owned, owned)], w_out_all.at[last], sem.at[3]),
     ]
     run(copies, "start")
-    bias_last = w_three[two : two + 16, :owned]
+    bias_last = bias_of(w_three, owned)
     bias_all[:, :three] = bias[...]
     bias_all[:, three:] = bias_last
     w_last[:owned, :] = w_out[two:, :]
@@ -211,13 +213,17 @@
 
 def diagonal_kernel(owned, *refs):
     w_in, w_out, bias, grad_first, grad_last = refs[:5]
-    mine_ref, other_ref, own_ref, one_ref, two_ref, three_ref = refs[9:15]
-    tok, cot, dpre, tok_sem, cot_sem = refs[15:]
+    tok_ref, cot_ref, far_ref = refs[5:8]
+    mine_ref, other_ref, own_ref, one_ref, two_ref, three_ref = refs[8:14]
+    tok, cot, dpre, tok_sem, cot_sem = refs[14:]
     core = lax.axis_index("core")
     rows, feats = mine_ref.shape
     two = 2 * owned
-    load = side_by_side(core, [ref.at[pl.ds(0, rows)] for ref in refs[5:7]], tok, 0, tok_sem)
-    load += side_by_side(core, [ref.at[pl.ds(EXTRA, rows)] for ref in refs[7:9]], cot, 0, cot_sem)
+    first, second = pl.ds(0, rows), pl.ds(rows, rows)
+    load = side_by_side(core, (tok_ref.at[first], far_ref.at[first]), tok, 0, tok_sem)
+    load += side_by_side(
+        core, (cot_ref.at[pl.ds(EXTRA, rows)], far_ref.at[second]), cot, 0, cot_sem
+    )
     run(load, "start")
     run(load, "wait")
     step = rows // 2
@@ -322,7 +328,7 @@
     def cost(flops, traffic):
         return pl.CostEstimate(flops=flops, bytes_accessed=traffic, transcendentals=0)
 
-    bias_rows = jnp.pad(b_in.reshape(1, owned), ((0, 15), (0, width - owned)))
+    bias_rows = jnp.pad(b_in.reshape(1, owned), ((0, BIAS_ROWS - 1), (0, width - owned)))
     own_w = jnp.concatenate([w_in, w_out, bias_rows], 0)
     own_w, tokens, cotangent = barrier((own_w, tokens, cotangent))
     own = jnp.stack([tokens, cotangent])
@@ -346,15 +352,15 @@
                 bf16(early_rows, width),
                 bf16(3 * owned, width),
                 bf16(3 * owned, width),
-                bf16(16, 3 * owned),
+                f32(BIAS_ROWS, 3 * owned),
             ),
-            in_specs=anywhere(9),
+            in_specs=anywhere(6) + vmem(3),
             out_specs=vmem(9),
             scratch_shapes=[
                 pltpu.VMEM((early_rows, 2 * owned), jnp.bfloat16),
                 dma((NEAR - 1, 2)),
                 dma((NEAR - 1, 2)),
-                dma((3, 3)),
+                dma((2, 3)),
             ],
             compiler_params=params,
             cost_estimate=cost(early_rows * units, early_rows),
@@ -370,7 +376,7 @@
             f32(early_rows, owned),
             bf16(units, width),
             bf16(units, width),
-            bf16(16, units),
+            f32(BIAS_ROWS, units),
         ),
         in_specs=vmem(7),
         out_specs=vmem(6),
@@ -381,7 +387,7 @@
     )(act_two, tok, mixed_terms, w_in_three, w_out_three, bias, w_three)
     tok_diag, cot_diag, other = barrier((tok_diag, cot_diag, other))
     received = to_core(other)
-    tok_diag_other, cot_diag_other = to_core(tok_diag), to_core(cot_diag)
+    diag_other = to_core(jnp.concatenate([tok_diag[:rows], cot_diag[EXTRA:]]))
     slope, tok_diag = barrier((slope, tok_diag))
     grad_last = pl.pallas_call(
         gradient_kernel,
@@ -410,7 +416,7 @@
     mine_diag, other_diag, grad_own, grad_one, grad_two, grad_three = pl.pallas_call(
         functools.partial(diagonal_kernel, owned),
         out_shape=[bf16(rows, feats)] * 2 + [bf16(owned, width)] * 4,
-        in_specs=vmem(5) + anywhere(4),
+        in_specs=vmem(5) + anywhere(3),
         out_specs=vmem(6),
         scratch_shapes=[
             pltpu.VMEM((rows, width), jnp.bfloat16),
@@ -424,12 +430,10 @@
         name="diagonal",
     )(
         w_in_all, w_out_all, bias, grad_terms, grad_last,
-        tok_diag, tok_diag_other, cot_diag, cot_diag_other,
+        tok_diag, cot_diag, diag_other,
     )
     received_diag = to_core(other_diag)
     relayed = to_far(grad_three, 1)
-    from_one = to_far(grad_one, 1)
-
     (sum_diag,) = pl.pallas_call(
         functools.partial(pair_kernel, rows),
         out_shape=[bf16(rows, feats)],
@@ -440,7 +444,8 @@
         name="pair_sum_diagonal",
     )(mine_diag, received_diag)
     mixed_diag = to_diagonal(sum_diag)
-    grad_two, _ = barrier((grad_two, sum_diag))
+    grad_one, grad_two, _ = barrier((grad_one, grad_two, sum_diag))
+    from_one = to_far(grad_one, 1)
     (line_sum,) = pl.pallas_call(
         functools.partial(pair_kernel, owned),
         out_shape=[bf16(owned, width)],

time: 88 us -> 88 us (level)
  waiting for transfers between devices: 44.1 us -> 42.4 us
  other arithmetic: 3.13 us -> 4.32 us
    ppermute x20 -> x19, waiting for transfers between devices: 44.1 us -> 42.4 us  [permute(): return lax.ppermute(value, AXES, pairs)]
    another operation x1, other arithmetic: 0.1 us -> 1.3 us  [on_device_lines(): own = jnp.stack([tokens, cotangent])]
    ppermute x20 -> x19, starting transfers between devices: 21.5 us -> 22.2 us  [permute(): return lax.ppermute(value, AXES, pairs)]
  transfers between devices with their start and end apart: 20 -> 19, of which waited for: 8 -> 10; matrix products, arithmetic and copies ran while one was open for 1% -> 1% of each run, Pallas kernels for 21% -> 21%
where the time goes in v11:
time: 88 us; the launch traced here: 87.9 us
  waiting for transfers between devices  42.4 us (48%)
  starting transfers between devices  22.2 us (25%)
  Pallas kernels  18.1 us (21%)
  other arithmetic  4.32 us (5%)
    ppermute x19, waiting for transfers between devices, permute(): return lax.ppermute(value, AXES, pairs)  42.4 us
    ppermute x19, starting transfers between devices, permute(): return lax.ppermute(value, AXES, pairs)  22.2 us
    pallas_call x1, Pallas kernels, on_device_lines(): pl.pallas_call(functools.partial(early_kernel, owned), out_shape=(bf16(ea...  7.43 us
    pallas_call x1, Pallas kernels, on_device_lines(): pl.pallas_call(functools.partial(output_kernel, owned), out_shape=(bf16(e...  4.05 us
    pallas_call x1, Pallas kernels, on_device_lines(): pl.pallas_call(functools.partial(diagonal_kernel, owned), out_shape=[bf16...  3.53 us
    pallas_call x1, Pallas kernels, on_device_lines(): pl.pallas_call(gradient_kernel, out_shape=f32(2 * owned, width), in_specs...  2.31 us
  transfers between devices with their start and end apart: 19, of which 10 were waited for; matrix products, arithmetic and copies ran while one was open for 1% of the time, Pallas kernels for 21%

profile of v11, /device:TPU:0, one launch (start us, length us, event | category | flops | bytes accessed | tf_op | source)
XLA Modules:
  0.0 87.9 jit_solution(5805387217343974955)
XLA Ops:
  0.6 1.1 %fusion.1.refs_6_ = bf16[264,1024]{1,0:T(8,128)(2,1)S(1)} fusion(bf16[1,128]{1,0:T(2,128)(2,1)} %bitcast.9, bf16[128,1024]{1,0:T(8,128)(2,1)} %param.9, bf16[128,1024]{1,0:T(8,128)(2,1)} %param.7), kind=kLoop, calls=%fused_computation.5 | loop fusion | flops 2162688 | bytes 1065216 | tf_op jit(solution)/shard_map/concatenate | solution.py:332
  1.7 1.3 %pad_maximum_fusion.refs_0_ = bf16[2,512,512]{2,1,0:T(8,128)(2,1)S(1)} fusion(bf16[1,512,512]{2,1,0:T(8,128)(2,1)} %bitcast.7, bf16[1,512,512]{2,1,0:T(8,128)(2,1)} %bitcast.8), kind=kLoop, calls=%fused_computation.2 | loop fusion | flops 524288 | bytes 2097152 | tf_op jit(solution)/shard_map/stack | solution.py:334
  3.0 3.0 %collective-permute-start = (bf16[2,512,512]{2,1,0:T(8,128)(2,1)S(1)}, bf16[2,512,512]{2,1,0:T(8,128)(2,1)S(1)}, u32[]{:S(2)}, u32[]{:S(2)}) collective-permute-start(bf16[2,512,512]{2,1,0:T(8,128)(2,1)S(1)} %pad_maximum_fusion.refs_0_), channel_id=1, source_target_pairs={{0,2},{1,3},{2,0},{3,1},{4,6},{5,7},{6,4},{7,5},{8,10},{9,11},{10,... | collective-permute-start | bytes 3145736 | tf_op jit(solution)/shard_map/ppermute | solution.py:291
  6.0 1.5 %collective-permute-start.1 = (bf16[2,512,512]{2,1,0:T(8,128)(2,1)S(1)}, bf16[2,512,512]{2,1,0:T(8,128)(2,1)S(1)}, u32[]{:S(2)}, u32[]{:S(2)}) collective-permute-start(bf16[2,512,512]{2,1,0:T(8,128)(2,1)S(1)} %pad_maximum_fusion.refs_0_), channel_id=1, source_target_pairs={{0,4},{1,5},{2,6},{3,7},{4,0},{5,1},{6,2},{7,3},{8,12},{9,13},{10,... | collective-permute-start | bytes 3145736 | tf_op jit(solution)/shard_map/ppermute | solution.py:291
  7.5 2.6 %collective-permute-start.6 = (bf16[264,1024]{1,0:T(8,128)(2,1)S(1)}, bf16[264,1024]{1,0:T(8,128)(2,1)S(1)}, u32[]{:S(2)}, u32[]{:S(2)}) collective-permute-start(bf16[264,1024]{1,0:T(8,128)(2,1)S(1)} %fusion.1.refs_6_), channel_id=1, source_target_pairs={{0,16},{1,17},{2,18},{3,19},{4,20},{5,21},{6,22},{7,23},{8,24},{9,... | collective-permute-start | bytes 1622024 | tf_op jit(solution)/shard_map/ppermute | solution.py:291
  10.1 1.6 %collective-permute-start.5 = (bf16[264,1024]{1,0:T(8,128)(2,1)S(1)}, bf16[264,1024]{1,0:T(8,128)(2,1)S(1)}, u32[]{:S(2)}, u32[]{:S(2)}) collective-permute-start(bf16[264,1024]{1,0:T(8,128)(2,1)S(1)} %fusion.1.refs_6_), channel_id=1, source_target_pairs={{0,8},{1,9},{2,10},{3,11},{4,12},{5,13},{6,14},{7,15},{8,0},{9,1},... | collective-permute-start | bytes 1622024 | tf_op jit(solution)/shard_map/ppermute | solution.py:291
  11.7 17.5 %collective-permute-done.refs_2_ = bf16[2,512,512]{2,1,0:T(8,128)(2,1)S(1)} collective-permute-done((bf16[2,512,512]{2,1,0:T(8,128)(2,1)S(1)}, bf16[2,512,512]{2,1,0:T(8,128)(2,1)S(1)}, u32[]{:S(2)}, u32[]{:S(2)}) %collective-permute-start) | collective-permute-done | bytes 1048608 | tf_op jit(solution)/shard_map/ppermute | solution.py:291
  29.2 1.5 %collective-permute-done.1.refs_4_ = bf16[2,512,512]{2,1,0:T(8,128)(2,1)S(1)} collective-permute-done((bf16[2,512,512]{2,1,0:T(8,128)(2,1)S(1)}, bf16[2,512,512]{2,1,0:T(8,128)(2,1)S(1)}, u32[]{:S(2)}, u32[]{:S(2)}) %collective-permute-start.1) | collective-permute-done | bytes 1048608 | tf_op jit(solution)/shard_map/ppermute | solution.py:291
  30.6 0.5 collective-permute-start.4
  31.2 1.6 %collective-permute-start.8 = (bf16[560,512]{1,0:T(8,128)(2,1)S(1)}, bf16[560,512]{1,0:T(8,128)(2,1)S(1)}, u32[]{:S(2)}, u32[]{:S(2)}) collective-permute-start(bf16[560,512]{1,0:T(8,128)(2,1)S(1)} %slice.16), channel_id=1, source_target_pairs={{0,4},{1,5},{2,6},{3,7},{4,0},{5,1},{6,2},{7,3},{8,12},{9,13},{10,... | collective-permute-start | bytes 1720328 | tf_op jit(solution)/shard_map/ppermute | solution.py:291
  32.8 2.0 %collective-permute-done.6.refs_8_ = bf16[264,1024]{1,0:T(8,128)(2,1)S(1)} collective-permute-done((bf16[264,1024]{1,0:T(8,128)(2,1)S(1)}, bf16[264,1024]{1,0:T(8,128)(2,1)S(1)}, u32[]{:S(2)}, u32[]{:S(2)}) %collective-permute-start.6) | collective-permute-done | bytes 540704 | tf_op jit(solution)/shard_map/ppermute | solution.py:291
  34.8 0.5 collective-permute-start.9
  35.4 1.1 %collective-permute-start.7 = (bf16[264,1024]{1,0:T(8,128)(2,1)S(1)}, bf16[264,1024]{1,0:T(8,128)(2,1)S(1)}, u32[]{:S(2)}, u32[]{:S(2)}) collective-permute-start(bf16[264,1024]{1,0:T(8,128)(2,1)S(1)} %collective-permute-done.6.refs_8_), channel_id=1, source_target_pairs={{0,8},{1,9},{2,10},{3,11},{4,12},{5,13},{6,14},{7,15},{8,0},{9,1},... | collective-permute-start | bytes 1622024 | tf_op jit(solution)/shard_map/ppermute | solution.py:291
  36.5 7.4 %early.1 = (bf16[1536,128]{1,0:T(8,128)(2,1)S(1)}, bf16[1536,128]{1,0:T(8,128)(2,1)S(1)}, f32[1536,1024]{1,0:T(8,128)S(1)}, f32[256,1024]{1,0:T(8,128)S(1)}, bf1...) custom-call(bf16[2,512,512]{2,1,0:T(8,128)(2,1)S(1)} %pad_maximum_fu, ...), custom_call_target="tpu_custom_call" | custom-call | flops 786432 | bytes 1536 | tf_op jit(solution)/shard_map/early/pallas_call | solution.py:344
  43.9 5.0 %collective-permute-done.7.refs_6_.w_three = bf16[264,1024]{1,0:T(8,128)(2,1)S(1)} collective-permute-done((bf16[264,1024]{1,0:T(8,128)(2,1)S(1)}, bf16[264,1024]{1,0:T(8,128)(2,1)S(1)}, u32[]{:S(2)}, u32[]{:S(2)}) %collective-permute-start.7) | collective-permute-done | bytes 540704 | tf_op jit(solution)/shard_map/ppermute | solution.py:291
  48.9 4.1 %output.1 = (bf16[1536,512]{1,0:T(8,128)(2,1)S(1)}, bf16[1536,512]{1,0:T(8,128)(2,1)S(1)}, f32[1536,128]{1,0:T(8,128)S(1)}, bf16[512,1024]{1,0:T(8,128)(2,1)S(1)...) custom-call(bf16[1536,128]{1,0:T(8,128)(2,1)S(1)} %get-tuple-element.50.refs_0_, ...), custom_call_target="tpu_custom_call" | custom-call | flops 786432 | bytes 1536 | tf_op jit(solution)/shard_map/output/pallas_call | solution.py:371
  53.3 0.6 collective-permute-start.13
  53.8 2.3 %gradient.1.refs_4_ = f32[256,1024]{1,0:T(8,128)S(1)} custom-call(bf16[1536,128]{1,0:T(8,128)(2,1)S(1)} %get-tuple-element.57.dpre_two, bf16[1536,1024]{1,0:T(8,128)(2,1)S(1)} %get-tuple-element.51.refs_1_.tok, bf16[1536,1024]{1,0:T(8,128)(2,1)S(1)} %get-tuple-element.58.cot, f32[1536,128]{1,0:T(8,128)S(1)} %get-tuple-element.62.slope, ...), custom_call_target="tpu_custom_call" | custom-call | flops 10000000000 | bytes 1536 | tf_op jit(solution)/shard_map/gradient/pallas_call | solution.py:392
  56.5 0.4 pair_sum.1
  56.9 1.6 %collective-permute-start.11 = (bf16[528,512]{1,0:T(8,128)(2,1)S(1)}, bf16[528,512]{1,0:T(8,128)(2,1)S(1)}, u32[]{:S(2)}, u32[]{:S(2)}) collective-permute-start(bf16[528,512]{1,0:T(8,128)(2,1)S(1)} %get-tuple-element.67), channel_id=1, source_target_pairs={{0,2},{1,3},{2,0},{3,1},{4,6},{5,7},{6,4},{7,5},{8,10},{9,11},{10,... | collective-permute-start | bytes 1622024 | tf_op jit(solution)/shard_map/ppermute | solution.py:291
  58.5 0.5 collective-permute-start.12
  59.0 3.5 %diagonal.1 = (bf16[512,512]{1,0:T(8,128)(2,1)S(1)}, bf16[512,512]{1,0:T(8,128)(2,1)S(1)}, bf16[128,1024]{1,0:T(8,128)(2,1)S(1)}, bf16[128,1024]{1,0:T(8,128)(2,...) custom-call(bf16[512,1024]{1,0:T(8,128)(2,1)S(1)} %get-tuple-element.69.refs_0_, ...), custom_call_target="tpu_custom_call" | custom-call | flops 1000000 | bytes 512 | tf_op jit(solution)/shard_map/diagonal/pallas_call | solution.py:416
  62.6 1.0 %collective-permute-start.17 = (bf16[128,1024]{1,0:T(8,128)(2,1)S(1)}, bf16[128,1024]{1,0:T(8,128)(2,1)S(1)}, u32[]{:S(2)}, u32[]{:S(2)}) collective-permute-start(bf16[128,1024]{1,0:T(8,128)(2,1)S(1)} %get-tuple-element.83), channel_id=1, source_target_pairs={{0,8},{1,9},{2,10},{3,11},{4,12},{5,13},{6,14},{7,15},{8,0},{9,1},... | collective-permute-start | bytes 786440 | tf_op jit(solution)/shard_map/ppermute | solution.py:291
  63.6 0.9 collective-permute-done.14.other_ref
  64.6 1.6 %collective-permute-start.15 = (bf16[512,512]{1,0:T(8,128)(2,1)S(1)}, bf16[512,512]{1,0:T(8,128)(2,1)S(1)}, u32[]{:S(2)}, u32[]{:S(2)}) collective-permute-start(bf16[512,512]{1,0:T(8,128)(2,1)S(1)} %pair_sum_diagonal.1), channel_id=1, source_target_pairs={{0,6},{1,7},{2,4},{3,5},{4,2},{5,3},{6,0},{7,1},{8,14},{9,15},{10,... | collective-permute-start | bytes 1572872 | tf_op jit(solution)/shard_map/ppermute | solution.py:291
  66.2 5.1 %collective-permute-done.17.other_ref = bf16[128,1024]{1,0:T(8,128)(2,1)S(1)} collective-permute-done((bf16[128,1024]{1,0:T(8,128)(2,1)S(1)}, bf16[128,1024]{1,0:T(8,128)(2,1)S(1)}, u32[]{:S(2)}, u32[]{:S(2)}) %collective-permute-start.17) | collective-permute-done | bytes 262176 | tf_op jit(solution)/shard_map/ppermute | solution.py:291
  71.4 2.7 %collective-permute-start.18 = (bf16[128,1024]{1,0:T(8,128)(2,1)S(1)}, bf16[128,1024]{1,0:T(8,128)(2,1)S(1)}, u32[]{:S(2)}, u32[]{:S(2)}) collective-permute-start(bf16[128,1024]{1,0:T(8,128)(2,1)S(1)} %line_sum.1), channel_id=1, source_target_pairs={{0,16},{1,17},{2,18},{3,19},{4,20},{5,21},{6,22},{7,23},{8,24},{9,... | collective-permute-start | bytes 786440 | tf_op jit(solution)/shard_map/ppermute | solution.py:291
  74.0 1.7 %collective-permute-start.16 = (bf16[128,1024]{1,0:T(8,128)(2,1)S(1)}, bf16[128,1024]{1,0:T(8,128)(2,1)S(1)}, u32[]{:S(2)}, u32[]{:S(2)}) collective-permute-start(bf16[128,1024]{1,0:T(8,128)(2,1)S(1)} %get-tuple-element.81), channel_id=1, source_target_pairs={{0,8},{1,9},{2,10},{3,11},{4,12},{5,13},{6,14},{7,15},{8,0},{9,1},... | collective-permute-start | bytes 786440 | tf_op jit(solution)/shard_map/ppermute | solution.py:291
  75.8 7.9 %collective-permute-done.12.y_ref = bf16[528,512]{1,0:T(8,128)(2,1)S(1)} collective-permute-done((bf16[528,512]{1,0:T(8,128)(2,1)S(1)}, bf16[528,512]{1,0:T(8,128)(2,1)S(1)}, u32[]{:S(2)}, u32[]{:S(2)}) %collective-permute-start.12) | collective-permute-done | bytes 540704 | tf_op jit(solution)/shard_map/ppermute | solution.py:291
  83.9 2.0 %collective-permute-done.18 = bf16[128,1024]{1,0:T(8,128)(2,1)S(1)} collective-permute-done((bf16[128,1024]{1,0:T(8,128)(2,1)S(1)}, bf16[128,1024]{1,0:T(8,128)(2,1)S(1)}, u32[]{:S(2)}, u32[]{:S(2)}) %collective-permute-start.18) | collective-permute-done | bytes 262176 | tf_op jit(solution)/shard_map/ppermute | solution.py:291
  86.0 0.9 %add_multiply_fusion = f32[128,1024]{1,0:T(8,128)} fusion(bf16[128,1024]{1,0:T(8,128)(2,1)S(1)} %collective-permute-done.18, bf16[128,1024]{1,0:T(8,128)(2,1)S(1)} %collective-permute-done.16, bf16[128,1024]{1,0:T(8,128)(2,1)S(1)} %get-tuple-element.78), kind=kLoop, calls=%fused_computation.6 | loop fusion | flops 786432 | bytes 1310720 | tf_op jit(solution)/shard_map/mul | solution.py:474
  86.9 1.0 %add_convert_fusion = bf16[512,512]{1,0:T(8,128)(2,1)} fusion(f32[512,512]{1,0:T(8,128)S(1)} %plane_sum.1, bf16[512,512]{1,0:T(8,128)(2,1)S(1)} %collective-permute-done.15), kind=kLoop, calls=%fused_computation.4 | loop fusion | flops 786432 | bytes 2097152 | tf_op jit(solution)/shard_map/convert_element_type | solution.py:473
  (23 shorter events, 1.2 us)
Async XLA Ops:
  3.0 26.2 %collective-permute-start = (bf16[2,512,512]{2,1,0:T(8,128)(2,1)S(1)}, bf16[2,512,512]{2,1,0:T(8,128)(2,1)S(1)}, u32[]{:S(2)}, u32[]{:S(2)}) collective-permute-start(bf16[2,512,512]{2,1,0:T(8,128)(2,1)S(1)} %pad_maximum_fusion.refs_0_), channel_id=1, source_target_pairs={{0,2},{1,3},{2,0},{3,1},{4,6},{5,7},{6,4},{7,5},{8,10},{9,11},{10,... | collective-permute-start | bytes 3145736 | tf_op jit(solution)/shard_map/ppermute | solution.py:291
  6.0 24.6 %collective-permute-start.1 = (bf16[2,512,512]{2,1,0:T(8,128)(2,1)S(1)}, bf16[2,512,512]{2,1,0:T(8,128)(2,1)S(1)}, u32[]{:S(2)}, u32[]{:S(2)}) collective-permute-start(bf16[2,512,512]{2,1,0:T(8,128)(2,1)S(1)} %pad_maximum_fusion.refs_0_), channel_id=1, source_target_pairs={{0,4},{1,5},{2,6},{3,7},{4,0},{5,1},{6,2},{7,3},{8,12},{9,13},{10,... | collective-permute-start | bytes 3145736 | tf_op jit(solution)/shard_map/ppermute | solution.py:291
  7.5 23.1 %collective-permute-start.2 = (bf16[2,512,512]{2,1,0:T(8,128)(2,1)S(1)}, bf16[2,512,512]{2,1,0:T(8,128)(2,1)S(1)}, u32[]{:S(2)}, u32[]{:S(2)}) collective-permute-start(bf16[2,512,512]{2,1,0:T(8,128)(2,1)S(1)} %pad_maximum_fusion.refs_0_), channel_id=1, source_target_pairs={{0,1},{1,0},{2,3},{3,2},{4,5},{5,4},{6,7},{7,6},{8,9},{9,8},{10,11... | collective-permute-start | bytes 3145736 | tf_op jit(solution)/shard_map/ppermute | solution.py:291
  7.5 27.3 %collective-permute-start.6 = (bf16[264,1024]{1,0:T(8,128)(2,1)S(1)}, bf16[264,1024]{1,0:T(8,128)(2,1)S(1)}, u32[]{:S(2)}, u32[]{:S(2)}) collective-permute-start(bf16[264,1024]{1,0:T(8,128)(2,1)S(1)} %fusion.1.refs_6_), channel_id=1, source_target_pairs={{0,16},{1,17},{2,18},{3,19},{4,20},{5,21},{6,22},{7,23},{8,24},{9,... | collective-permute-start | bytes 1622024 | tf_op jit(solution)/shard_map/ppermute | solution.py:291
  10.1 25.2 %collective-permute-start.5 = (bf16[264,1024]{1,0:T(8,128)(2,1)S(1)}, bf16[264,1024]{1,0:T(8,128)(2,1)S(1)}, u32[]{:S(2)}, u32[]{:S(2)}) collective-permute-start(bf16[264,1024]{1,0:T(8,128)(2,1)S(1)} %fusion.1.refs_6_), channel_id=1, source_target_pairs={{0,8},{1,9},{2,10},{3,11},{4,12},{5,13},{6,14},{7,15},{8,0},{9,1},... | collective-permute-start | bytes 1622024 | tf_op jit(solution)/shard_map/ppermute | solution.py:291
  30.6 5.8 %collective-permute-start.3 = (bf16[2,512,512]{2,1,0:T(8,128)(2,1)S(1)}, bf16[2,512,512]{2,1,0:T(8,128)(2,1)S(1)}, u32[]{:S(2)}, u32[]{:S(2)}) collective-permute-start(bf16[2,512,512]{2,1,0:T(8,128)(2,1)S(1)} %collective-permute-done.refs_2_), channel_id=1, source_target_pairs={{0,1},{1,0},{2,3},{3,2},{4,5},{5,4},{6,7},{7,6},{8,9},{9,8},{10,11... | collective-permute-start | bytes 3145736 | tf_op jit(solution)/shard_map/ppermute | solution.py:291
  30.6 5.8 %collective-permute-start.4 = (bf16[2,512,512]{2,1,0:T(8,128)(2,1)S(1)}, bf16[2,512,512]{2,1,0:T(8,128)(2,1)S(1)}, u32[]{:S(2)}, u32[]{:S(2)}) collective-permute-start(bf16[2,512,512]{2,1,0:T(8,128)(2,1)S(1)} %collective-permute-done.1.refs_4_), channel_id=1, source_target_pairs={{0,1},{1,0},{2,3},{3,2},{4,5},{5,4},{6,7},{7,6},{8,9},{9,8},{10,11... | collective-permute-start | bytes 3145736 | tf_op jit(solution)/shard_map/ppermute | solution.py:291
  31.2 21.8 %collective-permute-start.8 = (bf16[560,512]{1,0:T(8,128)(2,1)S(1)}, bf16[560,512]{1,0:T(8,128)(2,1)S(1)}, u32[]{:S(2)}, u32[]{:S(2)}) collective-permute-start(bf16[560,512]{1,0:T(8,128)(2,1)S(1)} %slice.16), channel_id=1, source_target_pairs={{0,4},{1,5},{2,6},{3,7},{4,0},{5,1},{6,2},{7,3},{8,12},{9,13},{10,... | collective-permute-start | bytes 1720328 | tf_op jit(solution)/shard_map/ppermute | solution.py:291
  34.8 18.2 %collective-permute-start.9 = (bf16[560,512]{1,0:T(8,128)(2,1)S(1)}, bf16[560,512]{1,0:T(8,128)(2,1)S(1)}, u32[]{:S(2)}, u32[]{:S(2)}) collective-permute-start(bf16[560,512]{1,0:T(8,128)(2,1)S(1)} %slice.17), channel_id=1, source_target_pairs={{0,2},{1,3},{2,0},{3,1},{4,6},{5,7},{6,4},{7,5},{8,10},{9,11},{10,... | collective-permute-start | bytes 1720328 | tf_op jit(solution)/shard_map/ppermute | solution.py:291
  35.4 13.6 %collective-permute-start.7 = (bf16[264,1024]{1,0:T(8,128)(2,1)S(1)}, bf16[264,1024]{1,0:T(8,128)(2,1)S(1)}, u32[]{:S(2)}, u32[]{:S(2)}) collective-permute-start(bf16[264,1024]{1,0:T(8,128)(2,1)S(1)} %collective-permute-done.6.refs_8_), channel_id=1, source_target_pairs={{0,8},{1,9},{2,10},{3,11},{4,12},{5,13},{6,14},{7,15},{8,0},{9,1},... | collective-permute-start | bytes 1622024 | tf_op jit(solution)/shard_map/ppermute | solution.py:291
  53.0 3.5 %collective-permute-start.10 = (bf16[1536,512]{1,0:T(8,128)(2,1)S(1)}, bf16[1536,512]{1,0:T(8,128)(2,1)S(1)}, u32[]{:S(2)}, u32[]{:S(2)}) collective-permute-start(bf16[1536,512]{1,0:T(8,128)(2,1)S(1)} %get-tuple-element.64), channel_id=1, source_target_pairs={{0,1},{1,0},{2,3},{3,2},{4,5},{5,4},{6,7},{7,6},{8,9},{9,8},{10,11... | collective-permute-start | bytes 4718600 | tf_op jit(solution)/shard_map/ppermute | solution.py:291
  53.3 5.7 %collective-permute-start.13 = (bf16[1024,512]{1,0:T(8,128)(2,1)S(1)}, bf16[1024,512]{1,0:T(8,128)(2,1)S(1)}, u32[]{:S(2)}, u32[]{:S(2)}) collective-permute-start(bf16[1024,512]{1,0:T(8,128)(2,1)S(1)} %pad_maximum_fusion.1), channel_id=1, source_target_pairs={{0,1},{1,0},{2,3},{3,2},{4,5},{5,4},{6,7},{7,6},{8,9},{9,8},{10,11... | collective-permute-start | bytes 3145736 | tf_op jit(solution)/shard_map/ppermute | solution.py:291
  56.9 18.9 %collective-permute-start.11 = (bf16[528,512]{1,0:T(8,128)(2,1)S(1)}, bf16[528,512]{1,0:T(8,128)(2,1)S(1)}, u32[]{:S(2)}, u32[]{:S(2)}) collective-permute-start(bf16[528,512]{1,0:T(8,128)(2,1)S(1)} %get-tuple-element.67), channel_id=1, source_target_pairs={{0,2},{1,3},{2,0},{3,1},{4,6},{5,7},{6,4},{7,5},{8,10},{9,11},{10,... | collective-permute-start | bytes 1622024 | tf_op jit(solution)/shard_map/ppermute | solution.py:291
  58.5 25.3 %collective-permute-start.12 = (bf16[528,512]{1,0:T(8,128)(2,1)S(1)}, bf16[528,512]{1,0:T(8,128)(2,1)S(1)}, u32[]{:S(2)}, u32[]{:S(2)}) collective-permute-start(bf16[528,512]{1,0:T(8,128)(2,1)S(1)} %get-tuple-element.68), channel_id=1, source_target_pairs={{0,4},{1,5},{2,6},{3,7},{4,0},{5,1},{6,2},{7,3},{8,12},{9,13},{10,... | collective-permute-start | bytes 1622024 | tf_op jit(solution)/shard_map/ppermute | solution.py:291
  62.5 2.0 %collective-permute-start.14 = (bf16[512,512]{1,0:T(8,128)(2,1)S(1)}, bf16[512,512]{1,0:T(8,128)(2,1)S(1)}, u32[]{:S(2)}, u32[]{:S(2)}) collective-permute-start(bf16[512,512]{1,0:T(8,128)(2,1)S(1)} %get-tuple-element.77), channel_id=1, source_target_pairs={{0,1},{1,0},{2,3},{3,2},{4,5},{5,4},{6,7},{7,6},{8,9},{9,8},{10,11... | collective-permute-start | bytes 1572872 | tf_op jit(solution)/shard_map/ppermute | solution.py:291
  62.6 8.7 %collective-permute-start.17 = (bf16[128,1024]{1,0:T(8,128)(2,1)S(1)}, bf16[128,1024]{1,0:T(8,128)(2,1)S(1)}, u32[]{:S(2)}, u32[]{:S(2)}) collective-permute-start(bf16[128,1024]{1,0:T(8,128)(2,1)S(1)} %get-tuple-element.83), channel_id=1, source_target_pairs={{0,8},{1,9},{2,10},{3,11},{4,12},{5,13},{6,14},{7,15},{8,0},{9,1},... | collective-permute-start | bytes 786440 | tf_op jit(solution)/shard_map/ppermute | solution.py:291
  64.6 22.3 %collective-permute-start.15 = (bf16[512,512]{1,0:T(8,128)(2,1)S(1)}, bf16[512,512]{1,0:T(8,128)(2,1)S(1)}, u32[]{:S(2)}, u32[]{:S(2)}) collective-permute-start(bf16[512,512]{1,0:T(8,128)(2,1)S(1)} %pair_sum_diagonal.1), channel_id=1, source_target_pairs={{0,6},{1,7},{2,4},{3,5},{4,2},{5,3},{6,0},{7,1},{8,14},{9,15},{10,... | collective-permute-start | bytes 1572872 | tf_op jit(solution)/shard_map/ppermute | solution.py:291
  71.4 14.6 %collective-permute-start.18 = (bf16[128,1024]{1,0:T(8,128)(2,1)S(1)}, bf16[128,1024]{1,0:T(8,128)(2,1)S(1)}, u32[]{:S(2)}, u32[]{:S(2)}) collective-permute-start(bf16[128,1024]{1,0:T(8,128)(2,1)S(1)} %line_sum.1), channel_id=1, source_target_pairs={{0,16},{1,17},{2,18},{3,19},{4,20},{5,21},{6,22},{7,23},{8,24},{9,... | collective-permute-start | bytes 786440 | tf_op jit(solution)/shard_map/ppermute | solution.py:291
  74.0 12.0 %collective-permute-start.16 = (bf16[128,1024]{1,0:T(8,128)(2,1)S(1)}, bf16[128,1024]{1,0:T(8,128)(2,1)S(1)}, u32[]{:S(2)}, u32[]{:S(2)}) collective-permute-start(bf16[128,1024]{1,0:T(8,128)(2,1)S(1)} %get-tuple-element.81), channel_id=1, source_target_pairs={{0,8},{1,9},{2,10},{3,11},{4,12},{5,13},{6,14},{7,15},{8,0},{9,1},... | collective-permute-start | bytes 786440 | tf_op jit(solution)/shard_map/ppermute | solution.py:291

commit v12 on v11

--- a/solution.py
+++ b/solution.py
@@ -179,11 +179,9 @@
     bias_all[:, three:] = bias_last
     w_last[:owned, :] = w_out[two:, :]
     w_last[owned:, :] = w_three[owned:two, :]
-    step = tok.shape[0] // 3
-
-    @pl.loop(0, 3)
-    def _(block):
-        spot = pl.ds(pl.multiple_of(block * step, step), step)
+    step = tok.shape[0] // 6
+    for at in range(6):
+        spot = slice(at * step, (at + 1) * step)
         value, slope = activate(tok[spot, :], w_three[:owned, :], bias_last[0:1, :])
         slope_ref[spot, :] = slope
         act = jnp.concatenate([act_two[spot, :], value.astype(jnp.bfloat16)], axis=1)
@@ -199,15 +197,12 @@
 
 def gradient_kernel(dpre_two, tok, cot, slope, w_three, grad_ref, dpre):
     owned = slope.shape[1]
-    step = tok.shape[0] // 3
-
-    @pl.loop(0, 3)
-    def _(block):
-        spot = pl.ds(pl.multiple_of(block * step, step), step)
+    step = tok.shape[0] // 6
+    for at in range(6):
+        spot = slice(at * step, (at + 1) * step)
         dact = dot_last(cot[spot, :], w_three[owned : 2 * owned, :])
         last = (dact * slope[spot, :]).astype(jnp.bfloat16)
         dpre[spot, :] = jnp.concatenate([dpre_two[spot, :], last], axis=1)
-
     grad_ref[...] = dot_first(dpre[...], tok[...])
 
 
@@ -228,9 +223,8 @@
     run(load, "wait")
     step = rows // 2
 
-    @pl.loop(0, 2)
-    def _(sub):
-        spot = pl.ds(pl.multiple_of(sub * step, step), step)
+    for sub in range(2):
+        spot = slice(sub * step, (sub + 1) * step)
         value, slope = activate(tok[spot, :], w_in[...], bias[0:1, :])
         act = value.astype(jnp.bfloat16)
         dact = dot_last(cot[spot, :], w_out[...])
@@ -330,7 +324,6 @@
 
     bias_rows = jnp.pad(b_in.reshape(1, owned), ((0, BIAS_ROWS - 1), (0, width - owned)))
     own_w = jnp.concatenate([w_in, w_out, bias_rows], 0)
-    own_w, tokens, cotangent = barrier((own_w, tokens, cotangent))
     own = jnp.stack([tokens, cotangent])
     w_two, w_one = to_far(own_w, 2), to_far(own_w, 1)
     from_x, from_y = to_x(own), to_y(own)

time: 88 us -> 85.3 us (0.969)
  Pallas kernels: 18.1 us -> 15.8 us
  other arithmetic: 4.32 us -> 3.33 us
    pallas_call x1, Pallas kernels: 4.05 us -> 2.62 us  [on_device_lines(): pl.pallas_call(functools.partial(output_kernel, owned), out_shape=(bf16(e...]
    concatenate x1, other arithmetic: 1.08 us -> 0.04 us  [on_device_lines(): own_w = jnp.concatenate([w_in, w_out, bias_rows], 0)]
  transfers between devices with their start and end apart: 19 -> 19, of which waited for: 10 -> 10; matrix products, arithmetic and copies ran while one was open for 1% -> 1% of each run, Pallas kernels for 21% -> 19%
where the time goes in v12:
time: 85.3 us; the launch traced here: 85.2 us
  waiting for transfers between devices  42.8 us (50%)
  starting transfers between devices  22.3 us (26%)
  Pallas kernels  15.8 us (19%)
  other arithmetic  3.33 us (4%)
    ppermute x19, waiting for transfers between devices, permute(): return lax.ppermute(value, AXES, pairs)  42.8 us
    ppermute x19, starting transfers between devices, permute(): return lax.ppermute(value, AXES, pairs)  22.3 us
    pallas_call x1, Pallas kernels, on_device_lines(): pl.pallas_call(functools.partial(early_kernel, owned), out_shape=(bf16(ea...  7.44 us
    pallas_call x1, Pallas kernels, on_device_lines(): pl.pallas_call(functools.partial(diagonal_kernel, owned), out_shape=[bf16...  3.14 us
    pallas_call x1, Pallas kernels, on_device_lines(): pl.pallas_call(functools.partial(output_kernel, owned), out_shape=(bf16(e...  2.62 us
    pallas_call x1, Pallas kernels, on_device_lines(): pl.pallas_call(gradient_kernel, out_shape=f32(2 * owned, width), in_specs...  1.82 us
  transfers between devices with their start and end apart: 19, of which 10 were waited for; matrix products, arithmetic and copies ran while one was open for 1% of the time, Pallas kernels for 19%

profile of v12, /device:TPU:0, one launch (start us, length us, event | category | flops | bytes accessed | tf_op | source)
XLA Modules:
  0.0 85.2 jit_solution(13796120933090700374)
XLA Ops:
  0.7 1.4 %pad_maximum_fusion.refs_0_ = bf16[2,512,512]{2,1,0:T(8,128)(2,1)S(1)} fusion(bf16[1,512,512]{2,1,0:T(8,128)(2,1)} %bitcast.7, bf16[1,512,512]{2,1,0:T(8,128)(2,1)} %bitcast.8), kind=kLoop, calls=%fused_computation.2 | loop fusion | flops 524288 | bytes 2097152 | tf_op jit(solution)/shard_map/stack | solution.py:327
  2.0 3.0 %collective-permute-start = (bf16[2,512,512]{2,1,0:T(8,128)(2,1)S(1)}, bf16[2,512,512]{2,1,0:T(8,128)(2,1)S(1)}, u32[]{:S(2)}, u32[]{:S(2)}) collective-permute-start(bf16[2,512,512]{2,1,0:T(8,128)(2,1)S(1)} %pad_maximum_fusion.refs_0_), channel_id=1, source_target_pairs={{0,2},{1,3},{2,0},{3,1},{4,6},{5,7},{6,4},{7,5},{8,10},{9,11},{10,... | collective-permute-start | bytes 3145736 | tf_op jit(solution)/shard_map/ppermute | solution.py:285
  5.0 1.5 %collective-permute-start.1 = (bf16[2,512,512]{2,1,0:T(8,128)(2,1)S(1)}, bf16[2,512,512]{2,1,0:T(8,128)(2,1)S(1)}, u32[]{:S(2)}, u32[]{:S(2)}) collective-permute-start(bf16[2,512,512]{2,1,0:T(8,128)(2,1)S(1)} %pad_maximum_fusion.refs_0_), channel_id=1, source_target_pairs={{0,4},{1,5},{2,6},{3,7},{4,0},{5,1},{6,2},{7,3},{8,12},{9,13},{10,... | collective-permute-start | bytes 3145736 | tf_op jit(solution)/shard_map/ppermute | solution.py:285
  6.6 2.7 %collective-permute-start.6 = (bf16[264,1024]{1,0:T(8,128)(2,1)S(1)}, bf16[264,1024]{1,0:T(8,128)(2,1)S(1)}, u32[]{:S(2)}, u32[]{:S(2)}) collective-permute-start(bf16[264,1024]{1,0:T(8,128)(2,1)S(1)} %fusion.1.refs_6_), channel_id=1, source_target_pairs={{0,16},{1,17},{2,18},{3,19},{4,20},{5,21},{6,22},{7,23},{8,24},{9,... | collective-permute-start | bytes 1622024 | tf_op jit(solution)/shard_map/ppermute | solution.py:285
  9.3 1.6 %collective-permute-start.5 = (bf16[264,1024]{1,0:T(8,128)(2,1)S(1)}, bf16[264,1024]{1,0:T(8,128)(2,1)S(1)}, u32[]{:S(2)}, u32[]{:S(2)}) collective-permute-start(bf16[264,1024]{1,0:T(8,128)(2,1)S(1)} %fusion.1.refs_6_), channel_id=1, source_target_pairs={{0,8},{1,9},{2,10},{3,11},{4,12},{5,13},{6,14},{7,15},{8,0},{9,1},... | collective-permute-start | bytes 1622024 | tf_op jit(solution)/shard_map/ppermute | solution.py:285
  10.8 17.3 %collective-permute-done.refs_2_ = bf16[2,512,512]{2,1,0:T(8,128)(2,1)S(1)} collective-permute-done((bf16[2,512,512]{2,1,0:T(8,128)(2,1)S(1)}, bf16[2,512,512]{2,1,0:T(8,128)(2,1)S(1)}, u32[]{:S(2)}, u32[]{:S(2)}) %collective-permute-start) | collective-permute-done | bytes 1048608 | tf_op jit(solution)/shard_map/ppermute | solution.py:285
  28.2 1.5 %collective-permute-done.1.refs_4_ = bf16[2,512,512]{2,1,0:T(8,128)(2,1)S(1)} collective-permute-done((bf16[2,512,512]{2,1,0:T(8,128)(2,1)S(1)}, bf16[2,512,512]{2,1,0:T(8,128)(2,1)S(1)}, u32[]{:S(2)}, u32[]{:S(2)}) %collective-permute-start.1) | collective-permute-done | bytes 1048608 | tf_op jit(solution)/shard_map/ppermute | solution.py:285
  29.6 0.5 collective-permute-start.4
  30.2 1.6 %collective-permute-start.8 = (bf16[560,512]{1,0:T(8,128)(2,1)S(1)}, bf16[560,512]{1,0:T(8,128)(2,1)S(1)}, u32[]{:S(2)}, u32[]{:S(2)}) collective-permute-start(bf16[560,512]{1,0:T(8,128)(2,1)S(1)} %slice.16), channel_id=1, source_target_pairs={{0,4},{1,5},{2,6},{3,7},{4,0},{5,1},{6,2},{7,3},{8,12},{9,13},{10,... | collective-permute-start | bytes 1720328 | tf_op jit(solution)/shard_map/ppermute | solution.py:285
  31.8 2.1 %collective-permute-done.6.refs_8_ = bf16[264,1024]{1,0:T(8,128)(2,1)S(1)} collective-permute-done((bf16[264,1024]{1,0:T(8,128)(2,1)S(1)}, bf16[264,1024]{1,0:T(8,128)(2,1)S(1)}, u32[]{:S(2)}, u32[]{:S(2)}) %collective-permute-start.6) | collective-permute-done | bytes 540704 | tf_op jit(solution)/shard_map/ppermute | solution.py:285
  33.9 0.5 collective-permute-start.9
  34.5 1.1 %collective-permute-start.7 = (bf16[264,1024]{1,0:T(8,128)(2,1)S(1)}, bf16[264,1024]{1,0:T(8,128)(2,1)S(1)}, u32[]{:S(2)}, u32[]{:S(2)}) collective-permute-start(bf16[264,1024]{1,0:T(8,128)(2,1)S(1)} %collective-permute-done.6.refs_8_), channel_id=1, source_target_pairs={{0,8},{1,9},{2,10},{3,11},{4,12},{5,13},{6,14},{7,15},{8,0},{9,1},... | collective-permute-start | bytes 1622024 | tf_op jit(solution)/shard_map/ppermute | solution.py:285
  35.6 7.4 %early.1 = (bf16[1536,128]{1,0:T(8,128)(2,1)S(1)}, bf16[1536,128]{1,0:T(8,128)(2,1)S(1)}, f32[1536,1024]{1,0:T(8,128)S(1)}, f32[256,1024]{1,0:T(8,128)S(1)}, bf1...) custom-call(bf16[2,512,512]{2,1,0:T(8,128)(2,1)S(1)} %pad_maximum_fu, ...), custom_call_target="tpu_custom_call" | custom-call | flops 786432 | bytes 1536 | tf_op jit(solution)/shard_map/early/pallas_call | solution.py:337
  43.0 5.0 %collective-permute-done.7.refs_6_.w_three = bf16[264,1024]{1,0:T(8,128)(2,1)S(1)} collective-permute-done((bf16[264,1024]{1,0:T(8,128)(2,1)S(1)}, bf16[264,1024]{1,0:T(8,128)(2,1)S(1)}, u32[]{:S(2)}, u32[]{:S(2)}) %collective-permute-start.7) | collective-permute-done | bytes 540704 | tf_op jit(solution)/shard_map/ppermute | solution.py:285
  48.0 2.6 %output.1 = (bf16[1536,512]{1,0:T(8,128)(2,1)S(1)}, bf16[1536,512]{1,0:T(8,128)(2,1)S(1)}, f32[1536,128]{1,0:T(8,128)S(1)}, bf16[512,1024]{1,0:T(8,128)(2,1)S(1)...) custom-call(bf16[1536,128]{1,0:T(8,128)(2,1)S(1)} %get-tuple-element.44.refs_0_, ...), custom_call_target="tpu_custom_call" | custom-call | flops 786432 | bytes 1536 | tf_op jit(solution)/shard_map/output/pallas_call | solution.py:364
  50.9 0.6 collective-permute-start.13
  51.5 1.8 %gradient.1.refs_4_ = f32[256,1024]{1,0:T(8,128)S(1)} custom-call(bf16[1536,128]{1,0:T(8,128)(2,1)S(1)} %get-tuple-element.51.dpre_two, bf16[1536,1024]{1,0:T(8,128)(2,1)S(1)} %get-tuple-element.45.refs_1_.tok, bf16[1536,1024]{1,0:T(8,128)(2,1)S(1)} %get-tuple-element.52.cot, f32[1536,128]{1,0:T(8,128)S(1)} %get-tuple-element.56.slope, ...), custom_call_target="tpu_custom_call" | custom-call | flops 10000000000 | bytes 1536 | tf_op jit(solution)/shard_map/gradient/pallas_call | solution.py:385
  53.3 0.9 %collective-permute-done.10.other_ref = bf16[1536,512]{1,0:T(8,128)(2,1)S(1)} collective-permute-done((bf16[1536,512]{1,0:T(8,128)(2,1)S(1)}, bf16[1536,512]{1,0:T(8,128)(2,1)S(1)}, u32[]{:S(2)}, u32[]{:S(2)}) %collective-permute-start.10) | collective-permute-done | bytes 1572896 | tf_op jit(solution)/shard_map/ppermute | solution.py:285
  54.2 0.4 pair_sum.1
  54.6 1.6 %collective-permute-start.11 = (bf16[528,512]{1,0:T(8,128)(2,1)S(1)}, bf16[528,512]{1,0:T(8,128)(2,1)S(1)}, u32[]{:S(2)}, u32[]{:S(2)}) collective-permute-start(bf16[528,512]{1,0:T(8,128)(2,1)S(1)} %get-tuple-element.61), channel_id=1, source_target_pairs={{0,2},{1,3},{2,0},{3,1},{4,6},{5,7},{6,4},{7,5},{8,10},{9,11},{10,... | collective-permute-start | bytes 1622024 | tf_op jit(solution)/shard_map/ppermute | solution.py:285
  56.1 0.5 collective-permute-start.12
  56.6 3.1 %diagonal.1 = (bf16[512,512]{1,0:T(8,128)(2,1)S(1)}, bf16[512,512]{1,0:T(8,128)(2,1)S(1)}, bf16[128,1024]{1,0:T(8,128)(2,1)S(1)}, bf16[128,1024]{1,0:T(8,128)(2,...) custom-call(bf16[512,1024]{1,0:T(8,128)(2,1)S(1)} %get-tuple-element.63.refs_0_, ...), custom_call_target="tpu_custom_call" | custom-call | flops 1000000 | bytes 512 | tf_op jit(solution)/shard_map/diagonal/pallas_call | solution.py:409
  59.9 1.1 %collective-permute-start.17 = (bf16[128,1024]{1,0:T(8,128)(2,1)S(1)}, bf16[128,1024]{1,0:T(8,128)(2,1)S(1)}, u32[]{:S(2)}, u32[]{:S(2)}) collective-permute-start(bf16[128,1024]{1,0:T(8,128)(2,1)S(1)} %get-tuple-element.77), channel_id=1, source_target_pairs={{0,8},{1,9},{2,10},{3,11},{4,12},{5,13},{6,14},{7,15},{8,0},{9,1},... | collective-permute-start | bytes 786440 | tf_op jit(solution)/shard_map/ppermute | solution.py:285
  60.9 0.8 collective-permute-done.14.other_ref
  61.9 1.6 %collective-permute-start.15 = (bf16[512,512]{1,0:T(8,128)(2,1)S(1)}, bf16[512,512]{1,0:T(8,128)(2,1)S(1)}, u32[]{:S(2)}, u32[]{:S(2)}) collective-permute-start(bf16[512,512]{1,0:T(8,128)(2,1)S(1)} %pair_sum_diagonal.1), channel_id=1, source_target_pairs={{0,6},{1,7},{2,4},{3,5},{4,2},{5,3},{6,0},{7,1},{8,14},{9,15},{10,... | collective-permute-start | bytes 1572872 | tf_op jit(solution)/shard_map/ppermute | solution.py:285
  63.4 5.1 %collective-permute-done.17.other_ref = bf16[128,1024]{1,0:T(8,128)(2,1)S(1)} collective-permute-done((bf16[128,1024]{1,0:T(8,128)(2,1)S(1)}, bf16[128,1024]{1,0:T(8,128)(2,1)S(1)}, u32[]{:S(2)}, u32[]{:S(2)}) %collective-permute-start.17) | collective-permute-done | bytes 262176 | tf_op jit(solution)/shard_map/ppermute | solution.py:285
  68.6 2.7 %collective-permute-start.18 = (bf16[128,1024]{1,0:T(8,128)(2,1)S(1)}, bf16[128,1024]{1,0:T(8,128)(2,1)S(1)}, u32[]{:S(2)}, u32[]{:S(2)}) collective-permute-start(bf16[128,1024]{1,0:T(8,128)(2,1)S(1)} %line_sum.1), channel_id=1, source_target_pairs={{0,16},{1,17},{2,18},{3,19},{4,20},{5,21},{6,22},{7,23},{8,24},{9,... | collective-permute-start | bytes 786440 | tf_op jit(solution)/shard_map/ppermute | solution.py:285
  71.3 1.7 %collective-permute-start.16 = (bf16[128,1024]{1,0:T(8,128)(2,1)S(1)}, bf16[128,1024]{1,0:T(8,128)(2,1)S(1)}, u32[]{:S(2)}, u32[]{:S(2)}) collective-permute-start(bf16[128,1024]{1,0:T(8,128)(2,1)S(1)} %get-tuple-element.75), channel_id=1, source_target_pairs={{0,8},{1,9},{2,10},{3,11},{4,12},{5,13},{6,14},{7,15},{8,0},{9,1},... | collective-permute-start | bytes 786440 | tf_op jit(solution)/shard_map/ppermute | solution.py:285
  73.1 8.3 %collective-permute-done.12.y_ref = bf16[528,512]{1,0:T(8,128)(2,1)S(1)} collective-permute-done((bf16[528,512]{1,0:T(8,128)(2,1)S(1)}, bf16[528,512]{1,0:T(8,128)(2,1)S(1)}, u32[]{:S(2)}, u32[]{:S(2)}) %collective-permute-start.12) | collective-permute-done | bytes 540704 | tf_op jit(solution)/shard_map/ppermute | solution.py:285
  81.6 1.6 %collective-permute-done.18 = bf16[128,1024]{1,0:T(8,128)(2,1)S(1)} collective-permute-done((bf16[128,1024]{1,0:T(8,128)(2,1)S(1)}, bf16[128,1024]{1,0:T(8,128)(2,1)S(1)}, u32[]{:S(2)}, u32[]{:S(2)}) %collective-permute-start.18) | collective-permute-done | bytes 262176 | tf_op jit(solution)/shard_map/ppermute | solution.py:285
  83.3 0.9 %add_multiply_fusion = f32[128,1024]{1,0:T(8,128)} fusion(bf16[128,1024]{1,0:T(8,128)(2,1)S(1)} %collective-permute-done.18, bf16[128,1024]{1,0:T(8,128)(2,1)S(1)} %collective-permute-done.16, bf16[128,1024]{1,0:T(8,128)(2,1)S(1)} %get-tuple-element.72), kind=kLoop, calls=%fused_computation.6 | loop fusion | flops 786432 | bytes 1310720 | tf_op jit(solution)/shard_map/mul | solution.py:467
  84.2 1.0 %add_convert_fusion = bf16[512,512]{1,0:T(8,128)(2,1)} fusion(f32[512,512]{1,0:T(8,128)S(1)} %plane_sum.1, bf16[512,512]{1,0:T(8,128)(2,1)S(1)} %collective-permute-done.15), kind=kLoop, calls=%fused_computation.4 | loop fusion | flops 786432 | bytes 2097152 | tf_op jit(solution)/shard_map/convert_element_type | solution.py:466
  (29 shorter events, 0.9 us)
Async XLA Ops:
  0.6 5.9 %copy-start.2 = (bf16[128]{0:T(256)(128)(2,1)S(1)}, bf16[128]{0:T(256)(128)(2,1)}, u32[]{:S(2)}) copy-start(bf16[128]{0:T(256)(128)(2,1)} %param.8) | copy-start | bytes 772
  0.6 5.9 %copy-start.1 = (bf16[128,1024]{1,0:T(8,128)(2,1)S(1)}, bf16[128,1024]{1,0:T(8,128)(2,1)}, u32[]{:S(2)}) copy-start(bf16[128,1024]{1,0:T(8,128)(2,1)} %param.7) | copy-start | bytes 786436
  0.7 5.9 %copy-start = (bf16[128,1024]{1,0:T(8,128)(2,1)S(1)}, bf16[128,1024]{1,0:T(8,128)(2,1)}, u32[]{:S(2)}) copy-start(bf16[128,1024]{1,0:T(8,128)(2,1)} %param.9) | copy-start | bytes 786436
  2.0 26.2 %collective-permute-start = (bf16[2,512,512]{2,1,0:T(8,128)(2,1)S(1)}, bf16[2,512,512]{2,1,0:T(8,128)(2,1)S(1)}, u32[]{:S(2)}, u32[]{:S(2)}) collective-permute-start(bf16[2,512,512]{2,1,0:T(8,128)(2,1)S(1)} %pad_maximum_fusion.refs_0_), channel_id=1, source_target_pairs={{0,2},{1,3},{2,0},{3,1},{4,6},{5,7},{6,4},{7,5},{8,10},{9,11},{10,... | collective-permute-start | bytes 3145736 | tf_op jit(solution)/shard_map/ppermute | solution.py:285
  5.0 24.6 %collective-permute-start.1 = (bf16[2,512,512]{2,1,0:T(8,128)(2,1)S(1)}, bf16[2,512,512]{2,1,0:T(8,128)(2,1)S(1)}, u32[]{:S(2)}, u32[]{:S(2)}) collective-permute-start(bf16[2,512,512]{2,1,0:T(8,128)(2,1)S(1)} %pad_maximum_fusion.refs_0_), channel_id=1, source_target_pairs={{0,4},{1,5},{2,6},{3,7},{4,0},{5,1},{6,2},{7,3},{8,12},{9,13},{10,... | collective-permute-start | bytes 3145736 | tf_op jit(solution)/shard_map/ppermute | solution.py:285
  6.5 23.1 %collective-permute-start.2 = (bf16[2,512,512]{2,1,0:T(8,128)(2,1)S(1)}, bf16[2,512,512]{2,1,0:T(8,128)(2,1)S(1)}, u32[]{:S(2)}, u32[]{:S(2)}) collective-permute-start(bf16[2,512,512]{2,1,0:T(8,128)(2,1)S(1)} %pad_maximum_fusion.refs_0_), channel_id=1, source_target_pairs={{0,1},{1,0},{2,3},{3,2},{4,5},{5,4},{6,7},{7,6},{8,9},{9,8},{10,11... | collective-permute-start | bytes 3145736 | tf_op jit(solution)/shard_map/ppermute | solution.py:285
  6.6 27.3 %collective-permute-start.6 = (bf16[264,1024]{1,0:T(8,128)(2,1)S(1)}, bf16[264,1024]{1,0:T(8,128)(2,1)S(1)}, u32[]{:S(2)}, u32[]{:S(2)}) collective-permute-start(bf16[264,1024]{1,0:T(8,128)(2,1)S(1)} %fusion.1.refs_6_), channel_id=1, source_target_pairs={{0,16},{1,17},{2,18},{3,19},{4,20},{5,21},{6,22},{7,23},{8,24},{9,... | collective-permute-start | bytes 1622024 | tf_op jit(solution)/shard_map/ppermute | solution.py:285
  9.3 25.2 %collective-permute-start.5 = (bf16[264,1024]{1,0:T(8,128)(2,1)S(1)}, bf16[264,1024]{1,0:T(8,128)(2,1)S(1)}, u32[]{:S(2)}, u32[]{:S(2)}) collective-permute-start(bf16[264,1024]{1,0:T(8,128)(2,1)S(1)} %fusion.1.refs_6_), channel_id=1, source_target_pairs={{0,8},{1,9},{2,10},{3,11},{4,12},{5,13},{6,14},{7,15},{8,0},{9,1},... | collective-permute-start | bytes 1622024 | tf_op jit(solution)/shard_map/ppermute | solution.py:285
  29.6 5.9 %collective-permute-start.3 = (bf16[2,512,512]{2,1,0:T(8,128)(2,1)S(1)}, bf16[2,512,512]{2,1,0:T(8,128)(2,1)S(1)}, u32[]{:S(2)}, u32[]{:S(2)}) collective-permute-start(bf16[2,512,512]{2,1,0:T(8,128)(2,1)S(1)} %collective-permute-done.refs_2_), channel_id=1, source_target_pairs={{0,1},{1,0},{2,3},{3,2},{4,5},{5,4},{6,7},{7,6},{8,9},{9,8},{10,11... | collective-permute-start | bytes 3145736 | tf_op jit(solution)/shard_map/ppermute | solution.py:285
  29.6 5.9 %collective-permute-start.4 = (bf16[2,512,512]{2,1,0:T(8,128)(2,1)S(1)}, bf16[2,512,512]{2,1,0:T(8,128)(2,1)S(1)}, u32[]{:S(2)}, u32[]{:S(2)}) collective-permute-start(bf16[2,512,512]{2,1,0:T(8,128)(2,1)S(1)} %collective-permute-done.1.refs_4_), channel_id=1, source_target_pairs={{0,1},{1,0},{2,3},{3,2},{4,5},{5,4},{6,7},{7,6},{8,9},{9,8},{10,11... | collective-permute-start | bytes 3145736 | tf_op jit(solution)/shard_map/ppermute | solution.py:285
  30.2 20.5 %collective-permute-start.8 = (bf16[560,512]{1,0:T(8,128)(2,1)S(1)}, bf16[560,512]{1,0:T(8,128)(2,1)S(1)}, u32[]{:S(2)}, u32[]{:S(2)}) collective-permute-start(bf16[560,512]{1,0:T(8,128)(2,1)S(1)} %slice.16), channel_id=1, source_target_pairs={{0,4},{1,5},{2,6},{3,7},{4,0},{5,1},{6,2},{7,3},{8,12},{9,13},{10,... | collective-permute-start | bytes 1720328 | tf_op jit(solution)/shard_map/ppermute | solution.py:285
  33.9 16.7 %collective-permute-start.9 = (bf16[560,512]{1,0:T(8,128)(2,1)S(1)}, bf16[560,512]{1,0:T(8,128)(2,1)S(1)}, u32[]{:S(2)}, u32[]{:S(2)}) collective-permute-start(bf16[560,512]{1,0:T(8,128)(2,1)S(1)} %slice.17), channel_id=1, source_target_pairs={{0,2},{1,3},{2,0},{3,1},{4,6},{5,7},{6,4},{7,5},{8,10},{9,11},{10,... | collective-permute-start | bytes 1720328 | tf_op jit(solution)/shard_map/ppermute | solution.py:285
  34.5 13.6 %collective-permute-start.7 = (bf16[264,1024]{1,0:T(8,128)(2,1)S(1)}, bf16[264,1024]{1,0:T(8,128)(2,1)S(1)}, u32[]{:S(2)}, u32[]{:S(2)}) collective-permute-start(bf16[264,1024]{1,0:T(8,128)(2,1)S(1)} %collective-permute-done.6.refs_8_), channel_id=1, source_target_pairs={{0,8},{1,9},{2,10},{3,11},{4,12},{5,13},{6,14},{7,15},{8,0},{9,1},... | collective-permute-start | bytes 1622024 | tf_op jit(solution)/shard_map/ppermute | solution.py:285
  50.7 3.5 %collective-permute-start.10 = (bf16[1536,512]{1,0:T(8,128)(2,1)S(1)}, bf16[1536,512]{1,0:T(8,128)(2,1)S(1)}, u32[]{:S(2)}, u32[]{:S(2)}) collective-permute-start(bf16[1536,512]{1,0:T(8,128)(2,1)S(1)} %get-tuple-element.58), channel_id=1, source_target_pairs={{0,1},{1,0},{2,3},{3,2},{4,5},{5,4},{6,7},{7,6},{8,9},{9,8},{10,11... | collective-permute-start | bytes 4718600 | tf_op jit(solution)/shard_map/ppermute | solution.py:285
  50.9 5.7 %collective-permute-start.13 = (bf16[1024,512]{1,0:T(8,128)(2,1)S(1)}, bf16[1024,512]{1,0:T(8,128)(2,1)S(1)}, u32[]{:S(2)}, u32[]{:S(2)}) collective-permute-start(bf16[1024,512]{1,0:T(8,128)(2,1)S(1)} %pad_maximum_fusion.1), channel_id=1, source_target_pairs={{0,1},{1,0},{2,3},{3,2},{4,5},{5,4},{6,7},{7,6},{8,9},{9,8},{10,11... | collective-permute-start | bytes 3145736 | tf_op jit(solution)/shard_map/ppermute | solution.py:285
  54.6 18.5 %collective-permute-start.11 = (bf16[528,512]{1,0:T(8,128)(2,1)S(1)}, bf16[528,512]{1,0:T(8,128)(2,1)S(1)}, u32[]{:S(2)}, u32[]{:S(2)}) collective-permute-start(bf16[528,512]{1,0:T(8,128)(2,1)S(1)} %get-tuple-element.61), channel_id=1, source_target_pairs={{0,2},{1,3},{2,0},{3,1},{4,6},{5,7},{6,4},{7,5},{8,10},{9,11},{10,... | collective-permute-start | bytes 1622024 | tf_op jit(solution)/shard_map/ppermute | solution.py:285
  56.1 25.3 %collective-permute-start.12 = (bf16[528,512]{1,0:T(8,128)(2,1)S(1)}, bf16[528,512]{1,0:T(8,128)(2,1)S(1)}, u32[]{:S(2)}, u32[]{:S(2)}) collective-permute-start(bf16[528,512]{1,0:T(8,128)(2,1)S(1)} %get-tuple-element.62), channel_id=1, source_target_pairs={{0,4},{1,5},{2,6},{3,7},{4,0},{5,1},{6,2},{7,3},{8,12},{9,13},{10,... | collective-permute-start | bytes 1622024 | tf_op jit(solution)/shard_map/ppermute | solution.py:285
  59.8 2.0 %collective-permute-start.14 = (bf16[512,512]{1,0:T(8,128)(2,1)S(1)}, bf16[512,512]{1,0:T(8,128)(2,1)S(1)}, u32[]{:S(2)}, u32[]{:S(2)}) collective-permute-start(bf16[512,512]{1,0:T(8,128)(2,1)S(1)} %get-tuple-element.71), channel_id=1, source_target_pairs={{0,1},{1,0},{2,3},{3,2},{4,5},{5,4},{6,7},{7,6},{8,9},{9,8},{10,11... | collective-permute-start | bytes 1572872 | tf_op jit(solution)/shard_map/ppermute | solution.py:285
  59.9 8.7 %collective-permute-start.17 = (bf16[128,1024]{1,0:T(8,128)(2,1)S(1)}, bf16[128,1024]{1,0:T(8,128)(2,1)S(1)}, u32[]{:S(2)}, u32[]{:S(2)}) collective-permute-start(bf16[128,1024]{1,0:T(8,128)(2,1)S(1)} %get-tuple-element.77), channel_id=1, source_target_pairs={{0,8},{1,9},{2,10},{3,11},{4,12},{5,13},{6,14},{7,15},{8,0},{9,1},... | collective-permute-start | bytes 786440 | tf_op jit(solution)/shard_map/ppermute | solution.py:285
  61.9 22.3 %collective-permute-start.15 = (bf16[512,512]{1,0:T(8,128)(2,1)S(1)}, bf16[512,512]{1,0:T(8,128)(2,1)S(1)}, u32[]{:S(2)}, u32[]{:S(2)}) collective-permute-start(bf16[512,512]{1,0:T(8,128)(2,1)S(1)} %pair_sum_diagonal.1), channel_id=1, source_target_pairs={{0,6},{1,7},{2,4},{3,5},{4,2},{5,3},{6,0},{7,1},{8,14},{9,15},{10,... | collective-permute-start | bytes 1572872 | tf_op jit(solution)/shard_map/ppermute | solution.py:285
  68.6 14.6 %collective-permute-start.18 = (bf16[128,1024]{1,0:T(8,128)(2,1)S(1)}, bf16[128,1024]{1,0:T(8,128)(2,1)S(1)}, u32[]{:S(2)}, u32[]{:S(2)}) collective-permute-start(bf16[128,1024]{1,0:T(8,128)(2,1)S(1)} %line_sum.1), channel_id=1, source_target_pairs={{0,16},{1,17},{2,18},{3,19},{4,20},{5,21},{6,22},{7,23},{8,24},{9,... | collective-permute-start | bytes 786440 | tf_op jit(solution)/shard_map/ppermute | solution.py:285
  71.3 11.9 %collective-permute-start.16 = (bf16[128,1024]{1,0:T(8,128)(2,1)S(1)}, bf16[128,1024]{1,0:T(8,128)(2,1)S(1)}, u32[]{:S(2)}, u32[]{:S(2)}) collective-permute-start(bf16[128,1024]{1,0:T(8,128)(2,1)S(1)} %get-tuple-element.75), channel_id=1, source_target_pairs={{0,8},{1,9},{2,10},{3,11},{4,12},{5,13},{6,14},{7,15},{8,0},{9,1},... | collective-permute-start | bytes 786440 | tf_op jit(solution)/shard_map/ppermute | solution.py:285

commit v13 on v12

--- a/solution.py
+++ b/solution.py
@@ -216,23 +216,24 @@
     two = 2 * owned
     first, second = pl.ds(0, rows), pl.ds(rows, rows)
     load = side_by_side(core, (tok_ref.at[first], far_ref.at[first]), tok, 0, tok_sem)
-    load += side_by_side(
-        core, (cot_ref.at[pl.ds(EXTRA, rows)], far_ref.at[second]), cot, 0, cot_sem
-    )
-    run(load, "start")
+    cot_load = side_by_side(core, (cot_ref, far_ref.at[second]), cot, 0, cot_sem)
+    run(load + cot_load, "start")
     run(load, "wait")
     step = rows // 2
-
+    slopes = []
     for sub in range(2):
         spot = slice(sub * step, (sub + 1) * step)
         value, slope = activate(tok[spot, :], w_in[...], bias[0:1, :])
+        slopes.append(slope)
         act = value.astype(jnp.bfloat16)
-        dact = dot_last(cot[spot, :], w_out[...])
-        dpre[spot, :] = (dact * slope).astype(jnp.bfloat16)
         for shift, ref in enumerate((mine_ref, other_ref)):
             ref[spot, :] = jnp.dot(
                 act, w_out[:, half_columns(core, shift, feats)], preferred_element_type=jnp.float32
             ).astype(jnp.bfloat16)
+    run(cot_load, "wait")
+    for sub in range(2):
+        spot = slice(sub * step, (sub + 1) * step)
+        dpre[spot, :] = (dot_last(cot[spot, :], w_out[...]) * slopes[sub]).astype(jnp.bfloat16)
 
     grad = grad_last[...] + dot_first(dpre[:, two:], tok[...])
     two_ref[...] = grad[:owned].astype(jnp.bfloat16)
@@ -330,7 +331,7 @@
     own_other = to_core(own)
     from_x, from_y, own_other = barrier((from_x, from_y, own_other))
     tok_diag = to_y(from_x.reshape(2 * rows, feats)[: rows + EXTRA])
-    cot_diag = to_x(from_y.reshape(2 * rows, feats)[rows - EXTRA :])
+    cot_diag = to_x(from_y[1])
     x_other, y_other = to_core(from_x), to_core(from_y)
     w_three = to_far(w_two, 1)
     act_two, dpre_two, mixed_terms, grad_terms, tok, cot, w_in_three, w_out_three, bias = (
@@ -380,7 +381,7 @@
     )(act_two, tok, mixed_terms, w_in_three, w_out_three, bias, w_three)
     tok_diag, cot_diag, other = barrier((tok_diag, cot_diag, other))
     received = to_core(other)
-    diag_other = to_core(jnp.concatenate([tok_diag[:rows], cot_diag[EXTRA:]]))
+    diag_other = to_core(jnp.concatenate([tok_diag[:rows], cot_diag]))
     slope, tok_diag = barrier((slope, tok_diag))
     grad_last = pl.pallas_call(
         gradient_kernel,
@@ -449,11 +450,6 @@
         name="line_sum",
     )(grad_two, relayed)
     from_two = to_far(line_sum, 2)
-    total = (
-        grad_own.astype(jnp.float32)
-        + from_one.astype(jnp.float32)
-        + from_two.astype(jnp.float32)
-    )
     mixed = pl.pallas_call(
         plane_kernel,
         out_shape=f32(rows, feats),
@@ -464,6 +460,12 @@
         name="plane_sum",
     )(mixed_own, mixed_x, mixed_y)
     mixed = (mixed + mixed_diag.astype(jnp.float32)).astype(jnp.bfloat16)
+    from_two, mixed = barrier((from_two, mixed))
+    total = (
+        grad_own.astype(jnp.float32)
+        + from_one.astype(jnp.float32)
+        + from_two.astype(jnp.float32)
+    )
     return (mixed, total * scale)
 
 

time: 85.3 us -> 83.9 us (0.984)
  starting transfers between devices: 22.3 us -> 20.5 us
    ppermute x19, starting transfers between devices: 22.3 us -> 20.5 us  [permute(): return lax.ppermute(value, AXES, pairs)]
where the time goes in v13:
time: 83.9 us; the launch traced here: 83.8 us
  waiting for transfers between devices  42.7 us (51%)
  starting transfers between devices  20.5 us (24%)
  Pallas kernels  16.3 us (19%)
  other arithmetic  3.33 us (4%)
    ppermute x19, waiting for transfers between devices, permute(): return lax.ppermute(value, AXES, pairs)  42.7 us
    ppermute x19, starting transfers between devices, permute(): return lax.ppermute(value, AXES, pairs)  20.5 us
    pallas_call x1, Pallas kernels, on_device_lines(): pl.pallas_call(functools.partial(early_kernel, owned), out_shape=(bf16(ea...  7.43 us
    pallas_call x1, Pallas kernels, on_device_lines(): pl.pallas_call(functools.partial(diagonal_kernel, owned), out_shape=[bf16...  3.71 us
    pallas_call x1, Pallas kernels, on_device_lines(): pl.pallas_call(functools.partial(output_kernel, owned), out_shape=(bf16(e...  2.62 us
    pallas_call x1, Pallas kernels, on_device_lines(): pl.pallas_call(gradient_kernel, out_shape=f32(2 * owned, width), in_specs...  1.81 us
  transfers between devices with their start and end apart: 19, of which 10 were waited for; matrix products, arithmetic and copies ran while one was open for 1% of the time, Pallas kernels for 19%

profile of v13, /device:TPU:0, one launch (start us, length us, event | category | flops | bytes accessed | tf_op | source)
XLA Modules:
  0.0 83.8 jit_solution(11819510637136355666)
XLA Ops:
  0.7 1.4 %pad_maximum_fusion.refs_0_ = bf16[2,512,512]{2,1,0:T(8,128)(2,1)S(1)} fusion(bf16[1,512,512]{2,1,0:T(8,128)(2,1)} %bitcast.7, bf16[1,512,512]{2,1,0:T(8,128)(2,1)} %bitcast.8), kind=kLoop, calls=%fused_computation.2 | loop fusion | flops 524288 | bytes 2097152 | tf_op jit(solution)/shard_map/stack | solution.py:328
  2.0 3.0 %collective-permute-start = (bf16[2,512,512]{2,1,0:T(8,128)(2,1)S(1)}, bf16[2,512,512]{2,1,0:T(8,128)(2,1)S(1)}, u32[]{:S(2)}, u32[]{:S(2)}) collective-permute-start(bf16[2,512,512]{2,1,0:T(8,128)(2,1)S(1)} %pad_maximum_fusion.refs_0_), channel_id=1, source_target_pairs={{0,2},{1,3},{2,0},{3,1},{4,6},{5,7},{6,4},{7,5},{8,10},{9,11},{10,... | collective-permute-start | bytes 3145736 | tf_op jit(solution)/shard_map/ppermute | solution.py:286
  5.0 1.5 %collective-permute-start.1 = (bf16[2,512,512]{2,1,0:T(8,128)(2,1)S(1)}, bf16[2,512,512]{2,1,0:T(8,128)(2,1)S(1)}, u32[]{:S(2)}, u32[]{:S(2)}) collective-permute-start(bf16[2,512,512]{2,1,0:T(8,128)(2,1)S(1)} %pad_maximum_fusion.refs_0_), channel_id=1, source_target_pairs={{0,4},{1,5},{2,6},{3,7},{4,0},{5,1},{6,2},{7,3},{8,12},{9,13},{10,... | collective-permute-start | bytes 3145736 | tf_op jit(solution)/shard_map/ppermute | solution.py:286
  6.6 2.7 %collective-permute-start.6 = (bf16[264,1024]{1,0:T(8,128)(2,1)S(1)}, bf16[264,1024]{1,0:T(8,128)(2,1)S(1)}, u32[]{:S(2)}, u32[]{:S(2)}) collective-permute-start(bf16[264,1024]{1,0:T(8,128)(2,1)S(1)} %fusion.1.refs_6_), channel_id=1, source_target_pairs={{0,16},{1,17},{2,18},{3,19},{4,20},{5,21},{6,22},{7,23},{8,24},{9,... | collective-permute-start | bytes 1622024 | tf_op jit(solution)/shard_map/ppermute | solution.py:286
  9.3 1.6 %collective-permute-start.5 = (bf16[264,1024]{1,0:T(8,128)(2,1)S(1)}, bf16[264,1024]{1,0:T(8,128)(2,1)S(1)}, u32[]{:S(2)}, u32[]{:S(2)}) collective-permute-start(bf16[264,1024]{1,0:T(8,128)(2,1)S(1)} %fusion.1.refs_6_), channel_id=1, source_target_pairs={{0,8},{1,9},{2,10},{3,11},{4,12},{5,13},{6,14},{7,15},{8,0},{9,1},... | collective-permute-start | bytes 1622024 | tf_op jit(solution)/shard_map/ppermute | solution.py:286
  10.8 17.3 %collective-permute-done.refs_2_ = bf16[2,512,512]{2,1,0:T(8,128)(2,1)S(1)} collective-permute-done((bf16[2,512,512]{2,1,0:T(8,128)(2,1)S(1)}, bf16[2,512,512]{2,1,0:T(8,128)(2,1)S(1)}, u32[]{:S(2)}, u32[]{:S(2)}) %collective-permute-start) | collective-permute-done | bytes 1048608 | tf_op jit(solution)/shard_map/ppermute | solution.py:286
  28.2 1.5 %collective-permute-done.1.refs_4_ = bf16[2,512,512]{2,1,0:T(8,128)(2,1)S(1)} collective-permute-done((bf16[2,512,512]{2,1,0:T(8,128)(2,1)S(1)}, bf16[2,512,512]{2,1,0:T(8,128)(2,1)S(1)}, u32[]{:S(2)}, u32[]{:S(2)}) %collective-permute-start.1) | collective-permute-done | bytes 1048608 | tf_op jit(solution)/shard_map/ppermute | solution.py:286
  29.6 0.5 collective-permute-start.4
  30.2 3.8 %collective-permute-done.6.refs_8_ = bf16[264,1024]{1,0:T(8,128)(2,1)S(1)} collective-permute-done((bf16[264,1024]{1,0:T(8,128)(2,1)S(1)}, bf16[264,1024]{1,0:T(8,128)(2,1)S(1)}, u32[]{:S(2)}, u32[]{:S(2)}) %collective-permute-start.6) | collective-permute-done | bytes 540704 | tf_op jit(solution)/shard_map/ppermute | solution.py:286
  33.9 0.6 collective-permute-start.7
  34.6 0.6 collective-permute-start.8
  35.2 0.6 collective-permute-start.9
  35.8 7.4 %early.1 = (bf16[1536,128]{1,0:T(8,128)(2,1)S(1)}, bf16[1536,128]{1,0:T(8,128)(2,1)S(1)}, f32[1536,1024]{1,0:T(8,128)S(1)}, f32[256,1024]{1,0:T(8,128)S(1)}, bf1...) custom-call(bf16[2,512,512]{2,1,0:T(8,128)(2,1)S(1)} %pad_maximum_fu, ...), custom_call_target="tpu_custom_call" | custom-call | flops 786432 | bytes 1536 | tf_op jit(solution)/shard_map/early/pallas_call | solution.py:338
  43.2 4.5 %collective-permute-done.7.refs_6_.w_three = bf16[264,1024]{1,0:T(8,128)(2,1)S(1)} collective-permute-done((bf16[264,1024]{1,0:T(8,128)(2,1)S(1)}, bf16[264,1024]{1,0:T(8,128)(2,1)S(1)}, u32[]{:S(2)}, u32[]{:S(2)}) %collective-permute-start.7) | collective-permute-done | bytes 540704 | tf_op jit(solution)/shard_map/ppermute | solution.py:286
  47.8 2.6 %output.1 = (bf16[1536,512]{1,0:T(8,128)(2,1)S(1)}, bf16[1536,512]{1,0:T(8,128)(2,1)S(1)}, f32[1536,128]{1,0:T(8,128)S(1)}, bf16[512,1024]{1,0:T(8,128)(2,1)S(1)...) custom-call(bf16[1536,128]{1,0:T(8,128)(2,1)S(1)} %get-tuple-element.45.refs_0_, ...), custom_call_target="tpu_custom_call" | custom-call | flops 786432 | bytes 1536 | tf_op jit(solution)/shard_map/output/pallas_call | solution.py:365
  50.6 0.6 collective-permute-start.11
  51.2 1.8 %gradient.1.refs_4_ = f32[256,1024]{1,0:T(8,128)S(1)} custom-call(bf16[1536,128]{1,0:T(8,128)(2,1)S(1)} %get-tuple-element.56.dpre_two, bf16[1536,1024]{1,0:T(8,128)(2,1)S(1)} %get-tuple-element.46.refs_1_.tok, bf16[1536,1024]{1,0:T(8,128)(2,1)S(1)} %get-tuple-element.57.cot, f32[1536,128]{1,0:T(8,128)S(1)} %get-tuple-element.61.slope, ...), custom_call_target="tpu_custom_call" | custom-call | flops 10000000000 | bytes 1536 | tf_op jit(solution)/shard_map/gradient/pallas_call | solution.py:386
  53.0 0.9 %collective-permute-done.10.other_ref = bf16[1536,512]{1,0:T(8,128)(2,1)S(1)} collective-permute-done((bf16[1536,512]{1,0:T(8,128)(2,1)S(1)}, bf16[1536,512]{1,0:T(8,128)(2,1)S(1)}, u32[]{:S(2)}, u32[]{:S(2)}) %collective-permute-start.10) | collective-permute-done | bytes 1572896 | tf_op jit(solution)/shard_map/ppermute | solution.py:286
  53.9 0.4 pair_sum.1
  54.3 0.6 collective-permute-start.15
  54.9 0.7 collective-permute-start.16
  55.6 3.7 %diagonal.1 = (bf16[512,512]{1,0:T(8,128)(2,1)S(1)}, bf16[512,512]{1,0:T(8,128)(2,1)S(1)}, bf16[128,1024]{1,0:T(8,128)(2,1)S(1)}, bf16[128,1024]{1,0:T(8,128)(2,...) custom-call(bf16[512,1024]{1,0:T(8,128)(2,1)S(1)} %get-tuple-element.51.refs_0_, ...), custom_call_target="tpu_custom_call" | custom-call | flops 1000000 | bytes 512 | tf_op jit(solution)/shard_map/diagonal/pallas_call | solution.py:410
  59.4 0.9 %collective-permute-start.13 = (bf16[128,1024]{1,0:T(8,128)(2,1)S(1)}, bf16[128,1024]{1,0:T(8,128)(2,1)S(1)}, u32[]{:S(2)}, u32[]{:S(2)}) collective-permute-start(bf16[128,1024]{1,0:T(8,128)(2,1)S(1)} %get-tuple-element.74), channel_id=1, source_target_pairs={{0,8},{1,9},{2,10},{3,11},{4,12},{5,13},{6,14},{7,15},{8,0},{9,1},... | collective-permute-start | bytes 786440 | tf_op jit(solution)/shard_map/ppermute | solution.py:286
  60.3 1.0 %collective-permute-done.12.other_ref = bf16[512,512]{1,0:T(8,128)(2,1)S(1)} collective-permute-done((bf16[512,512]{1,0:T(8,128)(2,1)S(1)}, bf16[512,512]{1,0:T(8,128)(2,1)S(1)}, u32[]{:S(2)}, u32[]{:S(2)}) %collective-permute-start.12) | collective-permute-done | bytes 524320 | tf_op jit(solution)/shard_map/ppermute | solution.py:286
  61.4 2.4 %collective-permute-start.17 = (bf16[512,512]{1,0:T(8,128)(2,1)S(1)}, bf16[512,512]{1,0:T(8,128)(2,1)S(1)}, u32[]{:S(2)}, u32[]{:S(2)}) collective-permute-start(bf16[512,512]{1,0:T(8,128)(2,1)S(1)} %pair_sum_diagonal.1), channel_id=1, source_target_pairs={{0,6},{1,7},{2,4},{3,5},{4,2},{5,3},{6,0},{7,1},{8,14},{9,15},{10,... | collective-permute-start | bytes 1572872 | tf_op jit(solution)/shard_map/ppermute | solution.py:286
  63.8 4.3 %collective-permute-done.13.other_ref = bf16[128,1024]{1,0:T(8,128)(2,1)S(1)} collective-permute-done((bf16[128,1024]{1,0:T(8,128)(2,1)S(1)}, bf16[128,1024]{1,0:T(8,128)(2,1)S(1)}, u32[]{:S(2)}, u32[]{:S(2)}) %collective-permute-start.13) | collective-permute-done | bytes 262176 | tf_op jit(solution)/shard_map/ppermute | solution.py:286
  68.2 2.5 %collective-permute-start.14 = (bf16[128,1024]{1,0:T(8,128)(2,1)S(1)}, bf16[128,1024]{1,0:T(8,128)(2,1)S(1)}, u32[]{:S(2)}, u32[]{:S(2)}) collective-permute-start(bf16[128,1024]{1,0:T(8,128)(2,1)S(1)} %line_sum.1), channel_id=1, source_target_pairs={{0,16},{1,17},{2,18},{3,19},{4,20},{5,21},{6,22},{7,23},{8,24},{9,... | collective-permute-start | bytes 786440 | tf_op jit(solution)/shard_map/ppermute | solution.py:286
  70.7 1.7 %collective-permute-start.18 = (bf16[128,1024]{1,0:T(8,128)(2,1)S(1)}, bf16[128,1024]{1,0:T(8,128)(2,1)S(1)}, u32[]{:S(2)}, u32[]{:S(2)}) collective-permute-start(bf16[128,1024]{1,0:T(8,128)(2,1)S(1)} %get-tuple-element.80), channel_id=1, source_target_pairs={{0,8},{1,9},{2,10},{3,11},{4,12},{5,13},{6,14},{7,15},{8,0},{9,1},... | collective-permute-start | bytes 786440 | tf_op jit(solution)/shard_map/ppermute | solution.py:286
  72.4 7.8 %collective-permute-done.16.y_ref = bf16[528,512]{1,0:T(8,128)(2,1)S(1)} collective-permute-done((bf16[528,512]{1,0:T(8,128)(2,1)S(1)}, bf16[528,512]{1,0:T(8,128)(2,1)S(1)}, u32[]{:S(2)}, u32[]{:S(2)}) %collective-permute-start.16) | collective-permute-done | bytes 540704 | tf_op jit(solution)/shard_map/ppermute | solution.py:286
  80.4 1.0 %add_convert_fusion = bf16[512,512]{1,0:T(8,128)(2,1)} fusion(f32[512,512]{1,0:T(8,128)S(1)} %plane_sum.1, bf16[512,512]{1,0:T(8,128)(2,1)S(1)} %collective-permute-done.17), kind=kLoop, calls=%fused_computation.4 | loop fusion | flops 786432 | bytes 2097152 | tf_op jit(solution)/shard_map/convert_element_type | solution.py:462
  81.3 1.4 %collective-permute-done.14 = bf16[128,1024]{1,0:T(8,128)(2,1)S(1)} collective-permute-done((bf16[128,1024]{1,0:T(8,128)(2,1)S(1)}, bf16[128,1024]{1,0:T(8,128)(2,1)S(1)}, u32[]{:S(2)}, u32[]{:S(2)}) %collective-permute-start.14) | collective-permute-done | bytes 262176 | tf_op jit(solution)/shard_map/ppermute | solution.py:286
  82.9 0.9 %add_multiply_fusion = f32[128,1024]{1,0:T(8,128)} fusion(bf16[128,1024]{1,0:T(8,128)(2,1)S(1)} %collective-permute-done.14, bf16[128,1024]{1,0:T(8,128)(2,1)S(1)} %collective-permute-done.18, bf16[128,1024]{1,0:T(8,128)(2,1)S(1)} %get-tuple-element.79), kind=kLoop, calls=%fused_computation.6 | loop fusion | flops 786432 | bytes 1310720 | tf_op jit(solution)/shard_map/mul | solution.py:469
  (28 shorter events, 0.9 us)
Async XLA Ops:
  0.6 5.9 %copy-start.2 = (bf16[128]{0:T(256)(128)(2,1)S(1)}, bf16[128]{0:T(256)(128)(2,1)}, u32[]{:S(2)}) copy-start(bf16[128]{0:T(256)(128)(2,1)} %param.8) | copy-start | bytes 772
  0.6 5.9 %copy-start.1 = (bf16[128,1024]{1,0:T(8,128)(2,1)S(1)}, bf16[128,1024]{1,0:T(8,128)(2,1)}, u32[]{:S(2)}) copy-start(bf16[128,1024]{1,0:T(8,128)(2,1)} %param.7) | copy-start | bytes 786436
  0.7 5.9 %copy-start = (bf16[128,1024]{1,0:T(8,128)(2,1)S(1)}, bf16[128,1024]{1,0:T(8,128)(2,1)}, u32[]{:S(2)}) copy-start(bf16[128,1024]{1,0:T(8,128)(2,1)} %param.9) | copy-start | bytes 786436
  2.0 26.2 %collective-permute-start = (bf16[2,512,512]{2,1,0:T(8,128)(2,1)S(1)}, bf16[2,512,512]{2,1,0:T(8,128)(2,1)S(1)}, u32[]{:S(2)}, u32[]{:S(2)}) collective-permute-start(bf16[2,512,512]{2,1,0:T(8,128)(2,1)S(1)} %pad_maximum_fusion.refs_0_), channel_id=1, source_target_pairs={{0,2},{1,3},{2,0},{3,1},{4,6},{5,7},{6,4},{7,5},{8,10},{9,11},{10,... | collective-permute-start | bytes 3145736 | tf_op jit(solution)/shard_map/ppermute | solution.py:286
  5.0 24.6 %collective-permute-start.1 = (bf16[2,512,512]{2,1,0:T(8,128)(2,1)S(1)}, bf16[2,512,512]{2,1,0:T(8,128)(2,1)S(1)}, u32[]{:S(2)}, u32[]{:S(2)}) collective-permute-start(bf16[2,512,512]{2,1,0:T(8,128)(2,1)S(1)} %pad_maximum_fusion.refs_0_), channel_id=1, source_target_pairs={{0,4},{1,5},{2,6},{3,7},{4,0},{5,1},{6,2},{7,3},{8,12},{9,13},{10,... | collective-permute-start | bytes 3145736 | tf_op jit(solution)/shard_map/ppermute | solution.py:286
  6.5 23.1 %collective-permute-start.2 = (bf16[2,512,512]{2,1,0:T(8,128)(2,1)S(1)}, bf16[2,512,512]{2,1,0:T(8,128)(2,1)S(1)}, u32[]{:S(2)}, u32[]{:S(2)}) collective-permute-start(bf16[2,512,512]{2,1,0:T(8,128)(2,1)S(1)} %pad_maximum_fusion.refs_0_), channel_id=1, source_target_pairs={{0,1},{1,0},{2,3},{3,2},{4,5},{5,4},{6,7},{7,6},{8,9},{9,8},{10,11... | collective-permute-start | bytes 3145736 | tf_op jit(solution)/shard_map/ppermute | solution.py:286
  6.6 27.3 %collective-permute-start.6 = (bf16[264,1024]{1,0:T(8,128)(2,1)S(1)}, bf16[264,1024]{1,0:T(8,128)(2,1)S(1)}, u32[]{:S(2)}, u32[]{:S(2)}) collective-permute-start(bf16[264,1024]{1,0:T(8,128)(2,1)S(1)} %fusion.1.refs_6_), channel_id=1, source_target_pairs={{0,16},{1,17},{2,18},{3,19},{4,20},{5,21},{6,22},{7,23},{8,24},{9,... | collective-permute-start | bytes 1622024 | tf_op jit(solution)/shard_map/ppermute | solution.py:286
  9.3 25.9 %collective-permute-start.5 = (bf16[264,1024]{1,0:T(8,128)(2,1)S(1)}, bf16[264,1024]{1,0:T(8,128)(2,1)S(1)}, u32[]{:S(2)}, u32[]{:S(2)}) collective-permute-start(bf16[264,1024]{1,0:T(8,128)(2,1)S(1)} %fusion.1.refs_6_), channel_id=1, source_target_pairs={{0,8},{1,9},{2,10},{3,11},{4,12},{5,13},{6,14},{7,15},{8,0},{9,1},... | collective-permute-start | bytes 1622024 | tf_op jit(solution)/shard_map/ppermute | solution.py:286
  29.6 6.1 %collective-permute-start.3 = (bf16[2,512,512]{2,1,0:T(8,128)(2,1)S(1)}, bf16[2,512,512]{2,1,0:T(8,128)(2,1)S(1)}, u32[]{:S(2)}, u32[]{:S(2)}) collective-permute-start(bf16[2,512,512]{2,1,0:T(8,128)(2,1)S(1)} %collective-permute-done.refs_2_), channel_id=1, source_target_pairs={{0,1},{1,0},{2,3},{3,2},{4,5},{5,4},{6,7},{7,6},{8,9},{9,8},{10,11... | collective-permute-start | bytes 3145736 | tf_op jit(solution)/shard_map/ppermute | solution.py:286
  29.6 6.1 %collective-permute-start.4 = (bf16[2,512,512]{2,1,0:T(8,128)(2,1)S(1)}, bf16[2,512,512]{2,1,0:T(8,128)(2,1)S(1)}, u32[]{:S(2)}, u32[]{:S(2)}) collective-permute-start(bf16[2,512,512]{2,1,0:T(8,128)(2,1)S(1)} %collective-permute-done.1.refs_4_), channel_id=1, source_target_pairs={{0,1},{1,0},{2,3},{3,2},{4,5},{5,4},{6,7},{7,6},{8,9},{9,8},{10,11... | collective-permute-start | bytes 3145736 | tf_op jit(solution)/shard_map/ppermute | solution.py:286
  33.9 13.8 %collective-permute-start.7 = (bf16[264,1024]{1,0:T(8,128)(2,1)S(1)}, bf16[264,1024]{1,0:T(8,128)(2,1)S(1)}, u32[]{:S(2)}, u32[]{:S(2)}) collective-permute-start(bf16[264,1024]{1,0:T(8,128)(2,1)S(1)} %collective-permute-done.6.refs_8_), channel_id=1, source_target_pairs={{0,8},{1,9},{2,10},{3,11},{4,12},{5,13},{6,14},{7,15},{8,0},{9,1},... | collective-permute-start | bytes 1622024 | tf_op jit(solution)/shard_map/ppermute | solution.py:286
  34.6 15.8 %collective-permute-start.8 = (bf16[560,512]{1,0:T(8,128)(2,1)S(1)}, bf16[560,512]{1,0:T(8,128)(2,1)S(1)}, u32[]{:S(2)}, u32[]{:S(2)}) collective-permute-start(bf16[560,512]{1,0:T(8,128)(2,1)S(1)} %slice.12), channel_id=1, source_target_pairs={{0,4},{1,5},{2,6},{3,7},{4,0},{5,1},{6,2},{7,3},{8,12},{9,13},{10,... | collective-permute-start | bytes 1720328 | tf_op jit(solution)/shard_map/ppermute | solution.py:286
  35.2 15.2 %collective-permute-start.9 = (bf16[512,512]{1,0:T(8,128)(2,1)S(1)}, bf16[512,512]{1,0:T(8,128)(2,1)S(1)}, u32[]{:S(2)}, u32[]{:S(2)}) collective-permute-start(bf16[512,512]{1,0:T(8,128)(2,1)S(1)} %slice_bitcast_fusion), channel_id=1, source_target_pairs={{0,2},{1,3},{2,0},{3,1},{4,6},{5,7},{6,4},{7,5},{8,10},{9,11},{10,... | collective-permute-start | bytes 1572872 | tf_op jit(solution)/shard_map/ppermute | solution.py:286
  50.4 3.5 %collective-permute-start.10 = (bf16[1536,512]{1,0:T(8,128)(2,1)S(1)}, bf16[1536,512]{1,0:T(8,128)(2,1)S(1)}, u32[]{:S(2)}, u32[]{:S(2)}) collective-permute-start(bf16[1536,512]{1,0:T(8,128)(2,1)S(1)} %get-tuple-element.63), channel_id=1, source_target_pairs={{0,1},{1,0},{2,3},{3,2},{4,5},{5,4},{6,7},{7,6},{8,9},{9,8},{10,11... | collective-permute-start | bytes 4718600 | tf_op jit(solution)/shard_map/ppermute | solution.py:286
  50.6 4.9 %collective-permute-start.11 = (bf16[1024,512]{1,0:T(8,128)(2,1)S(1)}, bf16[1024,512]{1,0:T(8,128)(2,1)S(1)}, u32[]{:S(2)}, u32[]{:S(2)}) collective-permute-start(bf16[1024,512]{1,0:T(8,128)(2,1)S(1)} %pad_maximum_fusion.1), channel_id=1, source_target_pairs={{0,1},{1,0},{2,3},{3,2},{4,5},{5,4},{6,7},{7,6},{8,9},{9,8},{10,11... | collective-permute-start | bytes 3145736 | tf_op jit(solution)/shard_map/ppermute | solution.py:286
  54.3 18.1 %collective-permute-start.15 = (bf16[528,512]{1,0:T(8,128)(2,1)S(1)}, bf16[528,512]{1,0:T(8,128)(2,1)S(1)}, u32[]{:S(2)}, u32[]{:S(2)}) collective-permute-start(bf16[528,512]{1,0:T(8,128)(2,1)S(1)} %get-tuple-element.76), channel_id=1, source_target_pairs={{0,2},{1,3},{2,0},{3,1},{4,6},{5,7},{6,4},{7,5},{8,10},{9,11},{10,... | collective-permute-start | bytes 1622024 | tf_op jit(solution)/shard_map/ppermute | solution.py:286
  54.9 25.3 %collective-permute-start.16 = (bf16[528,512]{1,0:T(8,128)(2,1)S(1)}, bf16[528,512]{1,0:T(8,128)(2,1)S(1)}, u32[]{:S(2)}, u32[]{:S(2)}) collective-permute-start(bf16[528,512]{1,0:T(8,128)(2,1)S(1)} %get-tuple-element.77), channel_id=1, source_target_pairs={{0,4},{1,5},{2,6},{3,7},{4,0},{5,1},{6,2},{7,3},{8,12},{9,13},{10,... | collective-permute-start | bytes 1622024 | tf_op jit(solution)/shard_map/ppermute | solution.py:286
  59.3 2.0 %collective-permute-start.12 = (bf16[512,512]{1,0:T(8,128)(2,1)S(1)}, bf16[512,512]{1,0:T(8,128)(2,1)S(1)}, u32[]{:S(2)}, u32[]{:S(2)}) collective-permute-start(bf16[512,512]{1,0:T(8,128)(2,1)S(1)} %get-tuple-element.72), channel_id=1, source_target_pairs={{0,1},{1,0},{2,3},{3,2},{4,5},{5,4},{6,7},{7,6},{8,9},{9,8},{10,11... | collective-permute-start | bytes 1572872 | tf_op jit(solution)/shard_map/ppermute | solution.py:286
  59.4 8.7 %collective-permute-start.13 = (bf16[128,1024]{1,0:T(8,128)(2,1)S(1)}, bf16[128,1024]{1,0:T(8,128)(2,1)S(1)}, u32[]{:S(2)}, u32[]{:S(2)}) collective-permute-start(bf16[128,1024]{1,0:T(8,128)(2,1)S(1)} %get-tuple-element.74), channel_id=1, source_target_pairs={{0,8},{1,9},{2,10},{3,11},{4,12},{5,13},{6,14},{7,15},{8,0},{9,1},... | collective-permute-start | bytes 786440 | tf_op jit(solution)/shard_map/ppermute | solution.py:286
  61.4 19.0 %collective-permute-start.17 = (bf16[512,512]{1,0:T(8,128)(2,1)S(1)}, bf16[512,512]{1,0:T(8,128)(2,1)S(1)}, u32[]{:S(2)}, u32[]{:S(2)}) collective-permute-start(bf16[512,512]{1,0:T(8,128)(2,1)S(1)} %pair_sum_diagonal.1), channel_id=1, source_target_pairs={{0,6},{1,7},{2,4},{3,5},{4,2},{5,3},{6,0},{7,1},{8,14},{9,15},{10,... | collective-permute-start | bytes 1572872 | tf_op jit(solution)/shard_map/ppermute | solution.py:286
  68.2 14.6 %collective-permute-start.14 = (bf16[128,1024]{1,0:T(8,128)(2,1)S(1)}, bf16[128,1024]{1,0:T(8,128)(2,1)S(1)}, u32[]{:S(2)}, u32[]{:S(2)}) collective-permute-start(bf16[128,1024]{1,0:T(8,128)(2,1)S(1)} %line_sum.1), channel_id=1, source_target_pairs={{0,16},{1,17},{2,18},{3,19},{4,20},{5,21},{6,22},{7,23},{8,24},{9,... | collective-permute-start | bytes 786440 | tf_op jit(solution)/shard_map/ppermute | solution.py:286
  70.7 12.2 %collective-permute-start.18 = (bf16[128,1024]{1,0:T(8,128)(2,1)S(1)}, bf16[128,1024]{1,0:T(8,128)(2,1)S(1)}, u32[]{:S(2)}, u32[]{:S(2)}) collective-permute-start(bf16[128,1024]{1,0:T(8,128)(2,1)S(1)} %get-tuple-element.80), channel_id=1, source_target_pairs={{0,8},{1,9},{2,10},{3,11},{4,12},{5,13},{6,14},{7,15},{8,0},{9,1},... | collective-permute-start | bytes 786440 | tf_op jit(solution)/shard_map/ppermute | solution.py:286

commit v14 on v13

--- a/solution.py
+++ b/solution.py
@@ -17,6 +17,7 @@
 GRADIENT_COST = 10**10
 DIAGONAL_COST = 10**6
 EXTRA = 48
+PARTS = 2
 BIAS_ROWS = 8
 MORE = 16
 
@@ -209,8 +210,9 @@
 def diagonal_kernel(owned, *refs):
     w_in, w_out, bias, grad_first, grad_last = refs[:5]
     tok_ref, cot_ref, far_ref = refs[5:8]
-    mine_ref, other_ref, own_ref, one_ref, two_ref, three_ref = refs[8:14]
-    tok, cot, dpre, tok_sem, cot_sem = refs[14:]
+    mine_ref, other_ref, own_ref, one_ref = refs[8:12]
+    two_refs, three_refs = refs[12 : 12 + PARTS], refs[12 + PARTS : 12 + 2 * PARTS]
+    tok, cot, dpre, tok_sem, cot_sem = refs[12 + 2 * PARTS :]
     core = lax.axis_index("core")
     rows, feats = mine_ref.shape
     two = 2 * owned
@@ -220,24 +222,24 @@
     run(load + cot_load, "start")
     run(load, "wait")
     step = rows // 2
-    slopes = []
     for sub in range(2):
         spot = slice(sub * step, (sub + 1) * step)
         value, slope = activate(tok[spot, :], w_in[...], bias[0:1, :])
-        slopes.append(slope)
         act = value.astype(jnp.bfloat16)
+        if sub == 0:
+            run(cot_load, "wait")
+        dact = dot_last(cot[spot, :], w_out[...])
+        dpre[spot, :] = (dact * slope).astype(jnp.bfloat16)
         for shift, ref in enumerate((mine_ref, other_ref)):
             ref[spot, :] = jnp.dot(
                 act, w_out[:, half_columns(core, shift, feats)], preferred_element_type=jnp.float32
             ).astype(jnp.bfloat16)
-    run(cot_load, "wait")
-    for sub in range(2):
-        spot = slice(sub * step, (sub + 1) * step)
-        dpre[spot, :] = (dot_last(cot[spot, :], w_out[...]) * slopes[sub]).astype(jnp.bfloat16)
 
     grad = grad_last[...] + dot_first(dpre[:, two:], tok[...])
-    two_ref[...] = grad[:owned].astype(jnp.bfloat16)
-    three_ref[...] = grad[owned:].astype(jnp.bfloat16)
+    part = owned // PARTS
+    for at in range(PARTS):
+        two_refs[at][...] = grad[at * part : (at + 1) * part].astype(jnp.bfloat16)
+        three_refs[at][...] = grad[owned + at * part : owned + (at + 1) * part].astype(jnp.bfloat16)
     grad = grad_first[...] + dot_first(dpre[:, :two], tok[...])
     own_ref[...] = grad[:owned].astype(jnp.bfloat16)
     one_ref[...] = grad[owned:].astype(jnp.bfloat16)
@@ -407,11 +409,13 @@
     mixed_x, mixed_y = to_x(sums[1]), to_y(sums[2])
     grad_terms, mixed_own = barrier((grad_terms, sums[0]))
 
-    mine_diag, other_diag, grad_own, grad_one, grad_two, grad_three = pl.pallas_call(
+    mine_diag, other_diag, grad_own, grad_one, *grad_far = pl.pallas_call(
         functools.partial(diagonal_kernel, owned),
-        out_shape=[bf16(rows, feats)] * 2 + [bf16(owned, width)] * 4,
+        out_shape=[bf16(rows, feats)] * 2
+        + [bf16(owned, width)] * 2
+        + [bf16(owned // PARTS, width)] * (2 * PARTS),
         in_specs=vmem(5) + anywhere(3),
-        out_specs=vmem(6),
+        out_specs=vmem(4 + 2 * PARTS),
         scratch_shapes=[
             pltpu.VMEM((rows, width), jnp.bfloat16),
             pltpu.VMEM((rows, width), jnp.bfloat16),
@@ -427,7 +431,7 @@
         tok_diag, cot_diag, diag_other,
     )
     received_diag = to_core(other_diag)
-    relayed = to_far(grad_three, 1)
+    relayed = [to_far(piece, 1) for piece in grad_far[PARTS:]]
     (sum_diag,) = pl.pallas_call(
         functools.partial(pair_kernel, rows),
         out_shape=[bf16(rows, feats)],
@@ -438,18 +442,21 @@
         name="pair_sum_diagonal",
     )(mine_diag, received_diag)
     mixed_diag = to_diagonal(sum_diag)
-    grad_one, grad_two, _ = barrier((grad_one, grad_two, sum_diag))
+    from_two = []
+    for at in range(PARTS):
+        piece, _ = barrier((grad_far[at], sum_diag))
+        (line_sum,) = pl.pallas_call(
+            functools.partial(pair_kernel, owned // PARTS),
+            out_shape=[bf16(owned // PARTS, width)],
+            in_specs=vmem(2),
+            out_specs=vmem(1),
+            compiler_params=params,
+            cost_estimate=cost(rows, rows),
+            name="line_sum",
+        )(piece, relayed[at])
+        from_two.append(to_far(line_sum, 2))
+    grad_one, mixed_x = barrier((grad_one, mixed_x))
     from_one = to_far(grad_one, 1)
-    (line_sum,) = pl.pallas_call(
-        functools.partial(pair_kernel, owned),
-        out_shape=[bf16(owned, width)],
-        in_specs=vmem(2),
-        out_specs=vmem(1),
-        compiler_params=params,
-        cost_estimate=cost(rows, rows),
-        name="line_sum",
-    )(grad_two, relayed)
-    from_two = to_far(line_sum, 2)
     mixed = pl.pallas_call(
         plane_kernel,
         out_shape=f32(rows, feats),
@@ -460,7 +467,8 @@
         name="plane_sum",
     )(mixed_own, mixed_x, mixed_y)
     mixed = (mixed + mixed_diag.astype(jnp.float32)).astype(jnp.bfloat16)
-    from_two, mixed = barrier((from_two, mixed))
+    *from_two, mixed = barrier((*from_two, mixed))
+    from_two = jnp.concatenate(from_two)
     total = (
         grad_own.astype(jnp.float32)
         + from_one.astype(jnp.float32)

time: 83.9 us -> 83.1 us (level)
  waiting for transfers between devices: 42.7 us -> 38.6 us
  starting transfers between devices: 20.5 us -> 24 us
    ppermute x19 -> x21, waiting for transfers between devices: 42.7 us -> 38.6 us  [permute(): return lax.ppermute(value, AXES, pairs)]
    ppermute x19 -> x21, starting transfers between devices: 20.5 us -> 24 us  [permute(): return lax.ppermute(value, AXES, pairs)]
  transfers between devices with their start and end apart: 19 -> 21, of which waited for: 10 -> 8; matrix products, arithmetic and copies ran while one was open for 1% -> 1% of each run, Pallas kernels for 19% -> 19%
where the time goes in v14:
time: 83.1 us; the launch traced here: 83 us
  waiting for transfers between devices  38.6 us (46%)
  starting transfers between devices  24 us (29%)
  Pallas kernels  16.1 us (19%)
  other arithmetic  3.33 us (4%)
    ppermute x21, waiting for transfers between devices, permute(): return lax.ppermute(value, AXES, pairs)  38.6 us
    ppermute x21, starting transfers between devices, permute(): return lax.ppermute(value, AXES, pairs)  24 us
    pallas_call x1, Pallas kernels, on_device_lines(): pl.pallas_call(functools.partial(early_kernel, owned), out_shape=(bf16(ea...  7.43 us
    pallas_call x1, Pallas kernels, on_device_lines(): pl.pallas_call(functools.partial(diagonal_kernel, owned), out_shape=[bf16...  3.47 us
    pallas_call x1, Pallas kernels, on_device_lines(): pl.pallas_call(functools.partial(output_kernel, owned), out_shape=(bf16(e...  2.62 us
    pallas_call x1, Pallas kernels, on_device_lines(): pl.pallas_call(gradient_kernel, out_shape=f32(2 * owned, width), in_specs...  1.81 us
  transfers between devices with their start and end apart: 21, of which 8 were waited for; matrix products, arithmetic and copies ran while one was open for 1% of the time, Pallas kernels for 19%

profile of v14, /device:TPU:0, one launch (start us, length us, event | category | flops | bytes accessed | tf_op | source)
XLA Modules:
  0.0 83.0 jit_solution(3400146851380964386)
XLA Ops:
  0.7 1.4 %pad_maximum_fusion.refs_0_ = bf16[2,512,512]{2,1,0:T(8,128)(2,1)S(1)} fusion(bf16[1,512,512]{2,1,0:T(8,128)(2,1)} %bitcast.7, bf16[1,512,512]{2,1,0:T(8,128)(2,1)} %bitcast.8), kind=kLoop, calls=%fused_computation.2 | loop fusion | flops 524288 | bytes 2097152 | tf_op jit(solution)/shard_map/stack | solution.py:330
  2.0 3.0 %collective-permute-start = (bf16[2,512,512]{2,1,0:T(8,128)(2,1)S(1)}, bf16[2,512,512]{2,1,0:T(8,128)(2,1)S(1)}, u32[]{:S(2)}, u32[]{:S(2)}) collective-permute-start(bf16[2,512,512]{2,1,0:T(8,128)(2,1)S(1)} %pad_maximum_fusion.refs_0_), channel_id=1, source_target_pairs={{0,2},{1,3},{2,0},{3,1},{4,6},{5,7},{6,4},{7,5},{8,10},{9,11},{10,... | collective-permute-start | bytes 3145736 | tf_op jit(solution)/shard_map/ppermute | solution.py:288
  5.0 1.5 %collective-permute-start.1 = (bf16[2,512,512]{2,1,0:T(8,128)(2,1)S(1)}, bf16[2,512,512]{2,1,0:T(8,128)(2,1)S(1)}, u32[]{:S(2)}, u32[]{:S(2)}) collective-permute-start(bf16[2,512,512]{2,1,0:T(8,128)(2,1)S(1)} %pad_maximum_fusion.refs_0_), channel_id=1, source_target_pairs={{0,4},{1,5},{2,6},{3,7},{4,0},{5,1},{6,2},{7,3},{8,12},{9,13},{10,... | collective-permute-start | bytes 3145736 | tf_op jit(solution)/shard_map/ppermute | solution.py:288
  6.6 2.7 %collective-permute-start.6 = (bf16[264,1024]{1,0:T(8,128)(2,1)S(1)}, bf16[264,1024]{1,0:T(8,128)(2,1)S(1)}, u32[]{:S(2)}, u32[]{:S(2)}) collective-permute-start(bf16[264,1024]{1,0:T(8,128)(2,1)S(1)} %fusion.1.refs_6_), channel_id=1, source_target_pairs={{0,16},{1,17},{2,18},{3,19},{4,20},{5,21},{6,22},{7,23},{8,24},{9,... | collective-permute-start | bytes 1622024 | tf_op jit(solution)/shard_map/ppermute | solution.py:288
  9.3 1.6 %collective-permute-start.5 = (bf16[264,1024]{1,0:T(8,128)(2,1)S(1)}, bf16[264,1024]{1,0:T(8,128)(2,1)S(1)}, u32[]{:S(2)}, u32[]{:S(2)}) collective-permute-start(bf16[264,1024]{1,0:T(8,128)(2,1)S(1)} %fusion.1.refs_6_), channel_id=1, source_target_pairs={{0,8},{1,9},{2,10},{3,11},{4,12},{5,13},{6,14},{7,15},{8,0},{9,1},... | collective-permute-start | bytes 1622024 | tf_op jit(solution)/shard_map/ppermute | solution.py:288
  10.8 17.3 %collective-permute-done.refs_2_ = bf16[2,512,512]{2,1,0:T(8,128)(2,1)S(1)} collective-permute-done((bf16[2,512,512]{2,1,0:T(8,128)(2,1)S(1)}, bf16[2,512,512]{2,1,0:T(8,128)(2,1)S(1)}, u32[]{:S(2)}, u32[]{:S(2)}) %collective-permute-start) | collective-permute-done | bytes 1048608 | tf_op jit(solution)/shard_map/ppermute | solution.py:288
  28.2 1.5 %collective-permute-done.1.refs_4_ = bf16[2,512,512]{2,1,0:T(8,128)(2,1)S(1)} collective-permute-done((bf16[2,512,512]{2,1,0:T(8,128)(2,1)S(1)}, bf16[2,512,512]{2,1,0:T(8,128)(2,1)S(1)}, u32[]{:S(2)}, u32[]{:S(2)}) %collective-permute-start.1) | collective-permute-done | bytes 1048608 | tf_op jit(solution)/shard_map/ppermute | solution.py:288
  29.6 0.5 collective-permute-start.4
  30.2 3.8 %collective-permute-done.6.refs_8_ = bf16[264,1024]{1,0:T(8,128)(2,1)S(1)} collective-permute-done((bf16[264,1024]{1,0:T(8,128)(2,1)S(1)}, bf16[264,1024]{1,0:T(8,128)(2,1)S(1)}, u32[]{:S(2)}, u32[]{:S(2)}) %collective-permute-start.6) | collective-permute-done | bytes 540704 | tf_op jit(solution)/shard_map/ppermute | solution.py:288
  33.9 0.6 collective-permute-start.7
  34.6 0.6 collective-permute-start.8
  35.2 0.6 collective-permute-start.9
  35.8 7.4 %early.1 = (bf16[1536,128]{1,0:T(8,128)(2,1)S(1)}, bf16[1536,128]{1,0:T(8,128)(2,1)S(1)}, f32[1536,1024]{1,0:T(8,128)S(1)}, f32[256,1024]{1,0:T(8,128)S(1)}, bf1...) custom-call(bf16[2,512,512]{2,1,0:T(8,128)(2,1)S(1)} %pad_maximum_fu, ...), custom_call_target="tpu_custom_call" | custom-call | flops 786432 | bytes 1536 | tf_op jit(solution)/shard_map/early/pallas_call | solution.py:340
  43.2 4.5 %collective-permute-done.7.refs_6_.w_three = bf16[264,1024]{1,0:T(8,128)(2,1)S(1)} collective-permute-done((bf16[264,1024]{1,0:T(8,128)(2,1)S(1)}, bf16[264,1024]{1,0:T(8,128)(2,1)S(1)}, u32[]{:S(2)}, u32[]{:S(2)}) %collective-permute-start.7) | collective-permute-done | bytes 540704 | tf_op jit(solution)/shard_map/ppermute | solution.py:288
  47.8 2.6 %output.1 = (bf16[1536,512]{1,0:T(8,128)(2,1)S(1)}, bf16[1536,512]{1,0:T(8,128)(2,1)S(1)}, f32[1536,128]{1,0:T(8,128)S(1)}, bf16[512,1024]{1,0:T(8,128)(2,1)S(1)...) custom-call(bf16[1536,128]{1,0:T(8,128)(2,1)S(1)} %get-tuple-element.50.refs_0_, ...), custom_call_target="tpu_custom_call" | custom-call | flops 786432 | bytes 1536 | tf_op jit(solution)/shard_map/output/pallas_call | solution.py:367
  50.6 0.6 collective-permute-start.11
  51.2 1.8 %gradient.1.refs_4_ = f32[256,1024]{1,0:T(8,128)S(1)} custom-call(bf16[1536,128]{1,0:T(8,128)(2,1)S(1)} %get-tuple-element.61.dpre_two, bf16[1536,1024]{1,0:T(8,128)(2,1)S(1)} %get-tuple-element.51.refs_1_.tok, bf16[1536,1024]{1,0:T(8,128)(2,1)S(1)} %get-tuple-element.62.cot, f32[1536,128]{1,0:T(8,128)S(1)} %get-tuple-element.66.slope, ...), custom_call_target="tpu_custom_call" | custom-call | flops 10000000000 | bytes 1536 | tf_op jit(solution)/shard_map/gradient/pallas_call | solution.py:388
  53.0 0.9 %collective-permute-done.10.other_ref = bf16[1536,512]{1,0:T(8,128)(2,1)S(1)} collective-permute-done((bf16[1536,512]{1,0:T(8,128)(2,1)S(1)}, bf16[1536,512]{1,0:T(8,128)(2,1)S(1)}, u32[]{:S(2)}, u32[]{:S(2)}) %collective-permute-start.10) | collective-permute-done | bytes 1572896 | tf_op jit(solution)/shard_map/ppermute | solution.py:288
  54.3 0.6 collective-permute-start.17
  54.9 0.7 collective-permute-start.18
  55.6 3.5 %diagonal.1 = (bf16[512,512]{1,0:T(8,128)(2,1)S(1)}, bf16[512,512]{1,0:T(8,128)(2,1)S(1)}, bf16[128,1024]{1,0:T(8,128)(2,1)S(1)}, bf16[128,1024]{1,0:T(8,128)(2,...) custom-call(bf16[512,1024]{1,0:T(8,128)(2,1)S(1)} %get-tuple-element, ...), custom_call_target="tpu_custom_call" | custom-call | flops 1000000 | bytes 512 | tf_op jit(solution)/shard_map/diagonal/pallas_call | solution.py:412
  59.1 0.9 %collective-permute-start.15 = (bf16[64,1024]{1,0:T(8,128)(2,1)S(1)}, bf16[64,1024]{1,0:T(8,128)(2,1)S(1)}, u32[]{:S(2)}, u32[]{:S(2)}) collective-permute-start(bf16[64,1024]{1,0:T(8,128)(2,1)S(1)} %get-tuple-element.81), channel_id=1, source_target_pairs={{0,8},{1,9},{2,10},{3,11},{4,12},{5,13},{6,14},{7,15},{8,0},{9,1},... | collective-permute-start | bytes 393224 | tf_op jit(solution)/shard_map/ppermute | solution.py:288
  60.1 1.2 %collective-permute-start.13 = (bf16[64,1024]{1,0:T(8,128)(2,1)S(1)}, bf16[64,1024]{1,0:T(8,128)(2,1)S(1)}, u32[]{:S(2)}, u32[]{:S(2)}) collective-permute-start(bf16[64,1024]{1,0:T(8,128)(2,1)S(1)} %get-tuple-element.78), channel_id=1, source_target_pairs={{0,8},{1,9},{2,10},{3,11},{4,12},{5,13},{6,14},{7,15},{8,0},{9,1},... | collective-permute-start | bytes 393224 | tf_op jit(solution)/shard_map/ppermute | solution.py:288
  61.3 2.4 %collective-permute-start.19 = (bf16[512,512]{1,0:T(8,128)(2,1)S(1)}, bf16[512,512]{1,0:T(8,128)(2,1)S(1)}, u32[]{:S(2)}, u32[]{:S(2)}) collective-permute-start(bf16[512,512]{1,0:T(8,128)(2,1)S(1)} %pair_sum_diagonal.1), channel_id=1, source_target_pairs={{0,6},{1,7},{2,4},{3,5},{4,2},{5,3},{6,0},{7,1},{8,14},{9,15},{10,... | collective-permute-start | bytes 1572872 | tf_op jit(solution)/shard_map/ppermute | solution.py:288
  63.7 1.8 %collective-permute-done.15.other_ref = bf16[64,1024]{1,0:T(8,128)(2,1)S(1)} collective-permute-done((bf16[64,1024]{1,0:T(8,128)(2,1)S(1)}, bf16[64,1024]{1,0:T(8,128)(2,1)S(1)}, u32[]{:S(2)}, u32[]{:S(2)}) %collective-permute-start.15) | collective-permute-done | bytes 131104 | tf_op jit(solution)/shard_map/ppermute | solution.py:288
  65.5 2.6 %collective-permute-start.16 = (bf16[64,1024]{1,0:T(8,128)(2,1)S(1)}, bf16[64,1024]{1,0:T(8,128)(2,1)S(1)}, u32[]{:S(2)}, u32[]{:S(2)}) collective-permute-start(bf16[64,1024]{1,0:T(8,128)(2,1)S(1)} %line_sum.3), channel_id=1, source_target_pairs={{0,16},{1,17},{2,18},{3,19},{4,20},{5,21},{6,22},{7,23},{8,24},{9,... | collective-permute-start | bytes 393224 | tf_op jit(solution)/shard_map/ppermute | solution.py:288
  68.1 2.8 %collective-permute-start.14 = (bf16[64,1024]{1,0:T(8,128)(2,1)S(1)}, bf16[64,1024]{1,0:T(8,128)(2,1)S(1)}, u32[]{:S(2)}, u32[]{:S(2)}) collective-permute-start(bf16[64,1024]{1,0:T(8,128)(2,1)S(1)} %line_sum.2), channel_id=1, source_target_pairs={{0,16},{1,17},{2,18},{3,19},{4,20},{5,21},{6,22},{7,23},{8,24},{9,... | collective-permute-start | bytes 393224 | tf_op jit(solution)/shard_map/ppermute | solution.py:288
  70.9 1.2 %collective-permute-start.20 = (bf16[128,1024]{1,0:T(8,128)(2,1)S(1)}, bf16[128,1024]{1,0:T(8,128)(2,1)S(1)}, u32[]{:S(2)}, u32[]{:S(2)}) collective-permute-start(bf16[128,1024]{1,0:T(8,128)(2,1)S(1)} %get-tuple-element.89), channel_id=1, source_target_pairs={{0,8},{1,9},{2,10},{3,11},{4,12},{5,13},{6,14},{7,15},{8,0},{9,1},... | collective-permute-start | bytes 786440 | tf_op jit(solution)/shard_map/ppermute | solution.py:288
  72.1 8.0 %collective-permute-done.18.y_ref = bf16[528,512]{1,0:T(8,128)(2,1)S(1)} collective-permute-done((bf16[528,512]{1,0:T(8,128)(2,1)S(1)}, bf16[528,512]{1,0:T(8,128)(2,1)S(1)}, u32[]{:S(2)}, u32[]{:S(2)}) %collective-permute-start.18) | collective-permute-done | bytes 540704 | tf_op jit(solution)/shard_map/ppermute | solution.py:288
  80.4 1.0 %add_convert_fusion = bf16[512,512]{1,0:T(8,128)(2,1)} fusion(f32[512,512]{1,0:T(8,128)S(1)} %plane_sum.1, bf16[512,512]{1,0:T(8,128)(2,1)S(1)} %collective-permute-done.19), kind=kLoop, calls=%fused_computation.4 | loop fusion | flops 786432 | bytes 2097152 | tf_op jit(solution)/shard_map/convert_element_type | solution.py:469
  81.3 0.7 collective-permute-done.20
  82.0 0.9 %add_multiply_fusion = f32[128,1024]{1,0:T(8,128)} fusion(bf16[128,1024]{1,0:T(8,128)(2,1)S(1)} %collective-permute-done.20, bf16[128,1024]{1,0:T(8,128)(2,1)S(1)} %get-tuple-element.88, bf16[64,1024]{1,0:T(8,128)(2,1)S(1)} %collective-permute-done.16, bf16[64,1024]{1,0:T(8,128)(2,1)S(1)} %collective-permute-done.14), kind=kLoop, calls=%fused_computation.6 | loop fusion | flops 1179648 | bytes 1310720 | tf_op jit(solution)/shard_map/mul | solution.py:477
  (33 shorter events, 1.2 us)
Async XLA Ops:
  0.6 5.9 %copy-start.2 = (bf16[128]{0:T(256)(128)(2,1)S(1)}, bf16[128]{0:T(256)(128)(2,1)}, u32[]{:S(2)}) copy-start(bf16[128]{0:T(256)(128)(2,1)} %param.8) | copy-start | bytes 772
  0.6 5.9 %copy-start.1 = (bf16[128,1024]{1,0:T(8,128)(2,1)S(1)}, bf16[128,1024]{1,0:T(8,128)(2,1)}, u32[]{:S(2)}) copy-start(bf16[128,1024]{1,0:T(8,128)(2,1)} %param.7) | copy-start | bytes 786436
  0.7 5.9 %copy-start = (bf16[128,1024]{1,0:T(8,128)(2,1)S(1)}, bf16[128,1024]{1,0:T(8,128)(2,1)}, u32[]{:S(2)}) copy-start(bf16[128,1024]{1,0:T(8,128)(2,1)} %param.9) | copy-start | bytes 786436
  2.0 26.2 %collective-permute-start = (bf16[2,512,512]{2,1,0:T(8,128)(2,1)S(1)}, bf16[2,512,512]{2,1,0:T(8,128)(2,1)S(1)}, u32[]{:S(2)}, u32[]{:S(2)}) collective-permute-start(bf16[2,512,512]{2,1,0:T(8,128)(2,1)S(1)} %pad_maximum_fusion.refs_0_), channel_id=1, source_target_pairs={{0,2},{1,3},{2,0},{3,1},{4,6},{5,7},{6,4},{7,5},{8,10},{9,11},{10,... | collective-permute-start | bytes 3145736 | tf_op jit(solution)/shard_map/ppermute | solution.py:288
  5.0 24.6 %collective-permute-start.1 = (bf16[2,512,512]{2,1,0:T(8,128)(2,1)S(1)}, bf16[2,512,512]{2,1,0:T(8,128)(2,1)S(1)}, u32[]{:S(2)}, u32[]{:S(2)}) collective-permute-start(bf16[2,512,512]{2,1,0:T(8,128)(2,1)S(1)} %pad_maximum_fusion.refs_0_), channel_id=1, source_target_pairs={{0,4},{1,5},{2,6},{3,7},{4,0},{5,1},{6,2},{7,3},{8,12},{9,13},{10,... | collective-permute-start | bytes 3145736 | tf_op jit(solution)/shard_map/ppermute | solution.py:288
  6.5 23.1 %collective-permute-start.2 = (bf16[2,512,512]{2,1,0:T(8,128)(2,1)S(1)}, bf16[2,512,512]{2,1,0:T(8,128)(2,1)S(1)}, u32[]{:S(2)}, u32[]{:S(2)}) collective-permute-start(bf16[2,512,512]{2,1,0:T(8,128)(2,1)S(1)} %pad_maximum_fusion.refs_0_), channel_id=1, source_target_pairs={{0,1},{1,0},{2,3},{3,2},{4,5},{5,4},{6,7},{7,6},{8,9},{9,8},{10,11... | collective-permute-start | bytes 3145736 | tf_op jit(solution)/shard_map/ppermute | solution.py:288
  6.6 27.3 %collective-permute-start.6 = (bf16[264,1024]{1,0:T(8,128)(2,1)S(1)}, bf16[264,1024]{1,0:T(8,128)(2,1)S(1)}, u32[]{:S(2)}, u32[]{:S(2)}) collective-permute-start(bf16[264,1024]{1,0:T(8,128)(2,1)S(1)} %fusion.1.refs_6_), channel_id=1, source_target_pairs={{0,16},{1,17},{2,18},{3,19},{4,20},{5,21},{6,22},{7,23},{8,24},{9,... | collective-permute-start | bytes 1622024 | tf_op jit(solution)/shard_map/ppermute | solution.py:288
  9.3 25.9 %collective-permute-start.5 = (bf16[264,1024]{1,0:T(8,128)(2,1)S(1)}, bf16[264,1024]{1,0:T(8,128)(2,1)S(1)}, u32[]{:S(2)}, u32[]{:S(2)}) collective-permute-start(bf16[264,1024]{1,0:T(8,128)(2,1)S(1)} %fusion.1.refs_6_), channel_id=1, source_target_pairs={{0,8},{1,9},{2,10},{3,11},{4,12},{5,13},{6,14},{7,15},{8,0},{9,1},... | collective-permute-start | bytes 1622024 | tf_op jit(solution)/shard_map/ppermute | solution.py:288
  29.6 6.1 %collective-permute-start.3 = (bf16[2,512,512]{2,1,0:T(8,128)(2,1)S(1)}, bf16[2,512,512]{2,1,0:T(8,128)(2,1)S(1)}, u32[]{:S(2)}, u32[]{:S(2)}) collective-permute-start(bf16[2,512,512]{2,1,0:T(8,128)(2,1)S(1)} %collective-permute-done.refs_2_), channel_id=1, source_target_pairs={{0,1},{1,0},{2,3},{3,2},{4,5},{5,4},{6,7},{7,6},{8,9},{9,8},{10,11... | collective-permute-start | bytes 3145736 | tf_op jit(solution)/shard_map/ppermute | solution.py:288
  29.6 6.1 %collective-permute-start.4 = (bf16[2,512,512]{2,1,0:T(8,128)(2,1)S(1)}, bf16[2,512,512]{2,1,0:T(8,128)(2,1)S(1)}, u32[]{:S(2)}, u32[]{:S(2)}) collective-permute-start(bf16[2,512,512]{2,1,0:T(8,128)(2,1)S(1)} %collective-permute-done.1.refs_4_), channel_id=1, source_target_pairs={{0,1},{1,0},{2,3},{3,2},{4,5},{5,4},{6,7},{7,6},{8,9},{9,8},{10,11... | collective-permute-start | bytes 3145736 | tf_op jit(solution)/shard_map/ppermute | solution.py:288
  33.9 13.8 %collective-permute-start.7 = (bf16[264,1024]{1,0:T(8,128)(2,1)S(1)}, bf16[264,1024]{1,0:T(8,128)(2,1)S(1)}, u32[]{:S(2)}, u32[]{:S(2)}) collective-permute-start(bf16[264,1024]{1,0:T(8,128)(2,1)S(1)} %collective-permute-done.6.refs_8_), channel_id=1, source_target_pairs={{0,8},{1,9},{2,10},{3,11},{4,12},{5,13},{6,14},{7,15},{8,0},{9,1},... | collective-permute-start | bytes 1622024 | tf_op jit(solution)/shard_map/ppermute | solution.py:288
  34.6 15.8 %collective-permute-start.8 = (bf16[560,512]{1,0:T(8,128)(2,1)S(1)}, bf16[560,512]{1,0:T(8,128)(2,1)S(1)}, u32[]{:S(2)}, u32[]{:S(2)}) collective-permute-start(bf16[560,512]{1,0:T(8,128)(2,1)S(1)} %slice.12), channel_id=1, source_target_pairs={{0,4},{1,5},{2,6},{3,7},{4,0},{5,1},{6,2},{7,3},{8,12},{9,13},{10,... | collective-permute-start | bytes 1720328 | tf_op jit(solution)/shard_map/ppermute | solution.py:288
  35.2 15.2 %collective-permute-start.9 = (bf16[512,512]{1,0:T(8,128)(2,1)S(1)}, bf16[512,512]{1,0:T(8,128)(2,1)S(1)}, u32[]{:S(2)}, u32[]{:S(2)}) collective-permute-start(bf16[512,512]{1,0:T(8,128)(2,1)S(1)} %slice_bitcast_fusion), channel_id=1, source_target_pairs={{0,2},{1,3},{2,0},{3,1},{4,6},{5,7},{6,4},{7,5},{8,10},{9,11},{10,... | collective-permute-start | bytes 1572872 | tf_op jit(solution)/shard_map/ppermute | solution.py:288
  50.4 3.5 %collective-permute-start.10 = (bf16[1536,512]{1,0:T(8,128)(2,1)S(1)}, bf16[1536,512]{1,0:T(8,128)(2,1)S(1)}, u32[]{:S(2)}, u32[]{:S(2)}) collective-permute-start(bf16[1536,512]{1,0:T(8,128)(2,1)S(1)} %get-tuple-element.68), channel_id=1, source_target_pairs={{0,1},{1,0},{2,3},{3,2},{4,5},{5,4},{6,7},{7,6},{8,9},{9,8},{10,11... | collective-permute-start | bytes 4718600 | tf_op jit(solution)/shard_map/ppermute | solution.py:288
  50.6 4.9 %collective-permute-start.11 = (bf16[1024,512]{1,0:T(8,128)(2,1)S(1)}, bf16[1024,512]{1,0:T(8,128)(2,1)S(1)}, u32[]{:S(2)}, u32[]{:S(2)}) collective-permute-start(bf16[1024,512]{1,0:T(8,128)(2,1)S(1)} %pad_maximum_fusion.1), channel_id=1, source_target_pairs={{0,1},{1,0},{2,3},{3,2},{4,5},{5,4},{6,7},{7,6},{8,9},{9,8},{10,11... | collective-permute-start | bytes 3145736 | tf_op jit(solution)/shard_map/ppermute | solution.py:288
  54.3 16.6 %collective-permute-start.17 = (bf16[528,512]{1,0:T(8,128)(2,1)S(1)}, bf16[528,512]{1,0:T(8,128)(2,1)S(1)}, u32[]{:S(2)}, u32[]{:S(2)}) collective-permute-start(bf16[528,512]{1,0:T(8,128)(2,1)S(1)} %get-tuple-element.84), channel_id=1, source_target_pairs={{0,2},{1,3},{2,0},{3,1},{4,6},{5,7},{6,4},{7,5},{8,10},{9,11},{10,... | collective-permute-start | bytes 1622024 | tf_op jit(solution)/shard_map/ppermute | solution.py:288
  54.9 25.3 %collective-permute-start.18 = (bf16[528,512]{1,0:T(8,128)(2,1)S(1)}, bf16[528,512]{1,0:T(8,128)(2,1)S(1)}, u32[]{:S(2)}, u32[]{:S(2)}) collective-permute-start(bf16[528,512]{1,0:T(8,128)(2,1)S(1)} %get-tuple-element.86), channel_id=1, source_target_pairs={{0,4},{1,5},{2,6},{3,7},{4,0},{5,1},{6,2},{7,3},{8,12},{9,13},{10,... | collective-permute-start | bytes 1622024 | tf_op jit(solution)/shard_map/ppermute | solution.py:288
  59.0 2.2 %collective-permute-start.12 = (bf16[512,512]{1,0:T(8,128)(2,1)S(1)}, bf16[512,512]{1,0:T(8,128)(2,1)S(1)}, u32[]{:S(2)}, u32[]{:S(2)}) collective-permute-start(bf16[512,512]{1,0:T(8,128)(2,1)S(1)} %get-tuple-element.76), channel_id=1, source_target_pairs={{0,1},{1,0},{2,3},{3,2},{4,5},{5,4},{6,7},{7,6},{8,9},{9,8},{10,11... | collective-permute-start | bytes 1572872 | tf_op jit(solution)/shard_map/ppermute | solution.py:288
  59.1 6.4 %collective-permute-start.15 = (bf16[64,1024]{1,0:T(8,128)(2,1)S(1)}, bf16[64,1024]{1,0:T(8,128)(2,1)S(1)}, u32[]{:S(2)}, u32[]{:S(2)}) collective-permute-start(bf16[64,1024]{1,0:T(8,128)(2,1)S(1)} %get-tuple-element.81), channel_id=1, source_target_pairs={{0,8},{1,9},{2,10},{3,11},{4,12},{5,13},{6,14},{7,15},{8,0},{9,1},... | collective-permute-start | bytes 393224 | tf_op jit(solution)/shard_map/ppermute | solution.py:288
  60.1 8.0 %collective-permute-start.13 = (bf16[64,1024]{1,0:T(8,128)(2,1)S(1)}, bf16[64,1024]{1,0:T(8,128)(2,1)S(1)}, u32[]{:S(2)}, u32[]{:S(2)}) collective-permute-start(bf16[64,1024]{1,0:T(8,128)(2,1)S(1)} %get-tuple-element.78), channel_id=1, source_target_pairs={{0,8},{1,9},{2,10},{3,11},{4,12},{5,13},{6,14},{7,15},{8,0},{9,1},... | collective-permute-start | bytes 393224 | tf_op jit(solution)/shard_map/ppermute | solution.py:288
  61.3 19.0 %collective-permute-start.19 = (bf16[512,512]{1,0:T(8,128)(2,1)S(1)}, bf16[512,512]{1,0:T(8,128)(2,1)S(1)}, u32[]{:S(2)}, u32[]{:S(2)}) collective-permute-start(bf16[512,512]{1,0:T(8,128)(2,1)S(1)} %pair_sum_diagonal.1), channel_id=1, source_target_pairs={{0,6},{1,7},{2,4},{3,5},{4,2},{5,3},{6,0},{7,1},{8,14},{9,15},{10,... | collective-permute-start | bytes 1572872 | tf_op jit(solution)/shard_map/ppermute | solution.py:288
  65.5 15.8 %collective-permute-start.16 = (bf16[64,1024]{1,0:T(8,128)(2,1)S(1)}, bf16[64,1024]{1,0:T(8,128)(2,1)S(1)}, u32[]{:S(2)}, u32[]{:S(2)}) collective-permute-start(bf16[64,1024]{1,0:T(8,128)(2,1)S(1)} %line_sum.3), channel_id=1, source_target_pairs={{0,16},{1,17},{2,18},{3,19},{4,20},{5,21},{6,22},{7,23},{8,24},{9,... | collective-permute-start | bytes 393224 | tf_op jit(solution)/shard_map/ppermute | solution.py:288
  68.1 13.2 %collective-permute-start.14 = (bf16[64,1024]{1,0:T(8,128)(2,1)S(1)}, bf16[64,1024]{1,0:T(8,128)(2,1)S(1)}, u32[]{:S(2)}, u32[]{:S(2)}) collective-permute-start(bf16[64,1024]{1,0:T(8,128)(2,1)S(1)} %line_sum.2), channel_id=1, source_target_pairs={{0,16},{1,17},{2,18},{3,19},{4,20},{5,21},{6,22},{7,23},{8,24},{9,... | collective-permute-start | bytes 393224 | tf_op jit(solution)/shard_map/ppermute | solution.py:288
  70.9 11.1 %collective-permute-start.20 = (bf16[128,1024]{1,0:T(8,128)(2,1)S(1)}, bf16[128,1024]{1,0:T(8,128)(2,1)S(1)}, u32[]{:S(2)}, u32[]{:S(2)}) collective-permute-start(bf16[128,1024]{1,0:T(8,128)(2,1)S(1)} %get-tuple-element.89), channel_id=1, source_target_pairs={{0,8},{1,9},{2,10},{3,11},{4,12},{5,13},{6,14},{7,15},{8,0},{9,1},... | collective-permute-start | bytes 786440 | tf_op jit(solution)/shard_map/ppermute | solution.py:288

commit v15 on v14

--- a/solution.py
+++ b/solution.py
@@ -162,10 +162,10 @@
 
 def output_kernel(owned, *refs):
     act_two, tok, early_mixed, w_in, w_out, bias, w_three = refs[:7]
-    mine_ref, other_ref, slope_ref, w_in_all, w_out_all, bias_all = refs[7:13]
-    w_last, sem = refs[13:]
+    mine_ref, near_ref, own_ref, slope_ref, w_in_all, w_out_all, bias_all = refs[7:14]
+    w_last, sem = refs[14:]
     core = lax.axis_index("core")
-    feats = mine_ref.shape[1]
+    rows, feats = own_ref.shape
     two, three = 2 * owned, 3 * owned
     first, last = pl.ds(0, three), pl.ds(three, owned)
     copies = [
@@ -186,9 +186,13 @@
         value, slope = activate(tok[spot, :], w_three[:owned, :], bias_last[0:1, :])
         slope_ref[spot, :] = slope
         act = jnp.concatenate([act_two[spot, :], value.astype(jnp.bfloat16)], axis=1)
-        for shift, ref in enumerate((mine_ref, other_ref)):
+        if at * step < rows:
+            far_ref, there = own_ref, spot
+        else:
+            far_ref, there = near_ref, slice(at * step - rows, (at + 1) * step - rows)
+        for shift, ref, to in ((0, mine_ref, spot), (1, far_ref, there)):
             half = half_columns(core, shift, feats)
-            ref[spot, :] = (
+            ref[to, :] = (
                 early_mixed[spot, half]
                 + jnp.dot(act, w_last[:, half], preferred_element_type=jnp.float32)
             ).astype(jnp.bfloat16)
@@ -245,14 +249,25 @@
     one_ref[...] = grad[owned:].astype(jnp.bfloat16)
 
 
-def pair_kernel(rows, mine_ref, other_ref, *out_refs):
+def pair_kernel(rows, first, mine_ref, other_ref, *out_refs):
     for block, ref in enumerate(out_refs):
-        spot = pl.ds(block * rows, rows)
+        mine, other = pl.ds((first + block) * rows, rows), pl.ds(block * rows, rows)
         ref[:rows, :] = (
-            mine_ref[spot, :].astype(jnp.float32) + other_ref[spot, :].astype(jnp.float32)
+            mine_ref[mine, :].astype(jnp.float32) + other_ref[other, :].astype(jnp.float32)
         ).astype(jnp.bfloat16)
         if ref.shape[0] > rows:
             ref[rows:, :] = jnp.zeros_like(ref[rows:, :])
+
+
+def last_pairs_kernel(mine_ref, far_ref, diag_ref, other_ref, own_sum_ref, diag_sum_ref):
+    rows = diag_ref.shape[0]
+    diag_sum_ref[...] = (
+        diag_ref[...].astype(jnp.float32) + other_ref[...].astype(jnp.float32)
+    ).astype(jnp.bfloat16)
+    own_sum_ref[...] = (
+        mine_ref[:rows, :].astype(jnp.float32)
+        + far_ref[2 * rows : 3 * rows, :].astype(jnp.float32)
+    ).astype(jnp.bfloat16)
 
 
 def plane_kernel(own_ref, x_ref, y_ref, out_ref):
@@ -364,18 +379,19 @@
         )(own, own_other, from_x, x_other, from_y, y_other, own_w, w_one, w_two)
     )
 
-    mine, other, slope, w_in_all, w_out_all, bias = pl.pallas_call(
+    mine, other, other_own, slope, w_in_all, w_out_all, bias = pl.pallas_call(
         functools.partial(output_kernel, owned),
         out_shape=(
             bf16(early_rows, feats),
-            bf16(early_rows, feats),
+            bf16(2 * rows, feats),
+            bf16(rows, feats),
             f32(early_rows, owned),
             bf16(units, width),
             bf16(units, width),
             f32(BIAS_ROWS, units),
         ),
         in_specs=vmem(7),
-        out_specs=vmem(6),
+        out_specs=vmem(7),
         scratch_shapes=[pltpu.VMEM((2 * owned, width), jnp.bfloat16), dma((4,))],
         compiler_params=params,
         cost_estimate=cost(early_rows * units, early_rows),
@@ -383,7 +399,7 @@
     )(act_two, tok, mixed_terms, w_in_three, w_out_three, bias, w_three)
     tok_diag, cot_diag, other = barrier((tok_diag, cot_diag, other))
     received = to_core(other)
-    diag_other = to_core(jnp.concatenate([tok_diag[:rows], cot_diag]))
+    diag_other = to_core(jnp.concatenate([tok_diag[:rows], cot_diag, other_own]))
     slope, tok_diag = barrier((slope, tok_diag))
     grad_last = pl.pallas_call(
         gradient_kernel,
@@ -398,15 +414,15 @@
 
     mine, grad_last = barrier((mine, grad_last))
     sums = pl.pallas_call(
-        functools.partial(pair_kernel, rows),
-        out_shape=[bf16(rows, feats)] + [bf16(rows + MORE, feats)] * 2,
+        functools.partial(pair_kernel, rows, 1),
+        out_shape=[bf16(rows + MORE, feats)] * 2,
         in_specs=vmem(2),
-        out_specs=vmem(NEAR - 1),
+        out_specs=vmem(2),
         compiler_params=params,
         cost_estimate=cost(rows, rows),
         name="pair_sum",
     )(mine, received)
-    mixed_x, mixed_y = to_x(sums[1]), to_y(sums[2])
+    mixed_x, mixed_y = to_x(sums[0]), to_y(sums[1])
     grad_terms, mixed_own = barrier((grad_terms, sums[0]))
 
     mine_diag, other_diag, grad_own, grad_one, *grad_far = pl.pallas_call(
@@ -432,21 +448,21 @@
     )
     received_diag = to_core(other_diag)
     relayed = [to_far(piece, 1) for piece in grad_far[PARTS:]]
-    (sum_diag,) = pl.pallas_call(
-        functools.partial(pair_kernel, rows),
-        out_shape=[bf16(rows, feats)],
-        in_specs=vmem(2),
-        out_specs=vmem(1),
+    mixed_own, sum_diag = pl.pallas_call(
+        last_pairs_kernel,
+        out_shape=[bf16(rows, feats)] * 2,
+        in_specs=vmem(4),
+        out_specs=vmem(2),
         compiler_params=params,
         cost_estimate=cost(rows, rows),
         name="pair_sum_diagonal",
-    )(mine_diag, received_diag)
+    )(mine, diag_other, mine_diag, received_diag)
     mixed_diag = to_diagonal(sum_diag)
     from_two = []
     for at in range(PARTS):
         piece, _ = barrier((grad_far[at], sum_diag))
         (line_sum,) = pl.pallas_call(
-            functools.partial(pair_kernel, owned // PARTS),
+            functools.partial(pair_kernel, owned // PARTS, 0),
             out_shape=[bf16(owned // PARTS, width)],
             in_specs=vmem(2),
             out_specs=vmem(1),
@@ -455,7 +471,7 @@
             name="line_sum",
         )(piece, relayed[at])
         from_two.append(to_far(line_sum, 2))
-    grad_one, mixed_x = barrier((grad_one, mixed_x))
+    grad_one, mixed_x, _ = barrier((grad_one, mixed_x, line_sum))
     from_one = to_far(grad_one, 1)
     mixed = pl.pallas_call(
         plane_kernel,

time: 83.1 us -> 85.1 us (1.024)
  waiting for transfers between devices: 38.6 us -> 40.4 us
    ppermute x21, waiting for transfers between devices: 38.6 us -> 40.4 us  [permute(): return lax.ppermute(value, AXES, pairs)]
  transfers between devices with their start and end apart: 21 -> 21, of which waited for: 8 -> 9; matrix products, arithmetic and copies ran while one was open for 1% -> 1% of each run, Pallas kernels for 19% -> 19%
where the time goes in v15:
time: 85.1 us; the launch traced here: 85 us
  waiting for transfers between devices  40.4 us (47%)
  starting transfers between devices  24.3 us (29%)
  Pallas kernels  16 us (19%)
  other arithmetic  3.36 us (4%)
    ppermute x21, waiting for transfers between devices, permute(): return lax.ppermute(value, AXES, pairs)  40.4 us
    ppermute x21, starting transfers between devices, permute(): return lax.ppermute(value, AXES, pairs)  24.3 us
    pallas_call x1, Pallas kernels, on_device_lines(): pl.pallas_call(functools.partial(early_kernel, owned), out_shape=(bf16(ea...  7.43 us
    pallas_call x1, Pallas kernels, on_device_lines(): pl.pallas_call(functools.partial(diagonal_kernel, owned), out_shape=[bf16...  3.46 us
    pallas_call x1, Pallas kernels, on_device_lines(): pl.pallas_call(functools.partial(output_kernel, owned), out_shape=(bf16(e...  2.57 us
    pallas_call x1, Pallas kernels, on_device_lines(): pl.pallas_call(gradient_kernel, out_shape=f32(2 * owned, width), in_specs...  1.82 us
  transfers between devices with their start and end apart: 21, of which 9 were waited for; matrix products, arithmetic and copies ran while one was open for 1% of the time, Pallas kernels for 19%

profile of v15, /device:TPU:0, one launch (start us, length us, event | category | flops | bytes accessed | tf_op | source)
XLA Modules:
  0.0 85.0 jit_solution(13725947912673310934)
XLA Ops:
  0.7 1.4 %pad_maximum_fusion.1.refs_0_ = bf16[2,512,512]{2,1,0:T(8,128)(2,1)S(1)} fusion(bf16[1,512,512]{2,1,0:T(8,128)(2,1)} %bitcast.7, bf16[1,512,512]{2,1,0:T(8,128)(2,1)} %bitcast.8), kind=kLoop, calls=%fused_computation.3 | loop fusion | flops 524288 | bytes 2097152 | tf_op jit(solution)/shard_map/stack | solution.py:345
  2.0 3.0 %collective-permute-start = (bf16[2,512,512]{2,1,0:T(8,128)(2,1)S(1)}, bf16[2,512,512]{2,1,0:T(8,128)(2,1)S(1)}, u32[]{:S(2)}, u32[]{:S(2)}) collective-permute-start(bf16[2,512,512]{2,1,0:T(8,128)(2,1)S(1)} %pad_maximum_fusion.1.refs_0_), channel_id=1, source_target_pairs={{0,2},{1,3},{2,0},{3,1},{4,6},{5,7},{6,4},{7,5},{8,10},{9,11},{10,... | collective-permute-start | bytes 3145736 | tf_op jit(solution)/shard_map/ppermute | solution.py:303
  5.0 1.5 %collective-permute-start.1 = (bf16[2,512,512]{2,1,0:T(8,128)(2,1)S(1)}, bf16[2,512,512]{2,1,0:T(8,128)(2,1)S(1)}, u32[]{:S(2)}, u32[]{:S(2)}) collective-permute-start(bf16[2,512,512]{2,1,0:T(8,128)(2,1)S(1)} %pad_maximum_fusion.1.refs_0_), channel_id=1, source_target_pairs={{0,4},{1,5},{2,6},{3,7},{4,0},{5,1},{6,2},{7,3},{8,12},{9,13},{10,... | collective-permute-start | bytes 3145736 | tf_op jit(solution)/shard_map/ppermute | solution.py:303
  6.6 2.7 %collective-permute-start.6 = (bf16[264,1024]{1,0:T(8,128)(2,1)S(1)}, bf16[264,1024]{1,0:T(8,128)(2,1)S(1)}, u32[]{:S(2)}, u32[]{:S(2)}) collective-permute-start(bf16[264,1024]{1,0:T(8,128)(2,1)S(1)} %fusion.1.refs_6_), channel_id=1, source_target_pairs={{0,16},{1,17},{2,18},{3,19},{4,20},{5,21},{6,22},{7,23},{8,24},{9,... | collective-permute-start | bytes 1622024 | tf_op jit(solution)/shard_map/ppermute | solution.py:303
  9.3 1.6 %collective-permute-start.5 = (bf16[264,1024]{1,0:T(8,128)(2,1)S(1)}, bf16[264,1024]{1,0:T(8,128)(2,1)S(1)}, u32[]{:S(2)}, u32[]{:S(2)}) collective-permute-start(bf16[264,1024]{1,0:T(8,128)(2,1)S(1)} %fusion.1.refs_6_), channel_id=1, source_target_pairs={{0,8},{1,9},{2,10},{3,11},{4,12},{5,13},{6,14},{7,15},{8,0},{9,1},... | collective-permute-start | bytes 1622024 | tf_op jit(solution)/shard_map/ppermute | solution.py:303
  10.8 17.3 %collective-permute-done.refs_2_ = bf16[2,512,512]{2,1,0:T(8,128)(2,1)S(1)} collective-permute-done((bf16[2,512,512]{2,1,0:T(8,128)(2,1)S(1)}, bf16[2,512,512]{2,1,0:T(8,128)(2,1)S(1)}, u32[]{:S(2)}, u32[]{:S(2)}) %collective-permute-start) | collective-permute-done | bytes 1048608 | tf_op jit(solution)/shard_map/ppermute | solution.py:303
  28.2 1.5 %collective-permute-done.1.refs_4_ = bf16[2,512,512]{2,1,0:T(8,128)(2,1)S(1)} collective-permute-done((bf16[2,512,512]{2,1,0:T(8,128)(2,1)S(1)}, bf16[2,512,512]{2,1,0:T(8,128)(2,1)S(1)}, u32[]{:S(2)}, u32[]{:S(2)}) %collective-permute-start.1) | collective-permute-done | bytes 1048608 | tf_op jit(solution)/shard_map/ppermute | solution.py:303
  29.6 0.5 collective-permute-start.4
  30.2 3.8 %collective-permute-done.6.refs_8_ = bf16[264,1024]{1,0:T(8,128)(2,1)S(1)} collective-permute-done((bf16[264,1024]{1,0:T(8,128)(2,1)S(1)}, bf16[264,1024]{1,0:T(8,128)(2,1)S(1)}, u32[]{:S(2)}, u32[]{:S(2)}) %collective-permute-start.6) | collective-permute-done | bytes 540704 | tf_op jit(solution)/shard_map/ppermute | solution.py:303
  33.9 0.6 collective-permute-start.7
  34.6 0.6 collective-permute-start.8
  35.2 0.6 collective-permute-start.9
  35.8 7.4 %early.1 = (bf16[1536,128]{1,0:T(8,128)(2,1)S(1)}, bf16[1536,128]{1,0:T(8,128)(2,1)S(1)}, f32[1536,1024]{1,0:T(8,128)S(1)}, f32[256,1024]{1,0:T(8,128)S(1)}, bf1...) custom-call(bf16[2,512,512]{2,1,0:T(8,128)(2,1)S(1)} %pad_maximum_fu, ...), custom_call_target="tpu_custom_call" | custom-call | flops 786432 | bytes 1536 | tf_op jit(solution)/shard_map/early/pallas_call | solution.py:355
  43.2 4.5 %collective-permute-done.7.refs_6_.w_three = bf16[264,1024]{1,0:T(8,128)(2,1)S(1)} collective-permute-done((bf16[264,1024]{1,0:T(8,128)(2,1)S(1)}, bf16[264,1024]{1,0:T(8,128)(2,1)S(1)}, u32[]{:S(2)}, u32[]{:S(2)}) %collective-permute-start.7) | collective-permute-done | bytes 540704 | tf_op jit(solution)/shard_map/ppermute | solution.py:303
  47.8 2.6 %output.1 = (bf16[1536,512]{1,0:T(8,128)(2,1)S(1)}, bf16[1024,512]{1,0:T(8,128)(2,1)S(1)}, bf16[512,512]{1,0:T(8,128)(2,1)S(1)}, f32[1536,128]{1,0:T(8,128)S(1)}...) custom-call(bf16[1536,128]{1,0:T(8,128)(2,1)S(1)} %get-tuple-element.51.refs_0_, ...), custom_call_target="tpu_custom_call" | custom-call | flops 786432 | bytes 1536 | tf_op jit(solution)/shard_map/output/pallas_call | solution.py:382
  51.1 1.8 %gradient.1.refs_4_ = f32[256,1024]{1,0:T(8,128)S(1)} custom-call(bf16[1536,128]{1,0:T(8,128)(2,1)S(1)} %get-tuple-element.62.dpre_two, bf16[1536,1024]{1,0:T(8,128)(2,1)S(1)} %get-tuple-element.52.refs_1_.tok, bf16[1536,1024]{1,0:T(8,128)(2,1)S(1)} %get-tuple-element.63.cot, f32[1536,128]{1,0:T(8,128)S(1)} %get-tuple-element.67.slope, ...), custom_call_target="tpu_custom_call" | custom-call | flops 10000000000 | bytes 1536 | tf_op jit(solution)/shard_map/gradient/pallas_call | solution.py:404
  52.9 2.6 %collective-permute-done.10.other_ref = bf16[1024,512]{1,0:T(8,128)(2,1)S(1)} collective-permute-done((bf16[1024,512]{1,0:T(8,128)(2,1)S(1)}, bf16[1024,512]{1,0:T(8,128)(2,1)S(1)}, u32[]{:S(2)}, u32[]{:S(2)}) %collective-permute-start.10) | collective-permute-done | bytes 1048608 | tf_op jit(solution)/shard_map/ppermute | solution.py:303
  55.8 0.6 collective-permute-start.17
  56.4 0.7 collective-permute-start.18
  57.0 3.5 %diagonal.1 = (bf16[512,512]{1,0:T(8,128)(2,1)S(1)}, bf16[512,512]{1,0:T(8,128)(2,1)S(1)}, bf16[128,1024]{1,0:T(8,128)(2,1)S(1)}, bf16[128,1024]{1,0:T(8,128)(2,...) custom-call(bf16[512,1024]{1,0:T(8,128)(2,1)S(1)} %get-tuple-element, ...), custom_call_target="tpu_custom_call" | custom-call | flops 1000000 | bytes 512 | tf_op jit(solution)/shard_map/diagonal/pallas_call | solution.py:428
  60.6 0.9 %collective-permute-start.15 = (bf16[64,1024]{1,0:T(8,128)(2,1)S(1)}, bf16[64,1024]{1,0:T(8,128)(2,1)S(1)}, u32[]{:S(2)}, u32[]{:S(2)}) collective-permute-start(bf16[64,1024]{1,0:T(8,128)(2,1)S(1)} %get-tuple-element.84), channel_id=1, source_target_pairs={{0,8},{1,9},{2,10},{3,11},{4,12},{5,13},{6,14},{7,15},{8,0},{9,1},... | collective-permute-start | bytes 393224 | tf_op jit(solution)/shard_map/ppermute | solution.py:303
  61.5 1.2 %collective-permute-start.13 = (bf16[64,1024]{1,0:T(8,128)(2,1)S(1)}, bf16[64,1024]{1,0:T(8,128)(2,1)S(1)}, u32[]{:S(2)}, u32[]{:S(2)}) collective-permute-start(bf16[64,1024]{1,0:T(8,128)(2,1)S(1)} %get-tuple-element.81), channel_id=1, source_target_pairs={{0,8},{1,9},{2,10},{3,11},{4,12},{5,13},{6,14},{7,15},{8,0},{9,1},... | collective-permute-start | bytes 393224 | tf_op jit(solution)/shard_map/ppermute | solution.py:303
  62.9 2.4 %collective-permute-start.19 = (bf16[512,512]{1,0:T(8,128)(2,1)S(1)}, bf16[512,512]{1,0:T(8,128)(2,1)S(1)}, u32[]{:S(2)}, u32[]{:S(2)}) collective-permute-start(bf16[512,512]{1,0:T(8,128)(2,1)S(1)} %get-tuple-element.79), channel_id=1, source_target_pairs={{0,6},{1,7},{2,4},{3,5},{4,2},{5,3},{6,0},{7,1},{8,14},{9,15},{10,... | collective-permute-start | bytes 1572872 | tf_op jit(solution)/shard_map/ppermute | solution.py:303
  65.3 1.6 %collective-permute-done.15.other_ref = bf16[64,1024]{1,0:T(8,128)(2,1)S(1)} collective-permute-done((bf16[64,1024]{1,0:T(8,128)(2,1)S(1)}, bf16[64,1024]{1,0:T(8,128)(2,1)S(1)}, u32[]{:S(2)}, u32[]{:S(2)}) %collective-permute-start.15) | collective-permute-done | bytes 131104 | tf_op jit(solution)/shard_map/ppermute | solution.py:303
  67.0 2.5 %collective-permute-start.16 = (bf16[64,1024]{1,0:T(8,128)(2,1)S(1)}, bf16[64,1024]{1,0:T(8,128)(2,1)S(1)}, u32[]{:S(2)}, u32[]{:S(2)}) collective-permute-start(bf16[64,1024]{1,0:T(8,128)(2,1)S(1)} %line_sum.3), channel_id=1, source_target_pairs={{0,16},{1,17},{2,18},{3,19},{4,20},{5,21},{6,22},{7,23},{8,24},{9,... | collective-permute-start | bytes 393224 | tf_op jit(solution)/shard_map/ppermute | solution.py:303
  69.6 1.4 %collective-permute-done.17.x_ref = bf16[528,512]{1,0:T(8,128)(2,1)S(1)} collective-permute-done((bf16[528,512]{1,0:T(8,128)(2,1)S(1)}, bf16[528,512]{1,0:T(8,128)(2,1)S(1)}, u32[]{:S(2)}, u32[]{:S(2)}) %collective-permute-start.17) | collective-permute-done | bytes 540704 | tf_op jit(solution)/shard_map/ppermute | solution.py:303
  71.0 2.6 %collective-permute-start.14 = (bf16[64,1024]{1,0:T(8,128)(2,1)S(1)}, bf16[64,1024]{1,0:T(8,128)(2,1)S(1)}, u32[]{:S(2)}, u32[]{:S(2)}) collective-permute-start(bf16[64,1024]{1,0:T(8,128)(2,1)S(1)} %line_sum.2), channel_id=1, source_target_pairs={{0,16},{1,17},{2,18},{3,19},{4,20},{5,21},{6,22},{7,23},{8,24},{9,... | collective-permute-start | bytes 393224 | tf_op jit(solution)/shard_map/ppermute | solution.py:303
  73.6 1.7 %collective-permute-start.20 = (bf16[128,1024]{1,0:T(8,128)(2,1)S(1)}, bf16[128,1024]{1,0:T(8,128)(2,1)S(1)}, u32[]{:S(2)}, u32[]{:S(2)}) collective-permute-start(bf16[128,1024]{1,0:T(8,128)(2,1)S(1)} %get-tuple-element.91), channel_id=1, source_target_pairs={{0,8},{1,9},{2,10},{3,11},{4,12},{5,13},{6,14},{7,15},{8,0},{9,1},... | collective-permute-start | bytes 786440 | tf_op jit(solution)/shard_map/ppermute | solution.py:303
  75.3 6.3 %collective-permute-done.18.y_ref = bf16[528,512]{1,0:T(8,128)(2,1)S(1)} collective-permute-done((bf16[528,512]{1,0:T(8,128)(2,1)S(1)}, bf16[528,512]{1,0:T(8,128)(2,1)S(1)}, u32[]{:S(2)}, u32[]{:S(2)}) %collective-permute-start.18) | collective-permute-done | bytes 540704 | tf_op jit(solution)/shard_map/ppermute | solution.py:303
  81.8 1.0 %add_convert_fusion = bf16[512,512]{1,0:T(8,128)(2,1)} fusion(f32[512,512]{1,0:T(8,128)S(1)} %plane_sum.1, bf16[512,512]{1,0:T(8,128)(2,1)S(1)} %collective-permute-done.19), kind=kLoop, calls=%fused_computation.4 | loop fusion | flops 786432 | bytes 2097152 | tf_op jit(solution)/shard_map/convert_element_type | solution.py:485
  82.8 1.3 %collective-permute-done.20 = bf16[128,1024]{1,0:T(8,128)(2,1)S(1)} collective-permute-done((bf16[128,1024]{1,0:T(8,128)(2,1)S(1)}, bf16[128,1024]{1,0:T(8,128)(2,1)S(1)}, u32[]{:S(2)}, u32[]{:S(2)}) %collective-permute-start.20) | collective-permute-done | bytes 262176 | tf_op jit(solution)/shard_map/ppermute | solution.py:303
  84.1 0.9 %add_multiply_fusion = f32[128,1024]{1,0:T(8,128)} fusion(bf16[128,1024]{1,0:T(8,128)(2,1)S(1)} %collective-permute-done.20, bf16[128,1024]{1,0:T(8,128)(2,1)S(1)} %get-tuple-element.90, bf16[64,1024]{1,0:T(8,128)(2,1)S(1)} %collective-permute-done.16, bf16[64,1024]{1,0:T(8,128)(2,1)S(1)} %collective-permute-done.14), kind=kLoop, calls=%fused_computation.6 | loop fusion | flops 1179648 | bytes 1310720 | tf_op jit(solution)/shard_map/mul | solution.py:493
  (33 shorter events, 1.7 us)
Async XLA Ops:
  0.6 5.9 %copy-start.2 = (bf16[128]{0:T(256)(128)(2,1)S(1)}, bf16[128]{0:T(256)(128)(2,1)}, u32[]{:S(2)}) copy-start(bf16[128]{0:T(256)(128)(2,1)} %param.8) | copy-start | bytes 772
  0.6 5.9 %copy-start.1 = (bf16[128,1024]{1,0:T(8,128)(2,1)S(1)}, bf16[128,1024]{1,0:T(8,128)(2,1)}, u32[]{:S(2)}) copy-start(bf16[128,1024]{1,0:T(8,128)(2,1)} %param.7) | copy-start | bytes 786436
  0.7 5.9 %copy-start = (bf16[128,1024]{1,0:T(8,128)(2,1)S(1)}, bf16[128,1024]{1,0:T(8,128)(2,1)}, u32[]{:S(2)}) copy-start(bf16[128,1024]{1,0:T(8,128)(2,1)} %param.9) | copy-start | bytes 786436
  2.0 26.2 %collective-permute-start = (bf16[2,512,512]{2,1,0:T(8,128)(2,1)S(1)}, bf16[2,512,512]{2,1,0:T(8,128)(2,1)S(1)}, u32[]{:S(2)}, u32[]{:S(2)}) collective-permute-start(bf16[2,512,512]{2,1,0:T(8,128)(2,1)S(1)} %pad_maximum_fusion.1.refs_0_), channel_id=1, source_target_pairs={{0,2},{1,3},{2,0},{3,1},{4,6},{5,7},{6,4},{7,5},{8,10},{9,11},{10,... | collective-permute-start | bytes 3145736 | tf_op jit(solution)/shard_map/ppermute | solution.py:303
  5.0 24.6 %collective-permute-start.1 = (bf16[2,512,512]{2,1,0:T(8,128)(2,1)S(1)}, bf16[2,512,512]{2,1,0:T(8,128)(2,1)S(1)}, u32[]{:S(2)}, u32[]{:S(2)}) collective-permute-start(bf16[2,512,512]{2,1,0:T(8,128)(2,1)S(1)} %pad_maximum_fusion.1.refs_0_), channel_id=1, source_target_pairs={{0,4},{1,5},{2,6},{3,7},{4,0},{5,1},{6,2},{7,3},{8,12},{9,13},{10,... | collective-permute-start | bytes 3145736 | tf_op jit(solution)/shard_map/ppermute | solution.py:303
  6.5 23.1 %collective-permute-start.2 = (bf16[2,512,512]{2,1,0:T(8,128)(2,1)S(1)}, bf16[2,512,512]{2,1,0:T(8,128)(2,1)S(1)}, u32[]{:S(2)}, u32[]{:S(2)}) collective-permute-start(bf16[2,512,512]{2,1,0:T(8,128)(2,1)S(1)} %pad_maximum_fusion.1.refs_0_), channel_id=1, source_target_pairs={{0,1},{1,0},{2,3},{3,2},{4,5},{5,4},{6,7},{7,6},{8,9},{9,8},{10,11... | collective-permute-start | bytes 3145736 | tf_op jit(solution)/shard_map/ppermute | solution.py:303
  6.6 27.3 %collective-permute-start.6 = (bf16[264,1024]{1,0:T(8,128)(2,1)S(1)}, bf16[264,1024]{1,0:T(8,128)(2,1)S(1)}, u32[]{:S(2)}, u32[]{:S(2)}) collective-permute-start(bf16[264,1024]{1,0:T(8,128)(2,1)S(1)} %fusion.1.refs_6_), channel_id=1, source_target_pairs={{0,16},{1,17},{2,18},{3,19},{4,20},{5,21},{6,22},{7,23},{8,24},{9,... | collective-permute-start | bytes 1622024 | tf_op jit(solution)/shard_map/ppermute | solution.py:303
  9.3 25.9 %collective-permute-start.5 = (bf16[264,1024]{1,0:T(8,128)(2,1)S(1)}, bf16[264,1024]{1,0:T(8,128)(2,1)S(1)}, u32[]{:S(2)}, u32[]{:S(2)}) collective-permute-start(bf16[264,1024]{1,0:T(8,128)(2,1)S(1)} %fusion.1.refs_6_), channel_id=1, source_target_pairs={{0,8},{1,9},{2,10},{3,11},{4,12},{5,13},{6,14},{7,15},{8,0},{9,1},... | collective-permute-start | bytes 1622024 | tf_op jit(solution)/shard_map/ppermute | solution.py:303
  29.6 6.1 %collective-permute-start.3 = (bf16[2,512,512]{2,1,0:T(8,128)(2,1)S(1)}, bf16[2,512,512]{2,1,0:T(8,128)(2,1)S(1)}, u32[]{:S(2)}, u32[]{:S(2)}) collective-permute-start(bf16[2,512,512]{2,1,0:T(8,128)(2,1)S(1)} %collective-permute-done.refs_2_), channel_id=1, source_target_pairs={{0,1},{1,0},{2,3},{3,2},{4,5},{5,4},{6,7},{7,6},{8,9},{9,8},{10,11... | collective-permute-start | bytes 3145736 | tf_op jit(solution)/shard_map/ppermute | solution.py:303
  29.6 6.1 %collective-permute-start.4 = (bf16[2,512,512]{2,1,0:T(8,128)(2,1)S(1)}, bf16[2,512,512]{2,1,0:T(8,128)(2,1)S(1)}, u32[]{:S(2)}, u32[]{:S(2)}) collective-permute-start(bf16[2,512,512]{2,1,0:T(8,128)(2,1)S(1)} %collective-permute-done.1.refs_4_), channel_id=1, source_target_pairs={{0,1},{1,0},{2,3},{3,2},{4,5},{5,4},{6,7},{7,6},{8,9},{9,8},{10,11... | collective-permute-start | bytes 3145736 | tf_op jit(solution)/shard_map/ppermute | solution.py:303
  33.9 13.8 %collective-permute-start.7 = (bf16[264,1024]{1,0:T(8,128)(2,1)S(1)}, bf16[264,1024]{1,0:T(8,128)(2,1)S(1)}, u32[]{:S(2)}, u32[]{:S(2)}) collective-permute-start(bf16[264,1024]{1,0:T(8,128)(2,1)S(1)} %collective-permute-done.6.refs_8_), channel_id=1, source_target_pairs={{0,8},{1,9},{2,10},{3,11},{4,12},{5,13},{6,14},{7,15},{8,0},{9,1},... | collective-permute-start | bytes 1622024 | tf_op jit(solution)/shard_map/ppermute | solution.py:303
  34.6 15.8 %collective-permute-start.8 = (bf16[560,512]{1,0:T(8,128)(2,1)S(1)}, bf16[560,512]{1,0:T(8,128)(2,1)S(1)}, u32[]{:S(2)}, u32[]{:S(2)}) collective-permute-start(bf16[560,512]{1,0:T(8,128)(2,1)S(1)} %slice.12), channel_id=1, source_target_pairs={{0,4},{1,5},{2,6},{3,7},{4,0},{5,1},{6,2},{7,3},{8,12},{9,13},{10,... | collective-permute-start | bytes 1720328 | tf_op jit(solution)/shard_map/ppermute | solution.py:303
  35.2 15.2 %collective-permute-start.9 = (bf16[512,512]{1,0:T(8,128)(2,1)S(1)}, bf16[512,512]{1,0:T(8,128)(2,1)S(1)}, u32[]{:S(2)}, u32[]{:S(2)}) collective-permute-start(bf16[512,512]{1,0:T(8,128)(2,1)S(1)} %slice_bitcast_fusion), channel_id=1, source_target_pairs={{0,2},{1,3},{2,0},{3,1},{4,6},{5,7},{6,4},{7,5},{8,10},{9,11},{10,... | collective-permute-start | bytes 1572872 | tf_op jit(solution)/shard_map/ppermute | solution.py:303
  50.5 6.5 %collective-permute-start.11 = (bf16[1536,512]{1,0:T(8,128)(2,1)S(1)}, bf16[1536,512]{1,0:T(8,128)(2,1)S(1)}, u32[]{:S(2)}, u32[]{:S(2)}) collective-permute-start(bf16[1536,512]{1,0:T(8,128)(2,1)S(1)} %pad_maximum_fusion), channel_id=1, source_target_pairs={{0,1},{1,0},{2,3},{3,2},{4,5},{5,4},{6,7},{7,6},{8,9},{9,8},{10,11... | collective-permute-start | bytes 4718600 | tf_op jit(solution)/shard_map/ppermute | solution.py:303
  50.6 4.9 %collective-permute-start.10 = (bf16[1024,512]{1,0:T(8,128)(2,1)S(1)}, bf16[1024,512]{1,0:T(8,128)(2,1)S(1)}, u32[]{:S(2)}, u32[]{:S(2)}) collective-permute-start(bf16[1024,512]{1,0:T(8,128)(2,1)S(1)} %get-tuple-element.69), channel_id=1, source_target_pairs={{0,1},{1,0},{2,3},{3,2},{4,5},{5,4},{6,7},{7,6},{8,9},{9,8},{10,11... | collective-permute-start | bytes 3145736 | tf_op jit(solution)/shard_map/ppermute | solution.py:303
  55.8 15.2 %collective-permute-start.17 = (bf16[528,512]{1,0:T(8,128)(2,1)S(1)}, bf16[528,512]{1,0:T(8,128)(2,1)S(1)}, u32[]{:S(2)}, u32[]{:S(2)}) collective-permute-start(bf16[528,512]{1,0:T(8,128)(2,1)S(1)} %get-tuple-element.70), channel_id=1, source_target_pairs={{0,2},{1,3},{2,0},{3,1},{4,6},{5,7},{6,4},{7,5},{8,10},{9,11},{10,... | collective-permute-start | bytes 1622024 | tf_op jit(solution)/shard_map/ppermute | solution.py:303
  56.4 25.3 %collective-permute-start.18 = (bf16[528,512]{1,0:T(8,128)(2,1)S(1)}, bf16[528,512]{1,0:T(8,128)(2,1)S(1)}, u32[]{:S(2)}, u32[]{:S(2)}) collective-permute-start(bf16[528,512]{1,0:T(8,128)(2,1)S(1)} %get-tuple-element.88), channel_id=1, source_target_pairs={{0,4},{1,5},{2,6},{3,7},{4,0},{5,1},{6,2},{7,3},{8,12},{9,13},{10,... | collective-permute-start | bytes 1622024 | tf_op jit(solution)/shard_map/ppermute | solution.py:303
  60.5 2.2 %collective-permute-start.12 = (bf16[512,512]{1,0:T(8,128)(2,1)S(1)}, bf16[512,512]{1,0:T(8,128)(2,1)S(1)}, u32[]{:S(2)}, u32[]{:S(2)}) collective-permute-start(bf16[512,512]{1,0:T(8,128)(2,1)S(1)} %get-tuple-element.78), channel_id=1, source_target_pairs={{0,1},{1,0},{2,3},{3,2},{4,5},{5,4},{6,7},{7,6},{8,9},{9,8},{10,11... | collective-permute-start | bytes 1572872 | tf_op jit(solution)/shard_map/ppermute | solution.py:303
  60.6 6.4 %collective-permute-start.15 = (bf16[64,1024]{1,0:T(8,128)(2,1)S(1)}, bf16[64,1024]{1,0:T(8,128)(2,1)S(1)}, u32[]{:S(2)}, u32[]{:S(2)}) collective-permute-start(bf16[64,1024]{1,0:T(8,128)(2,1)S(1)} %get-tuple-element.84), channel_id=1, source_target_pairs={{0,8},{1,9},{2,10},{3,11},{4,12},{5,13},{6,14},{7,15},{8,0},{9,1},... | collective-permute-start | bytes 393224 | tf_op jit(solution)/shard_map/ppermute | solution.py:303
  61.5 8.0 %collective-permute-start.13 = (bf16[64,1024]{1,0:T(8,128)(2,1)S(1)}, bf16[64,1024]{1,0:T(8,128)(2,1)S(1)}, u32[]{:S(2)}, u32[]{:S(2)}) collective-permute-start(bf16[64,1024]{1,0:T(8,128)(2,1)S(1)} %get-tuple-element.81), channel_id=1, source_target_pairs={{0,8},{1,9},{2,10},{3,11},{4,12},{5,13},{6,14},{7,15},{8,0},{9,1},... | collective-permute-start | bytes 393224 | tf_op jit(solution)/shard_map/ppermute | solution.py:303
  62.9 18.9 %collective-permute-start.19 = (bf16[512,512]{1,0:T(8,128)(2,1)S(1)}, bf16[512,512]{1,0:T(8,128)(2,1)S(1)}, u32[]{:S(2)}, u32[]{:S(2)}) collective-permute-start(bf16[512,512]{1,0:T(8,128)(2,1)S(1)} %get-tuple-element.79), channel_id=1, source_target_pairs={{0,6},{1,7},{2,4},{3,5},{4,2},{5,3},{6,0},{7,1},{8,14},{9,15},{10,... | collective-permute-start | bytes 1572872 | tf_op jit(solution)/shard_map/ppermute | solution.py:303
  67.0 15.8 %collective-permute-start.16 = (bf16[64,1024]{1,0:T(8,128)(2,1)S(1)}, bf16[64,1024]{1,0:T(8,128)(2,1)S(1)}, u32[]{:S(2)}, u32[]{:S(2)}) collective-permute-start(bf16[64,1024]{1,0:T(8,128)(2,1)S(1)} %line_sum.3), channel_id=1, source_target_pairs={{0,16},{1,17},{2,18},{3,19},{4,20},{5,21},{6,22},{7,23},{8,24},{9,... | collective-permute-start | bytes 393224 | tf_op jit(solution)/shard_map/ppermute | solution.py:303
  71.0 11.8 %collective-permute-start.14 = (bf16[64,1024]{1,0:T(8,128)(2,1)S(1)}, bf16[64,1024]{1,0:T(8,128)(2,1)S(1)}, u32[]{:S(2)}, u32[]{:S(2)}) collective-permute-start(bf16[64,1024]{1,0:T(8,128)(2,1)S(1)} %line_sum.2), channel_id=1, source_target_pairs={{0,16},{1,17},{2,18},{3,19},{4,20},{5,21},{6,22},{7,23},{8,24},{9,... | collective-permute-start | bytes 393224 | tf_op jit(solution)/shard_map/ppermute | solution.py:303
  73.6 10.5 %collective-permute-start.20 = (bf16[128,1024]{1,0:T(8,128)(2,1)S(1)}, bf16[128,1024]{1,0:T(8,128)(2,1)S(1)}, u32[]{:S(2)}, u32[]{:S(2)}) collective-permute-start(bf16[128,1024]{1,0:T(8,128)(2,1)S(1)} %get-tuple-element.91), channel_id=1, source_target_pairs={{0,8},{1,9},{2,10},{3,11},{4,12},{5,13},{6,14},{7,15},{8,0},{9,1},... | collective-permute-start | bytes 786440 | tf_op jit(solution)/shard_map/ppermute | solution.py:303

commit v16 on v15

--- a/solution.py
+++ b/solution.py
@@ -17,6 +17,7 @@
 GRADIENT_COST = 10**10
 DIAGONAL_COST = 10**6
 EXTRA = 48
+PAIR_COST = 10**10
 PARTS = 2
 BIAS_ROWS = 8
 MORE = 16
@@ -419,11 +420,11 @@
         in_specs=vmem(2),
         out_specs=vmem(2),
         compiler_params=params,
-        cost_estimate=cost(rows, rows),
+        cost_estimate=cost(PAIR_COST, rows),
         name="pair_sum",
     )(mine, received)
     mixed_x, mixed_y = to_x(sums[0]), to_y(sums[1])
-    grad_terms, mixed_own = barrier((grad_terms, sums[0]))
+    grad_terms, _ = barrier((grad_terms, sums[0]))
 
     mine_diag, other_diag, grad_own, grad_one, *grad_far = pl.pallas_call(
         functools.partial(diagonal_kernel, owned),

time: 85.1 us -> 82.9 us (0.974)
  waiting for transfers between devices: 40.4 us -> 38.6 us
    ppermute x21, waiting for transfers between devices: 40.4 us -> 38.6 us  [permute(): return lax.ppermute(value, AXES, pairs)]
  transfers between devices with their start and end apart: 21 -> 21, of which waited for: 9 -> 10; matrix products, arithmetic and copies ran while one was open for 1% -> 1% of each run, Pallas kernels for 19% -> 19%
where the time goes in v16:
time: 82.9 us; the launch traced here: 82.7 us
  waiting for transfers between devices  38.6 us (47%)
  starting transfers between devices  23.8 us (29%)
  Pallas kernels  16 us (19%)
  other arithmetic  3.36 us (4%)
    ppermute x21, waiting for transfers between devices, permute(): return lax.ppermute(value, AXES, pairs)  38.6 us
    ppermute x21, starting transfers between devices, permute(): return lax.ppermute(value, AXES, pairs)  23.8 us
    pallas_call x1, Pallas kernels, on_device_lines(): pl.pallas_call(functools.partial(early_kernel, owned), out_shape=(bf16(ea...  7.43 us
    pallas_call x1, Pallas kernels, on_device_lines(): pl.pallas_call(functools.partial(diagonal_kernel, owned), out_shape=[bf16...  3.45 us
    pallas_call x1, Pallas kernels, on_device_lines(): pl.pallas_call(functools.partial(output_kernel, owned), out_shape=(bf16(e...  2.57 us
    pallas_call x1, Pallas kernels, on_device_lines(): pl.pallas_call(gradient_kernel, out_shape=f32(2 * owned, width), in_specs...  1.82 us
  transfers between devices with their start and end apart: 21, of which 10 were waited for; matrix products, arithmetic and copies ran while one was open for 1% of the time, Pallas kernels for 19%

profile of v16, /device:TPU:0, one launch (start us, length us, event | category | flops | bytes accessed | tf_op | source)
XLA Modules:
  0.0 82.7 jit_solution(15770688744066865993)
XLA Ops:
  0.7 1.4 %pad_maximum_fusion.1.refs_0_ = bf16[2,512,512]{2,1,0:T(8,128)(2,1)S(1)} fusion(bf16[1,512,512]{2,1,0:T(8,128)(2,1)} %bitcast.7, bf16[1,512,512]{2,1,0:T(8,128)(2,1)} %bitcast.8), kind=kLoop, calls=%fused_computation.3 | loop fusion | flops 524288 | bytes 2097152 | tf_op jit(solution)/shard_map/stack | solution.py:346
  2.0 3.0 %collective-permute-start = (bf16[2,512,512]{2,1,0:T(8,128)(2,1)S(1)}, bf16[2,512,512]{2,1,0:T(8,128)(2,1)S(1)}, u32[]{:S(2)}, u32[]{:S(2)}) collective-permute-start(bf16[2,512,512]{2,1,0:T(8,128)(2,1)S(1)} %pad_maximum_fusion.1.refs_0_), channel_id=1, source_target_pairs={{0,2},{1,3},{2,0},{3,1},{4,6},{5,7},{6,4},{7,5},{8,10},{9,11},{10,... | collective-permute-start | bytes 3145736 | tf_op jit(solution)/shard_map/ppermute | solution.py:304
  5.0 1.5 %collective-permute-start.1 = (bf16[2,512,512]{2,1,0:T(8,128)(2,1)S(1)}, bf16[2,512,512]{2,1,0:T(8,128)(2,1)S(1)}, u32[]{:S(2)}, u32[]{:S(2)}) collective-permute-start(bf16[2,512,512]{2,1,0:T(8,128)(2,1)S(1)} %pad_maximum_fusion.1.refs_0_), channel_id=1, source_target_pairs={{0,4},{1,5},{2,6},{3,7},{4,0},{5,1},{6,2},{7,3},{8,12},{9,13},{10,... | collective-permute-start | bytes 3145736 | tf_op jit(solution)/shard_map/ppermute | solution.py:304
  6.6 2.7 %collective-permute-start.6 = (bf16[264,1024]{1,0:T(8,128)(2,1)S(1)}, bf16[264,1024]{1,0:T(8,128)(2,1)S(1)}, u32[]{:S(2)}, u32[]{:S(2)}) collective-permute-start(bf16[264,1024]{1,0:T(8,128)(2,1)S(1)} %fusion.1.refs_6_), channel_id=1, source_target_pairs={{0,16},{1,17},{2,18},{3,19},{4,20},{5,21},{6,22},{7,23},{8,24},{9,... | collective-permute-start | bytes 1622024 | tf_op jit(solution)/shard_map/ppermute | solution.py:304
  9.3 1.6 %collective-permute-start.5 = (bf16[264,1024]{1,0:T(8,128)(2,1)S(1)}, bf16[264,1024]{1,0:T(8,128)(2,1)S(1)}, u32[]{:S(2)}, u32[]{:S(2)}) collective-permute-start(bf16[264,1024]{1,0:T(8,128)(2,1)S(1)} %fusion.1.refs_6_), channel_id=1, source_target_pairs={{0,8},{1,9},{2,10},{3,11},{4,12},{5,13},{6,14},{7,15},{8,0},{9,1},... | collective-permute-start | bytes 1622024 | tf_op jit(solution)/shard_map/ppermute | solution.py:304
  10.8 17.3 %collective-permute-done.refs_2_ = bf16[2,512,512]{2,1,0:T(8,128)(2,1)S(1)} collective-permute-done((bf16[2,512,512]{2,1,0:T(8,128)(2,1)S(1)}, bf16[2,512,512]{2,1,0:T(8,128)(2,1)S(1)}, u32[]{:S(2)}, u32[]{:S(2)}) %collective-permute-start) | collective-permute-done | bytes 1048608 | tf_op jit(solution)/shard_map/ppermute | solution.py:304
  28.2 1.5 %collective-permute-done.1.refs_4_ = bf16[2,512,512]{2,1,0:T(8,128)(2,1)S(1)} collective-permute-done((bf16[2,512,512]{2,1,0:T(8,128)(2,1)S(1)}, bf16[2,512,512]{2,1,0:T(8,128)(2,1)S(1)}, u32[]{:S(2)}, u32[]{:S(2)}) %collective-permute-start.1) | collective-permute-done | bytes 1048608 | tf_op jit(solution)/shard_map/ppermute | solution.py:304
  29.6 0.5 collective-permute-start.4
  30.2 3.8 %collective-permute-done.6.refs_8_ = bf16[264,1024]{1,0:T(8,128)(2,1)S(1)} collective-permute-done((bf16[264,1024]{1,0:T(8,128)(2,1)S(1)}, bf16[264,1024]{1,0:T(8,128)(2,1)S(1)}, u32[]{:S(2)}, u32[]{:S(2)}) %collective-permute-start.6) | collective-permute-done | bytes 540704 | tf_op jit(solution)/shard_map/ppermute | solution.py:304
  33.9 0.6 collective-permute-start.7
  34.6 0.6 collective-permute-start.8
  35.2 0.6 collective-permute-start.9
  35.8 7.4 %early.1 = (bf16[1536,128]{1,0:T(8,128)(2,1)S(1)}, bf16[1536,128]{1,0:T(8,128)(2,1)S(1)}, f32[1536,1024]{1,0:T(8,128)S(1)}, f32[256,1024]{1,0:T(8,128)S(1)}, bf1...) custom-call(bf16[2,512,512]{2,1,0:T(8,128)(2,1)S(1)} %pad_maximum_fu, ...), custom_call_target="tpu_custom_call" | custom-call | flops 786432 | bytes 1536 | tf_op jit(solution)/shard_map/early/pallas_call | solution.py:356
  43.2 4.5 %collective-permute-done.7.refs_6_.w_three = bf16[264,1024]{1,0:T(8,128)(2,1)S(1)} collective-permute-done((bf16[264,1024]{1,0:T(8,128)(2,1)S(1)}, bf16[264,1024]{1,0:T(8,128)(2,1)S(1)}, u32[]{:S(2)}, u32[]{:S(2)}) %collective-permute-start.7) | collective-permute-done | bytes 540704 | tf_op jit(solution)/shard_map/ppermute | solution.py:304
  47.8 2.6 %output.1 = (bf16[1536,512]{1,0:T(8,128)(2,1)S(1)}, bf16[1024,512]{1,0:T(8,128)(2,1)S(1)}, bf16[512,512]{1,0:T(8,128)(2,1)S(1)}, f32[1536,128]{1,0:T(8,128)S(1)}...) custom-call(bf16[1536,128]{1,0:T(8,128)(2,1)S(1)} %get-tuple-element.51.refs_0_, ...), custom_call_target="tpu_custom_call" | custom-call | flops 786432 | bytes 1536 | tf_op jit(solution)/shard_map/output/pallas_call | solution.py:383
  50.6 0.6 collective-permute-start.11
  51.2 1.8 %gradient.1.refs_4_ = f32[256,1024]{1,0:T(8,128)S(1)} custom-call(bf16[1536,128]{1,0:T(8,128)(2,1)S(1)} %get-tuple-element.62.dpre_two, bf16[1536,1024]{1,0:T(8,128)(2,1)S(1)} %get-tuple-element.52.refs_1_.tok, bf16[1536,1024]{1,0:T(8,128)(2,1)S(1)} %get-tuple-element.63.cot, f32[1536,128]{1,0:T(8,128)S(1)} %get-tuple-element.67.slope, ...), custom_call_target="tpu_custom_call" | custom-call | flops 10000000000 | bytes 1536 | tf_op jit(solution)/shard_map/gradient/pallas_call | solution.py:405
  53.4 0.6 collective-permute-start.17
  54.0 0.7 collective-permute-start.18
  54.7 0.7 collective-permute-done.11.refs_7_.far_ref
  55.4 3.5 %diagonal.1 = (bf16[512,512]{1,0:T(8,128)(2,1)S(1)}, bf16[512,512]{1,0:T(8,128)(2,1)S(1)}, bf16[128,1024]{1,0:T(8,128)(2,1)S(1)}, bf16[128,1024]{1,0:T(8,128)(2,...) custom-call(bf16[512,1024]{1,0:T(8,128)(2,1)S(1)} %get-tuple-element, ...), custom_call_target="tpu_custom_call" | custom-call | flops 1000000 | bytes 512 | tf_op jit(solution)/shard_map/diagonal/pallas_call | solution.py:429
  59.1 1.0 %collective-permute-start.15 = (bf16[64,1024]{1,0:T(8,128)(2,1)S(1)}, bf16[64,1024]{1,0:T(8,128)(2,1)S(1)}, u32[]{:S(2)}, u32[]{:S(2)}) collective-permute-start(bf16[64,1024]{1,0:T(8,128)(2,1)S(1)} %get-tuple-element.84), channel_id=1, source_target_pairs={{0,8},{1,9},{2,10},{3,11},{4,12},{5,13},{6,14},{7,15},{8,0},{9,1},... | collective-permute-start | bytes 393224 | tf_op jit(solution)/shard_map/ppermute | solution.py:304
  60.1 1.0 %collective-permute-start.13 = (bf16[64,1024]{1,0:T(8,128)(2,1)S(1)}, bf16[64,1024]{1,0:T(8,128)(2,1)S(1)}, u32[]{:S(2)}, u32[]{:S(2)}) collective-permute-start(bf16[64,1024]{1,0:T(8,128)(2,1)S(1)} %get-tuple-element.81), channel_id=1, source_target_pairs={{0,8},{1,9},{2,10},{3,11},{4,12},{5,13},{6,14},{7,15},{8,0},{9,1},... | collective-permute-start | bytes 393224 | tf_op jit(solution)/shard_map/ppermute | solution.py:304
  61.4 1.6 %collective-permute-start.19 = (bf16[512,512]{1,0:T(8,128)(2,1)S(1)}, bf16[512,512]{1,0:T(8,128)(2,1)S(1)}, u32[]{:S(2)}, u32[]{:S(2)}) collective-permute-start(bf16[512,512]{1,0:T(8,128)(2,1)S(1)} %get-tuple-element.79), channel_id=1, source_target_pairs={{0,6},{1,7},{2,4},{3,5},{4,2},{5,3},{6,0},{7,1},{8,14},{9,15},{10,... | collective-permute-start | bytes 1572872 | tf_op jit(solution)/shard_map/ppermute | solution.py:304
  62.9 2.4 %collective-permute-done.15.other_ref = bf16[64,1024]{1,0:T(8,128)(2,1)S(1)} collective-permute-done((bf16[64,1024]{1,0:T(8,128)(2,1)S(1)}, bf16[64,1024]{1,0:T(8,128)(2,1)S(1)}, u32[]{:S(2)}, u32[]{:S(2)}) %collective-permute-start.15) | collective-permute-done | bytes 131104 | tf_op jit(solution)/shard_map/ppermute | solution.py:304
  65.4 2.7 %collective-permute-start.16 = (bf16[64,1024]{1,0:T(8,128)(2,1)S(1)}, bf16[64,1024]{1,0:T(8,128)(2,1)S(1)}, u32[]{:S(2)}, u32[]{:S(2)}) collective-permute-start(bf16[64,1024]{1,0:T(8,128)(2,1)S(1)} %line_sum.3), channel_id=1, source_target_pairs={{0,16},{1,17},{2,18},{3,19},{4,20},{5,21},{6,22},{7,23},{8,24},{9,... | collective-permute-start | bytes 393224 | tf_op jit(solution)/shard_map/ppermute | solution.py:304
  68.6 2.6 %collective-permute-start.14 = (bf16[64,1024]{1,0:T(8,128)(2,1)S(1)}, bf16[64,1024]{1,0:T(8,128)(2,1)S(1)}, u32[]{:S(2)}, u32[]{:S(2)}) collective-permute-start(bf16[64,1024]{1,0:T(8,128)(2,1)S(1)} %line_sum.2), channel_id=1, source_target_pairs={{0,16},{1,17},{2,18},{3,19},{4,20},{5,21},{6,22},{7,23},{8,24},{9,... | collective-permute-start | bytes 393224 | tf_op jit(solution)/shard_map/ppermute | solution.py:304
  71.2 1.7 %collective-permute-start.20 = (bf16[128,1024]{1,0:T(8,128)(2,1)S(1)}, bf16[128,1024]{1,0:T(8,128)(2,1)S(1)}, u32[]{:S(2)}, u32[]{:S(2)}) collective-permute-start(bf16[128,1024]{1,0:T(8,128)(2,1)S(1)} %get-tuple-element.91), channel_id=1, source_target_pairs={{0,8},{1,9},{2,10},{3,11},{4,12},{5,13},{6,14},{7,15},{8,0},{9,1},... | collective-permute-start | bytes 786440 | tf_op jit(solution)/shard_map/ppermute | solution.py:304
  73.0 6.3 %collective-permute-done.18.y_ref = bf16[528,512]{1,0:T(8,128)(2,1)S(1)} collective-permute-done((bf16[528,512]{1,0:T(8,128)(2,1)S(1)}, bf16[528,512]{1,0:T(8,128)(2,1)S(1)}, u32[]{:S(2)}, u32[]{:S(2)}) %collective-permute-start.18) | collective-permute-done | bytes 540704 | tf_op jit(solution)/shard_map/ppermute | solution.py:304
  79.5 1.0 %add_convert_fusion = bf16[512,512]{1,0:T(8,128)(2,1)} fusion(f32[512,512]{1,0:T(8,128)S(1)} %plane_sum.1, bf16[512,512]{1,0:T(8,128)(2,1)S(1)} %collective-permute-done.19), kind=kLoop, calls=%fused_computation.4 | loop fusion | flops 786432 | bytes 2097152 | tf_op jit(solution)/shard_map/convert_element_type | solution.py:486
  80.4 1.4 %collective-permute-done.20 = bf16[128,1024]{1,0:T(8,128)(2,1)S(1)} collective-permute-done((bf16[128,1024]{1,0:T(8,128)(2,1)S(1)}, bf16[128,1024]{1,0:T(8,128)(2,1)S(1)}, u32[]{:S(2)}, u32[]{:S(2)}) %collective-permute-start.20) | collective-permute-done | bytes 262176 | tf_op jit(solution)/shard_map/ppermute | solution.py:304
  81.8 0.9 %add_multiply_fusion = f32[128,1024]{1,0:T(8,128)} fusion(bf16[128,1024]{1,0:T(8,128)(2,1)S(1)} %collective-permute-done.20, bf16[128,1024]{1,0:T(8,128)(2,1)S(1)} %get-tuple-element.90, bf16[64,1024]{1,0:T(8,128)(2,1)S(1)} %collective-permute-done.16, bf16[64,1024]{1,0:T(8,128)(2,1)S(1)} %collective-permute-done.14), kind=kLoop, calls=%fused_computation.6 | loop fusion | flops 1179648 | bytes 1310720 | tf_op jit(solution)/shard_map/mul | solution.py:494
  (33 shorter events, 1.9 us)
Async XLA Ops:
  0.6 5.9 %copy-start.2 = (bf16[128]{0:T(256)(128)(2,1)S(1)}, bf16[128]{0:T(256)(128)(2,1)}, u32[]{:S(2)}) copy-start(bf16[128]{0:T(256)(128)(2,1)} %param.8) | copy-start | bytes 772
  0.6 5.9 %copy-start.1 = (bf16[128,1024]{1,0:T(8,128)(2,1)S(1)}, bf16[128,1024]{1,0:T(8,128)(2,1)}, u32[]{:S(2)}) copy-start(bf16[128,1024]{1,0:T(8,128)(2,1)} %param.7) | copy-start | bytes 786436
  0.7 5.9 %copy-start = (bf16[128,1024]{1,0:T(8,128)(2,1)S(1)}, bf16[128,1024]{1,0:T(8,128)(2,1)}, u32[]{:S(2)}) copy-start(bf16[128,1024]{1,0:T(8,128)(2,1)} %param.9) | copy-start | bytes 786436
  2.0 26.2 %collective-permute-start = (bf16[2,512,512]{2,1,0:T(8,128)(2,1)S(1)}, bf16[2,512,512]{2,1,0:T(8,128)(2,1)S(1)}, u32[]{:S(2)}, u32[]{:S(2)}) collective-permute-start(bf16[2,512,512]{2,1,0:T(8,128)(2,1)S(1)} %pad_maximum_fusion.1.refs_0_), channel_id=1, source_target_pairs={{0,2},{1,3},{2,0},{3,1},{4,6},{5,7},{6,4},{7,5},{8,10},{9,11},{10,... | collective-permute-start | bytes 3145736 | tf_op jit(solution)/shard_map/ppermute | solution.py:304
  5.0 24.6 %collective-permute-start.1 = (bf16[2,512,512]{2,1,0:T(8,128)(2,1)S(1)}, bf16[2,512,512]{2,1,0:T(8,128)(2,1)S(1)}, u32[]{:S(2)}, u32[]{:S(2)}) collective-permute-start(bf16[2,512,512]{2,1,0:T(8,128)(2,1)S(1)} %pad_maximum_fusion.1.refs_0_), channel_id=1, source_target_pairs={{0,4},{1,5},{2,6},{3,7},{4,0},{5,1},{6,2},{7,3},{8,12},{9,13},{10,... | collective-permute-start | bytes 3145736 | tf_op jit(solution)/shard_map/ppermute | solution.py:304
  6.5 23.1 %collective-permute-start.2 = (bf16[2,512,512]{2,1,0:T(8,128)(2,1)S(1)}, bf16[2,512,512]{2,1,0:T(8,128)(2,1)S(1)}, u32[]{:S(2)}, u32[]{:S(2)}) collective-permute-start(bf16[2,512,512]{2,1,0:T(8,128)(2,1)S(1)} %pad_maximum_fusion.1.refs_0_), channel_id=1, source_target_pairs={{0,1},{1,0},{2,3},{3,2},{4,5},{5,4},{6,7},{7,6},{8,9},{9,8},{10,11... | collective-permute-start | bytes 3145736 | tf_op jit(solution)/shard_map/ppermute | solution.py:304
  6.6 27.3 %collective-permute-start.6 = (bf16[264,1024]{1,0:T(8,128)(2,1)S(1)}, bf16[264,1024]{1,0:T(8,128)(2,1)S(1)}, u32[]{:S(2)}, u32[]{:S(2)}) collective-permute-start(bf16[264,1024]{1,0:T(8,128)(2,1)S(1)} %fusion.1.refs_6_), channel_id=1, source_target_pairs={{0,16},{1,17},{2,18},{3,19},{4,20},{5,21},{6,22},{7,23},{8,24},{9,... | collective-permute-start | bytes 1622024 | tf_op jit(solution)/shard_map/ppermute | solution.py:304
  9.3 25.9 %collective-permute-start.5 = (bf16[264,1024]{1,0:T(8,128)(2,1)S(1)}, bf16[264,1024]{1,0:T(8,128)(2,1)S(1)}, u32[]{:S(2)}, u32[]{:S(2)}) collective-permute-start(bf16[264,1024]{1,0:T(8,128)(2,1)S(1)} %fusion.1.refs_6_), channel_id=1, source_target_pairs={{0,8},{1,9},{2,10},{3,11},{4,12},{5,13},{6,14},{7,15},{8,0},{9,1},... | collective-permute-start | bytes 1622024 | tf_op jit(solution)/shard_map/ppermute | solution.py:304
  29.6 6.1 %collective-permute-start.3 = (bf16[2,512,512]{2,1,0:T(8,128)(2,1)S(1)}, bf16[2,512,512]{2,1,0:T(8,128)(2,1)S(1)}, u32[]{:S(2)}, u32[]{:S(2)}) collective-permute-start(bf16[2,512,512]{2,1,0:T(8,128)(2,1)S(1)} %collective-permute-done.refs_2_), channel_id=1, source_target_pairs={{0,1},{1,0},{2,3},{3,2},{4,5},{5,4},{6,7},{7,6},{8,9},{9,8},{10,11... | collective-permute-start | bytes 3145736 | tf_op jit(solution)/shard_map/ppermute | solution.py:304
  29.6 6.1 %collective-permute-start.4 = (bf16[2,512,512]{2,1,0:T(8,128)(2,1)S(1)}, bf16[2,512,512]{2,1,0:T(8,128)(2,1)S(1)}, u32[]{:S(2)}, u32[]{:S(2)}) collective-permute-start(bf16[2,512,512]{2,1,0:T(8,128)(2,1)S(1)} %collective-permute-done.1.refs_4_), channel_id=1, source_target_pairs={{0,1},{1,0},{2,3},{3,2},{4,5},{5,4},{6,7},{7,6},{8,9},{9,8},{10,11... | collective-permute-start | bytes 3145736 | tf_op jit(solution)/shard_map/ppermute | solution.py:304
  33.9 13.8 %collective-permute-start.7 = (bf16[264,1024]{1,0:T(8,128)(2,1)S(1)}, bf16[264,1024]{1,0:T(8,128)(2,1)S(1)}, u32[]{:S(2)}, u32[]{:S(2)}) collective-permute-start(bf16[264,1024]{1,0:T(8,128)(2,1)S(1)} %collective-permute-done.6.refs_8_), channel_id=1, source_target_pairs={{0,8},{1,9},{2,10},{3,11},{4,12},{5,13},{6,14},{7,15},{8,0},{9,1},... | collective-permute-start | bytes 1622024 | tf_op jit(solution)/shard_map/ppermute | solution.py:304
  34.6 15.8 %collective-permute-start.8 = (bf16[560,512]{1,0:T(8,128)(2,1)S(1)}, bf16[560,512]{1,0:T(8,128)(2,1)S(1)}, u32[]{:S(2)}, u32[]{:S(2)}) collective-permute-start(bf16[560,512]{1,0:T(8,128)(2,1)S(1)} %slice.12), channel_id=1, source_target_pairs={{0,4},{1,5},{2,6},{3,7},{4,0},{5,1},{6,2},{7,3},{8,12},{9,13},{10,... | collective-permute-start | bytes 1720328 | tf_op jit(solution)/shard_map/ppermute | solution.py:304
  35.2 15.2 %collective-permute-start.9 = (bf16[512,512]{1,0:T(8,128)(2,1)S(1)}, bf16[512,512]{1,0:T(8,128)(2,1)S(1)}, u32[]{:S(2)}, u32[]{:S(2)}) collective-permute-start(bf16[512,512]{1,0:T(8,128)(2,1)S(1)} %slice_bitcast_fusion), channel_id=1, source_target_pairs={{0,2},{1,3},{2,0},{3,1},{4,6},{5,7},{6,4},{7,5},{8,10},{9,11},{10,... | collective-permute-start | bytes 1572872 | tf_op jit(solution)/shard_map/ppermute | solution.py:304
  50.4 2.7 %collective-permute-start.10 = (bf16[1024,512]{1,0:T(8,128)(2,1)S(1)}, bf16[1024,512]{1,0:T(8,128)(2,1)S(1)}, u32[]{:S(2)}, u32[]{:S(2)}) collective-permute-start(bf16[1024,512]{1,0:T(8,128)(2,1)S(1)} %get-tuple-element.69), channel_id=1, source_target_pairs={{0,1},{1,0},{2,3},{3,2},{4,5},{5,4},{6,7},{7,6},{8,9},{9,8},{10,11... | collective-permute-start | bytes 3145736 | tf_op jit(solution)/shard_map/ppermute | solution.py:304
  50.6 4.8 %collective-permute-start.11 = (bf16[1536,512]{1,0:T(8,128)(2,1)S(1)}, bf16[1536,512]{1,0:T(8,128)(2,1)S(1)}, u32[]{:S(2)}, u32[]{:S(2)}) collective-permute-start(bf16[1536,512]{1,0:T(8,128)(2,1)S(1)} %pad_maximum_fusion), channel_id=1, source_target_pairs={{0,1},{1,0},{2,3},{3,2},{4,5},{5,4},{6,7},{7,6},{8,9},{9,8},{10,11... | collective-permute-start | bytes 4718600 | tf_op jit(solution)/shard_map/ppermute | solution.py:304
  53.4 15.2 %collective-permute-start.17 = (bf16[528,512]{1,0:T(8,128)(2,1)S(1)}, bf16[528,512]{1,0:T(8,128)(2,1)S(1)}, u32[]{:S(2)}, u32[]{:S(2)}) collective-permute-start(bf16[528,512]{1,0:T(8,128)(2,1)S(1)} %get-tuple-element.70), channel_id=1, source_target_pairs={{0,2},{1,3},{2,0},{3,1},{4,6},{5,7},{6,4},{7,5},{8,10},{9,11},{10,... | collective-permute-start | bytes 1622024 | tf_op jit(solution)/shard_map/ppermute | solution.py:304
  54.0 25.3 %collective-permute-start.18 = (bf16[528,512]{1,0:T(8,128)(2,1)S(1)}, bf16[528,512]{1,0:T(8,128)(2,1)S(1)}, u32[]{:S(2)}, u32[]{:S(2)}) collective-permute-start(bf16[528,512]{1,0:T(8,128)(2,1)S(1)} %get-tuple-element.88), channel_id=1, source_target_pairs={{0,4},{1,5},{2,6},{3,7},{4,0},{5,1},{6,2},{7,3},{8,12},{9,13},{10,... | collective-permute-start | bytes 1622024 | tf_op jit(solution)/shard_map/ppermute | solution.py:304
  58.9 2.2 %collective-permute-start.12 = (bf16[512,512]{1,0:T(8,128)(2,1)S(1)}, bf16[512,512]{1,0:T(8,128)(2,1)S(1)}, u32[]{:S(2)}, u32[]{:S(2)}) collective-permute-start(bf16[512,512]{1,0:T(8,128)(2,1)S(1)} %get-tuple-element.78), channel_id=1, source_target_pairs={{0,1},{1,0},{2,3},{3,2},{4,5},{5,4},{6,7},{7,6},{8,9},{9,8},{10,11... | collective-permute-start | bytes 1572872 | tf_op jit(solution)/shard_map/ppermute | solution.py:304
  59.1 6.3 %collective-permute-start.15 = (bf16[64,1024]{1,0:T(8,128)(2,1)S(1)}, bf16[64,1024]{1,0:T(8,128)(2,1)S(1)}, u32[]{:S(2)}, u32[]{:S(2)}) collective-permute-start(bf16[64,1024]{1,0:T(8,128)(2,1)S(1)} %get-tuple-element.84), channel_id=1, source_target_pairs={{0,8},{1,9},{2,10},{3,11},{4,12},{5,13},{6,14},{7,15},{8,0},{9,1},... | collective-permute-start | bytes 393224 | tf_op jit(solution)/shard_map/ppermute | solution.py:304
  60.1 8.1 %collective-permute-start.13 = (bf16[64,1024]{1,0:T(8,128)(2,1)S(1)}, bf16[64,1024]{1,0:T(8,128)(2,1)S(1)}, u32[]{:S(2)}, u32[]{:S(2)}) collective-permute-start(bf16[64,1024]{1,0:T(8,128)(2,1)S(1)} %get-tuple-element.81), channel_id=1, source_target_pairs={{0,8},{1,9},{2,10},{3,11},{4,12},{5,13},{6,14},{7,15},{8,0},{9,1},... | collective-permute-start | bytes 393224 | tf_op jit(solution)/shard_map/ppermute | solution.py:304
  61.4 18.1 %collective-permute-start.19 = (bf16[512,512]{1,0:T(8,128)(2,1)S(1)}, bf16[512,512]{1,0:T(8,128)(2,1)S(1)}, u32[]{:S(2)}, u32[]{:S(2)}) collective-permute-start(bf16[512,512]{1,0:T(8,128)(2,1)S(1)} %get-tuple-element.79), channel_id=1, source_target_pairs={{0,6},{1,7},{2,4},{3,5},{4,2},{5,3},{6,0},{7,1},{8,14},{9,15},{10,... | collective-permute-start | bytes 1572872 | tf_op jit(solution)/shard_map/ppermute | solution.py:304
  65.4 15.0 %collective-permute-start.16 = (bf16[64,1024]{1,0:T(8,128)(2,1)S(1)}, bf16[64,1024]{1,0:T(8,128)(2,1)S(1)}, u32[]{:S(2)}, u32[]{:S(2)}) collective-permute-start(bf16[64,1024]{1,0:T(8,128)(2,1)S(1)} %line_sum.3), channel_id=1, source_target_pairs={{0,16},{1,17},{2,18},{3,19},{4,20},{5,21},{6,22},{7,23},{8,24},{9,... | collective-permute-start | bytes 393224 | tf_op jit(solution)/shard_map/ppermute | solution.py:304
  68.6 11.8 %collective-permute-start.14 = (bf16[64,1024]{1,0:T(8,128)(2,1)S(1)}, bf16[64,1024]{1,0:T(8,128)(2,1)S(1)}, u32[]{:S(2)}, u32[]{:S(2)}) collective-permute-start(bf16[64,1024]{1,0:T(8,128)(2,1)S(1)} %line_sum.2), channel_id=1, source_target_pairs={{0,16},{1,17},{2,18},{3,19},{4,20},{5,21},{6,22},{7,23},{8,24},{9,... | collective-permute-start | bytes 393224 | tf_op jit(solution)/shard_map/ppermute | solution.py:304
  71.2 10.6 %collective-permute-start.20 = (bf16[128,1024]{1,0:T(8,128)(2,1)S(1)}, bf16[128,1024]{1,0:T(8,128)(2,1)S(1)}, u32[]{:S(2)}, u32[]{:S(2)}) collective-permute-start(bf16[128,1024]{1,0:T(8,128)(2,1)S(1)} %get-tuple-element.91), channel_id=1, source_target_pairs={{0,8},{1,9},{2,10},{3,11},{4,12},{5,13},{6,14},{7,15},{8,0},{9,1},... | collective-permute-start | bytes 786440 | tf_op jit(solution)/shard_map/ppermute | solution.py:304

commit v17 on v16

--- a/solution.py
+++ b/solution.py
@@ -225,14 +225,12 @@
     load = side_by_side(core, (tok_ref.at[first], far_ref.at[first]), tok, 0, tok_sem)
     cot_load = side_by_side(core, (cot_ref, far_ref.at[second]), cot, 0, cot_sem)
     run(load + cot_load, "start")
-    run(load, "wait")
+    run(load + cot_load, "wait")
     step = rows // 2
     for sub in range(2):
         spot = slice(sub * step, (sub + 1) * step)
         value, slope = activate(tok[spot, :], w_in[...], bias[0:1, :])
         act = value.astype(jnp.bfloat16)
-        if sub == 0:
-            run(cot_load, "wait")
         dact = dot_last(cot[spot, :], w_out[...])
         dpre[spot, :] = (dact * slope).astype(jnp.bfloat16)
         for shift, ref in enumerate((mine_ref, other_ref)):
@@ -472,7 +470,7 @@
             name="line_sum",
         )(piece, relayed[at])
         from_two.append(to_far(line_sum, 2))
-    grad_one, mixed_x, _ = barrier((grad_one, mixed_x, line_sum))
+    grad_one, _ = barrier((grad_one, line_sum))
     from_one = to_far(grad_one, 1)
     mixed = pl.pallas_call(
         plane_kernel,

time: 82.9 us -> 81.5 us (0.983)
  transfers between devices with their start and end apart: 21 -> 21, of which waited for: 10 -> 8; matrix products, arithmetic and copies ran while one was open for 1% -> 1% of each run, Pallas kernels for 19% -> 19%
where the time goes in v17:
time: 81.5 us; the launch traced here: 81.4 us
  waiting for transfers between devices  38 us (47%)
  starting transfers between devices  23.4 us (29%)
  Pallas kernels  15.7 us (19%)
  other arithmetic  3.36 us (4%)
    ppermute x21, waiting for transfers between devices, permute(): return lax.ppermute(value, AXES, pairs)  38 us
    ppermute x21, starting transfers between devices, permute(): return lax.ppermute(value, AXES, pairs)  23.4 us
    pallas_call x1, Pallas kernels, on_device_lines(): pl.pallas_call(functools.partial(early_kernel, owned), out_shape=(bf16(ea...  7.43 us
    pallas_call x1, Pallas kernels, on_device_lines(): pl.pallas_call(functools.partial(diagonal_kernel, owned), out_shape=[bf16...  3.13 us
    pallas_call x1, Pallas kernels, on_device_lines(): pl.pallas_call(functools.partial(output_kernel, owned), out_shape=(bf16(e...  2.57 us
    pallas_call x1, Pallas kernels, on_device_lines(): pl.pallas_call(gradient_kernel, out_shape=f32(2 * owned, width), in_specs...  1.82 us
  transfers between devices with their start and end apart: 21, of which 8 were waited for; matrix products, arithmetic and copies ran while one was open for 1% of the time, Pallas kernels for 19%

profile of v17, /device:TPU:0, one launch (start us, length us, event | category | flops | bytes accessed | tf_op | source)
XLA Modules:
  0.0 81.4 jit_solution(1308656568250650918)
XLA Ops:
  0.7 1.4 %pad_maximum_fusion.1.refs_0_ = bf16[2,512,512]{2,1,0:T(8,128)(2,1)S(1)} fusion(bf16[1,512,512]{2,1,0:T(8,128)(2,1)} %bitcast.7, bf16[1,512,512]{2,1,0:T(8,128)(2,1)} %bitcast.8), kind=kLoop, calls=%fused_computation.3 | loop fusion | flops 524288 | bytes 2097152 | tf_op jit(solution)/shard_map/stack | solution.py:344
  2.0 3.0 %collective-permute-start = (bf16[2,512,512]{2,1,0:T(8,128)(2,1)S(1)}, bf16[2,512,512]{2,1,0:T(8,128)(2,1)S(1)}, u32[]{:S(2)}, u32[]{:S(2)}) collective-permute-start(bf16[2,512,512]{2,1,0:T(8,128)(2,1)S(1)} %pad_maximum_fusion.1.refs_0_), channel_id=1, source_target_pairs={{0,2},{1,3},{2,0},{3,1},{4,6},{5,7},{6,4},{7,5},{8,10},{9,11},{10,... | collective-permute-start | bytes 3145736 | tf_op jit(solution)/shard_map/ppermute | solution.py:302
  5.0 1.5 %collective-permute-start.1 = (bf16[2,512,512]{2,1,0:T(8,128)(2,1)S(1)}, bf16[2,512,512]{2,1,0:T(8,128)(2,1)S(1)}, u32[]{:S(2)}, u32[]{:S(2)}) collective-permute-start(bf16[2,512,512]{2,1,0:T(8,128)(2,1)S(1)} %pad_maximum_fusion.1.refs_0_), channel_id=1, source_target_pairs={{0,4},{1,5},{2,6},{3,7},{4,0},{5,1},{6,2},{7,3},{8,12},{9,13},{10,... | collective-permute-start | bytes 3145736 | tf_op jit(solution)/shard_map/ppermute | solution.py:302
  6.6 2.7 %collective-permute-start.6 = (bf16[264,1024]{1,0:T(8,128)(2,1)S(1)}, bf16[264,1024]{1,0:T(8,128)(2,1)S(1)}, u32[]{:S(2)}, u32[]{:S(2)}) collective-permute-start(bf16[264,1024]{1,0:T(8,128)(2,1)S(1)} %fusion.1.refs_6_), channel_id=1, source_target_pairs={{0,16},{1,17},{2,18},{3,19},{4,20},{5,21},{6,22},{7,23},{8,24},{9,... | collective-permute-start | bytes 1622024 | tf_op jit(solution)/shard_map/ppermute | solution.py:302
  9.3 1.6 %collective-permute-start.5 = (bf16[264,1024]{1,0:T(8,128)(2,1)S(1)}, bf16[264,1024]{1,0:T(8,128)(2,1)S(1)}, u32[]{:S(2)}, u32[]{:S(2)}) collective-permute-start(bf16[264,1024]{1,0:T(8,128)(2,1)S(1)} %fusion.1.refs_6_), channel_id=1, source_target_pairs={{0,8},{1,9},{2,10},{3,11},{4,12},{5,13},{6,14},{7,15},{8,0},{9,1},... | collective-permute-start | bytes 1622024 | tf_op jit(solution)/shard_map/ppermute | solution.py:302
  10.8 17.3 %collective-permute-done.refs_2_ = bf16[2,512,512]{2,1,0:T(8,128)(2,1)S(1)} collective-permute-done((bf16[2,512,512]{2,1,0:T(8,128)(2,1)S(1)}, bf16[2,512,512]{2,1,0:T(8,128)(2,1)S(1)}, u32[]{:S(2)}, u32[]{:S(2)}) %collective-permute-start) | collective-permute-done | bytes 1048608 | tf_op jit(solution)/shard_map/ppermute | solution.py:302
  28.2 1.5 %collective-permute-done.1.refs_4_ = bf16[2,512,512]{2,1,0:T(8,128)(2,1)S(1)} collective-permute-done((bf16[2,512,512]{2,1,0:T(8,128)(2,1)S(1)}, bf16[2,512,512]{2,1,0:T(8,128)(2,1)S(1)}, u32[]{:S(2)}, u32[]{:S(2)}) %collective-permute-start.1) | collective-permute-done | bytes 1048608 | tf_op jit(solution)/shard_map/ppermute | solution.py:302
  29.6 0.5 collective-permute-start.4
  30.2 3.8 %collective-permute-done.6.refs_8_ = bf16[264,1024]{1,0:T(8,128)(2,1)S(1)} collective-permute-done((bf16[264,1024]{1,0:T(8,128)(2,1)S(1)}, bf16[264,1024]{1,0:T(8,128)(2,1)S(1)}, u32[]{:S(2)}, u32[]{:S(2)}) %collective-permute-start.6) | collective-permute-done | bytes 540704 | tf_op jit(solution)/shard_map/ppermute | solution.py:302
  33.9 0.6 collective-permute-start.7
  34.6 0.6 collective-permute-start.8
  35.2 0.6 collective-permute-start.9
  35.8 7.4 %early.1 = (bf16[1536,128]{1,0:T(8,128)(2,1)S(1)}, bf16[1536,128]{1,0:T(8,128)(2,1)S(1)}, f32[1536,1024]{1,0:T(8,128)S(1)}, f32[256,1024]{1,0:T(8,128)S(1)}, bf1...) custom-call(bf16[2,512,512]{2,1,0:T(8,128)(2,1)S(1)} %pad_maximum_fu, ...), custom_call_target="tpu_custom_call" | custom-call | flops 786432 | bytes 1536 | tf_op jit(solution)/shard_map/early/pallas_call | solution.py:354
  43.2 4.5 %collective-permute-done.7.refs_6_.w_three = bf16[264,1024]{1,0:T(8,128)(2,1)S(1)} collective-permute-done((bf16[264,1024]{1,0:T(8,128)(2,1)S(1)}, bf16[264,1024]{1,0:T(8,128)(2,1)S(1)}, u32[]{:S(2)}, u32[]{:S(2)}) %collective-permute-start.7) | collective-permute-done | bytes 540704 | tf_op jit(solution)/shard_map/ppermute | solution.py:302
  47.8 2.6 %output.1 = (bf16[1536,512]{1,0:T(8,128)(2,1)S(1)}, bf16[1024,512]{1,0:T(8,128)(2,1)S(1)}, bf16[512,512]{1,0:T(8,128)(2,1)S(1)}, f32[1536,128]{1,0:T(8,128)S(1)}...) custom-call(bf16[1536,128]{1,0:T(8,128)(2,1)S(1)} %get-tuple-element.50.refs_0_, ...), custom_call_target="tpu_custom_call" | custom-call | flops 786432 | bytes 1536 | tf_op jit(solution)/shard_map/output/pallas_call | solution.py:381
  50.6 0.6 collective-permute-start.11
  51.2 1.8 %gradient.1.refs_4_ = f32[256,1024]{1,0:T(8,128)S(1)} custom-call(bf16[1536,128]{1,0:T(8,128)(2,1)S(1)} %get-tuple-element.61.dpre_two, bf16[1536,1024]{1,0:T(8,128)(2,1)S(1)} %get-tuple-element.51.refs_1_.tok, bf16[1536,1024]{1,0:T(8,128)(2,1)S(1)} %get-tuple-element.62.cot, f32[1536,128]{1,0:T(8,128)S(1)} %get-tuple-element.66.slope, ...), custom_call_target="tpu_custom_call" | custom-call | flops 10000000000 | bytes 1536 | tf_op jit(solution)/shard_map/gradient/pallas_call | solution.py:403
  53.1 0.3 pair_sum.1
  53.4 0.6 collective-permute-start.17
  54.0 0.7 collective-permute-start.18
  54.7 0.7 collective-permute-done.11.refs_7_.far_ref
  55.4 3.1 %diagonal.1 = (bf16[512,512]{1,0:T(8,128)(2,1)S(1)}, bf16[512,512]{1,0:T(8,128)(2,1)S(1)}, bf16[128,1024]{1,0:T(8,128)(2,1)S(1)}, bf16[128,1024]{1,0:T(8,128)(2,...) custom-call(bf16[512,1024]{1,0:T(8,128)(2,1)S(1)} %get-tuple-element, ...), custom_call_target="tpu_custom_call" | custom-call | flops 1000000 | bytes 512 | tf_op jit(solution)/shard_map/diagonal/pallas_call | solution.py:427
  58.7 1.0 %collective-permute-start.15 = (bf16[64,1024]{1,0:T(8,128)(2,1)S(1)}, bf16[64,1024]{1,0:T(8,128)(2,1)S(1)}, u32[]{:S(2)}, u32[]{:S(2)}) collective-permute-start(bf16[64,1024]{1,0:T(8,128)(2,1)S(1)} %get-tuple-element.83), channel_id=1, source_target_pairs={{0,8},{1,9},{2,10},{3,11},{4,12},{5,13},{6,14},{7,15},{8,0},{9,1},... | collective-permute-start | bytes 393224 | tf_op jit(solution)/shard_map/ppermute | solution.py:302
  59.7 1.0 %collective-permute-start.13 = (bf16[64,1024]{1,0:T(8,128)(2,1)S(1)}, bf16[64,1024]{1,0:T(8,128)(2,1)S(1)}, u32[]{:S(2)}, u32[]{:S(2)}) collective-permute-start(bf16[64,1024]{1,0:T(8,128)(2,1)S(1)} %get-tuple-element.80), channel_id=1, source_target_pairs={{0,8},{1,9},{2,10},{3,11},{4,12},{5,13},{6,14},{7,15},{8,0},{9,1},... | collective-permute-start | bytes 393224 | tf_op jit(solution)/shard_map/ppermute | solution.py:302
  61.0 1.6 %collective-permute-start.19 = (bf16[512,512]{1,0:T(8,128)(2,1)S(1)}, bf16[512,512]{1,0:T(8,128)(2,1)S(1)}, u32[]{:S(2)}, u32[]{:S(2)}) collective-permute-start(bf16[512,512]{1,0:T(8,128)(2,1)S(1)} %get-tuple-element.78), channel_id=1, source_target_pairs={{0,6},{1,7},{2,4},{3,5},{4,2},{5,3},{6,0},{7,1},{8,14},{9,15},{10,... | collective-permute-start | bytes 1572872 | tf_op jit(solution)/shard_map/ppermute | solution.py:302
  62.6 2.4 %collective-permute-done.15.other_ref = bf16[64,1024]{1,0:T(8,128)(2,1)S(1)} collective-permute-done((bf16[64,1024]{1,0:T(8,128)(2,1)S(1)}, bf16[64,1024]{1,0:T(8,128)(2,1)S(1)}, u32[]{:S(2)}, u32[]{:S(2)}) %collective-permute-start.15) | collective-permute-done | bytes 131104 | tf_op jit(solution)/shard_map/ppermute | solution.py:302
  65.1 2.7 %collective-permute-start.16 = (bf16[64,1024]{1,0:T(8,128)(2,1)S(1)}, bf16[64,1024]{1,0:T(8,128)(2,1)S(1)}, u32[]{:S(2)}, u32[]{:S(2)}) collective-permute-start(bf16[64,1024]{1,0:T(8,128)(2,1)S(1)} %line_sum.3), channel_id=1, source_target_pairs={{0,16},{1,17},{2,18},{3,19},{4,20},{5,21},{6,22},{7,23},{8,24},{9,... | collective-permute-start | bytes 393224 | tf_op jit(solution)/shard_map/ppermute | solution.py:302
  67.8 1.8 %collective-permute-start.20 = (bf16[128,1024]{1,0:T(8,128)(2,1)S(1)}, bf16[128,1024]{1,0:T(8,128)(2,1)S(1)}, u32[]{:S(2)}, u32[]{:S(2)}) collective-permute-start(bf16[128,1024]{1,0:T(8,128)(2,1)S(1)} %get-tuple-element.89), channel_id=1, source_target_pairs={{0,8},{1,9},{2,10},{3,11},{4,12},{5,13},{6,14},{7,15},{8,0},{9,1},... | collective-permute-start | bytes 786440 | tf_op jit(solution)/shard_map/ppermute | solution.py:302
  69.6 2.2 %collective-permute-start.14 = (bf16[64,1024]{1,0:T(8,128)(2,1)S(1)}, bf16[64,1024]{1,0:T(8,128)(2,1)S(1)}, u32[]{:S(2)}, u32[]{:S(2)}) collective-permute-start(bf16[64,1024]{1,0:T(8,128)(2,1)S(1)} %line_sum.2), channel_id=1, source_target_pairs={{0,16},{1,17},{2,18},{3,19},{4,20},{5,21},{6,22},{7,23},{8,24},{9,... | collective-permute-start | bytes 393224 | tf_op jit(solution)/shard_map/ppermute | solution.py:302
  71.8 7.5 %collective-permute-done.18.y_ref = bf16[528,512]{1,0:T(8,128)(2,1)S(1)} collective-permute-done((bf16[528,512]{1,0:T(8,128)(2,1)S(1)}, bf16[528,512]{1,0:T(8,128)(2,1)S(1)}, u32[]{:S(2)}, u32[]{:S(2)}) %collective-permute-start.18) | collective-permute-done | bytes 540704 | tf_op jit(solution)/shard_map/ppermute | solution.py:302
  79.5 1.0 %add_convert_fusion = bf16[512,512]{1,0:T(8,128)(2,1)} fusion(f32[512,512]{1,0:T(8,128)S(1)} %plane_sum.1, bf16[512,512]{1,0:T(8,128)(2,1)S(1)} %collective-permute-done.19), kind=kLoop, calls=%fused_computation.4 | loop fusion | flops 786432 | bytes 2097152 | tf_op jit(solution)/shard_map/convert_element_type | solution.py:484
  80.4 0.9 %add_multiply_fusion = f32[128,1024]{1,0:T(8,128)} fusion(bf16[128,1024]{1,0:T(8,128)(2,1)S(1)} %collective-permute-done.20, bf16[128,1024]{1,0:T(8,128)(2,1)S(1)} %get-tuple-element.87, bf16[64,1024]{1,0:T(8,128)(2,1)S(1)} %collective-permute-done.16, bf16[64,1024]{1,0:T(8,128)(2,1)S(1)} %collective-permute-done.14), kind=kLoop, calls=%fused_computation.6 | loop fusion | flops 1179648 | bytes 1310720 | tf_op jit(solution)/shard_map/mul | solution.py:492
  (33 shorter events, 1.2 us)
Async XLA Ops:
  0.6 5.9 %copy-start.2 = (bf16[128]{0:T(256)(128)(2,1)S(1)}, bf16[128]{0:T(256)(128)(2,1)}, u32[]{:S(2)}) copy-start(bf16[128]{0:T(256)(128)(2,1)} %param.8) | copy-start | bytes 772
  0.6 5.9 %copy-start.1 = (bf16[128,1024]{1,0:T(8,128)(2,1)S(1)}, bf16[128,1024]{1,0:T(8,128)(2,1)}, u32[]{:S(2)}) copy-start(bf16[128,1024]{1,0:T(8,128)(2,1)} %param.7) | copy-start | bytes 786436
  0.7 5.9 %copy-start = (bf16[128,1024]{1,0:T(8,128)(2,1)S(1)}, bf16[128,1024]{1,0:T(8,128)(2,1)}, u32[]{:S(2)}) copy-start(bf16[128,1024]{1,0:T(8,128)(2,1)} %param.9) | copy-start | bytes 786436
  2.0 26.2 %collective-permute-start = (bf16[2,512,512]{2,1,0:T(8,128)(2,1)S(1)}, bf16[2,512,512]{2,1,0:T(8,128)(2,1)S(1)}, u32[]{:S(2)}, u32[]{:S(2)}) collective-permute-start(bf16[2,512,512]{2,1,0:T(8,128)(2,1)S(1)} %pad_maximum_fusion.1.refs_0_), channel_id=1, source_target_pairs={{0,2},{1,3},{2,0},{3,1},{4,6},{5,7},{6,4},{7,5},{8,10},{9,11},{10,... | collective-permute-start | bytes 3145736 | tf_op jit(solution)/shard_map/ppermute | solution.py:302
  5.0 24.6 %collective-permute-start.1 = (bf16[2,512,512]{2,1,0:T(8,128)(2,1)S(1)}, bf16[2,512,512]{2,1,0:T(8,128)(2,1)S(1)}, u32[]{:S(2)}, u32[]{:S(2)}) collective-permute-start(bf16[2,512,512]{2,1,0:T(8,128)(2,1)S(1)} %pad_maximum_fusion.1.refs_0_), channel_id=1, source_target_pairs={{0,4},{1,5},{2,6},{3,7},{4,0},{5,1},{6,2},{7,3},{8,12},{9,13},{10,... | collective-permute-start | bytes 3145736 | tf_op jit(solution)/shard_map/ppermute | solution.py:302
  6.5 23.1 %collective-permute-start.2 = (bf16[2,512,512]{2,1,0:T(8,128)(2,1)S(1)}, bf16[2,512,512]{2,1,0:T(8,128)(2,1)S(1)}, u32[]{:S(2)}, u32[]{:S(2)}) collective-permute-start(bf16[2,512,512]{2,1,0:T(8,128)(2,1)S(1)} %pad_maximum_fusion.1.refs_0_), channel_id=1, source_target_pairs={{0,1},{1,0},{2,3},{3,2},{4,5},{5,4},{6,7},{7,6},{8,9},{9,8},{10,11... | collective-permute-start | bytes 3145736 | tf_op jit(solution)/shard_map/ppermute | solution.py:302
  6.6 27.3 %collective-permute-start.6 = (bf16[264,1024]{1,0:T(8,128)(2,1)S(1)}, bf16[264,1024]{1,0:T(8,128)(2,1)S(1)}, u32[]{:S(2)}, u32[]{:S(2)}) collective-permute-start(bf16[264,1024]{1,0:T(8,128)(2,1)S(1)} %fusion.1.refs_6_), channel_id=1, source_target_pairs={{0,16},{1,17},{2,18},{3,19},{4,20},{5,21},{6,22},{7,23},{8,24},{9,... | collective-permute-start | bytes 1622024 | tf_op jit(solution)/shard_map/ppermute | solution.py:302
  9.3 25.9 %collective-permute-start.5 = (bf16[264,1024]{1,0:T(8,128)(2,1)S(1)}, bf16[264,1024]{1,0:T(8,128)(2,1)S(1)}, u32[]{:S(2)}, u32[]{:S(2)}) collective-permute-start(bf16[264,1024]{1,0:T(8,128)(2,1)S(1)} %fusion.1.refs_6_), channel_id=1, source_target_pairs={{0,8},{1,9},{2,10},{3,11},{4,12},{5,13},{6,14},{7,15},{8,0},{9,1},... | collective-permute-start | bytes 1622024 | tf_op jit(solution)/shard_map/ppermute | solution.py:302
  29.6 6.1 %collective-permute-start.3 = (bf16[2,512,512]{2,1,0:T(8,128)(2,1)S(1)}, bf16[2,512,512]{2,1,0:T(8,128)(2,1)S(1)}, u32[]{:S(2)}, u32[]{:S(2)}) collective-permute-start(bf16[2,512,512]{2,1,0:T(8,128)(2,1)S(1)} %collective-permute-done.refs_2_), channel_id=1, source_target_pairs={{0,1},{1,0},{2,3},{3,2},{4,5},{5,4},{6,7},{7,6},{8,9},{9,8},{10,11... | collective-permute-start | bytes 3145736 | tf_op jit(solution)/shard_map/ppermute | solution.py:302
  29.6 6.1 %collective-permute-start.4 = (bf16[2,512,512]{2,1,0:T(8,128)(2,1)S(1)}, bf16[2,512,512]{2,1,0:T(8,128)(2,1)S(1)}, u32[]{:S(2)}, u32[]{:S(2)}) collective-permute-start(bf16[2,512,512]{2,1,0:T(8,128)(2,1)S(1)} %collective-permute-done.1.refs_4_), channel_id=1, source_target_pairs={{0,1},{1,0},{2,3},{3,2},{4,5},{5,4},{6,7},{7,6},{8,9},{9,8},{10,11... | collective-permute-start | bytes 3145736 | tf_op jit(solution)/shard_map/ppermute | solution.py:302
  33.9 13.8 %collective-permute-start.7 = (bf16[264,1024]{1,0:T(8,128)(2,1)S(1)}, bf16[264,1024]{1,0:T(8,128)(2,1)S(1)}, u32[]{:S(2)}, u32[]{:S(2)}) collective-permute-start(bf16[264,1024]{1,0:T(8,128)(2,1)S(1)} %collective-permute-done.6.refs_8_), channel_id=1, source_target_pairs={{0,8},{1,9},{2,10},{3,11},{4,12},{5,13},{6,14},{7,15},{8,0},{9,1},... | collective-permute-start | bytes 1622024 | tf_op jit(solution)/shard_map/ppermute | solution.py:302
  34.6 15.8 %collective-permute-start.8 = (bf16[560,512]{1,0:T(8,128)(2,1)S(1)}, bf16[560,512]{1,0:T(8,128)(2,1)S(1)}, u32[]{:S(2)}, u32[]{:S(2)}) collective-permute-start(bf16[560,512]{1,0:T(8,128)(2,1)S(1)} %slice.12), channel_id=1, source_target_pairs={{0,4},{1,5},{2,6},{3,7},{4,0},{5,1},{6,2},{7,3},{8,12},{9,13},{10,... | collective-permute-start | bytes 1720328 | tf_op jit(solution)/shard_map/ppermute | solution.py:302
  35.2 15.2 %collective-permute-start.9 = (bf16[512,512]{1,0:T(8,128)(2,1)S(1)}, bf16[512,512]{1,0:T(8,128)(2,1)S(1)}, u32[]{:S(2)}, u32[]{:S(2)}) collective-permute-start(bf16[512,512]{1,0:T(8,128)(2,1)S(1)} %slice_bitcast_fusion), channel_id=1, source_target_pairs={{0,2},{1,3},{2,0},{3,1},{4,6},{5,7},{6,4},{7,5},{8,10},{9,11},{10,... | collective-permute-start | bytes 1572872 | tf_op jit(solution)/shard_map/ppermute | solution.py:302
  50.4 2.7 %collective-permute-start.10 = (bf16[1024,512]{1,0:T(8,128)(2,1)S(1)}, bf16[1024,512]{1,0:T(8,128)(2,1)S(1)}, u32[]{:S(2)}, u32[]{:S(2)}) collective-permute-start(bf16[1024,512]{1,0:T(8,128)(2,1)S(1)} %get-tuple-element.68), channel_id=1, source_target_pairs={{0,1},{1,0},{2,3},{3,2},{4,5},{5,4},{6,7},{7,6},{8,9},{9,8},{10,11... | collective-permute-start | bytes 3145736 | tf_op jit(solution)/shard_map/ppermute | solution.py:302
  50.6 4.8 %collective-permute-start.11 = (bf16[1536,512]{1,0:T(8,128)(2,1)S(1)}, bf16[1536,512]{1,0:T(8,128)(2,1)S(1)}, u32[]{:S(2)}, u32[]{:S(2)}) collective-permute-start(bf16[1536,512]{1,0:T(8,128)(2,1)S(1)} %pad_maximum_fusion), channel_id=1, source_target_pairs={{0,1},{1,0},{2,3},{3,2},{4,5},{5,4},{6,7},{7,6},{8,9},{9,8},{10,11... | collective-permute-start | bytes 4718600 | tf_op jit(solution)/shard_map/ppermute | solution.py:302
  53.4 16.2 %collective-permute-start.17 = (bf16[528,512]{1,0:T(8,128)(2,1)S(1)}, bf16[528,512]{1,0:T(8,128)(2,1)S(1)}, u32[]{:S(2)}, u32[]{:S(2)}) collective-permute-start(bf16[528,512]{1,0:T(8,128)(2,1)S(1)} %get-tuple-element.69), channel_id=1, source_target_pairs={{0,2},{1,3},{2,0},{3,1},{4,6},{5,7},{6,4},{7,5},{8,10},{9,11},{10,... | collective-permute-start | bytes 1622024 | tf_op jit(solution)/shard_map/ppermute | solution.py:302
  54.0 25.3 %collective-permute-start.18 = (bf16[528,512]{1,0:T(8,128)(2,1)S(1)}, bf16[528,512]{1,0:T(8,128)(2,1)S(1)}, u32[]{:S(2)}, u32[]{:S(2)}) collective-permute-start(bf16[528,512]{1,0:T(8,128)(2,1)S(1)} %get-tuple-element.85), channel_id=1, source_target_pairs={{0,4},{1,5},{2,6},{3,7},{4,0},{5,1},{6,2},{7,3},{8,12},{9,13},{10,... | collective-permute-start | bytes 1622024 | tf_op jit(solution)/shard_map/ppermute | solution.py:302
  58.5 2.2 %collective-permute-start.12 = (bf16[512,512]{1,0:T(8,128)(2,1)S(1)}, bf16[512,512]{1,0:T(8,128)(2,1)S(1)}, u32[]{:S(2)}, u32[]{:S(2)}) collective-permute-start(bf16[512,512]{1,0:T(8,128)(2,1)S(1)} %get-tuple-element.77), channel_id=1, source_target_pairs={{0,1},{1,0},{2,3},{3,2},{4,5},{5,4},{6,7},{7,6},{8,9},{9,8},{10,11... | collective-permute-start | bytes 1572872 | tf_op jit(solution)/shard_map/ppermute | solution.py:302
  58.7 6.3 %collective-permute-start.15 = (bf16[64,1024]{1,0:T(8,128)(2,1)S(1)}, bf16[64,1024]{1,0:T(8,128)(2,1)S(1)}, u32[]{:S(2)}, u32[]{:S(2)}) collective-permute-start(bf16[64,1024]{1,0:T(8,128)(2,1)S(1)} %get-tuple-element.83), channel_id=1, source_target_pairs={{0,8},{1,9},{2,10},{3,11},{4,12},{5,13},{6,14},{7,15},{8,0},{9,1},... | collective-permute-start | bytes 393224 | tf_op jit(solution)/shard_map/ppermute | solution.py:302
  59.7 8.0 %collective-permute-start.13 = (bf16[64,1024]{1,0:T(8,128)(2,1)S(1)}, bf16[64,1024]{1,0:T(8,128)(2,1)S(1)}, u32[]{:S(2)}, u32[]{:S(2)}) collective-permute-start(bf16[64,1024]{1,0:T(8,128)(2,1)S(1)} %get-tuple-element.80), channel_id=1, source_target_pairs={{0,8},{1,9},{2,10},{3,11},{4,12},{5,13},{6,14},{7,15},{8,0},{9,1},... | collective-permute-start | bytes 393224 | tf_op jit(solution)/shard_map/ppermute | solution.py:302
  61.0 18.4 %collective-permute-start.19 = (bf16[512,512]{1,0:T(8,128)(2,1)S(1)}, bf16[512,512]{1,0:T(8,128)(2,1)S(1)}, u32[]{:S(2)}, u32[]{:S(2)}) collective-permute-start(bf16[512,512]{1,0:T(8,128)(2,1)S(1)} %get-tuple-element.78), channel_id=1, source_target_pairs={{0,6},{1,7},{2,4},{3,5},{4,2},{5,3},{6,0},{7,1},{8,14},{9,15},{10,... | collective-permute-start | bytes 1572872 | tf_op jit(solution)/shard_map/ppermute | solution.py:302
  65.1 15.3 %collective-permute-start.16 = (bf16[64,1024]{1,0:T(8,128)(2,1)S(1)}, bf16[64,1024]{1,0:T(8,128)(2,1)S(1)}, u32[]{:S(2)}, u32[]{:S(2)}) collective-permute-start(bf16[64,1024]{1,0:T(8,128)(2,1)S(1)} %line_sum.3), channel_id=1, source_target_pairs={{0,16},{1,17},{2,18},{3,19},{4,20},{5,21},{6,22},{7,23},{8,24},{9,... | collective-permute-start | bytes 393224 | tf_op jit(solution)/shard_map/ppermute | solution.py:302
  67.8 12.6 %collective-permute-start.20 = (bf16[128,1024]{1,0:T(8,128)(2,1)S(1)}, bf16[128,1024]{1,0:T(8,128)(2,1)S(1)}, u32[]{:S(2)}, u32[]{:S(2)}) collective-permute-start(bf16[128,1024]{1,0:T(8,128)(2,1)S(1)} %get-tuple-element.89), channel_id=1, source_target_pairs={{0,8},{1,9},{2,10},{3,11},{4,12},{5,13},{6,14},{7,15},{8,0},{9,1},... | collective-permute-start | bytes 786440 | tf_op jit(solution)/shard_map/ppermute | solution.py:302
  69.6 10.8 %collective-permute-start.14 = (bf16[64,1024]{1,0:T(8,128)(2,1)S(1)}, bf16[64,1024]{1,0:T(8,128)(2,1)S(1)}, u32[]{:S(2)}, u32[]{:S(2)}) collective-permute-start(bf16[64,1024]{1,0:T(8,128)(2,1)S(1)} %line_sum.2), channel_id=1, source_target_pairs={{0,16},{1,17},{2,18},{3,19},{4,20},{5,21},{6,22},{7,23},{8,24},{9,... | collective-permute-start | bytes 393224 | tf_op jit(solution)/shard_map/ppermute | solution.py:302

commit v18 on v17

--- a/solution.py
+++ b/solution.py
@@ -116,26 +116,22 @@
     return lax.dot_general(left, right, CONTRACT_FIRST, preferred_element_type=jnp.float32)
 
 
-def early_block(start, step, tok, cot, w_in, w_out, bias, two, act_ref, dpre_ref, mixed_ref, dpre):
+def early_block(start, step, tok, cot, w_in, w_out, bias, mixed_ref, dpre):
     @pl.loop(0, 2)
     def _(sub):
         spot = pl.ds(pl.multiple_of(start + sub * step, step), step)
         value, slope = activate(tok[spot, :], w_in[...], bias[0:1, :])
-        act = value.astype(jnp.bfloat16)
-        act_ref[spot, :] = act[:, two:]
         dact = dot_last(cot[spot, :], w_out[...])
-        terms = (dact * slope).astype(jnp.bfloat16)
-        dpre[spot, :] = terms[:, :two]
-        dpre_ref[spot, :] = terms[:, two:]
+        dpre[spot, :] = (dact * slope).astype(jnp.bfloat16)
         mixed_ref[spot, :] = jnp.dot(
-            act[:, :two], w_out[:two, :], preferred_element_type=jnp.float32
+            value.astype(jnp.bfloat16), w_out[...], preferred_element_type=jnp.float32
         )
 
 
 def early_kernel(owned, *refs):
     pair_refs, w_refs = refs[:6], refs[6:9]
-    act_ref, dpre_ref, mixed_ref, grad_ref, tok, cot, w_in, w_out, bias = refs[9:18]
-    dpre, tok_sem, cot_sem, w_sem = refs[18:]
+    mixed_ref, grad_ref, tok, cot, w_in, w_out, bias = refs[9:16]
+    dpre, tok_sem, cot_sem, w_sem = refs[16:]
     core = lax.axis_index("core")
     rows = pair_refs[0].shape[1]
     w_copies = weight_copies(w_refs, owned, w_in, w_out, w_sem)
@@ -155,16 +151,14 @@
     for block, load in enumerate(loads):
         run(load, "wait")
         early_block(
-            block * rows, rows // 2, tok, cot, w_in, w_out, bias, 2 * owned,
-            act_ref, dpre_ref, mixed_ref, dpre,
+            block * rows, rows // 2, tok, cot, w_in, w_out, bias, mixed_ref, dpre
         )
     grad_ref[...] = dot_first(dpre[...], tok[...])
 
 
 def output_kernel(owned, *refs):
-    act_two, tok, early_mixed, w_in, w_out, bias, w_three = refs[:7]
-    mine_ref, near_ref, own_ref, slope_ref, w_in_all, w_out_all, bias_all = refs[7:14]
-    w_last, sem = refs[14:]
+    tok, early_mixed, w_in, w_out, bias, w_three = refs[:6]
+    mine_ref, near_ref, own_ref, slope_ref, w_in_all, w_out_all, bias_all, sem = refs[6:]
     core = lax.axis_index("core")
     rows, feats = own_ref.shape
     two, three = 2 * owned, 3 * owned
@@ -179,14 +173,12 @@
     bias_last = bias_of(w_three, owned)
     bias_all[:, :three] = bias[...]
     bias_all[:, three:] = bias_last
-    w_last[:owned, :] = w_out[two:, :]
-    w_last[owned:, :] = w_three[owned:two, :]
     step = tok.shape[0] // 6
     for at in range(6):
         spot = slice(at * step, (at + 1) * step)
         value, slope = activate(tok[spot, :], w_three[:owned, :], bias_last[0:1, :])
         slope_ref[spot, :] = slope
-        act = jnp.concatenate([act_two[spot, :], value.astype(jnp.bfloat16)], axis=1)
+        act = value.astype(jnp.bfloat16)
         if at * step < rows:
             far_ref, there = own_ref, spot
         else:
@@ -195,20 +187,19 @@
             half = half_columns(core, shift, feats)
             ref[to, :] = (
                 early_mixed[spot, half]
-                + jnp.dot(act, w_last[:, half], preferred_element_type=jnp.float32)
+                + jnp.dot(act, w_three[owned:two, half], preferred_element_type=jnp.float32)
             ).astype(jnp.bfloat16)
 
     run(copies, "wait")
 
 
-def gradient_kernel(dpre_two, tok, cot, slope, w_three, grad_ref, dpre):
+def gradient_kernel(tok, cot, slope, w_three, grad_ref, dpre):
     owned = slope.shape[1]
     step = tok.shape[0] // 6
     for at in range(6):
         spot = slice(at * step, (at + 1) * step)
         dact = dot_last(cot[spot, :], w_three[owned : 2 * owned, :])
-        last = (dact * slope[spot, :]).astype(jnp.bfloat16)
-        dpre[spot, :] = jnp.concatenate([dpre_two[spot, :], last], axis=1)
+        dpre[spot, :] = (dact * slope[spot, :]).astype(jnp.bfloat16)
     grad_ref[...] = dot_first(dpre[...], tok[...])
 
 
@@ -238,12 +229,13 @@
                 act, w_out[:, half_columns(core, shift, feats)], preferred_element_type=jnp.float32
             ).astype(jnp.bfloat16)
 
-    grad = grad_last[...] + dot_first(dpre[:, two:], tok[...])
+    grad = dot_first(dpre[:, two:], tok[...])
+    middle, last = grad[:owned] + grad_first[two:, :], grad[owned:] + grad_last[...]
     part = owned // PARTS
     for at in range(PARTS):
-        two_refs[at][...] = grad[at * part : (at + 1) * part].astype(jnp.bfloat16)
-        three_refs[at][...] = grad[owned + at * part : owned + (at + 1) * part].astype(jnp.bfloat16)
-    grad = grad_first[...] + dot_first(dpre[:, :two], tok[...])
+        two_refs[at][...] = middle[at * part : (at + 1) * part].astype(jnp.bfloat16)
+        three_refs[at][...] = last[at * part : (at + 1) * part].astype(jnp.bfloat16)
+    grad = grad_first[:two, :] + dot_first(dpre[:, :two], tok[...])
     own_ref[...] = grad[:owned].astype(jnp.bfloat16)
     one_ref[...] = grad[owned:].astype(jnp.bfloat16)
 
@@ -350,14 +342,12 @@
     cot_diag = to_x(from_y[1])
     x_other, y_other = to_core(from_x), to_core(from_y)
     w_three = to_far(w_two, 1)
-    act_two, dpre_two, mixed_terms, grad_terms, tok, cot, w_in_three, w_out_three, bias = (
+    mixed_terms, grad_terms, tok, cot, w_in_three, w_out_three, bias = (
         pl.pallas_call(
             functools.partial(early_kernel, owned),
             out_shape=(
-                bf16(early_rows, owned),
-                bf16(early_rows, owned),
                 f32(early_rows, width),
-                f32(2 * owned, width),
+                f32(3 * owned, width),
                 bf16(early_rows, width),
                 bf16(early_rows, width),
                 bf16(3 * owned, width),
@@ -365,9 +355,9 @@
                 f32(BIAS_ROWS, 3 * owned),
             ),
             in_specs=anywhere(6) + vmem(3),
-            out_specs=vmem(9),
+            out_specs=vmem(7),
             scratch_shapes=[
-                pltpu.VMEM((early_rows, 2 * owned), jnp.bfloat16),
+                pltpu.VMEM((early_rows, 3 * owned), jnp.bfloat16),
                 dma((NEAR - 1, 2)),
                 dma((NEAR - 1, 2)),
                 dma((2, 3)),
@@ -389,27 +379,27 @@
             bf16(units, width),
             f32(BIAS_ROWS, units),
         ),
-        in_specs=vmem(7),
+        in_specs=vmem(6),
         out_specs=vmem(7),
-        scratch_shapes=[pltpu.VMEM((2 * owned, width), jnp.bfloat16), dma((4,))],
+        scratch_shapes=[dma((4,))],
         compiler_params=params,
         cost_estimate=cost(early_rows * units, early_rows),
         name="output",
-    )(act_two, tok, mixed_terms, w_in_three, w_out_three, bias, w_three)
+    )(tok, mixed_terms, w_in_three, w_out_three, bias, w_three)
     tok_diag, cot_diag, other = barrier((tok_diag, cot_diag, other))
     received = to_core(other)
     diag_other = to_core(jnp.concatenate([tok_diag[:rows], cot_diag, other_own]))
     slope, tok_diag = barrier((slope, tok_diag))
     grad_last = pl.pallas_call(
         gradient_kernel,
-        out_shape=f32(2 * owned, width),
-        in_specs=vmem(5),
+        out_shape=f32(owned, width),
+        in_specs=vmem(4),
         out_specs=pl.BlockSpec(memory_space=pltpu.VMEM),
-        scratch_shapes=[pltpu.VMEM((early_rows, 2 * owned), jnp.bfloat16)],
+        scratch_shapes=[pltpu.VMEM((early_rows, owned), jnp.bfloat16)],
         compiler_params=params,
         cost_estimate=cost(GRADIENT_COST, early_rows),
         name="gradient",
-    )(dpre_two, tok, cot, slope, w_three)
+    )(tok, cot, slope, w_three)
 
     mine, grad_last = barrier((mine, grad_last))
     sums = pl.pallas_call(

time: 81.5 us -> 81.8 us (level)
  Pallas kernels: 15.7 us -> 17.2 us
  waiting for transfers between devices: 38 us -> 36.8 us
    ppermute x21, waiting for transfers between devices: 38 us -> 36.8 us  [permute(): return lax.ppermute(value, AXES, pairs)]
    pallas_call x2, Pallas kernels: 9.25 us -> 10.3 us  [the longest x1 8.77 us: on_device_lines(): pl.pallas_call(functools.partial(early_kernel, owned), out_shape=(f32(ear...]
  transfers between devices with their start and end apart: 21 -> 21, of which waited for: 8 -> 8; matrix products, arithmetic and copies ran while one was open for 1% -> 1% of each run, Pallas kernels for 19% -> 21%
where the time goes in v18:
time: 81.8 us; the launch traced here: 81.7 us
  waiting for transfers between devices  36.8 us (45%)
  starting transfers between devices  23.4 us (29%)
  Pallas kernels  17.2 us (21%)
  other arithmetic  3.36 us (4%)
  between operations  0.82 us (1%)
    ppermute x21, waiting for transfers between devices, permute(): return lax.ppermute(value, AXES, pairs)  36.8 us
    ppermute x21, starting transfers between devices, permute(): return lax.ppermute(value, AXES, pairs)  23.4 us
    pallas_call x1, Pallas kernels, on_device_lines(): pl.pallas_call(functools.partial(early_kernel, owned), out_shape=(f32(ear...  8.77 us
    pallas_call x1, Pallas kernels, on_device_lines(): pl.pallas_call(functools.partial(diagonal_kernel, owned), out_shape=[bf16...  3.29 us
    pallas_call x1, Pallas kernels, on_device_lines(): pl.pallas_call(functools.partial(output_kernel, owned), out_shape=(bf16(e...  2.87 us
  transfers between devices with their start and end apart: 21, of which 8 were waited for; matrix products, arithmetic and copies ran while one was open for 1% of the time, Pallas kernels for 21%

profile of v18, /device:TPU:0, one launch (start us, length us, event | category | flops | bytes accessed | tf_op | source)
XLA Modules:
  0.0 81.7 jit_solution(17420588238118288008)
XLA Ops:
  0.7 1.4 %pad_maximum_fusion.1.refs_0_ = bf16[2,512,512]{2,1,0:T(8,128)(2,1)S(1)} fusion(bf16[1,512,512]{2,1,0:T(8,128)(2,1)} %bitcast.7, bf16[1,512,512]{2,1,0:T(8,128)(2,1)} %bitcast.8), kind=kLoop, calls=%fused_computation.3 | loop fusion | flops 524288 | bytes 2097152 | tf_op jit(solution)/shard_map/stack | solution.py:336
  2.0 3.0 %collective-permute-start = (bf16[2,512,512]{2,1,0:T(8,128)(2,1)S(1)}, bf16[2,512,512]{2,1,0:T(8,128)(2,1)S(1)}, u32[]{:S(2)}, u32[]{:S(2)}) collective-permute-start(bf16[2,512,512]{2,1,0:T(8,128)(2,1)S(1)} %pad_maximum_fusion.1.refs_0_), channel_id=1, source_target_pairs={{0,2},{1,3},{2,0},{3,1},{4,6},{5,7},{6,4},{7,5},{8,10},{9,11},{10,... | collective-permute-start | bytes 3145736 | tf_op jit(solution)/shard_map/ppermute | solution.py:294
  5.0 1.5 %collective-permute-start.1 = (bf16[2,512,512]{2,1,0:T(8,128)(2,1)S(1)}, bf16[2,512,512]{2,1,0:T(8,128)(2,1)S(1)}, u32[]{:S(2)}, u32[]{:S(2)}) collective-permute-start(bf16[2,512,512]{2,1,0:T(8,128)(2,1)S(1)} %pad_maximum_fusion.1.refs_0_), channel_id=1, source_target_pairs={{0,4},{1,5},{2,6},{3,7},{4,0},{5,1},{6,2},{7,3},{8,12},{9,13},{10,... | collective-permute-start | bytes 3145736 | tf_op jit(solution)/shard_map/ppermute | solution.py:294
  6.6 2.7 %collective-permute-start.6 = (bf16[264,1024]{1,0:T(8,128)(2,1)S(1)}, bf16[264,1024]{1,0:T(8,128)(2,1)S(1)}, u32[]{:S(2)}, u32[]{:S(2)}) collective-permute-start(bf16[264,1024]{1,0:T(8,128)(2,1)S(1)} %fusion.1.refs_6_), channel_id=1, source_target_pairs={{0,16},{1,17},{2,18},{3,19},{4,20},{5,21},{6,22},{7,23},{8,24},{9,... | collective-permute-start | bytes 1622024 | tf_op jit(solution)/shard_map/ppermute | solution.py:294
  9.3 1.6 %collective-permute-start.5 = (bf16[264,1024]{1,0:T(8,128)(2,1)S(1)}, bf16[264,1024]{1,0:T(8,128)(2,1)S(1)}, u32[]{:S(2)}, u32[]{:S(2)}) collective-permute-start(bf16[264,1024]{1,0:T(8,128)(2,1)S(1)} %fusion.1.refs_6_), channel_id=1, source_target_pairs={{0,8},{1,9},{2,10},{3,11},{4,12},{5,13},{6,14},{7,15},{8,0},{9,1},... | collective-permute-start | bytes 1622024 | tf_op jit(solution)/shard_map/ppermute | solution.py:294
  10.8 17.3 %collective-permute-done.refs_2_ = bf16[2,512,512]{2,1,0:T(8,128)(2,1)S(1)} collective-permute-done((bf16[2,512,512]{2,1,0:T(8,128)(2,1)S(1)}, bf16[2,512,512]{2,1,0:T(8,128)(2,1)S(1)}, u32[]{:S(2)}, u32[]{:S(2)}) %collective-permute-start) | collective-permute-done | bytes 1048608 | tf_op jit(solution)/shard_map/ppermute | solution.py:294
  28.2 1.5 %collective-permute-done.1.refs_4_ = bf16[2,512,512]{2,1,0:T(8,128)(2,1)S(1)} collective-permute-done((bf16[2,512,512]{2,1,0:T(8,128)(2,1)S(1)}, bf16[2,512,512]{2,1,0:T(8,128)(2,1)S(1)}, u32[]{:S(2)}, u32[]{:S(2)}) %collective-permute-start.1) | collective-permute-done | bytes 1048608 | tf_op jit(solution)/shard_map/ppermute | solution.py:294
  29.6 0.5 collective-permute-start.4
  30.2 3.8 %collective-permute-done.6.refs_8_ = bf16[264,1024]{1,0:T(8,128)(2,1)S(1)} collective-permute-done((bf16[264,1024]{1,0:T(8,128)(2,1)S(1)}, bf16[264,1024]{1,0:T(8,128)(2,1)S(1)}, u32[]{:S(2)}, u32[]{:S(2)}) %collective-permute-start.6) | collective-permute-done | bytes 540704 | tf_op jit(solution)/shard_map/ppermute | solution.py:294
  33.9 0.6 collective-permute-start.7
  34.6 0.6 collective-permute-start.8
  35.2 0.6 collective-permute-start.9
  35.8 8.8 %early.1 = (f32[1536,1024]{1,0:T(8,128)S(1)}, f32[384,1024]{1,0:T(8,128)S(1)}, bf16[1536,1024]{1,0:T(8,128)(2,1)S(1)}, bf16[1536,1024]{1,0:T(8,128)(2,1)S(1)}, b...) custom-call(bf16[2,512,512]{2,1,0:T(8,128)(2,1)S(1)} %pad_maximum_fusion.1.refs_0_, ...), custom_call_target="tpu_custom_call" | custom-call | flops 786432 | bytes 1536 | tf_op jit(solution)/shard_map/early/pallas_call | solution.py:346
  44.6 3.2 %collective-permute-done.7.refs_5_.w_three = bf16[264,1024]{1,0:T(8,128)(2,1)S(1)} collective-permute-done((bf16[264,1024]{1,0:T(8,128)(2,1)S(1)}, bf16[264,1024]{1,0:T(8,128)(2,1)S(1)}, u32[]{:S(2)}, u32[]{:S(2)}) %collective-permute-start.7) | collective-permute-done | bytes 540704 | tf_op jit(solution)/shard_map/ppermute | solution.py:294
  47.8 2.9 %output.1 = (bf16[1536,512]{1,0:T(8,128)(2,1)S(1)}, bf16[1024,512]{1,0:T(8,128)(2,1)S(1)}, bf16[512,512]{1,0:T(8,128)(2,1)S(1)}, f32[1536,128]{1,0:T(8,128)S(1)}...) custom-call(bf16[1536,1024]{1,0:T(8,128)(2,1)S(1)} %get-tuple-element.48.refs_0_.tok, ...), custom_call_target="tpu_custom_call" | custom-call | flops 786432 | bytes 1536 | tf_op jit(solution)/shard_map/output/pallas_call | solution.py:371
  50.9 0.6 collective-permute-start.11
  51.5 1.5 %gradient.1.refs_4_ = f32[128,1024]{1,0:T(8,128)S(1)} custom-call(bf16[1536,1024]{1,0:T(8,128)(2,1)S(1)} %get-tuple-element.48.refs_0_.tok, bf16[1536,1024]{1,0:T(8,128)(2,1)S(1)} %get-tuple-element.58.cot, f32[1536,128]{1,0:T(8,128)S(1)} %get-tuple-element.62.slope, bf16[264,1024]{1,0:T(8,128)(2,1)S(1)} %collective-permute-done.7.refs_5_.w_three), custom_call_target="tpu_custom_call" | custom-call | flops 10000000000 | bytes 1536 | tf_op jit(solution)/shard_map/gradient/pallas_call | solution.py:393
  53.0 0.4 collective-permute-done.10.other_ref
  53.7 0.6 collective-permute-start.17
  54.3 0.7 collective-permute-start.18
  55.0 0.7 collective-permute-done.11.refs_7_.far_ref
  55.7 3.3 %diagonal.1 = (bf16[512,512]{1,0:T(8,128)(2,1)S(1)}, bf16[512,512]{1,0:T(8,128)(2,1)S(1)}, bf16[128,1024]{1,0:T(8,128)(2,1)S(1)}, bf16[128,1024]{1,0:T(8,128)(2,...) custom-call(bf16[512,1024]{1,0:T(8,128)(2,1)S(1)} %get-tuple-element, ...), custom_call_target="tpu_custom_call" | custom-call | flops 1000000 | bytes 512 | tf_op jit(solution)/shard_map/diagonal/pallas_call | solution.py:417
  59.2 1.0 %collective-permute-start.15 = (bf16[64,1024]{1,0:T(8,128)(2,1)S(1)}, bf16[64,1024]{1,0:T(8,128)(2,1)S(1)}, u32[]{:S(2)}, u32[]{:S(2)}) collective-permute-start(bf16[64,1024]{1,0:T(8,128)(2,1)S(1)} %get-tuple-element.79), channel_id=1, source_target_pairs={{0,8},{1,9},{2,10},{3,11},{4,12},{5,13},{6,14},{7,15},{8,0},{9,1},... | collective-permute-start | bytes 393224 | tf_op jit(solution)/shard_map/ppermute | solution.py:294
  60.2 1.0 %collective-permute-start.13 = (bf16[64,1024]{1,0:T(8,128)(2,1)S(1)}, bf16[64,1024]{1,0:T(8,128)(2,1)S(1)}, u32[]{:S(2)}, u32[]{:S(2)}) collective-permute-start(bf16[64,1024]{1,0:T(8,128)(2,1)S(1)} %get-tuple-element.76), channel_id=1, source_target_pairs={{0,8},{1,9},{2,10},{3,11},{4,12},{5,13},{6,14},{7,15},{8,0},{9,1},... | collective-permute-start | bytes 393224 | tf_op jit(solution)/shard_map/ppermute | solution.py:294
  61.5 1.6 %collective-permute-start.19 = (bf16[512,512]{1,0:T(8,128)(2,1)S(1)}, bf16[512,512]{1,0:T(8,128)(2,1)S(1)}, u32[]{:S(2)}, u32[]{:S(2)}) collective-permute-start(bf16[512,512]{1,0:T(8,128)(2,1)S(1)} %get-tuple-element.74), channel_id=1, source_target_pairs={{0,6},{1,7},{2,4},{3,5},{4,2},{5,3},{6,0},{7,1},{8,14},{9,15},{10,... | collective-permute-start | bytes 1572872 | tf_op jit(solution)/shard_map/ppermute | solution.py:294
  63.1 2.5 %collective-permute-done.15.other_ref = bf16[64,1024]{1,0:T(8,128)(2,1)S(1)} collective-permute-done((bf16[64,1024]{1,0:T(8,128)(2,1)S(1)}, bf16[64,1024]{1,0:T(8,128)(2,1)S(1)}, u32[]{:S(2)}, u32[]{:S(2)}) %collective-permute-start.15) | collective-permute-done | bytes 131104 | tf_op jit(solution)/shard_map/ppermute | solution.py:294
  65.6 2.7 %collective-permute-start.16 = (bf16[64,1024]{1,0:T(8,128)(2,1)S(1)}, bf16[64,1024]{1,0:T(8,128)(2,1)S(1)}, u32[]{:S(2)}, u32[]{:S(2)}) collective-permute-start(bf16[64,1024]{1,0:T(8,128)(2,1)S(1)} %line_sum.3), channel_id=1, source_target_pairs={{0,16},{1,17},{2,18},{3,19},{4,20},{5,21},{6,22},{7,23},{8,24},{9,... | collective-permute-start | bytes 393224 | tf_op jit(solution)/shard_map/ppermute | solution.py:294
  68.3 1.8 %collective-permute-start.20 = (bf16[128,1024]{1,0:T(8,128)(2,1)S(1)}, bf16[128,1024]{1,0:T(8,128)(2,1)S(1)}, u32[]{:S(2)}, u32[]{:S(2)}) collective-permute-start(bf16[128,1024]{1,0:T(8,128)(2,1)S(1)} %get-tuple-element.85), channel_id=1, source_target_pairs={{0,8},{1,9},{2,10},{3,11},{4,12},{5,13},{6,14},{7,15},{8,0},{9,1},... | collective-permute-start | bytes 786440 | tf_op jit(solution)/shard_map/ppermute | solution.py:294
  70.1 2.2 %collective-permute-start.14 = (bf16[64,1024]{1,0:T(8,128)(2,1)S(1)}, bf16[64,1024]{1,0:T(8,128)(2,1)S(1)}, u32[]{:S(2)}, u32[]{:S(2)}) collective-permute-start(bf16[64,1024]{1,0:T(8,128)(2,1)S(1)} %line_sum.2), channel_id=1, source_target_pairs={{0,16},{1,17},{2,18},{3,19},{4,20},{5,21},{6,22},{7,23},{8,24},{9,... | collective-permute-start | bytes 393224 | tf_op jit(solution)/shard_map/ppermute | solution.py:294
  72.3 7.3 %collective-permute-done.18.y_ref = bf16[528,512]{1,0:T(8,128)(2,1)S(1)} collective-permute-done((bf16[528,512]{1,0:T(8,128)(2,1)S(1)}, bf16[528,512]{1,0:T(8,128)(2,1)S(1)}, u32[]{:S(2)}, u32[]{:S(2)}) %collective-permute-start.18) | collective-permute-done | bytes 540704 | tf_op jit(solution)/shard_map/ppermute | solution.py:294
  79.8 1.0 %add_convert_fusion = bf16[512,512]{1,0:T(8,128)(2,1)} fusion(f32[512,512]{1,0:T(8,128)S(1)} %plane_sum.1, bf16[512,512]{1,0:T(8,128)(2,1)S(1)} %collective-permute-done.19), kind=kLoop, calls=%fused_computation.4 | loop fusion | flops 786432 | bytes 2097152 | tf_op jit(solution)/shard_map/convert_element_type | solution.py:474
  80.7 0.9 %add_multiply_fusion = f32[128,1024]{1,0:T(8,128)} fusion(bf16[128,1024]{1,0:T(8,128)(2,1)S(1)} %collective-permute-done.20, bf16[128,1024]{1,0:T(8,128)(2,1)S(1)} %get-tuple-element.83, bf16[64,1024]{1,0:T(8,128)(2,1)S(1)} %collective-permute-done.16, bf16[64,1024]{1,0:T(8,128)(2,1)S(1)} %collective-permute-done.14), kind=kLoop, calls=%fused_computation.6 | loop fusion | flops 1179648 | bytes 1310720 | tf_op jit(solution)/shard_map/mul | solution.py:482
  (33 shorter events, 1.4 us)
Async XLA Ops:
  0.6 5.9 %copy-start.2 = (bf16[128]{0:T(256)(128)(2,1)S(1)}, bf16[128]{0:T(256)(128)(2,1)}, u32[]{:S(2)}) copy-start(bf16[128]{0:T(256)(128)(2,1)} %param.8) | copy-start | bytes 772
  0.6 5.9 %copy-start.1 = (bf16[128,1024]{1,0:T(8,128)(2,1)S(1)}, bf16[128,1024]{1,0:T(8,128)(2,1)}, u32[]{:S(2)}) copy-start(bf16[128,1024]{1,0:T(8,128)(2,1)} %param.7) | copy-start | bytes 786436
  0.7 5.9 %copy-start = (bf16[128,1024]{1,0:T(8,128)(2,1)S(1)}, bf16[128,1024]{1,0:T(8,128)(2,1)}, u32[]{:S(2)}) copy-start(bf16[128,1024]{1,0:T(8,128)(2,1)} %param.9) | copy-start | bytes 786436
  2.0 26.2 %collective-permute-start = (bf16[2,512,512]{2,1,0:T(8,128)(2,1)S(1)}, bf16[2,512,512]{2,1,0:T(8,128)(2,1)S(1)}, u32[]{:S(2)}, u32[]{:S(2)}) collective-permute-start(bf16[2,512,512]{2,1,0:T(8,128)(2,1)S(1)} %pad_maximum_fusion.1.refs_0_), channel_id=1, source_target_pairs={{0,2},{1,3},{2,0},{3,1},{4,6},{5,7},{6,4},{7,5},{8,10},{9,11},{10,... | collective-permute-start | bytes 3145736 | tf_op jit(solution)/shard_map/ppermute | solution.py:294
  5.0 24.6 %collective-permute-start.1 = (bf16[2,512,512]{2,1,0:T(8,128)(2,1)S(1)}, bf16[2,512,512]{2,1,0:T(8,128)(2,1)S(1)}, u32[]{:S(2)}, u32[]{:S(2)}) collective-permute-start(bf16[2,512,512]{2,1,0:T(8,128)(2,1)S(1)} %pad_maximum_fusion.1.refs_0_), channel_id=1, source_target_pairs={{0,4},{1,5},{2,6},{3,7},{4,0},{5,1},{6,2},{7,3},{8,12},{9,13},{10,... | collective-permute-start | bytes 3145736 | tf_op jit(solution)/shard_map/ppermute | solution.py:294
  6.5 23.1 %collective-permute-start.2 = (bf16[2,512,512]{2,1,0:T(8,128)(2,1)S(1)}, bf16[2,512,512]{2,1,0:T(8,128)(2,1)S(1)}, u32[]{:S(2)}, u32[]{:S(2)}) collective-permute-start(bf16[2,512,512]{2,1,0:T(8,128)(2,1)S(1)} %pad_maximum_fusion.1.refs_0_), channel_id=1, source_target_pairs={{0,1},{1,0},{2,3},{3,2},{4,5},{5,4},{6,7},{7,6},{8,9},{9,8},{10,11... | collective-permute-start | bytes 3145736 | tf_op jit(solution)/shard_map/ppermute | solution.py:294
  6.6 27.3 %collective-permute-start.6 = (bf16[264,1024]{1,0:T(8,128)(2,1)S(1)}, bf16[264,1024]{1,0:T(8,128)(2,1)S(1)}, u32[]{:S(2)}, u32[]{:S(2)}) collective-permute-start(bf16[264,1024]{1,0:T(8,128)(2,1)S(1)} %fusion.1.refs_6_), channel_id=1, source_target_pairs={{0,16},{1,17},{2,18},{3,19},{4,20},{5,21},{6,22},{7,23},{8,24},{9,... | collective-permute-start | bytes 1622024 | tf_op jit(solution)/shard_map/ppermute | solution.py:294
  9.3 25.9 %collective-permute-start.5 = (bf16[264,1024]{1,0:T(8,128)(2,1)S(1)}, bf16[264,1024]{1,0:T(8,128)(2,1)S(1)}, u32[]{:S(2)}, u32[]{:S(2)}) collective-permute-start(bf16[264,1024]{1,0:T(8,128)(2,1)S(1)} %fusion.1.refs_6_), channel_id=1, source_target_pairs={{0,8},{1,9},{2,10},{3,11},{4,12},{5,13},{6,14},{7,15},{8,0},{9,1},... | collective-permute-start | bytes 1622024 | tf_op jit(solution)/shard_map/ppermute | solution.py:294
  29.6 6.1 %collective-permute-start.3 = (bf16[2,512,512]{2,1,0:T(8,128)(2,1)S(1)}, bf16[2,512,512]{2,1,0:T(8,128)(2,1)S(1)}, u32[]{:S(2)}, u32[]{:S(2)}) collective-permute-start(bf16[2,512,512]{2,1,0:T(8,128)(2,1)S(1)} %collective-permute-done.refs_2_), channel_id=1, source_target_pairs={{0,1},{1,0},{2,3},{3,2},{4,5},{5,4},{6,7},{7,6},{8,9},{9,8},{10,11... | collective-permute-start | bytes 3145736 | tf_op jit(solution)/shard_map/ppermute | solution.py:294
  29.6 6.1 %collective-permute-start.4 = (bf16[2,512,512]{2,1,0:T(8,128)(2,1)S(1)}, bf16[2,512,512]{2,1,0:T(8,128)(2,1)S(1)}, u32[]{:S(2)}, u32[]{:S(2)}) collective-permute-start(bf16[2,512,512]{2,1,0:T(8,128)(2,1)S(1)} %collective-permute-done.1.refs_4_), channel_id=1, source_target_pairs={{0,1},{1,0},{2,3},{3,2},{4,5},{5,4},{6,7},{7,6},{8,9},{9,8},{10,11... | collective-permute-start | bytes 3145736 | tf_op jit(solution)/shard_map/ppermute | solution.py:294
  33.9 13.8 %collective-permute-start.7 = (bf16[264,1024]{1,0:T(8,128)(2,1)S(1)}, bf16[264,1024]{1,0:T(8,128)(2,1)S(1)}, u32[]{:S(2)}, u32[]{:S(2)}) collective-permute-start(bf16[264,1024]{1,0:T(8,128)(2,1)S(1)} %collective-permute-done.6.refs_8_), channel_id=1, source_target_pairs={{0,8},{1,9},{2,10},{3,11},{4,12},{5,13},{6,14},{7,15},{8,0},{9,1},... | collective-permute-start | bytes 1622024 | tf_op jit(solution)/shard_map/ppermute | solution.py:294
  34.6 16.1 %collective-permute-start.8 = (bf16[560,512]{1,0:T(8,128)(2,1)S(1)}, bf16[560,512]{1,0:T(8,128)(2,1)S(1)}, u32[]{:S(2)}, u32[]{:S(2)}) collective-permute-start(bf16[560,512]{1,0:T(8,128)(2,1)S(1)} %slice.12), channel_id=1, source_target_pairs={{0,4},{1,5},{2,6},{3,7},{4,0},{5,1},{6,2},{7,3},{8,12},{9,13},{10,... | collective-permute-start | bytes 1720328 | tf_op jit(solution)/shard_map/ppermute | solution.py:294
  35.2 15.5 %collective-permute-start.9 = (bf16[512,512]{1,0:T(8,128)(2,1)S(1)}, bf16[512,512]{1,0:T(8,128)(2,1)S(1)}, u32[]{:S(2)}, u32[]{:S(2)}) collective-permute-start(bf16[512,512]{1,0:T(8,128)(2,1)S(1)} %slice_bitcast_fusion), channel_id=1, source_target_pairs={{0,2},{1,3},{2,0},{3,1},{4,6},{5,7},{6,4},{7,5},{8,10},{9,11},{10,... | collective-permute-start | bytes 1572872 | tf_op jit(solution)/shard_map/ppermute | solution.py:294
  50.7 2.7 %collective-permute-start.10 = (bf16[1024,512]{1,0:T(8,128)(2,1)S(1)}, bf16[1024,512]{1,0:T(8,128)(2,1)S(1)}, u32[]{:S(2)}, u32[]{:S(2)}) collective-permute-start(bf16[1024,512]{1,0:T(8,128)(2,1)S(1)} %get-tuple-element.64), channel_id=1, source_target_pairs={{0,1},{1,0},{2,3},{3,2},{4,5},{5,4},{6,7},{7,6},{8,9},{9,8},{10,11... | collective-permute-start | bytes 3145736 | tf_op jit(solution)/shard_map/ppermute | solution.py:294
  50.9 4.8 %collective-permute-start.11 = (bf16[1536,512]{1,0:T(8,128)(2,1)S(1)}, bf16[1536,512]{1,0:T(8,128)(2,1)S(1)}, u32[]{:S(2)}, u32[]{:S(2)}) collective-permute-start(bf16[1536,512]{1,0:T(8,128)(2,1)S(1)} %pad_maximum_fusion), channel_id=1, source_target_pairs={{0,1},{1,0},{2,3},{3,2},{4,5},{5,4},{6,7},{7,6},{8,9},{9,8},{10,11... | collective-permute-start | bytes 4718600 | tf_op jit(solution)/shard_map/ppermute | solution.py:294
  53.7 16.3 %collective-permute-start.17 = (bf16[528,512]{1,0:T(8,128)(2,1)S(1)}, bf16[528,512]{1,0:T(8,128)(2,1)S(1)}, u32[]{:S(2)}, u32[]{:S(2)}) collective-permute-start(bf16[528,512]{1,0:T(8,128)(2,1)S(1)} %get-tuple-element.65), channel_id=1, source_target_pairs={{0,2},{1,3},{2,0},{3,1},{4,6},{5,7},{6,4},{7,5},{8,10},{9,11},{10,... | collective-permute-start | bytes 1622024 | tf_op jit(solution)/shard_map/ppermute | solution.py:294
  54.3 25.3 %collective-permute-start.18 = (bf16[528,512]{1,0:T(8,128)(2,1)S(1)}, bf16[528,512]{1,0:T(8,128)(2,1)S(1)}, u32[]{:S(2)}, u32[]{:S(2)}) collective-permute-start(bf16[528,512]{1,0:T(8,128)(2,1)S(1)} %get-tuple-element.81), channel_id=1, source_target_pairs={{0,4},{1,5},{2,6},{3,7},{4,0},{5,1},{6,2},{7,3},{8,12},{9,13},{10,... | collective-permute-start | bytes 1622024 | tf_op jit(solution)/shard_map/ppermute | solution.py:294
  59.0 2.3 %collective-permute-start.12 = (bf16[512,512]{1,0:T(8,128)(2,1)S(1)}, bf16[512,512]{1,0:T(8,128)(2,1)S(1)}, u32[]{:S(2)}, u32[]{:S(2)}) collective-permute-start(bf16[512,512]{1,0:T(8,128)(2,1)S(1)} %get-tuple-element.73), channel_id=1, source_target_pairs={{0,1},{1,0},{2,3},{3,2},{4,5},{5,4},{6,7},{7,6},{8,9},{9,8},{10,11... | collective-permute-start | bytes 1572872 | tf_op jit(solution)/shard_map/ppermute | solution.py:294
  59.2 6.3 %collective-permute-start.15 = (bf16[64,1024]{1,0:T(8,128)(2,1)S(1)}, bf16[64,1024]{1,0:T(8,128)(2,1)S(1)}, u32[]{:S(2)}, u32[]{:S(2)}) collective-permute-start(bf16[64,1024]{1,0:T(8,128)(2,1)S(1)} %get-tuple-element.79), channel_id=1, source_target_pairs={{0,8},{1,9},{2,10},{3,11},{4,12},{5,13},{6,14},{7,15},{8,0},{9,1},... | collective-permute-start | bytes 393224 | tf_op jit(solution)/shard_map/ppermute | solution.py:294
  60.2 8.1 %collective-permute-start.13 = (bf16[64,1024]{1,0:T(8,128)(2,1)S(1)}, bf16[64,1024]{1,0:T(8,128)(2,1)S(1)}, u32[]{:S(2)}, u32[]{:S(2)}) collective-permute-start(bf16[64,1024]{1,0:T(8,128)(2,1)S(1)} %get-tuple-element.76), channel_id=1, source_target_pairs={{0,8},{1,9},{2,10},{3,11},{4,12},{5,13},{6,14},{7,15},{8,0},{9,1},... | collective-permute-start | bytes 393224 | tf_op jit(solution)/shard_map/ppermute | solution.py:294
  61.5 18.3 %collective-permute-start.19 = (bf16[512,512]{1,0:T(8,128)(2,1)S(1)}, bf16[512,512]{1,0:T(8,128)(2,1)S(1)}, u32[]{:S(2)}, u32[]{:S(2)}) collective-permute-start(bf16[512,512]{1,0:T(8,128)(2,1)S(1)} %get-tuple-element.74), channel_id=1, source_target_pairs={{0,6},{1,7},{2,4},{3,5},{4,2},{5,3},{6,0},{7,1},{8,14},{9,15},{10,... | collective-permute-start | bytes 1572872 | tf_op jit(solution)/shard_map/ppermute | solution.py:294
  65.6 15.2 %collective-permute-start.16 = (bf16[64,1024]{1,0:T(8,128)(2,1)S(1)}, bf16[64,1024]{1,0:T(8,128)(2,1)S(1)}, u32[]{:S(2)}, u32[]{:S(2)}) collective-permute-start(bf16[64,1024]{1,0:T(8,128)(2,1)S(1)} %line_sum.3), channel_id=1, source_target_pairs={{0,16},{1,17},{2,18},{3,19},{4,20},{5,21},{6,22},{7,23},{8,24},{9,... | collective-permute-start | bytes 393224 | tf_op jit(solution)/shard_map/ppermute | solution.py:294
  68.3 12.5 %collective-permute-start.20 = (bf16[128,1024]{1,0:T(8,128)(2,1)S(1)}, bf16[128,1024]{1,0:T(8,128)(2,1)S(1)}, u32[]{:S(2)}, u32[]{:S(2)}) collective-permute-start(bf16[128,1024]{1,0:T(8,128)(2,1)S(1)} %get-tuple-element.85), channel_id=1, source_target_pairs={{0,8},{1,9},{2,10},{3,11},{4,12},{5,13},{6,14},{7,15},{8,0},{9,1},... | collective-permute-start | bytes 786440 | tf_op jit(solution)/shard_map/ppermute | solution.py:294
  70.1 10.7 %collective-permute-start.14 = (bf16[64,1024]{1,0:T(8,128)(2,1)S(1)}, bf16[64,1024]{1,0:T(8,128)(2,1)S(1)}, u32[]{:S(2)}, u32[]{:S(2)}) collective-permute-start(bf16[64,1024]{1,0:T(8,128)(2,1)S(1)} %line_sum.2), channel_id=1, source_target_pairs={{0,16},{1,17},{2,18},{3,19},{4,20},{5,21},{6,22},{7,23},{8,24},{9,... | collective-permute-start | bytes 393224 | tf_op jit(solution)/shard_map/ppermute | solution.py:294

commit v19 on v17

--- a/solution.py
+++ b/solution.py
@@ -276,6 +276,19 @@
         + x_ref[:rows, :].astype(jnp.float32)
         + y_ref[:rows, :].astype(jnp.float32)
     )
+
+
+def final_kernel(scale, plane_ref, diag_ref, own_ref, one_ref, *refs):
+    two_refs, mixed_ref, grad_ref = refs[:-2], refs[-2], refs[-1]
+    mixed_ref[...] = (plane_ref[...] + diag_ref[...].astype(jnp.float32)).astype(jnp.bfloat16)
+    part = two_refs[0].shape[0]
+    for at, ref in enumerate(two_refs):
+        spot = slice(at * part, (at + 1) * part)
+        grad_ref[spot, :] = scale * (
+            own_ref[spot, :].astype(jnp.float32)
+            + one_ref[spot, :].astype(jnp.float32)
+            + ref[...].astype(jnp.float32)
+        )
 
 
 def vmem(count):
@@ -481,15 +494,16 @@
         cost_estimate=cost(PLANE_COST, rows),
         name="plane_sum",
     )(mixed_own, mixed_x, mixed_y)
-    mixed = (mixed + mixed_diag.astype(jnp.float32)).astype(jnp.bfloat16)
-    *from_two, mixed = barrier((*from_two, mixed))
-    from_two = jnp.concatenate(from_two)
-    total = (
-        grad_own.astype(jnp.float32)
-        + from_one.astype(jnp.float32)
-        + from_two.astype(jnp.float32)
-    )
-    return (mixed, total * scale)
+    *from_two, from_one, mixed = barrier((*from_two, from_one, mixed))
+    return pl.pallas_call(
+        functools.partial(final_kernel, scale),
+        out_shape=(bf16(rows, feats), f32(owned, width)),
+        in_specs=vmem(4 + PARTS),
+        out_specs=(vmem(1)[0], vmem(1)[0]),
+        compiler_params=params,
+        cost_estimate=cost(rows, rows),
+        name="results",
+    )(mixed, mixed_diag, grad_own, from_one, *from_two)
 
 
 def solution(mesh):

time: 81.5 us -> 80.7 us (level)
  other arithmetic: 3.36 us -> 1.49 us
  Pallas kernels: 15.7 us -> 16.8 us
    pallas_call x0 -> x1, Pallas kernels: none -> 1.09 us  [on_device_lines(): pl.pallas_call(functools.partial(final_kernel, scale), out_shape=(bf16(ro...]
    convert_element_type x1 -> x0, other arithmetic: 0.95 us -> none  [on_device_lines(): mixed = (mixed + mixed_diag.astype(jnp.float32)).astype(jnp.bfloat16)]
    mul x1 -> x0, other arithmetic: 0.91 us -> none  [on_device_lines(): return (mixed, total * scale)]
  transfers between devices with their start and end apart: 21 -> 21, of which waited for: 8 -> 8; matrix products, arithmetic and copies ran while one was open for 1% -> 0% of each run, Pallas kernels for 19% -> 20%
where the time goes in v19:
time: 80.7 us; the launch traced here: 80.6 us
  waiting for transfers between devices  38 us (47%)
  starting transfers between devices  23.4 us (29%)
  Pallas kernels  16.8 us (21%)
  other arithmetic  1.49 us (2%)
  between operations  0.83 us (1%)
    ppermute x21, waiting for transfers between devices, permute(): return lax.ppermute(value, AXES, pairs)  38 us
    ppermute x21, starting transfers between devices, permute(): return lax.ppermute(value, AXES, pairs)  23.4 us
    pallas_call x1, Pallas kernels, on_device_lines(): pl.pallas_call(functools.partial(early_kernel, owned), out_shape=(bf16(ea...  7.43 us
    pallas_call x1, Pallas kernels, on_device_lines(): pl.pallas_call(functools.partial(diagonal_kernel, owned), out_shape=[bf16...  3.13 us
    pallas_call x1, Pallas kernels, on_device_lines(): pl.pallas_call(functools.partial(output_kernel, owned), out_shape=(bf16(e...  2.57 us
    pallas_call x1, Pallas kernels, on_device_lines(): pl.pallas_call(gradient_kernel, out_shape=f32(2 * owned, width), in_specs...  1.82 us
  transfers between devices with their start and end apart: 21, of which 8 were waited for; matrix products, arithmetic and copies ran while one was open for 0% of the time, Pallas kernels for 20%

profile of v19, /device:TPU:0, one launch (start us, length us, event | category | flops | bytes accessed | tf_op | source)
XLA Modules:
  0.0 80.6 jit_solution(14577638633236207145)
XLA Ops:
  0.7 1.4 %pad_maximum_fusion.1.refs_0_ = bf16[2,512,512]{2,1,0:T(8,128)(2,1)S(1)} fusion(bf16[1,512,512]{2,1,0:T(8,128)(2,1)} %bitcast.7, bf16[1,512,512]{2,1,0:T(8,128)(2,1)} %bitcast.8), kind=kLoop, calls=%fused_computation.3 | loop fusion | flops 524288 | bytes 2097152 | tf_op jit(solution)/shard_map/stack | solution.py:357
  2.0 3.0 %collective-permute-start = (bf16[2,512,512]{2,1,0:T(8,128)(2,1)S(1)}, bf16[2,512,512]{2,1,0:T(8,128)(2,1)S(1)}, u32[]{:S(2)}, u32[]{:S(2)}) collective-permute-start(bf16[2,512,512]{2,1,0:T(8,128)(2,1)S(1)} %pad_maximum_fusion.1.refs_0_), channel_id=1, source_target_pairs={{0,2},{1,3},{2,0},{3,1},{4,6},{5,7},{6,4},{7,5},{8,10},{9,11},{10,... | collective-permute-start | bytes 3145736 | tf_op jit(solution)/shard_map/ppermute | solution.py:315
  5.0 1.5 %collective-permute-start.1 = (bf16[2,512,512]{2,1,0:T(8,128)(2,1)S(1)}, bf16[2,512,512]{2,1,0:T(8,128)(2,1)S(1)}, u32[]{:S(2)}, u32[]{:S(2)}) collective-permute-start(bf16[2,512,512]{2,1,0:T(8,128)(2,1)S(1)} %pad_maximum_fusion.1.refs_0_), channel_id=1, source_target_pairs={{0,4},{1,5},{2,6},{3,7},{4,0},{5,1},{6,2},{7,3},{8,12},{9,13},{10,... | collective-permute-start | bytes 3145736 | tf_op jit(solution)/shard_map/ppermute | solution.py:315
  6.6 2.7 %collective-permute-start.6 = (bf16[264,1024]{1,0:T(8,128)(2,1)S(1)}, bf16[264,1024]{1,0:T(8,128)(2,1)S(1)}, u32[]{:S(2)}, u32[]{:S(2)}) collective-permute-start(bf16[264,1024]{1,0:T(8,128)(2,1)S(1)} %fusion.1.refs_6_), channel_id=1, source_target_pairs={{0,16},{1,17},{2,18},{3,19},{4,20},{5,21},{6,22},{7,23},{8,24},{9,... | collective-permute-start | bytes 1622024 | tf_op jit(solution)/shard_map/ppermute | solution.py:315
  9.3 1.6 %collective-permute-start.5 = (bf16[264,1024]{1,0:T(8,128)(2,1)S(1)}, bf16[264,1024]{1,0:T(8,128)(2,1)S(1)}, u32[]{:S(2)}, u32[]{:S(2)}) collective-permute-start(bf16[264,1024]{1,0:T(8,128)(2,1)S(1)} %fusion.1.refs_6_), channel_id=1, source_target_pairs={{0,8},{1,9},{2,10},{3,11},{4,12},{5,13},{6,14},{7,15},{8,0},{9,1},... | collective-permute-start | bytes 1622024 | tf_op jit(solution)/shard_map/ppermute | solution.py:315
  10.8 17.3 %collective-permute-done.refs_2_ = bf16[2,512,512]{2,1,0:T(8,128)(2,1)S(1)} collective-permute-done((bf16[2,512,512]{2,1,0:T(8,128)(2,1)S(1)}, bf16[2,512,512]{2,1,0:T(8,128)(2,1)S(1)}, u32[]{:S(2)}, u32[]{:S(2)}) %collective-permute-start) | collective-permute-done | bytes 1048608 | tf_op jit(solution)/shard_map/ppermute | solution.py:315
  28.2 1.5 %collective-permute-done.1.refs_4_ = bf16[2,512,512]{2,1,0:T(8,128)(2,1)S(1)} collective-permute-done((bf16[2,512,512]{2,1,0:T(8,128)(2,1)S(1)}, bf16[2,512,512]{2,1,0:T(8,128)(2,1)S(1)}, u32[]{:S(2)}, u32[]{:S(2)}) %collective-permute-start.1) | collective-permute-done | bytes 1048608 | tf_op jit(solution)/shard_map/ppermute | solution.py:315
  29.6 0.5 collective-permute-start.4
  30.2 3.8 %collective-permute-done.6.refs_8_ = bf16[264,1024]{1,0:T(8,128)(2,1)S(1)} collective-permute-done((bf16[264,1024]{1,0:T(8,128)(2,1)S(1)}, bf16[264,1024]{1,0:T(8,128)(2,1)S(1)}, u32[]{:S(2)}, u32[]{:S(2)}) %collective-permute-start.6) | collective-permute-done | bytes 540704 | tf_op jit(solution)/shard_map/ppermute | solution.py:315
  33.9 0.6 collective-permute-start.7
  34.6 0.6 collective-permute-start.8
  35.2 0.6 collective-permute-start.9
  35.8 7.4 %early.1 = (bf16[1536,128]{1,0:T(8,128)(2,1)S(1)}, bf16[1536,128]{1,0:T(8,128)(2,1)S(1)}, f32[1536,1024]{1,0:T(8,128)S(1)}, f32[256,1024]{1,0:T(8,128)S(1)}, bf1...) custom-call(bf16[2,512,512]{2,1,0:T(8,128)(2,1)S(1)} %pad_maximum_fu, ...), custom_call_target="tpu_custom_call" | custom-call | flops 786432 | bytes 1536 | tf_op jit(solution)/shard_map/early/pallas_call | solution.py:367
  43.2 4.5 %collective-permute-done.7.refs_6_.w_three = bf16[264,1024]{1,0:T(8,128)(2,1)S(1)} collective-permute-done((bf16[264,1024]{1,0:T(8,128)(2,1)S(1)}, bf16[264,1024]{1,0:T(8,128)(2,1)S(1)}, u32[]{:S(2)}, u32[]{:S(2)}) %collective-permute-start.7) | collective-permute-done | bytes 540704 | tf_op jit(solution)/shard_map/ppermute | solution.py:315
  47.8 2.6 %output.1 = (bf16[1536,512]{1,0:T(8,128)(2,1)S(1)}, bf16[1024,512]{1,0:T(8,128)(2,1)S(1)}, bf16[512,512]{1,0:T(8,128)(2,1)S(1)}, f32[1536,128]{1,0:T(8,128)S(1)}...) custom-call(bf16[1536,128]{1,0:T(8,128)(2,1)S(1)} %get-tuple-element.51.refs_0_, ...), custom_call_target="tpu_custom_call" | custom-call | flops 786432 | bytes 1536 | tf_op jit(solution)/shard_map/output/pallas_call | solution.py:394
  50.6 0.6 collective-permute-start.11
  51.2 1.8 %gradient.1.refs_4_ = f32[256,1024]{1,0:T(8,128)S(1)} custom-call(bf16[1536,128]{1,0:T(8,128)(2,1)S(1)} %get-tuple-element.62.dpre_two, bf16[1536,1024]{1,0:T(8,128)(2,1)S(1)} %get-tuple-element.52.refs_1_.tok, bf16[1536,1024]{1,0:T(8,128)(2,1)S(1)} %get-tuple-element.63.cot, f32[1536,128]{1,0:T(8,128)S(1)} %get-tuple-element.67.slope, ...), custom_call_target="tpu_custom_call" | custom-call | flops 10000000000 | bytes 1536 | tf_op jit(solution)/shard_map/gradient/pallas_call | solution.py:416
  53.1 0.3 pair_sum.1
  53.4 0.6 collective-permute-start.18
  54.0 0.7 collective-permute-start.19
  54.7 0.7 collective-permute-done.11.refs_7_.far_ref
  55.4 3.1 %diagonal.1 = (bf16[512,512]{1,0:T(8,128)(2,1)S(1)}, bf16[512,512]{1,0:T(8,128)(2,1)S(1)}, bf16[128,1024]{1,0:T(8,128)(2,1)S(1)}, bf16[128,1024]{1,0:T(8,128)(2,...) custom-call(bf16[512,1024]{1,0:T(8,128)(2,1)S(1)} %get-tuple-element, ...), custom_call_target="tpu_custom_call" | custom-call | flops 1000000 | bytes 512 | tf_op jit(solution)/shard_map/diagonal/pallas_call | solution.py:440
  58.7 1.0 %collective-permute-start.15 = (bf16[64,1024]{1,0:T(8,128)(2,1)S(1)}, bf16[64,1024]{1,0:T(8,128)(2,1)S(1)}, u32[]{:S(2)}, u32[]{:S(2)}) collective-permute-start(bf16[64,1024]{1,0:T(8,128)(2,1)S(1)} %get-tuple-element.84), channel_id=1, source_target_pairs={{0,8},{1,9},{2,10},{3,11},{4,12},{5,13},{6,14},{7,15},{8,0},{9,1},... | collective-permute-start | bytes 393224 | tf_op jit(solution)/shard_map/ppermute | solution.py:315
  59.7 1.0 %collective-permute-start.13 = (bf16[64,1024]{1,0:T(8,128)(2,1)S(1)}, bf16[64,1024]{1,0:T(8,128)(2,1)S(1)}, u32[]{:S(2)}, u32[]{:S(2)}) collective-permute-start(bf16[64,1024]{1,0:T(8,128)(2,1)S(1)} %get-tuple-element.81), channel_id=1, source_target_pairs={{0,8},{1,9},{2,10},{3,11},{4,12},{5,13},{6,14},{7,15},{8,0},{9,1},... | collective-permute-start | bytes 393224 | tf_op jit(solution)/shard_map/ppermute | solution.py:315
  60.8 0.3 pair_sum_diagonal.1
  61.0 1.6 %collective-permute-start.20 = (bf16[512,512]{1,0:T(8,128)(2,1)S(1)}, bf16[512,512]{1,0:T(8,128)(2,1)S(1)}, u32[]{:S(2)}, u32[]{:S(2)}) collective-permute-start(bf16[512,512]{1,0:T(8,128)(2,1)S(1)} %get-tuple-element.79), channel_id=1, source_target_pairs={{0,6},{1,7},{2,4},{3,5},{4,2},{5,3},{6,0},{7,1},{8,14},{9,15},{10,... | collective-permute-start | bytes 1572872 | tf_op jit(solution)/shard_map/ppermute | solution.py:315
  62.6 2.4 %collective-permute-done.15.other_ref = bf16[64,1024]{1,0:T(8,128)(2,1)S(1)} collective-permute-done((bf16[64,1024]{1,0:T(8,128)(2,1)S(1)}, bf16[64,1024]{1,0:T(8,128)(2,1)S(1)}, u32[]{:S(2)}, u32[]{:S(2)}) %collective-permute-start.15) | collective-permute-done | bytes 131104 | tf_op jit(solution)/shard_map/ppermute | solution.py:315
  65.1 2.7 %collective-permute-start.16 = (bf16[64,1024]{1,0:T(8,128)(2,1)S(1)}, bf16[64,1024]{1,0:T(8,128)(2,1)S(1)}, u32[]{:S(2)}, u32[]{:S(2)}) collective-permute-start(bf16[64,1024]{1,0:T(8,128)(2,1)S(1)} %line_sum.3), channel_id=1, source_target_pairs={{0,16},{1,17},{2,18},{3,19},{4,20},{5,21},{6,22},{7,23},{8,24},{9,... | collective-permute-start | bytes 393224 | tf_op jit(solution)/shard_map/ppermute | solution.py:315
  67.8 1.8 %collective-permute-start.17 = (bf16[128,1024]{1,0:T(8,128)(2,1)S(1)}, bf16[128,1024]{1,0:T(8,128)(2,1)S(1)}, u32[]{:S(2)}, u32[]{:S(2)}) collective-permute-start(bf16[128,1024]{1,0:T(8,128)(2,1)S(1)} %get-tuple-element.86), channel_id=1, source_target_pairs={{0,8},{1,9},{2,10},{3,11},{4,12},{5,13},{6,14},{7,15},{8,0},{9,1},... | collective-permute-start | bytes 786440 | tf_op jit(solution)/shard_map/ppermute | solution.py:315
  69.6 2.2 %collective-permute-start.14 = (bf16[64,1024]{1,0:T(8,128)(2,1)S(1)}, bf16[64,1024]{1,0:T(8,128)(2,1)S(1)}, u32[]{:S(2)}, u32[]{:S(2)}) collective-permute-start(bf16[64,1024]{1,0:T(8,128)(2,1)S(1)} %line_sum.2), channel_id=1, source_target_pairs={{0,16},{1,17},{2,18},{3,19},{4,20},{5,21},{6,22},{7,23},{8,24},{9,... | collective-permute-start | bytes 393224 | tf_op jit(solution)/shard_map/ppermute | solution.py:315
  71.8 7.5 %collective-permute-done.19.y_ref = bf16[528,512]{1,0:T(8,128)(2,1)S(1)} collective-permute-done((bf16[528,512]{1,0:T(8,128)(2,1)S(1)}, bf16[528,512]{1,0:T(8,128)(2,1)S(1)}, u32[]{:S(2)}, u32[]{:S(2)}) %collective-permute-start.19) | collective-permute-done | bytes 540704 | tf_op jit(solution)/shard_map/ppermute | solution.py:315
  79.5 1.1 %results.1 = (bf16[512,512]{1,0:T(8,128)(2,1)}, f32[128,1024]{1,0:T(8,128)}) custom-call(f32[512,512]{1,0:T(8,128)S(1)} %plane_sum.1.plane_ref, bf16[512,512]{1,0:T(8,128)(2,1)S(1)} %collective-permute-done.20.diag_ref, bf16[128,1024]{1,0:T(8,128)(2,1)S(1)} %get-tuple-element.90.own_ref, bf16[128,1024]{1,0:T(8,128)(2,1)S(1)} %collective-permute-done.17.one_ref, ...), custom_call_target="tpu_custom_call" | custom-call | flops 512 | bytes 512 | tf_op jit(solution)/shard_map/results/pallas_call | solution.py:498
  (32 shorter events, 1.0 us)
Async XLA Ops:
  0.6 5.9 %copy-start.2 = (bf16[128]{0:T(256)(128)(2,1)S(1)}, bf16[128]{0:T(256)(128)(2,1)}, u32[]{:S(2)}) copy-start(bf16[128]{0:T(256)(128)(2,1)} %param.8) | copy-start | bytes 772
  0.6 5.9 %copy-start.1 = (bf16[128,1024]{1,0:T(8,128)(2,1)S(1)}, bf16[128,1024]{1,0:T(8,128)(2,1)}, u32[]{:S(2)}) copy-start(bf16[128,1024]{1,0:T(8,128)(2,1)} %param.7) | copy-start | bytes 786436
  0.7 5.9 %copy-start = (bf16[128,1024]{1,0:T(8,128)(2,1)S(1)}, bf16[128,1024]{1,0:T(8,128)(2,1)}, u32[]{:S(2)}) copy-start(bf16[128,1024]{1,0:T(8,128)(2,1)} %param.9) | copy-start | bytes 786436
  2.0 26.2 %collective-permute-start = (bf16[2,512,512]{2,1,0:T(8,128)(2,1)S(1)}, bf16[2,512,512]{2,1,0:T(8,128)(2,1)S(1)}, u32[]{:S(2)}, u32[]{:S(2)}) collective-permute-start(bf16[2,512,512]{2,1,0:T(8,128)(2,1)S(1)} %pad_maximum_fusion.1.refs_0_), channel_id=1, source_target_pairs={{0,2},{1,3},{2,0},{3,1},{4,6},{5,7},{6,4},{7,5},{8,10},{9,11},{10,... | collective-permute-start | bytes 3145736 | tf_op jit(solution)/shard_map/ppermute | solution.py:315
  5.0 24.6 %collective-permute-start.1 = (bf16[2,512,512]{2,1,0:T(8,128)(2,1)S(1)}, bf16[2,512,512]{2,1,0:T(8,128)(2,1)S(1)}, u32[]{:S(2)}, u32[]{:S(2)}) collective-permute-start(bf16[2,512,512]{2,1,0:T(8,128)(2,1)S(1)} %pad_maximum_fusion.1.refs_0_), channel_id=1, source_target_pairs={{0,4},{1,5},{2,6},{3,7},{4,0},{5,1},{6,2},{7,3},{8,12},{9,13},{10,... | collective-permute-start | bytes 3145736 | tf_op jit(solution)/shard_map/ppermute | solution.py:315
  6.5 23.1 %collective-permute-start.2 = (bf16[2,512,512]{2,1,0:T(8,128)(2,1)S(1)}, bf16[2,512,512]{2,1,0:T(8,128)(2,1)S(1)}, u32[]{:S(2)}, u32[]{:S(2)}) collective-permute-start(bf16[2,512,512]{2,1,0:T(8,128)(2,1)S(1)} %pad_maximum_fusion.1.refs_0_), channel_id=1, source_target_pairs={{0,1},{1,0},{2,3},{3,2},{4,5},{5,4},{6,7},{7,6},{8,9},{9,8},{10,11... | collective-permute-start | bytes 3145736 | tf_op jit(solution)/shard_map/ppermute | solution.py:315
  6.6 27.3 %collective-permute-start.6 = (bf16[264,1024]{1,0:T(8,128)(2,1)S(1)}, bf16[264,1024]{1,0:T(8,128)(2,1)S(1)}, u32[]{:S(2)}, u32[]{:S(2)}) collective-permute-start(bf16[264,1024]{1,0:T(8,128)(2,1)S(1)} %fusion.1.refs_6_), channel_id=1, source_target_pairs={{0,16},{1,17},{2,18},{3,19},{4,20},{5,21},{6,22},{7,23},{8,24},{9,... | collective-permute-start | bytes 1622024 | tf_op jit(solution)/shard_map/ppermute | solution.py:315
  9.3 25.9 %collective-permute-start.5 = (bf16[264,1024]{1,0:T(8,128)(2,1)S(1)}, bf16[264,1024]{1,0:T(8,128)(2,1)S(1)}, u32[]{:S(2)}, u32[]{:S(2)}) collective-permute-start(bf16[264,1024]{1,0:T(8,128)(2,1)S(1)} %fusion.1.refs_6_), channel_id=1, source_target_pairs={{0,8},{1,9},{2,10},{3,11},{4,12},{5,13},{6,14},{7,15},{8,0},{9,1},... | collective-permute-start | bytes 1622024 | tf_op jit(solution)/shard_map/ppermute | solution.py:315
  29.6 6.1 %collective-permute-start.3 = (bf16[2,512,512]{2,1,0:T(8,128)(2,1)S(1)}, bf16[2,512,512]{2,1,0:T(8,128)(2,1)S(1)}, u32[]{:S(2)}, u32[]{:S(2)}) collective-permute-start(bf16[2,512,512]{2,1,0:T(8,128)(2,1)S(1)} %collective-permute-done.refs_2_), channel_id=1, source_target_pairs={{0,1},{1,0},{2,3},{3,2},{4,5},{5,4},{6,7},{7,6},{8,9},{9,8},{10,11... | collective-permute-start | bytes 3145736 | tf_op jit(solution)/shard_map/ppermute | solution.py:315
  29.6 6.1 %collective-permute-start.4 = (bf16[2,512,512]{2,1,0:T(8,128)(2,1)S(1)}, bf16[2,512,512]{2,1,0:T(8,128)(2,1)S(1)}, u32[]{:S(2)}, u32[]{:S(2)}) collective-permute-start(bf16[2,512,512]{2,1,0:T(8,128)(2,1)S(1)} %collective-permute-done.1.refs_4_), channel_id=1, source_target_pairs={{0,1},{1,0},{2,3},{3,2},{4,5},{5,4},{6,7},{7,6},{8,9},{9,8},{10,11... | collective-permute-start | bytes 3145736 | tf_op jit(solution)/shard_map/ppermute | solution.py:315
  33.9 13.8 %collective-permute-start.7 = (bf16[264,1024]{1,0:T(8,128)(2,1)S(1)}, bf16[264,1024]{1,0:T(8,128)(2,1)S(1)}, u32[]{:S(2)}, u32[]{:S(2)}) collective-permute-start(bf16[264,1024]{1,0:T(8,128)(2,1)S(1)} %collective-permute-done.6.refs_8_), channel_id=1, source_target_pairs={{0,8},{1,9},{2,10},{3,11},{4,12},{5,13},{6,14},{7,15},{8,0},{9,1},... | collective-permute-start | bytes 1622024 | tf_op jit(solution)/shard_map/ppermute | solution.py:315
  34.6 15.8 %collective-permute-start.8 = (bf16[560,512]{1,0:T(8,128)(2,1)S(1)}, bf16[560,512]{1,0:T(8,128)(2,1)S(1)}, u32[]{:S(2)}, u32[]{:S(2)}) collective-permute-start(bf16[560,512]{1,0:T(8,128)(2,1)S(1)} %slice.12), channel_id=1, source_target_pairs={{0,4},{1,5},{2,6},{3,7},{4,0},{5,1},{6,2},{7,3},{8,12},{9,13},{10,... | collective-permute-start | bytes 1720328 | tf_op jit(solution)/shard_map/ppermute | solution.py:315
  35.2 15.2 %collective-permute-start.9 = (bf16[512,512]{1,0:T(8,128)(2,1)S(1)}, bf16[512,512]{1,0:T(8,128)(2,1)S(1)}, u32[]{:S(2)}, u32[]{:S(2)}) collective-permute-start(bf16[512,512]{1,0:T(8,128)(2,1)S(1)} %slice_bitcast_fusion), channel_id=1, source_target_pairs={{0,2},{1,3},{2,0},{3,1},{4,6},{5,7},{6,4},{7,5},{8,10},{9,11},{10,... | collective-permute-start | bytes 1572872 | tf_op jit(solution)/shard_map/ppermute | solution.py:315
  50.4 2.7 %collective-permute-start.10 = (bf16[1024,512]{1,0:T(8,128)(2,1)S(1)}, bf16[1024,512]{1,0:T(8,128)(2,1)S(1)}, u32[]{:S(2)}, u32[]{:S(2)}) collective-permute-start(bf16[1024,512]{1,0:T(8,128)(2,1)S(1)} %get-tuple-element.69), channel_id=1, source_target_pairs={{0,1},{1,0},{2,3},{3,2},{4,5},{5,4},{6,7},{7,6},{8,9},{9,8},{10,11... | collective-permute-start | bytes 3145736 | tf_op jit(solution)/shard_map/ppermute | solution.py:315
  50.6 4.8 %collective-permute-start.11 = (bf16[1536,512]{1,0:T(8,128)(2,1)S(1)}, bf16[1536,512]{1,0:T(8,128)(2,1)S(1)}, u32[]{:S(2)}, u32[]{:S(2)}) collective-permute-start(bf16[1536,512]{1,0:T(8,128)(2,1)S(1)} %pad_maximum_fusion), channel_id=1, source_target_pairs={{0,1},{1,0},{2,3},{3,2},{4,5},{5,4},{6,7},{7,6},{8,9},{9,8},{10,11... | collective-permute-start | bytes 4718600 | tf_op jit(solution)/shard_map/ppermute | solution.py:315
  53.4 16.2 %collective-permute-start.18 = (bf16[528,512]{1,0:T(8,128)(2,1)S(1)}, bf16[528,512]{1,0:T(8,128)(2,1)S(1)}, u32[]{:S(2)}, u32[]{:S(2)}) collective-permute-start(bf16[528,512]{1,0:T(8,128)(2,1)S(1)} %get-tuple-element.70), channel_id=1, source_target_pairs={{0,2},{1,3},{2,0},{3,1},{4,6},{5,7},{6,4},{7,5},{8,10},{9,11},{10,... | collective-permute-start | bytes 1622024 | tf_op jit(solution)/shard_map/ppermute | solution.py:315
  54.0 25.3 %collective-permute-start.19 = (bf16[528,512]{1,0:T(8,128)(2,1)S(1)}, bf16[528,512]{1,0:T(8,128)(2,1)S(1)}, u32[]{:S(2)}, u32[]{:S(2)}) collective-permute-start(bf16[528,512]{1,0:T(8,128)(2,1)S(1)} %get-tuple-element.88), channel_id=1, source_target_pairs={{0,4},{1,5},{2,6},{3,7},{4,0},{5,1},{6,2},{7,3},{8,12},{9,13},{10,... | collective-permute-start | bytes 1622024 | tf_op jit(solution)/shard_map/ppermute | solution.py:315
  58.5 2.2 %collective-permute-start.12 = (bf16[512,512]{1,0:T(8,128)(2,1)S(1)}, bf16[512,512]{1,0:T(8,128)(2,1)S(1)}, u32[]{:S(2)}, u32[]{:S(2)}) collective-permute-start(bf16[512,512]{1,0:T(8,128)(2,1)S(1)} %get-tuple-element.78), channel_id=1, source_target_pairs={{0,1},{1,0},{2,3},{3,2},{4,5},{5,4},{6,7},{7,6},{8,9},{9,8},{10,11... | collective-permute-start | bytes 1572872 | tf_op jit(solution)/shard_map/ppermute | solution.py:315
  58.7 6.3 %collective-permute-start.15 = (bf16[64,1024]{1,0:T(8,128)(2,1)S(1)}, bf16[64,1024]{1,0:T(8,128)(2,1)S(1)}, u32[]{:S(2)}, u32[]{:S(2)}) collective-permute-start(bf16[64,1024]{1,0:T(8,128)(2,1)S(1)} %get-tuple-element.84), channel_id=1, source_target_pairs={{0,8},{1,9},{2,10},{3,11},{4,12},{5,13},{6,14},{7,15},{8,0},{9,1},... | collective-permute-start | bytes 393224 | tf_op jit(solution)/shard_map/ppermute | solution.py:315
  59.7 8.0 %collective-permute-start.13 = (bf16[64,1024]{1,0:T(8,128)(2,1)S(1)}, bf16[64,1024]{1,0:T(8,128)(2,1)S(1)}, u32[]{:S(2)}, u32[]{:S(2)}) collective-permute-start(bf16[64,1024]{1,0:T(8,128)(2,1)S(1)} %get-tuple-element.81), channel_id=1, source_target_pairs={{0,8},{1,9},{2,10},{3,11},{4,12},{5,13},{6,14},{7,15},{8,0},{9,1},... | collective-permute-start | bytes 393224 | tf_op jit(solution)/shard_map/ppermute | solution.py:315
  61.0 18.5 %collective-permute-start.20 = (bf16[512,512]{1,0:T(8,128)(2,1)S(1)}, bf16[512,512]{1,0:T(8,128)(2,1)S(1)}, u32[]{:S(2)}, u32[]{:S(2)}) collective-permute-start(bf16[512,512]{1,0:T(8,128)(2,1)S(1)} %get-tuple-element.79), channel_id=1, source_target_pairs={{0,6},{1,7},{2,4},{3,5},{4,2},{5,3},{6,0},{7,1},{8,14},{9,15},{10,... | collective-permute-start | bytes 1572872 | tf_op jit(solution)/shard_map/ppermute | solution.py:315
  65.1 14.4 %collective-permute-start.16 = (bf16[64,1024]{1,0:T(8,128)(2,1)S(1)}, bf16[64,1024]{1,0:T(8,128)(2,1)S(1)}, u32[]{:S(2)}, u32[]{:S(2)}) collective-permute-start(bf16[64,1024]{1,0:T(8,128)(2,1)S(1)} %line_sum.3), channel_id=1, source_target_pairs={{0,16},{1,17},{2,18},{3,19},{4,20},{5,21},{6,22},{7,23},{8,24},{9,... | collective-permute-start | bytes 393224 | tf_op jit(solution)/shard_map/ppermute | solution.py:315
  67.8 11.7 %collective-permute-start.17 = (bf16[128,1024]{1,0:T(8,128)(2,1)S(1)}, bf16[128,1024]{1,0:T(8,128)(2,1)S(1)}, u32[]{:S(2)}, u32[]{:S(2)}) collective-permute-start(bf16[128,1024]{1,0:T(8,128)(2,1)S(1)} %get-tuple-element.86), channel_id=1, source_target_pairs={{0,8},{1,9},{2,10},{3,11},{4,12},{5,13},{6,14},{7,15},{8,0},{9,1},... | collective-permute-start | bytes 786440 | tf_op jit(solution)/shard_map/ppermute | solution.py:315
  69.6 9.9 %collective-permute-start.14 = (bf16[64,1024]{1,0:T(8,128)(2,1)S(1)}, bf16[64,1024]{1,0:T(8,128)(2,1)S(1)}, u32[]{:S(2)}, u32[]{:S(2)}) collective-permute-start(bf16[64,1024]{1,0:T(8,128)(2,1)S(1)} %line_sum.2), channel_id=1, source_target_pairs={{0,16},{1,17},{2,18},{3,19},{4,20},{5,21},{6,22},{7,23},{8,24},{9,... | collective-permute-start | bytes 393224 | tf_op jit(solution)/shard_map/ppermute | solution.py:315

commit v20 on v19

--- a/solution.py
+++ b/solution.py
@@ -427,7 +427,7 @@
     mine, grad_last = barrier((mine, grad_last))
     sums = pl.pallas_call(
         functools.partial(pair_kernel, rows, 1),
-        out_shape=[bf16(rows + MORE, feats)] * 2,
+        out_shape=[bf16(rows + MORE, feats), bf16(rows + 2 * MORE, feats)],
         in_specs=vmem(2),
         out_specs=vmem(2),
         compiler_params=params,

time: 80.7 us -> 81.5 us (level)
  transfers between devices with their start and end apart: 21 -> 21, of which waited for: 8 -> 11; matrix products, arithmetic and copies ran while one was open for 0% -> 0% of each run, Pallas kernels for 20% -> 19%
where the time goes in v20:
time: 81.5 us; the launch traced here: 81.3 us
  waiting for transfers between devices  38.7 us (47%)
  starting transfers between devices  23.4 us (29%)
  Pallas kernels  16.8 us (21%)
  other arithmetic  1.49 us (2%)
    ppermute x21, waiting for transfers between devices, permute(): return lax.ppermute(value, AXES, pairs)  38.7 us
    ppermute x21, starting transfers between devices, permute(): return lax.ppermute(value, AXES, pairs)  23.4 us
    pallas_call x1, Pallas kernels, on_device_lines(): pl.pallas_call(functools.partial(early_kernel, owned), out_shape=(bf16(ea...  7.43 us
    pallas_call x1, Pallas kernels, on_device_lines(): pl.pallas_call(functools.partial(diagonal_kernel, owned), out_shape=[bf16...  3.13 us
    pallas_call x1, Pallas kernels, on_device_lines(): pl.pallas_call(functools.partial(output_kernel, owned), out_shape=(bf16(e...  2.57 us
    pallas_call x1, Pallas kernels, on_device_lines(): pl.pallas_call(gradient_kernel, out_shape=f32(2 * owned, width), in_specs...  1.82 us
  transfers between devices with their start and end apart: 21, of which 11 were waited for; matrix products, arithmetic and copies ran while one was open for 0% of the time, Pallas kernels for 19%

profile of v20, /device:TPU:0, one launch (start us, length us, event | category | flops | bytes accessed | tf_op | source)
XLA Modules:
  0.0 81.3 jit_solution(13866635706546606444)
XLA Ops:
  0.7 1.4 %pad_maximum_fusion.1.refs_0_ = bf16[2,512,512]{2,1,0:T(8,128)(2,1)S(1)} fusion(bf16[1,512,512]{2,1,0:T(8,128)(2,1)} %bitcast.7, bf16[1,512,512]{2,1,0:T(8,128)(2,1)} %bitcast.8), kind=kLoop, calls=%fused_computation.3 | loop fusion | flops 524288 | bytes 2097152 | tf_op jit(solution)/shard_map/stack | solution.py:357
  2.0 3.0 %collective-permute-start = (bf16[2,512,512]{2,1,0:T(8,128)(2,1)S(1)}, bf16[2,512,512]{2,1,0:T(8,128)(2,1)S(1)}, u32[]{:S(2)}, u32[]{:S(2)}) collective-permute-start(bf16[2,512,512]{2,1,0:T(8,128)(2,1)S(1)} %pad_maximum_fusion.1.refs_0_), channel_id=1, source_target_pairs={{0,2},{1,3},{2,0},{3,1},{4,6},{5,7},{6,4},{7,5},{8,10},{9,11},{10,... | collective-permute-start | bytes 3145736 | tf_op jit(solution)/shard_map/ppermute | solution.py:315
  5.0 1.5 %collective-permute-start.1 = (bf16[2,512,512]{2,1,0:T(8,128)(2,1)S(1)}, bf16[2,512,512]{2,1,0:T(8,128)(2,1)S(1)}, u32[]{:S(2)}, u32[]{:S(2)}) collective-permute-start(bf16[2,512,512]{2,1,0:T(8,128)(2,1)S(1)} %pad_maximum_fusion.1.refs_0_), channel_id=1, source_target_pairs={{0,4},{1,5},{2,6},{3,7},{4,0},{5,1},{6,2},{7,3},{8,12},{9,13},{10,... | collective-permute-start | bytes 3145736 | tf_op jit(solution)/shard_map/ppermute | solution.py:315
  6.6 2.7 %collective-permute-start.6 = (bf16[264,1024]{1,0:T(8,128)(2,1)S(1)}, bf16[264,1024]{1,0:T(8,128)(2,1)S(1)}, u32[]{:S(2)}, u32[]{:S(2)}) collective-permute-start(bf16[264,1024]{1,0:T(8,128)(2,1)S(1)} %fusion.1.refs_6_), channel_id=1, source_target_pairs={{0,16},{1,17},{2,18},{3,19},{4,20},{5,21},{6,22},{7,23},{8,24},{9,... | collective-permute-start | bytes 1622024 | tf_op jit(solution)/shard_map/ppermute | solution.py:315
  9.3 1.6 %collective-permute-start.5 = (bf16[264,1024]{1,0:T(8,128)(2,1)S(1)}, bf16[264,1024]{1,0:T(8,128)(2,1)S(1)}, u32[]{:S(2)}, u32[]{:S(2)}) collective-permute-start(bf16[264,1024]{1,0:T(8,128)(2,1)S(1)} %fusion.1.refs_6_), channel_id=1, source_target_pairs={{0,8},{1,9},{2,10},{3,11},{4,12},{5,13},{6,14},{7,15},{8,0},{9,1},... | collective-permute-start | bytes 1622024 | tf_op jit(solution)/shard_map/ppermute | solution.py:315
  10.8 17.3 %collective-permute-done.refs_2_ = bf16[2,512,512]{2,1,0:T(8,128)(2,1)S(1)} collective-permute-done((bf16[2,512,512]{2,1,0:T(8,128)(2,1)S(1)}, bf16[2,512,512]{2,1,0:T(8,128)(2,1)S(1)}, u32[]{:S(2)}, u32[]{:S(2)}) %collective-permute-start) | collective-permute-done | bytes 1048608 | tf_op jit(solution)/shard_map/ppermute | solution.py:315
  28.2 1.5 %collective-permute-done.1.refs_4_ = bf16[2,512,512]{2,1,0:T(8,128)(2,1)S(1)} collective-permute-done((bf16[2,512,512]{2,1,0:T(8,128)(2,1)S(1)}, bf16[2,512,512]{2,1,0:T(8,128)(2,1)S(1)}, u32[]{:S(2)}, u32[]{:S(2)}) %collective-permute-start.1) | collective-permute-done | bytes 1048608 | tf_op jit(solution)/shard_map/ppermute | solution.py:315
  30.2 3.8 %collective-permute-done.6.refs_8_ = bf16[264,1024]{1,0:T(8,128)(2,1)S(1)} collective-permute-done((bf16[264,1024]{1,0:T(8,128)(2,1)S(1)}, bf16[264,1024]{1,0:T(8,128)(2,1)S(1)}, u32[]{:S(2)}, u32[]{:S(2)}) %collective-permute-start.6) | collective-permute-done | bytes 540704 | tf_op jit(solution)/shard_map/ppermute | solution.py:315
  33.9 0.6 collective-permute-start.7
  34.6 0.6 collective-permute-start.8
  35.2 0.6 collective-permute-start.9
  35.8 7.4 %early.1 = (bf16[1536,128]{1,0:T(8,128)(2,1)S(1)}, bf16[1536,128]{1,0:T(8,128)(2,1)S(1)}, f32[1536,1024]{1,0:T(8,128)S(1)}, f32[256,1024]{1,0:T(8,128)S(1)}, bf1...) custom-call(bf16[2,512,512]{2,1,0:T(8,128)(2,1)S(1)} %pad_maximum_fu, ...), custom_call_target="tpu_custom_call" | custom-call | flops 786432 | bytes 1536 | tf_op jit(solution)/shard_map/early/pallas_call | solution.py:367
  43.2 4.5 %collective-permute-done.7.refs_6_.w_three = bf16[264,1024]{1,0:T(8,128)(2,1)S(1)} collective-permute-done((bf16[264,1024]{1,0:T(8,128)(2,1)S(1)}, bf16[264,1024]{1,0:T(8,128)(2,1)S(1)}, u32[]{:S(2)}, u32[]{:S(2)}) %collective-permute-start.7) | collective-permute-done | bytes 540704 | tf_op jit(solution)/shard_map/ppermute | solution.py:315
  47.8 2.6 %output.1 = (bf16[1536,512]{1,0:T(8,128)(2,1)S(1)}, bf16[1024,512]{1,0:T(8,128)(2,1)S(1)}, bf16[512,512]{1,0:T(8,128)(2,1)S(1)}, f32[1536,128]{1,0:T(8,128)S(1)}...) custom-call(bf16[1536,128]{1,0:T(8,128)(2,1)S(1)} %get-tuple-element.51.refs_0_, ...), custom_call_target="tpu_custom_call" | custom-call | flops 786432 | bytes 1536 | tf_op jit(solution)/shard_map/output/pallas_call | solution.py:394
  50.6 0.6 collective-permute-start.11
  51.2 1.8 %gradient.1.refs_4_ = f32[256,1024]{1,0:T(8,128)S(1)} custom-call(bf16[1536,128]{1,0:T(8,128)(2,1)S(1)} %get-tuple-element.62.dpre_two, bf16[1536,1024]{1,0:T(8,128)(2,1)S(1)} %get-tuple-element.52.refs_1_.tok, bf16[1536,1024]{1,0:T(8,128)(2,1)S(1)} %get-tuple-element.63.cot, f32[1536,128]{1,0:T(8,128)S(1)} %get-tuple-element.67.slope, ...), custom_call_target="tpu_custom_call" | custom-call | flops 10000000000 | bytes 1536 | tf_op jit(solution)/shard_map/gradient/pallas_call | solution.py:416
  53.4 0.6 collective-permute-start.19
  54.0 0.7 collective-permute-start.18
  54.7 0.7 collective-permute-done.11.refs_7_.far_ref
  55.4 3.1 %diagonal.1 = (bf16[512,512]{1,0:T(8,128)(2,1)S(1)}, bf16[512,512]{1,0:T(8,128)(2,1)S(1)}, bf16[128,1024]{1,0:T(8,128)(2,1)S(1)}, bf16[128,1024]{1,0:T(8,128)(2,...) custom-call(bf16[512,1024]{1,0:T(8,128)(2,1)S(1)} %get-tuple-element, ...), custom_call_target="tpu_custom_call" | custom-call | flops 1000000 | bytes 512 | tf_op jit(solution)/shard_map/diagonal/pallas_call | solution.py:440
  58.7 1.0 %collective-permute-start.15 = (bf16[64,1024]{1,0:T(8,128)(2,1)S(1)}, bf16[64,1024]{1,0:T(8,128)(2,1)S(1)}, u32[]{:S(2)}, u32[]{:S(2)}) collective-permute-start(bf16[64,1024]{1,0:T(8,128)(2,1)S(1)} %get-tuple-element.84), channel_id=1, source_target_pairs={{0,8},{1,9},{2,10},{3,11},{4,12},{5,13},{6,14},{7,15},{8,0},{9,1},... | collective-permute-start | bytes 393224 | tf_op jit(solution)/shard_map/ppermute | solution.py:315
  59.7 1.0 %collective-permute-start.13 = (bf16[64,1024]{1,0:T(8,128)(2,1)S(1)}, bf16[64,1024]{1,0:T(8,128)(2,1)S(1)}, u32[]{:S(2)}, u32[]{:S(2)}) collective-permute-start(bf16[64,1024]{1,0:T(8,128)(2,1)S(1)} %get-tuple-element.81), channel_id=1, source_target_pairs={{0,8},{1,9},{2,10},{3,11},{4,12},{5,13},{6,14},{7,15},{8,0},{9,1},... | collective-permute-start | bytes 393224 | tf_op jit(solution)/shard_map/ppermute | solution.py:315
  61.0 1.6 %collective-permute-start.20 = (bf16[512,512]{1,0:T(8,128)(2,1)S(1)}, bf16[512,512]{1,0:T(8,128)(2,1)S(1)}, u32[]{:S(2)}, u32[]{:S(2)}) collective-permute-start(bf16[512,512]{1,0:T(8,128)(2,1)S(1)} %get-tuple-element.79), channel_id=1, source_target_pairs={{0,6},{1,7},{2,4},{3,5},{4,2},{5,3},{6,0},{7,1},{8,14},{9,15},{10,... | collective-permute-start | bytes 1572872 | tf_op jit(solution)/shard_map/ppermute | solution.py:315
  62.6 2.4 %collective-permute-done.15.other_ref = bf16[64,1024]{1,0:T(8,128)(2,1)S(1)} collective-permute-done((bf16[64,1024]{1,0:T(8,128)(2,1)S(1)}, bf16[64,1024]{1,0:T(8,128)(2,1)S(1)}, u32[]{:S(2)}, u32[]{:S(2)}) %collective-permute-start.15) | collective-permute-done | bytes 131104 | tf_op jit(solution)/shard_map/ppermute | solution.py:315
  65.1 2.7 %collective-permute-start.16 = (bf16[64,1024]{1,0:T(8,128)(2,1)S(1)}, bf16[64,1024]{1,0:T(8,128)(2,1)S(1)}, u32[]{:S(2)}, u32[]{:S(2)}) collective-permute-start(bf16[64,1024]{1,0:T(8,128)(2,1)S(1)} %line_sum.3), channel_id=1, source_target_pairs={{0,16},{1,17},{2,18},{3,19},{4,20},{5,21},{6,22},{7,23},{8,24},{9,... | collective-permute-start | bytes 393224 | tf_op jit(solution)/shard_map/ppermute | solution.py:315
  67.8 1.8 %collective-permute-start.17 = (bf16[128,1024]{1,0:T(8,128)(2,1)S(1)}, bf16[128,1024]{1,0:T(8,128)(2,1)S(1)}, u32[]{:S(2)}, u32[]{:S(2)}) collective-permute-start(bf16[128,1024]{1,0:T(8,128)(2,1)S(1)} %get-tuple-element.86), channel_id=1, source_target_pairs={{0,8},{1,9},{2,10},{3,11},{4,12},{5,13},{6,14},{7,15},{8,0},{9,1},... | collective-permute-start | bytes 786440 | tf_op jit(solution)/shard_map/ppermute | solution.py:315
  69.6 2.2 %collective-permute-start.14 = (bf16[64,1024]{1,0:T(8,128)(2,1)S(1)}, bf16[64,1024]{1,0:T(8,128)(2,1)S(1)}, u32[]{:S(2)}, u32[]{:S(2)}) collective-permute-start(bf16[64,1024]{1,0:T(8,128)(2,1)S(1)} %line_sum.2), channel_id=1, source_target_pairs={{0,16},{1,17},{2,18},{3,19},{4,20},{5,21},{6,22},{7,23},{8,24},{9,... | collective-permute-start | bytes 393224 | tf_op jit(solution)/shard_map/ppermute | solution.py:315
  72.0 2.5 %collective-permute-done.16.refs_1_ = bf16[64,1024]{1,0:T(8,128)(2,1)S(1)} collective-permute-done((bf16[64,1024]{1,0:T(8,128)(2,1)S(1)}, bf16[64,1024]{1,0:T(8,128)(2,1)S(1)}, u32[]{:S(2)}, u32[]{:S(2)}) %collective-permute-start.16) | collective-permute-done | bytes 131104 | tf_op jit(solution)/shard_map/ppermute | solution.py:315
  74.5 3.7 %collective-permute-done.14.refs_0_ = bf16[64,1024]{1,0:T(8,128)(2,1)S(1)} collective-permute-done((bf16[64,1024]{1,0:T(8,128)(2,1)S(1)}, bf16[64,1024]{1,0:T(8,128)(2,1)S(1)}, u32[]{:S(2)}, u32[]{:S(2)}) %collective-permute-start.14) | collective-permute-done | bytes 131104 | tf_op jit(solution)/shard_map/ppermute | solution.py:315
  78.2 1.1 %collective-permute-done.17.one_ref = bf16[128,1024]{1,0:T(8,128)(2,1)S(1)} collective-permute-done((bf16[128,1024]{1,0:T(8,128)(2,1)S(1)}, bf16[128,1024]{1,0:T(8,128)(2,1)S(1)}, u32[]{:S(2)}, u32[]{:S(2)}) %collective-permute-start.17) | collective-permute-done | bytes 262176 | tf_op jit(solution)/shard_map/ppermute | solution.py:315
  79.3 0.9 %collective-permute-done.20.diag_ref = bf16[512,512]{1,0:T(8,128)(2,1)S(1)} collective-permute-done((bf16[512,512]{1,0:T(8,128)(2,1)S(1)}, bf16[512,512]{1,0:T(8,128)(2,1)S(1)}, u32[]{:S(2)}, u32[]{:S(2)}) %collective-permute-start.20) | collective-permute-done | bytes 524320 | tf_op jit(solution)/shard_map/ppermute | solution.py:315
  80.2 1.1 %results.1 = (bf16[512,512]{1,0:T(8,128)(2,1)}, f32[128,1024]{1,0:T(8,128)}) custom-call(f32[512,512]{1,0:T(8,128)S(1)} %plane_sum.1.plane_ref, bf16[512,512]{1,0:T(8,128)(2,1)S(1)} %collective-permute-done.20.diag_ref, bf16[128,1024]{1,0:T(8,128)(2,1)S(1)} %get-tuple-element.90.own_ref, bf16[128,1024]{1,0:T(8,128)(2,1)S(1)} %collective-permute-done.17.one_ref, ...), custom_call_target="tpu_custom_call" | custom-call | flops 512 | bytes 512 | tf_op jit(solution)/shard_map/results/pallas_call | solution.py:498
  (32 shorter events, 2.0 us)
Async XLA Ops:
  0.6 5.9 %copy-start.2 = (bf16[128]{0:T(256)(128)(2,1)S(1)}, bf16[128]{0:T(256)(128)(2,1)}, u32[]{:S(2)}) copy-start(bf16[128]{0:T(256)(128)(2,1)} %param.8) | copy-start | bytes 772
  0.6 5.9 %copy-start.1 = (bf16[128,1024]{1,0:T(8,128)(2,1)S(1)}, bf16[128,1024]{1,0:T(8,128)(2,1)}, u32[]{:S(2)}) copy-start(bf16[128,1024]{1,0:T(8,128)(2,1)} %param.7) | copy-start | bytes 786436
  0.7 5.9 %copy-start = (bf16[128,1024]{1,0:T(8,128)(2,1)S(1)}, bf16[128,1024]{1,0:T(8,128)(2,1)}, u32[]{:S(2)}) copy-start(bf16[128,1024]{1,0:T(8,128)(2,1)} %param.9) | copy-start | bytes 786436
  2.0 26.2 %collective-permute-start = (bf16[2,512,512]{2,1,0:T(8,128)(2,1)S(1)}, bf16[2,512,512]{2,1,0:T(8,128)(2,1)S(1)}, u32[]{:S(2)}, u32[]{:S(2)}) collective-permute-start(bf16[2,512,512]{2,1,0:T(8,128)(2,1)S(1)} %pad_maximum_fusion.1.refs_0_), channel_id=1, source_target_pairs={{0,2},{1,3},{2,0},{3,1},{4,6},{5,7},{6,4},{7,5},{8,10},{9,11},{10,... | collective-permute-start | bytes 3145736 | tf_op jit(solution)/shard_map/ppermute | solution.py:315
  5.0 24.6 %collective-permute-start.1 = (bf16[2,512,512]{2,1,0:T(8,128)(2,1)S(1)}, bf16[2,512,512]{2,1,0:T(8,128)(2,1)S(1)}, u32[]{:S(2)}, u32[]{:S(2)}) collective-permute-start(bf16[2,512,512]{2,1,0:T(8,128)(2,1)S(1)} %pad_maximum_fusion.1.refs_0_), channel_id=1, source_target_pairs={{0,4},{1,5},{2,6},{3,7},{4,0},{5,1},{6,2},{7,3},{8,12},{9,13},{10,... | collective-permute-start | bytes 3145736 | tf_op jit(solution)/shard_map/ppermute | solution.py:315
  6.5 23.1 %collective-permute-start.2 = (bf16[2,512,512]{2,1,0:T(8,128)(2,1)S(1)}, bf16[2,512,512]{2,1,0:T(8,128)(2,1)S(1)}, u32[]{:S(2)}, u32[]{:S(2)}) collective-permute-start(bf16[2,512,512]{2,1,0:T(8,128)(2,1)S(1)} %pad_maximum_fusion.1.refs_0_), channel_id=1, source_target_pairs={{0,1},{1,0},{2,3},{3,2},{4,5},{5,4},{6,7},{7,6},{8,9},{9,8},{10,11... | collective-permute-start | bytes 3145736 | tf_op jit(solution)/shard_map/ppermute | solution.py:315
  6.6 27.3 %collective-permute-start.6 = (bf16[264,1024]{1,0:T(8,128)(2,1)S(1)}, bf16[264,1024]{1,0:T(8,128)(2,1)S(1)}, u32[]{:S(2)}, u32[]{:S(2)}) collective-permute-start(bf16[264,1024]{1,0:T(8,128)(2,1)S(1)} %fusion.1.refs_6_), channel_id=1, source_target_pairs={{0,16},{1,17},{2,18},{3,19},{4,20},{5,21},{6,22},{7,23},{8,24},{9,... | collective-permute-start | bytes 1622024 | tf_op jit(solution)/shard_map/ppermute | solution.py:315
  9.3 25.9 %collective-permute-start.5 = (bf16[264,1024]{1,0:T(8,128)(2,1)S(1)}, bf16[264,1024]{1,0:T(8,128)(2,1)S(1)}, u32[]{:S(2)}, u32[]{:S(2)}) collective-permute-start(bf16[264,1024]{1,0:T(8,128)(2,1)S(1)} %fusion.1.refs_6_), channel_id=1, source_target_pairs={{0,8},{1,9},{2,10},{3,11},{4,12},{5,13},{6,14},{7,15},{8,0},{9,1},... | collective-permute-start | bytes 1622024 | tf_op jit(solution)/shard_map/ppermute | solution.py:315
  29.6 6.1 %collective-permute-start.3 = (bf16[2,512,512]{2,1,0:T(8,128)(2,1)S(1)}, bf16[2,512,512]{2,1,0:T(8,128)(2,1)S(1)}, u32[]{:S(2)}, u32[]{:S(2)}) collective-permute-start(bf16[2,512,512]{2,1,0:T(8,128)(2,1)S(1)} %collective-permute-done.refs_2_), channel_id=1, source_target_pairs={{0,1},{1,0},{2,3},{3,2},{4,5},{5,4},{6,7},{7,6},{8,9},{9,8},{10,11... | collective-permute-start | bytes 3145736 | tf_op jit(solution)/shard_map/ppermute | solution.py:315
  29.6 6.1 %collective-permute-start.4 = (bf16[2,512,512]{2,1,0:T(8,128)(2,1)S(1)}, bf16[2,512,512]{2,1,0:T(8,128)(2,1)S(1)}, u32[]{:S(2)}, u32[]{:S(2)}) collective-permute-start(bf16[2,512,512]{2,1,0:T(8,128)(2,1)S(1)} %collective-permute-done.1.refs_4_), channel_id=1, source_target_pairs={{0,1},{1,0},{2,3},{3,2},{4,5},{5,4},{6,7},{7,6},{8,9},{9,8},{10,11... | collective-permute-start | bytes 3145736 | tf_op jit(solution)/shard_map/ppermute | solution.py:315
  33.9 13.8 %collective-permute-start.7 = (bf16[264,1024]{1,0:T(8,128)(2,1)S(1)}, bf16[264,1024]{1,0:T(8,128)(2,1)S(1)}, u32[]{:S(2)}, u32[]{:S(2)}) collective-permute-start(bf16[264,1024]{1,0:T(8,128)(2,1)S(1)} %collective-permute-done.6.refs_8_), channel_id=1, source_target_pairs={{0,8},{1,9},{2,10},{3,11},{4,12},{5,13},{6,14},{7,15},{8,0},{9,1},... | collective-permute-start | bytes 1622024 | tf_op jit(solution)/shard_map/ppermute | solution.py:315
  34.6 15.8 %collective-permute-start.8 = (bf16[560,512]{1,0:T(8,128)(2,1)S(1)}, bf16[560,512]{1,0:T(8,128)(2,1)S(1)}, u32[]{:S(2)}, u32[]{:S(2)}) collective-permute-start(bf16[560,512]{1,0:T(8,128)(2,1)S(1)} %slice.12), channel_id=1, source_target_pairs={{0,4},{1,5},{2,6},{3,7},{4,0},{5,1},{6,2},{7,3},{8,12},{9,13},{10,... | collective-permute-start | bytes 1720328 | tf_op jit(solution)/shard_map/ppermute | solution.py:315
  35.2 15.2 %collective-permute-start.9 = (bf16[512,512]{1,0:T(8,128)(2,1)S(1)}, bf16[512,512]{1,0:T(8,128)(2,1)S(1)}, u32[]{:S(2)}, u32[]{:S(2)}) collective-permute-start(bf16[512,512]{1,0:T(8,128)(2,1)S(1)} %slice_bitcast_fusion), channel_id=1, source_target_pairs={{0,2},{1,3},{2,0},{3,1},{4,6},{5,7},{6,4},{7,5},{8,10},{9,11},{10,... | collective-permute-start | bytes 1572872 | tf_op jit(solution)/shard_map/ppermute | solution.py:315
  50.4 2.7 %collective-permute-start.10 = (bf16[1024,512]{1,0:T(8,128)(2,1)S(1)}, bf16[1024,512]{1,0:T(8,128)(2,1)S(1)}, u32[]{:S(2)}, u32[]{:S(2)}) collective-permute-start(bf16[1024,512]{1,0:T(8,128)(2,1)S(1)} %get-tuple-element.69), channel_id=1, source_target_pairs={{0,1},{1,0},{2,3},{3,2},{4,5},{5,4},{6,7},{7,6},{8,9},{9,8},{10,11... | collective-permute-start | bytes 3145736 | tf_op jit(solution)/shard_map/ppermute | solution.py:315
  50.6 4.8 %collective-permute-start.11 = (bf16[1536,512]{1,0:T(8,128)(2,1)S(1)}, bf16[1536,512]{1,0:T(8,128)(2,1)S(1)}, u32[]{:S(2)}, u32[]{:S(2)}) collective-permute-start(bf16[1536,512]{1,0:T(8,128)(2,1)S(1)} %pad_maximum_fusion), channel_id=1, source_target_pairs={{0,1},{1,0},{2,3},{3,2},{4,5},{5,4},{6,7},{7,6},{8,9},{9,8},{10,11... | collective-permute-start | bytes 4718600 | tf_op jit(solution)/shard_map/ppermute | solution.py:315
  53.4 18.4 %collective-permute-start.19 = (bf16[544,512]{1,0:T(8,128)(2,1)S(1)}, bf16[544,512]{1,0:T(8,128)(2,1)S(1)}, u32[]{:S(2)}, u32[]{:S(2)}) collective-permute-start(bf16[544,512]{1,0:T(8,128)(2,1)S(1)} %get-tuple-element.88), channel_id=1, source_target_pairs={{0,4},{1,5},{2,6},{3,7},{4,0},{5,1},{6,2},{7,3},{8,12},{9,13},{10,... | collective-permute-start | bytes 1671176 | tf_op jit(solution)/shard_map/ppermute | solution.py:315
  54.0 15.6 %collective-permute-start.18 = (bf16[528,512]{1,0:T(8,128)(2,1)S(1)}, bf16[528,512]{1,0:T(8,128)(2,1)S(1)}, u32[]{:S(2)}, u32[]{:S(2)}) collective-permute-start(bf16[528,512]{1,0:T(8,128)(2,1)S(1)} %get-tuple-element.70), channel_id=1, source_target_pairs={{0,2},{1,3},{2,0},{3,1},{4,6},{5,7},{6,4},{7,5},{8,10},{9,11},{10,... | collective-permute-start | bytes 1622024 | tf_op jit(solution)/shard_map/ppermute | solution.py:315
  58.5 2.2 %collective-permute-start.12 = (bf16[512,512]{1,0:T(8,128)(2,1)S(1)}, bf16[512,512]{1,0:T(8,128)(2,1)S(1)}, u32[]{:S(2)}, u32[]{:S(2)}) collective-permute-start(bf16[512,512]{1,0:T(8,128)(2,1)S(1)} %get-tuple-element.78), channel_id=1, source_target_pairs={{0,1},{1,0},{2,3},{3,2},{4,5},{5,4},{6,7},{7,6},{8,9},{9,8},{10,11... | collective-permute-start | bytes 1572872 | tf_op jit(solution)/shard_map/ppermute | solution.py:315
  58.7 6.3 %collective-permute-start.15 = (bf16[64,1024]{1,0:T(8,128)(2,1)S(1)}, bf16[64,1024]{1,0:T(8,128)(2,1)S(1)}, u32[]{:S(2)}, u32[]{:S(2)}) collective-permute-start(bf16[64,1024]{1,0:T(8,128)(2,1)S(1)} %get-tuple-element.84), channel_id=1, source_target_pairs={{0,8},{1,9},{2,10},{3,11},{4,12},{5,13},{6,14},{7,15},{8,0},{9,1},... | collective-permute-start | bytes 393224 | tf_op jit(solution)/shard_map/ppermute | solution.py:315
  59.7 8.0 %collective-permute-start.13 = (bf16[64,1024]{1,0:T(8,128)(2,1)S(1)}, bf16[64,1024]{1,0:T(8,128)(2,1)S(1)}, u32[]{:S(2)}, u32[]{:S(2)}) collective-permute-start(bf16[64,1024]{1,0:T(8,128)(2,1)S(1)} %get-tuple-element.81), channel_id=1, source_target_pairs={{0,8},{1,9},{2,10},{3,11},{4,12},{5,13},{6,14},{7,15},{8,0},{9,1},... | collective-permute-start | bytes 393224 | tf_op jit(solution)/shard_map/ppermute | solution.py:315
  61.0 19.2 %collective-permute-start.20 = (bf16[512,512]{1,0:T(8,128)(2,1)S(1)}, bf16[512,512]{1,0:T(8,128)(2,1)S(1)}, u32[]{:S(2)}, u32[]{:S(2)}) collective-permute-start(bf16[512,512]{1,0:T(8,128)(2,1)S(1)} %get-tuple-element.79), channel_id=1, source_target_pairs={{0,6},{1,7},{2,4},{3,5},{4,2},{5,3},{6,0},{7,1},{8,14},{9,15},{10,... | collective-permute-start | bytes 1572872 | tf_op jit(solution)/shard_map/ppermute | solution.py:315
  65.1 9.4 %collective-permute-start.16 = (bf16[64,1024]{1,0:T(8,128)(2,1)S(1)}, bf16[64,1024]{1,0:T(8,128)(2,1)S(1)}, u32[]{:S(2)}, u32[]{:S(2)}) collective-permute-start(bf16[64,1024]{1,0:T(8,128)(2,1)S(1)} %line_sum.3), channel_id=1, source_target_pairs={{0,16},{1,17},{2,18},{3,19},{4,20},{5,21},{6,22},{7,23},{8,24},{9,... | collective-permute-start | bytes 393224 | tf_op jit(solution)/shard_map/ppermute | solution.py:315
  67.8 11.5 %collective-permute-start.17 = (bf16[128,1024]{1,0:T(8,128)(2,1)S(1)}, bf16[128,1024]{1,0:T(8,128)(2,1)S(1)}, u32[]{:S(2)}, u32[]{:S(2)}) collective-permute-start(bf16[128,1024]{1,0:T(8,128)(2,1)S(1)} %get-tuple-element.86), channel_id=1, source_target_pairs={{0,8},{1,9},{2,10},{3,11},{4,12},{5,13},{6,14},{7,15},{8,0},{9,1},... | collective-permute-start | bytes 786440 | tf_op jit(solution)/shard_map/ppermute | solution.py:315
  69.6 8.6 %collective-permute-start.14 = (bf16[64,1024]{1,0:T(8,128)(2,1)S(1)}, bf16[64,1024]{1,0:T(8,128)(2,1)S(1)}, u32[]{:S(2)}, u32[]{:S(2)}) collective-permute-start(bf16[64,1024]{1,0:T(8,128)(2,1)S(1)} %line_sum.2), channel_id=1, source_target_pairs={{0,16},{1,17},{2,18},{3,19},{4,20},{5,21},{6,22},{7,23},{8,24},{9,... | collective-permute-start | bytes 393224 | tf_op jit(solution)/shard_map/ppermute | solution.py:315

commit v21 on v19

--- a/solution.py
+++ b/solution.py
@@ -182,11 +182,10 @@
     w_last[:owned, :] = w_out[two:, :]
     w_last[owned:, :] = w_three[owned:two, :]
     step = tok.shape[0] // 6
-    for at in range(6):
+    acts = {}
+
+    def mix(at):
         spot = slice(at * step, (at + 1) * step)
-        value, slope = activate(tok[spot, :], w_three[:owned, :], bias_last[0:1, :])
-        slope_ref[spot, :] = slope
-        act = jnp.concatenate([act_two[spot, :], value.astype(jnp.bfloat16)], axis=1)
         if at * step < rows:
             far_ref, there = own_ref, spot
         else:
@@ -195,9 +194,17 @@
             half = half_columns(core, shift, feats)
             ref[to, :] = (
                 early_mixed[spot, half]
-                + jnp.dot(act, w_last[:, half], preferred_element_type=jnp.float32)
+                + jnp.dot(acts[at], w_last[:, half], preferred_element_type=jnp.float32)
             ).astype(jnp.bfloat16)
 
+    for at in range(6):
+        spot = slice(at * step, (at + 1) * step)
+        value, slope = activate(tok[spot, :], w_three[:owned, :], bias_last[0:1, :])
+        slope_ref[spot, :] = slope
+        acts[at] = jnp.concatenate([act_two[spot, :], value.astype(jnp.bfloat16)], axis=1)
+        if at:
+            mix(at - 1)
+    mix(5)
     run(copies, "wait")
 
 

time: 80.7 us -> 80.6 us (level)
  transfers between devices with their start and end apart: 21 -> 21, of which waited for: 8 -> 8; matrix products, arithmetic and copies ran while one was open for 0% -> 0% of each run, Pallas kernels for 20% -> 19%
where the time goes in v21:
time: 80.6 us; the launch traced here: 80.5 us
  waiting for transfers between devices  38 us (47%)
  starting transfers between devices  23.4 us (29%)
  Pallas kernels  16.7 us (21%)
  other arithmetic  1.49 us (2%)
  between operations  0.83 us (1%)
    ppermute x21, waiting for transfers between devices, permute(): return lax.ppermute(value, AXES, pairs)  38 us
    ppermute x21, starting transfers between devices, permute(): return lax.ppermute(value, AXES, pairs)  23.4 us
    pallas_call x1, Pallas kernels, on_device_lines(): pl.pallas_call(functools.partial(early_kernel, owned), out_shape=(bf16(ea...  7.43 us
    pallas_call x1, Pallas kernels, on_device_lines(): pl.pallas_call(functools.partial(diagonal_kernel, owned), out_shape=[bf16...  3.13 us
    pallas_call x1, Pallas kernels, on_device_lines(): pl.pallas_call(functools.partial(output_kernel, owned), out_shape=(bf16(e...  2.45 us
    pallas_call x1, Pallas kernels, on_device_lines(): pl.pallas_call(gradient_kernel, out_shape=f32(2 * owned, width), in_specs...  1.81 us
  transfers between devices with their start and end apart: 21, of which 8 were waited for; matrix products, arithmetic and copies ran while one was open for 0% of the time, Pallas kernels for 19%

profile of v21, /device:TPU:0, one launch (start us, length us, event | category | flops | bytes accessed | tf_op | source)
XLA Modules:
  0.0 80.5 jit_solution(2710983987100161772)
XLA Ops:
  0.7 1.4 %pad_maximum_fusion.1.refs_0_ = bf16[2,512,512]{2,1,0:T(8,128)(2,1)S(1)} fusion(bf16[1,512,512]{2,1,0:T(8,128)(2,1)} %bitcast.7, bf16[1,512,512]{2,1,0:T(8,128)(2,1)} %bitcast.8), kind=kLoop, calls=%fused_computation.3 | loop fusion | flops 524288 | bytes 2097152 | tf_op jit(solution)/shard_map/stack | solution.py:364
  2.0 3.0 %collective-permute-start = (bf16[2,512,512]{2,1,0:T(8,128)(2,1)S(1)}, bf16[2,512,512]{2,1,0:T(8,128)(2,1)S(1)}, u32[]{:S(2)}, u32[]{:S(2)}) collective-permute-start(bf16[2,512,512]{2,1,0:T(8,128)(2,1)S(1)} %pad_maximum_fusion.1.refs_0_), channel_id=1, source_target_pairs={{0,2},{1,3},{2,0},{3,1},{4,6},{5,7},{6,4},{7,5},{8,10},{9,11},{10,... | collective-permute-start | bytes 3145736 | tf_op jit(solution)/shard_map/ppermute | solution.py:322
  5.0 1.5 %collective-permute-start.1 = (bf16[2,512,512]{2,1,0:T(8,128)(2,1)S(1)}, bf16[2,512,512]{2,1,0:T(8,128)(2,1)S(1)}, u32[]{:S(2)}, u32[]{:S(2)}) collective-permute-start(bf16[2,512,512]{2,1,0:T(8,128)(2,1)S(1)} %pad_maximum_fusion.1.refs_0_), channel_id=1, source_target_pairs={{0,4},{1,5},{2,6},{3,7},{4,0},{5,1},{6,2},{7,3},{8,12},{9,13},{10,... | collective-permute-start | bytes 3145736 | tf_op jit(solution)/shard_map/ppermute | solution.py:322
  6.6 2.7 %collective-permute-start.6 = (bf16[264,1024]{1,0:T(8,128)(2,1)S(1)}, bf16[264,1024]{1,0:T(8,128)(2,1)S(1)}, u32[]{:S(2)}, u32[]{:S(2)}) collective-permute-start(bf16[264,1024]{1,0:T(8,128)(2,1)S(1)} %fusion.1.refs_6_), channel_id=1, source_target_pairs={{0,16},{1,17},{2,18},{3,19},{4,20},{5,21},{6,22},{7,23},{8,24},{9,... | collective-permute-start | bytes 1622024 | tf_op jit(solution)/shard_map/ppermute | solution.py:322
  9.3 1.6 %collective-permute-start.5 = (bf16[264,1024]{1,0:T(8,128)(2,1)S(1)}, bf16[264,1024]{1,0:T(8,128)(2,1)S(1)}, u32[]{:S(2)}, u32[]{:S(2)}) collective-permute-start(bf16[264,1024]{1,0:T(8,128)(2,1)S(1)} %fusion.1.refs_6_), channel_id=1, source_target_pairs={{0,8},{1,9},{2,10},{3,11},{4,12},{5,13},{6,14},{7,15},{8,0},{9,1},... | collective-permute-start | bytes 1622024 | tf_op jit(solution)/shard_map/ppermute | solution.py:322
  10.8 17.3 %collective-permute-done.refs_2_ = bf16[2,512,512]{2,1,0:T(8,128)(2,1)S(1)} collective-permute-done((bf16[2,512,512]{2,1,0:T(8,128)(2,1)S(1)}, bf16[2,512,512]{2,1,0:T(8,128)(2,1)S(1)}, u32[]{:S(2)}, u32[]{:S(2)}) %collective-permute-start) | collective-permute-done | bytes 1048608 | tf_op jit(solution)/shard_map/ppermute | solution.py:322
  28.2 1.5 %collective-permute-done.1.refs_4_ = bf16[2,512,512]{2,1,0:T(8,128)(2,1)S(1)} collective-permute-done((bf16[2,512,512]{2,1,0:T(8,128)(2,1)S(1)}, bf16[2,512,512]{2,1,0:T(8,128)(2,1)S(1)}, u32[]{:S(2)}, u32[]{:S(2)}) %collective-permute-start.1) | collective-permute-done | bytes 1048608 | tf_op jit(solution)/shard_map/ppermute | solution.py:322
  29.6 0.5 collective-permute-start.4
  30.2 3.8 %collective-permute-done.6.refs_8_ = bf16[264,1024]{1,0:T(8,128)(2,1)S(1)} collective-permute-done((bf16[264,1024]{1,0:T(8,128)(2,1)S(1)}, bf16[264,1024]{1,0:T(8,128)(2,1)S(1)}, u32[]{:S(2)}, u32[]{:S(2)}) %collective-permute-start.6) | collective-permute-done | bytes 540704 | tf_op jit(solution)/shard_map/ppermute | solution.py:322
  33.9 0.6 collective-permute-start.7
  34.6 0.6 collective-permute-start.8
  35.2 0.6 collective-permute-start.9
  35.8 7.4 %early.1 = (bf16[1536,128]{1,0:T(8,128)(2,1)S(1)}, bf16[1536,128]{1,0:T(8,128)(2,1)S(1)}, f32[1536,1024]{1,0:T(8,128)S(1)}, f32[256,1024]{1,0:T(8,128)S(1)}, bf1...) custom-call(bf16[2,512,512]{2,1,0:T(8,128)(2,1)S(1)} %pad_maximum_fu, ...), custom_call_target="tpu_custom_call" | custom-call | flops 786432 | bytes 1536 | tf_op jit(solution)/shard_map/early/pallas_call | solution.py:374
  43.2 4.5 %collective-permute-done.7.refs_6_.w_three = bf16[264,1024]{1,0:T(8,128)(2,1)S(1)} collective-permute-done((bf16[264,1024]{1,0:T(8,128)(2,1)S(1)}, bf16[264,1024]{1,0:T(8,128)(2,1)S(1)}, u32[]{:S(2)}, u32[]{:S(2)}) %collective-permute-start.7) | collective-permute-done | bytes 540704 | tf_op jit(solution)/shard_map/ppermute | solution.py:322
  47.8 2.5 %output.1 = (bf16[1536,512]{1,0:T(8,128)(2,1)S(1)}, bf16[1024,512]{1,0:T(8,128)(2,1)S(1)}, bf16[512,512]{1,0:T(8,128)(2,1)S(1)}, f32[1536,128]{1,0:T(8,128)S(1)}...) custom-call(bf16[1536,128]{1,0:T(8,128)(2,1)S(1)} %get-tuple-element.51.refs_0_, ...), custom_call_target="tpu_custom_call" | custom-call | flops 786432 | bytes 1536 | tf_op jit(solution)/shard_map/output/pallas_call | solution.py:401
  50.5 0.6 collective-permute-start.11
  51.0 1.8 %gradient.1.refs_4_ = f32[256,1024]{1,0:T(8,128)S(1)} custom-call(bf16[1536,128]{1,0:T(8,128)(2,1)S(1)} %get-tuple-element.62.dpre_two, bf16[1536,1024]{1,0:T(8,128)(2,1)S(1)} %get-tuple-element.52.refs_1_.tok, bf16[1536,1024]{1,0:T(8,128)(2,1)S(1)} %get-tuple-element.63.cot, f32[1536,128]{1,0:T(8,128)S(1)} %get-tuple-element.67.slope, ...), custom_call_target="tpu_custom_call" | custom-call | flops 10000000000 | bytes 1536 | tf_op jit(solution)/shard_map/gradient/pallas_call | solution.py:423
  53.0 0.3 pair_sum.1
  53.3 0.6 collective-permute-start.18
  53.9 0.7 collective-permute-start.19
  54.6 0.7 collective-permute-done.11.refs_7_.far_ref
  55.3 3.1 %diagonal.1 = (bf16[512,512]{1,0:T(8,128)(2,1)S(1)}, bf16[512,512]{1,0:T(8,128)(2,1)S(1)}, bf16[128,1024]{1,0:T(8,128)(2,1)S(1)}, bf16[128,1024]{1,0:T(8,128)(2,...) custom-call(bf16[512,1024]{1,0:T(8,128)(2,1)S(1)} %get-tuple-element, ...), custom_call_target="tpu_custom_call" | custom-call | flops 1000000 | bytes 512 | tf_op jit(solution)/shard_map/diagonal/pallas_call | solution.py:447
  58.6 1.0 %collective-permute-start.15 = (bf16[64,1024]{1,0:T(8,128)(2,1)S(1)}, bf16[64,1024]{1,0:T(8,128)(2,1)S(1)}, u32[]{:S(2)}, u32[]{:S(2)}) collective-permute-start(bf16[64,1024]{1,0:T(8,128)(2,1)S(1)} %get-tuple-element.84), channel_id=1, source_target_pairs={{0,8},{1,9},{2,10},{3,11},{4,12},{5,13},{6,14},{7,15},{8,0},{9,1},... | collective-permute-start | bytes 393224 | tf_op jit(solution)/shard_map/ppermute | solution.py:322
  59.6 1.0 %collective-permute-start.13 = (bf16[64,1024]{1,0:T(8,128)(2,1)S(1)}, bf16[64,1024]{1,0:T(8,128)(2,1)S(1)}, u32[]{:S(2)}, u32[]{:S(2)}) collective-permute-start(bf16[64,1024]{1,0:T(8,128)(2,1)S(1)} %get-tuple-element.81), channel_id=1, source_target_pairs={{0,8},{1,9},{2,10},{3,11},{4,12},{5,13},{6,14},{7,15},{8,0},{9,1},... | collective-permute-start | bytes 393224 | tf_op jit(solution)/shard_map/ppermute | solution.py:322
  60.7 0.3 pair_sum_diagonal.1
  60.9 1.6 %collective-permute-start.20 = (bf16[512,512]{1,0:T(8,128)(2,1)S(1)}, bf16[512,512]{1,0:T(8,128)(2,1)S(1)}, u32[]{:S(2)}, u32[]{:S(2)}) collective-permute-start(bf16[512,512]{1,0:T(8,128)(2,1)S(1)} %get-tuple-element.79), channel_id=1, source_target_pairs={{0,6},{1,7},{2,4},{3,5},{4,2},{5,3},{6,0},{7,1},{8,14},{9,15},{10,... | collective-permute-start | bytes 1572872 | tf_op jit(solution)/shard_map/ppermute | solution.py:322
  62.5 2.4 %collective-permute-done.15.other_ref = bf16[64,1024]{1,0:T(8,128)(2,1)S(1)} collective-permute-done((bf16[64,1024]{1,0:T(8,128)(2,1)S(1)}, bf16[64,1024]{1,0:T(8,128)(2,1)S(1)}, u32[]{:S(2)}, u32[]{:S(2)}) %collective-permute-start.15) | collective-permute-done | bytes 131104 | tf_op jit(solution)/shard_map/ppermute | solution.py:322
  65.0 2.7 %collective-permute-start.16 = (bf16[64,1024]{1,0:T(8,128)(2,1)S(1)}, bf16[64,1024]{1,0:T(8,128)(2,1)S(1)}, u32[]{:S(2)}, u32[]{:S(2)}) collective-permute-start(bf16[64,1024]{1,0:T(8,128)(2,1)S(1)} %line_sum.3), channel_id=1, source_target_pairs={{0,16},{1,17},{2,18},{3,19},{4,20},{5,21},{6,22},{7,23},{8,24},{9,... | collective-permute-start | bytes 393224 | tf_op jit(solution)/shard_map/ppermute | solution.py:322
  67.7 1.8 %collective-permute-start.17 = (bf16[128,1024]{1,0:T(8,128)(2,1)S(1)}, bf16[128,1024]{1,0:T(8,128)(2,1)S(1)}, u32[]{:S(2)}, u32[]{:S(2)}) collective-permute-start(bf16[128,1024]{1,0:T(8,128)(2,1)S(1)} %get-tuple-element.86), channel_id=1, source_target_pairs={{0,8},{1,9},{2,10},{3,11},{4,12},{5,13},{6,14},{7,15},{8,0},{9,1},... | collective-permute-start | bytes 786440 | tf_op jit(solution)/shard_map/ppermute | solution.py:322
  69.5 2.2 %collective-permute-start.14 = (bf16[64,1024]{1,0:T(8,128)(2,1)S(1)}, bf16[64,1024]{1,0:T(8,128)(2,1)S(1)}, u32[]{:S(2)}, u32[]{:S(2)}) collective-permute-start(bf16[64,1024]{1,0:T(8,128)(2,1)S(1)} %line_sum.2), channel_id=1, source_target_pairs={{0,16},{1,17},{2,18},{3,19},{4,20},{5,21},{6,22},{7,23},{8,24},{9,... | collective-permute-start | bytes 393224 | tf_op jit(solution)/shard_map/ppermute | solution.py:322
  71.7 7.5 %collective-permute-done.19.y_ref = bf16[528,512]{1,0:T(8,128)(2,1)S(1)} collective-permute-done((bf16[528,512]{1,0:T(8,128)(2,1)S(1)}, bf16[528,512]{1,0:T(8,128)(2,1)S(1)}, u32[]{:S(2)}, u32[]{:S(2)}) %collective-permute-start.19) | collective-permute-done | bytes 540704 | tf_op jit(solution)/shard_map/ppermute | solution.py:322
  79.4 1.1 %results.1 = (bf16[512,512]{1,0:T(8,128)(2,1)}, f32[128,1024]{1,0:T(8,128)}) custom-call(f32[512,512]{1,0:T(8,128)S(1)} %plane_sum.1.plane_ref, bf16[512,512]{1,0:T(8,128)(2,1)S(1)} %collective-permute-done.20.diag_ref, bf16[128,1024]{1,0:T(8,128)(2,1)S(1)} %get-tuple-element.90.own_ref, bf16[128,1024]{1,0:T(8,128)(2,1)S(1)} %collective-permute-done.17.one_ref, ...), custom_call_target="tpu_custom_call" | custom-call | flops 512 | bytes 512 | tf_op jit(solution)/shard_map/results/pallas_call | solution.py:505
  (32 shorter events, 1.0 us)
Async XLA Ops:
  0.6 5.9 %copy-start.2 = (bf16[128]{0:T(256)(128)(2,1)S(1)}, bf16[128]{0:T(256)(128)(2,1)}, u32[]{:S(2)}) copy-start(bf16[128]{0:T(256)(128)(2,1)} %param.8) | copy-start | bytes 772
  0.6 5.9 %copy-start.1 = (bf16[128,1024]{1,0:T(8,128)(2,1)S(1)}, bf16[128,1024]{1,0:T(8,128)(2,1)}, u32[]{:S(2)}) copy-start(bf16[128,1024]{1,0:T(8,128)(2,1)} %param.7) | copy-start | bytes 786436
  0.7 5.9 %copy-start = (bf16[128,1024]{1,0:T(8,128)(2,1)S(1)}, bf16[128,1024]{1,0:T(8,128)(2,1)}, u32[]{:S(2)}) copy-start(bf16[128,1024]{1,0:T(8,128)(2,1)} %param.9) | copy-start | bytes 786436
  2.0 26.2 %collective-permute-start = (bf16[2,512,512]{2,1,0:T(8,128)(2,1)S(1)}, bf16[2,512,512]{2,1,0:T(8,128)(2,1)S(1)}, u32[]{:S(2)}, u32[]{:S(2)}) collective-permute-start(bf16[2,512,512]{2,1,0:T(8,128)(2,1)S(1)} %pad_maximum_fusion.1.refs_0_), channel_id=1, source_target_pairs={{0,2},{1,3},{2,0},{3,1},{4,6},{5,7},{6,4},{7,5},{8,10},{9,11},{10,... | collective-permute-start | bytes 3145736 | tf_op jit(solution)/shard_map/ppermute | solution.py:322
  5.0 24.6 %collective-permute-start.1 = (bf16[2,512,512]{2,1,0:T(8,128)(2,1)S(1)}, bf16[2,512,512]{2,1,0:T(8,128)(2,1)S(1)}, u32[]{:S(2)}, u32[]{:S(2)}) collective-permute-start(bf16[2,512,512]{2,1,0:T(8,128)(2,1)S(1)} %pad_maximum_fusion.1.refs_0_), channel_id=1, source_target_pairs={{0,4},{1,5},{2,6},{3,7},{4,0},{5,1},{6,2},{7,3},{8,12},{9,13},{10,... | collective-permute-start | bytes 3145736 | tf_op jit(solution)/shard_map/ppermute | solution.py:322
  6.5 23.1 %collective-permute-start.2 = (bf16[2,512,512]{2,1,0:T(8,128)(2,1)S(1)}, bf16[2,512,512]{2,1,0:T(8,128)(2,1)S(1)}, u32[]{:S(2)}, u32[]{:S(2)}) collective-permute-start(bf16[2,512,512]{2,1,0:T(8,128)(2,1)S(1)} %pad_maximum_fusion.1.refs_0_), channel_id=1, source_target_pairs={{0,1},{1,0},{2,3},{3,2},{4,5},{5,4},{6,7},{7,6},{8,9},{9,8},{10,11... | collective-permute-start | bytes 3145736 | tf_op jit(solution)/shard_map/ppermute | solution.py:322
  6.6 27.3 %collective-permute-start.6 = (bf16[264,1024]{1,0:T(8,128)(2,1)S(1)}, bf16[264,1024]{1,0:T(8,128)(2,1)S(1)}, u32[]{:S(2)}, u32[]{:S(2)}) collective-permute-start(bf16[264,1024]{1,0:T(8,128)(2,1)S(1)} %fusion.1.refs_6_), channel_id=1, source_target_pairs={{0,16},{1,17},{2,18},{3,19},{4,20},{5,21},{6,22},{7,23},{8,24},{9,... | collective-permute-start | bytes 1622024 | tf_op jit(solution)/shard_map/ppermute | solution.py:322
  9.3 25.9 %collective-permute-start.5 = (bf16[264,1024]{1,0:T(8,128)(2,1)S(1)}, bf16[264,1024]{1,0:T(8,128)(2,1)S(1)}, u32[]{:S(2)}, u32[]{:S(2)}) collective-permute-start(bf16[264,1024]{1,0:T(8,128)(2,1)S(1)} %fusion.1.refs_6_), channel_id=1, source_target_pairs={{0,8},{1,9},{2,10},{3,11},{4,12},{5,13},{6,14},{7,15},{8,0},{9,1},... | collective-permute-start | bytes 1622024 | tf_op jit(solution)/shard_map/ppermute | solution.py:322
  29.6 6.1 %collective-permute-start.3 = (bf16[2,512,512]{2,1,0:T(8,128)(2,1)S(1)}, bf16[2,512,512]{2,1,0:T(8,128)(2,1)S(1)}, u32[]{:S(2)}, u32[]{:S(2)}) collective-permute-start(bf16[2,512,512]{2,1,0:T(8,128)(2,1)S(1)} %collective-permute-done.refs_2_), channel_id=1, source_target_pairs={{0,1},{1,0},{2,3},{3,2},{4,5},{5,4},{6,7},{7,6},{8,9},{9,8},{10,11... | collective-permute-start | bytes 3145736 | tf_op jit(solution)/shard_map/ppermute | solution.py:322
  29.6 6.1 %collective-permute-start.4 = (bf16[2,512,512]{2,1,0:T(8,128)(2,1)S(1)}, bf16[2,512,512]{2,1,0:T(8,128)(2,1)S(1)}, u32[]{:S(2)}, u32[]{:S(2)}) collective-permute-start(bf16[2,512,512]{2,1,0:T(8,128)(2,1)S(1)} %collective-permute-done.1.refs_4_), channel_id=1, source_target_pairs={{0,1},{1,0},{2,3},{3,2},{4,5},{5,4},{6,7},{7,6},{8,9},{9,8},{10,11... | collective-permute-start | bytes 3145736 | tf_op jit(solution)/shard_map/ppermute | solution.py:322
  33.9 13.8 %collective-permute-start.7 = (bf16[264,1024]{1,0:T(8,128)(2,1)S(1)}, bf16[264,1024]{1,0:T(8,128)(2,1)S(1)}, u32[]{:S(2)}, u32[]{:S(2)}) collective-permute-start(bf16[264,1024]{1,0:T(8,128)(2,1)S(1)} %collective-permute-done.6.refs_8_), channel_id=1, source_target_pairs={{0,8},{1,9},{2,10},{3,11},{4,12},{5,13},{6,14},{7,15},{8,0},{9,1},... | collective-permute-start | bytes 1622024 | tf_op jit(solution)/shard_map/ppermute | solution.py:322
  34.6 15.7 %collective-permute-start.8 = (bf16[560,512]{1,0:T(8,128)(2,1)S(1)}, bf16[560,512]{1,0:T(8,128)(2,1)S(1)}, u32[]{:S(2)}, u32[]{:S(2)}) collective-permute-start(bf16[560,512]{1,0:T(8,128)(2,1)S(1)} %slice.12), channel_id=1, source_target_pairs={{0,4},{1,5},{2,6},{3,7},{4,0},{5,1},{6,2},{7,3},{8,12},{9,13},{10,... | collective-permute-start | bytes 1720328 | tf_op jit(solution)/shard_map/ppermute | solution.py:322
  35.2 15.0 %collective-permute-start.9 = (bf16[512,512]{1,0:T(8,128)(2,1)S(1)}, bf16[512,512]{1,0:T(8,128)(2,1)S(1)}, u32[]{:S(2)}, u32[]{:S(2)}) collective-permute-start(bf16[512,512]{1,0:T(8,128)(2,1)S(1)} %slice_bitcast_fusion), channel_id=1, source_target_pairs={{0,2},{1,3},{2,0},{3,1},{4,6},{5,7},{6,4},{7,5},{8,10},{9,11},{10,... | collective-permute-start | bytes 1572872 | tf_op jit(solution)/shard_map/ppermute | solution.py:322
  50.3 2.7 %collective-permute-start.10 = (bf16[1024,512]{1,0:T(8,128)(2,1)S(1)}, bf16[1024,512]{1,0:T(8,128)(2,1)S(1)}, u32[]{:S(2)}, u32[]{:S(2)}) collective-permute-start(bf16[1024,512]{1,0:T(8,128)(2,1)S(1)} %get-tuple-element.69), channel_id=1, source_target_pairs={{0,1},{1,0},{2,3},{3,2},{4,5},{5,4},{6,7},{7,6},{8,9},{9,8},{10,11... | collective-permute-start | bytes 3145736 | tf_op jit(solution)/shard_map/ppermute | solution.py:322
  50.5 4.8 %collective-permute-start.11 = (bf16[1536,512]{1,0:T(8,128)(2,1)S(1)}, bf16[1536,512]{1,0:T(8,128)(2,1)S(1)}, u32[]{:S(2)}, u32[]{:S(2)}) collective-permute-start(bf16[1536,512]{1,0:T(8,128)(2,1)S(1)} %pad_maximum_fusion), channel_id=1, source_target_pairs={{0,1},{1,0},{2,3},{3,2},{4,5},{5,4},{6,7},{7,6},{8,9},{9,8},{10,11... | collective-permute-start | bytes 4718600 | tf_op jit(solution)/shard_map/ppermute | solution.py:322
  53.3 16.2 %collective-permute-start.18 = (bf16[528,512]{1,0:T(8,128)(2,1)S(1)}, bf16[528,512]{1,0:T(8,128)(2,1)S(1)}, u32[]{:S(2)}, u32[]{:S(2)}) collective-permute-start(bf16[528,512]{1,0:T(8,128)(2,1)S(1)} %get-tuple-element.70), channel_id=1, source_target_pairs={{0,2},{1,3},{2,0},{3,1},{4,6},{5,7},{6,4},{7,5},{8,10},{9,11},{10,... | collective-permute-start | bytes 1622024 | tf_op jit(solution)/shard_map/ppermute | solution.py:322
  53.9 25.3 %collective-permute-start.19 = (bf16[528,512]{1,0:T(8,128)(2,1)S(1)}, bf16[528,512]{1,0:T(8,128)(2,1)S(1)}, u32[]{:S(2)}, u32[]{:S(2)}) collective-permute-start(bf16[528,512]{1,0:T(8,128)(2,1)S(1)} %get-tuple-element.88), channel_id=1, source_target_pairs={{0,4},{1,5},{2,6},{3,7},{4,0},{5,1},{6,2},{7,3},{8,12},{9,13},{10,... | collective-permute-start | bytes 1622024 | tf_op jit(solution)/shard_map/ppermute | solution.py:322
  58.4 2.2 %collective-permute-start.12 = (bf16[512,512]{1,0:T(8,128)(2,1)S(1)}, bf16[512,512]{1,0:T(8,128)(2,1)S(1)}, u32[]{:S(2)}, u32[]{:S(2)}) collective-permute-start(bf16[512,512]{1,0:T(8,128)(2,1)S(1)} %get-tuple-element.78), channel_id=1, source_target_pairs={{0,1},{1,0},{2,3},{3,2},{4,5},{5,4},{6,7},{7,6},{8,9},{9,8},{10,11... | collective-permute-start | bytes 1572872 | tf_op jit(solution)/shard_map/ppermute | solution.py:322
  58.6 6.3 %collective-permute-start.15 = (bf16[64,1024]{1,0:T(8,128)(2,1)S(1)}, bf16[64,1024]{1,0:T(8,128)(2,1)S(1)}, u32[]{:S(2)}, u32[]{:S(2)}) collective-permute-start(bf16[64,1024]{1,0:T(8,128)(2,1)S(1)} %get-tuple-element.84), channel_id=1, source_target_pairs={{0,8},{1,9},{2,10},{3,11},{4,12},{5,13},{6,14},{7,15},{8,0},{9,1},... | collective-permute-start | bytes 393224 | tf_op jit(solution)/shard_map/ppermute | solution.py:322
  59.6 8.1 %collective-permute-start.13 = (bf16[64,1024]{1,0:T(8,128)(2,1)S(1)}, bf16[64,1024]{1,0:T(8,128)(2,1)S(1)}, u32[]{:S(2)}, u32[]{:S(2)}) collective-permute-start(bf16[64,1024]{1,0:T(8,128)(2,1)S(1)} %get-tuple-element.81), channel_id=1, source_target_pairs={{0,8},{1,9},{2,10},{3,11},{4,12},{5,13},{6,14},{7,15},{8,0},{9,1},... | collective-permute-start | bytes 393224 | tf_op jit(solution)/shard_map/ppermute | solution.py:322
  60.9 18.5 %collective-permute-start.20 = (bf16[512,512]{1,0:T(8,128)(2,1)S(1)}, bf16[512,512]{1,0:T(8,128)(2,1)S(1)}, u32[]{:S(2)}, u32[]{:S(2)}) collective-permute-start(bf16[512,512]{1,0:T(8,128)(2,1)S(1)} %get-tuple-element.79), channel_id=1, source_target_pairs={{0,6},{1,7},{2,4},{3,5},{4,2},{5,3},{6,0},{7,1},{8,14},{9,15},{10,... | collective-permute-start | bytes 1572872 | tf_op jit(solution)/shard_map/ppermute | solution.py:322
  65.0 14.4 %collective-permute-start.16 = (bf16[64,1024]{1,0:T(8,128)(2,1)S(1)}, bf16[64,1024]{1,0:T(8,128)(2,1)S(1)}, u32[]{:S(2)}, u32[]{:S(2)}) collective-permute-start(bf16[64,1024]{1,0:T(8,128)(2,1)S(1)} %line_sum.3), channel_id=1, source_target_pairs={{0,16},{1,17},{2,18},{3,19},{4,20},{5,21},{6,22},{7,23},{8,24},{9,... | collective-permute-start | bytes 393224 | tf_op jit(solution)/shard_map/ppermute | solution.py:322
  67.7 11.7 %collective-permute-start.17 = (bf16[128,1024]{1,0:T(8,128)(2,1)S(1)}, bf16[128,1024]{1,0:T(8,128)(2,1)S(1)}, u32[]{:S(2)}, u32[]{:S(2)}) collective-permute-start(bf16[128,1024]{1,0:T(8,128)(2,1)S(1)} %get-tuple-element.86), channel_id=1, source_target_pairs={{0,8},{1,9},{2,10},{3,11},{4,12},{5,13},{6,14},{7,15},{8,0},{9,1},... | collective-permute-start | bytes 786440 | tf_op jit(solution)/shard_map/ppermute | solution.py:322
  69.5 9.9 %collective-permute-start.14 = (bf16[64,1024]{1,0:T(8,128)(2,1)S(1)}, bf16[64,1024]{1,0:T(8,128)(2,1)S(1)}, u32[]{:S(2)}, u32[]{:S(2)}) collective-permute-start(bf16[64,1024]{1,0:T(8,128)(2,1)S(1)} %line_sum.2), channel_id=1, source_target_pairs={{0,16},{1,17},{2,18},{3,19},{4,20},{5,21},{6,22},{7,23},{8,24},{9,... | collective-permute-start | bytes 393224 | tf_op jit(solution)/shard_map/ppermute | solution.py:322
